TPU v7x, 32 devices: a whole 2x2x4 slice. The times are simulated.
32 devices in a mesh: img: 4 (over y, x), txt: 8 (over z, core).
Axes of the slice: x: 2, y: 2, z: 4, core: 2. Of those that a mesh axis runs over, the one named last changes fastest.
Arguments:
- images: float32 [2048, 1152], P('txt'), may hold values from -520 to 520, as said below
- texts: float32 [2048, 1152], P(('img', 'txt')), may hold values from -520 to 520, as said below
- perm: int32 [2048], P('txt'), may hold values from 0 to 2047, each once
- scale: float32 [1], replicated, may hold values from 6 to 12
- shift: float32 [1], replicated, may hold values from -3 to -1
Outputs:
- grad_images: float32 [2048, 1152], P('txt')
- grad_texts: float32 [2048, 1152], P(('img', 'txt'))
Inputs may be any that keep to these rules, and one draw needn't show every extreme that they name: `images`: every row has nonzero entries. `texts`: every row has nonzero entries.
All inputs are finite; a program needn't handle non-finite values.
Results may differ from a plain program's by a relative error of at most 0.0043.
Values may be sent and summed in bfloat16 or wider, within the bound.
No kernel may reach another device: no remote copies, remote signals or barrier semaphores. Data moves between devices by JAX's collectives and lax.ppermute only.
A program may use at most 64 MiB of HBM per device.

v0:
```python
import jax
import jax.numpy as jnp
from jax import lax
from jax.sharding import PartitionSpec as P

EPSILON = 1e-06


def shifted(value, axis, steps):
    count = lax.axis_size(axis)
    pairs = [(source, (source + steps) % count) for source in range(count)]
    return lax.ppermute(value, axis, pairs)


def unit_rows(values):
    inverse = lax.rsqrt(jnp.sum(values * values, axis=1, keepdims=True) + EPSILON)
    return (values * inverse, inverse)


def backward_unit(unit, inverse, upstream):
    return inverse * (upstream - unit * jnp.sum(unit * upstream, axis=1, keepdims=True))


def pair_terms(img_bf, paired, tile, first_id, factor, offset):
    text_ids = first_id + lax.broadcasted_iota(jnp.int32, (1, tile.shape[0]), 1)
    logits = (
        factor
        * lax.dot_general(
            img_bf, tile, (((1,), (1,)), ((), ())), preferred_element_type=jnp.float32
        )
        + offset
    )
    positive = (paired[:, None] == text_ids).astype(jnp.float32)
    weights = (jax.nn.sigmoid(logits) - positive).astype(jnp.bfloat16)
    to_images = jnp.dot(weights, tile, preferred_element_type=jnp.float32)
    to_texts = lax.dot_general(
        weights, img_bf, (((0,), (0,)), ((), ())), preferred_element_type=jnp.float32
    )
    return (to_images, to_texts)


def local(images, texts, perm, scale, shift):
    factor = scale[0]
    offset = shift[0]
    img_unit, img_inv = unit_rows(images)
    txt_unit, txt_inv = unit_rows(texts)
    img_bf = img_unit.astype(jnp.bfloat16)
    txt_bf = txt_unit.astype(jnp.bfloat16)
    rows_txt = texts.shape[0]
    cycle_len = lax.axis_size("txt")
    column = lax.axis_index("txt")
    first_block = lax.axis_index("img") * cycle_len

    def terms(tile, block_id):
        return pair_terms(img_bf, perm, tile, block_id * rows_txt, factor, offset)

    own_img, own_txt = terms(txt_bf, first_block + column)

    def hop(step, carry):
        tile, text_acc, image_acc = carry
        tile = shifted(tile, "txt", 1)
        text_acc = shifted(text_acc, "txt", 1)
        add_img, add_txt = terms(tile, first_block + (column - step) % cycle_len)
        return (tile, text_acc + add_txt, image_acc + add_img)

    tile, text_acc, image_acc = lax.fori_loop(1, cycle_len, hop, (txt_bf, own_txt, own_img))
    text_acc = shifted(text_acc, "txt", 1)
    image_total = lax.psum(image_acc, "img")
    grad_images = backward_unit(img_unit, img_inv, factor * image_total)
    grad_texts = backward_unit(txt_unit, txt_inv, factor * text_acc)
    return (grad_images, grad_texts)


def solution(mesh):
    placed = (P("txt", None), P(("img", "txt"), None), P("txt"), P(), P())
    return jax.shard_map(
        local,
        mesh=mesh,
        in_specs=placed,
        out_specs=(P("txt", None), P(("img", "txt"), None)),
        check_vma=False,
    )
```

profile of v0, /device:TPU:0, one launch (start us, length us, event | category | flops | bytes accessed | tf_op | source)
XLA Modules:
  0.0 151.9 jit_solution(13908033909894381847)
XLA Ops:
  7.2 0.0 copy-start.3
  7.2 0.0 copy-start.1
  7.2 0.0 all-reduce.2.cloned.1.call-start
  8.6 1.1 multiply_reduce_fusion.3
  9.7 1.4 multiply_reduce_fusion.1
  11.2 0.1 multiply_convert_fusion.1
  11.3 0.1 multiply_convert_fusion
  11.5 0.4 copy-done.6
  11.9 0.3 fusion.13
  12.2 0.9 fusion.14
  13.1 0.3 fusion.15
  13.5 74.3 %while.19 = (s32[]{:T(128)}, bf16[64,1152]{1,0:T(8,128)(2,1)S(1)}, f32[64,1152]{1,0:T(8,128)}, f32[256,1152]{1,0:T(8,128)S(1)}, f32[]{:T(128)}, /*index=5*/bf16[...) while((s32[]{:T(128)}, bf16[64,1152]{1,0:T(8,128)(2,1)S(1)}, ...), condition=%wide.region_3.4_spmd, body=%wide.region_2.3_spmd.sunk | while | flops 113762384 | bytes 6588282 | solution.py:66
  13.5 0.5 collective-permute-start
  14.0 2.7 %collective-permute-start.1 = (f32[64,1152]{1,0:T(8,128)}, f32[64,1152]{1,0:T(8,128)S(1)}, u32[]{:S(2)}, u32[]{:S(2)}) collective-permute-start(f32[64,1152]{1,0:T(8,128)} %get-tuple-element.346), channel_id=1, source_target_pairs={{0,1},{1,2},{2,3},{3,4},{4,5},{5,6},{6,7},{7,0},{8,9},{9,10},{10,1... | collective-permute-start | bytes 884744 | tf_op jit(solution)/shard_map/while/body/eval_jaxpr/ppermute | solution.py:12
  16.7 4.2 %collective-permute-done = bf16[64,1152]{1,0:T(8,128)(2,1)S(1)} collective-permute-done((bf16[64,1152]{1,0:T(8,128)(2,1)S(1)}, bf16[64,1152]{1,0:T(8,128)(2,1)S(1)}, u32[]{:S(2)}, u32[]{:S(2)}) %collective-permute-start) | collective-permute-done | bytes 147488 | tf_op jit(solution)/shard_map/while/body/eval_jaxpr/ppermute | solution.py:12
  20.9 1.6 %fusion.41 = bf16[256,64]{0,1:T(8,128)(2,1)S(1)} fusion(bf16[256,1152]{1,0:T(8,128)(2,1)S(1)} %get-tuple-element.364, bf16[64,1152]{1,0:T(8,128)(2,1)S(1)} %collective-permute-done, s32[256]{0:T(256)S(1)} %get-tuple-element.366, f32[]{:T(128)} %get-tuple-element.365, f32[]{:T(128)} %get-tuple-element.363, s32[64]{0:T(128)S(1)} %iota_add_fusion.3), kind=kOutput, calls=%fused_computation.9.clone.1 | convolution fusion | flops 37896192 | bytes 771336 | tf_op jit(solution)/shard_map/while/body/eval_jaxpr/dot_general | solution.py:28
  22.5 0.4 convolution_add_fusion.5
  22.9 1.1 collective-permute-done.1
  24.0 0.9 convolution_add_fusion.4
  25.0 0.4 collective-permute-start.1
  25.4 6.0 %collective-permute-done = bf16[64,1152]{1,0:T(8,128)(2,1)S(1)} collective-permute-done((bf16[64,1152]{1,0:T(8,128)(2,1)S(1)}, bf16[64,1152]{1,0:T(8,128)(2,1)S(1)}, u32[]{:S(2)}, u32[]{:S(2)}) %collective-permute-start) | collective-permute-done | bytes 147488 | tf_op jit(solution)/shard_map/while/body/eval_jaxpr/ppermute | solution.py:12
  31.3 1.6 %fusion.41 = bf16[256,64]{0,1:T(8,128)(2,1)S(1)} fusion(bf16[256,1152]{1,0:T(8,128)(2,1)S(1)} %get-tuple-element.364, bf16[64,1152]{1,0:T(8,128)(2,1)S(1)} %collective-permute-done, s32[256]{0:T(256)S(1)} %get-tuple-element.366, f32[]{:T(128)} %get-tuple-element.365, f32[]{:T(128)} %get-tuple-element.363, s32[64]{0:T(128)S(1)} %iota_add_fusion.3), kind=kOutput, calls=%fused_computation.9.clone.1 | convolution fusion | flops 37896192 | bytes 771336 | tf_op jit(solution)/shard_map/while/body/eval_jaxpr/dot_general | solution.py:28
  33.0 0.4 convolution_add_fusion.5
  33.4 1.1 collective-permute-done.1
  34.5 0.9 convolution_add_fusion.4
  35.4 6.4 %collective-permute-done = bf16[64,1152]{1,0:T(8,128)(2,1)S(1)} collective-permute-done((bf16[64,1152]{1,0:T(8,128)(2,1)S(1)}, bf16[64,1152]{1,0:T(8,128)(2,1)S(1)}, u32[]{:S(2)}, u32[]{:S(2)}) %collective-permute-start) | collective-permute-done | bytes 147488 | tf_op jit(solution)/shard_map/while/body/eval_jaxpr/ppermute | solution.py:12
  41.8 1.6 %fusion.41 = bf16[256,64]{0,1:T(8,128)(2,1)S(1)} fusion(bf16[256,1152]{1,0:T(8,128)(2,1)S(1)} %get-tuple-element.364, bf16[64,1152]{1,0:T(8,128)(2,1)S(1)} %collective-permute-done, s32[256]{0:T(256)S(1)} %get-tuple-element.366, f32[]{:T(128)} %get-tuple-element.365, f32[]{:T(128)} %get-tuple-element.363, s32[64]{0:T(128)S(1)} %iota_add_fusion.3), kind=kOutput, calls=%fused_computation.9.clone.1 | convolution fusion | flops 37896192 | bytes 771336 | tf_op jit(solution)/shard_map/while/body/eval_jaxpr/dot_general | solution.py:28
  43.4 0.4 convolution_add_fusion.5
  43.8 1.1 collective-permute-done.1
  45.0 0.9 convolution_add_fusion.4
  45.9 0.0 collective-permute-start
  45.9 0.0 collective-permute-start.1
  45.9 6.4 %collective-permute-done = bf16[64,1152]{1,0:T(8,128)(2,1)S(1)} collective-permute-done((bf16[64,1152]{1,0:T(8,128)(2,1)S(1)}, bf16[64,1152]{1,0:T(8,128)(2,1)S(1)}, u32[]{:S(2)}, u32[]{:S(2)}) %collective-permute-start) | collective-permute-done | bytes 147488 | tf_op jit(solution)/shard_map/while/body/eval_jaxpr/ppermute | solution.py:12
  52.3 1.6 %fusion.41 = bf16[256,64]{0,1:T(8,128)(2,1)S(1)} fusion(bf16[256,1152]{1,0:T(8,128)(2,1)S(1)} %get-tuple-element.364, bf16[64,1152]{1,0:T(8,128)(2,1)S(1)} %collective-permute-done, s32[256]{0:T(256)S(1)} %get-tuple-element.366, f32[]{:T(128)} %get-tuple-element.365, f32[]{:T(128)} %get-tuple-element.363, s32[64]{0:T(128)S(1)} %iota_add_fusion.3), kind=kOutput, calls=%fused_computation.9.clone.1 | convolution fusion | flops 37896192 | bytes 771336 | tf_op jit(solution)/shard_map/while/body/eval_jaxpr/dot_general | solution.py:28
  53.9 0.4 convolution_add_fusion.5
  54.3 1.1 collective-permute-done.1
  55.4 0.9 convolution_add_fusion.4
  56.4 0.0 collective-permute-start
  56.4 0.0 collective-permute-start.1
  56.4 6.4 %collective-permute-done = bf16[64,1152]{1,0:T(8,128)(2,1)S(1)} collective-permute-done((bf16[64,1152]{1,0:T(8,128)(2,1)S(1)}, bf16[64,1152]{1,0:T(8,128)(2,1)S(1)}, u32[]{:S(2)}, u32[]{:S(2)}) %collective-permute-start) | collective-permute-done | bytes 147488 | tf_op jit(solution)/shard_map/while/body/eval_jaxpr/ppermute | solution.py:12
  62.7 1.6 %fusion.41 = bf16[256,64]{0,1:T(8,128)(2,1)S(1)} fusion(bf16[256,1152]{1,0:T(8,128)(2,1)S(1)} %get-tuple-element.364, bf16[64,1152]{1,0:T(8,128)(2,1)S(1)} %collective-permute-done, s32[256]{0:T(256)S(1)} %get-tuple-element.366, f32[]{:T(128)} %get-tuple-element.365, f32[]{:T(128)} %get-tuple-element.363, s32[64]{0:T(128)S(1)} %iota_add_fusion.3), kind=kOutput, calls=%fused_computation.9.clone.1 | convolution fusion | flops 37896192 | bytes 771336 | tf_op jit(solution)/shard_map/while/body/eval_jaxpr/dot_general | solution.py:28
  64.4 0.4 convolution_add_fusion.5
  64.8 1.1 collective-permute-done.1
  65.9 0.9 convolution_add_fusion.4
  66.8 6.4 %collective-permute-done = bf16[64,1152]{1,0:T(8,128)(2,1)S(1)} collective-permute-done((bf16[64,1152]{1,0:T(8,128)(2,1)S(1)}, bf16[64,1152]{1,0:T(8,128)(2,1)S(1)}, u32[]{:S(2)}, u32[]{:S(2)}) %collective-permute-start) | collective-permute-done | bytes 147488 | tf_op jit(solution)/shard_map/while/body/eval_jaxpr/ppermute | solution.py:12
  73.2 1.6 %fusion.41 = bf16[256,64]{0,1:T(8,128)(2,1)S(1)} fusion(bf16[256,1152]{1,0:T(8,128)(2,1)S(1)} %get-tuple-element.364, bf16[64,1152]{1,0:T(8,128)(2,1)S(1)} %collective-permute-done, s32[256]{0:T(256)S(1)} %get-tuple-element.366, f32[]{:T(128)} %get-tuple-element.365, f32[]{:T(128)} %get-tuple-element.363, s32[64]{0:T(128)S(1)} %iota_add_fusion.3), kind=kOutput, calls=%fused_computation.9.clone.1 | convolution fusion | flops 37896192 | bytes 771336 | tf_op jit(solution)/shard_map/while/body/eval_jaxpr/dot_general | solution.py:28
  74.9 0.4 convolution_add_fusion.5
  75.2 1.1 collective-permute-done.1
  76.4 0.9 convolution_add_fusion.4
  77.3 0.0 collective-permute-start
  77.3 6.4 %collective-permute-done = bf16[64,1152]{1,0:T(8,128)(2,1)S(1)} collective-permute-done((bf16[64,1152]{1,0:T(8,128)(2,1)S(1)}, bf16[64,1152]{1,0:T(8,128)(2,1)S(1)}, u32[]{:S(2)}, u32[]{:S(2)}) %collective-permute-start) | collective-permute-done | bytes 147488 | tf_op jit(solution)/shard_map/while/body/eval_jaxpr/ppermute | solution.py:12
  83.7 1.6 %fusion.41 = bf16[256,64]{0,1:T(8,128)(2,1)S(1)} fusion(bf16[256,1152]{1,0:T(8,128)(2,1)S(1)} %get-tuple-element.364, bf16[64,1152]{1,0:T(8,128)(2,1)S(1)} %collective-permute-done, s32[256]{0:T(256)S(1)} %get-tuple-element.366, f32[]{:T(128)} %get-tuple-element.365, f32[]{:T(128)} %get-tuple-element.363, s32[64]{0:T(128)S(1)} %iota_add_fusion.3), kind=kOutput, calls=%fused_computation.9.clone.1 | convolution fusion | flops 37896192 | bytes 771336 | tf_op jit(solution)/shard_map/while/body/eval_jaxpr/dot_general | solution.py:28
  85.3 0.4 convolution_add_fusion.5
  85.7 1.1 collective-permute-done.1
  86.8 0.9 convolution_add_fusion.4
  87.8 1.0 copy-done
  88.8 0.0 all-reduce.2.cloned.1.call-update
  88.8 0.1 copy-done.5
  88.9 7.9 %collective-permute-done.2 = f32[64,1152]{1,0:T(8,128)S(1)} collective-permute-done((f32[64,1152]{1,0:T(8,128)S(1)}, f32[64,1152]{1,0:T(8,128)S(1)}, u32[]{:S(2)}, u32[]{:S(2)}) %collective-permute-start.2) | collective-permute-done | bytes 294944 | tf_op jit(solution)/shard_map/ppermute | solution.py:12
  96.9 0.2 multiply_reduce_fusion.2
  97.1 0.8 subtract_multiply_fusion.1
  97.9 44.2 %all-reduce.2.cloned.1.call-done = f32[256,1152]{1,0:T(8,128)} async-done(((f32[256,1152]{1,0:T(8,128)}), f32[256,1152]{1,0:T(8,128)}) %all-reduce.2.cloned.1.call-update) | async-done | bytes 1179664 | tf_op jit(solution)/shard_map/psum | solution.py:68
  142.2 1.6 %multiply_reduce_fusion = f32[256]{0:T(256)S(1)} fusion(f32[256,1152]{1,0:T(8,128)} %all-reduce.2.cloned.1.call-done, f32[256,1152]{1,0:T(8,128)S(1)} %copy-done.1, f32[]{:T(128)} %bitcast.26, f32[256]{0:T(256)S(1)} %add_rsqrt_fusion), kind=kLoop, calls=%fused_computation.12 | loop fusion | flops 1179392 | bytes 2361348 | tf_op jit(solution)/shard_map/reduce_sum | solution.py:21
  143.8 1.3 subtract_multiply_fusion
  (33 shorter events, 0.2 us)
Async XLA Ops:
  7.2 4.0 %copy-start.3 = (f32[64,1152]{1,0:T(8,128)S(1)}, f32[64,1152]{1,0:T(8,128)}, u32[]{:S(2)}) copy-start(f32[64,1152]{1,0:T(8,128)} %param.8) | copy-start | bytes 884740
  7.2 4.1 %copy-start.1 = (f32[256,1152]{1,0:T(8,128)S(1)}, f32[256,1152]{1,0:T(8,128)}, u32[]{:S(2)}) copy-start(f32[256,1152]{1,0:T(8,128)} %param.7) | copy-start | bytes 3538948
  7.2 135.0 %all-reduce.2.cloned.1.call-start = ((), (), s32[]{:S(2)}) async-start(), calls=%async_computation | async-start | bytes 2359296 | tf_op jit(solution)/shard_map/psum | solution.py:68
  11.2 0.7 copy-start.6
  13.5 7.4 %collective-permute-start = (bf16[64,1152]{1,0:T(8,128)(2,1)S(1)}, bf16[64,1152]{1,0:T(8,128)(2,1)S(1)}, u32[]{:S(2)}, u32[]{:S(2)}) collective-permute-start(bf16[64,1152]{1,0:T(8,128)(2,1)S(1)} %get-tuple-element.345), channel_id=1, source_target_pairs={{0,1},{1,2},{2,3},{3,4},{4,5},{5,6},{6,7},{7,0},{8,9},{9,10},{10,1... | collective-permute-start | bytes 442376 | tf_op jit(solution)/shard_map/while/body/eval_jaxpr/ppermute | solution.py:12
  14.0 10.0 %collective-permute-start.1 = (f32[64,1152]{1,0:T(8,128)}, f32[64,1152]{1,0:T(8,128)S(1)}, u32[]{:S(2)}, u32[]{:S(2)}) collective-permute-start(f32[64,1152]{1,0:T(8,128)} %get-tuple-element.346), channel_id=1, source_target_pairs={{0,1},{1,2},{2,3},{3,4},{4,5},{5,6},{6,7},{7,0},{8,9},{9,10},{10,1... | collective-permute-start | bytes 884744 | tf_op jit(solution)/shard_map/while/body/eval_jaxpr/ppermute | solution.py:12
  25.0 6.4 %collective-permute-start = (bf16[64,1152]{1,0:T(8,128)(2,1)S(1)}, bf16[64,1152]{1,0:T(8,128)(2,1)S(1)}, u32[]{:S(2)}, u32[]{:S(2)}) collective-permute-start(bf16[64,1152]{1,0:T(8,128)(2,1)S(1)} %get-tuple-element.345), channel_id=1, source_target_pairs={{0,1},{1,2},{2,3},{3,4},{4,5},{5,6},{6,7},{7,0},{8,9},{9,10},{10,1... | collective-permute-start | bytes 442376 | tf_op jit(solution)/shard_map/while/body/eval_jaxpr/ppermute | solution.py:12
  25.0 9.5 %collective-permute-start.1 = (f32[64,1152]{1,0:T(8,128)}, f32[64,1152]{1,0:T(8,128)S(1)}, u32[]{:S(2)}, u32[]{:S(2)}) collective-permute-start(f32[64,1152]{1,0:T(8,128)} %get-tuple-element.346), channel_id=1, source_target_pairs={{0,1},{1,2},{2,3},{3,4},{4,5},{5,6},{6,7},{7,0},{8,9},{9,10},{10,1... | collective-permute-start | bytes 884744 | tf_op jit(solution)/shard_map/while/body/eval_jaxpr/ppermute | solution.py:12
  35.4 6.4 %collective-permute-start = (bf16[64,1152]{1,0:T(8,128)(2,1)S(1)}, bf16[64,1152]{1,0:T(8,128)(2,1)S(1)}, u32[]{:S(2)}, u32[]{:S(2)}) collective-permute-start(bf16[64,1152]{1,0:T(8,128)(2,1)S(1)} %get-tuple-element.345), channel_id=1, source_target_pairs={{0,1},{1,2},{2,3},{3,4},{4,5},{5,6},{6,7},{7,0},{8,9},{9,10},{10,1... | collective-permute-start | bytes 442376 | tf_op jit(solution)/shard_map/while/body/eval_jaxpr/ppermute | solution.py:12
  35.4 9.5 %collective-permute-start.1 = (f32[64,1152]{1,0:T(8,128)}, f32[64,1152]{1,0:T(8,128)S(1)}, u32[]{:S(2)}, u32[]{:S(2)}) collective-permute-start(f32[64,1152]{1,0:T(8,128)} %get-tuple-element.346), channel_id=1, source_target_pairs={{0,1},{1,2},{2,3},{3,4},{4,5},{5,6},{6,7},{7,0},{8,9},{9,10},{10,1... | collective-permute-start | bytes 884744 | tf_op jit(solution)/shard_map/while/body/eval_jaxpr/ppermute | solution.py:12
  45.9 6.4 %collective-permute-start = (bf16[64,1152]{1,0:T(8,128)(2,1)S(1)}, bf16[64,1152]{1,0:T(8,128)(2,1)S(1)}, u32[]{:S(2)}, u32[]{:S(2)}) collective-permute-start(bf16[64,1152]{1,0:T(8,128)(2,1)S(1)} %get-tuple-element.345), channel_id=1, source_target_pairs={{0,1},{1,2},{2,3},{3,4},{4,5},{5,6},{6,7},{7,0},{8,9},{9,10},{10,1... | collective-permute-start | bytes 442376 | tf_op jit(solution)/shard_map/while/body/eval_jaxpr/ppermute | solution.py:12
  45.9 9.5 %collective-permute-start.1 = (f32[64,1152]{1,0:T(8,128)}, f32[64,1152]{1,0:T(8,128)S(1)}, u32[]{:S(2)}, u32[]{:S(2)}) collective-permute-start(f32[64,1152]{1,0:T(8,128)} %get-tuple-element.346), channel_id=1, source_target_pairs={{0,1},{1,2},{2,3},{3,4},{4,5},{5,6},{6,7},{7,0},{8,9},{9,10},{10,1... | collective-permute-start | bytes 884744 | tf_op jit(solution)/shard_map/while/body/eval_jaxpr/ppermute | solution.py:12
  56.4 6.4 %collective-permute-start = (bf16[64,1152]{1,0:T(8,128)(2,1)S(1)}, bf16[64,1152]{1,0:T(8,128)(2,1)S(1)}, u32[]{:S(2)}, u32[]{:S(2)}) collective-permute-start(bf16[64,1152]{1,0:T(8,128)(2,1)S(1)} %get-tuple-element.345), channel_id=1, source_target_pairs={{0,1},{1,2},{2,3},{3,4},{4,5},{5,6},{6,7},{7,0},{8,9},{9,10},{10,1... | collective-permute-start | bytes 442376 | tf_op jit(solution)/shard_map/while/body/eval_jaxpr/ppermute | solution.py:12
  56.4 9.5 %collective-permute-start.1 = (f32[64,1152]{1,0:T(8,128)}, f32[64,1152]{1,0:T(8,128)S(1)}, u32[]{:S(2)}, u32[]{:S(2)}) collective-permute-start(f32[64,1152]{1,0:T(8,128)} %get-tuple-element.346), channel_id=1, source_target_pairs={{0,1},{1,2},{2,3},{3,4},{4,5},{5,6},{6,7},{7,0},{8,9},{9,10},{10,1... | collective-permute-start | bytes 884744 | tf_op jit(solution)/shard_map/while/body/eval_jaxpr/ppermute | solution.py:12
  66.8 6.4 %collective-permute-start = (bf16[64,1152]{1,0:T(8,128)(2,1)S(1)}, bf16[64,1152]{1,0:T(8,128)(2,1)S(1)}, u32[]{:S(2)}, u32[]{:S(2)}) collective-permute-start(bf16[64,1152]{1,0:T(8,128)(2,1)S(1)} %get-tuple-element.345), channel_id=1, source_target_pairs={{0,1},{1,2},{2,3},{3,4},{4,5},{5,6},{6,7},{7,0},{8,9},{9,10},{10,1... | collective-permute-start | bytes 442376 | tf_op jit(solution)/shard_map/while/body/eval_jaxpr/ppermute | solution.py:12
  66.8 9.5 %collective-permute-start.1 = (f32[64,1152]{1,0:T(8,128)}, f32[64,1152]{1,0:T(8,128)S(1)}, u32[]{:S(2)}, u32[]{:S(2)}) collective-permute-start(f32[64,1152]{1,0:T(8,128)} %get-tuple-element.346), channel_id=1, source_target_pairs={{0,1},{1,2},{2,3},{3,4},{4,5},{5,6},{6,7},{7,0},{8,9},{9,10},{10,1... | collective-permute-start | bytes 884744 | tf_op jit(solution)/shard_map/while/body/eval_jaxpr/ppermute | solution.py:12
  77.3 6.4 %collective-permute-start = (bf16[64,1152]{1,0:T(8,128)(2,1)S(1)}, bf16[64,1152]{1,0:T(8,128)(2,1)S(1)}, u32[]{:S(2)}, u32[]{:S(2)}) collective-permute-start(bf16[64,1152]{1,0:T(8,128)(2,1)S(1)} %get-tuple-element.345), channel_id=1, source_target_pairs={{0,1},{1,2},{2,3},{3,4},{4,5},{5,6},{6,7},{7,0},{8,9},{9,10},{10,1... | collective-permute-start | bytes 442376 | tf_op jit(solution)/shard_map/while/body/eval_jaxpr/ppermute | solution.py:12
  77.3 9.5 %collective-permute-start.1 = (f32[64,1152]{1,0:T(8,128)}, f32[64,1152]{1,0:T(8,128)S(1)}, u32[]{:S(2)}, u32[]{:S(2)}) collective-permute-start(f32[64,1152]{1,0:T(8,128)} %get-tuple-element.346), channel_id=1, source_target_pairs={{0,1},{1,2},{2,3},{3,4},{4,5},{5,6},{6,7},{7,0},{8,9},{9,10},{10,1... | collective-permute-start | bytes 884744 | tf_op jit(solution)/shard_map/while/body/eval_jaxpr/ppermute | solution.py:12
  87.8 1.0 copy-start
  87.8 1.2 copy-start.5
  87.8 9.1 %copy-start.4 = (f32[64,1152]{1,0:T(8,128)S(1)}, f32[64,1152]{1,0:T(8,128)}, u32[]{:S(2)}) copy-start(f32[64,1152]{1,0:T(8,128)} %param.8) | copy-start | bytes 884740
  88.9 7.9 %collective-permute-start.2 = (f32[64,1152]{1,0:T(8,128)S(1)}, f32[64,1152]{1,0:T(8,128)S(1)}, u32[]{:S(2)}, u32[]{:S(2)}) collective-permute-start(f32[64,1152]{1,0:T(8,128)S(1)} %copy-done.5), channel_id=1, source_target_pairs={{0,1},{1,2},{2,3},{3,4},{4,5},{5,6},{6,7},{7,0},{8,9},{9,10},{10,1... | collective-permute-start | bytes 884744 | tf_op jit(solution)/shard_map/ppermute | solution.py:12
  142.1 1.6 %copy-start.2 = (f32[256,1152]{1,0:T(8,128)S(1)}, f32[256,1152]{1,0:T(8,128)}, u32[]{:S(2)}) copy-start(f32[256,1152]{1,0:T(8,128)} %all-reduce.2.cloned.1.call-done) | copy-start | bytes 3538948
Sparse Core Ops, SparseCore 0:
  88.9 53.1 all-reduce.1
where the time goes:
time: 152 us
  waiting for transfers between devices  102 us (67%)
  matrix products  22.2 us (15%)
  between operations  15.5 us (10%)
  other arithmetic  6.72 us (4%)
  starting transfers between devices  3.66 us (2%)
  local copies, waits for them, and re-layouts  1.65 us (1%)
    ppermute x15, waiting for transfers between devices, shifted(): return lax.ppermute(value, axis, pairs)  57.6 us
    psum x1, waiting for transfers between devices, local(): image_total = lax.psum(image_acc, 'img')  44.2 us
    dot_general x8, matrix products, pair_terms(): lax.dot_general(img_bf, tile, (((1,), (1,)), ((), ())), preferred_element...  11.7 us
    dot_general x8, matrix products, pair_terms(): lax.dot_general(weights, img_bf, (((0,), (0,)), ((), ())), preferred_elem...  7.52 us
    ppermute x15, starting transfers between devices, shifted(): return lax.ppermute(value, axis, pairs)  3.62 us
  transfers between devices with their start and end apart: 16, of which 16 were waited for; matrix products, arithmetic and copies ran while one was open for 10% of the time, Pallas kernels for 0%

commit v1 on v0

v1 whole, which is shorter than its diff:
```python
import functools

import jax
import jax.numpy as jnp
from jax import lax
from jax.experimental import pallas as pl
from jax.experimental.pallas import tpu as pltpu
from jax.sharding import PartitionSpec as P

EPSILON = 1e-06
F32 = jnp.float32
BF16 = jnp.bfloat16
VMEM = pl.BlockSpec(memory_space=pltpu.VMEM)
SMEM = pl.BlockSpec(memory_space=pltpu.SMEM)


def call(body, outs, args, specs, limit, flops):
    size = sum(a.size * a.dtype.itemsize for a in args)
    size += sum(o.size * o.dtype.itemsize for o in outs)
    return pl.pallas_call(
        body,
        out_shape=outs,
        in_specs=specs,
        out_specs=[VMEM] * len(outs),
        compiler_params=pltpu.CompilerParams(vmem_limit_bytes=limit),
        cost_estimate=pl.CostEstimate(flops=flops, bytes_accessed=size, transcendentals=0),
    )(*args)


def struct(rows, cols, dtype):
    return jax.ShapeDtypeStruct((rows, cols), dtype)


def inverse_norm(values):
    return lax.rsqrt(jnp.sum(values * values, axis=1, keepdims=True) + EPSILON)


def backward_unit(values, upstream):
    inverse = inverse_norm(values)
    unit = values * inverse
    return inverse * (upstream - unit * jnp.sum(unit * upstream, axis=1, keepdims=True))


def unit_body(img_ref, txt_ref, img_out, txt_out):
    txt = txt_ref[...]
    txt_out[...] = (txt * inverse_norm(txt)).astype(BF16)
    img = img_ref[...]
    img_out[...] = (img * inverse_norm(img)).astype(BF16)


def pair_body(blocks, scalars, factors, perm_own, perm_other, img_own, img_other, *refs):
    txt = refs[:blocks]
    own_img, other_img, own_txt = refs[blocks : blocks + 3]
    other_txt = refs[blocks + 3 :]
    factor = factors[0]
    offset = factors[1]
    rows = txt[0].shape[0]
    tile = jnp.concatenate([t[...] for t in txt], axis=0)
    row = lax.broadcasted_iota(jnp.int32, (rows, 1), 0)
    ids = jnp.concatenate([row + scalars[k] for k in range(blocks)], axis=0)

    def weights(img, perm):
        logits = (
            factor
            * lax.dot_general(tile, img[...], (((1,), (1,)), ((), ())), preferred_element_type=F32)
            + offset
        )
        positive = (ids == perm[...]).astype(F32)
        return (jax.nn.sigmoid(logits) - positive).astype(BF16)

    w_other = weights(img_other, perm_other)
    other_img[...] = lax.dot_general(
        w_other, tile, (((0,), (0,)), ((), ())), preferred_element_type=F32
    ).astype(BF16)
    w_own = weights(img_own, perm_own)
    own_img[...] = lax.dot_general(
        w_own, tile, (((0,), (0,)), ((), ())), preferred_element_type=F32
    )
    to_txt = jnp.dot(w_own, img_own[...], preferred_element_type=F32) + jnp.dot(
        w_other, img_other[...], preferred_element_type=F32
    )
    own_txt[...] = to_txt[:rows]
    for k in range(1, blocks):
        other_txt[k - 1][...] = to_txt[k * rows : (k + 1) * rows].astype(BF16)


def split_body(count, position, own, other, keep, *send):
    rows = keep.shape[0]
    for k in range(count):
        start = pl.multiple_of(lax.rem(position[0] + k, count) * rows, rows)
        part = own[pl.ds(start, rows), :] + other[pl.ds(start, rows), :].astype(F32)
        if k == 0:
            keep[...] = part
        else:
            send[k - 1][...] = part.astype(BF16)


def total_of(own, parts):
    total = own[...]
    for part in parts:
        total = total + part[...].astype(F32)
    return total


def finish_img_body(position, factors, img_ref, own, *refs):
    *parts, out = refs
    rows = own.shape[0]
    start = pl.multiple_of(position[0] * rows, rows)
    upstream = factors[0] * total_of(own, parts)
    out[...] = backward_unit(img_ref[pl.ds(start, rows), :], upstream).astype(BF16)


def finish_txt_body(factors, txt_ref, own, *refs):
    *parts, out = refs
    out[...] = backward_unit(txt_ref[...], factors[0] * total_of(own, parts))


def join_body(count, position, *refs):
    *parts, out = refs
    rows = parts[0].shape[0]
    for k in range(count):
        start = pl.multiple_of(lax.rem(position[0] + count - k, count) * rows, rows)
        out[pl.ds(start, rows), :] = parts[k][...].astype(F32)


def shifted(value, axis, steps):
    count = lax.axis_size(axis)
    return lax.ppermute(value, axis, [(s, (s + steps) % count) for s in range(count)])


def swapped(value):
    count = lax.axis_size("txt")
    return lax.ppermute(value, "txt", [(s, s ^ 1) for s in range(count)])


def local(images, texts, perm, scale, shift):
    rows, width = images.shape
    txt_rows = texts.shape[0]
    line = lax.axis_size("txt")
    blocks = line // 2
    count = lax.axis_size("img")
    part = rows // count
    column = lax.axis_index("txt")
    place = lax.axis_index("img")
    position = place.reshape(1).astype(jnp.int32)
    factors = jnp.concatenate([scale, shift])
    perm_row = perm.reshape(1, rows)

    img_bf, txt_bf = call(
        unit_body,
        [struct(rows, width, BF16), struct(txt_rows, width, BF16)],
        [images, texts],
        [VMEM] * 2,
        16 << 20,
        4 * rows * width,
    )
    tiles = [txt_bf] + [shifted(txt_bf, "txt", 2 * k) for k in range(1, blocks)]
    img_other = swapped(img_bf)
    perm_other = swapped(perm_row)
    firsts = jnp.stack(
        [(place * line + (column - 2 * k) % line) * txt_rows for k in range(blocks)]
    ).astype(jnp.int32)
    own_img, other_img, own_txt, *other_txt = call(
        functools.partial(pair_body, blocks),
        [struct(rows, width, F32), struct(rows, width, BF16), struct(txt_rows, width, F32)]
        + [struct(txt_rows, width, BF16)] * (blocks - 1),
        [firsts, factors, perm_row, perm_other, img_bf, img_other, *tiles],
        [SMEM] * 2 + [VMEM] * (4 + blocks),
        48 << 20,
        12 * rows * blocks * txt_rows * width,
    )
    from_other = swapped(other_img)
    back = [shifted(other_txt[k - 1], "txt", -2 * k) for k in range(1, blocks)]

    keep, *send = call(
        functools.partial(split_body, count),
        [struct(part, width, F32)] + [struct(part, width, BF16)] * (count - 1),
        [position, own_img, from_other],
        [SMEM, VMEM, VMEM],
        24 << 20,
        rows * width,
    )
    got = [shifted(send[k - 1], "img", k) for k in range(1, count)]
    (grad_part,) = call(
        finish_img_body,
        [struct(part, width, BF16)],
        [position, factors, images, keep, *got],
        [SMEM] * 2 + [VMEM] * (1 + count),
        24 << 20,
        10 * part * width,
    )
    grads = [grad_part] + [shifted(grad_part, "img", k) for k in range(1, count)]
    (grad_images,) = call(
        functools.partial(join_body, count),
        [struct(rows, width, F32)],
        [position, *grads],
        [SMEM] + [VMEM] * count,
        24 << 20,
        rows * width,
    )
    (grad_texts,) = call(
        finish_txt_body,
        [struct(txt_rows, width, F32)],
        [factors, texts, own_txt, *back],
        [SMEM] + [VMEM] * (1 + blocks),
        24 << 20,
        10 * txt_rows * width,
    )
    return (grad_images, grad_texts)


def solution(mesh):
    placed = (P("txt", None), P(("img", "txt"), None), P("txt"), P(), P())
    return jax.shard_map(
        local,
        mesh=mesh,
        in_specs=placed,
        out_specs=(P("txt", None), P(("img", "txt"), None)),
        check_vma=False,
    )
```

time: 152 us -> 49.5 us (0.33)
  waiting for transfers between devices: 102 us -> 19.6 us
  matrix products: 22.2 us -> 0 us
  starting transfers between devices: 3.66 us -> 18.6 us
  between operations: 15.5 us -> 2 us
  other arithmetic: 6.72 us -> 0.15 us
  Pallas kernels: 0 us -> 6.36 us
    psum x1 -> x0, waiting for transfers between devices: 44.2 us -> none  [local(): image_total = lax.psum(image_acc, 'img')]
    ppermute x15, waiting for transfers between devices: 57.6 us -> 19.6 us  [the longest x12 17.6 us: shifted(): lax.ppermute(value, axis, [(s, (s + steps) % count) for s in range(count)])]
    dot_general x24 -> x0, matrix products: 22.2 us -> none  [the longest x8 11.7 us: pair_terms(): lax.dot_general(img_bf, tile, (((1,), (1,)), ((), ())), preferred_element...]
    ppermute x15, starting transfers between devices: 3.62 us -> 18.6 us  [the longest x12 18 us: shifted(): lax.ppermute(value, axis, [(s, (s + steps) % count) for s in range(count)])]
    pallas_call x0 -> x6, Pallas kernels: none -> 6.36 us  [call(): pl.pallas_call(body, out_shape=outs, in_specs=specs, out_specs=[VMEM] * l...]
    reduce_sum x4 -> x0, other arithmetic: 4.36 us -> none  [the longest x2 2.52 us: unit_rows(): jnp.sum(values * values, axis=1, keepdims=True) + EPSILON]
    mul x2 -> x0, other arithmetic: 2.11 us -> none  [backward_unit(): inverse * (upstream - unit * jnp.sum(unit * upstream, axis=1, keepdims=Tr...]
  transfers between devices with their start and end apart: 16 -> 15, of which waited for: 16 -> 7; matrix products, arithmetic and copies ran while one was open for 10% -> 0% of each run, Pallas kernels for 0% -> 5%
where the time goes in v1:
time: 49.5 us; the launch traced here: 48.9 us
  waiting for transfers between devices  19.6 us (40%)
  starting transfers between devices  18.6 us (38%)
  Pallas kernels  6.36 us (13%)
  local copies, waits for them, and re-layouts  2.24 us (5%)
  between operations  2 us (4%)
    ppermute x12, starting transfers between devices, shifted(): lax.ppermute(value, axis, [(s, (s + steps) % count) for s in range(count)])  18 us
    ppermute x12, waiting for transfers between devices, shifted(): lax.ppermute(value, axis, [(s, (s + steps) % count) for s in range(count)])  17.6 us
    pallas_call x6, Pallas kernels, call(): pl.pallas_call(body, out_shape=outs, in_specs=specs, out_specs=[VMEM] * l...  6.36 us
    unnamed x10, local copies, waits for them, and re-layouts  2.24 us
    ppermute x3, waiting for transfers between devices, swapped(): return lax.ppermute(value, 'txt', [(s, s ^ 1) for s in range(count)])  2 us
  transfers between devices with their start and end apart: 15, of which 7 were waited for; matrix products, arithmetic and copies ran while one was open for 0% of the time, Pallas kernels for 5%

profile of v1, /device:TPU:0, one launch (start us, length us, event | category | flops | bytes accessed | tf_op | source)
XLA Modules:
  0.0 48.9 jit_solution(16145363999113795664)
XLA Ops:
  0.6 0.0 copy-start
  0.6 1.3 %copy-done = f32[256,1152]{1,0:T(8,128)S(1)} copy-done((f32[256,1152]{1,0:T(8,128)S(1)}, f32[256,1152]{1,0:T(8,128)}, u32[]{:S(2)}) %copy-start) | copy-done | bytes 1179672
  1.9 0.0 copy-start.2
  1.9 1.0 %copy-done.2 = f32[64,1152]{1,0:T(8,128)S(1)} copy-done((f32[64,1152]{1,0:T(8,128)S(1)}, f32[64,1152]{1,0:T(8,128)}, u32[]{:S(2)}) %copy-start.2) | copy-done | bytes 294936
  2.9 0.0 copy-start.4
  2.9 0.2 shard_map.68
  3.1 0.5 %collective-permute-start.1 = (bf16[256,1152]{1,0:T(8,128)(2,1)S(1)}, bf16[256,1152]{1,0:T(8,128)(2,1)S(1)}, u32[]{:S(2)}, u32[]{:S(2)}) collective-permute-start(bf16[256,1152]{1,0:T(8,128)(2,1)S(1)} %get-tuple-element.14.img_own), channel_id=1, source_target_pairs={{0,1},{1,0},{2,3},{3,2},{4,5},{5,4},{6,7},{7,6},{8,9},{9,8},{10,11... | collective-permute-start | bytes 1769480 | tf_op jit(solution)/shard_map/ppermute | solution.py:133
  3.6 4.7 %collective-permute-start.4 = (bf16[64,1152]{1,0:T(8,128)(2,1)S(1)}, bf16[64,1152]{1,0:T(8,128)(2,1)S(1)}, u32[]{:S(2)}, u32[]{:S(2)}) collective-permute-start(bf16[64,1152]{1,0:T(8,128)(2,1)S(1)} %get-tuple-element.15.refs_0_), channel_id=1, source_target_pairs={{0,6},{1,7},{2,0},{3,1},{4,2},{5,3},{6,4},{7,5},{8,14},{9,15},{10,... | collective-permute-start | bytes 442376 | tf_op jit(solution)/shard_map/ppermute | solution.py:128
  8.2 0.0 collective-permute-start.3
  8.2 1.0 %collective-permute-start.2 = (bf16[64,1152]{1,0:T(8,128)(2,1)S(1)}, bf16[64,1152]{1,0:T(8,128)(2,1)S(1)}, u32[]{:S(2)}, u32[]{:S(2)}) collective-permute-start(bf16[64,1152]{1,0:T(8,128)(2,1)S(1)} %get-tuple-element.15.refs_0_), channel_id=1, source_target_pairs={{0,2},{1,3},{2,4},{3,5},{4,6},{5,7},{6,0},{7,1},{8,10},{9,11},{10,... | collective-permute-start | bytes 442376 | tf_op jit(solution)/shard_map/ppermute | solution.py:128
  9.3 0.0 copy-done.4
  9.3 0.0 collective-permute-start
  10.6 0.1 pad_maximum_fusion.factors
  10.6 0.1 pad_add_fusion.scalars
  10.7 0.0 collective-permute-done.perm_other
  10.7 1.8 %collective-permute-done.4.refs_3_ = bf16[64,1152]{1,0:T(8,128)(2,1)S(1)} collective-permute-done((bf16[64,1152]{1,0:T(8,128)(2,1)S(1)}, bf16[64,1152]{1,0:T(8,128)(2,1)S(1)}, u32[]{:S(2)}, u32[]{:S(2)}) %collective-permute-start.4) | collective-permute-done | bytes 147488 | tf_op jit(solution)/shard_map/ppermute | solution.py:128
  12.5 8.9 %collective-permute-done.3.refs_2_ = bf16[64,1152]{1,0:T(8,128)(2,1)S(1)} collective-permute-done((bf16[64,1152]{1,0:T(8,128)(2,1)S(1)}, bf16[64,1152]{1,0:T(8,128)(2,1)S(1)}, u32[]{:S(2)}, u32[]{:S(2)}) %collective-permute-start.3) | collective-permute-done | bytes 147488 | tf_op jit(solution)/shard_map/ppermute | solution.py:128
  21.4 0.0 collective-permute-done.2.refs_1_
  21.4 0.0 collective-permute-done.1.img_other
  21.4 2.7 %shard_map.69 = (f32[256,1152]{1,0:T(8,128)S(1)}, bf16[256,1152]{1,0:T(8,128)(2,1)S(1)}, f32[64,1152]{1,0:T(8,128)S(1)}, bf16[64,1152]{1,0:T(8,128)(2,1)S(1)}, b...) custom-call(s32[4]{0:T(128)S(1)} %pad_add_fusion.scalars, f32[2]{0:T(128)S(1)} %pad_maximum_fusion.factors, ...), custom_call_target="tpu_custom_call" | custom-call | flops 905969664 | bytes 4278296 | tf_op jit(solution)/shard_map/pallas_call | solution.py:20
  24.1 0.0 copy-start.1
  24.1 0.1 collective-permute-start.5
  24.2 2.0 %collective-permute-done.5.other = bf16[256,1152]{1,0:T(8,128)(2,1)S(1)} collective-permute-done((bf16[256,1152]{1,0:T(8,128)(2,1)S(1)}, bf16[256,1152]{1,0:T(8,128)(2,1)S(1)}, u32[]{:S(2)}, u32[]{:S(2)}) %collective-permute-start.5) | collective-permute-done | bytes 589856 | tf_op jit(solution)/shard_map/ppermute | solution.py:133
  26.2 0.1 shard_map.70
  26.3 0.0 copy-start.3
  26.3 1.5 %collective-permute-start.6 = (bf16[64,1152]{1,0:T(8,128)(2,1)S(1)}, bf16[64,1152]{1,0:T(8,128)(2,1)S(1)}, u32[]{:S(2)}, u32[]{:S(2)}) collective-permute-start(bf16[64,1152]{1,0:T(8,128)(2,1)S(1)} %get-tuple-element.19), channel_id=1, source_target_pairs={{0,8},{8,16},{16,24},{24,0},{1,9},{9,17},{17,25},{25,1},{2,10},{10... | collective-permute-start | bytes 442376 | tf_op jit(solution)/shard_map/ppermute | solution.py:128
  27.9 1.5 %collective-permute-start.7 = (bf16[64,1152]{1,0:T(8,128)(2,1)S(1)}, bf16[64,1152]{1,0:T(8,128)(2,1)S(1)}, u32[]{:S(2)}, u32[]{:S(2)}) collective-permute-start(bf16[64,1152]{1,0:T(8,128)(2,1)S(1)} %get-tuple-element.20), channel_id=1, source_target_pairs={{0,16},{8,24},{16,0},{24,8},{1,17},{9,25},{17,1},{25,9},{2,18},{10... | collective-permute-start | bytes 442376 | tf_op jit(solution)/shard_map/ppermute | solution.py:128
  29.4 1.4 %collective-permute-start.8 = (bf16[64,1152]{1,0:T(8,128)(2,1)S(1)}, bf16[64,1152]{1,0:T(8,128)(2,1)S(1)}, u32[]{:S(2)}, u32[]{:S(2)}) collective-permute-start(bf16[64,1152]{1,0:T(8,128)(2,1)S(1)} %get-tuple-element.21), channel_id=1, source_target_pairs={{0,24},{8,0},{16,8},{24,16},{1,25},{9,1},{17,9},{25,17},{2,26},{10... | collective-permute-start | bytes 442376 | tf_op jit(solution)/shard_map/ppermute | solution.py:128
  30.8 1.3 %collective-permute-start.12 = (bf16[64,1152]{1,0:T(8,128)(2,1)S(1)}, bf16[64,1152]{1,0:T(8,128)(2,1)S(1)}, u32[]{:S(2)}, u32[]{:S(2)}) collective-permute-start(bf16[64,1152]{1,0:T(8,128)(2,1)S(1)} %get-tuple-element.23), channel_id=1, source_target_pairs={{0,6},{1,7},{2,0},{3,1},{4,2},{5,3},{6,4},{7,5},{8,14},{9,15},{10,... | collective-permute-start | bytes 442376 | tf_op jit(solution)/shard_map/ppermute | solution.py:128
  32.1 1.5 %collective-permute-start.13 = (bf16[64,1152]{1,0:T(8,128)(2,1)S(1)}, bf16[64,1152]{1,0:T(8,128)(2,1)S(1)}, u32[]{:S(2)}, u32[]{:S(2)}) collective-permute-start(bf16[64,1152]{1,0:T(8,128)(2,1)S(1)} %get-tuple-element.24), channel_id=1, source_target_pairs={{0,4},{1,5},{2,6},{3,7},{4,0},{5,1},{6,2},{7,3},{8,12},{9,13},{10,... | collective-permute-start | bytes 442376 | tf_op jit(solution)/shard_map/ppermute | solution.py:128
  33.6 0.4 collective-permute-done.6.refs_0_
  34.0 1.6 %collective-permute-start.14 = (bf16[64,1152]{1,0:T(8,128)(2,1)S(1)}, bf16[64,1152]{1,0:T(8,128)(2,1)S(1)}, u32[]{:S(2)}, u32[]{:S(2)}) collective-permute-start(bf16[64,1152]{1,0:T(8,128)(2,1)S(1)} %get-tuple-element.25), channel_id=1, source_target_pairs={{0,2},{1,3},{2,4},{3,5},{4,6},{5,7},{6,0},{7,1},{8,10},{9,11},{10,... | collective-permute-start | bytes 442376 | tf_op jit(solution)/shard_map/ppermute | solution.py:128
  35.6 0.7 %collective-permute-done.7.refs_1_ = bf16[64,1152]{1,0:T(8,128)(2,1)S(1)} collective-permute-done((bf16[64,1152]{1,0:T(8,128)(2,1)S(1)}, bf16[64,1152]{1,0:T(8,128)(2,1)S(1)}, u32[]{:S(2)}, u32[]{:S(2)}) %collective-permute-start.7) | collective-permute-done | bytes 147488 | tf_op jit(solution)/shard_map/ppermute | solution.py:128
  36.3 0.1 collective-permute-done.8.refs_2_
  36.4 0.0 copy-done.1
  36.4 0.8 %shard_map.71.refs_0_ = bf16[64,1152]{1,0:T(8,128)(2,1)S(1)} custom-call(s32[1]{0:T(128)} %bitcast.position, f32[2]{0:T(128)S(1)} %pad_maximum_fusion.factors, f32[256,1152]{1,0:T(8,128)S(1)} %copy-done.1, f32[64,1152]{1,0:T(8,128)S(1)} %get-tuple-element.18.own, bf16[64,1152]{1,0:T(8,128)(2,1)S(1)} %collective-permute-done.6.refs_0_, ...), custom_call_target="tpu_custom_call" | custom-call | flops 737280 | bytes 2064396 | tf_op jit(solution)/shard_map/pallas_call | solution.py:20
  37.2 1.7 %collective-permute-start.11 = (bf16[64,1152]{1,0:T(8,128)(2,1)S(1)}, bf16[64,1152]{1,0:T(8,128)(2,1)S(1)}, u32[]{:S(2)}, u32[]{:S(2)}) collective-permute-start(bf16[64,1152]{1,0:T(8,128)(2,1)S(1)} %shard_map.71.refs_0_), channel_id=1, source_target_pairs={{0,24},{8,0},{16,8},{24,16},{1,25},{9,1},{17,9},{25,17},{2,26},{10... | collective-permute-start | bytes 442376 | tf_op jit(solution)/shard_map/ppermute | solution.py:128
  38.9 1.5 %collective-permute-start.10 = (bf16[64,1152]{1,0:T(8,128)(2,1)S(1)}, bf16[64,1152]{1,0:T(8,128)(2,1)S(1)}, u32[]{:S(2)}, u32[]{:S(2)}) collective-permute-start(bf16[64,1152]{1,0:T(8,128)(2,1)S(1)} %shard_map.71.refs_0_), channel_id=1, source_target_pairs={{0,16},{8,24},{16,0},{24,8},{1,17},{9,25},{17,1},{25,9},{2,18},{10... | collective-permute-start | bytes 442376 | tf_op jit(solution)/shard_map/ppermute | solution.py:128
  40.4 0.0 collective-permute-done.12.refs_0_
  40.4 0.3 collective-permute-start.9
  40.7 5.7 %collective-permute-done.13.refs_1_ = bf16[64,1152]{1,0:T(8,128)(2,1)S(1)} collective-permute-done((bf16[64,1152]{1,0:T(8,128)(2,1)S(1)}, bf16[64,1152]{1,0:T(8,128)(2,1)S(1)}, u32[]{:S(2)}, u32[]{:S(2)}) %collective-permute-start.13) | collective-permute-done | bytes 147488 | tf_op jit(solution)/shard_map/ppermute | solution.py:128
  46.4 0.0 collective-permute-done.14.refs_2_
  46.4 0.0 copy-done.3
  46.4 1.5 %shard_map.73 = f32[64,1152]{1,0:T(8,128)} custom-call(f32[2]{0:T(128)S(1)} %pad_maximum_fusion.factors, f32[64,1152]{1,0:T(8,128)S(1)} %copy-done.3, f32[64,1152]{1,0:T(8,128)S(1)} %get-tuple-element.22.own, bf16[64,1152]{1,0:T(8,128)(2,1)S(1)} %collective-permute-done.12.refs_0_, bf16[64,1152]{1,0:T(8,128)(2,1)S(1)} %collective-permute-done.13.refs_1_, ...), custom_call_target="tpu_custom_call" | custom-call | flops 737280 | bytes 1327112 | tf_op jit(solution)/shard_map/pallas_call | solution.py:20
  47.8 0.0 collective-permute-done.11.refs_3_
  47.8 0.0 collective-permute-done.10.refs_2_
  47.8 0.0 collective-permute-done.9.refs_1_
  47.8 1.1 %shard_map.72 = f32[256,1152]{1,0:T(8,128)} custom-call(s32[1]{0:T(128)} %bitcast.position, bf16[64,1152]{1,0:T(8,128)(2,1)S(1)} %shard_map.71.refs_0_, bf16[64,1152]{1,0:T(8,128)(2,1)S(1)} %collective-permute-done.9.refs_1_, bf16[64,1152]{1,0:T(8,128)(2,1)S(1)} %collective-permute-done.10.refs_2_, bf16[64,1152]{1,0:T(8,128)(2,1)S(1)} %collective-permute-done.11.refs_3_), custom_call_target="tpu_custom_call" | custom-call | flops 294912 | bytes 1769476 | tf_op jit(solution)/shard_map/pallas_call | solution.py:20
Async XLA Ops:
  0.6 1.3 %copy-start = (f32[256,1152]{1,0:T(8,128)S(1)}, f32[256,1152]{1,0:T(8,128)}, u32[]{:S(2)}) copy-start(f32[256,1152]{1,0:T(8,128)} %img_ref.3) | copy-start | bytes 3538948
  1.9 1.0 %copy-start.2 = (f32[64,1152]{1,0:T(8,128)S(1)}, f32[64,1152]{1,0:T(8,128)}, u32[]{:S(2)}) copy-start(f32[64,1152]{1,0:T(8,128)} %txt_ref.3) | copy-start | bytes 884740
  2.9 6.4 %copy-start.4 = (s32[256]{0:T(256)S(1)}, s32[256]{0:T(256)}, u32[]{:S(2)}) copy-start(s32[256]{0:T(256)} %param.7) | copy-start | bytes 3076
  3.1 18.3 %collective-permute-start.1 = (bf16[256,1152]{1,0:T(8,128)(2,1)S(1)}, bf16[256,1152]{1,0:T(8,128)(2,1)S(1)}, u32[]{:S(2)}, u32[]{:S(2)}) collective-permute-start(bf16[256,1152]{1,0:T(8,128)(2,1)S(1)} %get-tuple-element.14.img_own), channel_id=1, source_target_pairs={{0,1},{1,0},{2,3},{3,2},{4,5},{5,4},{6,7},{7,6},{8,9},{9,8},{10,11... | collective-permute-start | bytes 1769480 | tf_op jit(solution)/shard_map/ppermute | solution.py:133
  3.6 8.9 %collective-permute-start.4 = (bf16[64,1152]{1,0:T(8,128)(2,1)S(1)}, bf16[64,1152]{1,0:T(8,128)(2,1)S(1)}, u32[]{:S(2)}, u32[]{:S(2)}) collective-permute-start(bf16[64,1152]{1,0:T(8,128)(2,1)S(1)} %get-tuple-element.15.refs_0_), channel_id=1, source_target_pairs={{0,6},{1,7},{2,0},{3,1},{4,2},{5,3},{6,4},{7,5},{8,14},{9,15},{10,... | collective-permute-start | bytes 442376 | tf_op jit(solution)/shard_map/ppermute | solution.py:128
  8.2 13.1 %collective-permute-start.3 = (bf16[64,1152]{1,0:T(8,128)(2,1)S(1)}, bf16[64,1152]{1,0:T(8,128)(2,1)S(1)}, u32[]{:S(2)}, u32[]{:S(2)}) collective-permute-start(bf16[64,1152]{1,0:T(8,128)(2,1)S(1)} %get-tuple-element.15.refs_0_), channel_id=1, source_target_pairs={{0,4},{1,5},{2,6},{3,7},{4,0},{5,1},{6,2},{7,3},{8,12},{9,13},{10,... | collective-permute-start | bytes 442376 | tf_op jit(solution)/shard_map/ppermute | solution.py:128
  8.2 13.1 %collective-permute-start.2 = (bf16[64,1152]{1,0:T(8,128)(2,1)S(1)}, bf16[64,1152]{1,0:T(8,128)(2,1)S(1)}, u32[]{:S(2)}, u32[]{:S(2)}) collective-permute-start(bf16[64,1152]{1,0:T(8,128)(2,1)S(1)} %get-tuple-element.15.refs_0_), channel_id=1, source_target_pairs={{0,2},{1,3},{2,4},{3,5},{4,6},{5,7},{6,0},{7,1},{8,10},{9,11},{10,... | collective-permute-start | bytes 442376 | tf_op jit(solution)/shard_map/ppermute | solution.py:128
  9.3 1.5 %collective-permute-start = (s32[1,256]{1,0:T(1,128)S(1)}, s32[1,256]{1,0:T(1,128)S(1)}, u32[]{:S(2)}, u32[]{:S(2)}) collective-permute-start(s32[1,256]{1,0:T(1,128)S(1)} %bitcast.6), channel_id=1, source_target_pairs={{0,1},{1,0},{2,3},{3,2},{4,5},{5,4},{6,7},{7,6},{8,9},{9,8},{10,11... | collective-permute-start | bytes 3080 | tf_op jit(solution)/shard_map/ppermute | solution.py:133
  24.1 12.3 %copy-start.1 = (f32[256,1152]{1,0:T(8,128)S(1)}, f32[256,1152]{1,0:T(8,128)}, u32[]{:S(2)}) copy-start(f32[256,1152]{1,0:T(8,128)} %img_ref.3) | copy-start | bytes 3538948
  24.1 2.1 %collective-permute-start.5 = (bf16[256,1152]{1,0:T(8,128)(2,1)S(1)}, bf16[256,1152]{1,0:T(8,128)(2,1)S(1)}, u32[]{:S(2)}, u32[]{:S(2)}) collective-permute-start(bf16[256,1152]{1,0:T(8,128)(2,1)S(1)} %get-tuple-element.17), channel_id=1, source_target_pairs={{0,1},{1,0},{2,3},{3,2},{4,5},{5,4},{6,7},{7,6},{8,9},{9,8},{10,11... | collective-permute-start | bytes 1769480 | tf_op jit(solution)/shard_map/ppermute | solution.py:133
  26.3 20.1 %copy-start.3 = (f32[64,1152]{1,0:T(8,128)S(1)}, f32[64,1152]{1,0:T(8,128)}, u32[]{:S(2)}) copy-start(f32[64,1152]{1,0:T(8,128)} %txt_ref.3) | copy-start | bytes 884740
  26.3 7.7 %collective-permute-start.6 = (bf16[64,1152]{1,0:T(8,128)(2,1)S(1)}, bf16[64,1152]{1,0:T(8,128)(2,1)S(1)}, u32[]{:S(2)}, u32[]{:S(2)}) collective-permute-start(bf16[64,1152]{1,0:T(8,128)(2,1)S(1)} %get-tuple-element.19), channel_id=1, source_target_pairs={{0,8},{8,16},{16,24},{24,0},{1,9},{9,17},{17,25},{25,1},{2,10},{10... | collective-permute-start | bytes 442376 | tf_op jit(solution)/shard_map/ppermute | solution.py:128
  27.9 8.5 %collective-permute-start.7 = (bf16[64,1152]{1,0:T(8,128)(2,1)S(1)}, bf16[64,1152]{1,0:T(8,128)(2,1)S(1)}, u32[]{:S(2)}, u32[]{:S(2)}) collective-permute-start(bf16[64,1152]{1,0:T(8,128)(2,1)S(1)} %get-tuple-element.20), channel_id=1, source_target_pairs={{0,16},{8,24},{16,0},{24,8},{1,17},{9,25},{17,1},{25,9},{2,18},{10... | collective-permute-start | bytes 442376 | tf_op jit(solution)/shard_map/ppermute | solution.py:128
  29.4 7.0 %collective-permute-start.8 = (bf16[64,1152]{1,0:T(8,128)(2,1)S(1)}, bf16[64,1152]{1,0:T(8,128)(2,1)S(1)}, u32[]{:S(2)}, u32[]{:S(2)}) collective-permute-start(bf16[64,1152]{1,0:T(8,128)(2,1)S(1)} %get-tuple-element.21), channel_id=1, source_target_pairs={{0,24},{8,0},{16,8},{24,16},{1,25},{9,1},{17,9},{25,17},{2,26},{10... | collective-permute-start | bytes 442376 | tf_op jit(solution)/shard_map/ppermute | solution.py:128
  30.8 9.6 %collective-permute-start.12 = (bf16[64,1152]{1,0:T(8,128)(2,1)S(1)}, bf16[64,1152]{1,0:T(8,128)(2,1)S(1)}, u32[]{:S(2)}, u32[]{:S(2)}) collective-permute-start(bf16[64,1152]{1,0:T(8,128)(2,1)S(1)} %get-tuple-element.23), channel_id=1, source_target_pairs={{0,6},{1,7},{2,0},{3,1},{4,2},{5,3},{6,4},{7,5},{8,14},{9,15},{10,... | collective-permute-start | bytes 442376 | tf_op jit(solution)/shard_map/ppermute | solution.py:128
  32.1 14.3 %collective-permute-start.13 = (bf16[64,1152]{1,0:T(8,128)(2,1)S(1)}, bf16[64,1152]{1,0:T(8,128)(2,1)S(1)}, u32[]{:S(2)}, u32[]{:S(2)}) collective-permute-start(bf16[64,1152]{1,0:T(8,128)(2,1)S(1)} %get-tuple-element.24), channel_id=1, source_target_pairs={{0,4},{1,5},{2,6},{3,7},{4,0},{5,1},{6,2},{7,3},{8,12},{9,13},{10,... | collective-permute-start | bytes 442376 | tf_op jit(solution)/shard_map/ppermute | solution.py:128
  34.0 12.4 %collective-permute-start.14 = (bf16[64,1152]{1,0:T(8,128)(2,1)S(1)}, bf16[64,1152]{1,0:T(8,128)(2,1)S(1)}, u32[]{:S(2)}, u32[]{:S(2)}) collective-permute-start(bf16[64,1152]{1,0:T(8,128)(2,1)S(1)} %get-tuple-element.25), channel_id=1, source_target_pairs={{0,2},{1,3},{2,4},{3,5},{4,6},{5,7},{6,0},{7,1},{8,10},{9,11},{10,... | collective-permute-start | bytes 442376 | tf_op jit(solution)/shard_map/ppermute | solution.py:128
  37.2 10.6 %collective-permute-start.11 = (bf16[64,1152]{1,0:T(8,128)(2,1)S(1)}, bf16[64,1152]{1,0:T(8,128)(2,1)S(1)}, u32[]{:S(2)}, u32[]{:S(2)}) collective-permute-start(bf16[64,1152]{1,0:T(8,128)(2,1)S(1)} %shard_map.71.refs_0_), channel_id=1, source_target_pairs={{0,24},{8,0},{16,8},{24,16},{1,25},{9,1},{17,9},{25,17},{2,26},{10... | collective-permute-start | bytes 442376 | tf_op jit(solution)/shard_map/ppermute | solution.py:128
  38.9 8.9 %collective-permute-start.10 = (bf16[64,1152]{1,0:T(8,128)(2,1)S(1)}, bf16[64,1152]{1,0:T(8,128)(2,1)S(1)}, u32[]{:S(2)}, u32[]{:S(2)}) collective-permute-start(bf16[64,1152]{1,0:T(8,128)(2,1)S(1)} %shard_map.71.refs_0_), channel_id=1, source_target_pairs={{0,16},{8,24},{16,0},{24,8},{1,17},{9,25},{17,1},{25,9},{2,18},{10... | collective-permute-start | bytes 442376 | tf_op jit(solution)/shard_map/ppermute | solution.py:128
  40.4 7.4 %collective-permute-start.9 = (bf16[64,1152]{1,0:T(8,128)(2,1)S(1)}, bf16[64,1152]{1,0:T(8,128)(2,1)S(1)}, u32[]{:S(2)}, u32[]{:S(2)}) collective-permute-start(bf16[64,1152]{1,0:T(8,128)(2,1)S(1)} %shard_map.71.refs_0_), channel_id=1, source_target_pairs={{0,8},{8,16},{16,24},{24,0},{1,9},{9,17},{17,25},{25,1},{2,10},{10... | collective-permute-start | bytes 442376 | tf_op jit(solution)/shard_map/ppermute | solution.py:128

commit v2 on v1

--- a/solution.py
+++ b/solution.py
@@ -12,6 +12,20 @@
 BF16 = jnp.bfloat16
 VMEM = pl.BlockSpec(memory_space=pltpu.VMEM)
 SMEM = pl.BlockSpec(memory_space=pltpu.SMEM)
+
+
+def unit_rows(texts, images):
+    sizes = [texts.shape, images.shape]
+    total = texts.size + images.size
+    return pl.pallas_call(
+        unit_body,
+        out_shape=[struct(*size, BF16) for size in sizes],
+        in_specs=[pl.BlockSpec(memory_space=pltpu.HBM)] * 2,
+        out_specs=[VMEM] * 2,
+        scratch_shapes=[pltpu.VMEM(size, F32) for size in sizes] + [pltpu.SemaphoreType.DMA((2,))],
+        compiler_params=pltpu.CompilerParams(vmem_limit_bytes=16 << 20),
+        cost_estimate=pl.CostEstimate(flops=4 * total, bytes_accessed=6 * total, transcendentals=0),
+    )(*[pltpu.with_memory_space_constraint(v, pltpu.HBM) for v in (texts, images)])
 
 
 def call(body, outs, args, specs, limit, flops):
@@ -41,43 +55,49 @@
     return inverse * (upstream - unit * jnp.sum(unit * upstream, axis=1, keepdims=True))
 
 
-def unit_body(img_ref, txt_ref, img_out, txt_out):
-    txt = txt_ref[...]
-    txt_out[...] = (txt * inverse_norm(txt)).astype(BF16)
-    img = img_ref[...]
-    img_out[...] = (img * inverse_norm(img)).astype(BF16)
-
-
-def pair_body(blocks, scalars, factors, perm_own, perm_other, img_own, img_other, *refs):
+def unit_body(txt, img, txt_out, img_out, txt_held, img_held, sems):
+    txt_copy = pltpu.make_async_copy(txt, txt_held, sems.at[0])
+    img_copy = pltpu.make_async_copy(img, img_held, sems.at[1])
+    txt_copy.start()
+    img_copy.start()
+    txt_copy.wait()
+    values = txt_held[...]
+    txt_out[...] = (values * inverse_norm(values)).astype(BF16)
+    img_copy.wait()
+    values = img_held[...]
+    img_out[...] = (values * inverse_norm(values)).astype(BF16)
+
+
+def weights_of(tile, scalars, factors, perm, img):
+    rows = tile.shape[0] // scalars.shape[0]
+    row = lax.broadcasted_iota(jnp.int32, (rows, 1), 0)
+    ids = jnp.concatenate([row + scalars[k] for k in range(scalars.shape[0])], axis=0)
+    products = lax.dot_general(tile, img, (((1,), (1,)), ((), ())), preferred_element_type=F32)
+    positive = (ids == perm).astype(F32)
+    return (jax.nn.sigmoid(factors[0] * products + factors[1]) - positive).astype(BF16)
+
+
+def to_images(weights, tile):
+    return lax.dot_general(weights, tile, (((0,), (0,)), ((), ())), preferred_element_type=F32)
+
+
+def other_body(blocks, scalars, factors, perm, img, *refs):
+    *txt, kept, out = refs
+    tile = jnp.concatenate([t[...] for t in txt], axis=0)
+    weights = weights_of(tile, scalars, factors, perm[...], img[...])
+    kept[...] = weights
+    out[...] = to_images(weights, tile).astype(BF16)
+
+
+def own_body(blocks, scalars, factors, perm, img_own, img_other, kept, *refs):
     txt = refs[:blocks]
-    own_img, other_img, own_txt = refs[blocks : blocks + 3]
-    other_txt = refs[blocks + 3 :]
-    factor = factors[0]
-    offset = factors[1]
-    rows = txt[0].shape[0]
+    own_img, own_txt, *other_txt = refs[blocks:]
+    rows = own_txt.shape[0]
     tile = jnp.concatenate([t[...] for t in txt], axis=0)
-    row = lax.broadcasted_iota(jnp.int32, (rows, 1), 0)
-    ids = jnp.concatenate([row + scalars[k] for k in range(blocks)], axis=0)
-
-    def weights(img, perm):
-        logits = (
-            factor
-            * lax.dot_general(tile, img[...], (((1,), (1,)), ((), ())), preferred_element_type=F32)
-            + offset
-        )
-        positive = (ids == perm[...]).astype(F32)
-        return (jax.nn.sigmoid(logits) - positive).astype(BF16)
-
-    w_other = weights(img_other, perm_other)
-    other_img[...] = lax.dot_general(
-        w_other, tile, (((0,), (0,)), ((), ())), preferred_element_type=F32
-    ).astype(BF16)
-    w_own = weights(img_own, perm_own)
-    own_img[...] = lax.dot_general(
-        w_own, tile, (((0,), (0,)), ((), ())), preferred_element_type=F32
-    )
-    to_txt = jnp.dot(w_own, img_own[...], preferred_element_type=F32) + jnp.dot(
-        w_other, img_other[...], preferred_element_type=F32
+    weights = weights_of(tile, scalars, factors, perm[...], img_own[...])
+    own_img[...] = to_images(weights, tile)
+    to_txt = jnp.dot(weights, img_own[...], preferred_element_type=F32) + jnp.dot(
+        kept[...], img_other[...], preferred_element_type=F32
     )
     own_txt[...] = to_txt[:rows]
     for k in range(1, blocks):
@@ -146,30 +166,32 @@
     factors = jnp.concatenate([scale, shift])
     perm_row = perm.reshape(1, rows)
 
-    img_bf, txt_bf = call(
-        unit_body,
-        [struct(rows, width, BF16), struct(txt_rows, width, BF16)],
-        [images, texts],
-        [VMEM] * 2,
-        16 << 20,
-        4 * rows * width,
-    )
+    txt_bf, img_bf = unit_rows(texts, images)
     tiles = [txt_bf] + [shifted(txt_bf, "txt", 2 * k) for k in range(1, blocks)]
+    perm_other = swapped(perm_row)
     img_other = swapped(img_bf)
-    perm_other = swapped(perm_row)
     firsts = jnp.stack(
         [(place * line + (column - 2 * k) % line) * txt_rows for k in range(blocks)]
     ).astype(jnp.int32)
-    own_img, other_img, own_txt, *other_txt = call(
-        functools.partial(pair_body, blocks),
-        [struct(rows, width, F32), struct(rows, width, BF16), struct(txt_rows, width, F32)]
+    pairs = 2 * rows * blocks * txt_rows * width
+    kept, other_img = call(
+        functools.partial(other_body, blocks),
+        [struct(blocks * txt_rows, rows, BF16), struct(rows, width, BF16)],
+        [firsts, factors, perm_other, img_other, *tiles],
+        [SMEM] * 2 + [VMEM] * (2 + blocks),
+        40 << 20,
+        2 * pairs,
+    )
+    from_other = swapped(other_img)
+    own_img, own_txt, *other_txt = call(
+        functools.partial(own_body, blocks),
+        [struct(rows, width, F32), struct(txt_rows, width, F32)]
         + [struct(txt_rows, width, BF16)] * (blocks - 1),
-        [firsts, factors, perm_row, perm_other, img_bf, img_other, *tiles],
+        [firsts, factors, perm_row, img_bf, img_other, kept, *tiles],
         [SMEM] * 2 + [VMEM] * (4 + blocks),
-        48 << 20,
-        12 * rows * blocks * txt_rows * width,
-    )
-    from_other = swapped(other_img)
+        40 << 20,
+        4 * pairs,
+    )
     back = [shifted(other_txt[k - 1], "txt", -2 * k) for k in range(1, blocks)]
 
     keep, *send = call(

time: 49.5 us -> 47.5 us (0.960)
  local copies, waits for them, and re-layouts: 2.24 us -> 0.02 us
  Pallas kernels: 6.36 us -> 8.53 us
  waiting for transfers between devices: 19.6 us -> 17.9 us
    unnamed x10 -> x6, local copies, waits for them, and re-layouts: 2.24 us -> 0.02 us
    ppermute x3, waiting for transfers between devices: 2 us -> 0.04 us  [swapped(): return lax.ppermute(value, 'txt', [(s, s ^ 1) for s in range(count)])]
    pallas_call x0 -> x1, Pallas kernels: none -> 1.56 us  [unit_rows(): pl.pallas_call(unit_body, out_shape=[struct(*size, BF16) for size in size...]
    pallas_call x6, Pallas kernels: 6.36 us -> 6.97 us  [call(): pl.pallas_call(body, out_shape=outs, in_specs=specs, out_specs=[VMEM] * l...]
  transfers between devices with their start and end apart: 15 -> 15, of which waited for: 7 -> 6; matrix products, arithmetic and copies ran while one was open for 0% -> 0% of each run, Pallas kernels for 5% -> 9%
where the time goes in v2:
time: 47.5 us; the launch traced here: 47.3 us
  starting transfers between devices  18.7 us (39%)
  waiting for transfers between devices  17.9 us (38%)
  Pallas kernels  8.53 us (18%)
  between operations  2.01 us (4%)
    ppermute x12, starting transfers between devices, shifted(): lax.ppermute(value, axis, [(s, (s + steps) % count) for s in range(count)])  18.1 us
    ppermute x12, waiting for transfers between devices, shifted(): lax.ppermute(value, axis, [(s, (s + steps) % count) for s in range(count)])  17.9 us
    pallas_call x6, Pallas kernels, call(): pl.pallas_call(body, out_shape=outs, in_specs=specs, out_specs=[VMEM] * l...  6.97 us
    pallas_call x1, Pallas kernels, unit_rows(): pl.pallas_call(unit_body, out_shape=[struct(*size, BF16) for size in size...  1.56 us
  transfers between devices with their start and end apart: 15, of which 6 were waited for; matrix products, arithmetic and copies ran while one was open for 0% of the time, Pallas kernels for 9%

profile of v2, /device:TPU:0, one launch (start us, length us, event | category | flops | bytes accessed | tf_op | source)
XLA Modules:
  0.0 47.3 jit_solution(14625321479259068292)
XLA Ops:
  0.6 0.0 copy-start.2
  0.6 1.6 %shard_map.68 = (bf16[64,1152]{1,0:T(8,128)(2,1)S(1)}, bf16[256,1152]{1,0:T(8,128)(2,1)S(1)}) custom-call(f32[64,1152]{1,0:T(8,128)} %txt_ref.1, f32[256,1152]{1,0:T(8,128)} %img_ref.1), custom_call_target="tpu_custom_call" | custom-call | flops 1474560 | bytes 2211840 | tf_op jit(solution)/shard_map/pallas_call | solution.py:20
  2.2 0.5 %collective-permute-start = (bf16[256,1152]{1,0:T(8,128)(2,1)S(1)}, bf16[256,1152]{1,0:T(8,128)(2,1)S(1)}, u32[]{:S(2)}, u32[]{:S(2)}) collective-permute-start(bf16[256,1152]{1,0:T(8,128)(2,1)S(1)} %get-tuple-element.15.img_own), channel_id=1, source_target_pairs={{0,1},{1,0},{2,3},{3,2},{4,5},{5,4},{6,7},{7,6},{8,9},{9,8},{10,11... | collective-permute-start | bytes 1769480 | tf_op jit(solution)/shard_map/ppermute | solution.py:153
  2.7 4.7 %collective-permute-start.4 = (bf16[64,1152]{1,0:T(8,128)(2,1)S(1)}, bf16[64,1152]{1,0:T(8,128)(2,1)S(1)}, u32[]{:S(2)}, u32[]{:S(2)}) collective-permute-start(bf16[64,1152]{1,0:T(8,128)(2,1)S(1)} %get-tuple-element.16.refs_0_), channel_id=1, source_target_pairs={{0,6},{1,7},{2,0},{3,1},{4,2},{5,3},{6,4},{7,5},{8,14},{9,15},{10,... | collective-permute-start | bytes 442376 | tf_op jit(solution)/shard_map/ppermute | solution.py:148
  7.4 0.0 collective-permute-start.3
  7.4 1.0 %collective-permute-start.2 = (bf16[64,1152]{1,0:T(8,128)(2,1)S(1)}, bf16[64,1152]{1,0:T(8,128)(2,1)S(1)}, u32[]{:S(2)}, u32[]{:S(2)}) collective-permute-start(bf16[64,1152]{1,0:T(8,128)(2,1)S(1)} %get-tuple-element.16.refs_0_), channel_id=1, source_target_pairs={{0,2},{1,3},{2,4},{3,5},{4,6},{5,7},{6,0},{7,1},{8,10},{9,11},{10,... | collective-permute-start | bytes 442376 | tf_op jit(solution)/shard_map/ppermute | solution.py:148
  8.4 0.0 copy-done.2
  8.4 0.0 collective-permute-start.1
  9.7 0.1 pad_maximum_fusion.factors
  9.8 0.1 pad_add_fusion.scalars
  9.9 0.0 collective-permute-done.1.perm
  9.9 1.8 %collective-permute-done.4.refs_3_ = bf16[64,1152]{1,0:T(8,128)(2,1)S(1)} collective-permute-done((bf16[64,1152]{1,0:T(8,128)(2,1)S(1)}, bf16[64,1152]{1,0:T(8,128)(2,1)S(1)}, u32[]{:S(2)}, u32[]{:S(2)}) %collective-permute-start.4) | collective-permute-done | bytes 147488 | tf_op jit(solution)/shard_map/ppermute | solution.py:148
  11.6 8.9 %collective-permute-done.3.refs_2_ = bf16[64,1152]{1,0:T(8,128)(2,1)S(1)} collective-permute-done((bf16[64,1152]{1,0:T(8,128)(2,1)S(1)}, bf16[64,1152]{1,0:T(8,128)(2,1)S(1)}, u32[]{:S(2)}, u32[]{:S(2)}) %collective-permute-start.3) | collective-permute-done | bytes 147488 | tf_op jit(solution)/shard_map/ppermute | solution.py:148
  20.5 0.0 collective-permute-done.2.refs_1_
  20.5 0.0 collective-permute-done.img.img_other
  20.5 1.6 %shard_map.69 = (bf16[256,256]{1,0:T(8,128)(2,1)S(1)}, bf16[256,1152]{1,0:T(8,128)(2,1)S(1)}) custom-call(s32[4]{0:T(128)S(1)} %pad_add_fusion.scalars, f32[2]{0:T(128)S(1)} %pad_maximum_fusion.factors, s32[1,256]{1,0:T(1,128)S(1)} %collective-permute-done.1.perm, bf16[256,1152]{1,0:T(8,128)(2,1)S(1)} %collective-permute-done.img.img_other, ...), custom_call_target="tpu_custom_call" | custom-call | flops 301989888 | bytes 1901592 | tf_op jit(solution)/shard_map/pallas_call | solution.py:34
  22.1 0.1 collective-permute-start.5
  22.2 1.9 %shard_map.70 = (f32[256,1152]{1,0:T(8,128)S(1)}, f32[64,1152]{1,0:T(8,128)S(1)}, bf16[64,1152]{1,0:T(8,128)(2,1)S(1)}, bf16[64,1152]{1,0:T(8,128)(2,1)S(1)}, bf16[64,1152]{1,0:T(8,128)(2,1)S(1)}) custom-call(s32[4]{0:T(128)S(1)} %pad_add_fusion.scalars, f32[2]{0:T(128)S(1)} %pad_maximum_fusion.factors, s32[1,256]{1,0:T(1,128)S(1)} %bitcast.7, ...), custom_call_target="tpu_custom_call" | custom-call | flops 603979776 | bytes 3818520 | tf_op jit(solution)/shard_map/pallas_call | solution.py:34
  24.1 0.0 copy-start
  24.1 0.0 collective-permute-done.5.other
  24.2 0.1 shard_map.71
  24.3 0.0 copy-start.1
  24.3 1.5 %collective-permute-start.6 = (bf16[64,1152]{1,0:T(8,128)(2,1)S(1)}, bf16[64,1152]{1,0:T(8,128)(2,1)S(1)}, u32[]{:S(2)}, u32[]{:S(2)}) collective-permute-start(bf16[64,1152]{1,0:T(8,128)(2,1)S(1)} %get-tuple-element.21), channel_id=1, source_target_pairs={{0,8},{8,16},{16,24},{24,0},{1,9},{9,17},{17,25},{25,1},{2,10},{10... | collective-permute-start | bytes 442376 | tf_op jit(solution)/shard_map/ppermute | solution.py:148
  25.9 1.5 %collective-permute-start.7 = (bf16[64,1152]{1,0:T(8,128)(2,1)S(1)}, bf16[64,1152]{1,0:T(8,128)(2,1)S(1)}, u32[]{:S(2)}, u32[]{:S(2)}) collective-permute-start(bf16[64,1152]{1,0:T(8,128)(2,1)S(1)} %get-tuple-element.22), channel_id=1, source_target_pairs={{0,16},{8,24},{16,0},{24,8},{1,17},{9,25},{17,1},{25,9},{2,18},{10... | collective-permute-start | bytes 442376 | tf_op jit(solution)/shard_map/ppermute | solution.py:148
  27.4 1.4 %collective-permute-start.8 = (bf16[64,1152]{1,0:T(8,128)(2,1)S(1)}, bf16[64,1152]{1,0:T(8,128)(2,1)S(1)}, u32[]{:S(2)}, u32[]{:S(2)}) collective-permute-start(bf16[64,1152]{1,0:T(8,128)(2,1)S(1)} %get-tuple-element.23), channel_id=1, source_target_pairs={{0,24},{8,0},{16,8},{24,16},{1,25},{9,1},{17,9},{25,17},{2,26},{10... | collective-permute-start | bytes 442376 | tf_op jit(solution)/shard_map/ppermute | solution.py:148
  28.8 1.3 %collective-permute-start.12 = (bf16[64,1152]{1,0:T(8,128)(2,1)S(1)}, bf16[64,1152]{1,0:T(8,128)(2,1)S(1)}, u32[]{:S(2)}, u32[]{:S(2)}) collective-permute-start(bf16[64,1152]{1,0:T(8,128)(2,1)S(1)} %get-tuple-element.25), channel_id=1, source_target_pairs={{0,6},{1,7},{2,0},{3,1},{4,2},{5,3},{6,4},{7,5},{8,14},{9,15},{10,... | collective-permute-start | bytes 442376 | tf_op jit(solution)/shard_map/ppermute | solution.py:148
  30.1 1.5 %collective-permute-start.13 = (bf16[64,1152]{1,0:T(8,128)(2,1)S(1)}, bf16[64,1152]{1,0:T(8,128)(2,1)S(1)}, u32[]{:S(2)}, u32[]{:S(2)}) collective-permute-start(bf16[64,1152]{1,0:T(8,128)(2,1)S(1)} %get-tuple-element.26), channel_id=1, source_target_pairs={{0,4},{1,5},{2,6},{3,7},{4,0},{5,1},{6,2},{7,3},{8,12},{9,13},{10,... | collective-permute-start | bytes 442376 | tf_op jit(solution)/shard_map/ppermute | solution.py:148
  31.6 0.4 collective-permute-done.6.refs_0_
  32.0 1.6 %collective-permute-start.14 = (bf16[64,1152]{1,0:T(8,128)(2,1)S(1)}, bf16[64,1152]{1,0:T(8,128)(2,1)S(1)}, u32[]{:S(2)}, u32[]{:S(2)}) collective-permute-start(bf16[64,1152]{1,0:T(8,128)(2,1)S(1)} %get-tuple-element.27), channel_id=1, source_target_pairs={{0,2},{1,3},{2,4},{3,5},{4,6},{5,7},{6,0},{7,1},{8,10},{9,11},{10,... | collective-permute-start | bytes 442376 | tf_op jit(solution)/shard_map/ppermute | solution.py:148
  33.6 1.1 %collective-permute-done.7.refs_1_ = bf16[64,1152]{1,0:T(8,128)(2,1)S(1)} collective-permute-done((bf16[64,1152]{1,0:T(8,128)(2,1)S(1)}, bf16[64,1152]{1,0:T(8,128)(2,1)S(1)}, u32[]{:S(2)}, u32[]{:S(2)}) %collective-permute-start.7) | collective-permute-done | bytes 147488 | tf_op jit(solution)/shard_map/ppermute | solution.py:148
  34.7 0.1 collective-permute-done.8.refs_2_
  34.8 0.0 copy-done
  34.8 0.8 %shard_map.72.refs_0_ = bf16[64,1152]{1,0:T(8,128)(2,1)S(1)} custom-call(s32[1]{0:T(128)} %bitcast.position, f32[2]{0:T(128)S(1)} %pad_maximum_fusion.factors, f32[256,1152]{1,0:T(8,128)S(1)} %copy-done, f32[64,1152]{1,0:T(8,128)S(1)} %get-tuple-element.20.own, bf16[64,1152]{1,0:T(8,128)(2,1)S(1)} %collective-permute-done.6.refs_0_, ...), custom_call_target="tpu_custom_call" | custom-call | flops 737280 | bytes 2064396 | tf_op jit(solution)/shard_map/pallas_call | solution.py:34
  35.5 1.7 %collective-permute-start.11 = (bf16[64,1152]{1,0:T(8,128)(2,1)S(1)}, bf16[64,1152]{1,0:T(8,128)(2,1)S(1)}, u32[]{:S(2)}, u32[]{:S(2)}) collective-permute-start(bf16[64,1152]{1,0:T(8,128)(2,1)S(1)} %shard_map.72.refs_0_), channel_id=1, source_target_pairs={{0,24},{8,0},{16,8},{24,16},{1,25},{9,1},{17,9},{25,17},{2,26},{10... | collective-permute-start | bytes 442376 | tf_op jit(solution)/shard_map/ppermute | solution.py:148
  37.2 1.5 %collective-permute-start.10 = (bf16[64,1152]{1,0:T(8,128)(2,1)S(1)}, bf16[64,1152]{1,0:T(8,128)(2,1)S(1)}, u32[]{:S(2)}, u32[]{:S(2)}) collective-permute-start(bf16[64,1152]{1,0:T(8,128)(2,1)S(1)} %shard_map.72.refs_0_), channel_id=1, source_target_pairs={{0,16},{8,24},{16,0},{24,8},{1,17},{9,25},{17,1},{25,9},{2,18},{10... | collective-permute-start | bytes 442376 | tf_op jit(solution)/shard_map/ppermute | solution.py:148
  38.8 0.0 collective-permute-done.12.refs_0_
  38.8 0.3 collective-permute-start.9
  39.0 5.7 %collective-permute-done.13.refs_1_ = bf16[64,1152]{1,0:T(8,128)(2,1)S(1)} collective-permute-done((bf16[64,1152]{1,0:T(8,128)(2,1)S(1)}, bf16[64,1152]{1,0:T(8,128)(2,1)S(1)}, u32[]{:S(2)}, u32[]{:S(2)}) %collective-permute-start.13) | collective-permute-done | bytes 147488 | tf_op jit(solution)/shard_map/ppermute | solution.py:148
  44.7 0.0 collective-permute-done.14.refs_2_
  44.7 0.0 copy-done.1
  44.7 1.5 %shard_map.74 = f32[64,1152]{1,0:T(8,128)} custom-call(f32[2]{0:T(128)S(1)} %pad_maximum_fusion.factors, f32[64,1152]{1,0:T(8,128)S(1)} %copy-done.1, f32[64,1152]{1,0:T(8,128)S(1)} %get-tuple-element.24.own, bf16[64,1152]{1,0:T(8,128)(2,1)S(1)} %collective-permute-done.12.refs_0_, bf16[64,1152]{1,0:T(8,128)(2,1)S(1)} %collective-permute-done.13.refs_1_, ...), custom_call_target="tpu_custom_call" | custom-call | flops 737280 | bytes 1327112 | tf_op jit(solution)/shard_map/pallas_call | solution.py:34
  46.2 0.0 collective-permute-done.11.refs_3_
  46.2 0.0 collective-permute-done.10.refs_2_
  46.2 0.0 collective-permute-done.9.refs_1_
  46.2 1.1 %shard_map.73 = f32[256,1152]{1,0:T(8,128)} custom-call(s32[1]{0:T(128)} %bitcast.position, bf16[64,1152]{1,0:T(8,128)(2,1)S(1)} %shard_map.72.refs_0_, bf16[64,1152]{1,0:T(8,128)(2,1)S(1)} %collective-permute-done.9.refs_1_, bf16[64,1152]{1,0:T(8,128)(2,1)S(1)} %collective-permute-done.10.refs_2_, bf16[64,1152]{1,0:T(8,128)(2,1)S(1)} %collective-permute-done.11.refs_3_), custom_call_target="tpu_custom_call" | custom-call | flops 294912 | bytes 1769476 | tf_op jit(solution)/shard_map/pallas_call | solution.py:34
Async XLA Ops:
  0.6 7.8 %copy-start.2 = (s32[256]{0:T(256)S(1)}, s32[256]{0:T(256)}, u32[]{:S(2)}) copy-start(s32[256]{0:T(256)} %param.7) | copy-start | bytes 3076
  2.2 18.3 %collective-permute-start = (bf16[256,1152]{1,0:T(8,128)(2,1)S(1)}, bf16[256,1152]{1,0:T(8,128)(2,1)S(1)}, u32[]{:S(2)}, u32[]{:S(2)}) collective-permute-start(bf16[256,1152]{1,0:T(8,128)(2,1)S(1)} %get-tuple-element.15.img_own), channel_id=1, source_target_pairs={{0,1},{1,0},{2,3},{3,2},{4,5},{5,4},{6,7},{7,6},{8,9},{9,8},{10,11... | collective-permute-start | bytes 1769480 | tf_op jit(solution)/shard_map/ppermute | solution.py:153
  2.7 8.9 %collective-permute-start.4 = (bf16[64,1152]{1,0:T(8,128)(2,1)S(1)}, bf16[64,1152]{1,0:T(8,128)(2,1)S(1)}, u32[]{:S(2)}, u32[]{:S(2)}) collective-permute-start(bf16[64,1152]{1,0:T(8,128)(2,1)S(1)} %get-tuple-element.16.refs_0_), channel_id=1, source_target_pairs={{0,6},{1,7},{2,0},{3,1},{4,2},{5,3},{6,4},{7,5},{8,14},{9,15},{10,... | collective-permute-start | bytes 442376 | tf_op jit(solution)/shard_map/ppermute | solution.py:148
  7.4 13.1 %collective-permute-start.3 = (bf16[64,1152]{1,0:T(8,128)(2,1)S(1)}, bf16[64,1152]{1,0:T(8,128)(2,1)S(1)}, u32[]{:S(2)}, u32[]{:S(2)}) collective-permute-start(bf16[64,1152]{1,0:T(8,128)(2,1)S(1)} %get-tuple-element.16.refs_0_), channel_id=1, source_target_pairs={{0,4},{1,5},{2,6},{3,7},{4,0},{5,1},{6,2},{7,3},{8,12},{9,13},{10,... | collective-permute-start | bytes 442376 | tf_op jit(solution)/shard_map/ppermute | solution.py:148
  7.4 13.1 %collective-permute-start.2 = (bf16[64,1152]{1,0:T(8,128)(2,1)S(1)}, bf16[64,1152]{1,0:T(8,128)(2,1)S(1)}, u32[]{:S(2)}, u32[]{:S(2)}) collective-permute-start(bf16[64,1152]{1,0:T(8,128)(2,1)S(1)} %get-tuple-element.16.refs_0_), channel_id=1, source_target_pairs={{0,2},{1,3},{2,4},{3,5},{4,6},{5,7},{6,0},{7,1},{8,10},{9,11},{10,... | collective-permute-start | bytes 442376 | tf_op jit(solution)/shard_map/ppermute | solution.py:148
  8.4 1.5 %collective-permute-start.1 = (s32[1,256]{1,0:T(1,128)S(1)}, s32[1,256]{1,0:T(1,128)S(1)}, u32[]{:S(2)}, u32[]{:S(2)}) collective-permute-start(s32[1,256]{1,0:T(1,128)S(1)} %bitcast.6), channel_id=1, source_target_pairs={{0,1},{1,0},{2,3},{3,2},{4,5},{5,4},{6,7},{7,6},{8,9},{9,8},{10,11... | collective-permute-start | bytes 3080 | tf_op jit(solution)/shard_map/ppermute | solution.py:153
  22.1 2.1 %collective-permute-start.5 = (bf16[256,1152]{1,0:T(8,128)(2,1)S(1)}, bf16[256,1152]{1,0:T(8,128)(2,1)S(1)}, u32[]{:S(2)}, u32[]{:S(2)}) collective-permute-start(bf16[256,1152]{1,0:T(8,128)(2,1)S(1)} %get-tuple-element.19), channel_id=1, source_target_pairs={{0,1},{1,0},{2,3},{3,2},{4,5},{5,4},{6,7},{7,6},{8,9},{9,8},{10,11... | collective-permute-start | bytes 1769480 | tf_op jit(solution)/shard_map/ppermute | solution.py:153
  24.1 10.6 %copy-start = (f32[256,1152]{1,0:T(8,128)S(1)}, f32[256,1152]{1,0:T(8,128)}, u32[]{:S(2)}) copy-start(f32[256,1152]{1,0:T(8,128)} %img_ref.1) | copy-start | bytes 3538948
  24.3 20.4 %copy-start.1 = (f32[64,1152]{1,0:T(8,128)S(1)}, f32[64,1152]{1,0:T(8,128)}, u32[]{:S(2)}) copy-start(f32[64,1152]{1,0:T(8,128)} %txt_ref.1) | copy-start | bytes 884740
  24.3 7.6 %collective-permute-start.6 = (bf16[64,1152]{1,0:T(8,128)(2,1)S(1)}, bf16[64,1152]{1,0:T(8,128)(2,1)S(1)}, u32[]{:S(2)}, u32[]{:S(2)}) collective-permute-start(bf16[64,1152]{1,0:T(8,128)(2,1)S(1)} %get-tuple-element.21), channel_id=1, source_target_pairs={{0,8},{8,16},{16,24},{24,0},{1,9},{9,17},{17,25},{25,1},{2,10},{10... | collective-permute-start | bytes 442376 | tf_op jit(solution)/shard_map/ppermute | solution.py:148
  25.9 8.8 %collective-permute-start.7 = (bf16[64,1152]{1,0:T(8,128)(2,1)S(1)}, bf16[64,1152]{1,0:T(8,128)(2,1)S(1)}, u32[]{:S(2)}, u32[]{:S(2)}) collective-permute-start(bf16[64,1152]{1,0:T(8,128)(2,1)S(1)} %get-tuple-element.22), channel_id=1, source_target_pairs={{0,16},{8,24},{16,0},{24,8},{1,17},{9,25},{17,1},{25,9},{2,18},{10... | collective-permute-start | bytes 442376 | tf_op jit(solution)/shard_map/ppermute | solution.py:148
  27.4 7.4 %collective-permute-start.8 = (bf16[64,1152]{1,0:T(8,128)(2,1)S(1)}, bf16[64,1152]{1,0:T(8,128)(2,1)S(1)}, u32[]{:S(2)}, u32[]{:S(2)}) collective-permute-start(bf16[64,1152]{1,0:T(8,128)(2,1)S(1)} %get-tuple-element.23), channel_id=1, source_target_pairs={{0,24},{8,0},{16,8},{24,16},{1,25},{9,1},{17,9},{25,17},{2,26},{10... | collective-permute-start | bytes 442376 | tf_op jit(solution)/shard_map/ppermute | solution.py:148
  28.8 9.9 %collective-permute-start.12 = (bf16[64,1152]{1,0:T(8,128)(2,1)S(1)}, bf16[64,1152]{1,0:T(8,128)(2,1)S(1)}, u32[]{:S(2)}, u32[]{:S(2)}) collective-permute-start(bf16[64,1152]{1,0:T(8,128)(2,1)S(1)} %get-tuple-element.25), channel_id=1, source_target_pairs={{0,6},{1,7},{2,0},{3,1},{4,2},{5,3},{6,4},{7,5},{8,14},{9,15},{10,... | collective-permute-start | bytes 442376 | tf_op jit(solution)/shard_map/ppermute | solution.py:148
  30.1 14.6 %collective-permute-start.13 = (bf16[64,1152]{1,0:T(8,128)(2,1)S(1)}, bf16[64,1152]{1,0:T(8,128)(2,1)S(1)}, u32[]{:S(2)}, u32[]{:S(2)}) collective-permute-start(bf16[64,1152]{1,0:T(8,128)(2,1)S(1)} %get-tuple-element.26), channel_id=1, source_target_pairs={{0,4},{1,5},{2,6},{3,7},{4,0},{5,1},{6,2},{7,3},{8,12},{9,13},{10,... | collective-permute-start | bytes 442376 | tf_op jit(solution)/shard_map/ppermute | solution.py:148
  32.0 12.7 %collective-permute-start.14 = (bf16[64,1152]{1,0:T(8,128)(2,1)S(1)}, bf16[64,1152]{1,0:T(8,128)(2,1)S(1)}, u32[]{:S(2)}, u32[]{:S(2)}) collective-permute-start(bf16[64,1152]{1,0:T(8,128)(2,1)S(1)} %get-tuple-element.27), channel_id=1, source_target_pairs={{0,2},{1,3},{2,4},{3,5},{4,6},{5,7},{6,0},{7,1},{8,10},{9,11},{10,... | collective-permute-start | bytes 442376 | tf_op jit(solution)/shard_map/ppermute | solution.py:148
  35.5 10.6 %collective-permute-start.11 = (bf16[64,1152]{1,0:T(8,128)(2,1)S(1)}, bf16[64,1152]{1,0:T(8,128)(2,1)S(1)}, u32[]{:S(2)}, u32[]{:S(2)}) collective-permute-start(bf16[64,1152]{1,0:T(8,128)(2,1)S(1)} %shard_map.72.refs_0_), channel_id=1, source_target_pairs={{0,24},{8,0},{16,8},{24,16},{1,25},{9,1},{17,9},{25,17},{2,26},{10... | collective-permute-start | bytes 442376 | tf_op jit(solution)/shard_map/ppermute | solution.py:148
  37.2 8.9 %collective-permute-start.10 = (bf16[64,1152]{1,0:T(8,128)(2,1)S(1)}, bf16[64,1152]{1,0:T(8,128)(2,1)S(1)}, u32[]{:S(2)}, u32[]{:S(2)}) collective-permute-start(bf16[64,1152]{1,0:T(8,128)(2,1)S(1)} %shard_map.72.refs_0_), channel_id=1, source_target_pairs={{0,16},{8,24},{16,0},{24,8},{1,17},{9,25},{17,1},{25,9},{2,18},{10... | collective-permute-start | bytes 442376 | tf_op jit(solution)/shard_map/ppermute | solution.py:148
  38.8 7.4 %collective-permute-start.9 = (bf16[64,1152]{1,0:T(8,128)(2,1)S(1)}, bf16[64,1152]{1,0:T(8,128)(2,1)S(1)}, u32[]{:S(2)}, u32[]{:S(2)}) collective-permute-start(bf16[64,1152]{1,0:T(8,128)(2,1)S(1)} %shard_map.72.refs_0_), channel_id=1, source_target_pairs={{0,8},{8,16},{16,24},{24,0},{1,9},{9,17},{17,25},{25,1},{2,10},{10... | collective-permute-start | bytes 442376 | tf_op jit(solution)/shard_map/ppermute | solution.py:148

commit v3 on v2

v3 whole, which is shorter than its diff:
```python
import functools

import jax
import jax.numpy as jnp
from jax import lax
from jax.experimental import pallas as pl
from jax.experimental.pallas import tpu as pltpu
from jax.sharding import PartitionSpec as P

EPSILON = 1e-06
F32 = jnp.float32
BF16 = jnp.bfloat16
VMEM = pl.BlockSpec(memory_space=pltpu.VMEM)
SMEM = pl.BlockSpec(memory_space=pltpu.SMEM)


def unit_rows(texts, images):
    sizes = [texts.shape, images.shape]
    total = texts.size + images.size
    return pl.pallas_call(
        unit_body,
        out_shape=[struct(*size, BF16) for size in sizes],
        in_specs=[pl.BlockSpec(memory_space=pltpu.HBM)] * 2,
        out_specs=[VMEM] * 2,
        scratch_shapes=[pltpu.VMEM(size, F32) for size in sizes] + [pltpu.SemaphoreType.DMA((2,))],
        compiler_params=pltpu.CompilerParams(vmem_limit_bytes=16 << 20),
        cost_estimate=pl.CostEstimate(flops=4 * total, bytes_accessed=6 * total, transcendentals=0),
    )(*[pltpu.with_memory_space_constraint(v, pltpu.HBM) for v in (texts, images)])


def call(body, outs, args, specs, limit, flops, scratch=()):
    size = sum(a.size * a.dtype.itemsize for a in args)
    size += sum(o.size * o.dtype.itemsize for o in outs)
    return pl.pallas_call(
        body,
        out_shape=outs,
        in_specs=specs,
        out_specs=[VMEM] * len(outs),
        scratch_shapes=scratch,
        compiler_params=pltpu.CompilerParams(vmem_limit_bytes=limit),
        cost_estimate=pl.CostEstimate(flops=flops, bytes_accessed=size, transcendentals=0),
    )(*args)


def struct(rows, cols, dtype):
    return jax.ShapeDtypeStruct((rows, cols), dtype)


def inverse_norm(values):
    return lax.rsqrt(jnp.sum(values * values, axis=1, keepdims=True) + EPSILON)


def backward_unit(values, upstream):
    inverse = inverse_norm(values)
    unit = values * inverse
    return inverse * (upstream - unit * jnp.sum(unit * upstream, axis=1, keepdims=True))


def unit_body(txt, img, txt_out, img_out, txt_held, img_held, sems):
    txt_copy = pltpu.make_async_copy(txt, txt_held, sems.at[0])
    img_copy = pltpu.make_async_copy(img, img_held, sems.at[1])
    txt_copy.start()
    img_copy.start()
    txt_copy.wait()
    values = txt_held[...]
    txt_out[...] = (values * inverse_norm(values)).astype(BF16)
    img_copy.wait()
    values = img_held[...]
    img_out[...] = (values * inverse_norm(values)).astype(BF16)


def weights_of(tile, scalars, factors, perm, img):
    rows = tile.shape[0] // scalars.shape[0]
    row = lax.broadcasted_iota(jnp.int32, (rows, 1), 0)
    ids = jnp.concatenate([row + scalars[k] for k in range(scalars.shape[0])], axis=0)
    products = lax.dot_general(tile, img, (((1,), (1,)), ((), ())), preferred_element_type=F32)
    positive = (ids == perm).astype(F32)
    return (jax.nn.sigmoid(factors[0] * products + factors[1]) - positive).astype(BF16)


def to_images(weights, tile):
    return lax.dot_general(weights, tile, (((0,), (0,)), ((), ())), preferred_element_type=F32)


def other_body(scalars, factors, perm, img, txt, kept, out):
    weights = weights_of(txt[...], scalars, factors, perm[...], img[...])
    kept[...] = weights
    out[...] = to_images(weights, txt[...]).astype(BF16)


def own_body(blocks, home, scalars, factors, perm, img_own, img_other, kept, txt, *refs):
    own_img, own_txt, *other_txt, held = refs
    rows = own_txt.shape[0]
    weights = weights_of(txt[...], scalars, factors, perm[...], img_own[...])
    own_img[...] = to_images(weights, txt[...])
    held[...] = jnp.dot(weights, img_own[...], preferred_element_type=F32) + jnp.dot(
        kept[...], img_other[...], preferred_element_type=F32
    )
    for k in range(blocks):
        start = pl.multiple_of(lax.rem(home[0] + k, blocks) * rows, rows)
        block = held[pl.ds(start, rows), :]
        if k == 0:
            own_txt[...] = block
        else:
            other_txt[k - 1][...] = block.astype(BF16)


def add_body(own, other, out):
    out[...] = (own[...] + other[...].astype(F32)).astype(BF16)


def total_of(parts, rows):
    total = parts[:rows, :].astype(F32)
    for k in range(1, parts.shape[0] // rows):
        total = total + parts[k * rows : (k + 1) * rows, :].astype(F32)
    return total


def finish_img(copies, position, factors, img_ref, parts, out):
    rows = parts.shape[0] // copies
    start = pl.multiple_of(position[0] * rows, rows)
    upstream = factors[0] * total_of(parts, rows)
    grad = backward_unit(img_ref[pl.ds(start, rows), :], upstream).astype(BF16)
    for k in range(copies):
        out[k * rows : (k + 1) * rows, :] = grad


def finish_body(factors, txt_ref, grads, own, *refs):
    *parts, img_out, txt_out = refs
    img_out[...] = grads[...].astype(F32)
    total = own[...]
    for part in parts:
        total = total + part[...].astype(F32)
    txt_out[...] = backward_unit(txt_ref[...], factors[0] * total)


def exchanged(value, axis, groups=None):
    return lax.all_to_all(value, axis, 0, 0, axis_index_groups=groups, tiled=True)


def shifted(value, axis, steps):
    count = lax.axis_size(axis)
    return lax.ppermute(value, axis, [(s, (s + steps) % count) for s in range(count)])


def swapped(value):
    count = lax.axis_size("txt")
    return lax.ppermute(value, "txt", [(s, s ^ 1) for s in range(count)])


def local(images, texts, perm, scale, shift):
    rows, width = images.shape
    txt_rows = texts.shape[0]
    line = lax.axis_size("txt")
    blocks = line // 2
    groups = [list(range(core, line, 2)) for core in range(2)]
    count = lax.axis_size("img")
    part = rows // count
    column = lax.axis_index("txt")
    place = lax.axis_index("img")
    position = place.reshape(1).astype(jnp.int32)
    factors = jnp.concatenate([scale, shift])
    perm_row = perm.reshape(1, rows)

    txt_bf, img_bf = unit_rows(texts, images)
    tiles = exchanged(jnp.concatenate([txt_bf] * blocks, axis=0), "txt", groups)
    perm_other = swapped(perm_row)
    img_other = swapped(img_bf)
    firsts = jnp.stack(
        [(place * line + column % 2 + 2 * k) * txt_rows for k in range(blocks)]
    ).astype(jnp.int32)
    pairs = 2 * rows * blocks * txt_rows * width
    kept, other_img = call(
        other_body,
        [struct(blocks * txt_rows, rows, BF16), struct(rows, width, BF16)],
        [firsts, factors, perm_other, img_other, tiles],
        [SMEM] * 2 + [VMEM] * 3,
        40 << 20,
        2 * pairs,
    )
    from_other = swapped(other_img)
    home = (column // 2).reshape(1).astype(jnp.int32)
    own_img, own_txt, *other_txt = call(
        functools.partial(own_body, blocks),
        [struct(rows, width, F32), struct(txt_rows, width, F32)]
        + [struct(txt_rows, width, BF16)] * (blocks - 1),
        [home, firsts, factors, perm_row, img_bf, img_other, kept, tiles],
        [SMEM] * 3 + [VMEM] * 5,
        40 << 20,
        4 * pairs,
        [pltpu.VMEM((blocks * txt_rows, width), F32)],
    )
    back = [shifted(other_txt[k - 1], "txt", 2 * k) for k in range(1, blocks)]
    (sums,) = call(
        add_body,
        [struct(rows, width, BF16)],
        [own_img, from_other],
        [VMEM] * 2,
        24 << 20,
        rows * width,
    )
    parts = exchanged(sums, "img")
    (grad_part,) = call(
        functools.partial(finish_img, count),
        [struct(rows, width, BF16)],
        [position, factors, images, parts],
        [SMEM] * 2 + [VMEM] * 2,
        24 << 20,
        10 * part * width,
    )
    grad_images, grad_texts = call(
        finish_body,
        [struct(rows, width, F32), struct(txt_rows, width, F32)],
        [factors, texts, exchanged(grad_part, "img"), own_txt, *back],
        [SMEM] + [VMEM] * (2 + blocks),
        24 << 20,
        10 * txt_rows * width,
    )
    return (grad_images, grad_texts)


def solution(mesh):
    placed = (P("txt", None), P(("img", "txt"), None), P("txt"), P(), P())
    return jax.shard_map(
        local,
        mesh=mesh,
        in_specs=placed,
        out_specs=(P("txt", None), P(("img", "txt"), None)),
        check_vma=False,
    )
```

time: 47.5 us -> 65.6 us (1.38)
  blocking collectives: 0 us -> 13.7 us
  waiting for transfers between devices: 17.9 us -> 23.4 us
  starting transfers between devices: 18.7 us -> 14.3 us
  local copies, waits for them, and re-layouts: 0.02 us -> 2.11 us
  other arithmetic: 0.15 us -> 1.01 us
    ppermute x12 -> x3, starting transfers between devices: 18.1 us -> 3.87 us  [shifted(): lax.ppermute(value, axis, [(s, (s + steps) % count) for s in range(count)])]
    all_to_all x0 -> x2, waiting for transfers between devices: none -> 13.9 us  [exchanged(): lax.all_to_all(value, axis, 0, 0, axis_index_groups=groups, tiled=True)]
    all_to_all x0 -> x1, blocking collectives: none -> 13.7 us  [exchanged(): lax.all_to_all(value, axis, 0, 0, axis_index_groups=groups, tiled=True)]
    all_to_all x0 -> x2, starting transfers between devices: none -> 9.93 us  [exchanged(): lax.all_to_all(value, axis, 0, 0, axis_index_groups=groups, tiled=True)]
    ppermute x12 -> x3, waiting for transfers between devices: 17.9 us -> 9.44 us  [shifted(): lax.ppermute(value, axis, [(s, (s + steps) % count) for s in range(count)])]
    unnamed x6 -> x14, local copies, waits for them, and re-layouts: 0.02 us -> 2.11 us
    concatenate x0 -> x1, other arithmetic: none -> 0.86 us  [local(): tiles = exchanged(jnp.concatenate([txt_bf] * blocks, axis=0), 'txt', groups)]
    pallas_call x6 -> x5, Pallas kernels: 6.97 us -> 7.13 us  [call(): pl.pallas_call(body, out_shape=outs, in_specs=specs, out_specs=[VMEM] * l...]
  transfers between devices with their start and end apart: 15 -> 8, of which waited for: 6 -> 3; matrix products, arithmetic and copies ran while one was open for 0% -> 0% of each run, Pallas kernels for 9% -> 3%
where the time goes in v3:
time: 65.6 us; the launch traced here: 65.2 us
  waiting for transfers between devices  23.4 us (36%)
  starting transfers between devices  14.3 us (22%)
  blocking collectives  13.7 us (21%)
  Pallas kernels  8.7 us (13%)
  local copies, waits for them, and re-layouts  2.11 us (3%)
  between operations  2.03 us (3%)
  other arithmetic  1.01 us (2%)
    all_to_all x2, waiting for transfers between devices, exchanged(): lax.all_to_all(value, axis, 0, 0, axis_index_groups=groups, tiled=True)  13.9 us
    all_to_all x1, blocking collectives, exchanged(): lax.all_to_all(value, axis, 0, 0, axis_index_groups=groups, tiled=True)  13.7 us
    all_to_all x2, starting transfers between devices, exchanged(): lax.all_to_all(value, axis, 0, 0, axis_index_groups=groups, tiled=True)  9.93 us
    ppermute x3, waiting for transfers between devices, shifted(): lax.ppermute(value, axis, [(s, (s + steps) % count) for s in range(count)])  9.44 us
    pallas_call x5, Pallas kernels, call(): pl.pallas_call(body, out_shape=outs, in_specs=specs, out_specs=[VMEM] * l...  7.13 us
    ppermute x3, starting transfers between devices, shifted(): lax.ppermute(value, axis, [(s, (s + steps) % count) for s in range(count)])  3.87 us
    unnamed x14, local copies, waits for them, and re-layouts  2.11 us
    pallas_call x1, Pallas kernels, unit_rows(): pl.pallas_call(unit_body, out_shape=[struct(*size, BF16) for size in size...  1.56 us
  transfers between devices with their start and end apart: 8, of which 3 were waited for; matrix products, arithmetic and copies ran while one was open for 0% of the time, Pallas kernels for 3%

profile of v3, /device:TPU:0, one launch (start us, length us, event | category | flops | bytes accessed | tf_op | source)
XLA Modules:
  0.0 65.2 jit_solution(13035823163274083818)
XLA Ops:
  0.6 1.6 %shard_map.68 = (bf16[64,1152]{1,0:T(8,128)(2,1)S(1)}, bf16[256,1152]{1,0:T(8,128)(2,1)S(1)}) custom-call(f32[64,1152]{1,0:T(8,128)} %txt_ref.1, f32[256,1152]{1,0:T(8,128)} %img_ref.1), custom_call_target="tpu_custom_call" | custom-call | flops 1474560 | bytes 2211840 | tf_op jit(solution)/shard_map/pallas_call | solution.py:20
  2.2 0.0 copy-start.6
  2.2 0.9 %pad_maximum_fusion = bf16[256,1152]{1,0:T(8,128)(2,1)} fusion(bf16[64,1152]{1,0:T(8,128)(2,1)S(1)} %get-tuple-element.12), kind=kLoop, calls=%fused_computation | loop fusion | flops 2359296 | bytes 737280 | tf_op jit(solution)/shard_map/concatenate | solution.py:166
  3.1 6.3 %all-to-all-start = ((bf16[4,64,1152]{2,1,0:T(8,128)(2,1)}), bf16[4,64,1152]{2,1,0:T(8,128)(2,1)S(1)}, u32[]{:S(2)}, u32[]{:S(2)}) async-start(bf16[4,64,1152]{2,1,0:T(8,128)(2,1)} %bitcast.7), calls=%async_computation | async-start | bytes 1179648 | tf_op jit(solution)/shard_map/all_to_all | solution.py:138
  9.4 0.0 collective-permute-start
  9.4 0.0 copy-done.6
  9.4 0.5 collective-permute-start.1
  11.2 0.1 pad_maximum_fusion.1.factors
  11.3 0.1 pad_add_fusion.scalars
  11.3 0.0 collective-permute-done.1.perm
  11.4 0.0 collective-permute-done.img.img_other
  11.4 13.9 %all-to-all-done = bf16[4,64,1152]{2,1,0:T(8,128)(2,1)S(1)} async-done(((bf16[4,64,1152]{2,1,0:T(8,128)(2,1)}), bf16[4,64,1152]{2,1,0:T(8,128)(2,1)S(1)}, u32[]{:S(2)}, u32[]{:S(2)}) %all-to-all-start) | async-done | bytes 589856 | tf_op jit(solution)/shard_map/all_to_all | solution.py:138
  25.3 1.6 %shard_map.69 = (bf16[256,256]{1,0:T(8,128)(2,1)S(1)}, bf16[256,1152]{1,0:T(8,128)(2,1)S(1)}) custom-call(s32[4]{0:T(128)S(1)} %pad_add_fusion.scalars, f32[2]{0:T(128)S(1)} %pad_maximum_fusion.1.factors, s32[1,256]{1,0:T(1,128)S(1)} %collective-permute-done.1.perm, bf16[256,1152]{1,0:T(8,128)(2,1)S(1)} %collective-permute-done.img.img_other, ...), custom_call_target="tpu_custom_call" | custom-call | flops 301989888 | bytes 1901592 | tf_op jit(solution)/shard_map/pallas_call | solution.py:34
  26.8 0.0 copy-start.4
  26.9 0.6 copy-done.4
  27.5 0.0 collective-permute-start.2
  27.5 0.0 copy-start.5
  27.5 0.9 %copy-done.5 = bf16[256,256]{1,0:T(8,128)(2,1)S(1)} copy-done((bf16[256,256]{1,0:T(8,128)(2,1)S(1)}, bf16[256,256]{1,0:T(8,128)(2,1)}, u32[]{:S(2)}) %copy-start.5) | copy-done | bytes 131096
  28.4 2.0 %shard_map.70 = (f32[256,1152]{1,0:T(8,128)S(1)}, f32[64,1152]{1,0:T(8,128)S(1)}, bf16[64,1152]{1,0:T(8,128)(2,1)S(1)}, bf16[64,1152]{1,0:T(8,128)(2,1)S(1)}, bf16[64,1152]{1,0:T(8,128)(2,1)S(1)}) custom-call(s32[1]{0:T(128)} %bitcast.1.home, s32[4]{0:T(128)S(1)} %pad_add_fusion.scalars, f32[2]{0:T(128)S(1)} %pad_maximum_fusion.1.factors, ...), custom_call_target="tpu_custom_call" | custom-call | flops 603979776 | bytes 3818524 | tf_op jit(solution)/shard_map/pallas_call | solution.py:34
  30.5 0.0 copy-start.2
  30.5 0.0 collective-permute-done.2.other
  30.5 0.1 shard_map.71
  30.6 0.5 copy-done.2
  31.1 0.0 copy-start
  31.1 13.7 %all_to_all.33 = bf16[4,64,1152]{2,1,0:T(8,128)(2,1)S(1)} all-to-all(bf16[4,64,1152]{2,1,0:T(8,128)(2,1)S(1)} %bitcast.16), channel_id=1, replica_groups=mesh['img'=4,'txt'=8] {'img'}, dimensions={0} | all-to-all | bytes 1179648 | tf_op jit(solution)/shard_map/all_to_all | solution.py:138
  44.8 0.0 copy-done
  44.8 1.6 %shard_map.72 = bf16[256,1152]{1,0:T(8,128)(2,1)} custom-call(s32[1]{0:T(128)} %bitcast.position, f32[2]{0:T(128)S(1)} %pad_maximum_fusion.1.factors, f32[256,1152]{1,0:T(8,128)S(1)} %copy-done, bf16[256,1152]{1,0:T(8,128)(2,1)S(1)} %bitcast.17), custom_call_target="tpu_custom_call" | custom-call | flops 737280 | bytes 2359308 | tf_op jit(solution)/shard_map/pallas_call | solution.py:34
  46.4 0.0 copy-start.3
  46.4 0.0 copy-start.1
  46.4 3.6 %all-to-all-start.2 = ((bf16[4,64,1152]{2,1,0:T(8,128)(2,1)}), bf16[4,64,1152]{2,1,0:T(8,128)(2,1)S(1)}, u32[]{:S(2)}, u32[]{:S(2)}) async-start(bf16[4,64,1152]{2,1,0:T(8,128)(2,1)} %bitcast.11), calls=%async_computation.2 | async-start | bytes 1179648 | tf_op jit(solution)/shard_map/all_to_all | solution.py:138
  50.0 0.0 copy-done.3
  50.0 0.1 collective-permute-start.3
  50.1 2.0 %collective-permute-start.4 = (bf16[64,1152]{1,0:T(8,128)(2,1)S(1)}, bf16[64,1152]{1,0:T(8,128)(2,1)S(1)}, u32[]{:S(2)}, u32[]{:S(2)}) collective-permute-start(bf16[64,1152]{1,0:T(8,128)(2,1)S(1)} %get-tuple-element.18), channel_id=1, source_target_pairs={{0,4},{1,5},{2,6},{3,7},{4,0},{5,1},{6,2},{7,3},{8,12},{9,13},{10,... | collective-permute-start | bytes 442376 | tf_op jit(solution)/shard_map/ppermute | solution.py:143
  52.1 1.8 %collective-permute-start.5 = (bf16[64,1152]{1,0:T(8,128)(2,1)S(1)}, bf16[64,1152]{1,0:T(8,128)(2,1)S(1)}, u32[]{:S(2)}, u32[]{:S(2)}) collective-permute-start(bf16[64,1152]{1,0:T(8,128)(2,1)S(1)} %get-tuple-element.19), channel_id=1, source_target_pairs={{0,6},{1,7},{2,0},{3,1},{4,2},{5,3},{6,4},{7,5},{8,14},{9,15},{10,... | collective-permute-start | bytes 442376 | tf_op jit(solution)/shard_map/ppermute | solution.py:143
  53.9 4.8 %collective-permute-done.3.refs_0_ = bf16[64,1152]{1,0:T(8,128)(2,1)S(1)} collective-permute-done((bf16[64,1152]{1,0:T(8,128)(2,1)S(1)}, bf16[64,1152]{1,0:T(8,128)(2,1)S(1)}, u32[]{:S(2)}, u32[]{:S(2)}) %collective-permute-start.3) | collective-permute-done | bytes 147488 | tf_op jit(solution)/shard_map/ppermute | solution.py:143
  58.7 4.6 %collective-permute-done.4.refs_1_ = bf16[64,1152]{1,0:T(8,128)(2,1)S(1)} collective-permute-done((bf16[64,1152]{1,0:T(8,128)(2,1)S(1)}, bf16[64,1152]{1,0:T(8,128)(2,1)S(1)}, u32[]{:S(2)}, u32[]{:S(2)}) %collective-permute-start.4) | collective-permute-done | bytes 147488 | tf_op jit(solution)/shard_map/ppermute | solution.py:143
  63.4 0.0 collective-permute-done.5.refs_2_
  63.4 0.0 all-to-all-done.2
  63.4 0.0 copy-done.1
  63.4 1.9 %shard_map.73 = (f32[256,1152]{1,0:T(8,128)}, f32[64,1152]{1,0:T(8,128)}) custom-call(f32[2]{0:T(128)S(1)} %pad_maximum_fusion.1.factors, f32[64,1152]{1,0:T(8,128)S(1)} %copy-done.1, bf16[256,1152]{1,0:T(8,128)(2,1)S(1)} %bitcast.15, f32[64,1152]{1,0:T(8,128)S(1)} %get-tuple-element.16.own, bf16[64,1152]{1,0:T(8,128)(2,1)S(1)} %collective-permute-done.3.refs_0_, ...), custom_call_target="tpu_custom_call" | custom-call | flops 737280 | bytes 3096584 | tf_op jit(solution)/shard_map/pallas_call | solution.py:34
Async XLA Ops:
  2.2 7.2 %copy-start.6 = (s32[256]{0:T(256)S(1)}, s32[256]{0:T(256)}, u32[]{:S(2)}) copy-start(s32[256]{0:T(256)} %param.7) | copy-start | bytes 3076
  3.1 22.2 %all-to-all-start = ((bf16[4,64,1152]{2,1,0:T(8,128)(2,1)}), bf16[4,64,1152]{2,1,0:T(8,128)(2,1)S(1)}, u32[]{:S(2)}, u32[]{:S(2)}) async-start(bf16[4,64,1152]{2,1,0:T(8,128)(2,1)} %bitcast.7), calls=%async_computation | async-start | bytes 1179648 | tf_op jit(solution)/shard_map/all_to_all | solution.py:138
  9.4 2.0 %collective-permute-start = (bf16[256,1152]{1,0:T(8,128)(2,1)S(1)}, bf16[256,1152]{1,0:T(8,128)(2,1)S(1)}, u32[]{:S(2)}, u32[]{:S(2)}) collective-permute-start(bf16[256,1152]{1,0:T(8,128)(2,1)S(1)} %get-tuple-element.11.img_own), channel_id=1, source_target_pairs={{0,1},{1,0},{2,3},{3,2},{4,5},{5,4},{6,7},{7,6},{8,9},{9,8},{10,11... | collective-permute-start | bytes 1769480 | tf_op jit(solution)/shard_map/ppermute | solution.py:148
  9.4 2.0 %collective-permute-start.1 = (s32[1,256]{1,0:T(1,128)S(1)}, s32[1,256]{1,0:T(1,128)S(1)}, u32[]{:S(2)}, u32[]{:S(2)}) collective-permute-start(s32[1,256]{1,0:T(1,128)S(1)} %bitcast.18), channel_id=1, source_target_pairs={{0,1},{1,0},{2,3},{3,2},{4,5},{5,4},{6,7},{7,6},{8,9},{9,8},{10,11... | collective-permute-start | bytes 3080 | tf_op jit(solution)/shard_map/ppermute | solution.py:148
  26.8 0.7 %copy-start.4 = (bf16[256,256]{1,0:T(8,128)(2,1)}, bf16[256,256]{1,0:T(8,128)(2,1)S(1)}, u32[]{:S(2)}) copy-start(bf16[256,256]{1,0:T(8,128)(2,1)S(1)} %get-tuple-element.13.kept) | copy-start | bytes 393220
  27.5 3.0 %collective-permute-start.2 = (bf16[256,1152]{1,0:T(8,128)(2,1)S(1)}, bf16[256,1152]{1,0:T(8,128)(2,1)S(1)}, u32[]{:S(2)}, u32[]{:S(2)}) collective-permute-start(bf16[256,1152]{1,0:T(8,128)(2,1)S(1)} %get-tuple-element.15), channel_id=1, source_target_pairs={{0,1},{1,0},{2,3},{3,2},{4,5},{5,4},{6,7},{7,6},{8,9},{9,8},{10,11... | collective-permute-start | bytes 1769480 | tf_op jit(solution)/shard_map/ppermute | solution.py:148
  27.5 0.9 %copy-start.5 = (bf16[256,256]{1,0:T(8,128)(2,1)S(1)}, bf16[256,256]{1,0:T(8,128)(2,1)}, u32[]{:S(2)}) copy-start(bf16[256,256]{1,0:T(8,128)(2,1)} %copy-done.4) | copy-start | bytes 393220
  30.5 0.7 %copy-start.2 = (bf16[64,1152]{1,0:T(8,128)(2,1)}, bf16[64,1152]{1,0:T(8,128)(2,1)S(1)}, u32[]{:S(2)}) copy-start(bf16[64,1152]{1,0:T(8,128)(2,1)S(1)} %get-tuple-element.17) | copy-start | bytes 442372
  31.1 13.7 %copy-start = (f32[256,1152]{1,0:T(8,128)S(1)}, f32[256,1152]{1,0:T(8,128)}, u32[]{:S(2)}) copy-start(f32[256,1152]{1,0:T(8,128)} %img_ref.1) | copy-start | bytes 3538948
  46.4 3.6 %copy-start.3 = (bf16[64,1152]{1,0:T(8,128)(2,1)S(1)}, bf16[64,1152]{1,0:T(8,128)(2,1)}, u32[]{:S(2)}) copy-start(bf16[64,1152]{1,0:T(8,128)(2,1)} %copy-done.2) | copy-start | bytes 442372
  46.4 17.0 %copy-start.1 = (f32[64,1152]{1,0:T(8,128)S(1)}, f32[64,1152]{1,0:T(8,128)}, u32[]{:S(2)}) copy-start(f32[64,1152]{1,0:T(8,128)} %txt_ref.1) | copy-start | bytes 884740
  46.4 17.0 %all-to-all-start.2 = ((bf16[4,64,1152]{2,1,0:T(8,128)(2,1)}), bf16[4,64,1152]{2,1,0:T(8,128)(2,1)S(1)}, u32[]{:S(2)}, u32[]{:S(2)}) async-start(bf16[4,64,1152]{2,1,0:T(8,128)(2,1)} %bitcast.11), calls=%async_computation.2 | async-start | bytes 1179648 | tf_op jit(solution)/shard_map/all_to_all | solution.py:138
  50.0 8.7 %collective-permute-start.3 = (bf16[64,1152]{1,0:T(8,128)(2,1)S(1)}, bf16[64,1152]{1,0:T(8,128)(2,1)S(1)}, u32[]{:S(2)}, u32[]{:S(2)}) collective-permute-start(bf16[64,1152]{1,0:T(8,128)(2,1)S(1)} %copy-done.3), channel_id=1, source_target_pairs={{0,2},{1,3},{2,4},{3,5},{4,6},{5,7},{6,0},{7,1},{8,10},{9,11},{10,... | collective-permute-start | bytes 442376 | tf_op jit(solution)/shard_map/ppermute | solution.py:143
  50.1 13.3 %collective-permute-start.4 = (bf16[64,1152]{1,0:T(8,128)(2,1)S(1)}, bf16[64,1152]{1,0:T(8,128)(2,1)S(1)}, u32[]{:S(2)}, u32[]{:S(2)}) collective-permute-start(bf16[64,1152]{1,0:T(8,128)(2,1)S(1)} %get-tuple-element.18), channel_id=1, source_target_pairs={{0,4},{1,5},{2,6},{3,7},{4,0},{5,1},{6,2},{7,3},{8,12},{9,13},{10,... | collective-permute-start | bytes 442376 | tf_op jit(solution)/shard_map/ppermute | solution.py:143
  52.1 11.2 %collective-permute-start.5 = (bf16[64,1152]{1,0:T(8,128)(2,1)S(1)}, bf16[64,1152]{1,0:T(8,128)(2,1)S(1)}, u32[]{:S(2)}, u32[]{:S(2)}) collective-permute-start(bf16[64,1152]{1,0:T(8,128)(2,1)S(1)} %get-tuple-element.19), channel_id=1, source_target_pairs={{0,6},{1,7},{2,0},{3,1},{4,2},{5,3},{6,4},{7,5},{8,14},{9,15},{10,... | collective-permute-start | bytes 442376 | tf_op jit(solution)/shard_map/ppermute | solution.py:143

commit v4 on v2

--- a/solution.py
+++ b/solution.py
@@ -81,33 +81,53 @@
     return lax.dot_general(weights, tile, (((0,), (0,)), ((), ())), preferred_element_type=F32)
 
 
-def other_body(blocks, scalars, factors, perm, img, *refs):
-    *txt, kept, out = refs
-    tile = jnp.concatenate([t[...] for t in txt], axis=0)
-    weights = weights_of(tile, scalars, factors, perm[...], img[...])
-    kept[...] = weights
-    out[...] = to_images(weights, tile).astype(BF16)
-
-
-def own_body(blocks, scalars, factors, perm, img_own, img_other, kept, *refs):
+def to_texts(weights, img):
+    return jnp.dot(weights, img, preferred_element_type=F32)
+
+
+def joined(tiles):
+    return jnp.concatenate([t[...] for t in tiles], axis=0)
+
+
+def early_body(blocks, scalars, factors, perm, perm_other, img, img_other, *refs):
     txt = refs[:blocks]
-    own_img, own_txt, *other_txt = refs[blocks:]
+    own_sum, other_sum, own_txt, *other_txt = refs[blocks:]
     rows = own_txt.shape[0]
-    tile = jnp.concatenate([t[...] for t in txt], axis=0)
-    weights = weights_of(tile, scalars, factors, perm[...], img_own[...])
-    own_img[...] = to_images(weights, tile)
-    to_txt = jnp.dot(weights, img_own[...], preferred_element_type=F32) + jnp.dot(
-        kept[...], img_other[...], preferred_element_type=F32
-    )
+    tile = joined(txt)
+    w_other = weights_of(tile, scalars, factors, perm_other[...], img_other[...])
+    other_sum[...] = to_images(w_other, tile)
+    w_own = weights_of(tile, scalars, factors, perm[...], img[...])
+    own_sum[...] = to_images(w_own, tile)
+    to_txt = to_texts(w_own, img[...]) + to_texts(w_other, img_other[...])
     own_txt[...] = to_txt[:rows]
     for k in range(1, blocks):
         other_txt[k - 1][...] = to_txt[k * rows : (k + 1) * rows].astype(BF16)
 
 
+def other_body(blocks, scalars, factors, perm, img, before, *refs):
+    *txt, kept, out = refs
+    tile = joined(txt)
+    weights = weights_of(tile, scalars, factors, perm[...], img[...])
+    kept[...] = weights
+    out[...] = (before[...] + to_images(weights, tile)).astype(BF16)
+
+
+def own_body(blocks, scalars, factors, perm, img, img_other, kept, before, *refs):
+    txt = refs[:blocks]
+    own_sum, *out_txt = refs[blocks:]
+    rows = out_txt[0].shape[0]
+    tile = joined(txt)
+    weights = weights_of(tile, scalars, factors, perm[...], img[...])
+    own_sum[...] = before[...] + to_images(weights, tile)
+    to_txt = to_texts(weights, img[...]) + to_texts(kept[...], img_other[...])
+    for k in range(blocks):
+        out_txt[k][...] = to_txt[k * rows : (k + 1) * rows].astype(BF16)
+
+
 def split_body(count, position, own, other, keep, *send):
     rows = keep.shape[0]
     for k in range(count):
-        start = pl.multiple_of(lax.rem(position[0] + k, count) * rows, rows)
+        start = pl.multiple_of((position[0] ^ k) * rows, rows)
         part = own[pl.ds(start, rows), :] + other[pl.ds(start, rows), :].astype(F32)
         if k == 0:
             keep[...] = part
@@ -139,18 +159,13 @@
     *parts, out = refs
     rows = parts[0].shape[0]
     for k in range(count):
-        start = pl.multiple_of(lax.rem(position[0] + count - k, count) * rows, rows)
+        start = pl.multiple_of((position[0] ^ k) * rows, rows)
         out[pl.ds(start, rows), :] = parts[k][...].astype(F32)
 
 
-def shifted(value, axis, steps):
+def swapped(value, axis, step):
     count = lax.axis_size(axis)
-    return lax.ppermute(value, axis, [(s, (s + steps) % count) for s in range(count)])
-
-
-def swapped(value):
-    count = lax.axis_size("txt")
-    return lax.ppermute(value, "txt", [(s, s ^ 1) for s in range(count)])
+    return lax.ppermute(value, axis, [(s, s ^ step) for s in range(count)])
 
 
 def local(images, texts, perm, scale, shift):
@@ -158,6 +173,7 @@
     txt_rows = texts.shape[0]
     line = lax.axis_size("txt")
     blocks = line // 2
+    early = 2
     count = lax.axis_size("img")
     part = rows // count
     column = lax.axis_index("txt")
@@ -167,32 +183,44 @@
     perm_row = perm.reshape(1, rows)
 
     txt_bf, img_bf = unit_rows(texts, images)
-    tiles = [txt_bf] + [shifted(txt_bf, "txt", 2 * k) for k in range(1, blocks)]
-    perm_other = swapped(perm_row)
-    img_other = swapped(img_bf)
+    far = [swapped(txt_bf, "txt", 2 * k) for k in range(blocks - 1, 1, -1)]
+    tiles = [txt_bf, swapped(txt_bf, "txt", 2)] + far[::-1]
+    perm_other = swapped(perm_row, "txt", 1)
+    img_other = swapped(img_bf, "txt", 1)
     firsts = jnp.stack(
-        [(place * line + (column - 2 * k) % line) * txt_rows for k in range(blocks)]
+        [(place * line + (column ^ (2 * k))) * txt_rows for k in range(blocks)]
     ).astype(jnp.int32)
-    pairs = 2 * rows * blocks * txt_rows * width
+    pairs = 2 * rows * txt_rows * width
+    tile_out = struct(txt_rows, width, BF16)
+    own_sum, other_sum, own_txt, *other_txt = call(
+        functools.partial(early_body, early),
+        [struct(rows, width, F32)] * 2 + [struct(txt_rows, width, F32)] + [tile_out] * (early - 1),
+        [firsts[:early], factors, perm_row, perm_other, img_bf, img_other, *tiles[:early]],
+        [SMEM] * 2 + [VMEM] * (4 + early),
+        40 << 20,
+        6 * early * pairs,
+    )
+    back = [swapped(other_txt[k - 1], "txt", 2 * k) for k in range(1, early)]
+
+    late = blocks - early
     kept, other_img = call(
-        functools.partial(other_body, blocks),
-        [struct(blocks * txt_rows, rows, BF16), struct(rows, width, BF16)],
-        [firsts, factors, perm_other, img_other, *tiles],
-        [SMEM] * 2 + [VMEM] * (2 + blocks),
+        functools.partial(other_body, late),
+        [struct(late * txt_rows, rows, BF16), struct(rows, width, BF16)],
+        [firsts[early:], factors, perm_other, img_other, other_sum, *tiles[early:]],
+        [SMEM] * 2 + [VMEM] * (3 + late),
         40 << 20,
-        2 * pairs,
-    )
-    from_other = swapped(other_img)
-    own_img, own_txt, *other_txt = call(
-        functools.partial(own_body, blocks),
-        [struct(rows, width, F32), struct(txt_rows, width, F32)]
-        + [struct(txt_rows, width, BF16)] * (blocks - 1),
-        [firsts, factors, perm_row, img_bf, img_other, kept, *tiles],
-        [SMEM] * 2 + [VMEM] * (4 + blocks),
+        2 * late * pairs,
+    )
+    from_other = swapped(other_img, "txt", 1)
+    own_img, *other_txt = call(
+        functools.partial(own_body, late),
+        [struct(rows, width, F32)] + [tile_out] * late,
+        [firsts[early:], factors, perm_row, img_bf, img_other, kept, own_sum, *tiles[early:]],
+        [SMEM] * 2 + [VMEM] * (5 + late),
         40 << 20,
-        4 * pairs,
-    )
-    back = [shifted(other_txt[k - 1], "txt", -2 * k) for k in range(1, blocks)]
+        4 * late * pairs,
+    )
+    back += [swapped(other_txt[k], "txt", 2 * (early + k)) for k in range(late)]
 
     keep, *send = call(
         functools.partial(split_body, count),
@@ -202,7 +230,7 @@
         24 << 20,
         rows * width,
     )
-    got = [shifted(send[k - 1], "img", k) for k in range(1, count)]
+    got = [swapped(send[k - 1], "img", k) for k in range(1, count)]
     (grad_part,) = call(
         finish_img_body,
         [struct(part, width, BF16)],
@@ -211,7 +239,7 @@
         24 << 20,
         10 * part * width,
     )
-    grads = [grad_part] + [shifted(grad_part, "img", k) for k in range(1, count)]
+    grads = [grad_part] + [swapped(grad_part, "img", k) for k in range(1, count)]
     (grad_images,) = call(
         functools.partial(join_body, count),
         [struct(rows, width, F32)],

time: 47.5 us -> 48 us (1.011)
  Pallas kernels: 8.53 us -> 10.6 us
  waiting for transfers between devices: 17.9 us -> 16.2 us
    pallas_call x6 -> x7, Pallas kernels: 6.97 us -> 9 us  [call(): pl.pallas_call(body, out_shape=outs, in_specs=specs, out_specs=[VMEM] * l...]
    ppermute x15, waiting for transfers between devices: 17.9 us -> 16.2 us  [swapped(): return lax.ppermute(value, axis, [(s, s ^ step) for s in range(count)])]
  transfers between devices with their start and end apart: 15 -> 15, of which waited for: 6 -> 6; matrix products, arithmetic and copies ran while one was open for 0% -> 0% of each run, Pallas kernels for 9% -> 13%
where the time goes in v4:
time: 48 us; the launch traced here: 47.9 us
  starting transfers between devices  18.9 us (39%)
  waiting for transfers between devices  16.2 us (34%)
  Pallas kernels  10.6 us (22%)
  between operations  2.02 us (4%)
    ppermute x15, starting transfers between devices, swapped(): return lax.ppermute(value, axis, [(s, s ^ step) for s in range(count)])  18.9 us
    ppermute x15, waiting for transfers between devices, swapped(): return lax.ppermute(value, axis, [(s, s ^ step) for s in range(count)])  16.2 us
    pallas_call x7, Pallas kernels, call(): pl.pallas_call(body, out_shape=outs, in_specs=specs, out_specs=[VMEM] * l...  9 us
    pallas_call x1, Pallas kernels, unit_rows(): pl.pallas_call(unit_body, out_shape=[struct(*size, BF16) for size in size...  1.56 us
  transfers between devices with their start and end apart: 15, of which 6 were waited for; matrix products, arithmetic and copies ran while one was open for 0% of the time, Pallas kernels for 13%

profile of v4, /device:TPU:0, one launch (start us, length us, event | category | flops | bytes accessed | tf_op | source)
XLA Modules:
  0.0 47.9 jit_solution(16212165766618866500)
XLA Ops:
  0.6 0.0 copy-start.2
  0.6 1.6 %shard_map.68 = (bf16[64,1152]{1,0:T(8,128)(2,1)S(1)}, bf16[256,1152]{1,0:T(8,128)(2,1)S(1)}) custom-call(f32[64,1152]{1,0:T(8,128)} %txt_ref.1, f32[256,1152]{1,0:T(8,128)} %img_ref.1), custom_call_target="tpu_custom_call" | custom-call | flops 1474560 | bytes 2211840 | tf_op jit(solution)/shard_map/pallas_call | solution.py:20
  2.2 0.5 %collective-permute-start = (bf16[256,1152]{1,0:T(8,128)(2,1)S(1)}, bf16[256,1152]{1,0:T(8,128)(2,1)S(1)}, u32[]{:S(2)}, u32[]{:S(2)}) collective-permute-start(bf16[256,1152]{1,0:T(8,128)(2,1)S(1)} %get-tuple-element.17.img), channel_id=1, source_target_pairs={{0,1},{1,0},{2,3},{3,2},{4,5},{5,4},{6,7},{7,6},{8,9},{9,8},{10,11... | collective-permute-start | bytes 1769480 | tf_op jit(solution)/shard_map/ppermute | solution.py:168
  2.7 4.7 %collective-permute-start.4 = (bf16[64,1152]{1,0:T(8,128)(2,1)S(1)}, bf16[64,1152]{1,0:T(8,128)(2,1)S(1)}, u32[]{:S(2)}, u32[]{:S(2)}) collective-permute-start(bf16[64,1152]{1,0:T(8,128)(2,1)S(1)} %get-tuple-element.18.refs_0_), channel_id=1, source_target_pairs={{0,6},{1,7},{2,4},{3,5},{4,2},{5,3},{6,0},{7,1},{8,14},{9,15},{10,... | collective-permute-start | bytes 442376 | tf_op jit(solution)/shard_map/ppermute | solution.py:168
  7.4 0.0 collective-permute-start.3
  7.4 0.6 %collective-permute-start.2 = (bf16[64,1152]{1,0:T(8,128)(2,1)S(1)}, bf16[64,1152]{1,0:T(8,128)(2,1)S(1)}, u32[]{:S(2)}, u32[]{:S(2)}) collective-permute-start(bf16[64,1152]{1,0:T(8,128)(2,1)S(1)} %get-tuple-element.18.refs_0_), channel_id=1, source_target_pairs={{0,2},{1,3},{2,0},{3,1},{4,6},{5,7},{6,4},{7,5},{8,10},{9,11},{10,... | collective-permute-start | bytes 442376 | tf_op jit(solution)/shard_map/ppermute | solution.py:168
  8.0 0.0 copy-done.2
  8.0 0.0 collective-permute-start.1
  9.4 0.1 pad_maximum_fusion.factors
  9.4 0.1 pad_add_fusion.scalars
  9.5 0.1 pad_add_fusion.1.scalars
  9.6 0.0 collective-permute-done.1.perm_other.perm
  9.6 8.0 %collective-permute-done.2.refs_1_ = bf16[64,1152]{1,0:T(8,128)(2,1)S(1)} collective-permute-done((bf16[64,1152]{1,0:T(8,128)(2,1)S(1)}, bf16[64,1152]{1,0:T(8,128)(2,1)S(1)}, u32[]{:S(2)}, u32[]{:S(2)}) %collective-permute-start.2) | collective-permute-done | bytes 147488 | tf_op jit(solution)/shard_map/ppermute | solution.py:168
  17.5 0.0 collective-permute-done.img_other.img
  17.5 2.4 %shard_map.69 = (f32[256,1152]{1,0:T(8,128)S(1)}, f32[256,1152]{1,0:T(8,128)S(1)}, f32[64,1152]{1,0:T(8,128)S(1)}, bf16[64,1152]{1,0:T(8,128)(2,1)S(1)}) custom-call(s32[2]{0:T(128)S(1)} %pad_add_fusion.1.scalars, f32[2]{0:T(128)S(1)} %pad_maximum_fusion.factors, s32[1,256]{1,0:T(1,128)S(1)} %bitcast.7, s32[1,256]{1,0:T(1,128)S(1)} %collective-permute-done.1.perm_other.perm, ...), custom_call_target="tpu_custom_call" | custom-call | flops 452984832 | bytes 4278288 | tf_op jit(solution)/shard_map/pallas_call | solution.py:34
  20.0 0.0 collective-permute-done.4.refs_1_
  20.0 0.5 %collective-permute-done.3.refs_0_ = bf16[64,1152]{1,0:T(8,128)(2,1)S(1)} collective-permute-done((bf16[64,1152]{1,0:T(8,128)(2,1)S(1)}, bf16[64,1152]{1,0:T(8,128)(2,1)S(1)}, u32[]{:S(2)}, u32[]{:S(2)}) %collective-permute-start.3) | collective-permute-done | bytes 147488 | tf_op jit(solution)/shard_map/ppermute | solution.py:168
  20.5 1.5 %shard_map.70 = (bf16[128,256]{1,0:T(8,128)(2,1)S(1)}, bf16[256,1152]{1,0:T(8,128)(2,1)S(1)}) custom-call(s32[2]{0:T(128)S(1)} %pad_add_fusion.scalars, f32[2]{0:T(128)S(1)} %pad_maximum_fusion.factors, s32[1,256]{1,0:T(1,128)S(1)} %collective-permute-done.1.perm_other.perm, bf16[256,1152]{1,0:T(8,128)(2,1)S(1)} %collective-permute-done.img_other.img, ...), custom_call_target="tpu_custom_call" | custom-call | flops 150994944 | bytes 2720784 | tf_op jit(solution)/shard_map/pallas_call | solution.py:34
  22.0 0.1 collective-permute-start.5
  22.0 1.7 %shard_map.71 = (f32[256,1152]{1,0:T(8,128)S(1)}, bf16[64,1152]{1,0:T(8,128)(2,1)S(1)}, bf16[64,1152]{1,0:T(8,128)(2,1)S(1)}) custom-call(s32[2]{0:T(128)S(1)} %pad_add_fusion.scalars, f32[2]{0:T(128)S(1)} %pad_maximum_fusion.factors, s32[1,256]{1,0:T(1,128)S(1)} %bitcast.8, bf16[256,1152]{1,0:T(8,128)(2,1)S(1)} %get-tuple-element.17.img, ...), custom_call_target="tpu_custom_call" | custom-call | flops 301989888 | bytes 4195344 | tf_op jit(solution)/shard_map/pallas_call | solution.py:34
  23.7 0.0 copy-start
  23.7 0.3 collective-permute-done.5.other
  24.0 0.1 shard_map.72
  24.2 0.0 copy-start.1
  24.2 1.6 %collective-permute-start.6 = (bf16[64,1152]{1,0:T(8,128)(2,1)S(1)}, bf16[64,1152]{1,0:T(8,128)(2,1)S(1)}, u32[]{:S(2)}, u32[]{:S(2)}) collective-permute-start(bf16[64,1152]{1,0:T(8,128)(2,1)S(1)} %get-tuple-element.25), channel_id=1, source_target_pairs={{0,8},{8,0},{16,24},{24,16},{1,9},{9,1},{17,25},{25,17},{2,10},{10... | collective-permute-start | bytes 442376 | tf_op jit(solution)/shard_map/ppermute | solution.py:168
  25.7 1.5 %collective-permute-start.7 = (bf16[64,1152]{1,0:T(8,128)(2,1)S(1)}, bf16[64,1152]{1,0:T(8,128)(2,1)S(1)}, u32[]{:S(2)}, u32[]{:S(2)}) collective-permute-start(bf16[64,1152]{1,0:T(8,128)(2,1)S(1)} %get-tuple-element.26), channel_id=1, source_target_pairs={{0,16},{8,24},{16,0},{24,8},{1,17},{9,25},{17,1},{25,9},{2,18},{10... | collective-permute-start | bytes 442376 | tf_op jit(solution)/shard_map/ppermute | solution.py:168
  27.3 0.5 collective-permute-start.8
  27.7 0.7 %collective-permute-start.13 = (bf16[64,1152]{1,0:T(8,128)(2,1)S(1)}, bf16[64,1152]{1,0:T(8,128)(2,1)S(1)}, u32[]{:S(2)}, u32[]{:S(2)}) collective-permute-start(bf16[64,1152]{1,0:T(8,128)(2,1)S(1)} %get-tuple-element.30), channel_id=1, source_target_pairs={{0,4},{1,5},{2,6},{3,7},{4,0},{5,1},{6,2},{7,3},{8,12},{9,13},{10,... | collective-permute-start | bytes 442376 | tf_op jit(solution)/shard_map/ppermute | solution.py:168
  28.5 3.6 %collective-permute-start.14 = (bf16[64,1152]{1,0:T(8,128)(2,1)S(1)}, bf16[64,1152]{1,0:T(8,128)(2,1)S(1)}, u32[]{:S(2)}, u32[]{:S(2)}) collective-permute-start(bf16[64,1152]{1,0:T(8,128)(2,1)S(1)} %get-tuple-element.31), channel_id=1, source_target_pairs={{0,6},{1,7},{2,4},{3,5},{4,2},{5,3},{6,0},{7,1},{8,14},{9,15},{10,... | collective-permute-start | bytes 442376 | tf_op jit(solution)/shard_map/ppermute | solution.py:168
  32.1 0.0 collective-permute-done.6.refs_0_
  32.1 0.8 %collective-permute-start.12 = (bf16[64,1152]{1,0:T(8,128)(2,1)S(1)}, bf16[64,1152]{1,0:T(8,128)(2,1)S(1)}, u32[]{:S(2)}, u32[]{:S(2)}) collective-permute-start(bf16[64,1152]{1,0:T(8,128)(2,1)S(1)} %get-tuple-element.29), channel_id=1, source_target_pairs={{0,2},{1,3},{2,0},{3,1},{4,6},{5,7},{6,4},{7,5},{8,10},{9,11},{10,... | collective-permute-start | bytes 442376 | tf_op jit(solution)/shard_map/ppermute | solution.py:168
  32.9 1.7 %collective-permute-done.7.refs_1_ = bf16[64,1152]{1,0:T(8,128)(2,1)S(1)} collective-permute-done((bf16[64,1152]{1,0:T(8,128)(2,1)S(1)}, bf16[64,1152]{1,0:T(8,128)(2,1)S(1)}, u32[]{:S(2)}, u32[]{:S(2)}) %collective-permute-start.7) | collective-permute-done | bytes 147488 | tf_op jit(solution)/shard_map/ppermute | solution.py:168
  34.6 0.0 collective-permute-done.8.refs_2_
  34.6 0.0 copy-done
  34.6 0.8 %shard_map.73.refs_0_ = bf16[64,1152]{1,0:T(8,128)(2,1)S(1)} custom-call(s32[1]{0:T(128)} %bitcast.position, f32[2]{0:T(128)S(1)} %pad_maximum_fusion.factors, f32[256,1152]{1,0:T(8,128)S(1)} %copy-done, f32[64,1152]{1,0:T(8,128)S(1)} %get-tuple-element.24.own, bf16[64,1152]{1,0:T(8,128)(2,1)S(1)} %collective-permute-done.6.refs_0_, ...), custom_call_target="tpu_custom_call" | custom-call | flops 737280 | bytes 2064396 | tf_op jit(solution)/shard_map/pallas_call | solution.py:34
  35.3 1.6 %collective-permute-start.11 = (bf16[64,1152]{1,0:T(8,128)(2,1)S(1)}, bf16[64,1152]{1,0:T(8,128)(2,1)S(1)}, u32[]{:S(2)}, u32[]{:S(2)}) collective-permute-start(bf16[64,1152]{1,0:T(8,128)(2,1)S(1)} %shard_map.73.refs_0_), channel_id=1, source_target_pairs={{0,24},{8,16},{16,8},{24,0},{1,25},{9,17},{17,9},{25,1},{2,26},{10... | collective-permute-start | bytes 442376 | tf_op jit(solution)/shard_map/ppermute | solution.py:168
  36.9 1.2 %collective-permute-start.10 = (bf16[64,1152]{1,0:T(8,128)(2,1)S(1)}, bf16[64,1152]{1,0:T(8,128)(2,1)S(1)}, u32[]{:S(2)}, u32[]{:S(2)}) collective-permute-start(bf16[64,1152]{1,0:T(8,128)(2,1)S(1)} %shard_map.73.refs_0_), channel_id=1, source_target_pairs={{0,16},{8,24},{16,0},{24,8},{1,17},{9,25},{17,1},{25,9},{2,18},{10... | collective-permute-start | bytes 442376 | tf_op jit(solution)/shard_map/ppermute | solution.py:168
  38.1 3.5 %collective-permute-done.13.refs_1_ = bf16[64,1152]{1,0:T(8,128)(2,1)S(1)} collective-permute-done((bf16[64,1152]{1,0:T(8,128)(2,1)S(1)}, bf16[64,1152]{1,0:T(8,128)(2,1)S(1)}, u32[]{:S(2)}, u32[]{:S(2)}) %collective-permute-start.13) | collective-permute-done | bytes 147488 | tf_op jit(solution)/shard_map/ppermute | solution.py:168
  41.6 1.5 %collective-permute-start.9 = (bf16[64,1152]{1,0:T(8,128)(2,1)S(1)}, bf16[64,1152]{1,0:T(8,128)(2,1)S(1)}, u32[]{:S(2)}, u32[]{:S(2)}) collective-permute-start(bf16[64,1152]{1,0:T(8,128)(2,1)S(1)} %shard_map.73.refs_0_), channel_id=1, source_target_pairs={{0,8},{8,0},{16,24},{24,16},{1,9},{9,1},{17,25},{25,17},{2,10},{10... | collective-permute-start | bytes 442376 | tf_op jit(solution)/shard_map/ppermute | solution.py:168
  43.1 0.0 collective-permute-done.14.refs_2_
  43.1 0.0 collective-permute-done.12.refs_0_
  43.1 0.0 copy-done.1
  43.1 1.5 %shard_map.75 = f32[64,1152]{1,0:T(8,128)} custom-call(f32[2]{0:T(128)S(1)} %pad_maximum_fusion.factors, f32[64,1152]{1,0:T(8,128)S(1)} %copy-done.1, f32[64,1152]{1,0:T(8,128)S(1)} %get-tuple-element.28.own, bf16[64,1152]{1,0:T(8,128)(2,1)S(1)} %collective-permute-done.12.refs_0_, bf16[64,1152]{1,0:T(8,128)(2,1)S(1)} %collective-permute-done.13.refs_1_, ...), custom_call_target="tpu_custom_call" | custom-call | flops 737280 | bytes 1327112 | tf_op jit(solution)/shard_map/pallas_call | solution.py:34
  44.6 0.0 collective-permute-done.11.refs_3_
  44.6 0.0 collective-permute-done.10.refs_2_
  44.6 2.2 %collective-permute-done.9.refs_1_ = bf16[64,1152]{1,0:T(8,128)(2,1)S(1)} collective-permute-done((bf16[64,1152]{1,0:T(8,128)(2,1)S(1)}, bf16[64,1152]{1,0:T(8,128)(2,1)S(1)}, u32[]{:S(2)}, u32[]{:S(2)}) %collective-permute-start.9) | collective-permute-done | bytes 147488 | tf_op jit(solution)/shard_map/ppermute | solution.py:168
  46.8 1.1 %shard_map.74 = f32[256,1152]{1,0:T(8,128)} custom-call(s32[1]{0:T(128)} %bitcast.position, bf16[64,1152]{1,0:T(8,128)(2,1)S(1)} %shard_map.73.refs_0_, bf16[64,1152]{1,0:T(8,128)(2,1)S(1)} %collective-permute-done.9.refs_1_, bf16[64,1152]{1,0:T(8,128)(2,1)S(1)} %collective-permute-done.10.refs_2_, bf16[64,1152]{1,0:T(8,128)(2,1)S(1)} %collective-permute-done.11.refs_3_), custom_call_target="tpu_custom_call" | custom-call | flops 294912 | bytes 1769476 | tf_op jit(solution)/shard_map/pallas_call | solution.py:34
Async XLA Ops:
  0.6 7.4 %copy-start.2 = (s32[256]{0:T(256)S(1)}, s32[256]{0:T(256)}, u32[]{:S(2)}) copy-start(s32[256]{0:T(256)} %param.7) | copy-start | bytes 3076
  2.2 15.3 %collective-permute-start = (bf16[256,1152]{1,0:T(8,128)(2,1)S(1)}, bf16[256,1152]{1,0:T(8,128)(2,1)S(1)}, u32[]{:S(2)}, u32[]{:S(2)}) collective-permute-start(bf16[256,1152]{1,0:T(8,128)(2,1)S(1)} %get-tuple-element.17.img), channel_id=1, source_target_pairs={{0,1},{1,0},{2,3},{3,2},{4,5},{5,4},{6,7},{7,6},{8,9},{9,8},{10,11... | collective-permute-start | bytes 1769480 | tf_op jit(solution)/shard_map/ppermute | solution.py:168
  2.7 17.2 %collective-permute-start.4 = (bf16[64,1152]{1,0:T(8,128)(2,1)S(1)}, bf16[64,1152]{1,0:T(8,128)(2,1)S(1)}, u32[]{:S(2)}, u32[]{:S(2)}) collective-permute-start(bf16[64,1152]{1,0:T(8,128)(2,1)S(1)} %get-tuple-element.18.refs_0_), channel_id=1, source_target_pairs={{0,6},{1,7},{2,4},{3,5},{4,2},{5,3},{6,0},{7,1},{8,14},{9,15},{10,... | collective-permute-start | bytes 442376 | tf_op jit(solution)/shard_map/ppermute | solution.py:168
  7.4 13.1 %collective-permute-start.3 = (bf16[64,1152]{1,0:T(8,128)(2,1)S(1)}, bf16[64,1152]{1,0:T(8,128)(2,1)S(1)}, u32[]{:S(2)}, u32[]{:S(2)}) collective-permute-start(bf16[64,1152]{1,0:T(8,128)(2,1)S(1)} %get-tuple-element.18.refs_0_), channel_id=1, source_target_pairs={{0,4},{1,5},{2,6},{3,7},{4,0},{5,1},{6,2},{7,3},{8,12},{9,13},{10,... | collective-permute-start | bytes 442376 | tf_op jit(solution)/shard_map/ppermute | solution.py:168
  7.4 10.1 %collective-permute-start.2 = (bf16[64,1152]{1,0:T(8,128)(2,1)S(1)}, bf16[64,1152]{1,0:T(8,128)(2,1)S(1)}, u32[]{:S(2)}, u32[]{:S(2)}) collective-permute-start(bf16[64,1152]{1,0:T(8,128)(2,1)S(1)} %get-tuple-element.18.refs_0_), channel_id=1, source_target_pairs={{0,2},{1,3},{2,0},{3,1},{4,6},{5,7},{6,4},{7,5},{8,10},{9,11},{10,... | collective-permute-start | bytes 442376 | tf_op jit(solution)/shard_map/ppermute | solution.py:168
  8.0 1.5 %collective-permute-start.1 = (s32[1,256]{1,0:T(1,128)S(1)}, s32[1,256]{1,0:T(1,128)S(1)}, u32[]{:S(2)}, u32[]{:S(2)}) collective-permute-start(s32[1,256]{1,0:T(1,128)S(1)} %bitcast.6), channel_id=1, source_target_pairs={{0,1},{1,0},{2,3},{3,2},{4,5},{5,4},{6,7},{7,6},{8,9},{9,8},{10,11... | collective-permute-start | bytes 3080 | tf_op jit(solution)/shard_map/ppermute | solution.py:168
  22.0 2.1 %collective-permute-start.5 = (bf16[256,1152]{1,0:T(8,128)(2,1)S(1)}, bf16[256,1152]{1,0:T(8,128)(2,1)S(1)}, u32[]{:S(2)}, u32[]{:S(2)}) collective-permute-start(bf16[256,1152]{1,0:T(8,128)(2,1)S(1)} %get-tuple-element.23), channel_id=1, source_target_pairs={{0,1},{1,0},{2,3},{3,2},{4,5},{5,4},{6,7},{7,6},{8,9},{9,8},{10,11... | collective-permute-start | bytes 1769480 | tf_op jit(solution)/shard_map/ppermute | solution.py:168
  23.7 10.9 %copy-start = (f32[256,1152]{1,0:T(8,128)S(1)}, f32[256,1152]{1,0:T(8,128)}, u32[]{:S(2)}) copy-start(f32[256,1152]{1,0:T(8,128)} %img_ref.1) | copy-start | bytes 3538948
  24.2 19.0 %copy-start.1 = (f32[64,1152]{1,0:T(8,128)S(1)}, f32[64,1152]{1,0:T(8,128)}, u32[]{:S(2)}) copy-start(f32[64,1152]{1,0:T(8,128)} %txt_ref.1) | copy-start | bytes 884740
  24.2 7.9 %collective-permute-start.6 = (bf16[64,1152]{1,0:T(8,128)(2,1)S(1)}, bf16[64,1152]{1,0:T(8,128)(2,1)S(1)}, u32[]{:S(2)}, u32[]{:S(2)}) collective-permute-start(bf16[64,1152]{1,0:T(8,128)(2,1)S(1)} %get-tuple-element.25), channel_id=1, source_target_pairs={{0,8},{8,0},{16,24},{24,16},{1,9},{9,1},{17,25},{25,17},{2,10},{10... | collective-permute-start | bytes 442376 | tf_op jit(solution)/shard_map/ppermute | solution.py:168
  25.7 8.8 %collective-permute-start.7 = (bf16[64,1152]{1,0:T(8,128)(2,1)S(1)}, bf16[64,1152]{1,0:T(8,128)(2,1)S(1)}, u32[]{:S(2)}, u32[]{:S(2)}) collective-permute-start(bf16[64,1152]{1,0:T(8,128)(2,1)S(1)} %get-tuple-element.26), channel_id=1, source_target_pairs={{0,16},{8,24},{16,0},{24,8},{1,17},{9,25},{17,1},{25,9},{2,18},{10... | collective-permute-start | bytes 442376 | tf_op jit(solution)/shard_map/ppermute | solution.py:168
  27.3 7.3 %collective-permute-start.8 = (bf16[64,1152]{1,0:T(8,128)(2,1)S(1)}, bf16[64,1152]{1,0:T(8,128)(2,1)S(1)}, u32[]{:S(2)}, u32[]{:S(2)}) collective-permute-start(bf16[64,1152]{1,0:T(8,128)(2,1)S(1)} %get-tuple-element.27), channel_id=1, source_target_pairs={{0,24},{8,16},{16,8},{24,0},{1,25},{9,17},{17,9},{25,1},{2,26},{10... | collective-permute-start | bytes 442376 | tf_op jit(solution)/shard_map/ppermute | solution.py:168
  27.7 13.9 %collective-permute-start.13 = (bf16[64,1152]{1,0:T(8,128)(2,1)S(1)}, bf16[64,1152]{1,0:T(8,128)(2,1)S(1)}, u32[]{:S(2)}, u32[]{:S(2)}) collective-permute-start(bf16[64,1152]{1,0:T(8,128)(2,1)S(1)} %get-tuple-element.30), channel_id=1, source_target_pairs={{0,4},{1,5},{2,6},{3,7},{4,0},{5,1},{6,2},{7,3},{8,12},{9,13},{10,... | collective-permute-start | bytes 442376 | tf_op jit(solution)/shard_map/ppermute | solution.py:168
  28.5 14.6 %collective-permute-start.14 = (bf16[64,1152]{1,0:T(8,128)(2,1)S(1)}, bf16[64,1152]{1,0:T(8,128)(2,1)S(1)}, u32[]{:S(2)}, u32[]{:S(2)}) collective-permute-start(bf16[64,1152]{1,0:T(8,128)(2,1)S(1)} %get-tuple-element.31), channel_id=1, source_target_pairs={{0,6},{1,7},{2,4},{3,5},{4,2},{5,3},{6,0},{7,1},{8,14},{9,15},{10,... | collective-permute-start | bytes 442376 | tf_op jit(solution)/shard_map/ppermute | solution.py:168
  32.1 11.1 %collective-permute-start.12 = (bf16[64,1152]{1,0:T(8,128)(2,1)S(1)}, bf16[64,1152]{1,0:T(8,128)(2,1)S(1)}, u32[]{:S(2)}, u32[]{:S(2)}) collective-permute-start(bf16[64,1152]{1,0:T(8,128)(2,1)S(1)} %get-tuple-element.29), channel_id=1, source_target_pairs={{0,2},{1,3},{2,0},{3,1},{4,6},{5,7},{6,4},{7,5},{8,10},{9,11},{10,... | collective-permute-start | bytes 442376 | tf_op jit(solution)/shard_map/ppermute | solution.py:168
  35.3 9.3 %collective-permute-start.11 = (bf16[64,1152]{1,0:T(8,128)(2,1)S(1)}, bf16[64,1152]{1,0:T(8,128)(2,1)S(1)}, u32[]{:S(2)}, u32[]{:S(2)}) collective-permute-start(bf16[64,1152]{1,0:T(8,128)(2,1)S(1)} %shard_map.73.refs_0_), channel_id=1, source_target_pairs={{0,24},{8,16},{16,8},{24,0},{1,25},{9,17},{17,9},{25,1},{2,26},{10... | collective-permute-start | bytes 442376 | tf_op jit(solution)/shard_map/ppermute | solution.py:168
  36.9 7.7 %collective-permute-start.10 = (bf16[64,1152]{1,0:T(8,128)(2,1)S(1)}, bf16[64,1152]{1,0:T(8,128)(2,1)S(1)}, u32[]{:S(2)}, u32[]{:S(2)}) collective-permute-start(bf16[64,1152]{1,0:T(8,128)(2,1)S(1)} %shard_map.73.refs_0_), channel_id=1, source_target_pairs={{0,16},{8,24},{16,0},{24,8},{1,17},{9,25},{17,1},{25,9},{2,18},{10... | collective-permute-start | bytes 442376 | tf_op jit(solution)/shard_map/ppermute | solution.py:168
  41.6 5.1 %collective-permute-start.9 = (bf16[64,1152]{1,0:T(8,128)(2,1)S(1)}, bf16[64,1152]{1,0:T(8,128)(2,1)S(1)}, u32[]{:S(2)}, u32[]{:S(2)}) collective-permute-start(bf16[64,1152]{1,0:T(8,128)(2,1)S(1)} %shard_map.73.refs_0_), channel_id=1, source_target_pairs={{0,8},{8,0},{16,24},{24,16},{1,9},{9,1},{17,25},{25,17},{2,10},{10... | collective-permute-start | bytes 442376 | tf_op jit(solution)/shard_map/ppermute | solution.py:168

commit v5 on v2

v5 whole, which is shorter than its diff:
```python
import functools

import jax
import jax.numpy as jnp
from jax import lax
from jax.experimental import pallas as pl
from jax.experimental.pallas import tpu as pltpu
from jax.sharding import PartitionSpec as P

EPSILON = 1e-06
F32 = jnp.float32
BF16 = jnp.bfloat16
VMEM = pl.BlockSpec(memory_space=pltpu.VMEM)
SMEM = pl.BlockSpec(memory_space=pltpu.SMEM)


def unit_rows(place, texts, images, part):
    width = texts.shape[1]
    sizes = [texts.shape, images.shape]
    total = texts.size + images.size
    own = [texts.shape, (part, width)]
    return pl.pallas_call(
        unit_body,
        out_shape=[struct(*size, BF16) for size in sizes]
        + [struct(*size, F32) for size in own]
        + [struct(size[0], 128, F32) for size in own],
        in_specs=[SMEM] + [pl.BlockSpec(memory_space=pl.ANY)] * 2,
        out_specs=[VMEM] * 6,
        scratch_shapes=[pltpu.VMEM(size, F32) for size in sizes] + [pltpu.SemaphoreType.DMA((2,))],
        compiler_params=pltpu.CompilerParams(vmem_limit_bytes=16 << 20),
        cost_estimate=pl.CostEstimate(flops=4 * total, bytes_accessed=6 * total, transcendentals=0),
    )(place, *[pltpu.with_memory_space_constraint(v, pltpu.HBM) for v in (texts, images)])


def call(body, outs, args, specs, limit, flops):
    size = sum(a.size * a.dtype.itemsize for a in args)
    size += sum(o.size * o.dtype.itemsize for o in outs)
    return pl.pallas_call(
        body,
        out_shape=outs,
        in_specs=specs,
        out_specs=[VMEM] * len(outs),
        compiler_params=pltpu.CompilerParams(vmem_limit_bytes=limit),
        cost_estimate=pl.CostEstimate(flops=flops, bytes_accessed=size, transcendentals=0),
    )(*args)


def struct(rows, cols, dtype):
    return jax.ShapeDtypeStruct((rows, cols), dtype)


def inverse_norm(values):
    return lax.rsqrt(jnp.sum(values * values, axis=1, keepdims=True) + EPSILON)


def unit_body(
    place, txt, img, txt_bf, img_bf, txt_unit, img_unit, txt_inv, img_inv, txt_held, img_held, sems
):
    txt_copy = pltpu.make_async_copy(txt, txt_held, sems.at[0])
    img_copy = pltpu.make_async_copy(img, img_held, sems.at[1])
    txt_copy.start()
    img_copy.start()
    txt_copy.wait()
    values = txt_held[...]
    inverse = inverse_norm(values)
    unit = values * inverse
    txt_bf[...] = unit.astype(BF16)
    txt_unit[...] = unit
    txt_inv[...] = jnp.broadcast_to(inverse, txt_inv.shape)
    img_copy.wait()
    values = img_held[...]
    img_bf[...] = (values * inverse_norm(values)).astype(BF16)
    rows = img_unit.shape[0]
    values = img_held[pl.ds(pl.multiple_of(place[0] * rows, rows), rows), :]
    inverse = inverse_norm(values)
    img_unit[...] = values * inverse
    img_inv[...] = jnp.broadcast_to(inverse, img_inv.shape)


def weights_of(tile, order, line, place, column, scale, shift, perm, img):
    rows = tile.shape[0] // len(order)
    row = lax.broadcasted_iota(jnp.int32, (rows, 1), 0)
    ids = jnp.concatenate(
        [row + (place[0] * line + (column[0] ^ (2 * k))) * rows for k in order], axis=0
    )
    products = lax.dot_general(tile, img, (((1,), (1,)), ((), ())), preferred_element_type=F32)
    positive = (ids == perm).astype(F32)
    return (jax.nn.sigmoid(scale[0] * products + shift[0]) - positive).astype(BF16)


def to_images(weights, tile):
    return lax.dot_general(weights, tile, (((0,), (0,)), ((), ())), preferred_element_type=F32)


def to_texts(weights, img):
    return jnp.dot(weights, img, preferred_element_type=F32)


def joined(tiles):
    return jnp.concatenate([t[...] for t in tiles], axis=0)


def other_body(order, line, place, column, scale, shift, perm, img, *refs):
    *txt, kept, out = refs
    tile = joined(txt)
    weights = weights_of(tile, order, line, place, column, scale, shift, perm[...], img[...])
    kept[...] = weights
    out[...] = to_images(weights, tile).astype(BF16)


def own_body(order, line, place, column, scale, shift, perm, img, img_other, kept, *refs):
    *txt, own_sum, own_txt, even_txt, odd_txt = refs
    rows = own_txt.shape[0]
    tile = joined(txt)
    weights = weights_of(tile, order, line, place, column, scale, shift, perm[...], img[...])
    own_sum[...] = to_images(weights, tile)
    to_txt = to_texts(weights, img[...]) + to_texts(kept[...], img_other[...])
    half = odd_txt.shape[0]
    own_txt[...] = to_txt[:rows]
    even_txt[...] = to_txt[rows:half]
    odd_txt[...] = to_txt[half:].astype(BF16)


def add_body(even, got, *outs):
    rows = outs[0].shape[0]
    for k, out in enumerate(outs):
        mine = even[k * rows : (k + 1) * rows, :]
        out[...] = (mine + got[(k + 1) * rows : (k + 2) * rows, :].astype(F32)).astype(BF16)


def split_body(count, position, own, other, keep, *send):
    rows = keep.shape[0]
    for k in range(count):
        start = pl.multiple_of((position[0] ^ k) * rows, rows)
        part = own[pl.ds(start, rows), :] + other[pl.ds(start, rows), :].astype(F32)
        if k == 0:
            keep[...] = part
        else:
            send[k - 1][...] = part.astype(BF16)


def total_of(own, parts):
    total = own[...]
    for part in parts:
        total = total + part[...].astype(F32)
    return total


def backward_unit(unit, inverse, upstream):
    along = jnp.sum(unit * upstream, axis=1, keepdims=True)
    return inverse[:, :1] * (upstream - unit * along)


def finish_img_body(scale, unit, inverse, own, *refs):
    *parts, out = refs
    out[...] = backward_unit(
        unit[...], inverse[...], scale[0] * total_of(own, parts)
    ).astype(BF16)


def last_body(count, place, scale, unit, inverse, own, *refs):
    parts = refs[:count]
    *back, img_out, txt_out, img_held, txt_held, sems = refs[count:]
    rows = parts[0].shape[0]
    copies = []
    for k in range(count):
        img_held[k * rows : (k + 1) * rows, :] = parts[k][...].astype(F32)
        start = pl.multiple_of((place[0] ^ k) * rows, rows)
        copies.append(
            pltpu.make_async_copy(
                img_held.at[pl.ds(k * rows, rows), :],
                img_out.at[pl.ds(start, rows), :],
                sems.at[k],
            )
        )
        copies[-1].start()
    rows = unit.shape[0]
    total = total_of(own, back[1:]) + back[0][:rows, :].astype(F32)
    txt_held[...] = backward_unit(unit[...], inverse[...], scale[0] * total)
    copies.append(pltpu.make_async_copy(txt_held, txt_out, sems.at[count]))
    copies[-1].start()
    for copy in copies:
        copy.wait()


def swapped(value, axis, step):
    count = lax.axis_size(axis)
    return lax.ppermute(value, axis, [(s, s ^ step) for s in range(count)])


def local(images, texts, perm, scale, shift):
    rows, width = images.shape
    txt_rows = texts.shape[0]
    line = lax.axis_size("txt")
    blocks = line // 2
    count = lax.axis_size("img")
    part = rows // count
    column = lax.axis_index("txt").reshape(1).astype(jnp.int32)
    place = lax.axis_index("img").reshape(1).astype(jnp.int32)
    perm_row = perm.reshape(1, rows)

    txt_bf, img_bf, txt_unit, img_unit, txt_inv, img_inv = unit_rows(place, texts, images, part)
    half = blocks // 2
    order = list(range(0, blocks, 2)) + list(range(1, blocks, 2))
    tiles = [txt_bf] + [swapped(txt_bf, "txt", 2 * k) for k in order[1:]]
    perm_other = swapped(perm_row, "txt", 1)
    img_other = swapped(img_bf, "txt", 1)
    scalars = [place, column, scale, shift]
    pairs = 2 * rows * blocks * txt_rows * width
    kept, other_img = call(
        functools.partial(other_body, order, line),
        [struct(blocks * txt_rows, rows, BF16), struct(rows, width, BF16)],
        [*scalars, perm_other, img_other, *tiles],
        [SMEM] * 4 + [VMEM] * (2 + blocks),
        40 << 20,
        2 * pairs,
    )
    from_other = swapped(other_img, "txt", 1)
    own_img, own_txt, even_txt, odd_txt = call(
        functools.partial(own_body, order, line),
        [
            struct(rows, width, F32),
            struct(txt_rows, width, F32),
            struct((half - 1) * txt_rows, width, F32),
            struct(half * txt_rows, width, BF16),
        ],
        [*scalars, perm_row, img_bf, img_other, kept, *tiles],
        [SMEM] * 4 + [VMEM] * (4 + blocks),
        40 << 20,
        4 * pairs,
    )
    near = swapped(odd_txt, "txt", 2)
    sums = call(
        add_body,
        [struct(txt_rows, width, BF16)] * (half - 1),
        [even_txt, near],
        [VMEM] * 2,
        24 << 20,
        rows * width,
    )
    back = [near] + [swapped(sums[k - 1], "txt", 4 * k) for k in range(1, half)]

    keep, *send = call(
        functools.partial(split_body, count),
        [struct(part, width, F32)] + [struct(part, width, BF16)] * (count - 1),
        [place, own_img, from_other],
        [SMEM, VMEM, VMEM],
        24 << 20,
        rows * width,
    )
    got = [swapped(send[k - 1], "img", k) for k in range(1, count)]
    (grad_part,) = call(
        finish_img_body,
        [struct(part, width, BF16)],
        [scale, img_unit, img_inv, keep, *got],
        [SMEM] + [VMEM] * (2 + count),
        24 << 20,
        10 * part * width,
    )
    grads = [grad_part] + [swapped(grad_part, "img", k) for k in range(1, count)]
    anywhere = pl.BlockSpec(memory_space=pl.ANY)
    return pl.pallas_call(
        functools.partial(last_body, count),
        out_shape=[struct(rows, width, F32), struct(txt_rows, width, F32)],
        in_specs=[SMEM] * 2 + [VMEM] * (3 + count + half),
        out_specs=[anywhere] * 2,
        scratch_shapes=[
            pltpu.VMEM((rows, width), F32),
            pltpu.VMEM((txt_rows, width), F32),
            pltpu.SemaphoreType.DMA((count + 1,)),
        ],
        compiler_params=pltpu.CompilerParams(vmem_limit_bytes=24 << 20),
        cost_estimate=pl.CostEstimate(
            flops=10 * txt_rows * width, bytes_accessed=8 * rows * width, transcendentals=0
        ),
    )(place, scale, txt_unit, txt_inv, own_txt, *grads, *back)


def solution(mesh):
    placed = (P("txt", None), P(("img", "txt"), None), P("txt"), P(), P())
    return jax.shard_map(
        local,
        mesh=mesh,
        in_specs=placed,
        out_specs=(P("txt", None), P(("img", "txt"), None)),
        check_vma=False,
    )
```

time: 47.5 us -> 45.1 us (0.949)
  waiting for transfers between devices: 17.9 us -> 22.9 us
  starting transfers between devices: 18.7 us -> 14.5 us
  Pallas kernels: 8.53 us -> 5.63 us
    ppermute x15 -> x14, waiting for transfers between devices: 17.9 us -> 22.9 us  [swapped(): return lax.ppermute(value, axis, [(s, s ^ step) for s in range(count)])]
    ppermute x15 -> x14, starting transfers between devices: 18.7 us -> 14.5 us  [swapped(): return lax.ppermute(value, axis, [(s, s ^ step) for s in range(count)])]
    pallas_call x6 -> x5, Pallas kernels: 6.97 us -> 2.77 us  [call(): pl.pallas_call(body, out_shape=outs, in_specs=specs, out_specs=[VMEM] * l...]
    pallas_call x0 -> x1, Pallas kernels: none -> 1.27 us  [local(): pl.pallas_call(functools.partial(last_body, count), out_shape=[struct(row...]
  transfers between devices with their start and end apart: 15 -> 14, of which waited for: 6 -> 9; matrix products, arithmetic and copies ran while one was open for 0% -> 0% of each run, Pallas kernels for 9% -> 4%
where the time goes in v5:
time: 45.1 us; the launch traced here: 44.9 us
  waiting for transfers between devices  22.9 us (51%)
  starting transfers between devices  14.5 us (32%)
  Pallas kernels  5.63 us (12%)
  between operations  2.01 us (4%)
    ppermute x14, waiting for transfers between devices, swapped(): return lax.ppermute(value, axis, [(s, s ^ step) for s in range(count)])  22.9 us
    ppermute x14, starting transfers between devices, swapped(): return lax.ppermute(value, axis, [(s, s ^ step) for s in range(count)])  14.5 us
    pallas_call x5, Pallas kernels, call(): pl.pallas_call(body, out_shape=outs, in_specs=specs, out_specs=[VMEM] * l...  2.77 us
    pallas_call x1, Pallas kernels, unit_rows(): pl.pallas_call(unit_body, out_shape=[struct(*size, BF16) for size in size...  1.58 us
    pallas_call x1, Pallas kernels, local(): pl.pallas_call(functools.partial(last_body, count), out_shape=[struct(row...  1.27 us
  transfers between devices with their start and end apart: 14, of which 9 were waited for; matrix products, arithmetic and copies ran while one was open for 0% of the time, Pallas kernels for 4%

profile of v5, /device:TPU:0, one launch (start us, length us, event | category | flops | bytes accessed | tf_op | source)
XLA Modules:
  0.0 44.9 jit_solution(14894259730504156720)
XLA Ops:
  0.6 0.0 copy-start
  0.6 1.6 %shard_map.68 = (bf16[64,1152]{1,0:T(8,128)(2,1)S(1)}, bf16[256,1152]{1,0:T(8,128)(2,1)S(1)}, f32[64,1152]{1,0:T(8,128)S(1)}, f32[64,1152]{1,0:T(8,128)S(1)}, f3...) custom-call(s32[1]{0:T(128)} %bitcast.place.position, f32[64,1152]{1,0:T(8,128)} %txt.1, f32[256,1152]{1,0:T(8,128)} %img.1), custom_call_target="tpu_custom_call" | custom-call | flops 1474560 | bytes 2211840 | tf_op jit(solution)/shard_map/pallas_call | solution.py:22
  2.2 0.5 %collective-permute-start = (bf16[256,1152]{1,0:T(8,128)(2,1)S(1)}, bf16[256,1152]{1,0:T(8,128)(2,1)S(1)}, u32[]{:S(2)}, u32[]{:S(2)}) collective-permute-start(bf16[256,1152]{1,0:T(8,128)(2,1)S(1)} %get-tuple-element.20.img), channel_id=1, source_target_pairs={{0,1},{1,0},{2,3},{3,2},{4,5},{5,4},{6,7},{7,6},{8,9},{9,8},{10,11... | collective-permute-start | bytes 1769480 | tf_op jit(solution)/shard_map/ppermute | solution.py:188
  2.8 4.7 %collective-permute-start.4 = (bf16[64,1152]{1,0:T(8,128)(2,1)S(1)}, bf16[64,1152]{1,0:T(8,128)(2,1)S(1)}, u32[]{:S(2)}, u32[]{:S(2)}) collective-permute-start(bf16[64,1152]{1,0:T(8,128)(2,1)S(1)} %get-tuple-element.21.refs_0_), channel_id=1, source_target_pairs={{0,6},{1,7},{2,4},{3,5},{4,2},{5,3},{6,0},{7,1},{8,14},{9,15},{10,... | collective-permute-start | bytes 442376 | tf_op jit(solution)/shard_map/ppermute | solution.py:188
  7.4 0.0 collective-permute-start.3
  7.4 0.6 %collective-permute-start.2 = (bf16[64,1152]{1,0:T(8,128)(2,1)S(1)}, bf16[64,1152]{1,0:T(8,128)(2,1)S(1)}, u32[]{:S(2)}, u32[]{:S(2)}) collective-permute-start(bf16[64,1152]{1,0:T(8,128)(2,1)S(1)} %get-tuple-element.21.refs_0_), channel_id=1, source_target_pairs={{0,4},{1,5},{2,6},{3,7},{4,0},{5,1},{6,2},{7,3},{8,12},{9,13},{10,... | collective-permute-start | bytes 442376 | tf_op jit(solution)/shard_map/ppermute | solution.py:188
  8.1 0.0 copy-done
  8.1 0.0 collective-permute-start.1
  9.4 0.0 collective-permute-done.1.perm
  9.4 2.8 %collective-permute-done.4.refs_3_ = bf16[64,1152]{1,0:T(8,128)(2,1)S(1)} collective-permute-done((bf16[64,1152]{1,0:T(8,128)(2,1)S(1)}, bf16[64,1152]{1,0:T(8,128)(2,1)S(1)}, u32[]{:S(2)}, u32[]{:S(2)}) %collective-permute-start.4) | collective-permute-done | bytes 147488 | tf_op jit(solution)/shard_map/ppermute | solution.py:188
  12.2 3.9 %collective-permute-done.3.refs_2_ = bf16[64,1152]{1,0:T(8,128)(2,1)S(1)} collective-permute-done((bf16[64,1152]{1,0:T(8,128)(2,1)S(1)}, bf16[64,1152]{1,0:T(8,128)(2,1)S(1)}, u32[]{:S(2)}, u32[]{:S(2)}) %collective-permute-start.3) | collective-permute-done | bytes 147488 | tf_op jit(solution)/shard_map/ppermute | solution.py:188
  16.1 4.4 %collective-permute-done.2.refs_1_ = bf16[64,1152]{1,0:T(8,128)(2,1)S(1)} collective-permute-done((bf16[64,1152]{1,0:T(8,128)(2,1)S(1)}, bf16[64,1152]{1,0:T(8,128)(2,1)S(1)}, u32[]{:S(2)}, u32[]{:S(2)}) %collective-permute-start.2) | collective-permute-done | bytes 147488 | tf_op jit(solution)/shard_map/ppermute | solution.py:188
  20.5 0.0 collective-permute-done.img.img_other
  20.5 1.0 %shard_map.69 = (bf16[256,256]{1,0:T(8,128)(2,1)S(1)}, bf16[256,1152]{1,0:T(8,128)(2,1)S(1)}) custom-call(s32[1]{0:T(128)} %bitcast.place.position, s32[1]{0:T(128)} %bitcast.1.column, f32[1]{0:T(128)S(6)} %copy.7.scale, f32[1]{0:T(128)S(6)} %copy.8.shift, s32[1,256]{1,0:T(1,128)S(1)} %collective-permute-done.1.perm, ...), custom_call_target="tpu_custom_call" | custom-call | flops 301989888 | bytes 1901584 | tf_op jit(solution)/shard_map/pallas_call | solution.py:38
  21.5 0.1 collective-permute-start.5
  21.6 1.4 %shard_map.70 = (f32[256,1152]{1,0:T(8,128)S(1)}, f32[64,1152]{1,0:T(8,128)S(1)}, f32[64,1152]{1,0:T(8,128)S(1)}, bf16[128,1152]{1,0:T(8,128)(2,1)S(1)}) custom-call(s32[1]{0:T(128)} %bitcast.place.position, s32[1]{0:T(128)} %bitcast.1.column, f32[1]{0:T(128)S(6)} %copy.7.scale, f32[1]{0:T(128)S(6)} %copy.8.shift, s32[1,256]{1,0:T(1,128)S(1)} %bitcast.4, ...), custom_call_target="tpu_custom_call" | custom-call | flops 603979776 | bytes 3965968 | tf_op jit(solution)/shard_map/pallas_call | solution.py:38
  23.0 0.1 collective-permute-start.12
  23.1 0.5 %collective-permute-done.5.other = bf16[256,1152]{1,0:T(8,128)(2,1)S(1)} collective-permute-done((bf16[256,1152]{1,0:T(8,128)(2,1)S(1)}, bf16[256,1152]{1,0:T(8,128)(2,1)S(1)}, u32[]{:S(2)}, u32[]{:S(2)}) %collective-permute-start.5) | collective-permute-done | bytes 589856 | tf_op jit(solution)/shard_map/ppermute | solution.py:188
  23.6 0.1 shard_map.71
  23.8 1.6 %collective-permute-start.6 = (bf16[64,1152]{1,0:T(8,128)(2,1)S(1)}, bf16[64,1152]{1,0:T(8,128)(2,1)S(1)}, u32[]{:S(2)}, u32[]{:S(2)}) collective-permute-start(bf16[64,1152]{1,0:T(8,128)(2,1)S(1)} %get-tuple-element.29), channel_id=1, source_target_pairs={{0,8},{8,0},{16,24},{24,16},{1,9},{9,1},{17,25},{25,17},{2,10},{10... | collective-permute-start | bytes 442376 | tf_op jit(solution)/shard_map/ppermute | solution.py:188
  25.3 1.5 %collective-permute-start.7 = (bf16[64,1152]{1,0:T(8,128)(2,1)S(1)}, bf16[64,1152]{1,0:T(8,128)(2,1)S(1)}, u32[]{:S(2)}, u32[]{:S(2)}) collective-permute-start(bf16[64,1152]{1,0:T(8,128)(2,1)S(1)} %get-tuple-element.30), channel_id=1, source_target_pairs={{0,16},{8,24},{16,0},{24,8},{1,17},{9,25},{17,1},{25,9},{2,18},{10... | collective-permute-start | bytes 442376 | tf_op jit(solution)/shard_map/ppermute | solution.py:188
  26.8 0.5 %collective-permute-start.8 = (bf16[64,1152]{1,0:T(8,128)(2,1)S(1)}, bf16[64,1152]{1,0:T(8,128)(2,1)S(1)}, u32[]{:S(2)}, u32[]{:S(2)}) collective-permute-start(bf16[64,1152]{1,0:T(8,128)(2,1)S(1)} %get-tuple-element.31), channel_id=1, source_target_pairs={{0,24},{8,16},{16,8},{24,0},{1,25},{9,17},{17,9},{25,1},{2,26},{10... | collective-permute-start | bytes 442376 | tf_op jit(solution)/shard_map/ppermute | solution.py:188
  27.3 5.2 %collective-permute-done.12.got.refs_4_ = bf16[128,1152]{1,0:T(8,128)(2,1)S(1)} collective-permute-done((bf16[128,1152]{1,0:T(8,128)(2,1)S(1)}, bf16[128,1152]{1,0:T(8,128)(2,1)S(1)}, u32[]{:S(2)}, u32[]{:S(2)}) %collective-permute-start.12) | collective-permute-done | bytes 294944 | tf_op jit(solution)/shard_map/ppermute | solution.py:188
  32.5 1.4 %collective-permute-start.13 = (bf16[64,1152]{1,0:T(8,128)(2,1)S(1)}, bf16[64,1152]{1,0:T(8,128)(2,1)S(1)}, u32[]{:S(2)}, u32[]{:S(2)}) collective-permute-start(bf16[64,1152]{1,0:T(8,128)(2,1)S(1)} %shard_map.73), channel_id=1, source_target_pairs={{0,4},{1,5},{2,6},{3,7},{4,0},{5,1},{6,2},{7,3},{8,12},{9,13},{10,... | collective-permute-start | bytes 442376 | tf_op jit(solution)/shard_map/ppermute | solution.py:188
  33.9 0.0 collective-permute-done.6.refs_0_
  33.9 0.2 collective-permute-done.7.refs_1_
  34.1 0.0 collective-permute-done.8.refs_2_
  34.1 0.2 shard_map.72.refs_0_
  34.3 2.3 %collective-permute-start.11 = (bf16[64,1152]{1,0:T(8,128)(2,1)S(1)}, bf16[64,1152]{1,0:T(8,128)(2,1)S(1)}, u32[]{:S(2)}, u32[]{:S(2)}) collective-permute-start(bf16[64,1152]{1,0:T(8,128)(2,1)S(1)} %shard_map.72.refs_0_), channel_id=1, source_target_pairs={{0,24},{8,16},{16,8},{24,0},{1,25},{9,17},{17,9},{25,1},{2,26},{10... | collective-permute-start | bytes 442376 | tf_op jit(solution)/shard_map/ppermute | solution.py:188
  36.6 0.5 %collective-permute-start.10 = (bf16[64,1152]{1,0:T(8,128)(2,1)S(1)}, bf16[64,1152]{1,0:T(8,128)(2,1)S(1)}, u32[]{:S(2)}, u32[]{:S(2)}) collective-permute-start(bf16[64,1152]{1,0:T(8,128)(2,1)S(1)} %shard_map.72.refs_0_), channel_id=1, source_target_pairs={{0,16},{8,24},{16,0},{24,8},{1,17},{9,25},{17,1},{25,9},{2,18},{10... | collective-permute-start | bytes 442376 | tf_op jit(solution)/shard_map/ppermute | solution.py:188
  37.1 0.7 %collective-permute-start.9 = (bf16[64,1152]{1,0:T(8,128)(2,1)S(1)}, bf16[64,1152]{1,0:T(8,128)(2,1)S(1)}, u32[]{:S(2)}, u32[]{:S(2)}) collective-permute-start(bf16[64,1152]{1,0:T(8,128)(2,1)S(1)} %shard_map.72.refs_0_), channel_id=1, source_target_pairs={{0,8},{8,0},{16,24},{24,16},{1,9},{9,1},{17,25},{25,17},{2,10},{10... | collective-permute-start | bytes 442376 | tf_op jit(solution)/shard_map/ppermute | solution.py:188
  37.8 4.2 %collective-permute-done.13.refs_5_ = bf16[64,1152]{1,0:T(8,128)(2,1)S(1)} collective-permute-done((bf16[64,1152]{1,0:T(8,128)(2,1)S(1)}, bf16[64,1152]{1,0:T(8,128)(2,1)S(1)}, u32[]{:S(2)}, u32[]{:S(2)}) %collective-permute-start.13) | collective-permute-done | bytes 147488 | tf_op jit(solution)/shard_map/ppermute | solution.py:188
  42.0 0.0 collective-permute-done.11.refs_3_
  42.1 1.6 %collective-permute-done.10.refs_2_ = bf16[64,1152]{1,0:T(8,128)(2,1)S(1)} collective-permute-done((bf16[64,1152]{1,0:T(8,128)(2,1)S(1)}, bf16[64,1152]{1,0:T(8,128)(2,1)S(1)}, u32[]{:S(2)}, u32[]{:S(2)}) %collective-permute-start.10) | collective-permute-done | bytes 147488 | tf_op jit(solution)/shard_map/ppermute | solution.py:188
  43.6 0.1 collective-permute-done.9.refs_1_
  43.7 1.3 %shard_map.74 = (f32[256,1152]{1,0:T(8,128)}, f32[64,1152]{1,0:T(8,128)}) custom-call(s32[1]{0:T(128)} %bitcast.place.position, f32[1]{0:T(128)S(6)} %copy.7.scale, f32[64,1152]{1,0:T(8,128)S(1)} %get-tuple-element.18.unit, f32[64,128]{1,0:T(8,128)S(1)} %get-tuple-element.19.inverse, f32[64,1152]{1,0:T(8,128)S(1)} %get-tuple-element.23.own, ...), custom_call_target="tpu_custom_call" | custom-call | flops 737280 | bytes 2359296 | tf_op jit(solution)/shard_map/pallas_call | solution.py:262
  (1 shorter events, 0.0 us)
Async XLA Ops:
  0.6 7.4 %copy-start = (s32[256]{0:T(256)S(1)}, s32[256]{0:T(256)}, u32[]{:S(2)}) copy-start(s32[256]{0:T(256)} %param.7) | copy-start | bytes 3076
  2.2 18.3 %collective-permute-start = (bf16[256,1152]{1,0:T(8,128)(2,1)S(1)}, bf16[256,1152]{1,0:T(8,128)(2,1)S(1)}, u32[]{:S(2)}, u32[]{:S(2)}) collective-permute-start(bf16[256,1152]{1,0:T(8,128)(2,1)S(1)} %get-tuple-element.20.img), channel_id=1, source_target_pairs={{0,1},{1,0},{2,3},{3,2},{4,5},{5,4},{6,7},{7,6},{8,9},{9,8},{10,11... | collective-permute-start | bytes 1769480 | tf_op jit(solution)/shard_map/ppermute | solution.py:188
  2.8 9.4 %collective-permute-start.4 = (bf16[64,1152]{1,0:T(8,128)(2,1)S(1)}, bf16[64,1152]{1,0:T(8,128)(2,1)S(1)}, u32[]{:S(2)}, u32[]{:S(2)}) collective-permute-start(bf16[64,1152]{1,0:T(8,128)(2,1)S(1)} %get-tuple-element.21.refs_0_), channel_id=1, source_target_pairs={{0,6},{1,7},{2,4},{3,5},{4,2},{5,3},{6,0},{7,1},{8,14},{9,15},{10,... | collective-permute-start | bytes 442376 | tf_op jit(solution)/shard_map/ppermute | solution.py:188
  7.4 8.7 %collective-permute-start.3 = (bf16[64,1152]{1,0:T(8,128)(2,1)S(1)}, bf16[64,1152]{1,0:T(8,128)(2,1)S(1)}, u32[]{:S(2)}, u32[]{:S(2)}) collective-permute-start(bf16[64,1152]{1,0:T(8,128)(2,1)S(1)} %get-tuple-element.21.refs_0_), channel_id=1, source_target_pairs={{0,2},{1,3},{2,0},{3,1},{4,6},{5,7},{6,4},{7,5},{8,10},{9,11},{10,... | collective-permute-start | bytes 442376 | tf_op jit(solution)/shard_map/ppermute | solution.py:188
  7.4 13.1 %collective-permute-start.2 = (bf16[64,1152]{1,0:T(8,128)(2,1)S(1)}, bf16[64,1152]{1,0:T(8,128)(2,1)S(1)}, u32[]{:S(2)}, u32[]{:S(2)}) collective-permute-start(bf16[64,1152]{1,0:T(8,128)(2,1)S(1)} %get-tuple-element.21.refs_0_), channel_id=1, source_target_pairs={{0,4},{1,5},{2,6},{3,7},{4,0},{5,1},{6,2},{7,3},{8,12},{9,13},{10,... | collective-permute-start | bytes 442376 | tf_op jit(solution)/shard_map/ppermute | solution.py:188
  8.1 1.3 %collective-permute-start.1 = (s32[1,256]{1,0:T(1,128)S(1)}, s32[1,256]{1,0:T(1,128)S(1)}, u32[]{:S(2)}, u32[]{:S(2)}) collective-permute-start(s32[1,256]{1,0:T(1,128)S(1)} %bitcast.3), channel_id=1, source_target_pairs={{0,1},{1,0},{2,3},{3,2},{4,5},{5,4},{6,7},{7,6},{8,9},{9,8},{10,11... | collective-permute-start | bytes 3080 | tf_op jit(solution)/shard_map/ppermute | solution.py:188
  21.5 2.1 %collective-permute-start.5 = (bf16[256,1152]{1,0:T(8,128)(2,1)S(1)}, bf16[256,1152]{1,0:T(8,128)(2,1)S(1)}, u32[]{:S(2)}, u32[]{:S(2)}) collective-permute-start(bf16[256,1152]{1,0:T(8,128)(2,1)S(1)} %get-tuple-element.27), channel_id=1, source_target_pairs={{0,1},{1,0},{2,3},{3,2},{4,5},{5,4},{6,7},{7,6},{8,9},{9,8},{10,11... | collective-permute-start | bytes 1769480 | tf_op jit(solution)/shard_map/ppermute | solution.py:188
  23.0 9.5 %collective-permute-start.12 = (bf16[128,1152]{1,0:T(8,128)(2,1)S(1)}, bf16[128,1152]{1,0:T(8,128)(2,1)S(1)}, u32[]{:S(2)}, u32[]{:S(2)}) collective-permute-start(bf16[128,1152]{1,0:T(8,128)(2,1)S(1)} %get-tuple-element.32), channel_id=1, source_target_pairs={{0,2},{1,3},{2,0},{3,1},{4,6},{5,7},{6,4},{7,5},{8,10},{9,11},{10,... | collective-permute-start | bytes 884744 | tf_op jit(solution)/shard_map/ppermute | solution.py:188
  23.8 10.1 %collective-permute-start.6 = (bf16[64,1152]{1,0:T(8,128)(2,1)S(1)}, bf16[64,1152]{1,0:T(8,128)(2,1)S(1)}, u32[]{:S(2)}, u32[]{:S(2)}) collective-permute-start(bf16[64,1152]{1,0:T(8,128)(2,1)S(1)} %get-tuple-element.29), channel_id=1, source_target_pairs={{0,8},{8,0},{16,24},{24,16},{1,9},{9,1},{17,25},{25,17},{2,10},{10... | collective-permute-start | bytes 442376 | tf_op jit(solution)/shard_map/ppermute | solution.py:188
  25.3 8.8 %collective-permute-start.7 = (bf16[64,1152]{1,0:T(8,128)(2,1)S(1)}, bf16[64,1152]{1,0:T(8,128)(2,1)S(1)}, u32[]{:S(2)}, u32[]{:S(2)}) collective-permute-start(bf16[64,1152]{1,0:T(8,128)(2,1)S(1)} %get-tuple-element.30), channel_id=1, source_target_pairs={{0,16},{8,24},{16,0},{24,8},{1,17},{9,25},{17,1},{25,9},{2,18},{10... | collective-permute-start | bytes 442376 | tf_op jit(solution)/shard_map/ppermute | solution.py:188
  26.8 7.3 %collective-permute-start.8 = (bf16[64,1152]{1,0:T(8,128)(2,1)S(1)}, bf16[64,1152]{1,0:T(8,128)(2,1)S(1)}, u32[]{:S(2)}, u32[]{:S(2)}) collective-permute-start(bf16[64,1152]{1,0:T(8,128)(2,1)S(1)} %get-tuple-element.31), channel_id=1, source_target_pairs={{0,24},{8,16},{16,8},{24,0},{1,25},{9,17},{17,9},{25,1},{2,26},{10... | collective-permute-start | bytes 442376 | tf_op jit(solution)/shard_map/ppermute | solution.py:188
  32.5 9.5 %collective-permute-start.13 = (bf16[64,1152]{1,0:T(8,128)(2,1)S(1)}, bf16[64,1152]{1,0:T(8,128)(2,1)S(1)}, u32[]{:S(2)}, u32[]{:S(2)}) collective-permute-start(bf16[64,1152]{1,0:T(8,128)(2,1)S(1)} %shard_map.73), channel_id=1, source_target_pairs={{0,4},{1,5},{2,6},{3,7},{4,0},{5,1},{6,2},{7,3},{8,12},{9,13},{10,... | collective-permute-start | bytes 442376 | tf_op jit(solution)/shard_map/ppermute | solution.py:188
  34.3 7.8 %collective-permute-start.11 = (bf16[64,1152]{1,0:T(8,128)(2,1)S(1)}, bf16[64,1152]{1,0:T(8,128)(2,1)S(1)}, u32[]{:S(2)}, u32[]{:S(2)}) collective-permute-start(bf16[64,1152]{1,0:T(8,128)(2,1)S(1)} %shard_map.72.refs_0_), channel_id=1, source_target_pairs={{0,24},{8,16},{16,8},{24,0},{1,25},{9,17},{17,9},{25,1},{2,26},{10... | collective-permute-start | bytes 442376 | tf_op jit(solution)/shard_map/ppermute | solution.py:188
  36.6 7.0 %collective-permute-start.10 = (bf16[64,1152]{1,0:T(8,128)(2,1)S(1)}, bf16[64,1152]{1,0:T(8,128)(2,1)S(1)}, u32[]{:S(2)}, u32[]{:S(2)}) collective-permute-start(bf16[64,1152]{1,0:T(8,128)(2,1)S(1)} %shard_map.72.refs_0_), channel_id=1, source_target_pairs={{0,16},{8,24},{16,0},{24,8},{1,17},{9,25},{17,1},{25,9},{2,18},{10... | collective-permute-start | bytes 442376 | tf_op jit(solution)/shard_map/ppermute | solution.py:188
  37.1 6.5 %collective-permute-start.9 = (bf16[64,1152]{1,0:T(8,128)(2,1)S(1)}, bf16[64,1152]{1,0:T(8,128)(2,1)S(1)}, u32[]{:S(2)}, u32[]{:S(2)}) collective-permute-start(bf16[64,1152]{1,0:T(8,128)(2,1)S(1)} %shard_map.72.refs_0_), channel_id=1, source_target_pairs={{0,8},{8,0},{16,24},{24,16},{1,9},{9,1},{17,25},{25,17},{2,10},{10... | collective-permute-start | bytes 442376 | tf_op jit(solution)/shard_map/ppermute | solution.py:188

commit v6 on v5

--- a/solution.py
+++ b/solution.py
@@ -109,23 +109,24 @@
 
 
 def own_body(order, line, place, column, scale, shift, perm, img, img_other, kept, *refs):
-    *txt, own_sum, own_txt, even_txt, odd_txt = refs
+    *txt, own_sum, own_txt, even_txt, near_txt, odd_txt = refs
     rows = own_txt.shape[0]
     tile = joined(txt)
     weights = weights_of(tile, order, line, place, column, scale, shift, perm[...], img[...])
     own_sum[...] = to_images(weights, tile)
     to_txt = to_texts(weights, img[...]) + to_texts(kept[...], img_other[...])
-    half = odd_txt.shape[0]
+    half = rows + even_txt.shape[0]
     own_txt[...] = to_txt[:rows]
     even_txt[...] = to_txt[rows:half]
-    odd_txt[...] = to_txt[half:].astype(BF16)
+    near_txt[...] = to_txt[half : half + rows].astype(BF16)
+    odd_txt[...] = to_txt[half + rows :].astype(BF16)
 
 
 def add_body(even, got, *outs):
     rows = outs[0].shape[0]
     for k, out in enumerate(outs):
         mine = even[k * rows : (k + 1) * rows, :]
-        out[...] = (mine + got[(k + 1) * rows : (k + 2) * rows, :].astype(F32)).astype(BF16)
+        out[...] = (mine + got[k * rows : (k + 1) * rows, :].astype(F32)).astype(BF16)
 
 
 def split_body(count, position, own, other, keep, *send):
@@ -174,9 +175,7 @@
             )
         )
         copies[-1].start()
-    rows = unit.shape[0]
-    total = total_of(own, back[1:]) + back[0][:rows, :].astype(F32)
-    txt_held[...] = backward_unit(unit[...], inverse[...], scale[0] * total)
+    txt_held[...] = backward_unit(unit[...], inverse[...], scale[0] * total_of(own, back))
     copies.append(pltpu.make_async_copy(txt_held, txt_out, sems.at[count]))
     copies[-1].start()
     for copy in copies:
@@ -202,7 +201,9 @@
     txt_bf, img_bf, txt_unit, img_unit, txt_inv, img_inv = unit_rows(place, texts, images, part)
     half = blocks // 2
     order = list(range(0, blocks, 2)) + list(range(1, blocks, 2))
-    tiles = [txt_bf] + [swapped(txt_bf, "txt", 2 * k) for k in order[1:]]
+    far = [swapped(txt_bf, "txt", 4 * k) for k in range(1, half)]
+    near = [swapped(tile, "txt", 2) for tile in [txt_bf] + far]
+    tiles = [txt_bf] + far + near
     perm_other = swapped(perm_row, "txt", 1)
     img_other = swapped(img_bf, "txt", 1)
     scalars = [place, column, scale, shift]
@@ -216,29 +217,29 @@
         2 * pairs,
     )
     from_other = swapped(other_img, "txt", 1)
-    own_img, own_txt, even_txt, odd_txt = call(
+    own_img, own_txt, even_txt, near_txt, odd_txt = call(
         functools.partial(own_body, order, line),
         [
             struct(rows, width, F32),
             struct(txt_rows, width, F32),
             struct((half - 1) * txt_rows, width, F32),
-            struct(half * txt_rows, width, BF16),
+            struct(txt_rows, width, BF16),
+            struct((half - 1) * txt_rows, width, BF16),
         ],
         [*scalars, perm_row, img_bf, img_other, kept, *tiles],
         [SMEM] * 4 + [VMEM] * (4 + blocks),
         40 << 20,
         4 * pairs,
     )
-    near = swapped(odd_txt, "txt", 2)
     sums = call(
         add_body,
         [struct(txt_rows, width, BF16)] * (half - 1),
-        [even_txt, near],
+        [even_txt, swapped(odd_txt, "txt", 2)],
         [VMEM] * 2,
         24 << 20,
         rows * width,
     )
-    back = [near] + [swapped(sums[k - 1], "txt", 4 * k) for k in range(1, half)]
+    back = [swapped(near_txt, "txt", 2)] + [swapped(sums[k - 1], "txt", 4 * k) for k in range(1, half)]
 
     keep, *send = call(
         functools.partial(split_body, count),

time: 45.1 us -> 44.4 us (0.984)
  waiting for transfers between devices: 22.9 us -> 18.3 us
  starting transfers between devices: 14.5 us -> 18.3 us
    ppermute x14 -> x15, waiting for transfers between devices: 22.9 us -> 18.3 us  [swapped(): return lax.ppermute(value, axis, [(s, s ^ step) for s in range(count)])]
    ppermute x14 -> x15, starting transfers between devices: 14.5 us -> 18.3 us  [swapped(): return lax.ppermute(value, axis, [(s, s ^ step) for s in range(count)])]
  transfers between devices with their start and end apart: 14 -> 15, of which waited for: 9 -> 7; matrix products, arithmetic and copies ran while one was open for 0% -> 0% of each run, Pallas kernels for 4% -> 4%
where the time goes in v6:
time: 44.4 us; the launch traced here: 44.2 us
  starting transfers between devices  18.3 us (41%)
  waiting for transfers between devices  18.3 us (41%)
  Pallas kernels  5.63 us (13%)
  between operations  2.02 us (5%)
    ppermute x15, starting transfers between devices, swapped(): return lax.ppermute(value, axis, [(s, s ^ step) for s in range(count)])  18.3 us
    ppermute x15, waiting for transfers between devices, swapped(): return lax.ppermute(value, axis, [(s, s ^ step) for s in range(count)])  18.3 us
    pallas_call x5, Pallas kernels, call(): pl.pallas_call(body, out_shape=outs, in_specs=specs, out_specs=[VMEM] * l...  2.77 us
    pallas_call x1, Pallas kernels, unit_rows(): pl.pallas_call(unit_body, out_shape=[struct(*size, BF16) for size in size...  1.58 us
    pallas_call x1, Pallas kernels, local(): pl.pallas_call(functools.partial(last_body, count), out_shape=[struct(row...  1.28 us
  transfers between devices with their start and end apart: 15, of which 7 were waited for; matrix products, arithmetic and copies ran while one was open for 0% of the time, Pallas kernels for 4%

profile of v6, /device:TPU:0, one launch (start us, length us, event | category | flops | bytes accessed | tf_op | source)
XLA Modules:
  0.0 44.2 jit_solution(1266837949247431719)
XLA Ops:
  0.6 0.0 copy-start
  0.6 1.6 %shard_map.68 = (bf16[64,1152]{1,0:T(8,128)(2,1)S(1)}, bf16[256,1152]{1,0:T(8,128)(2,1)S(1)}, f32[64,1152]{1,0:T(8,128)S(1)}, f32[64,1152]{1,0:T(8,128)S(1)}, f3...) custom-call(s32[1]{0:T(128)} %bitcast.place.position, f32[64,1152]{1,0:T(8,128)} %txt.1, f32[256,1152]{1,0:T(8,128)} %img.1), custom_call_target="tpu_custom_call" | custom-call | flops 1474560 | bytes 2211840 | tf_op jit(solution)/shard_map/pallas_call | solution.py:22
  2.2 0.5 %collective-permute-start = (bf16[256,1152]{1,0:T(8,128)(2,1)S(1)}, bf16[256,1152]{1,0:T(8,128)(2,1)S(1)}, u32[]{:S(2)}, u32[]{:S(2)}) collective-permute-start(bf16[256,1152]{1,0:T(8,128)(2,1)S(1)} %get-tuple-element.21.img), channel_id=1, source_target_pairs={{0,1},{1,0},{2,3},{3,2},{4,5},{5,4},{6,7},{7,6},{8,9},{9,8},{10,11... | collective-permute-start | bytes 1769480 | tf_op jit(solution)/shard_map/ppermute | solution.py:187
  2.8 3.7 %collective-permute-start.2 = (bf16[64,1152]{1,0:T(8,128)(2,1)S(1)}, bf16[64,1152]{1,0:T(8,128)(2,1)S(1)}, u32[]{:S(2)}, u32[]{:S(2)}) collective-permute-start(bf16[64,1152]{1,0:T(8,128)(2,1)S(1)} %get-tuple-element.22.refs_0_), channel_id=1, source_target_pairs={{0,4},{1,5},{2,6},{3,7},{4,0},{5,1},{6,2},{7,3},{8,12},{9,13},{10,... | collective-permute-start | bytes 442376 | tf_op jit(solution)/shard_map/ppermute | solution.py:187
  6.4 1.6 %collective-permute-start.3 = (bf16[64,1152]{1,0:T(8,128)(2,1)S(1)}, bf16[64,1152]{1,0:T(8,128)(2,1)S(1)}, u32[]{:S(2)}, u32[]{:S(2)}) collective-permute-start(bf16[64,1152]{1,0:T(8,128)(2,1)S(1)} %get-tuple-element.22.refs_0_), channel_id=1, source_target_pairs={{0,2},{1,3},{2,0},{3,1},{4,6},{5,7},{6,4},{7,5},{8,10},{9,11},{10,... | collective-permute-start | bytes 442376 | tf_op jit(solution)/shard_map/ppermute | solution.py:187
  8.0 6.1 %collective-permute-done.2.refs_1_ = bf16[64,1152]{1,0:T(8,128)(2,1)S(1)} collective-permute-done((bf16[64,1152]{1,0:T(8,128)(2,1)S(1)}, bf16[64,1152]{1,0:T(8,128)(2,1)S(1)}, u32[]{:S(2)}, u32[]{:S(2)}) %collective-permute-start.2) | collective-permute-done | bytes 147488 | tf_op jit(solution)/shard_map/ppermute | solution.py:187
  14.1 0.6 %collective-permute-start.4 = (bf16[64,1152]{1,0:T(8,128)(2,1)S(1)}, bf16[64,1152]{1,0:T(8,128)(2,1)S(1)}, u32[]{:S(2)}, u32[]{:S(2)}) collective-permute-start(bf16[64,1152]{1,0:T(8,128)(2,1)S(1)} %collective-permute-done.2.refs_1_), channel_id=1, source_target_pairs={{0,2},{1,3},{2,0},{3,1},{4,6},{5,7},{6,4},{7,5},{8,10},{9,11},{10,... | collective-permute-start | bytes 442376 | tf_op jit(solution)/shard_map/ppermute | solution.py:187
  14.8 0.0 copy-done
  14.8 0.0 collective-permute-start.1
  16.1 0.0 collective-permute-done.1.perm
  16.1 0.0 collective-permute-done.3.refs_2_
  16.1 3.6 %collective-permute-done.4.refs_3_ = bf16[64,1152]{1,0:T(8,128)(2,1)S(1)} collective-permute-done((bf16[64,1152]{1,0:T(8,128)(2,1)S(1)}, bf16[64,1152]{1,0:T(8,128)(2,1)S(1)}, u32[]{:S(2)}, u32[]{:S(2)}) %collective-permute-start.4) | collective-permute-done | bytes 147488 | tf_op jit(solution)/shard_map/ppermute | solution.py:187
  19.7 0.0 collective-permute-done.img.img_other
  19.7 1.0 %shard_map.69 = (bf16[256,256]{1,0:T(8,128)(2,1)S(1)}, bf16[256,1152]{1,0:T(8,128)(2,1)S(1)}) custom-call(s32[1]{0:T(128)} %bitcast.place.position, s32[1]{0:T(128)} %bitcast.1.column, f32[1]{0:T(128)S(6)} %copy.7.scale, f32[1]{0:T(128)S(6)} %copy.8.shift, s32[1,256]{1,0:T(1,128)S(1)} %collective-permute-done.1.perm, ...), custom_call_target="tpu_custom_call" | custom-call | flops 301989888 | bytes 1901584 | tf_op jit(solution)/shard_map/pallas_call | solution.py:38
  20.7 0.1 collective-permute-start.5
  20.8 1.4 %shard_map.70 = (f32[256,1152]{1,0:T(8,128)S(1)}, f32[64,1152]{1,0:T(8,128)S(1)}, f32[64,1152]{1,0:T(8,128)S(1)}, bf16[64,1152]{1,0:T(8,128)(2,1)S(1)}, bf16[64,1152]{1,0:T(8,128)(2,1)S(1)}) custom-call(s32[1]{0:T(128)} %bitcast.place.position, s32[1]{0:T(128)} %bitcast.1.column, f32[1]{0:T(128)S(6)} %copy.7.scale, f32[1]{0:T(128)S(6)} %copy.8.shift, ...), custom_call_target="tpu_custom_call" | custom-call | flops 603979776 | bytes 3965968 | tf_op jit(solution)/shard_map/pallas_call | solution.py:38
  22.2 1.0 %collective-permute-start.13 = (bf16[64,1152]{1,0:T(8,128)(2,1)S(1)}, bf16[64,1152]{1,0:T(8,128)(2,1)S(1)}, u32[]{:S(2)}, u32[]{:S(2)}) collective-permute-start(bf16[64,1152]{1,0:T(8,128)(2,1)S(1)} %get-tuple-element.35), channel_id=1, source_target_pairs={{0,2},{1,3},{2,0},{3,1},{4,6},{5,7},{6,4},{7,5},{8,10},{9,11},{10,... | collective-permute-start | bytes 442376 | tf_op jit(solution)/shard_map/ppermute | solution.py:187
  23.2 0.0 collective-permute-done.5.other
  23.2 0.1 shard_map.71
  23.3 1.6 %collective-permute-start.6 = (bf16[64,1152]{1,0:T(8,128)(2,1)S(1)}, bf16[64,1152]{1,0:T(8,128)(2,1)S(1)}, u32[]{:S(2)}, u32[]{:S(2)}) collective-permute-start(bf16[64,1152]{1,0:T(8,128)(2,1)S(1)} %get-tuple-element.30), channel_id=1, source_target_pairs={{0,8},{8,0},{16,24},{24,16},{1,9},{9,1},{17,25},{25,17},{2,10},{10... | collective-permute-start | bytes 442376 | tf_op jit(solution)/shard_map/ppermute | solution.py:187
  24.9 1.5 %collective-permute-start.7 = (bf16[64,1152]{1,0:T(8,128)(2,1)S(1)}, bf16[64,1152]{1,0:T(8,128)(2,1)S(1)}, u32[]{:S(2)}, u32[]{:S(2)}) collective-permute-start(bf16[64,1152]{1,0:T(8,128)(2,1)S(1)} %get-tuple-element.31), channel_id=1, source_target_pairs={{0,16},{8,24},{16,0},{24,8},{1,17},{9,25},{17,1},{25,9},{2,18},{10... | collective-permute-start | bytes 442376 | tf_op jit(solution)/shard_map/ppermute | solution.py:187
  26.4 0.5 %collective-permute-start.8 = (bf16[64,1152]{1,0:T(8,128)(2,1)S(1)}, bf16[64,1152]{1,0:T(8,128)(2,1)S(1)}, u32[]{:S(2)}, u32[]{:S(2)}) collective-permute-start(bf16[64,1152]{1,0:T(8,128)(2,1)S(1)} %get-tuple-element.32), channel_id=1, source_target_pairs={{0,24},{8,16},{16,8},{24,0},{1,25},{9,17},{17,9},{25,1},{2,26},{10... | collective-permute-start | bytes 442376 | tf_op jit(solution)/shard_map/ppermute | solution.py:187
  26.9 1.1 %collective-permute-start.12 = (bf16[64,1152]{1,0:T(8,128)(2,1)S(1)}, bf16[64,1152]{1,0:T(8,128)(2,1)S(1)}, u32[]{:S(2)}, u32[]{:S(2)}) collective-permute-start(bf16[64,1152]{1,0:T(8,128)(2,1)S(1)} %get-tuple-element.33), channel_id=1, source_target_pairs={{0,2},{1,3},{2,0},{3,1},{4,6},{5,7},{6,4},{7,5},{8,10},{9,11},{10,... | collective-permute-start | bytes 442376 | tf_op jit(solution)/shard_map/ppermute | solution.py:187
  28.0 0.5 %collective-permute-done.13.got = bf16[64,1152]{1,0:T(8,128)(2,1)S(1)} collective-permute-done((bf16[64,1152]{1,0:T(8,128)(2,1)S(1)}, bf16[64,1152]{1,0:T(8,128)(2,1)S(1)}, u32[]{:S(2)}, u32[]{:S(2)}) %collective-permute-start.13) | collective-permute-done | bytes 147488 | tf_op jit(solution)/shard_map/ppermute | solution.py:187
  28.5 2.6 %collective-permute-start.14 = (bf16[64,1152]{1,0:T(8,128)(2,1)S(1)}, bf16[64,1152]{1,0:T(8,128)(2,1)S(1)}, u32[]{:S(2)}, u32[]{:S(2)}) collective-permute-start(bf16[64,1152]{1,0:T(8,128)(2,1)S(1)} %shard_map.73), channel_id=1, source_target_pairs={{0,4},{1,5},{2,6},{3,7},{4,0},{5,1},{6,2},{7,3},{8,12},{9,13},{10,... | collective-permute-start | bytes 442376 | tf_op jit(solution)/shard_map/ppermute | solution.py:187
  31.1 0.0 collective-permute-done.6.refs_0_
  31.1 2.6 %collective-permute-done.7.refs_1_ = bf16[64,1152]{1,0:T(8,128)(2,1)S(1)} collective-permute-done((bf16[64,1152]{1,0:T(8,128)(2,1)S(1)}, bf16[64,1152]{1,0:T(8,128)(2,1)S(1)}, u32[]{:S(2)}, u32[]{:S(2)}) %collective-permute-start.7) | collective-permute-done | bytes 147488 | tf_op jit(solution)/shard_map/ppermute | solution.py:187
  33.7 0.0 collective-permute-done.8.refs_2_
  33.7 0.2 shard_map.72.refs_0_
  33.9 1.6 %collective-permute-start.11 = (bf16[64,1152]{1,0:T(8,128)(2,1)S(1)}, bf16[64,1152]{1,0:T(8,128)(2,1)S(1)}, u32[]{:S(2)}, u32[]{:S(2)}) collective-permute-start(bf16[64,1152]{1,0:T(8,128)(2,1)S(1)} %shard_map.72.refs_0_), channel_id=1, source_target_pairs={{0,24},{8,16},{16,8},{24,0},{1,25},{9,17},{17,9},{25,1},{2,26},{10... | collective-permute-start | bytes 442376 | tf_op jit(solution)/shard_map/ppermute | solution.py:187
  35.4 1.2 %collective-permute-start.10 = (bf16[64,1152]{1,0:T(8,128)(2,1)S(1)}, bf16[64,1152]{1,0:T(8,128)(2,1)S(1)}, u32[]{:S(2)}, u32[]{:S(2)}) collective-permute-start(bf16[64,1152]{1,0:T(8,128)(2,1)S(1)} %shard_map.72.refs_0_), channel_id=1, source_target_pairs={{0,16},{8,24},{16,0},{24,8},{1,17},{9,25},{17,1},{25,9},{2,18},{10... | collective-permute-start | bytes 442376 | tf_op jit(solution)/shard_map/ppermute | solution.py:187
  36.7 0.8 %collective-permute-start.9 = (bf16[64,1152]{1,0:T(8,128)(2,1)S(1)}, bf16[64,1152]{1,0:T(8,128)(2,1)S(1)}, u32[]{:S(2)}, u32[]{:S(2)}) collective-permute-start(bf16[64,1152]{1,0:T(8,128)(2,1)S(1)} %shard_map.72.refs_0_), channel_id=1, source_target_pairs={{0,8},{8,0},{16,24},{24,16},{1,9},{9,1},{17,25},{25,17},{2,10},{10... | collective-permute-start | bytes 442376 | tf_op jit(solution)/shard_map/ppermute | solution.py:187
  37.4 0.0 collective-permute-done.12.refs_4_
  37.5 0.7 %collective-permute-done.14.refs_5_ = bf16[64,1152]{1,0:T(8,128)(2,1)S(1)} collective-permute-done((bf16[64,1152]{1,0:T(8,128)(2,1)S(1)}, bf16[64,1152]{1,0:T(8,128)(2,1)S(1)}, u32[]{:S(2)}, u32[]{:S(2)}) %collective-permute-start.14) | collective-permute-done | bytes 147488 | tf_op jit(solution)/shard_map/ppermute | solution.py:187
  38.2 3.2 %collective-permute-done.11.refs_3_ = bf16[64,1152]{1,0:T(8,128)(2,1)S(1)} collective-permute-done((bf16[64,1152]{1,0:T(8,128)(2,1)S(1)}, bf16[64,1152]{1,0:T(8,128)(2,1)S(1)}, u32[]{:S(2)}, u32[]{:S(2)}) %collective-permute-start.11) | collective-permute-done | bytes 147488 | tf_op jit(solution)/shard_map/ppermute | solution.py:187
  41.4 1.6 %collective-permute-done.10.refs_2_ = bf16[64,1152]{1,0:T(8,128)(2,1)S(1)} collective-permute-done((bf16[64,1152]{1,0:T(8,128)(2,1)S(1)}, bf16[64,1152]{1,0:T(8,128)(2,1)S(1)}, u32[]{:S(2)}, u32[]{:S(2)}) %collective-permute-start.10) | collective-permute-done | bytes 147488 | tf_op jit(solution)/shard_map/ppermute | solution.py:187
  42.9 0.0 collective-permute-done.9.refs_1_
  42.9 1.3 %shard_map.74 = (f32[256,1152]{1,0:T(8,128)}, f32[64,1152]{1,0:T(8,128)}) custom-call(s32[1]{0:T(128)} %bitcast.place.position, f32[1]{0:T(128)S(6)} %copy.7.scale, f32[64,1152]{1,0:T(8,128)S(1)} %get-tuple-element.19.unit, f32[64,128]{1,0:T(8,128)S(1)} %get-tuple-element.20.inverse, f32[64,1152]{1,0:T(8,128)S(1)} %get-tuple-element.24.own, ...), custom_call_target="tpu_custom_call" | custom-call | flops 737280 | bytes 2359296 | tf_op jit(solution)/shard_map/pallas_call | solution.py:263
  (1 shorter events, 0.0 us)
Async XLA Ops:
  0.6 14.1 %copy-start = (s32[256]{0:T(256)S(1)}, s32[256]{0:T(256)}, u32[]{:S(2)}) copy-start(s32[256]{0:T(256)} %param.7) | copy-start | bytes 3076
  2.2 17.4 %collective-permute-start = (bf16[256,1152]{1,0:T(8,128)(2,1)S(1)}, bf16[256,1152]{1,0:T(8,128)(2,1)S(1)}, u32[]{:S(2)}, u32[]{:S(2)}) collective-permute-start(bf16[256,1152]{1,0:T(8,128)(2,1)S(1)} %get-tuple-element.21.img), channel_id=1, source_target_pairs={{0,1},{1,0},{2,3},{3,2},{4,5},{5,4},{6,7},{7,6},{8,9},{9,8},{10,11... | collective-permute-start | bytes 1769480 | tf_op jit(solution)/shard_map/ppermute | solution.py:187
  2.8 11.4 %collective-permute-start.2 = (bf16[64,1152]{1,0:T(8,128)(2,1)S(1)}, bf16[64,1152]{1,0:T(8,128)(2,1)S(1)}, u32[]{:S(2)}, u32[]{:S(2)}) collective-permute-start(bf16[64,1152]{1,0:T(8,128)(2,1)S(1)} %get-tuple-element.22.refs_0_), channel_id=1, source_target_pairs={{0,4},{1,5},{2,6},{3,7},{4,0},{5,1},{6,2},{7,3},{8,12},{9,13},{10,... | collective-permute-start | bytes 442376 | tf_op jit(solution)/shard_map/ppermute | solution.py:187
  6.4 9.7 %collective-permute-start.3 = (bf16[64,1152]{1,0:T(8,128)(2,1)S(1)}, bf16[64,1152]{1,0:T(8,128)(2,1)S(1)}, u32[]{:S(2)}, u32[]{:S(2)}) collective-permute-start(bf16[64,1152]{1,0:T(8,128)(2,1)S(1)} %get-tuple-element.22.refs_0_), channel_id=1, source_target_pairs={{0,2},{1,3},{2,0},{3,1},{4,6},{5,7},{6,4},{7,5},{8,10},{9,11},{10,... | collective-permute-start | bytes 442376 | tf_op jit(solution)/shard_map/ppermute | solution.py:187
  14.1 5.5 %collective-permute-start.4 = (bf16[64,1152]{1,0:T(8,128)(2,1)S(1)}, bf16[64,1152]{1,0:T(8,128)(2,1)S(1)}, u32[]{:S(2)}, u32[]{:S(2)}) collective-permute-start(bf16[64,1152]{1,0:T(8,128)(2,1)S(1)} %collective-permute-done.2.refs_1_), channel_id=1, source_target_pairs={{0,2},{1,3},{2,0},{3,1},{4,6},{5,7},{6,4},{7,5},{8,10},{9,11},{10,... | collective-permute-start | bytes 442376 | tf_op jit(solution)/shard_map/ppermute | solution.py:187
  14.8 1.3 %collective-permute-start.1 = (s32[1,256]{1,0:T(1,128)S(1)}, s32[1,256]{1,0:T(1,128)S(1)}, u32[]{:S(2)}, u32[]{:S(2)}) collective-permute-start(s32[1,256]{1,0:T(1,128)S(1)} %bitcast.3), channel_id=1, source_target_pairs={{0,1},{1,0},{2,3},{3,2},{4,5},{5,4},{6,7},{7,6},{8,9},{9,8},{10,11... | collective-permute-start | bytes 3080 | tf_op jit(solution)/shard_map/ppermute | solution.py:187
  20.7 2.5 %collective-permute-start.5 = (bf16[256,1152]{1,0:T(8,128)(2,1)S(1)}, bf16[256,1152]{1,0:T(8,128)(2,1)S(1)}, u32[]{:S(2)}, u32[]{:S(2)}) collective-permute-start(bf16[256,1152]{1,0:T(8,128)(2,1)S(1)} %get-tuple-element.28), channel_id=1, source_target_pairs={{0,1},{1,0},{2,3},{3,2},{4,5},{5,4},{6,7},{7,6},{8,9},{9,8},{10,11... | collective-permute-start | bytes 1769480 | tf_op jit(solution)/shard_map/ppermute | solution.py:187
  22.2 6.3 %collective-permute-start.13 = (bf16[64,1152]{1,0:T(8,128)(2,1)S(1)}, bf16[64,1152]{1,0:T(8,128)(2,1)S(1)}, u32[]{:S(2)}, u32[]{:S(2)}) collective-permute-start(bf16[64,1152]{1,0:T(8,128)(2,1)S(1)} %get-tuple-element.35), channel_id=1, source_target_pairs={{0,2},{1,3},{2,0},{3,1},{4,6},{5,7},{6,4},{7,5},{8,10},{9,11},{10,... | collective-permute-start | bytes 442376 | tf_op jit(solution)/shard_map/ppermute | solution.py:187
  23.3 7.8 %collective-permute-start.6 = (bf16[64,1152]{1,0:T(8,128)(2,1)S(1)}, bf16[64,1152]{1,0:T(8,128)(2,1)S(1)}, u32[]{:S(2)}, u32[]{:S(2)}) collective-permute-start(bf16[64,1152]{1,0:T(8,128)(2,1)S(1)} %get-tuple-element.30), channel_id=1, source_target_pairs={{0,8},{8,0},{16,24},{24,16},{1,9},{9,1},{17,25},{25,17},{2,10},{10... | collective-permute-start | bytes 442376 | tf_op jit(solution)/shard_map/ppermute | solution.py:187
  24.9 8.8 %collective-permute-start.7 = (bf16[64,1152]{1,0:T(8,128)(2,1)S(1)}, bf16[64,1152]{1,0:T(8,128)(2,1)S(1)}, u32[]{:S(2)}, u32[]{:S(2)}) collective-permute-start(bf16[64,1152]{1,0:T(8,128)(2,1)S(1)} %get-tuple-element.31), channel_id=1, source_target_pairs={{0,16},{8,24},{16,0},{24,8},{1,17},{9,25},{17,1},{25,9},{2,18},{10... | collective-permute-start | bytes 442376 | tf_op jit(solution)/shard_map/ppermute | solution.py:187
  26.4 7.3 %collective-permute-start.8 = (bf16[64,1152]{1,0:T(8,128)(2,1)S(1)}, bf16[64,1152]{1,0:T(8,128)(2,1)S(1)}, u32[]{:S(2)}, u32[]{:S(2)}) collective-permute-start(bf16[64,1152]{1,0:T(8,128)(2,1)S(1)} %get-tuple-element.32), channel_id=1, source_target_pairs={{0,24},{8,16},{16,8},{24,0},{1,25},{9,17},{17,9},{25,1},{2,26},{10... | collective-permute-start | bytes 442376 | tf_op jit(solution)/shard_map/ppermute | solution.py:187
  26.9 10.6 %collective-permute-start.12 = (bf16[64,1152]{1,0:T(8,128)(2,1)S(1)}, bf16[64,1152]{1,0:T(8,128)(2,1)S(1)}, u32[]{:S(2)}, u32[]{:S(2)}) collective-permute-start(bf16[64,1152]{1,0:T(8,128)(2,1)S(1)} %get-tuple-element.33), channel_id=1, source_target_pairs={{0,2},{1,3},{2,0},{3,1},{4,6},{5,7},{6,4},{7,5},{8,10},{9,11},{10,... | collective-permute-start | bytes 442376 | tf_op jit(solution)/shard_map/ppermute | solution.py:187
  28.5 9.6 %collective-permute-start.14 = (bf16[64,1152]{1,0:T(8,128)(2,1)S(1)}, bf16[64,1152]{1,0:T(8,128)(2,1)S(1)}, u32[]{:S(2)}, u32[]{:S(2)}) collective-permute-start(bf16[64,1152]{1,0:T(8,128)(2,1)S(1)} %shard_map.73), channel_id=1, source_target_pairs={{0,4},{1,5},{2,6},{3,7},{4,0},{5,1},{6,2},{7,3},{8,12},{9,13},{10,... | collective-permute-start | bytes 442376 | tf_op jit(solution)/shard_map/ppermute | solution.py:187
  33.9 7.5 %collective-permute-start.11 = (bf16[64,1152]{1,0:T(8,128)(2,1)S(1)}, bf16[64,1152]{1,0:T(8,128)(2,1)S(1)}, u32[]{:S(2)}, u32[]{:S(2)}) collective-permute-start(bf16[64,1152]{1,0:T(8,128)(2,1)S(1)} %shard_map.72.refs_0_), channel_id=1, source_target_pairs={{0,24},{8,16},{16,8},{24,0},{1,25},{9,17},{17,9},{25,1},{2,26},{10... | collective-permute-start | bytes 442376 | tf_op jit(solution)/shard_map/ppermute | solution.py:187
  35.4 7.5 %collective-permute-start.10 = (bf16[64,1152]{1,0:T(8,128)(2,1)S(1)}, bf16[64,1152]{1,0:T(8,128)(2,1)S(1)}, u32[]{:S(2)}, u32[]{:S(2)}) collective-permute-start(bf16[64,1152]{1,0:T(8,128)(2,1)S(1)} %shard_map.72.refs_0_), channel_id=1, source_target_pairs={{0,16},{8,24},{16,0},{24,8},{1,17},{9,25},{17,1},{25,9},{2,18},{10... | collective-permute-start | bytes 442376 | tf_op jit(solution)/shard_map/ppermute | solution.py:187
  36.7 6.3 %collective-permute-start.9 = (bf16[64,1152]{1,0:T(8,128)(2,1)S(1)}, bf16[64,1152]{1,0:T(8,128)(2,1)S(1)}, u32[]{:S(2)}, u32[]{:S(2)}) collective-permute-start(bf16[64,1152]{1,0:T(8,128)(2,1)S(1)} %shard_map.72.refs_0_), channel_id=1, source_target_pairs={{0,8},{8,0},{16,24},{24,16},{1,9},{9,1},{17,25},{25,17},{2,10},{10... | collective-permute-start | bytes 442376 | tf_op jit(solution)/shard_map/ppermute | solution.py:187

commit v7 on v6

--- a/solution.py
+++ b/solution.py
@@ -11,28 +11,15 @@
 F32 = jnp.float32
 BF16 = jnp.bfloat16
 VMEM = pl.BlockSpec(memory_space=pltpu.VMEM)
+ANY = pl.BlockSpec(memory_space=pl.ANY)
 SMEM = pl.BlockSpec(memory_space=pltpu.SMEM)
 
 
-def unit_rows(place, texts, images, part):
-    width = texts.shape[1]
-    sizes = [texts.shape, images.shape]
-    total = texts.size + images.size
-    own = [texts.shape, (part, width)]
-    return pl.pallas_call(
-        unit_body,
-        out_shape=[struct(*size, BF16) for size in sizes]
-        + [struct(*size, F32) for size in own]
-        + [struct(size[0], 128, F32) for size in own],
-        in_specs=[SMEM] + [pl.BlockSpec(memory_space=pl.ANY)] * 2,
-        out_specs=[VMEM] * 6,
-        scratch_shapes=[pltpu.VMEM(size, F32) for size in sizes] + [pltpu.SemaphoreType.DMA((2,))],
-        compiler_params=pltpu.CompilerParams(vmem_limit_bytes=16 << 20),
-        cost_estimate=pl.CostEstimate(flops=4 * total, bytes_accessed=6 * total, transcendentals=0),
-    )(place, *[pltpu.with_memory_space_constraint(v, pltpu.HBM) for v in (texts, images)])
-
-
-def call(body, outs, args, specs, limit, flops):
+def in_hbm(value):
+    return pltpu.with_memory_space_constraint(value, pltpu.HBM)
+
+
+def call(body, outs, args, specs, limit, flops, scratch=()):
     size = sum(a.size * a.dtype.itemsize for a in args)
     size += sum(o.size * o.dtype.itemsize for o in outs)
     return pl.pallas_call(
@@ -40,6 +27,7 @@
         out_shape=outs,
         in_specs=specs,
         out_specs=[VMEM] * len(outs),
+        scratch_shapes=scratch,
         compiler_params=pltpu.CompilerParams(vmem_limit_bytes=limit),
         cost_estimate=pl.CostEstimate(flops=flops, bytes_accessed=size, transcendentals=0),
     )(*args)
@@ -53,28 +41,31 @@
     return lax.rsqrt(jnp.sum(values * values, axis=1, keepdims=True) + EPSILON)
 
 
-def unit_body(
-    place, txt, img, txt_bf, img_bf, txt_unit, img_unit, txt_inv, img_inv, txt_held, img_held, sems
-):
-    txt_copy = pltpu.make_async_copy(txt, txt_held, sems.at[0])
-    img_copy = pltpu.make_async_copy(img, img_held, sems.at[1])
-    txt_copy.start()
-    img_copy.start()
-    txt_copy.wait()
-    values = txt_held[...]
+def unit_txt_body(source, bf, unit_out, inv, held, sem):
+    copy = pltpu.make_async_copy(source, held, sem)
+    copy.start()
+    copy.wait()
+    values = held[...]
     inverse = inverse_norm(values)
     unit = values * inverse
-    txt_bf[...] = unit.astype(BF16)
-    txt_unit[...] = unit
-    txt_inv[...] = jnp.broadcast_to(inverse, txt_inv.shape)
-    img_copy.wait()
-    values = img_held[...]
-    img_bf[...] = (values * inverse_norm(values)).astype(BF16)
-    rows = img_unit.shape[0]
-    values = img_held[pl.ds(pl.multiple_of(place[0] * rows, rows), rows), :]
+    bf[...] = unit.astype(BF16)
+    unit_out[...] = unit
+    inv[...] = jnp.broadcast_to(inverse, inv.shape)
+
+
+def unit_img_body(place, other, source, bf, other_bf, unit_out, inv, held, sem):
+    copy = pltpu.make_async_copy(source, held, sem)
+    copy.start()
+    values = other[...]
+    other_bf[...] = (values * inverse_norm(values)).astype(BF16)
+    copy.wait()
+    values = held[...]
+    bf[...] = (values * inverse_norm(values)).astype(BF16)
+    rows = unit_out.shape[0]
+    values = held[pl.ds(pl.multiple_of(place[0] * rows, rows), rows), :]
     inverse = inverse_norm(values)
-    img_unit[...] = values * inverse
-    img_inv[...] = jnp.broadcast_to(inverse, img_inv.shape)
+    unit_out[...] = values * inverse
+    inv[...] = jnp.broadcast_to(inverse, inv.shape)
 
 
 def weights_of(tile, order, line, place, column, scale, shift, perm, img):
@@ -198,14 +189,31 @@
     place = lax.axis_index("img").reshape(1).astype(jnp.int32)
     perm_row = perm.reshape(1, rows)
 
-    txt_bf, img_bf, txt_unit, img_unit, txt_inv, img_inv = unit_rows(place, texts, images, part)
+    perm_other = swapped(perm_row, "txt", 1)
+    raw_other = swapped(images, "txt", 1)
+    txt_bf, txt_unit, txt_inv = call(
+        unit_txt_body,
+        [struct(txt_rows, width, BF16), struct(txt_rows, width, F32), struct(txt_rows, 128, F32)],
+        [in_hbm(texts)],
+        [ANY],
+        16 << 20,
+        4 * txt_rows * width,
+        [pltpu.VMEM((txt_rows, width), F32), pltpu.SemaphoreType.DMA],
+    )
     half = blocks // 2
     order = list(range(0, blocks, 2)) + list(range(1, blocks, 2))
     far = [swapped(txt_bf, "txt", 4 * k) for k in range(1, half)]
     near = [swapped(tile, "txt", 2) for tile in [txt_bf] + far]
     tiles = [txt_bf] + far + near
-    perm_other = swapped(perm_row, "txt", 1)
-    img_other = swapped(img_bf, "txt", 1)
+    img_bf, img_other, img_unit, img_inv = call(
+        unit_img_body,
+        [struct(rows, width, BF16)] * 2 + [struct(part, width, F32), struct(part, 128, F32)],
+        [place, raw_other, in_hbm(images)],
+        [SMEM, VMEM, ANY],
+        24 << 20,
+        8 * rows * width,
+        [pltpu.VMEM((rows, width), F32), pltpu.SemaphoreType.DMA],
+    )
     scalars = [place, column, scale, shift]
     pairs = 2 * rows * blocks * txt_rows * width
     kept, other_img = call(
@@ -259,12 +267,11 @@
         10 * part * width,
     )
     grads = [grad_part] + [swapped(grad_part, "img", k) for k in range(1, count)]
-    anywhere = pl.BlockSpec(memory_space=pl.ANY)
     return pl.pallas_call(
         functools.partial(last_body, count),
         out_shape=[struct(rows, width, F32), struct(txt_rows, width, F32)],
         in_specs=[SMEM] * 2 + [VMEM] * (3 + count + half),
-        out_specs=[anywhere] * 2,
+        out_specs=[ANY] * 2,
         scratch_shapes=[
             pltpu.VMEM((rows, width), F32),
             pltpu.VMEM((txt_rows, width), F32),

time: 44.4 us -> 44 us (level)
  waiting for transfers between devices: 18.3 us -> 16.9 us
  Pallas kernels: 5.63 us -> 6.65 us
    pallas_call x5 -> x7, Pallas kernels: 2.77 us -> 5.37 us  [call(): pl.pallas_call(body, out_shape=outs, in_specs=specs, out_specs=[VMEM] * l...]
    pallas_call x1 -> x0, Pallas kernels: 1.58 us -> none  [unit_rows(): pl.pallas_call(unit_body, out_shape=[struct(*size, BF16) for size in size...]
    ppermute x15, waiting for transfers between devices: 18.3 us -> 16.9 us  [swapped(): return lax.ppermute(value, axis, [(s, s ^ step) for s in range(count)])]
  transfers between devices with their start and end apart: 15 -> 15, of which waited for: 7 -> 7; matrix products, arithmetic and copies ran while one was open for 0% -> 0% of each run, Pallas kernels for 4% -> 10%
where the time goes in v7:
time: 44 us; the launch traced here: 43.8 us
  starting transfers between devices  18.2 us (41%)
  waiting for transfers between devices  16.9 us (38%)
  Pallas kernels  6.65 us (15%)
  between operations  2.03 us (5%)
    ppermute x15, starting transfers between devices, swapped(): return lax.ppermute(value, axis, [(s, s ^ step) for s in range(count)])  18.2 us
    ppermute x15, waiting for transfers between devices, swapped(): return lax.ppermute(value, axis, [(s, s ^ step) for s in range(count)])  16.9 us
    pallas_call x7, Pallas kernels, call(): pl.pallas_call(body, out_shape=outs, in_specs=specs, out_specs=[VMEM] * l...  5.37 us
    pallas_call x1, Pallas kernels, local(): pl.pallas_call(functools.partial(last_body, count), out_shape=[struct(row...  1.28 us
  transfers between devices with their start and end apart: 15, of which 7 were waited for; matrix products, arithmetic and copies ran while one was open for 0% of the time, Pallas kernels for 10%

profile of v7, /device:TPU:0, one launch (start us, length us, event | category | flops | bytes accessed | tf_op | source)
XLA Modules:
  0.0 43.8 jit_solution(10176975908306214863)
XLA Ops:
  0.6 0.5 %collective-permute-start = (f32[256,1152]{1,0:T(8,128)}, f32[256,1152]{1,0:T(8,128)S(1)}, u32[]{:S(2)}, u32[]{:S(2)}) collective-permute-start(f32[256,1152]{1,0:T(8,128)} %source.3), channel_id=1, source_target_pairs={{0,1},{1,0},{2,3},{3,2},{4,5},{5,4},{6,7},{7,6},{8,9},{9,8},{10,11... | collective-permute-start | bytes 3538952 | tf_op jit(solution)/shard_map/ppermute | solution.py:178
  1.1 1.1 %shard_map.68 = (bf16[64,1152]{1,0:T(8,128)(2,1)S(1)}, f32[64,1152]{1,0:T(8,128)S(1)}, f32[64,128]{1,0:T(8,128)S(1)}) custom-call(f32[64,1152]{1,0:T(8,128)} %source.2), custom_call_target="tpu_custom_call" | custom-call | flops 294912 | bytes 770048 | tf_op jit(solution)/shard_map/pallas_call | solution.py:25
  2.2 3.7 %collective-permute-start.2 = (bf16[64,1152]{1,0:T(8,128)(2,1)S(1)}, bf16[64,1152]{1,0:T(8,128)(2,1)S(1)}, u32[]{:S(2)}, u32[]{:S(2)}) collective-permute-start(bf16[64,1152]{1,0:T(8,128)(2,1)S(1)} %get-tuple-element.24.refs_0_), channel_id=1, source_target_pairs={{0,4},{1,5},{2,6},{3,7},{4,0},{5,1},{6,2},{7,3},{8,12},{9,13},{10,... | collective-permute-start | bytes 442376 | tf_op jit(solution)/shard_map/ppermute | solution.py:178
  5.9 1.6 %collective-permute-start.3 = (bf16[64,1152]{1,0:T(8,128)(2,1)S(1)}, bf16[64,1152]{1,0:T(8,128)(2,1)S(1)}, u32[]{:S(2)}, u32[]{:S(2)}) collective-permute-start(bf16[64,1152]{1,0:T(8,128)(2,1)S(1)} %get-tuple-element.24.refs_0_), channel_id=1, source_target_pairs={{0,2},{1,3},{2,0},{3,1},{4,6},{5,7},{6,4},{7,5},{8,10},{9,11},{10,... | collective-permute-start | bytes 442376 | tf_op jit(solution)/shard_map/ppermute | solution.py:178
  7.5 6.2 %collective-permute-done.2.refs_1_ = bf16[64,1152]{1,0:T(8,128)(2,1)S(1)} collective-permute-done((bf16[64,1152]{1,0:T(8,128)(2,1)S(1)}, bf16[64,1152]{1,0:T(8,128)(2,1)S(1)}, u32[]{:S(2)}, u32[]{:S(2)}) %collective-permute-start.2) | collective-permute-done | bytes 147488 | tf_op jit(solution)/shard_map/ppermute | solution.py:178
  13.7 0.6 %collective-permute-start.4 = (bf16[64,1152]{1,0:T(8,128)(2,1)S(1)}, bf16[64,1152]{1,0:T(8,128)(2,1)S(1)}, u32[]{:S(2)}, u32[]{:S(2)}) collective-permute-start(bf16[64,1152]{1,0:T(8,128)(2,1)S(1)} %collective-permute-done.2.refs_1_), channel_id=1, source_target_pairs={{0,2},{1,3},{2,0},{3,1},{4,6},{5,7},{6,4},{7,5},{8,10},{9,11},{10,... | collective-permute-start | bytes 442376 | tf_op jit(solution)/shard_map/ppermute | solution.py:178
  14.3 0.0 collective-permute-start.1
  15.6 0.0 collective-permute-done.other
  15.6 1.5 %shard_map.69 = (bf16[256,1152]{1,0:T(8,128)(2,1)S(1)}, bf16[256,1152]{1,0:T(8,128)(2,1)S(1)}, f32[64,1152]{1,0:T(8,128)S(1)}, f32[64,128]{1,0:T(8,128)S(1)}) custom-call(s32[1]{0:T(128)} %bitcast.place.position, f32[256,1152]{1,0:T(8,128)S(1)} %collective-permute-done.other, f32[256,1152]{1,0:T(8,128)} %source.3), custom_call_target="tpu_custom_call" | custom-call | flops 2359296 | bytes 3866628 | tf_op jit(solution)/shard_map/pallas_call | solution.py:25
  17.1 0.0 copy-start
  17.1 0.0 collective-permute-done.1.perm
  17.1 0.0 collective-permute-done.3.refs_2_
  17.2 2.1 %collective-permute-done.4.refs_3_ = bf16[64,1152]{1,0:T(8,128)(2,1)S(1)} collective-permute-done((bf16[64,1152]{1,0:T(8,128)(2,1)S(1)}, bf16[64,1152]{1,0:T(8,128)(2,1)S(1)}, u32[]{:S(2)}, u32[]{:S(2)}) %collective-permute-start.4) | collective-permute-done | bytes 147488 | tf_op jit(solution)/shard_map/ppermute | solution.py:178
  19.3 1.0 %shard_map.70 = (bf16[256,256]{1,0:T(8,128)(2,1)S(1)}, bf16[256,1152]{1,0:T(8,128)(2,1)S(1)}) custom-call(s32[1]{0:T(128)} %bitcast.place.position, s32[1]{0:T(128)} %bitcast.1.column, f32[1]{0:T(128)S(6)} %copy.7.scale, f32[1]{0:T(128)S(6)} %copy.8.shift, s32[1,256]{1,0:T(1,128)S(1)} %collective-permute-done.1.perm, ...), custom_call_target="tpu_custom_call" | custom-call | flops 301989888 | bytes 1901584 | tf_op jit(solution)/shard_map/pallas_call | solution.py:25
  20.3 0.1 collective-permute-start.5
  20.4 0.0 copy-done
  20.4 1.4 %shard_map.71 = (f32[256,1152]{1,0:T(8,128)S(1)}, f32[64,1152]{1,0:T(8,128)S(1)}, f32[64,1152]{1,0:T(8,128)S(1)}, bf16[64,1152]{1,0:T(8,128)(2,1)S(1)}, bf16[64,1152]{1,0:T(8,128)(2,1)S(1)}) custom-call(s32[1]{0:T(128)} %bitcast.place.position, s32[1]{0:T(128)} %bitcast.1.column, f32[1]{0:T(128)S(6)} %copy.7.scale, f32[1]{0:T(128)S(6)} %copy.8.shift, ...), custom_call_target="tpu_custom_call" | custom-call | flops 603979776 | bytes 3965968 | tf_op jit(solution)/shard_map/pallas_call | solution.py:25
  21.8 0.9 %collective-permute-start.13 = (bf16[64,1152]{1,0:T(8,128)(2,1)S(1)}, bf16[64,1152]{1,0:T(8,128)(2,1)S(1)}, u32[]{:S(2)}, u32[]{:S(2)}) collective-permute-start(bf16[64,1152]{1,0:T(8,128)(2,1)S(1)} %get-tuple-element.37), channel_id=1, source_target_pairs={{0,2},{1,3},{2,0},{3,1},{4,6},{5,7},{6,4},{7,5},{8,10},{9,11},{10,... | collective-permute-start | bytes 442376 | tf_op jit(solution)/shard_map/ppermute | solution.py:178
  22.7 0.0 collective-permute-done.5.other
  22.7 0.2 shard_map.72
  22.9 1.6 %collective-permute-start.6 = (bf16[64,1152]{1,0:T(8,128)(2,1)S(1)}, bf16[64,1152]{1,0:T(8,128)(2,1)S(1)}, u32[]{:S(2)}, u32[]{:S(2)}) collective-permute-start(bf16[64,1152]{1,0:T(8,128)(2,1)S(1)} %get-tuple-element.32), channel_id=1, source_target_pairs={{0,8},{8,0},{16,24},{24,16},{1,9},{9,1},{17,25},{25,17},{2,10},{10... | collective-permute-start | bytes 442376 | tf_op jit(solution)/shard_map/ppermute | solution.py:178
  24.4 1.5 %collective-permute-start.7 = (bf16[64,1152]{1,0:T(8,128)(2,1)S(1)}, bf16[64,1152]{1,0:T(8,128)(2,1)S(1)}, u32[]{:S(2)}, u32[]{:S(2)}) collective-permute-start(bf16[64,1152]{1,0:T(8,128)(2,1)S(1)} %get-tuple-element.33), channel_id=1, source_target_pairs={{0,16},{8,24},{16,0},{24,8},{1,17},{9,25},{17,1},{25,9},{2,18},{10... | collective-permute-start | bytes 442376 | tf_op jit(solution)/shard_map/ppermute | solution.py:178
  26.0 0.5 %collective-permute-start.8 = (bf16[64,1152]{1,0:T(8,128)(2,1)S(1)}, bf16[64,1152]{1,0:T(8,128)(2,1)S(1)}, u32[]{:S(2)}, u32[]{:S(2)}) collective-permute-start(bf16[64,1152]{1,0:T(8,128)(2,1)S(1)} %get-tuple-element.34), channel_id=1, source_target_pairs={{0,24},{8,16},{16,8},{24,0},{1,25},{9,17},{17,9},{25,1},{2,26},{10... | collective-permute-start | bytes 442376 | tf_op jit(solution)/shard_map/ppermute | solution.py:178
  26.4 1.2 %collective-permute-start.12 = (bf16[64,1152]{1,0:T(8,128)(2,1)S(1)}, bf16[64,1152]{1,0:T(8,128)(2,1)S(1)}, u32[]{:S(2)}, u32[]{:S(2)}) collective-permute-start(bf16[64,1152]{1,0:T(8,128)(2,1)S(1)} %get-tuple-element.35), channel_id=1, source_target_pairs={{0,2},{1,3},{2,0},{3,1},{4,6},{5,7},{6,4},{7,5},{8,10},{9,11},{10,... | collective-permute-start | bytes 442376 | tf_op jit(solution)/shard_map/ppermute | solution.py:178
  27.6 0.5 %collective-permute-done.13.got = bf16[64,1152]{1,0:T(8,128)(2,1)S(1)} collective-permute-done((bf16[64,1152]{1,0:T(8,128)(2,1)S(1)}, bf16[64,1152]{1,0:T(8,128)(2,1)S(1)}, u32[]{:S(2)}, u32[]{:S(2)}) %collective-permute-start.13) | collective-permute-done | bytes 147488 | tf_op jit(solution)/shard_map/ppermute | solution.py:178
  28.2 2.5 %collective-permute-start.14 = (bf16[64,1152]{1,0:T(8,128)(2,1)S(1)}, bf16[64,1152]{1,0:T(8,128)(2,1)S(1)}, u32[]{:S(2)}, u32[]{:S(2)}) collective-permute-start(bf16[64,1152]{1,0:T(8,128)(2,1)S(1)} %shard_map.74), channel_id=1, source_target_pairs={{0,4},{1,5},{2,6},{3,7},{4,0},{5,1},{6,2},{7,3},{8,12},{9,13},{10,... | collective-permute-start | bytes 442376 | tf_op jit(solution)/shard_map/ppermute | solution.py:178
  30.7 0.0 collective-permute-done.6.refs_0_
  30.7 2.6 %collective-permute-done.7.refs_1_ = bf16[64,1152]{1,0:T(8,128)(2,1)S(1)} collective-permute-done((bf16[64,1152]{1,0:T(8,128)(2,1)S(1)}, bf16[64,1152]{1,0:T(8,128)(2,1)S(1)}, u32[]{:S(2)}, u32[]{:S(2)}) %collective-permute-start.7) | collective-permute-done | bytes 147488 | tf_op jit(solution)/shard_map/ppermute | solution.py:178
  33.3 0.0 collective-permute-done.8.refs_2_
  33.3 0.2 shard_map.73.refs_0_
  33.5 1.6 %collective-permute-start.11 = (bf16[64,1152]{1,0:T(8,128)(2,1)S(1)}, bf16[64,1152]{1,0:T(8,128)(2,1)S(1)}, u32[]{:S(2)}, u32[]{:S(2)}) collective-permute-start(bf16[64,1152]{1,0:T(8,128)(2,1)S(1)} %shard_map.73.refs_0_), channel_id=1, source_target_pairs={{0,24},{8,16},{16,8},{24,0},{1,25},{9,17},{17,9},{25,1},{2,26},{10... | collective-permute-start | bytes 442376 | tf_op jit(solution)/shard_map/ppermute | solution.py:178
  35.0 1.2 %collective-permute-start.10 = (bf16[64,1152]{1,0:T(8,128)(2,1)S(1)}, bf16[64,1152]{1,0:T(8,128)(2,1)S(1)}, u32[]{:S(2)}, u32[]{:S(2)}) collective-permute-start(bf16[64,1152]{1,0:T(8,128)(2,1)S(1)} %shard_map.73.refs_0_), channel_id=1, source_target_pairs={{0,16},{8,24},{16,0},{24,8},{1,17},{9,25},{17,1},{25,9},{2,18},{10... | collective-permute-start | bytes 442376 | tf_op jit(solution)/shard_map/ppermute | solution.py:178
  36.2 0.8 %collective-permute-start.9 = (bf16[64,1152]{1,0:T(8,128)(2,1)S(1)}, bf16[64,1152]{1,0:T(8,128)(2,1)S(1)}, u32[]{:S(2)}, u32[]{:S(2)}) collective-permute-start(bf16[64,1152]{1,0:T(8,128)(2,1)S(1)} %shard_map.73.refs_0_), channel_id=1, source_target_pairs={{0,8},{8,0},{16,24},{24,16},{1,9},{9,1},{17,25},{25,17},{2,10},{10... | collective-permute-start | bytes 442376 | tf_op jit(solution)/shard_map/ppermute | solution.py:178
  37.0 0.0 collective-permute-done.12.refs_4_
  37.0 0.7 %collective-permute-done.14.refs_5_ = bf16[64,1152]{1,0:T(8,128)(2,1)S(1)} collective-permute-done((bf16[64,1152]{1,0:T(8,128)(2,1)S(1)}, bf16[64,1152]{1,0:T(8,128)(2,1)S(1)}, u32[]{:S(2)}, u32[]{:S(2)}) %collective-permute-start.14) | collective-permute-done | bytes 147488 | tf_op jit(solution)/shard_map/ppermute | solution.py:178
  37.8 3.2 %collective-permute-done.11.refs_3_ = bf16[64,1152]{1,0:T(8,128)(2,1)S(1)} collective-permute-done((bf16[64,1152]{1,0:T(8,128)(2,1)S(1)}, bf16[64,1152]{1,0:T(8,128)(2,1)S(1)}, u32[]{:S(2)}, u32[]{:S(2)}) %collective-permute-start.11) | collective-permute-done | bytes 147488 | tf_op jit(solution)/shard_map/ppermute | solution.py:178
  41.0 1.6 %collective-permute-done.10.refs_2_ = bf16[64,1152]{1,0:T(8,128)(2,1)S(1)} collective-permute-done((bf16[64,1152]{1,0:T(8,128)(2,1)S(1)}, bf16[64,1152]{1,0:T(8,128)(2,1)S(1)}, u32[]{:S(2)}, u32[]{:S(2)}) %collective-permute-start.10) | collective-permute-done | bytes 147488 | tf_op jit(solution)/shard_map/ppermute | solution.py:178
  42.5 0.0 collective-permute-done.9.refs_1_
  42.5 1.3 %shard_map.75 = (f32[256,1152]{1,0:T(8,128)}, f32[64,1152]{1,0:T(8,128)}) custom-call(s32[1]{0:T(128)} %bitcast.place.position, f32[1]{0:T(128)S(6)} %copy.7.scale, f32[64,1152]{1,0:T(8,128)S(1)} %get-tuple-element.20.unit, f32[64,128]{1,0:T(8,128)S(1)} %get-tuple-element.21.inverse, f32[64,1152]{1,0:T(8,128)S(1)} %get-tuple-element.26.own, ...), custom_call_target="tpu_custom_call" | custom-call | flops 737280 | bytes 2359296 | tf_op jit(solution)/shard_map/pallas_call | solution.py:270
  (1 shorter events, 0.0 us)
Async XLA Ops:
  0.6 15.0 %collective-permute-start = (f32[256,1152]{1,0:T(8,128)}, f32[256,1152]{1,0:T(8,128)S(1)}, u32[]{:S(2)}, u32[]{:S(2)}) collective-permute-start(f32[256,1152]{1,0:T(8,128)} %source.3), channel_id=1, source_target_pairs={{0,1},{1,0},{2,3},{3,2},{4,5},{5,4},{6,7},{7,6},{8,9},{9,8},{10,11... | collective-permute-start | bytes 3538952 | tf_op jit(solution)/shard_map/ppermute | solution.py:178
  2.2 11.4 %collective-permute-start.2 = (bf16[64,1152]{1,0:T(8,128)(2,1)S(1)}, bf16[64,1152]{1,0:T(8,128)(2,1)S(1)}, u32[]{:S(2)}, u32[]{:S(2)}) collective-permute-start(bf16[64,1152]{1,0:T(8,128)(2,1)S(1)} %get-tuple-element.24.refs_0_), channel_id=1, source_target_pairs={{0,4},{1,5},{2,6},{3,7},{4,0},{5,1},{6,2},{7,3},{8,12},{9,13},{10,... | collective-permute-start | bytes 442376 | tf_op jit(solution)/shard_map/ppermute | solution.py:178
  5.9 11.2 %collective-permute-start.3 = (bf16[64,1152]{1,0:T(8,128)(2,1)S(1)}, bf16[64,1152]{1,0:T(8,128)(2,1)S(1)}, u32[]{:S(2)}, u32[]{:S(2)}) collective-permute-start(bf16[64,1152]{1,0:T(8,128)(2,1)S(1)} %get-tuple-element.24.refs_0_), channel_id=1, source_target_pairs={{0,2},{1,3},{2,0},{3,1},{4,6},{5,7},{6,4},{7,5},{8,10},{9,11},{10,... | collective-permute-start | bytes 442376 | tf_op jit(solution)/shard_map/ppermute | solution.py:178
  13.7 5.6 %collective-permute-start.4 = (bf16[64,1152]{1,0:T(8,128)(2,1)S(1)}, bf16[64,1152]{1,0:T(8,128)(2,1)S(1)}, u32[]{:S(2)}, u32[]{:S(2)}) collective-permute-start(bf16[64,1152]{1,0:T(8,128)(2,1)S(1)} %collective-permute-done.2.refs_1_), channel_id=1, source_target_pairs={{0,2},{1,3},{2,0},{3,1},{4,6},{5,7},{6,4},{7,5},{8,10},{9,11},{10,... | collective-permute-start | bytes 442376 | tf_op jit(solution)/shard_map/ppermute | solution.py:178
  14.3 2.8 %collective-permute-start.1 = (s32[1,256]{1,0:T(1,128)}, s32[1,256]{1,0:T(1,128)S(1)}, u32[]{:S(2)}, u32[]{:S(2)}) collective-permute-start(s32[1,256]{1,0:T(1,128)} %bitcast.3), channel_id=1, source_target_pairs={{0,1},{1,0},{2,3},{3,2},{4,5},{5,4},{6,7},{7,6},{8,9},{9,8},{10,11... | collective-permute-start | bytes 3080 | tf_op jit(solution)/shard_map/ppermute | solution.py:178
  17.1 3.3 %copy-start = (s32[256]{0:T(256)S(1)}, s32[256]{0:T(256)}, u32[]{:S(2)}) copy-start(s32[256]{0:T(256)} %param.7) | copy-start | bytes 3076
  20.3 2.4 %collective-permute-start.5 = (bf16[256,1152]{1,0:T(8,128)(2,1)S(1)}, bf16[256,1152]{1,0:T(8,128)(2,1)S(1)}, u32[]{:S(2)}, u32[]{:S(2)}) collective-permute-start(bf16[256,1152]{1,0:T(8,128)(2,1)S(1)} %get-tuple-element.30), channel_id=1, source_target_pairs={{0,1},{1,0},{2,3},{3,2},{4,5},{5,4},{6,7},{7,6},{8,9},{9,8},{10,11... | collective-permute-start | bytes 1769480 | tf_op jit(solution)/shard_map/ppermute | solution.py:178
  21.8 6.3 %collective-permute-start.13 = (bf16[64,1152]{1,0:T(8,128)(2,1)S(1)}, bf16[64,1152]{1,0:T(8,128)(2,1)S(1)}, u32[]{:S(2)}, u32[]{:S(2)}) collective-permute-start(bf16[64,1152]{1,0:T(8,128)(2,1)S(1)} %get-tuple-element.37), channel_id=1, source_target_pairs={{0,2},{1,3},{2,0},{3,1},{4,6},{5,7},{6,4},{7,5},{8,10},{9,11},{10,... | collective-permute-start | bytes 442376 | tf_op jit(solution)/shard_map/ppermute | solution.py:178
  22.9 7.8 %collective-permute-start.6 = (bf16[64,1152]{1,0:T(8,128)(2,1)S(1)}, bf16[64,1152]{1,0:T(8,128)(2,1)S(1)}, u32[]{:S(2)}, u32[]{:S(2)}) collective-permute-start(bf16[64,1152]{1,0:T(8,128)(2,1)S(1)} %get-tuple-element.32), channel_id=1, source_target_pairs={{0,8},{8,0},{16,24},{24,16},{1,9},{9,1},{17,25},{25,17},{2,10},{10... | collective-permute-start | bytes 442376 | tf_op jit(solution)/shard_map/ppermute | solution.py:178
  24.4 8.8 %collective-permute-start.7 = (bf16[64,1152]{1,0:T(8,128)(2,1)S(1)}, bf16[64,1152]{1,0:T(8,128)(2,1)S(1)}, u32[]{:S(2)}, u32[]{:S(2)}) collective-permute-start(bf16[64,1152]{1,0:T(8,128)(2,1)S(1)} %get-tuple-element.33), channel_id=1, source_target_pairs={{0,16},{8,24},{16,0},{24,8},{1,17},{9,25},{17,1},{25,9},{2,18},{10... | collective-permute-start | bytes 442376 | tf_op jit(solution)/shard_map/ppermute | solution.py:178
  26.0 7.3 %collective-permute-start.8 = (bf16[64,1152]{1,0:T(8,128)(2,1)S(1)}, bf16[64,1152]{1,0:T(8,128)(2,1)S(1)}, u32[]{:S(2)}, u32[]{:S(2)}) collective-permute-start(bf16[64,1152]{1,0:T(8,128)(2,1)S(1)} %get-tuple-element.34), channel_id=1, source_target_pairs={{0,24},{8,16},{16,8},{24,0},{1,25},{9,17},{17,9},{25,1},{2,26},{10... | collective-permute-start | bytes 442376 | tf_op jit(solution)/shard_map/ppermute | solution.py:178
  26.4 10.6 %collective-permute-start.12 = (bf16[64,1152]{1,0:T(8,128)(2,1)S(1)}, bf16[64,1152]{1,0:T(8,128)(2,1)S(1)}, u32[]{:S(2)}, u32[]{:S(2)}) collective-permute-start(bf16[64,1152]{1,0:T(8,128)(2,1)S(1)} %get-tuple-element.35), channel_id=1, source_target_pairs={{0,2},{1,3},{2,0},{3,1},{4,6},{5,7},{6,4},{7,5},{8,10},{9,11},{10,... | collective-permute-start | bytes 442376 | tf_op jit(solution)/shard_map/ppermute | solution.py:178
  28.2 9.6 %collective-permute-start.14 = (bf16[64,1152]{1,0:T(8,128)(2,1)S(1)}, bf16[64,1152]{1,0:T(8,128)(2,1)S(1)}, u32[]{:S(2)}, u32[]{:S(2)}) collective-permute-start(bf16[64,1152]{1,0:T(8,128)(2,1)S(1)} %shard_map.74), channel_id=1, source_target_pairs={{0,4},{1,5},{2,6},{3,7},{4,0},{5,1},{6,2},{7,3},{8,12},{9,13},{10,... | collective-permute-start | bytes 442376 | tf_op jit(solution)/shard_map/ppermute | solution.py:178
  33.5 7.5 %collective-permute-start.11 = (bf16[64,1152]{1,0:T(8,128)(2,1)S(1)}, bf16[64,1152]{1,0:T(8,128)(2,1)S(1)}, u32[]{:S(2)}, u32[]{:S(2)}) collective-permute-start(bf16[64,1152]{1,0:T(8,128)(2,1)S(1)} %shard_map.73.refs_0_), channel_id=1, source_target_pairs={{0,24},{8,16},{16,8},{24,0},{1,25},{9,17},{17,9},{25,1},{2,26},{10... | collective-permute-start | bytes 442376 | tf_op jit(solution)/shard_map/ppermute | solution.py:178
  35.0 7.5 %collective-permute-start.10 = (bf16[64,1152]{1,0:T(8,128)(2,1)S(1)}, bf16[64,1152]{1,0:T(8,128)(2,1)S(1)}, u32[]{:S(2)}, u32[]{:S(2)}) collective-permute-start(bf16[64,1152]{1,0:T(8,128)(2,1)S(1)} %shard_map.73.refs_0_), channel_id=1, source_target_pairs={{0,16},{8,24},{16,0},{24,8},{1,17},{9,25},{17,1},{25,9},{2,18},{10... | collective-permute-start | bytes 442376 | tf_op jit(solution)/shard_map/ppermute | solution.py:178
  36.2 6.3 %collective-permute-start.9 = (bf16[64,1152]{1,0:T(8,128)(2,1)S(1)}, bf16[64,1152]{1,0:T(8,128)(2,1)S(1)}, u32[]{:S(2)}, u32[]{:S(2)}) collective-permute-start(bf16[64,1152]{1,0:T(8,128)(2,1)S(1)} %shard_map.73.refs_0_), channel_id=1, source_target_pairs={{0,8},{8,0},{16,24},{24,16},{1,9},{9,1},{17,25},{25,17},{2,10},{10... | collective-permute-start | bytes 442376 | tf_op jit(solution)/shard_map/ppermute | solution.py:178

commit v8 on v7

--- a/solution.py
+++ b/solution.py
@@ -257,7 +257,7 @@
         24 << 20,
         rows * width,
     )
-    got = [swapped(send[k - 1], "img", k) for k in range(1, count)]
+    got = [swapped(send[k - 1], "img", k) for k in range(count - 1, 0, -1)]
     (grad_part,) = call(
         finish_img_body,
         [struct(part, width, BF16)],

time: 44 us -> 44.6 us (1.014)
  waiting for transfers between devices: 16.9 us -> 17.5 us
    ppermute x15, waiting for transfers between devices: 16.9 us -> 17.5 us  [swapped(): return lax.ppermute(value, axis, [(s, s ^ step) for s in range(count)])]
  transfers between devices with their start and end apart: 15 -> 15, of which waited for: 7 -> 9; matrix products, arithmetic and copies ran while one was open for 0% -> 0% of each run, Pallas kernels for 10% -> 10%
where the time goes in v8:
time: 44.6 us; the launch traced here: 44.4 us
  starting transfers between devices  18.2 us (41%)
  waiting for transfers between devices  17.5 us (39%)
  Pallas kernels  6.64 us (15%)
  between operations  2.03 us (5%)
    ppermute x15, starting transfers between devices, swapped(): return lax.ppermute(value, axis, [(s, s ^ step) for s in range(count)])  18.2 us
    ppermute x15, waiting for transfers between devices, swapped(): return lax.ppermute(value, axis, [(s, s ^ step) for s in range(count)])  17.5 us
    pallas_call x7, Pallas kernels, call(): pl.pallas_call(body, out_shape=outs, in_specs=specs, out_specs=[VMEM] * l...  5.37 us
    pallas_call x1, Pallas kernels, local(): pl.pallas_call(functools.partial(last_body, count), out_shape=[struct(row...  1.28 us
  transfers between devices with their start and end apart: 15, of which 9 were waited for; matrix products, arithmetic and copies ran while one was open for 0% of the time, Pallas kernels for 10%

profile of v8, /device:TPU:0, one launch (start us, length us, event | category | flops | bytes accessed | tf_op | source)
XLA Modules:
  0.0 44.4 jit_solution(3425352349752059191)
XLA Ops:
  0.6 0.5 %collective-permute-start = (f32[256,1152]{1,0:T(8,128)}, f32[256,1152]{1,0:T(8,128)S(1)}, u32[]{:S(2)}, u32[]{:S(2)}) collective-permute-start(f32[256,1152]{1,0:T(8,128)} %source.3), channel_id=1, source_target_pairs={{0,1},{1,0},{2,3},{3,2},{4,5},{5,4},{6,7},{7,6},{8,9},{9,8},{10,11... | collective-permute-start | bytes 3538952 | tf_op jit(solution)/shard_map/ppermute | solution.py:178
  1.1 1.1 %shard_map.68 = (bf16[64,1152]{1,0:T(8,128)(2,1)S(1)}, f32[64,1152]{1,0:T(8,128)S(1)}, f32[64,128]{1,0:T(8,128)S(1)}) custom-call(f32[64,1152]{1,0:T(8,128)} %source.2), custom_call_target="tpu_custom_call" | custom-call | flops 294912 | bytes 770048 | tf_op jit(solution)/shard_map/pallas_call | solution.py:25
  2.2 3.7 %collective-permute-start.2 = (bf16[64,1152]{1,0:T(8,128)(2,1)S(1)}, bf16[64,1152]{1,0:T(8,128)(2,1)S(1)}, u32[]{:S(2)}, u32[]{:S(2)}) collective-permute-start(bf16[64,1152]{1,0:T(8,128)(2,1)S(1)} %get-tuple-element.24.refs_0_), channel_id=1, source_target_pairs={{0,4},{1,5},{2,6},{3,7},{4,0},{5,1},{6,2},{7,3},{8,12},{9,13},{10,... | collective-permute-start | bytes 442376 | tf_op jit(solution)/shard_map/ppermute | solution.py:178
  5.9 1.6 %collective-permute-start.3 = (bf16[64,1152]{1,0:T(8,128)(2,1)S(1)}, bf16[64,1152]{1,0:T(8,128)(2,1)S(1)}, u32[]{:S(2)}, u32[]{:S(2)}) collective-permute-start(bf16[64,1152]{1,0:T(8,128)(2,1)S(1)} %get-tuple-element.24.refs_0_), channel_id=1, source_target_pairs={{0,2},{1,3},{2,0},{3,1},{4,6},{5,7},{6,4},{7,5},{8,10},{9,11},{10,... | collective-permute-start | bytes 442376 | tf_op jit(solution)/shard_map/ppermute | solution.py:178
  7.5 6.2 %collective-permute-done.2.refs_1_ = bf16[64,1152]{1,0:T(8,128)(2,1)S(1)} collective-permute-done((bf16[64,1152]{1,0:T(8,128)(2,1)S(1)}, bf16[64,1152]{1,0:T(8,128)(2,1)S(1)}, u32[]{:S(2)}, u32[]{:S(2)}) %collective-permute-start.2) | collective-permute-done | bytes 147488 | tf_op jit(solution)/shard_map/ppermute | solution.py:178
  13.7 0.6 %collective-permute-start.4 = (bf16[64,1152]{1,0:T(8,128)(2,1)S(1)}, bf16[64,1152]{1,0:T(8,128)(2,1)S(1)}, u32[]{:S(2)}, u32[]{:S(2)}) collective-permute-start(bf16[64,1152]{1,0:T(8,128)(2,1)S(1)} %collective-permute-done.2.refs_1_), channel_id=1, source_target_pairs={{0,2},{1,3},{2,0},{3,1},{4,6},{5,7},{6,4},{7,5},{8,10},{9,11},{10,... | collective-permute-start | bytes 442376 | tf_op jit(solution)/shard_map/ppermute | solution.py:178
  14.3 0.0 collective-permute-start.1
  15.6 0.0 collective-permute-done.other
  15.6 1.5 %shard_map.69 = (bf16[256,1152]{1,0:T(8,128)(2,1)S(1)}, bf16[256,1152]{1,0:T(8,128)(2,1)S(1)}, f32[64,1152]{1,0:T(8,128)S(1)}, f32[64,128]{1,0:T(8,128)S(1)}) custom-call(s32[1]{0:T(128)} %bitcast.place.position, f32[256,1152]{1,0:T(8,128)S(1)} %collective-permute-done.other, f32[256,1152]{1,0:T(8,128)} %source.3), custom_call_target="tpu_custom_call" | custom-call | flops 2359296 | bytes 3866628 | tf_op jit(solution)/shard_map/pallas_call | solution.py:25
  17.1 0.0 copy-start
  17.1 0.0 collective-permute-done.1.perm
  17.1 0.0 collective-permute-done.3.refs_2_
  17.2 2.1 %collective-permute-done.4.refs_3_ = bf16[64,1152]{1,0:T(8,128)(2,1)S(1)} collective-permute-done((bf16[64,1152]{1,0:T(8,128)(2,1)S(1)}, bf16[64,1152]{1,0:T(8,128)(2,1)S(1)}, u32[]{:S(2)}, u32[]{:S(2)}) %collective-permute-start.4) | collective-permute-done | bytes 147488 | tf_op jit(solution)/shard_map/ppermute | solution.py:178
  19.3 1.0 %shard_map.70 = (bf16[256,256]{1,0:T(8,128)(2,1)S(1)}, bf16[256,1152]{1,0:T(8,128)(2,1)S(1)}) custom-call(s32[1]{0:T(128)} %bitcast.place.position, s32[1]{0:T(128)} %bitcast.1.column, f32[1]{0:T(128)S(6)} %copy.7.scale, f32[1]{0:T(128)S(6)} %copy.8.shift, s32[1,256]{1,0:T(1,128)S(1)} %collective-permute-done.1.perm, ...), custom_call_target="tpu_custom_call" | custom-call | flops 301989888 | bytes 1901584 | tf_op jit(solution)/shard_map/pallas_call | solution.py:25
  20.3 0.1 collective-permute-start.5
  20.4 0.0 copy-done
  20.4 1.4 %shard_map.71 = (f32[256,1152]{1,0:T(8,128)S(1)}, f32[64,1152]{1,0:T(8,128)S(1)}, f32[64,1152]{1,0:T(8,128)S(1)}, bf16[64,1152]{1,0:T(8,128)(2,1)S(1)}, bf16[64,1152]{1,0:T(8,128)(2,1)S(1)}) custom-call(s32[1]{0:T(128)} %bitcast.place.position, s32[1]{0:T(128)} %bitcast.1.column, f32[1]{0:T(128)S(6)} %copy.7.scale, f32[1]{0:T(128)S(6)} %copy.8.shift, ...), custom_call_target="tpu_custom_call" | custom-call | flops 603979776 | bytes 3965968 | tf_op jit(solution)/shard_map/pallas_call | solution.py:25
  21.8 0.9 %collective-permute-start.13 = (bf16[64,1152]{1,0:T(8,128)(2,1)S(1)}, bf16[64,1152]{1,0:T(8,128)(2,1)S(1)}, u32[]{:S(2)}, u32[]{:S(2)}) collective-permute-start(bf16[64,1152]{1,0:T(8,128)(2,1)S(1)} %get-tuple-element.37), channel_id=1, source_target_pairs={{0,2},{1,3},{2,0},{3,1},{4,6},{5,7},{6,4},{7,5},{8,10},{9,11},{10,... | collective-permute-start | bytes 442376 | tf_op jit(solution)/shard_map/ppermute | solution.py:178
  22.7 0.0 collective-permute-done.5.other
  22.7 0.2 shard_map.72
  22.9 2.5 %collective-permute-start.6 = (bf16[64,1152]{1,0:T(8,128)(2,1)S(1)}, bf16[64,1152]{1,0:T(8,128)(2,1)S(1)}, u32[]{:S(2)}, u32[]{:S(2)}) collective-permute-start(bf16[64,1152]{1,0:T(8,128)(2,1)S(1)} %get-tuple-element.32), channel_id=1, source_target_pairs={{0,24},{8,16},{16,8},{24,0},{1,25},{9,17},{17,9},{25,1},{2,26},{10... | collective-permute-start | bytes 442376 | tf_op jit(solution)/shard_map/ppermute | solution.py:178
  25.4 0.5 %collective-permute-start.7 = (bf16[64,1152]{1,0:T(8,128)(2,1)S(1)}, bf16[64,1152]{1,0:T(8,128)(2,1)S(1)}, u32[]{:S(2)}, u32[]{:S(2)}) collective-permute-start(bf16[64,1152]{1,0:T(8,128)(2,1)S(1)} %get-tuple-element.33), channel_id=1, source_target_pairs={{0,16},{8,24},{16,0},{24,8},{1,17},{9,25},{17,1},{25,9},{2,18},{10... | collective-permute-start | bytes 442376 | tf_op jit(solution)/shard_map/ppermute | solution.py:178
  25.9 0.5 %collective-permute-start.8 = (bf16[64,1152]{1,0:T(8,128)(2,1)S(1)}, bf16[64,1152]{1,0:T(8,128)(2,1)S(1)}, u32[]{:S(2)}, u32[]{:S(2)}) collective-permute-start(bf16[64,1152]{1,0:T(8,128)(2,1)S(1)} %get-tuple-element.34), channel_id=1, source_target_pairs={{0,8},{8,0},{16,24},{24,16},{1,9},{9,1},{17,25},{25,17},{2,10},{10... | collective-permute-start | bytes 442376 | tf_op jit(solution)/shard_map/ppermute | solution.py:178
  26.4 1.2 %collective-permute-start.12 = (bf16[64,1152]{1,0:T(8,128)(2,1)S(1)}, bf16[64,1152]{1,0:T(8,128)(2,1)S(1)}, u32[]{:S(2)}, u32[]{:S(2)}) collective-permute-start(bf16[64,1152]{1,0:T(8,128)(2,1)S(1)} %get-tuple-element.35), channel_id=1, source_target_pairs={{0,2},{1,3},{2,0},{3,1},{4,6},{5,7},{6,4},{7,5},{8,10},{9,11},{10,... | collective-permute-start | bytes 442376 | tf_op jit(solution)/shard_map/ppermute | solution.py:178
  27.6 0.5 %collective-permute-done.13.got = bf16[64,1152]{1,0:T(8,128)(2,1)S(1)} collective-permute-done((bf16[64,1152]{1,0:T(8,128)(2,1)S(1)}, bf16[64,1152]{1,0:T(8,128)(2,1)S(1)}, u32[]{:S(2)}, u32[]{:S(2)}) %collective-permute-start.13) | collective-permute-done | bytes 147488 | tf_op jit(solution)/shard_map/ppermute | solution.py:178
  28.2 2.5 %collective-permute-start.14 = (bf16[64,1152]{1,0:T(8,128)(2,1)S(1)}, bf16[64,1152]{1,0:T(8,128)(2,1)S(1)}, u32[]{:S(2)}, u32[]{:S(2)}) collective-permute-start(bf16[64,1152]{1,0:T(8,128)(2,1)S(1)} %shard_map.74), channel_id=1, source_target_pairs={{0,4},{1,5},{2,6},{3,7},{4,0},{5,1},{6,2},{7,3},{8,12},{9,13},{10,... | collective-permute-start | bytes 442376 | tf_op jit(solution)/shard_map/ppermute | solution.py:178
  30.7 0.0 collective-permute-done.6.refs_0_
  30.7 2.3 %collective-permute-done.7.refs_1_ = bf16[64,1152]{1,0:T(8,128)(2,1)S(1)} collective-permute-done((bf16[64,1152]{1,0:T(8,128)(2,1)S(1)}, bf16[64,1152]{1,0:T(8,128)(2,1)S(1)}, u32[]{:S(2)}, u32[]{:S(2)}) %collective-permute-start.7) | collective-permute-done | bytes 147488 | tf_op jit(solution)/shard_map/ppermute | solution.py:178
  33.0 0.1 collective-permute-done.8.refs_2_
  33.1 0.2 shard_map.73.refs_0_
  33.3 1.7 %collective-permute-start.11 = (bf16[64,1152]{1,0:T(8,128)(2,1)S(1)}, bf16[64,1152]{1,0:T(8,128)(2,1)S(1)}, u32[]{:S(2)}, u32[]{:S(2)}) collective-permute-start(bf16[64,1152]{1,0:T(8,128)(2,1)S(1)} %shard_map.73.refs_0_), channel_id=1, source_target_pairs={{0,24},{8,16},{16,8},{24,0},{1,25},{9,17},{17,9},{25,1},{2,26},{10... | collective-permute-start | bytes 442376 | tf_op jit(solution)/shard_map/ppermute | solution.py:178
  35.0 1.3 %collective-permute-start.10 = (bf16[64,1152]{1,0:T(8,128)(2,1)S(1)}, bf16[64,1152]{1,0:T(8,128)(2,1)S(1)}, u32[]{:S(2)}, u32[]{:S(2)}) collective-permute-start(bf16[64,1152]{1,0:T(8,128)(2,1)S(1)} %shard_map.73.refs_0_), channel_id=1, source_target_pairs={{0,16},{8,24},{16,0},{24,8},{1,17},{9,25},{17,1},{25,9},{2,18},{10... | collective-permute-start | bytes 442376 | tf_op jit(solution)/shard_map/ppermute | solution.py:178
  36.3 0.5 %collective-permute-start.9 = (bf16[64,1152]{1,0:T(8,128)(2,1)S(1)}, bf16[64,1152]{1,0:T(8,128)(2,1)S(1)}, u32[]{:S(2)}, u32[]{:S(2)}) collective-permute-start(bf16[64,1152]{1,0:T(8,128)(2,1)S(1)} %shard_map.73.refs_0_), channel_id=1, source_target_pairs={{0,8},{8,0},{16,24},{24,16},{1,9},{9,1},{17,25},{25,17},{2,10},{10... | collective-permute-start | bytes 442376 | tf_op jit(solution)/shard_map/ppermute | solution.py:178
  36.8 0.0 collective-permute-done.12.refs_4_
  36.8 1.0 %collective-permute-done.14.refs_5_ = bf16[64,1152]{1,0:T(8,128)(2,1)S(1)} collective-permute-done((bf16[64,1152]{1,0:T(8,128)(2,1)S(1)}, bf16[64,1152]{1,0:T(8,128)(2,1)S(1)}, u32[]{:S(2)}, u32[]{:S(2)}) %collective-permute-start.14) | collective-permute-done | bytes 147488 | tf_op jit(solution)/shard_map/ppermute | solution.py:178
  37.8 3.2 %collective-permute-done.11.refs_3_ = bf16[64,1152]{1,0:T(8,128)(2,1)S(1)} collective-permute-done((bf16[64,1152]{1,0:T(8,128)(2,1)S(1)}, bf16[64,1152]{1,0:T(8,128)(2,1)S(1)}, u32[]{:S(2)}, u32[]{:S(2)}) %collective-permute-start.11) | collective-permute-done | bytes 147488 | tf_op jit(solution)/shard_map/ppermute | solution.py:178
  41.0 2.1 %collective-permute-done.10.refs_2_ = bf16[64,1152]{1,0:T(8,128)(2,1)S(1)} collective-permute-done((bf16[64,1152]{1,0:T(8,128)(2,1)S(1)}, bf16[64,1152]{1,0:T(8,128)(2,1)S(1)}, u32[]{:S(2)}, u32[]{:S(2)}) %collective-permute-start.10) | collective-permute-done | bytes 147488 | tf_op jit(solution)/shard_map/ppermute | solution.py:178
  43.1 0.1 collective-permute-done.9.refs_1_
  43.2 1.3 %shard_map.75 = (f32[256,1152]{1,0:T(8,128)}, f32[64,1152]{1,0:T(8,128)}) custom-call(s32[1]{0:T(128)} %bitcast.place.position, f32[1]{0:T(128)S(6)} %copy.7.scale, f32[64,1152]{1,0:T(8,128)S(1)} %get-tuple-element.20.unit, f32[64,128]{1,0:T(8,128)S(1)} %get-tuple-element.21.inverse, f32[64,1152]{1,0:T(8,128)S(1)} %get-tuple-element.26.own, ...), custom_call_target="tpu_custom_call" | custom-call | flops 737280 | bytes 2359296 | tf_op jit(solution)/shard_map/pallas_call | solution.py:270
  (1 shorter events, 0.0 us)
Async XLA Ops:
  0.6 15.0 %collective-permute-start = (f32[256,1152]{1,0:T(8,128)}, f32[256,1152]{1,0:T(8,128)S(1)}, u32[]{:S(2)}, u32[]{:S(2)}) collective-permute-start(f32[256,1152]{1,0:T(8,128)} %source.3), channel_id=1, source_target_pairs={{0,1},{1,0},{2,3},{3,2},{4,5},{5,4},{6,7},{7,6},{8,9},{9,8},{10,11... | collective-permute-start | bytes 3538952 | tf_op jit(solution)/shard_map/ppermute | solution.py:178
  2.2 11.4 %collective-permute-start.2 = (bf16[64,1152]{1,0:T(8,128)(2,1)S(1)}, bf16[64,1152]{1,0:T(8,128)(2,1)S(1)}, u32[]{:S(2)}, u32[]{:S(2)}) collective-permute-start(bf16[64,1152]{1,0:T(8,128)(2,1)S(1)} %get-tuple-element.24.refs_0_), channel_id=1, source_target_pairs={{0,4},{1,5},{2,6},{3,7},{4,0},{5,1},{6,2},{7,3},{8,12},{9,13},{10,... | collective-permute-start | bytes 442376 | tf_op jit(solution)/shard_map/ppermute | solution.py:178
  5.9 11.2 %collective-permute-start.3 = (bf16[64,1152]{1,0:T(8,128)(2,1)S(1)}, bf16[64,1152]{1,0:T(8,128)(2,1)S(1)}, u32[]{:S(2)}, u32[]{:S(2)}) collective-permute-start(bf16[64,1152]{1,0:T(8,128)(2,1)S(1)} %get-tuple-element.24.refs_0_), channel_id=1, source_target_pairs={{0,2},{1,3},{2,0},{3,1},{4,6},{5,7},{6,4},{7,5},{8,10},{9,11},{10,... | collective-permute-start | bytes 442376 | tf_op jit(solution)/shard_map/ppermute | solution.py:178
  13.7 5.6 %collective-permute-start.4 = (bf16[64,1152]{1,0:T(8,128)(2,1)S(1)}, bf16[64,1152]{1,0:T(8,128)(2,1)S(1)}, u32[]{:S(2)}, u32[]{:S(2)}) collective-permute-start(bf16[64,1152]{1,0:T(8,128)(2,1)S(1)} %collective-permute-done.2.refs_1_), channel_id=1, source_target_pairs={{0,2},{1,3},{2,0},{3,1},{4,6},{5,7},{6,4},{7,5},{8,10},{9,11},{10,... | collective-permute-start | bytes 442376 | tf_op jit(solution)/shard_map/ppermute | solution.py:178
  14.3 2.8 %collective-permute-start.1 = (s32[1,256]{1,0:T(1,128)}, s32[1,256]{1,0:T(1,128)S(1)}, u32[]{:S(2)}, u32[]{:S(2)}) collective-permute-start(s32[1,256]{1,0:T(1,128)} %bitcast.3), channel_id=1, source_target_pairs={{0,1},{1,0},{2,3},{3,2},{4,5},{5,4},{6,7},{7,6},{8,9},{9,8},{10,11... | collective-permute-start | bytes 3080 | tf_op jit(solution)/shard_map/ppermute | solution.py:178
  17.1 3.3 %copy-start = (s32[256]{0:T(256)S(1)}, s32[256]{0:T(256)}, u32[]{:S(2)}) copy-start(s32[256]{0:T(256)} %param.7) | copy-start | bytes 3076
  20.3 2.4 %collective-permute-start.5 = (bf16[256,1152]{1,0:T(8,128)(2,1)S(1)}, bf16[256,1152]{1,0:T(8,128)(2,1)S(1)}, u32[]{:S(2)}, u32[]{:S(2)}) collective-permute-start(bf16[256,1152]{1,0:T(8,128)(2,1)S(1)} %get-tuple-element.30), channel_id=1, source_target_pairs={{0,1},{1,0},{2,3},{3,2},{4,5},{5,4},{6,7},{7,6},{8,9},{9,8},{10,11... | collective-permute-start | bytes 1769480 | tf_op jit(solution)/shard_map/ppermute | solution.py:178
  21.8 6.3 %collective-permute-start.13 = (bf16[64,1152]{1,0:T(8,128)(2,1)S(1)}, bf16[64,1152]{1,0:T(8,128)(2,1)S(1)}, u32[]{:S(2)}, u32[]{:S(2)}) collective-permute-start(bf16[64,1152]{1,0:T(8,128)(2,1)S(1)} %get-tuple-element.37), channel_id=1, source_target_pairs={{0,2},{1,3},{2,0},{3,1},{4,6},{5,7},{6,4},{7,5},{8,10},{9,11},{10,... | collective-permute-start | bytes 442376 | tf_op jit(solution)/shard_map/ppermute | solution.py:178
  22.9 7.8 %collective-permute-start.6 = (bf16[64,1152]{1,0:T(8,128)(2,1)S(1)}, bf16[64,1152]{1,0:T(8,128)(2,1)S(1)}, u32[]{:S(2)}, u32[]{:S(2)}) collective-permute-start(bf16[64,1152]{1,0:T(8,128)(2,1)S(1)} %get-tuple-element.32), channel_id=1, source_target_pairs={{0,24},{8,16},{16,8},{24,0},{1,25},{9,17},{17,9},{25,1},{2,26},{10... | collective-permute-start | bytes 442376 | tf_op jit(solution)/shard_map/ppermute | solution.py:178
  25.4 7.6 %collective-permute-start.7 = (bf16[64,1152]{1,0:T(8,128)(2,1)S(1)}, bf16[64,1152]{1,0:T(8,128)(2,1)S(1)}, u32[]{:S(2)}, u32[]{:S(2)}) collective-permute-start(bf16[64,1152]{1,0:T(8,128)(2,1)S(1)} %get-tuple-element.33), channel_id=1, source_target_pairs={{0,16},{8,24},{16,0},{24,8},{1,17},{9,25},{17,1},{25,9},{2,18},{10... | collective-permute-start | bytes 442376 | tf_op jit(solution)/shard_map/ppermute | solution.py:178
  25.9 7.2 %collective-permute-start.8 = (bf16[64,1152]{1,0:T(8,128)(2,1)S(1)}, bf16[64,1152]{1,0:T(8,128)(2,1)S(1)}, u32[]{:S(2)}, u32[]{:S(2)}) collective-permute-start(bf16[64,1152]{1,0:T(8,128)(2,1)S(1)} %get-tuple-element.34), channel_id=1, source_target_pairs={{0,8},{8,0},{16,24},{24,16},{1,9},{9,1},{17,25},{25,17},{2,10},{10... | collective-permute-start | bytes 442376 | tf_op jit(solution)/shard_map/ppermute | solution.py:178
  26.4 10.4 %collective-permute-start.12 = (bf16[64,1152]{1,0:T(8,128)(2,1)S(1)}, bf16[64,1152]{1,0:T(8,128)(2,1)S(1)}, u32[]{:S(2)}, u32[]{:S(2)}) collective-permute-start(bf16[64,1152]{1,0:T(8,128)(2,1)S(1)} %get-tuple-element.35), channel_id=1, source_target_pairs={{0,2},{1,3},{2,0},{3,1},{4,6},{5,7},{6,4},{7,5},{8,10},{9,11},{10,... | collective-permute-start | bytes 442376 | tf_op jit(solution)/shard_map/ppermute | solution.py:178
  28.2 9.6 %collective-permute-start.14 = (bf16[64,1152]{1,0:T(8,128)(2,1)S(1)}, bf16[64,1152]{1,0:T(8,128)(2,1)S(1)}, u32[]{:S(2)}, u32[]{:S(2)}) collective-permute-start(bf16[64,1152]{1,0:T(8,128)(2,1)S(1)} %shard_map.74), channel_id=1, source_target_pairs={{0,4},{1,5},{2,6},{3,7},{4,0},{5,1},{6,2},{7,3},{8,12},{9,13},{10,... | collective-permute-start | bytes 442376 | tf_op jit(solution)/shard_map/ppermute | solution.py:178
  33.3 7.7 %collective-permute-start.11 = (bf16[64,1152]{1,0:T(8,128)(2,1)S(1)}, bf16[64,1152]{1,0:T(8,128)(2,1)S(1)}, u32[]{:S(2)}, u32[]{:S(2)}) collective-permute-start(bf16[64,1152]{1,0:T(8,128)(2,1)S(1)} %shard_map.73.refs_0_), channel_id=1, source_target_pairs={{0,24},{8,16},{16,8},{24,0},{1,25},{9,17},{17,9},{25,1},{2,26},{10... | collective-permute-start | bytes 442376 | tf_op jit(solution)/shard_map/ppermute | solution.py:178
  35.0 8.1 %collective-permute-start.10 = (bf16[64,1152]{1,0:T(8,128)(2,1)S(1)}, bf16[64,1152]{1,0:T(8,128)(2,1)S(1)}, u32[]{:S(2)}, u32[]{:S(2)}) collective-permute-start(bf16[64,1152]{1,0:T(8,128)(2,1)S(1)} %shard_map.73.refs_0_), channel_id=1, source_target_pairs={{0,16},{8,24},{16,0},{24,8},{1,17},{9,25},{17,1},{25,9},{2,18},{10... | collective-permute-start | bytes 442376 | tf_op jit(solution)/shard_map/ppermute | solution.py:178
  36.3 6.9 %collective-permute-start.9 = (bf16[64,1152]{1,0:T(8,128)(2,1)S(1)}, bf16[64,1152]{1,0:T(8,128)(2,1)S(1)}, u32[]{:S(2)}, u32[]{:S(2)}) collective-permute-start(bf16[64,1152]{1,0:T(8,128)(2,1)S(1)} %shard_map.73.refs_0_), channel_id=1, source_target_pairs={{0,8},{8,0},{16,24},{24,16},{1,9},{9,1},{17,25},{25,17},{2,10},{10... | collective-permute-start | bytes 442376 | tf_op jit(solution)/shard_map/ppermute | solution.py:178

commit v9 on v7

--- a/solution.py
+++ b/solution.py
@@ -41,14 +41,17 @@
     return lax.rsqrt(jnp.sum(values * values, axis=1, keepdims=True) + EPSILON)
 
 
-def unit_txt_body(source, bf, unit_out, inv, held, sem):
+def unit_txt_body(source, bf, head, tail, unit_out, inv, held, sem):
     copy = pltpu.make_async_copy(source, held, sem)
     copy.start()
     copy.wait()
     values = held[...]
     inverse = inverse_norm(values)
     unit = values * inverse
-    bf[...] = unit.astype(BF16)
+    rounded = unit.astype(BF16)
+    bf[...] = rounded
+    head[...] = rounded[: head.shape[0]]
+    tail[...] = rounded[head.shape[0] :]
     unit_out[...] = unit
     inv[...] = jnp.broadcast_to(inverse, inv.shape)
 
@@ -191,9 +194,11 @@
 
     perm_other = swapped(perm_row, "txt", 1)
     raw_other = swapped(images, "txt", 1)
-    txt_bf, txt_unit, txt_inv = call(
+    first = txt_rows // 2
+    txt_bf, head, tail, txt_unit, txt_inv = call(
         unit_txt_body,
-        [struct(txt_rows, width, BF16), struct(txt_rows, width, F32), struct(txt_rows, 128, F32)],
+        [struct(size, width, BF16) for size in (txt_rows, first, txt_rows - first)]
+        + [struct(txt_rows, width, F32), struct(txt_rows, 128, F32)],
         [in_hbm(texts)],
         [ANY],
         16 << 20,
@@ -202,7 +207,7 @@
     )
     half = blocks // 2
     order = list(range(0, blocks, 2)) + list(range(1, blocks, 2))
-    far = [swapped(txt_bf, "txt", 4 * k) for k in range(1, half)]
+    far = [swapped(piece, "txt", 4 * k) for k in range(1, half) for piece in (head, tail)]
     near = [swapped(tile, "txt", 2) for tile in [txt_bf] + far]
     tiles = [txt_bf] + far + near
     img_bf, img_other, img_unit, img_inv = call(
@@ -220,7 +225,7 @@
         functools.partial(other_body, order, line),
         [struct(blocks * txt_rows, rows, BF16), struct(rows, width, BF16)],
         [*scalars, perm_other, img_other, *tiles],
-        [SMEM] * 4 + [VMEM] * (2 + blocks),
+        [SMEM] * 4 + [VMEM] * (2 + len(tiles)),
         40 << 20,
         2 * pairs,
     )
@@ -235,7 +240,7 @@
             struct((half - 1) * txt_rows, width, BF16),
         ],
         [*scalars, perm_row, img_bf, img_other, kept, *tiles],
-        [SMEM] * 4 + [VMEM] * (4 + blocks),
+        [SMEM] * 4 + [VMEM] * (4 + len(tiles)),
         40 << 20,
         4 * pairs,
     )

time: 44 us -> 42.4 us (0.964)
  waiting for transfers between devices: 16.9 us -> 12.6 us
  starting transfers between devices: 18.2 us -> 20.9 us
    ppermute x15 -> x17, waiting for transfers between devices: 16.9 us -> 12.6 us  [swapped(): return lax.ppermute(value, axis, [(s, s ^ step) for s in range(count)])]
    ppermute x15 -> x17, starting transfers between devices: 18.2 us -> 20.9 us  [swapped(): return lax.ppermute(value, axis, [(s, s ^ step) for s in range(count)])]
  transfers between devices with their start and end apart: 15 -> 17, of which waited for: 7 -> 8; matrix products, arithmetic and copies ran while one was open for 0% -> 0% of each run, Pallas kernels for 10% -> 10%
where the time goes in v9:
time: 42.4 us; the launch traced here: 42.2 us
  starting transfers between devices  20.9 us (49%)
  waiting for transfers between devices  12.6 us (30%)
  Pallas kernels  6.65 us (16%)
  between operations  2.03 us (5%)
    ppermute x17, starting transfers between devices, swapped(): return lax.ppermute(value, axis, [(s, s ^ step) for s in range(count)])  20.9 us
    ppermute x17, waiting for transfers between devices, swapped(): return lax.ppermute(value, axis, [(s, s ^ step) for s in range(count)])  12.6 us
    pallas_call x7, Pallas kernels, call(): pl.pallas_call(body, out_shape=outs, in_specs=specs, out_specs=[VMEM] * l...  5.38 us
    pallas_call x1, Pallas kernels, local(): pl.pallas_call(functools.partial(last_body, count), out_shape=[struct(row...  1.28 us
  transfers between devices with their start and end apart: 17, of which 8 were waited for; matrix products, arithmetic and copies ran while one was open for 0% of the time, Pallas kernels for 10%

profile of v9, /device:TPU:0, one launch (start us, length us, event | category | flops | bytes accessed | tf_op | source)
XLA Modules:
  0.0 42.2 jit_solution(8268222929124824358)
XLA Ops:
  0.6 0.5 %collective-permute-start = (f32[256,1152]{1,0:T(8,128)}, f32[256,1152]{1,0:T(8,128)S(1)}, u32[]{:S(2)}, u32[]{:S(2)}) collective-permute-start(f32[256,1152]{1,0:T(8,128)} %source.3), channel_id=1, source_target_pairs={{0,1},{1,0},{2,3},{3,2},{4,5},{5,4},{6,7},{7,6},{8,9},{9,8},{10,11... | collective-permute-start | bytes 3538952 | tf_op jit(solution)/shard_map/ppermute | solution.py:181
  1.1 1.1 %shard_map.68 = (bf16[64,1152]{1,0:T(8,128)(2,1)S(1)}, bf16[32,1152]{1,0:T(8,128)(2,1)S(1)}, bf16[32,1152]{1,0:T(8,128)(2,1)S(1)}, f32[64,1152]{1,0:T(8,128)S(1)}, f32[64,128]{1,0:T(8,128)S(1)}) custom-call(f32[64,1152]{1,0:T(8,128)} %source.2), custom_call_target="tpu_custom_call" | custom-call | flops 294912 | bytes 917504 | tf_op jit(solution)/shard_map/pallas_call | solution.py:25
  2.3 3.7 %collective-permute-start.2 = (bf16[32,1152]{1,0:T(8,128)(2,1)S(1)}, bf16[32,1152]{1,0:T(8,128)(2,1)S(1)}, u32[]{:S(2)}, u32[]{:S(2)}) collective-permute-start(bf16[32,1152]{1,0:T(8,128)(2,1)S(1)} %get-tuple-element.27), channel_id=1, source_target_pairs={{0,4},{1,5},{2,6},{3,7},{4,0},{5,1},{6,2},{7,3},{8,12},{9,13},{10,... | collective-permute-start | bytes 221192 | tf_op jit(solution)/shard_map/ppermute | solution.py:181
  5.9 0.1 collective-permute-start.3
  6.0 1.8 %collective-permute-start.4 = (bf16[64,1152]{1,0:T(8,128)(2,1)S(1)}, bf16[64,1152]{1,0:T(8,128)(2,1)S(1)}, u32[]{:S(2)}, u32[]{:S(2)}) collective-permute-start(bf16[64,1152]{1,0:T(8,128)(2,1)S(1)} %get-tuple-element.26.refs_0_), channel_id=1, source_target_pairs={{0,2},{1,3},{2,0},{3,1},{4,6},{5,7},{6,4},{7,5},{8,10},{9,11},{10,... | collective-permute-start | bytes 442376 | tf_op jit(solution)/shard_map/ppermute | solution.py:181
  7.8 2.9 %collective-permute-done.2.refs_1_ = bf16[32,1152]{1,0:T(8,128)(2,1)S(1)} collective-permute-done((bf16[32,1152]{1,0:T(8,128)(2,1)S(1)}, bf16[32,1152]{1,0:T(8,128)(2,1)S(1)}, u32[]{:S(2)}, u32[]{:S(2)}) %collective-permute-start.2) | collective-permute-done | bytes 73760 | tf_op jit(solution)/shard_map/ppermute | solution.py:181
  10.7 2.1 %collective-permute-start.5 = (bf16[32,1152]{1,0:T(8,128)(2,1)S(1)}, bf16[32,1152]{1,0:T(8,128)(2,1)S(1)}, u32[]{:S(2)}, u32[]{:S(2)}) collective-permute-start(bf16[32,1152]{1,0:T(8,128)(2,1)S(1)} %collective-permute-done.2.refs_1_), channel_id=1, source_target_pairs={{0,2},{1,3},{2,0},{3,1},{4,6},{5,7},{6,4},{7,5},{8,10},{9,11},{10,... | collective-permute-start | bytes 221192 | tf_op jit(solution)/shard_map/ppermute | solution.py:181
  12.8 0.9 %collective-permute-done.3.refs_2_ = bf16[32,1152]{1,0:T(8,128)(2,1)S(1)} collective-permute-done((bf16[32,1152]{1,0:T(8,128)(2,1)S(1)}, bf16[32,1152]{1,0:T(8,128)(2,1)S(1)}, u32[]{:S(2)}, u32[]{:S(2)}) %collective-permute-start.3) | collective-permute-done | bytes 73760 | tf_op jit(solution)/shard_map/ppermute | solution.py:181
  13.7 0.7 %collective-permute-start.6 = (bf16[32,1152]{1,0:T(8,128)(2,1)S(1)}, bf16[32,1152]{1,0:T(8,128)(2,1)S(1)}, u32[]{:S(2)}, u32[]{:S(2)}) collective-permute-start(bf16[32,1152]{1,0:T(8,128)(2,1)S(1)} %collective-permute-done.3.refs_2_), channel_id=1, source_target_pairs={{0,2},{1,3},{2,0},{3,1},{4,6},{5,7},{6,4},{7,5},{8,10},{9,11},{10,... | collective-permute-start | bytes 221192 | tf_op jit(solution)/shard_map/ppermute | solution.py:181
  14.4 0.0 collective-permute-start.1
  15.7 0.0 collective-permute-done.other
  15.7 1.5 %shard_map.69 = (bf16[256,1152]{1,0:T(8,128)(2,1)S(1)}, bf16[256,1152]{1,0:T(8,128)(2,1)S(1)}, f32[64,1152]{1,0:T(8,128)S(1)}, f32[64,128]{1,0:T(8,128)S(1)}) custom-call(s32[1]{0:T(128)} %bitcast.place.position, f32[256,1152]{1,0:T(8,128)S(1)} %collective-permute-done.other, f32[256,1152]{1,0:T(8,128)} %source.3), custom_call_target="tpu_custom_call" | custom-call | flops 2359296 | bytes 3866628 | tf_op jit(solution)/shard_map/pallas_call | solution.py:25
  17.2 0.0 copy-start
  17.2 0.0 collective-permute-done.1.perm
  17.2 0.0 collective-permute-done.5.refs_4_
  17.2 0.8 %collective-permute-done.6.refs_5_ = bf16[32,1152]{1,0:T(8,128)(2,1)S(1)} collective-permute-done((bf16[32,1152]{1,0:T(8,128)(2,1)S(1)}, bf16[32,1152]{1,0:T(8,128)(2,1)S(1)}, u32[]{:S(2)}, u32[]{:S(2)}) %collective-permute-start.6) | collective-permute-done | bytes 73760 | tf_op jit(solution)/shard_map/ppermute | solution.py:181
  18.1 0.0 collective-permute-done.4.refs_3_
  18.1 1.0 %shard_map.70 = (bf16[256,256]{1,0:T(8,128)(2,1)S(1)}, bf16[256,1152]{1,0:T(8,128)(2,1)S(1)}) custom-call(s32[1]{0:T(128)} %bitcast.place.position, s32[1]{0:T(128)} %bitcast.1.column, f32[1]{0:T(128)S(6)} %copy.7.scale, f32[1]{0:T(128)S(6)} %copy.8.shift, s32[1,256]{1,0:T(1,128)S(1)} %collective-permute-done.1.perm, ...), custom_call_target="tpu_custom_call" | custom-call | flops 301989888 | bytes 1901584 | tf_op jit(solution)/shard_map/pallas_call | solution.py:25
  19.1 0.1 collective-permute-start.7
  19.2 0.0 copy-done
  19.2 1.4 %shard_map.71 = (f32[256,1152]{1,0:T(8,128)S(1)}, f32[64,1152]{1,0:T(8,128)S(1)}, f32[64,1152]{1,0:T(8,128)S(1)}, bf16[64,1152]{1,0:T(8,128)(2,1)S(1)}, bf16[64,1152]{1,0:T(8,128)(2,1)S(1)}) custom-call(s32[1]{0:T(128)} %bitcast.place.position, s32[1]{0:T(128)} %bitcast.1.column, f32[1]{0:T(128)S(6)} %copy.7.scale, f32[1]{0:T(128)S(6)} %copy.8.shift, ...), custom_call_target="tpu_custom_call" | custom-call | flops 603979776 | bytes 3965968 | tf_op jit(solution)/shard_map/pallas_call | solution.py:25
  20.6 1.1 %collective-permute-start.15 = (bf16[64,1152]{1,0:T(8,128)(2,1)S(1)}, bf16[64,1152]{1,0:T(8,128)(2,1)S(1)}, u32[]{:S(2)}, u32[]{:S(2)}) collective-permute-start(bf16[64,1152]{1,0:T(8,128)(2,1)S(1)} %get-tuple-element.41), channel_id=1, source_target_pairs={{0,2},{1,3},{2,0},{3,1},{4,6},{5,7},{6,4},{7,5},{8,10},{9,11},{10,... | collective-permute-start | bytes 442376 | tf_op jit(solution)/shard_map/ppermute | solution.py:181
  21.6 0.0 collective-permute-done.7.other
  21.6 0.2 shard_map.72
  21.8 1.6 %collective-permute-start.8 = (bf16[64,1152]{1,0:T(8,128)(2,1)S(1)}, bf16[64,1152]{1,0:T(8,128)(2,1)S(1)}, u32[]{:S(2)}, u32[]{:S(2)}) collective-permute-start(bf16[64,1152]{1,0:T(8,128)(2,1)S(1)} %get-tuple-element.36), channel_id=1, source_target_pairs={{0,8},{8,0},{16,24},{24,16},{1,9},{9,1},{17,25},{25,17},{2,10},{10... | collective-permute-start | bytes 442376 | tf_op jit(solution)/shard_map/ppermute | solution.py:181
  23.4 1.5 %collective-permute-start.9 = (bf16[64,1152]{1,0:T(8,128)(2,1)S(1)}, bf16[64,1152]{1,0:T(8,128)(2,1)S(1)}, u32[]{:S(2)}, u32[]{:S(2)}) collective-permute-start(bf16[64,1152]{1,0:T(8,128)(2,1)S(1)} %get-tuple-element.37), channel_id=1, source_target_pairs={{0,16},{8,24},{16,0},{24,8},{1,17},{9,25},{17,1},{25,9},{2,18},{10... | collective-permute-start | bytes 442376 | tf_op jit(solution)/shard_map/ppermute | solution.py:181
  24.9 0.4 %collective-permute-start.10 = (bf16[64,1152]{1,0:T(8,128)(2,1)S(1)}, bf16[64,1152]{1,0:T(8,128)(2,1)S(1)}, u32[]{:S(2)}, u32[]{:S(2)}) collective-permute-start(bf16[64,1152]{1,0:T(8,128)(2,1)S(1)} %get-tuple-element.38), channel_id=1, source_target_pairs={{0,24},{8,16},{16,8},{24,0},{1,25},{9,17},{17,9},{25,1},{2,26},{10... | collective-permute-start | bytes 442376 | tf_op jit(solution)/shard_map/ppermute | solution.py:181
  25.4 1.0 %collective-permute-start.14 = (bf16[64,1152]{1,0:T(8,128)(2,1)S(1)}, bf16[64,1152]{1,0:T(8,128)(2,1)S(1)}, u32[]{:S(2)}, u32[]{:S(2)}) collective-permute-start(bf16[64,1152]{1,0:T(8,128)(2,1)S(1)} %get-tuple-element.39), channel_id=1, source_target_pairs={{0,2},{1,3},{2,0},{3,1},{4,6},{5,7},{6,4},{7,5},{8,10},{9,11},{10,... | collective-permute-start | bytes 442376 | tf_op jit(solution)/shard_map/ppermute | solution.py:181
  26.4 0.5 %collective-permute-done.15.got = bf16[64,1152]{1,0:T(8,128)(2,1)S(1)} collective-permute-done((bf16[64,1152]{1,0:T(8,128)(2,1)S(1)}, bf16[64,1152]{1,0:T(8,128)(2,1)S(1)}, u32[]{:S(2)}, u32[]{:S(2)}) %collective-permute-start.15) | collective-permute-done | bytes 147488 | tf_op jit(solution)/shard_map/ppermute | solution.py:181
  26.9 2.7 %collective-permute-start.16 = (bf16[64,1152]{1,0:T(8,128)(2,1)S(1)}, bf16[64,1152]{1,0:T(8,128)(2,1)S(1)}, u32[]{:S(2)}, u32[]{:S(2)}) collective-permute-start(bf16[64,1152]{1,0:T(8,128)(2,1)S(1)} %shard_map.74), channel_id=1, source_target_pairs={{0,4},{1,5},{2,6},{3,7},{4,0},{5,1},{6,2},{7,3},{8,12},{9,13},{10,... | collective-permute-start | bytes 442376 | tf_op jit(solution)/shard_map/ppermute | solution.py:181
  29.6 0.0 collective-permute-done.8.refs_0_
  29.6 2.3 %collective-permute-done.9.refs_1_ = bf16[64,1152]{1,0:T(8,128)(2,1)S(1)} collective-permute-done((bf16[64,1152]{1,0:T(8,128)(2,1)S(1)}, bf16[64,1152]{1,0:T(8,128)(2,1)S(1)}, u32[]{:S(2)}, u32[]{:S(2)}) %collective-permute-start.9) | collective-permute-done | bytes 147488 | tf_op jit(solution)/shard_map/ppermute | solution.py:181
  31.9 0.0 collective-permute-done.10.refs_2_
  31.9 0.2 shard_map.73.refs_0_
  32.1 1.6 %collective-permute-start.13 = (bf16[64,1152]{1,0:T(8,128)(2,1)S(1)}, bf16[64,1152]{1,0:T(8,128)(2,1)S(1)}, u32[]{:S(2)}, u32[]{:S(2)}) collective-permute-start(bf16[64,1152]{1,0:T(8,128)(2,1)S(1)} %shard_map.73.refs_0_), channel_id=1, source_target_pairs={{0,24},{8,16},{16,8},{24,0},{1,25},{9,17},{17,9},{25,1},{2,26},{10... | collective-permute-start | bytes 442376 | tf_op jit(solution)/shard_map/ppermute | solution.py:181
  33.6 1.2 %collective-permute-start.12 = (bf16[64,1152]{1,0:T(8,128)(2,1)S(1)}, bf16[64,1152]{1,0:T(8,128)(2,1)S(1)}, u32[]{:S(2)}, u32[]{:S(2)}) collective-permute-start(bf16[64,1152]{1,0:T(8,128)(2,1)S(1)} %shard_map.73.refs_0_), channel_id=1, source_target_pairs={{0,16},{8,24},{16,0},{24,8},{1,17},{9,25},{17,1},{25,9},{2,18},{10... | collective-permute-start | bytes 442376 | tf_op jit(solution)/shard_map/ppermute | solution.py:181
  34.8 0.8 %collective-permute-start.11 = (bf16[64,1152]{1,0:T(8,128)(2,1)S(1)}, bf16[64,1152]{1,0:T(8,128)(2,1)S(1)}, u32[]{:S(2)}, u32[]{:S(2)}) collective-permute-start(bf16[64,1152]{1,0:T(8,128)(2,1)S(1)} %shard_map.73.refs_0_), channel_id=1, source_target_pairs={{0,8},{8,0},{16,24},{24,16},{1,9},{9,1},{17,25},{25,17},{2,10},{10... | collective-permute-start | bytes 442376 | tf_op jit(solution)/shard_map/ppermute | solution.py:181
  35.6 0.0 collective-permute-done.14.refs_4_
  35.6 0.9 %collective-permute-done.16.refs_5_ = bf16[64,1152]{1,0:T(8,128)(2,1)S(1)} collective-permute-done((bf16[64,1152]{1,0:T(8,128)(2,1)S(1)}, bf16[64,1152]{1,0:T(8,128)(2,1)S(1)}, u32[]{:S(2)}, u32[]{:S(2)}) %collective-permute-start.16) | collective-permute-done | bytes 147488 | tf_op jit(solution)/shard_map/ppermute | solution.py:181
  36.5 2.8 %collective-permute-done.13.refs_3_ = bf16[64,1152]{1,0:T(8,128)(2,1)S(1)} collective-permute-done((bf16[64,1152]{1,0:T(8,128)(2,1)S(1)}, bf16[64,1152]{1,0:T(8,128)(2,1)S(1)}, u32[]{:S(2)}, u32[]{:S(2)}) %collective-permute-start.13) | collective-permute-done | bytes 147488 | tf_op jit(solution)/shard_map/ppermute | solution.py:181
  39.4 1.5 %collective-permute-done.12.refs_2_ = bf16[64,1152]{1,0:T(8,128)(2,1)S(1)} collective-permute-done((bf16[64,1152]{1,0:T(8,128)(2,1)S(1)}, bf16[64,1152]{1,0:T(8,128)(2,1)S(1)}, u32[]{:S(2)}, u32[]{:S(2)}) %collective-permute-start.12) | collective-permute-done | bytes 147488 | tf_op jit(solution)/shard_map/ppermute | solution.py:181
  40.9 0.0 collective-permute-done.11.refs_1_
  40.9 1.3 %shard_map.75 = (f32[256,1152]{1,0:T(8,128)}, f32[64,1152]{1,0:T(8,128)}) custom-call(s32[1]{0:T(128)} %bitcast.place.position, f32[1]{0:T(128)S(6)} %copy.7.scale, f32[64,1152]{1,0:T(8,128)S(1)} %get-tuple-element.22.unit, f32[64,128]{1,0:T(8,128)S(1)} %get-tuple-element.23.inverse, f32[64,1152]{1,0:T(8,128)S(1)} %get-tuple-element.30.own, ...), custom_call_target="tpu_custom_call" | custom-call | flops 737280 | bytes 2359296 | tf_op jit(solution)/shard_map/pallas_call | solution.py:275
  (1 shorter events, 0.0 us)
Async XLA Ops:
  0.6 15.1 %collective-permute-start = (f32[256,1152]{1,0:T(8,128)}, f32[256,1152]{1,0:T(8,128)S(1)}, u32[]{:S(2)}, u32[]{:S(2)}) collective-permute-start(f32[256,1152]{1,0:T(8,128)} %source.3), channel_id=1, source_target_pairs={{0,1},{1,0},{2,3},{3,2},{4,5},{5,4},{6,7},{7,6},{8,9},{9,8},{10,11... | collective-permute-start | bytes 3538952 | tf_op jit(solution)/shard_map/ppermute | solution.py:181
  2.3 8.5 %collective-permute-start.2 = (bf16[32,1152]{1,0:T(8,128)(2,1)S(1)}, bf16[32,1152]{1,0:T(8,128)(2,1)S(1)}, u32[]{:S(2)}, u32[]{:S(2)}) collective-permute-start(bf16[32,1152]{1,0:T(8,128)(2,1)S(1)} %get-tuple-element.27), channel_id=1, source_target_pairs={{0,4},{1,5},{2,6},{3,7},{4,0},{5,1},{6,2},{7,3},{8,12},{9,13},{10,... | collective-permute-start | bytes 221192 | tf_op jit(solution)/shard_map/ppermute | solution.py:181
  5.9 7.8 %collective-permute-start.3 = (bf16[32,1152]{1,0:T(8,128)(2,1)S(1)}, bf16[32,1152]{1,0:T(8,128)(2,1)S(1)}, u32[]{:S(2)}, u32[]{:S(2)}) collective-permute-start(bf16[32,1152]{1,0:T(8,128)(2,1)S(1)} %get-tuple-element.28), channel_id=1, source_target_pairs={{0,4},{1,5},{2,6},{3,7},{4,0},{5,1},{6,2},{7,3},{8,12},{9,13},{10,... | collective-permute-start | bytes 221192 | tf_op jit(solution)/shard_map/ppermute | solution.py:181
  6.0 12.1 %collective-permute-start.4 = (bf16[64,1152]{1,0:T(8,128)(2,1)S(1)}, bf16[64,1152]{1,0:T(8,128)(2,1)S(1)}, u32[]{:S(2)}, u32[]{:S(2)}) collective-permute-start(bf16[64,1152]{1,0:T(8,128)(2,1)S(1)} %get-tuple-element.26.refs_0_), channel_id=1, source_target_pairs={{0,2},{1,3},{2,0},{3,1},{4,6},{5,7},{6,4},{7,5},{8,10},{9,11},{10,... | collective-permute-start | bytes 442376 | tf_op jit(solution)/shard_map/ppermute | solution.py:181
  10.7 6.5 %collective-permute-start.5 = (bf16[32,1152]{1,0:T(8,128)(2,1)S(1)}, bf16[32,1152]{1,0:T(8,128)(2,1)S(1)}, u32[]{:S(2)}, u32[]{:S(2)}) collective-permute-start(bf16[32,1152]{1,0:T(8,128)(2,1)S(1)} %collective-permute-done.2.refs_1_), channel_id=1, source_target_pairs={{0,2},{1,3},{2,0},{3,1},{4,6},{5,7},{6,4},{7,5},{8,10},{9,11},{10,... | collective-permute-start | bytes 221192 | tf_op jit(solution)/shard_map/ppermute | solution.py:181
  13.7 4.4 %collective-permute-start.6 = (bf16[32,1152]{1,0:T(8,128)(2,1)S(1)}, bf16[32,1152]{1,0:T(8,128)(2,1)S(1)}, u32[]{:S(2)}, u32[]{:S(2)}) collective-permute-start(bf16[32,1152]{1,0:T(8,128)(2,1)S(1)} %collective-permute-done.3.refs_2_), channel_id=1, source_target_pairs={{0,2},{1,3},{2,0},{3,1},{4,6},{5,7},{6,4},{7,5},{8,10},{9,11},{10,... | collective-permute-start | bytes 221192 | tf_op jit(solution)/shard_map/ppermute | solution.py:181
  14.4 2.8 %collective-permute-start.1 = (s32[1,256]{1,0:T(1,128)}, s32[1,256]{1,0:T(1,128)S(1)}, u32[]{:S(2)}, u32[]{:S(2)}) collective-permute-start(s32[1,256]{1,0:T(1,128)} %bitcast.3), channel_id=1, source_target_pairs={{0,1},{1,0},{2,3},{3,2},{4,5},{5,4},{6,7},{7,6},{8,9},{9,8},{10,11... | collective-permute-start | bytes 3080 | tf_op jit(solution)/shard_map/ppermute | solution.py:181
  17.2 2.0 %copy-start = (s32[256]{0:T(256)S(1)}, s32[256]{0:T(256)}, u32[]{:S(2)}) copy-start(s32[256]{0:T(256)} %param.7) | copy-start | bytes 3076
  19.1 2.6 %collective-permute-start.7 = (bf16[256,1152]{1,0:T(8,128)(2,1)S(1)}, bf16[256,1152]{1,0:T(8,128)(2,1)S(1)}, u32[]{:S(2)}, u32[]{:S(2)}) collective-permute-start(bf16[256,1152]{1,0:T(8,128)(2,1)S(1)} %get-tuple-element.34), channel_id=1, source_target_pairs={{0,1},{1,0},{2,3},{3,2},{4,5},{5,4},{6,7},{7,6},{8,9},{9,8},{10,11... | collective-permute-start | bytes 1769480 | tf_op jit(solution)/shard_map/ppermute | solution.py:181
  20.6 6.3 %collective-permute-start.15 = (bf16[64,1152]{1,0:T(8,128)(2,1)S(1)}, bf16[64,1152]{1,0:T(8,128)(2,1)S(1)}, u32[]{:S(2)}, u32[]{:S(2)}) collective-permute-start(bf16[64,1152]{1,0:T(8,128)(2,1)S(1)} %get-tuple-element.41), channel_id=1, source_target_pairs={{0,2},{1,3},{2,0},{3,1},{4,6},{5,7},{6,4},{7,5},{8,10},{9,11},{10,... | collective-permute-start | bytes 442376 | tf_op jit(solution)/shard_map/ppermute | solution.py:181
  21.8 7.8 %collective-permute-start.8 = (bf16[64,1152]{1,0:T(8,128)(2,1)S(1)}, bf16[64,1152]{1,0:T(8,128)(2,1)S(1)}, u32[]{:S(2)}, u32[]{:S(2)}) collective-permute-start(bf16[64,1152]{1,0:T(8,128)(2,1)S(1)} %get-tuple-element.36), channel_id=1, source_target_pairs={{0,8},{8,0},{16,24},{24,16},{1,9},{9,1},{17,25},{25,17},{2,10},{10... | collective-permute-start | bytes 442376 | tf_op jit(solution)/shard_map/ppermute | solution.py:181
  23.4 8.5 %collective-permute-start.9 = (bf16[64,1152]{1,0:T(8,128)(2,1)S(1)}, bf16[64,1152]{1,0:T(8,128)(2,1)S(1)}, u32[]{:S(2)}, u32[]{:S(2)}) collective-permute-start(bf16[64,1152]{1,0:T(8,128)(2,1)S(1)} %get-tuple-element.37), channel_id=1, source_target_pairs={{0,16},{8,24},{16,0},{24,8},{1,17},{9,25},{17,1},{25,9},{2,18},{10... | collective-permute-start | bytes 442376 | tf_op jit(solution)/shard_map/ppermute | solution.py:181
  24.9 7.0 %collective-permute-start.10 = (bf16[64,1152]{1,0:T(8,128)(2,1)S(1)}, bf16[64,1152]{1,0:T(8,128)(2,1)S(1)}, u32[]{:S(2)}, u32[]{:S(2)}) collective-permute-start(bf16[64,1152]{1,0:T(8,128)(2,1)S(1)} %get-tuple-element.38), channel_id=1, source_target_pairs={{0,24},{8,16},{16,8},{24,0},{1,25},{9,17},{17,9},{25,1},{2,26},{10... | collective-permute-start | bytes 442376 | tf_op jit(solution)/shard_map/ppermute | solution.py:181
  25.4 10.3 %collective-permute-start.14 = (bf16[64,1152]{1,0:T(8,128)(2,1)S(1)}, bf16[64,1152]{1,0:T(8,128)(2,1)S(1)}, u32[]{:S(2)}, u32[]{:S(2)}) collective-permute-start(bf16[64,1152]{1,0:T(8,128)(2,1)S(1)} %get-tuple-element.39), channel_id=1, source_target_pairs={{0,2},{1,3},{2,0},{3,1},{4,6},{5,7},{6,4},{7,5},{8,10},{9,11},{10,... | collective-permute-start | bytes 442376 | tf_op jit(solution)/shard_map/ppermute | solution.py:181
  26.9 9.6 %collective-permute-start.16 = (bf16[64,1152]{1,0:T(8,128)(2,1)S(1)}, bf16[64,1152]{1,0:T(8,128)(2,1)S(1)}, u32[]{:S(2)}, u32[]{:S(2)}) collective-permute-start(bf16[64,1152]{1,0:T(8,128)(2,1)S(1)} %shard_map.74), channel_id=1, source_target_pairs={{0,4},{1,5},{2,6},{3,7},{4,0},{5,1},{6,2},{7,3},{8,12},{9,13},{10,... | collective-permute-start | bytes 442376 | tf_op jit(solution)/shard_map/ppermute | solution.py:181
  32.1 7.3 %collective-permute-start.13 = (bf16[64,1152]{1,0:T(8,128)(2,1)S(1)}, bf16[64,1152]{1,0:T(8,128)(2,1)S(1)}, u32[]{:S(2)}, u32[]{:S(2)}) collective-permute-start(bf16[64,1152]{1,0:T(8,128)(2,1)S(1)} %shard_map.73.refs_0_), channel_id=1, source_target_pairs={{0,24},{8,16},{16,8},{24,0},{1,25},{9,17},{17,9},{25,1},{2,26},{10... | collective-permute-start | bytes 442376 | tf_op jit(solution)/shard_map/ppermute | solution.py:181
  33.6 7.2 %collective-permute-start.12 = (bf16[64,1152]{1,0:T(8,128)(2,1)S(1)}, bf16[64,1152]{1,0:T(8,128)(2,1)S(1)}, u32[]{:S(2)}, u32[]{:S(2)}) collective-permute-start(bf16[64,1152]{1,0:T(8,128)(2,1)S(1)} %shard_map.73.refs_0_), channel_id=1, source_target_pairs={{0,16},{8,24},{16,0},{24,8},{1,17},{9,25},{17,1},{25,9},{2,18},{10... | collective-permute-start | bytes 442376 | tf_op jit(solution)/shard_map/ppermute | solution.py:181
  34.8 6.0 %collective-permute-start.11 = (bf16[64,1152]{1,0:T(8,128)(2,1)S(1)}, bf16[64,1152]{1,0:T(8,128)(2,1)S(1)}, u32[]{:S(2)}, u32[]{:S(2)}) collective-permute-start(bf16[64,1152]{1,0:T(8,128)(2,1)S(1)} %shard_map.73.refs_0_), channel_id=1, source_target_pairs={{0,8},{8,0},{16,24},{24,16},{1,9},{9,1},{17,25},{25,17},{2,10},{10... | collective-permute-start | bytes 442376 | tf_op jit(solution)/shard_map/ppermute | solution.py:181

commit v10 on v9

--- a/solution.py
+++ b/solution.py
@@ -123,15 +123,14 @@
         out[...] = (mine + got[k * rows : (k + 1) * rows, :].astype(F32)).astype(BF16)
 
 
-def split_body(count, position, own, other, keep, *send):
+def split_body(partners, place, column, own, other, keep, *send):
     rows = keep.shape[0]
-    for k in range(count):
-        start = pl.multiple_of((position[0] ^ k) * rows, rows)
+    core = column[0] & 1
+    for out, (even, odd) in zip([keep, *send], [(0, 0), *partners]):
+        block = place[0] ^ (even + core * (odd - even))
+        start = pl.multiple_of(block * rows, rows)
         part = own[pl.ds(start, rows), :] + other[pl.ds(start, rows), :].astype(F32)
-        if k == 0:
-            keep[...] = part
-        else:
-            send[k - 1][...] = part.astype(BF16)
+        out[...] = part.astype(out.dtype)
 
 
 def total_of(own, parts):
@@ -181,6 +180,16 @@
     return lax.ppermute(value, axis, [(s, s ^ step) for s in range(count)])
 
 
+def plane_swapped(value, even, odd):
+    count, line = lax.axis_size("img"), lax.axis_size("txt")
+    pairs = [
+        (i * line + t, (i ^ (odd if t % 2 else even)) * line + t)
+        for i in range(count)
+        for t in range(line)
+    ]
+    return lax.ppermute(value, ("img", "txt"), pairs)
+
+
 def local(images, texts, perm, scale, shift):
     rows, width = images.shape
     txt_rows = texts.shape[0]
@@ -254,15 +263,16 @@
     )
     back = [swapped(near_txt, "txt", 2)] + [swapped(sums[k - 1], "txt", 4 * k) for k in range(1, half)]
 
+    partners = [(1, 2), (2, 1)] + [(k, k) for k in range(3, count)]
     keep, *send = call(
-        functools.partial(split_body, count),
+        functools.partial(split_body, partners),
         [struct(part, width, F32)] + [struct(part, width, BF16)] * (count - 1),
-        [place, own_img, from_other],
-        [SMEM, VMEM, VMEM],
+        [place, column, own_img, from_other],
+        [SMEM] * 2 + [VMEM] * 2,
         24 << 20,
         rows * width,
     )
-    got = [swapped(send[k - 1], "img", k) for k in range(1, count)]
+    got = [plane_swapped(block, *pair) for block, pair in zip(send, partners)]
     (grad_part,) = call(
         finish_img_body,
         [struct(part, width, BF16)],

time: 42.4 us -> 43.4 us (1.024)
  waiting for transfers between devices: 12.6 us -> 13.7 us
    ppermute x0 -> x3, starting transfers between devices: none -> 3.55 us  [plane_swapped(): return lax.ppermute(value, ('img', 'txt'), pairs)]
    ppermute x17 -> x14, starting transfers between devices: 20.9 us -> 17.3 us  [swapped(): return lax.ppermute(value, axis, [(s, s ^ step) for s in range(count)])]
    ppermute x0 -> x3, waiting for transfers between devices: none -> 2.2 us  [plane_swapped(): return lax.ppermute(value, ('img', 'txt'), pairs)]
    ppermute x17 -> x14, waiting for transfers between devices: 12.6 us -> 11.5 us  [swapped(): return lax.ppermute(value, axis, [(s, s ^ step) for s in range(count)])]
  transfers between devices with their start and end apart: 17 -> 17, of which waited for: 8 -> 9; matrix products, arithmetic and copies ran while one was open for 0% -> 0% of each run, Pallas kernels for 10% -> 10%
where the time goes in v10:
time: 43.4 us; the launch traced here: 43.2 us
  starting transfers between devices  20.9 us (48%)
  waiting for transfers between devices  13.7 us (32%)
  Pallas kernels  6.6 us (15%)
  between operations  2.03 us (5%)
    ppermute x14, starting transfers between devices, swapped(): return lax.ppermute(value, axis, [(s, s ^ step) for s in range(count)])  17.3 us
    ppermute x14, waiting for transfers between devices, swapped(): return lax.ppermute(value, axis, [(s, s ^ step) for s in range(count)])  11.5 us
    pallas_call x7, Pallas kernels, call(): pl.pallas_call(body, out_shape=outs, in_specs=specs, out_specs=[VMEM] * l...  5.33 us
    ppermute x3, starting transfers between devices, plane_swapped(): return lax.ppermute(value, ('img', 'txt'), pairs)  3.55 us
    ppermute x3, waiting for transfers between devices, plane_swapped(): return lax.ppermute(value, ('img', 'txt'), pairs)  2.2 us
    pallas_call x1, Pallas kernels, local(): pl.pallas_call(functools.partial(last_body, count), out_shape=[struct(row...  1.28 us
  transfers between devices with their start and end apart: 17, of which 9 were waited for; matrix products, arithmetic and copies ran while one was open for 0% of the time, Pallas kernels for 10%

profile of v10, /device:TPU:0, one launch (start us, length us, event | category | flops | bytes accessed | tf_op | source)
XLA Modules:
  0.0 43.2 jit_solution(9497810021342314304)
XLA Ops:
  0.6 0.5 %collective-permute-start = (f32[256,1152]{1,0:T(8,128)}, f32[256,1152]{1,0:T(8,128)S(1)}, u32[]{:S(2)}, u32[]{:S(2)}) collective-permute-start(f32[256,1152]{1,0:T(8,128)} %source.3), channel_id=1, source_target_pairs={{0,1},{1,0},{2,3},{3,2},{4,5},{5,4},{6,7},{7,6},{8,9},{9,8},{10,11... | collective-permute-start | bytes 3538952 | tf_op jit(solution)/shard_map/ppermute | solution.py:180
  1.1 1.1 %shard_map.68 = (bf16[64,1152]{1,0:T(8,128)(2,1)S(1)}, bf16[32,1152]{1,0:T(8,128)(2,1)S(1)}, bf16[32,1152]{1,0:T(8,128)(2,1)S(1)}, f32[64,1152]{1,0:T(8,128)S(1)}, f32[64,128]{1,0:T(8,128)S(1)}) custom-call(f32[64,1152]{1,0:T(8,128)} %source.2), custom_call_target="tpu_custom_call" | custom-call | flops 294912 | bytes 917504 | tf_op jit(solution)/shard_map/pallas_call | solution.py:25
  2.3 3.7 %collective-permute-start.2 = (bf16[32,1152]{1,0:T(8,128)(2,1)S(1)}, bf16[32,1152]{1,0:T(8,128)(2,1)S(1)}, u32[]{:S(2)}, u32[]{:S(2)}) collective-permute-start(bf16[32,1152]{1,0:T(8,128)(2,1)S(1)} %get-tuple-element.27), channel_id=1, source_target_pairs={{0,4},{1,5},{2,6},{3,7},{4,0},{5,1},{6,2},{7,3},{8,12},{9,13},{10,... | collective-permute-start | bytes 221192 | tf_op jit(solution)/shard_map/ppermute | solution.py:180
  5.9 0.1 collective-permute-start.3
  6.0 1.8 %collective-permute-start.4 = (bf16[64,1152]{1,0:T(8,128)(2,1)S(1)}, bf16[64,1152]{1,0:T(8,128)(2,1)S(1)}, u32[]{:S(2)}, u32[]{:S(2)}) collective-permute-start(bf16[64,1152]{1,0:T(8,128)(2,1)S(1)} %get-tuple-element.26.refs_0_), channel_id=1, source_target_pairs={{0,2},{1,3},{2,0},{3,1},{4,6},{5,7},{6,4},{7,5},{8,10},{9,11},{10,... | collective-permute-start | bytes 442376 | tf_op jit(solution)/shard_map/ppermute | solution.py:180
  7.8 2.9 %collective-permute-done.2.refs_1_ = bf16[32,1152]{1,0:T(8,128)(2,1)S(1)} collective-permute-done((bf16[32,1152]{1,0:T(8,128)(2,1)S(1)}, bf16[32,1152]{1,0:T(8,128)(2,1)S(1)}, u32[]{:S(2)}, u32[]{:S(2)}) %collective-permute-start.2) | collective-permute-done | bytes 73760 | tf_op jit(solution)/shard_map/ppermute | solution.py:180
  10.7 2.1 %collective-permute-start.5 = (bf16[32,1152]{1,0:T(8,128)(2,1)S(1)}, bf16[32,1152]{1,0:T(8,128)(2,1)S(1)}, u32[]{:S(2)}, u32[]{:S(2)}) collective-permute-start(bf16[32,1152]{1,0:T(8,128)(2,1)S(1)} %collective-permute-done.2.refs_1_), channel_id=1, source_target_pairs={{0,2},{1,3},{2,0},{3,1},{4,6},{5,7},{6,4},{7,5},{8,10},{9,11},{10,... | collective-permute-start | bytes 221192 | tf_op jit(solution)/shard_map/ppermute | solution.py:180
  12.8 0.9 %collective-permute-done.3.refs_2_ = bf16[32,1152]{1,0:T(8,128)(2,1)S(1)} collective-permute-done((bf16[32,1152]{1,0:T(8,128)(2,1)S(1)}, bf16[32,1152]{1,0:T(8,128)(2,1)S(1)}, u32[]{:S(2)}, u32[]{:S(2)}) %collective-permute-start.3) | collective-permute-done | bytes 73760 | tf_op jit(solution)/shard_map/ppermute | solution.py:180
  13.7 0.7 %collective-permute-start.6 = (bf16[32,1152]{1,0:T(8,128)(2,1)S(1)}, bf16[32,1152]{1,0:T(8,128)(2,1)S(1)}, u32[]{:S(2)}, u32[]{:S(2)}) collective-permute-start(bf16[32,1152]{1,0:T(8,128)(2,1)S(1)} %collective-permute-done.3.refs_2_), channel_id=1, source_target_pairs={{0,2},{1,3},{2,0},{3,1},{4,6},{5,7},{6,4},{7,5},{8,10},{9,11},{10,... | collective-permute-start | bytes 221192 | tf_op jit(solution)/shard_map/ppermute | solution.py:180
  14.4 0.0 collective-permute-start.1
  15.7 0.0 collective-permute-done.other
  15.7 1.5 %shard_map.69 = (bf16[256,1152]{1,0:T(8,128)(2,1)S(1)}, bf16[256,1152]{1,0:T(8,128)(2,1)S(1)}, f32[64,1152]{1,0:T(8,128)S(1)}, f32[64,128]{1,0:T(8,128)S(1)}) custom-call(s32[1]{0:T(128)} %bitcast.place, f32[256,1152]{1,0:T(8,128)S(1)} %collective-permute-done.other, f32[256,1152]{1,0:T(8,128)} %source.3), custom_call_target="tpu_custom_call" | custom-call | flops 2359296 | bytes 3866628 | tf_op jit(solution)/shard_map/pallas_call | solution.py:25
  17.2 0.0 copy-start
  17.2 0.0 collective-permute-done.1.perm
  17.2 0.0 collective-permute-done.5.refs_4_
  17.2 0.8 %collective-permute-done.6.refs_5_ = bf16[32,1152]{1,0:T(8,128)(2,1)S(1)} collective-permute-done((bf16[32,1152]{1,0:T(8,128)(2,1)S(1)}, bf16[32,1152]{1,0:T(8,128)(2,1)S(1)}, u32[]{:S(2)}, u32[]{:S(2)}) %collective-permute-start.6) | collective-permute-done | bytes 73760 | tf_op jit(solution)/shard_map/ppermute | solution.py:180
  18.1 0.0 collective-permute-done.4.refs_3_
  18.1 1.0 %shard_map.70 = (bf16[256,256]{1,0:T(8,128)(2,1)S(1)}, bf16[256,1152]{1,0:T(8,128)(2,1)S(1)}) custom-call(s32[1]{0:T(128)} %bitcast.place, s32[1]{0:T(128)} %bitcast.1.column, f32[1]{0:T(128)S(6)} %copy.7.scale, f32[1]{0:T(128)S(6)} %copy.8.shift, s32[1,256]{1,0:T(1,128)S(1)} %collective-permute-done.1.perm, ...), custom_call_target="tpu_custom_call" | custom-call | flops 301989888 | bytes 1901584 | tf_op jit(solution)/shard_map/pallas_call | solution.py:25
  19.1 0.1 collective-permute-start.7
  19.2 0.0 copy-done
  19.2 1.4 %shard_map.71 = (f32[256,1152]{1,0:T(8,128)S(1)}, f32[64,1152]{1,0:T(8,128)S(1)}, f32[64,1152]{1,0:T(8,128)S(1)}, bf16[64,1152]{1,0:T(8,128)(2,1)S(1)}, bf16[64,1152]{1,0:T(8,128)(2,1)S(1)}) custom-call(s32[1]{0:T(128)} %bitcast.place, s32[1]{0:T(128)} %bitcast.1.column, f32[1]{0:T(128)S(6)} %copy.7.scale, f32[1]{0:T(128)S(6)} %copy.8.shift, ...), custom_call_target="tpu_custom_call" | custom-call | flops 603979776 | bytes 3965968 | tf_op jit(solution)/shard_map/pallas_call | solution.py:25
  20.6 1.1 %collective-permute-start.15 = (bf16[64,1152]{1,0:T(8,128)(2,1)S(1)}, bf16[64,1152]{1,0:T(8,128)(2,1)S(1)}, u32[]{:S(2)}, u32[]{:S(2)}) collective-permute-start(bf16[64,1152]{1,0:T(8,128)(2,1)S(1)} %get-tuple-element.41), channel_id=1, source_target_pairs={{0,2},{1,3},{2,0},{3,1},{4,6},{5,7},{6,4},{7,5},{8,10},{9,11},{10,... | collective-permute-start | bytes 442376 | tf_op jit(solution)/shard_map/ppermute | solution.py:180
  21.6 0.0 collective-permute-done.7.other
  21.6 0.1 shard_map.72
  21.8 1.6 %collective-permute-start.8 = (bf16[64,1152]{1,0:T(8,128)(2,1)S(1)}, bf16[64,1152]{1,0:T(8,128)(2,1)S(1)}, u32[]{:S(2)}, u32[]{:S(2)}) collective-permute-start(bf16[64,1152]{1,0:T(8,128)(2,1)S(1)} %get-tuple-element.36), channel_id=1, source_target_pairs={{0,8},{1,17},{2,10},{3,19},{4,12},{5,21},{6,14},{7,23},{8,0},{9,25... | collective-permute-start | bytes 442376 | tf_op jit(solution)/shard_map/ppermute | solution.py:190
  23.4 1.5 %collective-permute-start.9 = (bf16[64,1152]{1,0:T(8,128)(2,1)S(1)}, bf16[64,1152]{1,0:T(8,128)(2,1)S(1)}, u32[]{:S(2)}, u32[]{:S(2)}) collective-permute-start(bf16[64,1152]{1,0:T(8,128)(2,1)S(1)} %get-tuple-element.37), channel_id=1, source_target_pairs={{0,16},{1,9},{2,18},{3,11},{4,20},{5,13},{6,22},{7,15},{8,24},{9,1... | collective-permute-start | bytes 442376 | tf_op jit(solution)/shard_map/ppermute | solution.py:190
  24.9 0.4 collective-permute-start.10
  25.3 1.0 %collective-permute-start.14 = (bf16[64,1152]{1,0:T(8,128)(2,1)S(1)}, bf16[64,1152]{1,0:T(8,128)(2,1)S(1)}, u32[]{:S(2)}, u32[]{:S(2)}) collective-permute-start(bf16[64,1152]{1,0:T(8,128)(2,1)S(1)} %get-tuple-element.39), channel_id=1, source_target_pairs={{0,2},{1,3},{2,0},{3,1},{4,6},{5,7},{6,4},{7,5},{8,10},{9,11},{10,... | collective-permute-start | bytes 442376 | tf_op jit(solution)/shard_map/ppermute | solution.py:180
  26.3 0.5 %collective-permute-done.15.got = bf16[64,1152]{1,0:T(8,128)(2,1)S(1)} collective-permute-done((bf16[64,1152]{1,0:T(8,128)(2,1)S(1)}, bf16[64,1152]{1,0:T(8,128)(2,1)S(1)}, u32[]{:S(2)}, u32[]{:S(2)}) %collective-permute-start.15) | collective-permute-done | bytes 147488 | tf_op jit(solution)/shard_map/ppermute | solution.py:180
  26.9 2.7 %collective-permute-start.16 = (bf16[64,1152]{1,0:T(8,128)(2,1)S(1)}, bf16[64,1152]{1,0:T(8,128)(2,1)S(1)}, u32[]{:S(2)}, u32[]{:S(2)}) collective-permute-start(bf16[64,1152]{1,0:T(8,128)(2,1)S(1)} %shard_map.74), channel_id=1, source_target_pairs={{0,4},{1,5},{2,6},{3,7},{4,0},{5,1},{6,2},{7,3},{8,12},{9,13},{10,... | collective-permute-start | bytes 442376 | tf_op jit(solution)/shard_map/ppermute | solution.py:180
  29.6 0.0 collective-permute-done.8.refs_0_
  29.6 0.0 collective-permute-done.9.refs_1_
  29.6 2.2 %collective-permute-done.10.refs_2_ = bf16[64,1152]{1,0:T(8,128)(2,1)S(1)} collective-permute-done((bf16[64,1152]{1,0:T(8,128)(2,1)S(1)}, bf16[64,1152]{1,0:T(8,128)(2,1)S(1)}, u32[]{:S(2)}, u32[]{:S(2)}) %collective-permute-start.10) | collective-permute-done | bytes 147488 | tf_op jit(solution)/shard_map/ppermute | solution.py:190
  31.8 0.2 shard_map.73.refs_0_
  32.0 2.3 %collective-permute-start.13 = (bf16[64,1152]{1,0:T(8,128)(2,1)S(1)}, bf16[64,1152]{1,0:T(8,128)(2,1)S(1)}, u32[]{:S(2)}, u32[]{:S(2)}) collective-permute-start(bf16[64,1152]{1,0:T(8,128)(2,1)S(1)} %shard_map.73.refs_0_), channel_id=1, source_target_pairs={{0,24},{8,16},{16,8},{24,0},{1,25},{9,17},{17,9},{25,1},{2,26},{10... | collective-permute-start | bytes 442376 | tf_op jit(solution)/shard_map/ppermute | solution.py:180
  34.3 0.7 %collective-permute-start.12 = (bf16[64,1152]{1,0:T(8,128)(2,1)S(1)}, bf16[64,1152]{1,0:T(8,128)(2,1)S(1)}, u32[]{:S(2)}, u32[]{:S(2)}) collective-permute-start(bf16[64,1152]{1,0:T(8,128)(2,1)S(1)} %shard_map.73.refs_0_), channel_id=1, source_target_pairs={{0,16},{8,24},{16,0},{24,8},{1,17},{9,25},{17,1},{25,9},{2,18},{10... | collective-permute-start | bytes 442376 | tf_op jit(solution)/shard_map/ppermute | solution.py:180
  35.0 0.6 %collective-permute-start.11 = (bf16[64,1152]{1,0:T(8,128)(2,1)S(1)}, bf16[64,1152]{1,0:T(8,128)(2,1)S(1)}, u32[]{:S(2)}, u32[]{:S(2)}) collective-permute-start(bf16[64,1152]{1,0:T(8,128)(2,1)S(1)} %shard_map.73.refs_0_), channel_id=1, source_target_pairs={{0,8},{8,0},{16,24},{24,16},{1,9},{9,1},{17,25},{25,17},{2,10},{10... | collective-permute-start | bytes 442376 | tf_op jit(solution)/shard_map/ppermute | solution.py:180
  35.6 0.0 collective-permute-done.14.refs_4_
  35.6 1.0 %collective-permute-done.16.refs_5_ = bf16[64,1152]{1,0:T(8,128)(2,1)S(1)} collective-permute-done((bf16[64,1152]{1,0:T(8,128)(2,1)S(1)}, bf16[64,1152]{1,0:T(8,128)(2,1)S(1)}, u32[]{:S(2)}, u32[]{:S(2)}) %collective-permute-start.16) | collective-permute-done | bytes 147488 | tf_op jit(solution)/shard_map/ppermute | solution.py:180
  36.5 2.5 %collective-permute-done.13.refs_3_ = bf16[64,1152]{1,0:T(8,128)(2,1)S(1)} collective-permute-done((bf16[64,1152]{1,0:T(8,128)(2,1)S(1)}, bf16[64,1152]{1,0:T(8,128)(2,1)S(1)}, u32[]{:S(2)}, u32[]{:S(2)}) %collective-permute-start.13) | collective-permute-done | bytes 147488 | tf_op jit(solution)/shard_map/ppermute | solution.py:180
  39.0 2.7 %collective-permute-done.12.refs_2_ = bf16[64,1152]{1,0:T(8,128)(2,1)S(1)} collective-permute-done((bf16[64,1152]{1,0:T(8,128)(2,1)S(1)}, bf16[64,1152]{1,0:T(8,128)(2,1)S(1)}, u32[]{:S(2)}, u32[]{:S(2)}) %collective-permute-start.12) | collective-permute-done | bytes 147488 | tf_op jit(solution)/shard_map/ppermute | solution.py:180
  41.7 0.2 collective-permute-done.11.refs_1_
  41.9 1.3 %shard_map.75 = (f32[256,1152]{1,0:T(8,128)}, f32[64,1152]{1,0:T(8,128)}) custom-call(s32[1]{0:T(128)} %bitcast.place, f32[1]{0:T(128)S(6)} %copy.7.scale, f32[64,1152]{1,0:T(8,128)S(1)} %get-tuple-element.22.unit, f32[64,128]{1,0:T(8,128)S(1)} %get-tuple-element.23.inverse, f32[64,1152]{1,0:T(8,128)S(1)} %get-tuple-element.30.own, ...), custom_call_target="tpu_custom_call" | custom-call | flops 737280 | bytes 2359296 | tf_op jit(solution)/shard_map/pallas_call | solution.py:285
  (1 shorter events, 0.0 us)
Async XLA Ops:
  0.6 15.1 %collective-permute-start = (f32[256,1152]{1,0:T(8,128)}, f32[256,1152]{1,0:T(8,128)S(1)}, u32[]{:S(2)}, u32[]{:S(2)}) collective-permute-start(f32[256,1152]{1,0:T(8,128)} %source.3), channel_id=1, source_target_pairs={{0,1},{1,0},{2,3},{3,2},{4,5},{5,4},{6,7},{7,6},{8,9},{9,8},{10,11... | collective-permute-start | bytes 3538952 | tf_op jit(solution)/shard_map/ppermute | solution.py:180
  2.3 8.5 %collective-permute-start.2 = (bf16[32,1152]{1,0:T(8,128)(2,1)S(1)}, bf16[32,1152]{1,0:T(8,128)(2,1)S(1)}, u32[]{:S(2)}, u32[]{:S(2)}) collective-permute-start(bf16[32,1152]{1,0:T(8,128)(2,1)S(1)} %get-tuple-element.27), channel_id=1, source_target_pairs={{0,4},{1,5},{2,6},{3,7},{4,0},{5,1},{6,2},{7,3},{8,12},{9,13},{10,... | collective-permute-start | bytes 221192 | tf_op jit(solution)/shard_map/ppermute | solution.py:180
  5.9 7.8 %collective-permute-start.3 = (bf16[32,1152]{1,0:T(8,128)(2,1)S(1)}, bf16[32,1152]{1,0:T(8,128)(2,1)S(1)}, u32[]{:S(2)}, u32[]{:S(2)}) collective-permute-start(bf16[32,1152]{1,0:T(8,128)(2,1)S(1)} %get-tuple-element.28), channel_id=1, source_target_pairs={{0,4},{1,5},{2,6},{3,7},{4,0},{5,1},{6,2},{7,3},{8,12},{9,13},{10,... | collective-permute-start | bytes 221192 | tf_op jit(solution)/shard_map/ppermute | solution.py:180
  6.0 12.1 %collective-permute-start.4 = (bf16[64,1152]{1,0:T(8,128)(2,1)S(1)}, bf16[64,1152]{1,0:T(8,128)(2,1)S(1)}, u32[]{:S(2)}, u32[]{:S(2)}) collective-permute-start(bf16[64,1152]{1,0:T(8,128)(2,1)S(1)} %get-tuple-element.26.refs_0_), channel_id=1, source_target_pairs={{0,2},{1,3},{2,0},{3,1},{4,6},{5,7},{6,4},{7,5},{8,10},{9,11},{10,... | collective-permute-start | bytes 442376 | tf_op jit(solution)/shard_map/ppermute | solution.py:180
  10.7 6.5 %collective-permute-start.5 = (bf16[32,1152]{1,0:T(8,128)(2,1)S(1)}, bf16[32,1152]{1,0:T(8,128)(2,1)S(1)}, u32[]{:S(2)}, u32[]{:S(2)}) collective-permute-start(bf16[32,1152]{1,0:T(8,128)(2,1)S(1)} %collective-permute-done.2.refs_1_), channel_id=1, source_target_pairs={{0,2},{1,3},{2,0},{3,1},{4,6},{5,7},{6,4},{7,5},{8,10},{9,11},{10,... | collective-permute-start | bytes 221192 | tf_op jit(solution)/shard_map/ppermute | solution.py:180
  13.7 4.4 %collective-permute-start.6 = (bf16[32,1152]{1,0:T(8,128)(2,1)S(1)}, bf16[32,1152]{1,0:T(8,128)(2,1)S(1)}, u32[]{:S(2)}, u32[]{:S(2)}) collective-permute-start(bf16[32,1152]{1,0:T(8,128)(2,1)S(1)} %collective-permute-done.3.refs_2_), channel_id=1, source_target_pairs={{0,2},{1,3},{2,0},{3,1},{4,6},{5,7},{6,4},{7,5},{8,10},{9,11},{10,... | collective-permute-start | bytes 221192 | tf_op jit(solution)/shard_map/ppermute | solution.py:180
  14.4 2.8 %collective-permute-start.1 = (s32[1,256]{1,0:T(1,128)}, s32[1,256]{1,0:T(1,128)S(1)}, u32[]{:S(2)}, u32[]{:S(2)}) collective-permute-start(s32[1,256]{1,0:T(1,128)} %bitcast.3), channel_id=1, source_target_pairs={{0,1},{1,0},{2,3},{3,2},{4,5},{5,4},{6,7},{7,6},{8,9},{9,8},{10,11... | collective-permute-start | bytes 3080 | tf_op jit(solution)/shard_map/ppermute | solution.py:180
  17.2 2.0 %copy-start = (s32[256]{0:T(256)S(1)}, s32[256]{0:T(256)}, u32[]{:S(2)}) copy-start(s32[256]{0:T(256)} %param.7) | copy-start | bytes 3076
  19.1 2.6 %collective-permute-start.7 = (bf16[256,1152]{1,0:T(8,128)(2,1)S(1)}, bf16[256,1152]{1,0:T(8,128)(2,1)S(1)}, u32[]{:S(2)}, u32[]{:S(2)}) collective-permute-start(bf16[256,1152]{1,0:T(8,128)(2,1)S(1)} %get-tuple-element.34), channel_id=1, source_target_pairs={{0,1},{1,0},{2,3},{3,2},{4,5},{5,4},{6,7},{7,6},{8,9},{9,8},{10,11... | collective-permute-start | bytes 1769480 | tf_op jit(solution)/shard_map/ppermute | solution.py:180
  20.6 6.3 %collective-permute-start.15 = (bf16[64,1152]{1,0:T(8,128)(2,1)S(1)}, bf16[64,1152]{1,0:T(8,128)(2,1)S(1)}, u32[]{:S(2)}, u32[]{:S(2)}) collective-permute-start(bf16[64,1152]{1,0:T(8,128)(2,1)S(1)} %get-tuple-element.41), channel_id=1, source_target_pairs={{0,2},{1,3},{2,0},{3,1},{4,6},{5,7},{6,4},{7,5},{8,10},{9,11},{10,... | collective-permute-start | bytes 442376 | tf_op jit(solution)/shard_map/ppermute | solution.py:180
  21.8 7.9 %collective-permute-start.8 = (bf16[64,1152]{1,0:T(8,128)(2,1)S(1)}, bf16[64,1152]{1,0:T(8,128)(2,1)S(1)}, u32[]{:S(2)}, u32[]{:S(2)}) collective-permute-start(bf16[64,1152]{1,0:T(8,128)(2,1)S(1)} %get-tuple-element.36), channel_id=1, source_target_pairs={{0,8},{1,17},{2,10},{3,19},{4,12},{5,21},{6,14},{7,23},{8,0},{9,25... | collective-permute-start | bytes 442376 | tf_op jit(solution)/shard_map/ppermute | solution.py:190
  23.4 6.3 %collective-permute-start.9 = (bf16[64,1152]{1,0:T(8,128)(2,1)S(1)}, bf16[64,1152]{1,0:T(8,128)(2,1)S(1)}, u32[]{:S(2)}, u32[]{:S(2)}) collective-permute-start(bf16[64,1152]{1,0:T(8,128)(2,1)S(1)} %get-tuple-element.37), channel_id=1, source_target_pairs={{0,16},{1,9},{2,18},{3,11},{4,20},{5,13},{6,22},{7,15},{8,24},{9,1... | collective-permute-start | bytes 442376 | tf_op jit(solution)/shard_map/ppermute | solution.py:190
  24.9 6.9 %collective-permute-start.10 = (bf16[64,1152]{1,0:T(8,128)(2,1)S(1)}, bf16[64,1152]{1,0:T(8,128)(2,1)S(1)}, u32[]{:S(2)}, u32[]{:S(2)}) collective-permute-start(bf16[64,1152]{1,0:T(8,128)(2,1)S(1)} %get-tuple-element.38), channel_id=1, source_target_pairs={{0,24},{1,25},{2,26},{3,27},{4,28},{5,29},{6,30},{7,31},{8,16},{9,... | collective-permute-start | bytes 442376 | tf_op jit(solution)/shard_map/ppermute | solution.py:190
  25.3 10.3 %collective-permute-start.14 = (bf16[64,1152]{1,0:T(8,128)(2,1)S(1)}, bf16[64,1152]{1,0:T(8,128)(2,1)S(1)}, u32[]{:S(2)}, u32[]{:S(2)}) collective-permute-start(bf16[64,1152]{1,0:T(8,128)(2,1)S(1)} %get-tuple-element.39), channel_id=1, source_target_pairs={{0,2},{1,3},{2,0},{3,1},{4,6},{5,7},{6,4},{7,5},{8,10},{9,11},{10,... | collective-permute-start | bytes 442376 | tf_op jit(solution)/shard_map/ppermute | solution.py:180
  26.9 9.6 %collective-permute-start.16 = (bf16[64,1152]{1,0:T(8,128)(2,1)S(1)}, bf16[64,1152]{1,0:T(8,128)(2,1)S(1)}, u32[]{:S(2)}, u32[]{:S(2)}) collective-permute-start(bf16[64,1152]{1,0:T(8,128)(2,1)S(1)} %shard_map.74), channel_id=1, source_target_pairs={{0,4},{1,5},{2,6},{3,7},{4,0},{5,1},{6,2},{7,3},{8,12},{9,13},{10,... | collective-permute-start | bytes 442376 | tf_op jit(solution)/shard_map/ppermute | solution.py:180
  32.0 7.0 %collective-permute-start.13 = (bf16[64,1152]{1,0:T(8,128)(2,1)S(1)}, bf16[64,1152]{1,0:T(8,128)(2,1)S(1)}, u32[]{:S(2)}, u32[]{:S(2)}) collective-permute-start(bf16[64,1152]{1,0:T(8,128)(2,1)S(1)} %shard_map.73.refs_0_), channel_id=1, source_target_pairs={{0,24},{8,16},{16,8},{24,0},{1,25},{9,17},{17,9},{25,1},{2,26},{10... | collective-permute-start | bytes 442376 | tf_op jit(solution)/shard_map/ppermute | solution.py:180
  34.3 7.4 %collective-permute-start.12 = (bf16[64,1152]{1,0:T(8,128)(2,1)S(1)}, bf16[64,1152]{1,0:T(8,128)(2,1)S(1)}, u32[]{:S(2)}, u32[]{:S(2)}) collective-permute-start(bf16[64,1152]{1,0:T(8,128)(2,1)S(1)} %shard_map.73.refs_0_), channel_id=1, source_target_pairs={{0,16},{8,24},{16,0},{24,8},{1,17},{9,25},{17,1},{25,9},{2,18},{10... | collective-permute-start | bytes 442376 | tf_op jit(solution)/shard_map/ppermute | solution.py:180
  35.0 6.9 %collective-permute-start.11 = (bf16[64,1152]{1,0:T(8,128)(2,1)S(1)}, bf16[64,1152]{1,0:T(8,128)(2,1)S(1)}, u32[]{:S(2)}, u32[]{:S(2)}) collective-permute-start(bf16[64,1152]{1,0:T(8,128)(2,1)S(1)} %shard_map.73.refs_0_), channel_id=1, source_target_pairs={{0,8},{8,0},{16,24},{24,16},{1,9},{9,1},{17,25},{25,17},{2,10},{10... | collective-permute-start | bytes 442376 | tf_op jit(solution)/shard_map/ppermute | solution.py:180

commit v11 on v9

--- a/solution.py
+++ b/solution.py
@@ -208,7 +208,9 @@
     half = blocks // 2
     order = list(range(0, blocks, 2)) + list(range(1, blocks, 2))
     far = [swapped(piece, "txt", 4 * k) for k in range(1, half) for piece in (head, tail)]
-    near = [swapped(tile, "txt", 2) for tile in [txt_bf] + far]
+    near = [swapped(txt_bf, "txt", 2)]
+    for k in range(1, half):
+        near += [swapped(far[2 * k - 2], "txt", 2), swapped(tail, "txt", 4 * k + 2)]
     tiles = [txt_bf] + far + near
     img_bf, img_other, img_unit, img_inv = call(
         unit_img_body,

time: 42.4 us -> 42.4 us (level)
  starting transfers between devices: 20.9 us -> 20.4 us
  waiting for transfers between devices: 12.6 us -> 13.1 us
    ppermute x17, waiting for transfers between devices: 12.6 us -> 13.1 us  [swapped(): return lax.ppermute(value, axis, [(s, s ^ step) for s in range(count)])]
    ppermute x17, starting transfers between devices: 20.9 us -> 20.4 us  [swapped(): return lax.ppermute(value, axis, [(s, s ^ step) for s in range(count)])]
  transfers between devices with their start and end apart: 17 -> 17, of which waited for: 8 -> 9; matrix products, arithmetic and copies ran while one was open for 0% -> 0% of each run, Pallas kernels for 10% -> 10%
where the time goes in v11:
time: 42.4 us; the launch traced here: 42.2 us
  starting transfers between devices  20.4 us (48%)
  waiting for transfers between devices  13.1 us (31%)
  Pallas kernels  6.65 us (16%)
  between operations  2.02 us (5%)
    ppermute x17, starting transfers between devices, swapped(): return lax.ppermute(value, axis, [(s, s ^ step) for s in range(count)])  20.4 us
    ppermute x17, waiting for transfers between devices, swapped(): return lax.ppermute(value, axis, [(s, s ^ step) for s in range(count)])  13.1 us
    pallas_call x7, Pallas kernels, call(): pl.pallas_call(body, out_shape=outs, in_specs=specs, out_specs=[VMEM] * l...  5.38 us
    pallas_call x1, Pallas kernels, local(): pl.pallas_call(functools.partial(last_body, count), out_shape=[struct(row...  1.28 us
  transfers between devices with their start and end apart: 17, of which 9 were waited for; matrix products, arithmetic and copies ran while one was open for 0% of the time, Pallas kernels for 10%

profile of v11, /device:TPU:0, one launch (start us, length us, event | category | flops | bytes accessed | tf_op | source)
XLA Modules:
  0.0 42.2 jit_solution(14851228913986991565)
XLA Ops:
  0.6 0.5 %collective-permute-start = (f32[256,1152]{1,0:T(8,128)}, f32[256,1152]{1,0:T(8,128)S(1)}, u32[]{:S(2)}, u32[]{:S(2)}) collective-permute-start(f32[256,1152]{1,0:T(8,128)} %source.3), channel_id=1, source_target_pairs={{0,1},{1,0},{2,3},{3,2},{4,5},{5,4},{6,7},{7,6},{8,9},{9,8},{10,11... | collective-permute-start | bytes 3538952 | tf_op jit(solution)/shard_map/ppermute | solution.py:181
  1.1 1.1 %shard_map.68 = (bf16[64,1152]{1,0:T(8,128)(2,1)S(1)}, bf16[32,1152]{1,0:T(8,128)(2,1)S(1)}, bf16[32,1152]{1,0:T(8,128)(2,1)S(1)}, f32[64,1152]{1,0:T(8,128)S(1)}, f32[64,128]{1,0:T(8,128)S(1)}) custom-call(f32[64,1152]{1,0:T(8,128)} %source.2), custom_call_target="tpu_custom_call" | custom-call | flops 294912 | bytes 917504 | tf_op jit(solution)/shard_map/pallas_call | solution.py:25
  2.3 3.7 %collective-permute-start.2 = (bf16[32,1152]{1,0:T(8,128)(2,1)S(1)}, bf16[32,1152]{1,0:T(8,128)(2,1)S(1)}, u32[]{:S(2)}, u32[]{:S(2)}) collective-permute-start(bf16[32,1152]{1,0:T(8,128)(2,1)S(1)} %get-tuple-element.27), channel_id=1, source_target_pairs={{0,4},{1,5},{2,6},{3,7},{4,0},{5,1},{6,2},{7,3},{8,12},{9,13},{10,... | collective-permute-start | bytes 221192 | tf_op jit(solution)/shard_map/ppermute | solution.py:181
  5.9 1.6 %collective-permute-start.4 = (bf16[64,1152]{1,0:T(8,128)(2,1)S(1)}, bf16[64,1152]{1,0:T(8,128)(2,1)S(1)}, u32[]{:S(2)}, u32[]{:S(2)}) collective-permute-start(bf16[64,1152]{1,0:T(8,128)(2,1)S(1)} %get-tuple-element.26.refs_0_), channel_id=1, source_target_pairs={{0,2},{1,3},{2,0},{3,1},{4,6},{5,7},{6,4},{7,5},{8,10},{9,11},{10,... | collective-permute-start | bytes 442376 | tf_op jit(solution)/shard_map/ppermute | solution.py:181
  7.5 0.0 collective-permute-start.6
  7.5 1.9 %collective-permute-start.3 = (bf16[32,1152]{1,0:T(8,128)(2,1)S(1)}, bf16[32,1152]{1,0:T(8,128)(2,1)S(1)}, u32[]{:S(2)}, u32[]{:S(2)}) collective-permute-start(bf16[32,1152]{1,0:T(8,128)(2,1)S(1)} %get-tuple-element.28), channel_id=1, source_target_pairs={{0,4},{1,5},{2,6},{3,7},{4,0},{5,1},{6,2},{7,3},{8,12},{9,13},{10,... | collective-permute-start | bytes 221192 | tf_op jit(solution)/shard_map/ppermute | solution.py:181
  9.4 1.2 %collective-permute-done.2.refs_1_ = bf16[32,1152]{1,0:T(8,128)(2,1)S(1)} collective-permute-done((bf16[32,1152]{1,0:T(8,128)(2,1)S(1)}, bf16[32,1152]{1,0:T(8,128)(2,1)S(1)}, u32[]{:S(2)}, u32[]{:S(2)}) %collective-permute-start.2) | collective-permute-done | bytes 73760 | tf_op jit(solution)/shard_map/ppermute | solution.py:181
  10.6 1.3 %collective-permute-start.5 = (bf16[32,1152]{1,0:T(8,128)(2,1)S(1)}, bf16[32,1152]{1,0:T(8,128)(2,1)S(1)}, u32[]{:S(2)}, u32[]{:S(2)}) collective-permute-start(bf16[32,1152]{1,0:T(8,128)(2,1)S(1)} %collective-permute-done.2.refs_1_), channel_id=1, source_target_pairs={{0,2},{1,3},{2,0},{3,1},{4,6},{5,7},{6,4},{7,5},{8,10},{9,11},{10,... | collective-permute-start | bytes 221192 | tf_op jit(solution)/shard_map/ppermute | solution.py:181
  11.9 0.0 collective-permute-done.other
  11.9 0.0 collective-permute-start.1
  13.2 1.5 %shard_map.69 = (bf16[256,1152]{1,0:T(8,128)(2,1)S(1)}, bf16[256,1152]{1,0:T(8,128)(2,1)S(1)}, f32[64,1152]{1,0:T(8,128)S(1)}, f32[64,128]{1,0:T(8,128)S(1)}) custom-call(s32[1]{0:T(128)} %bitcast.place.position, f32[256,1152]{1,0:T(8,128)S(1)} %collective-permute-done.other, f32[256,1152]{1,0:T(8,128)} %source.3), custom_call_target="tpu_custom_call" | custom-call | flops 2359296 | bytes 3866628 | tf_op jit(solution)/shard_map/pallas_call | solution.py:25
  14.7 0.0 copy-start
  14.7 0.0 collective-permute-done.1.perm
  14.7 0.5 %collective-permute-done.6.refs_5_ = bf16[32,1152]{1,0:T(8,128)(2,1)S(1)} collective-permute-done((bf16[32,1152]{1,0:T(8,128)(2,1)S(1)}, bf16[32,1152]{1,0:T(8,128)(2,1)S(1)}, u32[]{:S(2)}, u32[]{:S(2)}) %collective-permute-start.6) | collective-permute-done | bytes 73760 | tf_op jit(solution)/shard_map/ppermute | solution.py:181
  15.2 1.7 %collective-permute-done.3.refs_2_ = bf16[32,1152]{1,0:T(8,128)(2,1)S(1)} collective-permute-done((bf16[32,1152]{1,0:T(8,128)(2,1)S(1)}, bf16[32,1152]{1,0:T(8,128)(2,1)S(1)}, u32[]{:S(2)}, u32[]{:S(2)}) %collective-permute-start.3) | collective-permute-done | bytes 73760 | tf_op jit(solution)/shard_map/ppermute | solution.py:181
  16.9 0.2 collective-permute-done.5.refs_4_
  17.0 0.0 collective-permute-done.4.refs_3_
  17.1 1.0 %shard_map.70 = (bf16[256,256]{1,0:T(8,128)(2,1)S(1)}, bf16[256,1152]{1,0:T(8,128)(2,1)S(1)}) custom-call(s32[1]{0:T(128)} %bitcast.place.position, s32[1]{0:T(128)} %bitcast.1.column, f32[1]{0:T(128)S(6)} %copy.7.scale, f32[1]{0:T(128)S(6)} %copy.8.shift, s32[1,256]{1,0:T(1,128)S(1)} %collective-permute-done.1.perm, ...), custom_call_target="tpu_custom_call" | custom-call | flops 301989888 | bytes 1901584 | tf_op jit(solution)/shard_map/pallas_call | solution.py:25
  18.1 0.1 collective-permute-start.7
  18.2 0.0 copy-done
  18.2 1.4 %shard_map.71 = (f32[256,1152]{1,0:T(8,128)S(1)}, f32[64,1152]{1,0:T(8,128)S(1)}, f32[64,1152]{1,0:T(8,128)S(1)}, bf16[64,1152]{1,0:T(8,128)(2,1)S(1)}, bf16[64,1152]{1,0:T(8,128)(2,1)S(1)}) custom-call(s32[1]{0:T(128)} %bitcast.place.position, s32[1]{0:T(128)} %bitcast.1.column, f32[1]{0:T(128)S(6)} %copy.7.scale, f32[1]{0:T(128)S(6)} %copy.8.shift, ...), custom_call_target="tpu_custom_call" | custom-call | flops 603979776 | bytes 3965968 | tf_op jit(solution)/shard_map/pallas_call | solution.py:25
  19.6 1.6 %collective-permute-start.15 = (bf16[64,1152]{1,0:T(8,128)(2,1)S(1)}, bf16[64,1152]{1,0:T(8,128)(2,1)S(1)}, u32[]{:S(2)}, u32[]{:S(2)}) collective-permute-start(bf16[64,1152]{1,0:T(8,128)(2,1)S(1)} %get-tuple-element.41), channel_id=1, source_target_pairs={{0,2},{1,3},{2,0},{3,1},{4,6},{5,7},{6,4},{7,5},{8,10},{9,11},{10,... | collective-permute-start | bytes 442376 | tf_op jit(solution)/shard_map/ppermute | solution.py:181
  21.1 0.0 collective-permute-done.7.other
  21.1 0.2 shard_map.72
  21.3 1.6 %collective-permute-start.8 = (bf16[64,1152]{1,0:T(8,128)(2,1)S(1)}, bf16[64,1152]{1,0:T(8,128)(2,1)S(1)}, u32[]{:S(2)}, u32[]{:S(2)}) collective-permute-start(bf16[64,1152]{1,0:T(8,128)(2,1)S(1)} %get-tuple-element.36), channel_id=1, source_target_pairs={{0,8},{8,0},{16,24},{24,16},{1,9},{9,1},{17,25},{25,17},{2,10},{10... | collective-permute-start | bytes 442376 | tf_op jit(solution)/shard_map/ppermute | solution.py:181
  22.8 1.5 %collective-permute-start.9 = (bf16[64,1152]{1,0:T(8,128)(2,1)S(1)}, bf16[64,1152]{1,0:T(8,128)(2,1)S(1)}, u32[]{:S(2)}, u32[]{:S(2)}) collective-permute-start(bf16[64,1152]{1,0:T(8,128)(2,1)S(1)} %get-tuple-element.37), channel_id=1, source_target_pairs={{0,16},{8,24},{16,0},{24,8},{1,17},{9,25},{17,1},{25,9},{2,18},{10... | collective-permute-start | bytes 442376 | tf_op jit(solution)/shard_map/ppermute | solution.py:181
  24.4 0.5 %collective-permute-start.10 = (bf16[64,1152]{1,0:T(8,128)(2,1)S(1)}, bf16[64,1152]{1,0:T(8,128)(2,1)S(1)}, u32[]{:S(2)}, u32[]{:S(2)}) collective-permute-start(bf16[64,1152]{1,0:T(8,128)(2,1)S(1)} %get-tuple-element.38), channel_id=1, source_target_pairs={{0,24},{8,16},{16,8},{24,0},{1,25},{9,17},{17,9},{25,1},{2,26},{10... | collective-permute-start | bytes 442376 | tf_op jit(solution)/shard_map/ppermute | solution.py:181
  24.8 0.5 %collective-permute-start.14 = (bf16[64,1152]{1,0:T(8,128)(2,1)S(1)}, bf16[64,1152]{1,0:T(8,128)(2,1)S(1)}, u32[]{:S(2)}, u32[]{:S(2)}) collective-permute-start(bf16[64,1152]{1,0:T(8,128)(2,1)S(1)} %get-tuple-element.39), channel_id=1, source_target_pairs={{0,2},{1,3},{2,0},{3,1},{4,6},{5,7},{6,4},{7,5},{8,10},{9,11},{10,... | collective-permute-start | bytes 442376 | tf_op jit(solution)/shard_map/ppermute | solution.py:181
  25.4 0.5 %collective-permute-done.15.got = bf16[64,1152]{1,0:T(8,128)(2,1)S(1)} collective-permute-done((bf16[64,1152]{1,0:T(8,128)(2,1)S(1)}, bf16[64,1152]{1,0:T(8,128)(2,1)S(1)}, u32[]{:S(2)}, u32[]{:S(2)}) %collective-permute-start.15) | collective-permute-done | bytes 147488 | tf_op jit(solution)/shard_map/ppermute | solution.py:181
  25.9 2.2 %collective-permute-start.16 = (bf16[64,1152]{1,0:T(8,128)(2,1)S(1)}, bf16[64,1152]{1,0:T(8,128)(2,1)S(1)}, u32[]{:S(2)}, u32[]{:S(2)}) collective-permute-start(bf16[64,1152]{1,0:T(8,128)(2,1)S(1)} %shard_map.74), channel_id=1, source_target_pairs={{0,4},{1,5},{2,6},{3,7},{4,0},{5,1},{6,2},{7,3},{8,12},{9,13},{10,... | collective-permute-start | bytes 442376 | tf_op jit(solution)/shard_map/ppermute | solution.py:181
  28.1 0.0 collective-permute-done.8.refs_0_
  28.1 3.6 %collective-permute-done.9.refs_1_ = bf16[64,1152]{1,0:T(8,128)(2,1)S(1)} collective-permute-done((bf16[64,1152]{1,0:T(8,128)(2,1)S(1)}, bf16[64,1152]{1,0:T(8,128)(2,1)S(1)}, u32[]{:S(2)}, u32[]{:S(2)}) %collective-permute-start.9) | collective-permute-done | bytes 147488 | tf_op jit(solution)/shard_map/ppermute | solution.py:181
  31.7 0.0 collective-permute-done.10.refs_2_
  31.7 0.2 shard_map.73.refs_0_
  31.9 1.6 %collective-permute-start.13 = (bf16[64,1152]{1,0:T(8,128)(2,1)S(1)}, bf16[64,1152]{1,0:T(8,128)(2,1)S(1)}, u32[]{:S(2)}, u32[]{:S(2)}) collective-permute-start(bf16[64,1152]{1,0:T(8,128)(2,1)S(1)} %shard_map.73.refs_0_), channel_id=1, source_target_pairs={{0,24},{8,16},{16,8},{24,0},{1,25},{9,17},{17,9},{25,1},{2,26},{10... | collective-permute-start | bytes 442376 | tf_op jit(solution)/shard_map/ppermute | solution.py:181
  33.4 1.2 %collective-permute-start.12 = (bf16[64,1152]{1,0:T(8,128)(2,1)S(1)}, bf16[64,1152]{1,0:T(8,128)(2,1)S(1)}, u32[]{:S(2)}, u32[]{:S(2)}) collective-permute-start(bf16[64,1152]{1,0:T(8,128)(2,1)S(1)} %shard_map.73.refs_0_), channel_id=1, source_target_pairs={{0,16},{8,24},{16,0},{24,8},{1,17},{9,25},{17,1},{25,9},{2,18},{10... | collective-permute-start | bytes 442376 | tf_op jit(solution)/shard_map/ppermute | solution.py:181
  34.6 0.8 %collective-permute-start.11 = (bf16[64,1152]{1,0:T(8,128)(2,1)S(1)}, bf16[64,1152]{1,0:T(8,128)(2,1)S(1)}, u32[]{:S(2)}, u32[]{:S(2)}) collective-permute-start(bf16[64,1152]{1,0:T(8,128)(2,1)S(1)} %shard_map.73.refs_0_), channel_id=1, source_target_pairs={{0,8},{8,0},{16,24},{24,16},{1,9},{9,1},{17,25},{25,17},{2,10},{10... | collective-permute-start | bytes 442376 | tf_op jit(solution)/shard_map/ppermute | solution.py:181
  35.4 0.0 collective-permute-done.14.refs_4_
  35.4 0.1 collective-permute-done.16.refs_5_
  35.5 3.8 %collective-permute-done.13.refs_3_ = bf16[64,1152]{1,0:T(8,128)(2,1)S(1)} collective-permute-done((bf16[64,1152]{1,0:T(8,128)(2,1)S(1)}, bf16[64,1152]{1,0:T(8,128)(2,1)S(1)}, u32[]{:S(2)}, u32[]{:S(2)}) %collective-permute-start.13) | collective-permute-done | bytes 147488 | tf_op jit(solution)/shard_map/ppermute | solution.py:181
  39.4 1.6 %collective-permute-done.12.refs_2_ = bf16[64,1152]{1,0:T(8,128)(2,1)S(1)} collective-permute-done((bf16[64,1152]{1,0:T(8,128)(2,1)S(1)}, bf16[64,1152]{1,0:T(8,128)(2,1)S(1)}, u32[]{:S(2)}, u32[]{:S(2)}) %collective-permute-start.12) | collective-permute-done | bytes 147488 | tf_op jit(solution)/shard_map/ppermute | solution.py:181
  40.9 0.0 collective-permute-done.11.refs_1_
  40.9 1.3 %shard_map.75 = (f32[256,1152]{1,0:T(8,128)}, f32[64,1152]{1,0:T(8,128)}) custom-call(s32[1]{0:T(128)} %bitcast.place.position, f32[1]{0:T(128)S(6)} %copy.7.scale, f32[64,1152]{1,0:T(8,128)S(1)} %get-tuple-element.22.unit, f32[64,128]{1,0:T(8,128)S(1)} %get-tuple-element.23.inverse, f32[64,1152]{1,0:T(8,128)S(1)} %get-tuple-element.30.own, ...), custom_call_target="tpu_custom_call" | custom-call | flops 737280 | bytes 2359296 | tf_op jit(solution)/shard_map/pallas_call | solution.py:277
  (1 shorter events, 0.0 us)
Async XLA Ops:
  0.6 11.3 %collective-permute-start = (f32[256,1152]{1,0:T(8,128)}, f32[256,1152]{1,0:T(8,128)S(1)}, u32[]{:S(2)}, u32[]{:S(2)}) collective-permute-start(f32[256,1152]{1,0:T(8,128)} %source.3), channel_id=1, source_target_pairs={{0,1},{1,0},{2,3},{3,2},{4,5},{5,4},{6,7},{7,6},{8,9},{9,8},{10,11... | collective-permute-start | bytes 3538952 | tf_op jit(solution)/shard_map/ppermute | solution.py:181
  2.3 8.4 %collective-permute-start.2 = (bf16[32,1152]{1,0:T(8,128)(2,1)S(1)}, bf16[32,1152]{1,0:T(8,128)(2,1)S(1)}, u32[]{:S(2)}, u32[]{:S(2)}) collective-permute-start(bf16[32,1152]{1,0:T(8,128)(2,1)S(1)} %get-tuple-element.27), channel_id=1, source_target_pairs={{0,4},{1,5},{2,6},{3,7},{4,0},{5,1},{6,2},{7,3},{8,12},{9,13},{10,... | collective-permute-start | bytes 221192 | tf_op jit(solution)/shard_map/ppermute | solution.py:181
  5.9 11.1 %collective-permute-start.4 = (bf16[64,1152]{1,0:T(8,128)(2,1)S(1)}, bf16[64,1152]{1,0:T(8,128)(2,1)S(1)}, u32[]{:S(2)}, u32[]{:S(2)}) collective-permute-start(bf16[64,1152]{1,0:T(8,128)(2,1)S(1)} %get-tuple-element.26.refs_0_), channel_id=1, source_target_pairs={{0,2},{1,3},{2,0},{3,1},{4,6},{5,7},{6,4},{7,5},{8,10},{9,11},{10,... | collective-permute-start | bytes 442376 | tf_op jit(solution)/shard_map/ppermute | solution.py:181
  7.5 7.7 %collective-permute-start.6 = (bf16[32,1152]{1,0:T(8,128)(2,1)S(1)}, bf16[32,1152]{1,0:T(8,128)(2,1)S(1)}, u32[]{:S(2)}, u32[]{:S(2)}) collective-permute-start(bf16[32,1152]{1,0:T(8,128)(2,1)S(1)} %get-tuple-element.28), channel_id=1, source_target_pairs={{0,6},{1,7},{2,4},{3,5},{4,2},{5,3},{6,0},{7,1},{8,14},{9,15},{10,... | collective-permute-start | bytes 221192 | tf_op jit(solution)/shard_map/ppermute | solution.py:181
  7.5 9.4 %collective-permute-start.3 = (bf16[32,1152]{1,0:T(8,128)(2,1)S(1)}, bf16[32,1152]{1,0:T(8,128)(2,1)S(1)}, u32[]{:S(2)}, u32[]{:S(2)}) collective-permute-start(bf16[32,1152]{1,0:T(8,128)(2,1)S(1)} %get-tuple-element.28), channel_id=1, source_target_pairs={{0,4},{1,5},{2,6},{3,7},{4,0},{5,1},{6,2},{7,3},{8,12},{9,13},{10,... | collective-permute-start | bytes 221192 | tf_op jit(solution)/shard_map/ppermute | solution.py:181
  10.6 6.4 %collective-permute-start.5 = (bf16[32,1152]{1,0:T(8,128)(2,1)S(1)}, bf16[32,1152]{1,0:T(8,128)(2,1)S(1)}, u32[]{:S(2)}, u32[]{:S(2)}) collective-permute-start(bf16[32,1152]{1,0:T(8,128)(2,1)S(1)} %collective-permute-done.2.refs_1_), channel_id=1, source_target_pairs={{0,2},{1,3},{2,0},{3,1},{4,6},{5,7},{6,4},{7,5},{8,10},{9,11},{10,... | collective-permute-start | bytes 221192 | tf_op jit(solution)/shard_map/ppermute | solution.py:181
  11.9 2.8 %collective-permute-start.1 = (s32[1,256]{1,0:T(1,128)}, s32[1,256]{1,0:T(1,128)S(1)}, u32[]{:S(2)}, u32[]{:S(2)}) collective-permute-start(s32[1,256]{1,0:T(1,128)} %bitcast.3), channel_id=1, source_target_pairs={{0,1},{1,0},{2,3},{3,2},{4,5},{5,4},{6,7},{7,6},{8,9},{9,8},{10,11... | collective-permute-start | bytes 3080 | tf_op jit(solution)/shard_map/ppermute | solution.py:181
  14.7 3.5 %copy-start = (s32[256]{0:T(256)S(1)}, s32[256]{0:T(256)}, u32[]{:S(2)}) copy-start(s32[256]{0:T(256)} %param.7) | copy-start | bytes 3076
  18.1 3.0 %collective-permute-start.7 = (bf16[256,1152]{1,0:T(8,128)(2,1)S(1)}, bf16[256,1152]{1,0:T(8,128)(2,1)S(1)}, u32[]{:S(2)}, u32[]{:S(2)}) collective-permute-start(bf16[256,1152]{1,0:T(8,128)(2,1)S(1)} %get-tuple-element.34), channel_id=1, source_target_pairs={{0,1},{1,0},{2,3},{3,2},{4,5},{5,4},{6,7},{7,6},{8,9},{9,8},{10,11... | collective-permute-start | bytes 1769480 | tf_op jit(solution)/shard_map/ppermute | solution.py:181
  19.6 6.3 %collective-permute-start.15 = (bf16[64,1152]{1,0:T(8,128)(2,1)S(1)}, bf16[64,1152]{1,0:T(8,128)(2,1)S(1)}, u32[]{:S(2)}, u32[]{:S(2)}) collective-permute-start(bf16[64,1152]{1,0:T(8,128)(2,1)S(1)} %get-tuple-element.41), channel_id=1, source_target_pairs={{0,2},{1,3},{2,0},{3,1},{4,6},{5,7},{6,4},{7,5},{8,10},{9,11},{10,... | collective-permute-start | bytes 442376 | tf_op jit(solution)/shard_map/ppermute | solution.py:181
  21.3 6.8 %collective-permute-start.8 = (bf16[64,1152]{1,0:T(8,128)(2,1)S(1)}, bf16[64,1152]{1,0:T(8,128)(2,1)S(1)}, u32[]{:S(2)}, u32[]{:S(2)}) collective-permute-start(bf16[64,1152]{1,0:T(8,128)(2,1)S(1)} %get-tuple-element.36), channel_id=1, source_target_pairs={{0,8},{8,0},{16,24},{24,16},{1,9},{9,1},{17,25},{25,17},{2,10},{10... | collective-permute-start | bytes 442376 | tf_op jit(solution)/shard_map/ppermute | solution.py:181
  22.8 8.8 %collective-permute-start.9 = (bf16[64,1152]{1,0:T(8,128)(2,1)S(1)}, bf16[64,1152]{1,0:T(8,128)(2,1)S(1)}, u32[]{:S(2)}, u32[]{:S(2)}) collective-permute-start(bf16[64,1152]{1,0:T(8,128)(2,1)S(1)} %get-tuple-element.37), channel_id=1, source_target_pairs={{0,16},{8,24},{16,0},{24,8},{1,17},{9,25},{17,1},{25,9},{2,18},{10... | collective-permute-start | bytes 442376 | tf_op jit(solution)/shard_map/ppermute | solution.py:181
  24.4 7.3 %collective-permute-start.10 = (bf16[64,1152]{1,0:T(8,128)(2,1)S(1)}, bf16[64,1152]{1,0:T(8,128)(2,1)S(1)}, u32[]{:S(2)}, u32[]{:S(2)}) collective-permute-start(bf16[64,1152]{1,0:T(8,128)(2,1)S(1)} %get-tuple-element.38), channel_id=1, source_target_pairs={{0,24},{8,16},{16,8},{24,0},{1,25},{9,17},{17,9},{25,1},{2,26},{10... | collective-permute-start | bytes 442376 | tf_op jit(solution)/shard_map/ppermute | solution.py:181
  24.8 10.6 %collective-permute-start.14 = (bf16[64,1152]{1,0:T(8,128)(2,1)S(1)}, bf16[64,1152]{1,0:T(8,128)(2,1)S(1)}, u32[]{:S(2)}, u32[]{:S(2)}) collective-permute-start(bf16[64,1152]{1,0:T(8,128)(2,1)S(1)} %get-tuple-element.39), channel_id=1, source_target_pairs={{0,2},{1,3},{2,0},{3,1},{4,6},{5,7},{6,4},{7,5},{8,10},{9,11},{10,... | collective-permute-start | bytes 442376 | tf_op jit(solution)/shard_map/ppermute | solution.py:181
  25.9 9.6 %collective-permute-start.16 = (bf16[64,1152]{1,0:T(8,128)(2,1)S(1)}, bf16[64,1152]{1,0:T(8,128)(2,1)S(1)}, u32[]{:S(2)}, u32[]{:S(2)}) collective-permute-start(bf16[64,1152]{1,0:T(8,128)(2,1)S(1)} %shard_map.74), channel_id=1, source_target_pairs={{0,4},{1,5},{2,6},{3,7},{4,0},{5,1},{6,2},{7,3},{8,12},{9,13},{10,... | collective-permute-start | bytes 442376 | tf_op jit(solution)/shard_map/ppermute | solution.py:181
  31.9 7.5 %collective-permute-start.13 = (bf16[64,1152]{1,0:T(8,128)(2,1)S(1)}, bf16[64,1152]{1,0:T(8,128)(2,1)S(1)}, u32[]{:S(2)}, u32[]{:S(2)}) collective-permute-start(bf16[64,1152]{1,0:T(8,128)(2,1)S(1)} %shard_map.73.refs_0_), channel_id=1, source_target_pairs={{0,24},{8,16},{16,8},{24,0},{1,25},{9,17},{17,9},{25,1},{2,26},{10... | collective-permute-start | bytes 442376 | tf_op jit(solution)/shard_map/ppermute | solution.py:181
  33.4 7.5 %collective-permute-start.12 = (bf16[64,1152]{1,0:T(8,128)(2,1)S(1)}, bf16[64,1152]{1,0:T(8,128)(2,1)S(1)}, u32[]{:S(2)}, u32[]{:S(2)}) collective-permute-start(bf16[64,1152]{1,0:T(8,128)(2,1)S(1)} %shard_map.73.refs_0_), channel_id=1, source_target_pairs={{0,16},{8,24},{16,0},{24,8},{1,17},{9,25},{17,1},{25,9},{2,18},{10... | collective-permute-start | bytes 442376 | tf_op jit(solution)/shard_map/ppermute | solution.py:181
  34.6 6.3 %collective-permute-start.11 = (bf16[64,1152]{1,0:T(8,128)(2,1)S(1)}, bf16[64,1152]{1,0:T(8,128)(2,1)S(1)}, u32[]{:S(2)}, u32[]{:S(2)}) collective-permute-start(bf16[64,1152]{1,0:T(8,128)(2,1)S(1)} %shard_map.73.refs_0_), channel_id=1, source_target_pairs={{0,8},{8,0},{16,24},{24,16},{1,9},{9,1},{17,25},{25,17},{2,10},{10... | collective-permute-start | bytes 442376 | tf_op jit(solution)/shard_map/ppermute | solution.py:181

commit v12 on v11

--- a/solution.py
+++ b/solution.py
@@ -103,30 +103,21 @@
 
 
 def own_body(order, line, place, column, scale, shift, perm, img, img_other, kept, *refs):
-    *txt, own_sum, own_txt, even_txt, near_txt, odd_txt = refs
-    rows = own_txt.shape[0]
+    *txt, own_sum, txt_sums = refs
     tile = joined(txt)
     weights = weights_of(tile, order, line, place, column, scale, shift, perm[...], img[...])
     own_sum[...] = to_images(weights, tile)
-    to_txt = to_texts(weights, img[...]) + to_texts(kept[...], img_other[...])
-    half = rows + even_txt.shape[0]
-    own_txt[...] = to_txt[:rows]
-    even_txt[...] = to_txt[rows:half]
-    near_txt[...] = to_txt[half : half + rows].astype(BF16)
-    odd_txt[...] = to_txt[half + rows :].astype(BF16)
-
-
-def add_body(even, got, *outs):
-    rows = outs[0].shape[0]
-    for k, out in enumerate(outs):
-        mine = even[k * rows : (k + 1) * rows, :]
-        out[...] = (mine + got[k * rows : (k + 1) * rows, :].astype(F32)).astype(BF16)
-
-
-def split_body(count, position, own, other, keep, *send):
+    txt_sums[...] = to_texts(weights, img[...]) + to_texts(kept[...], img_other[...])
+
+
+def split_body(count, blocks, place, own, other, txt_sums, *refs):
+    txt_out, (keep, *send) = refs[:blocks], refs[blocks:]
+    rows = txt_out[0].shape[0]
+    for k, out in enumerate(txt_out):
+        out[...] = txt_sums[k * rows : (k + 1) * rows, :].astype(out.dtype)
     rows = keep.shape[0]
     for k in range(count):
-        start = pl.multiple_of((position[0] ^ k) * rows, rows)
+        start = pl.multiple_of((place[0] ^ k) * rows, rows)
         part = own[pl.ds(start, rows), :] + other[pl.ds(start, rows), :].astype(F32)
         if k == 0:
             keep[...] = part
@@ -232,39 +223,29 @@
         2 * pairs,
     )
     from_other = swapped(other_img, "txt", 1)
-    own_img, own_txt, even_txt, near_txt, odd_txt = call(
+    own_img, txt_sums = call(
         functools.partial(own_body, order, line),
-        [
-            struct(rows, width, F32),
-            struct(txt_rows, width, F32),
-            struct((half - 1) * txt_rows, width, F32),
-            struct(txt_rows, width, BF16),
-            struct((half - 1) * txt_rows, width, BF16),
-        ],
+        [struct(rows, width, F32), struct(blocks * txt_rows, width, F32)],
         [*scalars, perm_row, img_bf, img_other, kept, *tiles],
         [SMEM] * 4 + [VMEM] * (4 + len(tiles)),
         40 << 20,
         4 * pairs,
     )
-    sums = call(
-        add_body,
-        [struct(txt_rows, width, BF16)] * (half - 1),
-        [even_txt, swapped(odd_txt, "txt", 2)],
-        [VMEM] * 2,
+    outs = call(
+        functools.partial(split_body, count, blocks),
+        [struct(txt_rows, width, F32)]
+        + [struct(txt_rows, width, BF16)] * (blocks - 1)
+        + [struct(part, width, F32)]
+        + [struct(part, width, BF16)] * (count - 1),
+        [place, own_img, from_other, txt_sums],
+        [SMEM] + [VMEM] * 3,
         24 << 20,
         rows * width,
     )
-    back = [swapped(near_txt, "txt", 2)] + [swapped(sums[k - 1], "txt", 4 * k) for k in range(1, half)]
-
-    keep, *send = call(
-        functools.partial(split_body, count),
-        [struct(part, width, F32)] + [struct(part, width, BF16)] * (count - 1),
-        [place, own_img, from_other],
-        [SMEM, VMEM, VMEM],
-        24 << 20,
-        rows * width,
-    )
+    (own_txt, *send_txt), (keep, *send) = outs[:blocks], outs[blocks:]
     got = [swapped(send[k - 1], "img", k) for k in range(1, count)]
+    homes = sorted(zip(order[1:], send_txt), key=lambda pair: pair[0])
+    back = [swapped(block, "txt", 2 * k) for k, block in homes]
     (grad_part,) = call(
         finish_img_body,
         [struct(part, width, BF16)],
@@ -277,7 +258,7 @@
     return pl.pallas_call(
         functools.partial(last_body, count),
         out_shape=[struct(rows, width, F32), struct(txt_rows, width, F32)],
-        in_specs=[SMEM] * 2 + [VMEM] * (3 + count + half),
+        in_specs=[SMEM] * 2 + [VMEM] * (2 + count + blocks),
         out_specs=[ANY] * 2,
         scratch_shapes=[
             pltpu.VMEM((rows, width), F32),

time: 42.4 us -> 41.5 us (0.979)
  waiting for transfers between devices: 13.1 us -> 10.1 us
  starting transfers between devices: 20.4 us -> 22.5 us
    ppermute x17, waiting for transfers between devices: 13.1 us -> 10.1 us  [swapped(): return lax.ppermute(value, axis, [(s, s ^ step) for s in range(count)])]
    ppermute x17, starting transfers between devices: 20.4 us -> 22.5 us  [swapped(): return lax.ppermute(value, axis, [(s, s ^ step) for s in range(count)])]
    pallas_call x7 -> x6, Pallas kernels: 5.38 us -> 5.38 us  [call(): pl.pallas_call(body, out_shape=outs, in_specs=specs, out_specs=[VMEM] * l...]
  transfers between devices with their start and end apart: 17 -> 17, of which waited for: 9 -> 8; matrix products, arithmetic and copies ran while one was open for 0% -> 0% of each run, Pallas kernels for 10% -> 10%
where the time goes in v12:
time: 41.5 us; the launch traced here: 41.3 us
  starting transfers between devices  22.5 us (54%)
  waiting for transfers between devices  10.1 us (24%)
  Pallas kernels  6.65 us (16%)
  between operations  2.01 us (5%)
    ppermute x17, starting transfers between devices, swapped(): return lax.ppermute(value, axis, [(s, s ^ step) for s in range(count)])  22.5 us
    ppermute x17, waiting for transfers between devices, swapped(): return lax.ppermute(value, axis, [(s, s ^ step) for s in range(count)])  10.1 us
    pallas_call x6, Pallas kernels, call(): pl.pallas_call(body, out_shape=outs, in_specs=specs, out_specs=[VMEM] * l...  5.38 us
    pallas_call x1, Pallas kernels, local(): pl.pallas_call(functools.partial(last_body, count), out_shape=[struct(row...  1.27 us
  transfers between devices with their start and end apart: 17, of which 8 were waited for; matrix products, arithmetic and copies ran while one was open for 0% of the time, Pallas kernels for 10%

profile of v12, /device:TPU:0, one launch (start us, length us, event | category | flops | bytes accessed | tf_op | source)
XLA Modules:
  0.0 41.3 jit_solution(11484511530581399502)
XLA Ops:
  0.6 0.5 %collective-permute-start = (f32[256,1152]{1,0:T(8,128)}, f32[256,1152]{1,0:T(8,128)S(1)}, u32[]{:S(2)}, u32[]{:S(2)}) collective-permute-start(f32[256,1152]{1,0:T(8,128)} %source.3), channel_id=1, source_target_pairs={{0,1},{1,0},{2,3},{3,2},{4,5},{5,4},{6,7},{7,6},{8,9},{9,8},{10,11... | collective-permute-start | bytes 3538952 | tf_op jit(solution)/shard_map/ppermute | solution.py:172
  1.1 1.1 %shard_map.68 = (bf16[64,1152]{1,0:T(8,128)(2,1)S(1)}, bf16[32,1152]{1,0:T(8,128)(2,1)S(1)}, bf16[32,1152]{1,0:T(8,128)(2,1)S(1)}, f32[64,1152]{1,0:T(8,128)S(1)}, f32[64,128]{1,0:T(8,128)S(1)}) custom-call(f32[64,1152]{1,0:T(8,128)} %source.2), custom_call_target="tpu_custom_call" | custom-call | flops 294912 | bytes 917504 | tf_op jit(solution)/shard_map/pallas_call | solution.py:25
  2.3 3.7 %collective-permute-start.2 = (bf16[32,1152]{1,0:T(8,128)(2,1)S(1)}, bf16[32,1152]{1,0:T(8,128)(2,1)S(1)}, u32[]{:S(2)}, u32[]{:S(2)}) collective-permute-start(bf16[32,1152]{1,0:T(8,128)(2,1)S(1)} %get-tuple-element.28), channel_id=1, source_target_pairs={{0,4},{1,5},{2,6},{3,7},{4,0},{5,1},{6,2},{7,3},{8,12},{9,13},{10,... | collective-permute-start | bytes 221192 | tf_op jit(solution)/shard_map/ppermute | solution.py:172
  5.9 1.6 %collective-permute-start.4 = (bf16[64,1152]{1,0:T(8,128)(2,1)S(1)}, bf16[64,1152]{1,0:T(8,128)(2,1)S(1)}, u32[]{:S(2)}, u32[]{:S(2)}) collective-permute-start(bf16[64,1152]{1,0:T(8,128)(2,1)S(1)} %get-tuple-element.27.refs_0_), channel_id=1, source_target_pairs={{0,2},{1,3},{2,0},{3,1},{4,6},{5,7},{6,4},{7,5},{8,10},{9,11},{10,... | collective-permute-start | bytes 442376 | tf_op jit(solution)/shard_map/ppermute | solution.py:172
  7.5 0.0 collective-permute-start.6
  7.5 1.9 %collective-permute-start.3 = (bf16[32,1152]{1,0:T(8,128)(2,1)S(1)}, bf16[32,1152]{1,0:T(8,128)(2,1)S(1)}, u32[]{:S(2)}, u32[]{:S(2)}) collective-permute-start(bf16[32,1152]{1,0:T(8,128)(2,1)S(1)} %get-tuple-element.29), channel_id=1, source_target_pairs={{0,4},{1,5},{2,6},{3,7},{4,0},{5,1},{6,2},{7,3},{8,12},{9,13},{10,... | collective-permute-start | bytes 221192 | tf_op jit(solution)/shard_map/ppermute | solution.py:172
  9.4 1.2 %collective-permute-done.2.refs_1_ = bf16[32,1152]{1,0:T(8,128)(2,1)S(1)} collective-permute-done((bf16[32,1152]{1,0:T(8,128)(2,1)S(1)}, bf16[32,1152]{1,0:T(8,128)(2,1)S(1)}, u32[]{:S(2)}, u32[]{:S(2)}) %collective-permute-start.2) | collective-permute-done | bytes 73760 | tf_op jit(solution)/shard_map/ppermute | solution.py:172
  10.6 1.3 %collective-permute-start.5 = (bf16[32,1152]{1,0:T(8,128)(2,1)S(1)}, bf16[32,1152]{1,0:T(8,128)(2,1)S(1)}, u32[]{:S(2)}, u32[]{:S(2)}) collective-permute-start(bf16[32,1152]{1,0:T(8,128)(2,1)S(1)} %collective-permute-done.2.refs_1_), channel_id=1, source_target_pairs={{0,2},{1,3},{2,0},{3,1},{4,6},{5,7},{6,4},{7,5},{8,10},{9,11},{10,... | collective-permute-start | bytes 221192 | tf_op jit(solution)/shard_map/ppermute | solution.py:172
  11.9 0.0 collective-permute-done.other
  11.9 0.0 collective-permute-start.1
  13.2 1.5 %shard_map.69 = (bf16[256,1152]{1,0:T(8,128)(2,1)S(1)}, bf16[256,1152]{1,0:T(8,128)(2,1)S(1)}, f32[64,1152]{1,0:T(8,128)S(1)}, f32[64,128]{1,0:T(8,128)S(1)}) custom-call(s32[1]{0:T(128)} %bitcast.place, f32[256,1152]{1,0:T(8,128)S(1)} %collective-permute-done.other, f32[256,1152]{1,0:T(8,128)} %source.3), custom_call_target="tpu_custom_call" | custom-call | flops 2359296 | bytes 3866628 | tf_op jit(solution)/shard_map/pallas_call | solution.py:25
  14.7 0.0 copy-start
  14.7 0.0 collective-permute-done.1.perm
  14.7 0.5 %collective-permute-done.6.refs_5_ = bf16[32,1152]{1,0:T(8,128)(2,1)S(1)} collective-permute-done((bf16[32,1152]{1,0:T(8,128)(2,1)S(1)}, bf16[32,1152]{1,0:T(8,128)(2,1)S(1)}, u32[]{:S(2)}, u32[]{:S(2)}) %collective-permute-start.6) | collective-permute-done | bytes 73760 | tf_op jit(solution)/shard_map/ppermute | solution.py:172
  15.2 1.7 %collective-permute-done.3.refs_2_ = bf16[32,1152]{1,0:T(8,128)(2,1)S(1)} collective-permute-done((bf16[32,1152]{1,0:T(8,128)(2,1)S(1)}, bf16[32,1152]{1,0:T(8,128)(2,1)S(1)}, u32[]{:S(2)}, u32[]{:S(2)}) %collective-permute-start.3) | collective-permute-done | bytes 73760 | tf_op jit(solution)/shard_map/ppermute | solution.py:172
  16.9 0.2 collective-permute-done.5.refs_4_
  17.0 0.0 collective-permute-done.4.refs_3_
  17.1 1.0 %shard_map.70 = (bf16[256,256]{1,0:T(8,128)(2,1)S(1)}, bf16[256,1152]{1,0:T(8,128)(2,1)S(1)}) custom-call(s32[1]{0:T(128)} %bitcast.place, s32[1]{0:T(128)} %bitcast.1.column, f32[1]{0:T(128)S(6)} %copy.7.scale, f32[1]{0:T(128)S(6)} %copy.8.shift, s32[1,256]{1,0:T(1,128)S(1)} %collective-permute-done.1.perm, ...), custom_call_target="tpu_custom_call" | custom-call | flops 301989888 | bytes 1901584 | tf_op jit(solution)/shard_map/pallas_call | solution.py:25
  18.1 0.1 collective-permute-start.7
  18.2 0.0 copy-done
  18.2 1.4 %shard_map.71 = (f32[256,1152]{1,0:T(8,128)S(1)}, f32[256,1152]{1,0:T(8,128)S(1)}) custom-call(s32[1]{0:T(128)} %bitcast.place, s32[1]{0:T(128)} %bitcast.1.column, f32[1]{0:T(128)S(6)} %copy.7.scale, f32[1]{0:T(128)S(6)} %copy.8.shift, s32[1,256]{1,0:T(1,128)S(1)} %bitcast.4, bf16[256,1152]{1,0:T(8,128)(2,1)S(1)} %get-tuple-element.25.img, ...), custom_call_target="tpu_custom_call" | custom-call | flops 603979776 | bytes 4260880 | tf_op jit(solution)/shard_map/pallas_call | solution.py:25
  19.6 0.6 %collective-permute-done.7.other = bf16[256,1152]{1,0:T(8,128)(2,1)S(1)} collective-permute-done((bf16[256,1152]{1,0:T(8,128)(2,1)S(1)}, bf16[256,1152]{1,0:T(8,128)(2,1)S(1)}, u32[]{:S(2)}, u32[]{:S(2)}) %collective-permute-start.7) | collective-permute-done | bytes 589856 | tf_op jit(solution)/shard_map/ppermute | solution.py:172
  20.2 0.2 shard_map.72
  20.4 1.6 %collective-permute-start.8 = (bf16[64,1152]{1,0:T(8,128)(2,1)S(1)}, bf16[64,1152]{1,0:T(8,128)(2,1)S(1)}, u32[]{:S(2)}, u32[]{:S(2)}) collective-permute-start(bf16[64,1152]{1,0:T(8,128)(2,1)S(1)} %get-tuple-element.38), channel_id=1, source_target_pairs={{0,8},{8,0},{16,24},{24,16},{1,9},{9,1},{17,25},{25,17},{2,10},{10... | collective-permute-start | bytes 442376 | tf_op jit(solution)/shard_map/ppermute | solution.py:172
  22.0 1.5 %collective-permute-start.9 = (bf16[64,1152]{1,0:T(8,128)(2,1)S(1)}, bf16[64,1152]{1,0:T(8,128)(2,1)S(1)}, u32[]{:S(2)}, u32[]{:S(2)}) collective-permute-start(bf16[64,1152]{1,0:T(8,128)(2,1)S(1)} %get-tuple-element.39), channel_id=1, source_target_pairs={{0,16},{8,24},{16,0},{24,8},{1,17},{9,25},{17,1},{25,9},{2,18},{10... | collective-permute-start | bytes 442376 | tf_op jit(solution)/shard_map/ppermute | solution.py:172
  23.5 0.4 %collective-permute-start.10 = (bf16[64,1152]{1,0:T(8,128)(2,1)S(1)}, bf16[64,1152]{1,0:T(8,128)(2,1)S(1)}, u32[]{:S(2)}, u32[]{:S(2)}) collective-permute-start(bf16[64,1152]{1,0:T(8,128)(2,1)S(1)} %get-tuple-element.40), channel_id=1, source_target_pairs={{0,24},{8,16},{16,8},{24,0},{1,25},{9,17},{17,9},{25,1},{2,26},{10... | collective-permute-start | bytes 442376 | tf_op jit(solution)/shard_map/ppermute | solution.py:172
  23.9 1.5 %collective-permute-start.14 = (bf16[64,1152]{1,0:T(8,128)(2,1)S(1)}, bf16[64,1152]{1,0:T(8,128)(2,1)S(1)}, u32[]{:S(2)}, u32[]{:S(2)}) collective-permute-start(bf16[64,1152]{1,0:T(8,128)(2,1)S(1)} %get-tuple-element.41), channel_id=1, source_target_pairs={{0,2},{1,3},{2,0},{3,1},{4,6},{5,7},{6,4},{7,5},{8,10},{9,11},{10,... | collective-permute-start | bytes 442376 | tf_op jit(solution)/shard_map/ppermute | solution.py:172
  25.4 2.4 %collective-permute-start.15 = (bf16[64,1152]{1,0:T(8,128)(2,1)S(1)}, bf16[64,1152]{1,0:T(8,128)(2,1)S(1)}, u32[]{:S(2)}, u32[]{:S(2)}) collective-permute-start(bf16[64,1152]{1,0:T(8,128)(2,1)S(1)} %get-tuple-element.42), channel_id=1, source_target_pairs={{0,4},{1,5},{2,6},{3,7},{4,0},{5,1},{6,2},{7,3},{8,12},{9,13},{10,... | collective-permute-start | bytes 442376 | tf_op jit(solution)/shard_map/ppermute | solution.py:172
  27.8 0.0 collective-permute-done.8.refs_0_
  27.8 2.5 %collective-permute-start.16 = (bf16[64,1152]{1,0:T(8,128)(2,1)S(1)}, bf16[64,1152]{1,0:T(8,128)(2,1)S(1)}, u32[]{:S(2)}, u32[]{:S(2)}) collective-permute-start(bf16[64,1152]{1,0:T(8,128)(2,1)S(1)} %get-tuple-element.43), channel_id=1, source_target_pairs={{0,6},{1,7},{2,4},{3,5},{4,2},{5,3},{6,0},{7,1},{8,14},{9,15},{10,... | collective-permute-start | bytes 442376 | tf_op jit(solution)/shard_map/ppermute | solution.py:172
  30.3 0.4 %collective-permute-done.9.refs_1_ = bf16[64,1152]{1,0:T(8,128)(2,1)S(1)} collective-permute-done((bf16[64,1152]{1,0:T(8,128)(2,1)S(1)}, bf16[64,1152]{1,0:T(8,128)(2,1)S(1)}, u32[]{:S(2)}, u32[]{:S(2)}) %collective-permute-start.9) | collective-permute-done | bytes 147488 | tf_op jit(solution)/shard_map/ppermute | solution.py:172
  30.7 0.0 collective-permute-done.10.refs_2_
  30.7 0.2 shard_map.73.refs_0_
  30.9 2.2 %collective-permute-start.13 = (bf16[64,1152]{1,0:T(8,128)(2,1)S(1)}, bf16[64,1152]{1,0:T(8,128)(2,1)S(1)}, u32[]{:S(2)}, u32[]{:S(2)}) collective-permute-start(bf16[64,1152]{1,0:T(8,128)(2,1)S(1)} %shard_map.73.refs_0_), channel_id=1, source_target_pairs={{0,24},{8,16},{16,8},{24,0},{1,25},{9,17},{17,9},{25,1},{2,26},{10... | collective-permute-start | bytes 442376 | tf_op jit(solution)/shard_map/ppermute | solution.py:172
  33.1 0.6 %collective-permute-start.12 = (bf16[64,1152]{1,0:T(8,128)(2,1)S(1)}, bf16[64,1152]{1,0:T(8,128)(2,1)S(1)}, u32[]{:S(2)}, u32[]{:S(2)}) collective-permute-start(bf16[64,1152]{1,0:T(8,128)(2,1)S(1)} %shard_map.73.refs_0_), channel_id=1, source_target_pairs={{0,16},{8,24},{16,0},{24,8},{1,17},{9,25},{17,1},{25,9},{2,18},{10... | collective-permute-start | bytes 442376 | tf_op jit(solution)/shard_map/ppermute | solution.py:172
  33.7 0.0 collective-permute-done.14.refs_4_
  33.7 0.8 %collective-permute-start.11 = (bf16[64,1152]{1,0:T(8,128)(2,1)S(1)}, bf16[64,1152]{1,0:T(8,128)(2,1)S(1)}, u32[]{:S(2)}, u32[]{:S(2)}) collective-permute-start(bf16[64,1152]{1,0:T(8,128)(2,1)S(1)} %shard_map.73.refs_0_), channel_id=1, source_target_pairs={{0,8},{8,0},{16,24},{24,16},{1,9},{9,1},{17,25},{25,17},{2,10},{10... | collective-permute-start | bytes 442376 | tf_op jit(solution)/shard_map/ppermute | solution.py:172
  34.5 4.5 %collective-permute-done.15.refs_5_ = bf16[64,1152]{1,0:T(8,128)(2,1)S(1)} collective-permute-done((bf16[64,1152]{1,0:T(8,128)(2,1)S(1)}, bf16[64,1152]{1,0:T(8,128)(2,1)S(1)}, u32[]{:S(2)}, u32[]{:S(2)}) %collective-permute-start.15) | collective-permute-done | bytes 147488 | tf_op jit(solution)/shard_map/ppermute | solution.py:172
  39.0 0.0 collective-permute-done.16.refs_6_
  39.0 0.0 collective-permute-done.13.refs_3_
  39.0 1.0 %collective-permute-done.12.refs_2_ = bf16[64,1152]{1,0:T(8,128)(2,1)S(1)} collective-permute-done((bf16[64,1152]{1,0:T(8,128)(2,1)S(1)}, bf16[64,1152]{1,0:T(8,128)(2,1)S(1)}, u32[]{:S(2)}, u32[]{:S(2)}) %collective-permute-start.12) | collective-permute-done | bytes 147488 | tf_op jit(solution)/shard_map/ppermute | solution.py:172
  40.0 0.0 collective-permute-done.11.refs_1_
  40.0 1.3 %shard_map.74 = (f32[256,1152]{1,0:T(8,128)}, f32[64,1152]{1,0:T(8,128)}) custom-call(s32[1]{0:T(128)} %bitcast.place, f32[1]{0:T(128)S(6)} %copy.7.scale, f32[64,1152]{1,0:T(8,128)S(1)} %get-tuple-element.23.unit, f32[64,128]{1,0:T(8,128)S(1)} %get-tuple-element.24.inverse, f32[64,1152]{1,0:T(8,128)S(1)} %get-tuple-element.34.own, ...), custom_call_target="tpu_custom_call" | custom-call | flops 737280 | bytes 2359296 | tf_op jit(solution)/shard_map/pallas_call | solution.py:258
Async XLA Ops:
  0.6 11.3 %collective-permute-start = (f32[256,1152]{1,0:T(8,128)}, f32[256,1152]{1,0:T(8,128)S(1)}, u32[]{:S(2)}, u32[]{:S(2)}) collective-permute-start(f32[256,1152]{1,0:T(8,128)} %source.3), channel_id=1, source_target_pairs={{0,1},{1,0},{2,3},{3,2},{4,5},{5,4},{6,7},{7,6},{8,9},{9,8},{10,11... | collective-permute-start | bytes 3538952 | tf_op jit(solution)/shard_map/ppermute | solution.py:172
  2.3 8.4 %collective-permute-start.2 = (bf16[32,1152]{1,0:T(8,128)(2,1)S(1)}, bf16[32,1152]{1,0:T(8,128)(2,1)S(1)}, u32[]{:S(2)}, u32[]{:S(2)}) collective-permute-start(bf16[32,1152]{1,0:T(8,128)(2,1)S(1)} %get-tuple-element.28), channel_id=1, source_target_pairs={{0,4},{1,5},{2,6},{3,7},{4,0},{5,1},{6,2},{7,3},{8,12},{9,13},{10,... | collective-permute-start | bytes 221192 | tf_op jit(solution)/shard_map/ppermute | solution.py:172
  5.9 11.1 %collective-permute-start.4 = (bf16[64,1152]{1,0:T(8,128)(2,1)S(1)}, bf16[64,1152]{1,0:T(8,128)(2,1)S(1)}, u32[]{:S(2)}, u32[]{:S(2)}) collective-permute-start(bf16[64,1152]{1,0:T(8,128)(2,1)S(1)} %get-tuple-element.27.refs_0_), channel_id=1, source_target_pairs={{0,2},{1,3},{2,0},{3,1},{4,6},{5,7},{6,4},{7,5},{8,10},{9,11},{10,... | collective-permute-start | bytes 442376 | tf_op jit(solution)/shard_map/ppermute | solution.py:172
  7.5 7.7 %collective-permute-start.6 = (bf16[32,1152]{1,0:T(8,128)(2,1)S(1)}, bf16[32,1152]{1,0:T(8,128)(2,1)S(1)}, u32[]{:S(2)}, u32[]{:S(2)}) collective-permute-start(bf16[32,1152]{1,0:T(8,128)(2,1)S(1)} %get-tuple-element.29), channel_id=1, source_target_pairs={{0,6},{1,7},{2,4},{3,5},{4,2},{5,3},{6,0},{7,1},{8,14},{9,15},{10,... | collective-permute-start | bytes 221192 | tf_op jit(solution)/shard_map/ppermute | solution.py:172
  7.5 9.4 %collective-permute-start.3 = (bf16[32,1152]{1,0:T(8,128)(2,1)S(1)}, bf16[32,1152]{1,0:T(8,128)(2,1)S(1)}, u32[]{:S(2)}, u32[]{:S(2)}) collective-permute-start(bf16[32,1152]{1,0:T(8,128)(2,1)S(1)} %get-tuple-element.29), channel_id=1, source_target_pairs={{0,4},{1,5},{2,6},{3,7},{4,0},{5,1},{6,2},{7,3},{8,12},{9,13},{10,... | collective-permute-start | bytes 221192 | tf_op jit(solution)/shard_map/ppermute | solution.py:172
  10.6 6.4 %collective-permute-start.5 = (bf16[32,1152]{1,0:T(8,128)(2,1)S(1)}, bf16[32,1152]{1,0:T(8,128)(2,1)S(1)}, u32[]{:S(2)}, u32[]{:S(2)}) collective-permute-start(bf16[32,1152]{1,0:T(8,128)(2,1)S(1)} %collective-permute-done.2.refs_1_), channel_id=1, source_target_pairs={{0,2},{1,3},{2,0},{3,1},{4,6},{5,7},{6,4},{7,5},{8,10},{9,11},{10,... | collective-permute-start | bytes 221192 | tf_op jit(solution)/shard_map/ppermute | solution.py:172
  11.9 2.8 %collective-permute-start.1 = (s32[1,256]{1,0:T(1,128)}, s32[1,256]{1,0:T(1,128)S(1)}, u32[]{:S(2)}, u32[]{:S(2)}) collective-permute-start(s32[1,256]{1,0:T(1,128)} %bitcast.3), channel_id=1, source_target_pairs={{0,1},{1,0},{2,3},{3,2},{4,5},{5,4},{6,7},{7,6},{8,9},{9,8},{10,11... | collective-permute-start | bytes 3080 | tf_op jit(solution)/shard_map/ppermute | solution.py:172
  14.7 3.5 %copy-start = (s32[256]{0:T(256)S(1)}, s32[256]{0:T(256)}, u32[]{:S(2)}) copy-start(s32[256]{0:T(256)} %param.7) | copy-start | bytes 3076
  18.1 2.1 %collective-permute-start.7 = (bf16[256,1152]{1,0:T(8,128)(2,1)S(1)}, bf16[256,1152]{1,0:T(8,128)(2,1)S(1)}, u32[]{:S(2)}, u32[]{:S(2)}) collective-permute-start(bf16[256,1152]{1,0:T(8,128)(2,1)S(1)} %get-tuple-element.32), channel_id=1, source_target_pairs={{0,1},{1,0},{2,3},{3,2},{4,5},{5,4},{6,7},{7,6},{8,9},{9,8},{10,11... | collective-permute-start | bytes 1769480 | tf_op jit(solution)/shard_map/ppermute | solution.py:172
  20.4 7.4 %collective-permute-start.8 = (bf16[64,1152]{1,0:T(8,128)(2,1)S(1)}, bf16[64,1152]{1,0:T(8,128)(2,1)S(1)}, u32[]{:S(2)}, u32[]{:S(2)}) collective-permute-start(bf16[64,1152]{1,0:T(8,128)(2,1)S(1)} %get-tuple-element.38), channel_id=1, source_target_pairs={{0,8},{8,0},{16,24},{24,16},{1,9},{9,1},{17,25},{25,17},{2,10},{10... | collective-permute-start | bytes 442376 | tf_op jit(solution)/shard_map/ppermute | solution.py:172
  22.0 8.8 %collective-permute-start.9 = (bf16[64,1152]{1,0:T(8,128)(2,1)S(1)}, bf16[64,1152]{1,0:T(8,128)(2,1)S(1)}, u32[]{:S(2)}, u32[]{:S(2)}) collective-permute-start(bf16[64,1152]{1,0:T(8,128)(2,1)S(1)} %get-tuple-element.39), channel_id=1, source_target_pairs={{0,16},{8,24},{16,0},{24,8},{1,17},{9,25},{17,1},{25,9},{2,18},{10... | collective-permute-start | bytes 442376 | tf_op jit(solution)/shard_map/ppermute | solution.py:172
  23.5 7.3 %collective-permute-start.10 = (bf16[64,1152]{1,0:T(8,128)(2,1)S(1)}, bf16[64,1152]{1,0:T(8,128)(2,1)S(1)}, u32[]{:S(2)}, u32[]{:S(2)}) collective-permute-start(bf16[64,1152]{1,0:T(8,128)(2,1)S(1)} %get-tuple-element.40), channel_id=1, source_target_pairs={{0,24},{8,16},{16,8},{24,0},{1,25},{9,17},{17,9},{25,1},{2,26},{10... | collective-permute-start | bytes 442376 | tf_op jit(solution)/shard_map/ppermute | solution.py:172
  23.9 9.8 %collective-permute-start.14 = (bf16[64,1152]{1,0:T(8,128)(2,1)S(1)}, bf16[64,1152]{1,0:T(8,128)(2,1)S(1)}, u32[]{:S(2)}, u32[]{:S(2)}) collective-permute-start(bf16[64,1152]{1,0:T(8,128)(2,1)S(1)} %get-tuple-element.41), channel_id=1, source_target_pairs={{0,2},{1,3},{2,0},{3,1},{4,6},{5,7},{6,4},{7,5},{8,10},{9,11},{10,... | collective-permute-start | bytes 442376 | tf_op jit(solution)/shard_map/ppermute | solution.py:172
  25.4 13.6 %collective-permute-start.15 = (bf16[64,1152]{1,0:T(8,128)(2,1)S(1)}, bf16[64,1152]{1,0:T(8,128)(2,1)S(1)}, u32[]{:S(2)}, u32[]{:S(2)}) collective-permute-start(bf16[64,1152]{1,0:T(8,128)(2,1)S(1)} %get-tuple-element.42), channel_id=1, source_target_pairs={{0,4},{1,5},{2,6},{3,7},{4,0},{5,1},{6,2},{7,3},{8,12},{9,13},{10,... | collective-permute-start | bytes 442376 | tf_op jit(solution)/shard_map/ppermute | solution.py:172
  27.8 11.2 %collective-permute-start.16 = (bf16[64,1152]{1,0:T(8,128)(2,1)S(1)}, bf16[64,1152]{1,0:T(8,128)(2,1)S(1)}, u32[]{:S(2)}, u32[]{:S(2)}) collective-permute-start(bf16[64,1152]{1,0:T(8,128)(2,1)S(1)} %get-tuple-element.43), channel_id=1, source_target_pairs={{0,6},{1,7},{2,4},{3,5},{4,2},{5,3},{6,0},{7,1},{8,14},{9,15},{10,... | collective-permute-start | bytes 442376 | tf_op jit(solution)/shard_map/ppermute | solution.py:172
  30.9 8.1 %collective-permute-start.13 = (bf16[64,1152]{1,0:T(8,128)(2,1)S(1)}, bf16[64,1152]{1,0:T(8,128)(2,1)S(1)}, u32[]{:S(2)}, u32[]{:S(2)}) collective-permute-start(bf16[64,1152]{1,0:T(8,128)(2,1)S(1)} %shard_map.73.refs_0_), channel_id=1, source_target_pairs={{0,24},{8,16},{16,8},{24,0},{1,25},{9,17},{17,9},{25,1},{2,26},{10... | collective-permute-start | bytes 442376 | tf_op jit(solution)/shard_map/ppermute | solution.py:172
  33.1 6.9 %collective-permute-start.12 = (bf16[64,1152]{1,0:T(8,128)(2,1)S(1)}, bf16[64,1152]{1,0:T(8,128)(2,1)S(1)}, u32[]{:S(2)}, u32[]{:S(2)}) collective-permute-start(bf16[64,1152]{1,0:T(8,128)(2,1)S(1)} %shard_map.73.refs_0_), channel_id=1, source_target_pairs={{0,16},{8,24},{16,0},{24,8},{1,17},{9,25},{17,1},{25,9},{2,18},{10... | collective-permute-start | bytes 442376 | tf_op jit(solution)/shard_map/ppermute | solution.py:172
  33.7 6.3 %collective-permute-start.11 = (bf16[64,1152]{1,0:T(8,128)(2,1)S(1)}, bf16[64,1152]{1,0:T(8,128)(2,1)S(1)}, u32[]{:S(2)}, u32[]{:S(2)}) collective-permute-start(bf16[64,1152]{1,0:T(8,128)(2,1)S(1)} %shard_map.73.refs_0_), channel_id=1, source_target_pairs={{0,8},{8,0},{16,24},{24,16},{1,9},{9,1},{17,25},{25,17},{2,10},{10... | collective-permute-start | bytes 442376 | tf_op jit(solution)/shard_map/ppermute | solution.py:172

commit v13 on v12

--- a/solution.py
+++ b/solution.py
@@ -144,14 +144,15 @@
     ).astype(BF16)
 
 
-def last_body(count, place, scale, unit, inverse, own, *refs):
+def last_body(partners, place, scale, unit, inverse, own, *refs):
+    count = len(partners)
     parts = refs[:count]
     *back, img_out, txt_out, img_held, txt_held, sems = refs[count:]
     rows = parts[0].shape[0]
     copies = []
-    for k in range(count):
+    for k, partner in enumerate(partners):
         img_held[k * rows : (k + 1) * rows, :] = parts[k][...].astype(F32)
-        start = pl.multiple_of((place[0] ^ k) * rows, rows)
+        start = pl.multiple_of((place[0] ^ partner) * rows, rows)
         copies.append(
             pltpu.make_async_copy(
                 img_held.at[pl.ds(k * rows, rows), :],
@@ -254,9 +255,10 @@
         24 << 20,
         10 * part * width,
     )
-    grads = [grad_part] + [swapped(grad_part, "img", k) for k in range(1, count)]
+    partners = list(range(count - 1, 0, -1))
+    grads = [grad_part] + [swapped(grad_part, "img", k) for k in partners]
     return pl.pallas_call(
-        functools.partial(last_body, count),
+        functools.partial(last_body, [0, *partners]),
         out_shape=[struct(rows, width, F32), struct(txt_rows, width, F32)],
         in_specs=[SMEM] * 2 + [VMEM] * (2 + count + blocks),
         out_specs=[ANY] * 2,

time: 41.5 us -> 41.6 us (level)
  no operation moved by 1% of the time
where the time goes in v13:
time: 41.6 us; the launch traced here: 41.4 us
  starting transfers between devices  22.5 us (54%)
  waiting for transfers between devices  10.3 us (25%)
  Pallas kernels  6.65 us (16%)
  between operations  2.01 us (5%)
    ppermute x17, starting transfers between devices, swapped(): return lax.ppermute(value, axis, [(s, s ^ step) for s in range(count)])  22.5 us
    ppermute x17, waiting for transfers between devices, swapped(): return lax.ppermute(value, axis, [(s, s ^ step) for s in range(count)])  10.3 us
    pallas_call x6, Pallas kernels, call(): pl.pallas_call(body, out_shape=outs, in_specs=specs, out_specs=[VMEM] * l...  5.38 us
    pallas_call x1, Pallas kernels, local(): pl.pallas_call(functools.partial(last_body, [0, *partners]), out_shape=[s...  1.27 us
  transfers between devices with their start and end apart: 17, of which 8 were waited for; matrix products, arithmetic and copies ran while one was open for 0% of the time, Pallas kernels for 10%

profile of v13, /device:TPU:0, one launch (start us, length us, event | category | flops | bytes accessed | tf_op | source)
XLA Modules:
  0.0 41.4 jit_solution(5128577265963076381)
XLA Ops:
  0.6 0.5 %collective-permute-start = (f32[256,1152]{1,0:T(8,128)}, f32[256,1152]{1,0:T(8,128)S(1)}, u32[]{:S(2)}, u32[]{:S(2)}) collective-permute-start(f32[256,1152]{1,0:T(8,128)} %source.3), channel_id=1, source_target_pairs={{0,1},{1,0},{2,3},{3,2},{4,5},{5,4},{6,7},{7,6},{8,9},{9,8},{10,11... | collective-permute-start | bytes 3538952 | tf_op jit(solution)/shard_map/ppermute | solution.py:173
  1.1 1.1 %shard_map.68 = (bf16[64,1152]{1,0:T(8,128)(2,1)S(1)}, bf16[32,1152]{1,0:T(8,128)(2,1)S(1)}, bf16[32,1152]{1,0:T(8,128)(2,1)S(1)}, f32[64,1152]{1,0:T(8,128)S(1)}, f32[64,128]{1,0:T(8,128)S(1)}) custom-call(f32[64,1152]{1,0:T(8,128)} %source.2), custom_call_target="tpu_custom_call" | custom-call | flops 294912 | bytes 917504 | tf_op jit(solution)/shard_map/pallas_call | solution.py:25
  2.3 3.7 %collective-permute-start.2 = (bf16[32,1152]{1,0:T(8,128)(2,1)S(1)}, bf16[32,1152]{1,0:T(8,128)(2,1)S(1)}, u32[]{:S(2)}, u32[]{:S(2)}) collective-permute-start(bf16[32,1152]{1,0:T(8,128)(2,1)S(1)} %get-tuple-element.28), channel_id=1, source_target_pairs={{0,4},{1,5},{2,6},{3,7},{4,0},{5,1},{6,2},{7,3},{8,12},{9,13},{10,... | collective-permute-start | bytes 221192 | tf_op jit(solution)/shard_map/ppermute | solution.py:173
  5.9 1.6 %collective-permute-start.4 = (bf16[64,1152]{1,0:T(8,128)(2,1)S(1)}, bf16[64,1152]{1,0:T(8,128)(2,1)S(1)}, u32[]{:S(2)}, u32[]{:S(2)}) collective-permute-start(bf16[64,1152]{1,0:T(8,128)(2,1)S(1)} %get-tuple-element.27.refs_0_), channel_id=1, source_target_pairs={{0,2},{1,3},{2,0},{3,1},{4,6},{5,7},{6,4},{7,5},{8,10},{9,11},{10,... | collective-permute-start | bytes 442376 | tf_op jit(solution)/shard_map/ppermute | solution.py:173
  7.5 0.0 collective-permute-start.6
  7.5 1.9 %collective-permute-start.3 = (bf16[32,1152]{1,0:T(8,128)(2,1)S(1)}, bf16[32,1152]{1,0:T(8,128)(2,1)S(1)}, u32[]{:S(2)}, u32[]{:S(2)}) collective-permute-start(bf16[32,1152]{1,0:T(8,128)(2,1)S(1)} %get-tuple-element.29), channel_id=1, source_target_pairs={{0,4},{1,5},{2,6},{3,7},{4,0},{5,1},{6,2},{7,3},{8,12},{9,13},{10,... | collective-permute-start | bytes 221192 | tf_op jit(solution)/shard_map/ppermute | solution.py:173
  9.4 1.2 %collective-permute-done.2.refs_1_ = bf16[32,1152]{1,0:T(8,128)(2,1)S(1)} collective-permute-done((bf16[32,1152]{1,0:T(8,128)(2,1)S(1)}, bf16[32,1152]{1,0:T(8,128)(2,1)S(1)}, u32[]{:S(2)}, u32[]{:S(2)}) %collective-permute-start.2) | collective-permute-done | bytes 73760 | tf_op jit(solution)/shard_map/ppermute | solution.py:173
  10.6 1.3 %collective-permute-start.5 = (bf16[32,1152]{1,0:T(8,128)(2,1)S(1)}, bf16[32,1152]{1,0:T(8,128)(2,1)S(1)}, u32[]{:S(2)}, u32[]{:S(2)}) collective-permute-start(bf16[32,1152]{1,0:T(8,128)(2,1)S(1)} %collective-permute-done.2.refs_1_), channel_id=1, source_target_pairs={{0,2},{1,3},{2,0},{3,1},{4,6},{5,7},{6,4},{7,5},{8,10},{9,11},{10,... | collective-permute-start | bytes 221192 | tf_op jit(solution)/shard_map/ppermute | solution.py:173
  11.9 0.0 collective-permute-done.other
  11.9 0.0 collective-permute-start.1
  13.2 1.5 %shard_map.69 = (bf16[256,1152]{1,0:T(8,128)(2,1)S(1)}, bf16[256,1152]{1,0:T(8,128)(2,1)S(1)}, f32[64,1152]{1,0:T(8,128)S(1)}, f32[64,128]{1,0:T(8,128)S(1)}) custom-call(s32[1]{0:T(128)} %bitcast.place, f32[256,1152]{1,0:T(8,128)S(1)} %collective-permute-done.other, f32[256,1152]{1,0:T(8,128)} %source.3), custom_call_target="tpu_custom_call" | custom-call | flops 2359296 | bytes 3866628 | tf_op jit(solution)/shard_map/pallas_call | solution.py:25
  14.7 0.0 copy-start
  14.7 0.0 collective-permute-done.1.perm
  14.7 0.5 %collective-permute-done.6.refs_5_ = bf16[32,1152]{1,0:T(8,128)(2,1)S(1)} collective-permute-done((bf16[32,1152]{1,0:T(8,128)(2,1)S(1)}, bf16[32,1152]{1,0:T(8,128)(2,1)S(1)}, u32[]{:S(2)}, u32[]{:S(2)}) %collective-permute-start.6) | collective-permute-done | bytes 73760 | tf_op jit(solution)/shard_map/ppermute | solution.py:173
  15.2 1.7 %collective-permute-done.3.refs_2_ = bf16[32,1152]{1,0:T(8,128)(2,1)S(1)} collective-permute-done((bf16[32,1152]{1,0:T(8,128)(2,1)S(1)}, bf16[32,1152]{1,0:T(8,128)(2,1)S(1)}, u32[]{:S(2)}, u32[]{:S(2)}) %collective-permute-start.3) | collective-permute-done | bytes 73760 | tf_op jit(solution)/shard_map/ppermute | solution.py:173
  16.9 0.2 collective-permute-done.5.refs_4_
  17.0 0.0 collective-permute-done.4.refs_3_
  17.1 1.0 %shard_map.70 = (bf16[256,256]{1,0:T(8,128)(2,1)S(1)}, bf16[256,1152]{1,0:T(8,128)(2,1)S(1)}) custom-call(s32[1]{0:T(128)} %bitcast.place, s32[1]{0:T(128)} %bitcast.1.column, f32[1]{0:T(128)S(6)} %copy.7.scale, f32[1]{0:T(128)S(6)} %copy.8.shift, s32[1,256]{1,0:T(1,128)S(1)} %collective-permute-done.1.perm, ...), custom_call_target="tpu_custom_call" | custom-call | flops 301989888 | bytes 1901584 | tf_op jit(solution)/shard_map/pallas_call | solution.py:25
  18.1 0.1 collective-permute-start.7
  18.2 0.0 copy-done
  18.2 1.4 %shard_map.71 = (f32[256,1152]{1,0:T(8,128)S(1)}, f32[256,1152]{1,0:T(8,128)S(1)}) custom-call(s32[1]{0:T(128)} %bitcast.place, s32[1]{0:T(128)} %bitcast.1.column, f32[1]{0:T(128)S(6)} %copy.7.scale, f32[1]{0:T(128)S(6)} %copy.8.shift, s32[1,256]{1,0:T(1,128)S(1)} %bitcast.4, bf16[256,1152]{1,0:T(8,128)(2,1)S(1)} %get-tuple-element.25.img, ...), custom_call_target="tpu_custom_call" | custom-call | flops 603979776 | bytes 4260880 | tf_op jit(solution)/shard_map/pallas_call | solution.py:25
  19.6 0.6 %collective-permute-done.7.other = bf16[256,1152]{1,0:T(8,128)(2,1)S(1)} collective-permute-done((bf16[256,1152]{1,0:T(8,128)(2,1)S(1)}, bf16[256,1152]{1,0:T(8,128)(2,1)S(1)}, u32[]{:S(2)}, u32[]{:S(2)}) %collective-permute-start.7) | collective-permute-done | bytes 589856 | tf_op jit(solution)/shard_map/ppermute | solution.py:173
  20.2 0.2 shard_map.72
  20.4 1.6 %collective-permute-start.8 = (bf16[64,1152]{1,0:T(8,128)(2,1)S(1)}, bf16[64,1152]{1,0:T(8,128)(2,1)S(1)}, u32[]{:S(2)}, u32[]{:S(2)}) collective-permute-start(bf16[64,1152]{1,0:T(8,128)(2,1)S(1)} %get-tuple-element.38), channel_id=1, source_target_pairs={{0,8},{8,0},{16,24},{24,16},{1,9},{9,1},{17,25},{25,17},{2,10},{10... | collective-permute-start | bytes 442376 | tf_op jit(solution)/shard_map/ppermute | solution.py:173
  22.0 1.5 %collective-permute-start.9 = (bf16[64,1152]{1,0:T(8,128)(2,1)S(1)}, bf16[64,1152]{1,0:T(8,128)(2,1)S(1)}, u32[]{:S(2)}, u32[]{:S(2)}) collective-permute-start(bf16[64,1152]{1,0:T(8,128)(2,1)S(1)} %get-tuple-element.39), channel_id=1, source_target_pairs={{0,16},{8,24},{16,0},{24,8},{1,17},{9,25},{17,1},{25,9},{2,18},{10... | collective-permute-start | bytes 442376 | tf_op jit(solution)/shard_map/ppermute | solution.py:173
  23.5 0.4 %collective-permute-start.10 = (bf16[64,1152]{1,0:T(8,128)(2,1)S(1)}, bf16[64,1152]{1,0:T(8,128)(2,1)S(1)}, u32[]{:S(2)}, u32[]{:S(2)}) collective-permute-start(bf16[64,1152]{1,0:T(8,128)(2,1)S(1)} %get-tuple-element.40), channel_id=1, source_target_pairs={{0,24},{8,16},{16,8},{24,0},{1,25},{9,17},{17,9},{25,1},{2,26},{10... | collective-permute-start | bytes 442376 | tf_op jit(solution)/shard_map/ppermute | solution.py:173
  23.9 1.5 %collective-permute-start.14 = (bf16[64,1152]{1,0:T(8,128)(2,1)S(1)}, bf16[64,1152]{1,0:T(8,128)(2,1)S(1)}, u32[]{:S(2)}, u32[]{:S(2)}) collective-permute-start(bf16[64,1152]{1,0:T(8,128)(2,1)S(1)} %get-tuple-element.41), channel_id=1, source_target_pairs={{0,2},{1,3},{2,0},{3,1},{4,6},{5,7},{6,4},{7,5},{8,10},{9,11},{10,... | collective-permute-start | bytes 442376 | tf_op jit(solution)/shard_map/ppermute | solution.py:173
  25.4 2.4 %collective-permute-start.15 = (bf16[64,1152]{1,0:T(8,128)(2,1)S(1)}, bf16[64,1152]{1,0:T(8,128)(2,1)S(1)}, u32[]{:S(2)}, u32[]{:S(2)}) collective-permute-start(bf16[64,1152]{1,0:T(8,128)(2,1)S(1)} %get-tuple-element.42), channel_id=1, source_target_pairs={{0,4},{1,5},{2,6},{3,7},{4,0},{5,1},{6,2},{7,3},{8,12},{9,13},{10,... | collective-permute-start | bytes 442376 | tf_op jit(solution)/shard_map/ppermute | solution.py:173
  27.8 0.0 collective-permute-done.8.refs_0_
  27.8 2.5 %collective-permute-start.16 = (bf16[64,1152]{1,0:T(8,128)(2,1)S(1)}, bf16[64,1152]{1,0:T(8,128)(2,1)S(1)}, u32[]{:S(2)}, u32[]{:S(2)}) collective-permute-start(bf16[64,1152]{1,0:T(8,128)(2,1)S(1)} %get-tuple-element.43), channel_id=1, source_target_pairs={{0,6},{1,7},{2,4},{3,5},{4,2},{5,3},{6,0},{7,1},{8,14},{9,15},{10,... | collective-permute-start | bytes 442376 | tf_op jit(solution)/shard_map/ppermute | solution.py:173
  30.3 0.4 %collective-permute-done.9.refs_1_ = bf16[64,1152]{1,0:T(8,128)(2,1)S(1)} collective-permute-done((bf16[64,1152]{1,0:T(8,128)(2,1)S(1)}, bf16[64,1152]{1,0:T(8,128)(2,1)S(1)}, u32[]{:S(2)}, u32[]{:S(2)}) %collective-permute-start.9) | collective-permute-done | bytes 147488 | tf_op jit(solution)/shard_map/ppermute | solution.py:173
  30.7 0.0 collective-permute-done.10.refs_2_
  30.7 0.2 shard_map.73.refs_0_
  30.9 1.3 %collective-permute-start.13 = (bf16[64,1152]{1,0:T(8,128)(2,1)S(1)}, bf16[64,1152]{1,0:T(8,128)(2,1)S(1)}, u32[]{:S(2)}, u32[]{:S(2)}) collective-permute-start(bf16[64,1152]{1,0:T(8,128)(2,1)S(1)} %shard_map.73.refs_0_), channel_id=1, source_target_pairs={{0,8},{8,0},{16,24},{24,16},{1,9},{9,1},{17,25},{25,17},{2,10},{10... | collective-permute-start | bytes 442376 | tf_op jit(solution)/shard_map/ppermute | solution.py:173
  32.2 1.5 %collective-permute-start.12 = (bf16[64,1152]{1,0:T(8,128)(2,1)S(1)}, bf16[64,1152]{1,0:T(8,128)(2,1)S(1)}, u32[]{:S(2)}, u32[]{:S(2)}) collective-permute-start(bf16[64,1152]{1,0:T(8,128)(2,1)S(1)} %shard_map.73.refs_0_), channel_id=1, source_target_pairs={{0,16},{8,24},{16,0},{24,8},{1,17},{9,25},{17,1},{25,9},{2,18},{10... | collective-permute-start | bytes 442376 | tf_op jit(solution)/shard_map/ppermute | solution.py:173
  33.7 0.0 collective-permute-done.14.refs_4_
  33.7 0.8 %collective-permute-start.11 = (bf16[64,1152]{1,0:T(8,128)(2,1)S(1)}, bf16[64,1152]{1,0:T(8,128)(2,1)S(1)}, u32[]{:S(2)}, u32[]{:S(2)}) collective-permute-start(bf16[64,1152]{1,0:T(8,128)(2,1)S(1)} %shard_map.73.refs_0_), channel_id=1, source_target_pairs={{0,24},{8,16},{16,8},{24,0},{1,25},{9,17},{17,9},{25,1},{2,26},{10... | collective-permute-start | bytes 442376 | tf_op jit(solution)/shard_map/ppermute | solution.py:173
  34.5 4.5 %collective-permute-done.15.refs_5_ = bf16[64,1152]{1,0:T(8,128)(2,1)S(1)} collective-permute-done((bf16[64,1152]{1,0:T(8,128)(2,1)S(1)}, bf16[64,1152]{1,0:T(8,128)(2,1)S(1)}, u32[]{:S(2)}, u32[]{:S(2)}) %collective-permute-start.15) | collective-permute-done | bytes 147488 | tf_op jit(solution)/shard_map/ppermute | solution.py:173
  39.0 0.0 collective-permute-done.16.refs_6_
  39.0 0.0 collective-permute-done.13.refs_3_
  39.0 1.2 %collective-permute-done.12.refs_2_ = bf16[64,1152]{1,0:T(8,128)(2,1)S(1)} collective-permute-done((bf16[64,1152]{1,0:T(8,128)(2,1)S(1)}, bf16[64,1152]{1,0:T(8,128)(2,1)S(1)}, u32[]{:S(2)}, u32[]{:S(2)}) %collective-permute-start.12) | collective-permute-done | bytes 147488 | tf_op jit(solution)/shard_map/ppermute | solution.py:173
  40.2 0.0 collective-permute-done.11.refs_1_
  40.2 1.3 %shard_map.74 = (f32[256,1152]{1,0:T(8,128)}, f32[64,1152]{1,0:T(8,128)}) custom-call(s32[1]{0:T(128)} %bitcast.place, f32[1]{0:T(128)S(6)} %copy.7.scale, f32[64,1152]{1,0:T(8,128)S(1)} %get-tuple-element.23.unit, f32[64,128]{1,0:T(8,128)S(1)} %get-tuple-element.24.inverse, f32[64,1152]{1,0:T(8,128)S(1)} %get-tuple-element.34.own, ...), custom_call_target="tpu_custom_call" | custom-call | flops 737280 | bytes 2359296 | tf_op jit(solution)/shard_map/pallas_call | solution.py:260
Async XLA Ops:
  0.6 11.3 %collective-permute-start = (f32[256,1152]{1,0:T(8,128)}, f32[256,1152]{1,0:T(8,128)S(1)}, u32[]{:S(2)}, u32[]{:S(2)}) collective-permute-start(f32[256,1152]{1,0:T(8,128)} %source.3), channel_id=1, source_target_pairs={{0,1},{1,0},{2,3},{3,2},{4,5},{5,4},{6,7},{7,6},{8,9},{9,8},{10,11... | collective-permute-start | bytes 3538952 | tf_op jit(solution)/shard_map/ppermute | solution.py:173
  2.3 8.4 %collective-permute-start.2 = (bf16[32,1152]{1,0:T(8,128)(2,1)S(1)}, bf16[32,1152]{1,0:T(8,128)(2,1)S(1)}, u32[]{:S(2)}, u32[]{:S(2)}) collective-permute-start(bf16[32,1152]{1,0:T(8,128)(2,1)S(1)} %get-tuple-element.28), channel_id=1, source_target_pairs={{0,4},{1,5},{2,6},{3,7},{4,0},{5,1},{6,2},{7,3},{8,12},{9,13},{10,... | collective-permute-start | bytes 221192 | tf_op jit(solution)/shard_map/ppermute | solution.py:173
  5.9 11.1 %collective-permute-start.4 = (bf16[64,1152]{1,0:T(8,128)(2,1)S(1)}, bf16[64,1152]{1,0:T(8,128)(2,1)S(1)}, u32[]{:S(2)}, u32[]{:S(2)}) collective-permute-start(bf16[64,1152]{1,0:T(8,128)(2,1)S(1)} %get-tuple-element.27.refs_0_), channel_id=1, source_target_pairs={{0,2},{1,3},{2,0},{3,1},{4,6},{5,7},{6,4},{7,5},{8,10},{9,11},{10,... | collective-permute-start | bytes 442376 | tf_op jit(solution)/shard_map/ppermute | solution.py:173
  7.5 7.7 %collective-permute-start.6 = (bf16[32,1152]{1,0:T(8,128)(2,1)S(1)}, bf16[32,1152]{1,0:T(8,128)(2,1)S(1)}, u32[]{:S(2)}, u32[]{:S(2)}) collective-permute-start(bf16[32,1152]{1,0:T(8,128)(2,1)S(1)} %get-tuple-element.29), channel_id=1, source_target_pairs={{0,6},{1,7},{2,4},{3,5},{4,2},{5,3},{6,0},{7,1},{8,14},{9,15},{10,... | collective-permute-start | bytes 221192 | tf_op jit(solution)/shard_map/ppermute | solution.py:173
  7.5 9.4 %collective-permute-start.3 = (bf16[32,1152]{1,0:T(8,128)(2,1)S(1)}, bf16[32,1152]{1,0:T(8,128)(2,1)S(1)}, u32[]{:S(2)}, u32[]{:S(2)}) collective-permute-start(bf16[32,1152]{1,0:T(8,128)(2,1)S(1)} %get-tuple-element.29), channel_id=1, source_target_pairs={{0,4},{1,5},{2,6},{3,7},{4,0},{5,1},{6,2},{7,3},{8,12},{9,13},{10,... | collective-permute-start | bytes 221192 | tf_op jit(solution)/shard_map/ppermute | solution.py:173
  10.6 6.4 %collective-permute-start.5 = (bf16[32,1152]{1,0:T(8,128)(2,1)S(1)}, bf16[32,1152]{1,0:T(8,128)(2,1)S(1)}, u32[]{:S(2)}, u32[]{:S(2)}) collective-permute-start(bf16[32,1152]{1,0:T(8,128)(2,1)S(1)} %collective-permute-done.2.refs_1_), channel_id=1, source_target_pairs={{0,2},{1,3},{2,0},{3,1},{4,6},{5,7},{6,4},{7,5},{8,10},{9,11},{10,... | collective-permute-start | bytes 221192 | tf_op jit(solution)/shard_map/ppermute | solution.py:173
  11.9 2.8 %collective-permute-start.1 = (s32[1,256]{1,0:T(1,128)}, s32[1,256]{1,0:T(1,128)S(1)}, u32[]{:S(2)}, u32[]{:S(2)}) collective-permute-start(s32[1,256]{1,0:T(1,128)} %bitcast.3), channel_id=1, source_target_pairs={{0,1},{1,0},{2,3},{3,2},{4,5},{5,4},{6,7},{7,6},{8,9},{9,8},{10,11... | collective-permute-start | bytes 3080 | tf_op jit(solution)/shard_map/ppermute | solution.py:173
  14.7 3.5 %copy-start = (s32[256]{0:T(256)S(1)}, s32[256]{0:T(256)}, u32[]{:S(2)}) copy-start(s32[256]{0:T(256)} %param.7) | copy-start | bytes 3076
  18.1 2.1 %collective-permute-start.7 = (bf16[256,1152]{1,0:T(8,128)(2,1)S(1)}, bf16[256,1152]{1,0:T(8,128)(2,1)S(1)}, u32[]{:S(2)}, u32[]{:S(2)}) collective-permute-start(bf16[256,1152]{1,0:T(8,128)(2,1)S(1)} %get-tuple-element.32), channel_id=1, source_target_pairs={{0,1},{1,0},{2,3},{3,2},{4,5},{5,4},{6,7},{7,6},{8,9},{9,8},{10,11... | collective-permute-start | bytes 1769480 | tf_op jit(solution)/shard_map/ppermute | solution.py:173
  20.4 7.4 %collective-permute-start.8 = (bf16[64,1152]{1,0:T(8,128)(2,1)S(1)}, bf16[64,1152]{1,0:T(8,128)(2,1)S(1)}, u32[]{:S(2)}, u32[]{:S(2)}) collective-permute-start(bf16[64,1152]{1,0:T(8,128)(2,1)S(1)} %get-tuple-element.38), channel_id=1, source_target_pairs={{0,8},{8,0},{16,24},{24,16},{1,9},{9,1},{17,25},{25,17},{2,10},{10... | collective-permute-start | bytes 442376 | tf_op jit(solution)/shard_map/ppermute | solution.py:173
  22.0 8.8 %collective-permute-start.9 = (bf16[64,1152]{1,0:T(8,128)(2,1)S(1)}, bf16[64,1152]{1,0:T(8,128)(2,1)S(1)}, u32[]{:S(2)}, u32[]{:S(2)}) collective-permute-start(bf16[64,1152]{1,0:T(8,128)(2,1)S(1)} %get-tuple-element.39), channel_id=1, source_target_pairs={{0,16},{8,24},{16,0},{24,8},{1,17},{9,25},{17,1},{25,9},{2,18},{10... | collective-permute-start | bytes 442376 | tf_op jit(solution)/shard_map/ppermute | solution.py:173
  23.5 7.3 %collective-permute-start.10 = (bf16[64,1152]{1,0:T(8,128)(2,1)S(1)}, bf16[64,1152]{1,0:T(8,128)(2,1)S(1)}, u32[]{:S(2)}, u32[]{:S(2)}) collective-permute-start(bf16[64,1152]{1,0:T(8,128)(2,1)S(1)} %get-tuple-element.40), channel_id=1, source_target_pairs={{0,24},{8,16},{16,8},{24,0},{1,25},{9,17},{17,9},{25,1},{2,26},{10... | collective-permute-start | bytes 442376 | tf_op jit(solution)/shard_map/ppermute | solution.py:173
  23.9 9.8 %collective-permute-start.14 = (bf16[64,1152]{1,0:T(8,128)(2,1)S(1)}, bf16[64,1152]{1,0:T(8,128)(2,1)S(1)}, u32[]{:S(2)}, u32[]{:S(2)}) collective-permute-start(bf16[64,1152]{1,0:T(8,128)(2,1)S(1)} %get-tuple-element.41), channel_id=1, source_target_pairs={{0,2},{1,3},{2,0},{3,1},{4,6},{5,7},{6,4},{7,5},{8,10},{9,11},{10,... | collective-permute-start | bytes 442376 | tf_op jit(solution)/shard_map/ppermute | solution.py:173
  25.4 13.6 %collective-permute-start.15 = (bf16[64,1152]{1,0:T(8,128)(2,1)S(1)}, bf16[64,1152]{1,0:T(8,128)(2,1)S(1)}, u32[]{:S(2)}, u32[]{:S(2)}) collective-permute-start(bf16[64,1152]{1,0:T(8,128)(2,1)S(1)} %get-tuple-element.42), channel_id=1, source_target_pairs={{0,4},{1,5},{2,6},{3,7},{4,0},{5,1},{6,2},{7,3},{8,12},{9,13},{10,... | collective-permute-start | bytes 442376 | tf_op jit(solution)/shard_map/ppermute | solution.py:173
  27.8 11.2 %collective-permute-start.16 = (bf16[64,1152]{1,0:T(8,128)(2,1)S(1)}, bf16[64,1152]{1,0:T(8,128)(2,1)S(1)}, u32[]{:S(2)}, u32[]{:S(2)}) collective-permute-start(bf16[64,1152]{1,0:T(8,128)(2,1)S(1)} %get-tuple-element.43), channel_id=1, source_target_pairs={{0,6},{1,7},{2,4},{3,5},{4,2},{5,3},{6,0},{7,1},{8,14},{9,15},{10,... | collective-permute-start | bytes 442376 | tf_op jit(solution)/shard_map/ppermute | solution.py:173
  30.9 8.1 %collective-permute-start.13 = (bf16[64,1152]{1,0:T(8,128)(2,1)S(1)}, bf16[64,1152]{1,0:T(8,128)(2,1)S(1)}, u32[]{:S(2)}, u32[]{:S(2)}) collective-permute-start(bf16[64,1152]{1,0:T(8,128)(2,1)S(1)} %shard_map.73.refs_0_), channel_id=1, source_target_pairs={{0,8},{8,0},{16,24},{24,16},{1,9},{9,1},{17,25},{25,17},{2,10},{10... | collective-permute-start | bytes 442376 | tf_op jit(solution)/shard_map/ppermute | solution.py:173
  32.2 7.9 %collective-permute-start.12 = (bf16[64,1152]{1,0:T(8,128)(2,1)S(1)}, bf16[64,1152]{1,0:T(8,128)(2,1)S(1)}, u32[]{:S(2)}, u32[]{:S(2)}) collective-permute-start(bf16[64,1152]{1,0:T(8,128)(2,1)S(1)} %shard_map.73.refs_0_), channel_id=1, source_target_pairs={{0,16},{8,24},{16,0},{24,8},{1,17},{9,25},{17,1},{25,9},{2,18},{10... | collective-permute-start | bytes 442376 | tf_op jit(solution)/shard_map/ppermute | solution.py:173
  33.7 6.5 %collective-permute-start.11 = (bf16[64,1152]{1,0:T(8,128)(2,1)S(1)}, bf16[64,1152]{1,0:T(8,128)(2,1)S(1)}, u32[]{:S(2)}, u32[]{:S(2)}) collective-permute-start(bf16[64,1152]{1,0:T(8,128)(2,1)S(1)} %shard_map.73.refs_0_), channel_id=1, source_target_pairs={{0,24},{8,16},{16,8},{24,0},{1,25},{9,17},{17,9},{25,1},{2,26},{10... | collective-permute-start | bytes 442376 | tf_op jit(solution)/shard_map/ppermute | solution.py:173

commit v14 on v13

--- a/solution.py
+++ b/solution.py
@@ -56,11 +56,13 @@
     inv[...] = jnp.broadcast_to(inverse, inv.shape)
 
 
-def unit_img_body(place, other, source, bf, other_bf, unit_out, inv, held, sem):
+def unit_img_body(place, other, source, bf, other_bf, other_turned, unit_out, inv, held, sem):
     copy = pltpu.make_async_copy(source, held, sem)
     copy.start()
     values = other[...]
-    other_bf[...] = (values * inverse_norm(values)).astype(BF16)
+    rounded = (values * inverse_norm(values)).astype(BF16)
+    other_bf[...] = rounded
+    other_turned[...] = rounded.T
     copy.wait()
     values = held[...]
     bf[...] = (values * inverse_norm(values)).astype(BF16)
@@ -71,13 +73,15 @@
     inv[...] = jnp.broadcast_to(inverse, inv.shape)
 
 
-def weights_of(tile, order, line, place, column, scale, shift, perm, img):
+def weights_of(tile, order, line, place, column, scale, shift, perm, img, img_dim=1):
     rows = tile.shape[0] // len(order)
     row = lax.broadcasted_iota(jnp.int32, (rows, 1), 0)
     ids = jnp.concatenate(
         [row + (place[0] * line + (column[0] ^ (2 * k))) * rows for k in order], axis=0
     )
-    products = lax.dot_general(tile, img, (((1,), (1,)), ((), ())), preferred_element_type=F32)
+    products = lax.dot_general(
+        tile, img, (((1,), (img_dim,)), ((), ())), preferred_element_type=F32
+    )
     positive = (ids == perm).astype(F32)
     return (jax.nn.sigmoid(scale[0] * products + shift[0]) - positive).astype(BF16)
 
@@ -94,10 +98,10 @@
     return jnp.concatenate([t[...] for t in tiles], axis=0)
 
 
-def other_body(order, line, place, column, scale, shift, perm, img, *refs):
+def other_body(order, line, place, column, scale, shift, perm, turned, *refs):
     *txt, kept, out = refs
     tile = joined(txt)
-    weights = weights_of(tile, order, line, place, column, scale, shift, perm[...], img[...])
+    weights = weights_of(tile, order, line, place, column, scale, shift, perm[...], turned[...], 0)
     kept[...] = weights
     out[...] = to_images(weights, tile).astype(BF16)
 
@@ -144,14 +148,11 @@
     ).astype(BF16)
 
 
-def last_body(partners, place, scale, unit, inverse, own, *refs):
-    count = len(partners)
-    parts = refs[:count]
-    *back, img_out, txt_out, img_held, txt_held, sems = refs[count:]
+def quarter_copies(partners, place, parts, img_out, img_held, sems):
     rows = parts[0].shape[0]
     copies = []
-    for k, partner in enumerate(partners):
-        img_held[k * rows : (k + 1) * rows, :] = parts[k][...].astype(F32)
+    for k, (partner, part) in enumerate(zip(partners, parts)):
+        img_held[k * rows : (k + 1) * rows, :] = part[...].astype(F32)
         start = pl.multiple_of((place[0] ^ partner) * rows, rows)
         copies.append(
             pltpu.make_async_copy(
@@ -161,10 +162,25 @@
             )
         )
         copies[-1].start()
+    return copies
+
+
+def first_body(partners, place, scale, unit, inverse, own, *refs):
+    count = len(partners)
+    parts = refs[:count]
+    *back, img_out, txt_out, img_held, txt_held, sems = refs[count:]
+    copies = quarter_copies(partners, place, parts, img_out, img_held, sems)
     txt_held[...] = backward_unit(unit[...], inverse[...], scale[0] * total_of(own, back))
     copies.append(pltpu.make_async_copy(txt_held, txt_out, sems.at[count]))
     copies[-1].start()
     for copy in copies:
+        copy.wait()
+
+
+def last_body(partners, place, begun, *refs):
+    del begun
+    *parts, img_out, img_held, sems = refs
+    for copy in quarter_copies(partners, place, parts, img_out, img_held, sems):
         copy.wait()
 
 
@@ -204,9 +220,10 @@
     for k in range(1, half):
         near += [swapped(far[2 * k - 2], "txt", 2), swapped(tail, "txt", 4 * k + 2)]
     tiles = [txt_bf] + far + near
-    img_bf, img_other, img_unit, img_inv = call(
+    img_bf, img_other, turned_other, img_unit, img_inv = call(
         unit_img_body,
-        [struct(rows, width, BF16)] * 2 + [struct(part, width, F32), struct(part, 128, F32)],
+        [struct(rows, width, BF16)] * 2
+        + [struct(width, rows, BF16), struct(part, width, F32), struct(part, 128, F32)],
         [place, raw_other, in_hbm(images)],
         [SMEM, VMEM, ANY],
         24 << 20,
@@ -218,7 +235,7 @@
     kept, other_img = call(
         functools.partial(other_body, order, line),
         [struct(blocks * txt_rows, rows, BF16), struct(rows, width, BF16)],
-        [*scalars, perm_other, img_other, *tiles],
+        [*scalars, perm_other, turned_other, *tiles],
         [SMEM] * 4 + [VMEM] * (2 + len(tiles)),
         40 << 20,
         2 * pairs,
@@ -255,23 +272,41 @@
         24 << 20,
         10 * part * width,
     )
-    partners = list(range(count - 1, 0, -1))
+    partners = [1, *range(count - 1, 1, -1)]
     grads = [grad_part] + [swapped(grad_part, "img", k) for k in partners]
-    return pl.pallas_call(
-        functools.partial(last_body, [0, *partners]),
+    partners = [0, *partners]
+    early = 2
+    begun, grad_texts = pl.pallas_call(
+        functools.partial(first_body, partners[:early]),
         out_shape=[struct(rows, width, F32), struct(txt_rows, width, F32)],
-        in_specs=[SMEM] * 2 + [VMEM] * (2 + count + blocks),
+        in_specs=[SMEM] * 2 + [VMEM] * (2 + early + blocks),
         out_specs=[ANY] * 2,
         scratch_shapes=[
-            pltpu.VMEM((rows, width), F32),
+            pltpu.VMEM((early * part, width), F32),
             pltpu.VMEM((txt_rows, width), F32),
-            pltpu.SemaphoreType.DMA((count + 1,)),
+            pltpu.SemaphoreType.DMA((early + 1,)),
         ],
         compiler_params=pltpu.CompilerParams(vmem_limit_bytes=24 << 20),
         cost_estimate=pl.CostEstimate(
             flops=10 * txt_rows * width, bytes_accessed=8 * rows * width, transcendentals=0
         ),
-    )(place, scale, txt_unit, txt_inv, own_txt, *grads, *back)
+    )(place, scale, txt_unit, txt_inv, own_txt, *grads[:early], *back)
+    grad_images = pl.pallas_call(
+        functools.partial(last_body, partners[early:]),
+        out_shape=struct(rows, width, F32),
+        in_specs=[SMEM, ANY] + [VMEM] * (count - early),
+        out_specs=ANY,
+        scratch_shapes=[
+            pltpu.VMEM(((count - early) * part, width), F32),
+            pltpu.SemaphoreType.DMA((count - early,)),
+        ],
+        input_output_aliases={1: 0},
+        compiler_params=pltpu.CompilerParams(vmem_limit_bytes=24 << 20),
+        cost_estimate=pl.CostEstimate(
+            flops=rows * width, bytes_accessed=8 * rows * width, transcendentals=0
+        ),
+    )(place, begun, *grads[early:])
+    return (grad_images, grad_texts)
 
 
 def solution(mesh):

time: 41.6 us -> 41.2 us (level)
  waiting for transfers between devices: 10.3 us -> 9.21 us
  Pallas kernels: 6.65 us -> 7.21 us
    ppermute x17, waiting for transfers between devices: 10.3 us -> 9.21 us  [swapped(): return lax.ppermute(value, axis, [(s, s ^ step) for s in range(count)])]
    pallas_call x1 -> x2, Pallas kernels: 1.27 us -> 1.9 us  [the longest x1 1.05 us: local(): pl.pallas_call(functools.partial(first_body, partners[:early]), out_shape...]
  transfers between devices with their start and end apart: 17 -> 17, of which waited for: 8 -> 8; matrix products, arithmetic and copies ran while one was open for 0% -> 0% of each run, Pallas kernels for 10% -> 13%
where the time goes in v14:
time: 41.2 us; the launch traced here: 41 us
  starting transfers between devices  22.5 us (55%)
  waiting for transfers between devices  9.21 us (22%)
  Pallas kernels  7.21 us (18%)
  between operations  2.02 us (5%)
    ppermute x17, starting transfers between devices, swapped(): return lax.ppermute(value, axis, [(s, s ^ step) for s in range(count)])  22.5 us
    ppermute x17, waiting for transfers between devices, swapped(): return lax.ppermute(value, axis, [(s, s ^ step) for s in range(count)])  9.21 us
    pallas_call x6, Pallas kernels, call(): pl.pallas_call(body, out_shape=outs, in_specs=specs, out_specs=[VMEM] * l...  5.31 us
    pallas_call x1, Pallas kernels, local(): pl.pallas_call(functools.partial(first_body, partners[:early]), out_shape...  1.05 us
    pallas_call x1, Pallas kernels, local(): pl.pallas_call(functools.partial(last_body, partners[early:]), out_shape=...  0.85 us
  transfers between devices with their start and end apart: 17, of which 8 were waited for; matrix products, arithmetic and copies ran while one was open for 0% of the time, Pallas kernels for 13%

profile of v14, /device:TPU:0, one launch (start us, length us, event | category | flops | bytes accessed | tf_op | source)
XLA Modules:
  0.0 41.0 jit_solution(9844950901633191858)
XLA Ops:
  0.6 0.5 %collective-permute-start = (f32[256,1152]{1,0:T(8,128)}, f32[256,1152]{1,0:T(8,128)S(1)}, u32[]{:S(2)}, u32[]{:S(2)}) collective-permute-start(f32[256,1152]{1,0:T(8,128)} %source.3), channel_id=1, source_target_pairs={{0,1},{1,0},{2,3},{3,2},{4,5},{5,4},{6,7},{7,6},{8,9},{9,8},{10,11... | collective-permute-start | bytes 3538952 | tf_op jit(solution)/shard_map/ppermute | solution.py:189
  1.1 1.1 %shard_map.68 = (bf16[64,1152]{1,0:T(8,128)(2,1)S(1)}, bf16[32,1152]{1,0:T(8,128)(2,1)S(1)}, bf16[32,1152]{1,0:T(8,128)(2,1)S(1)}, f32[64,1152]{1,0:T(8,128)S(1)}, f32[64,128]{1,0:T(8,128)S(1)}) custom-call(f32[64,1152]{1,0:T(8,128)} %source.2), custom_call_target="tpu_custom_call" | custom-call | flops 294912 | bytes 917504 | tf_op jit(solution)/shard_map/pallas_call | solution.py:25
  2.3 3.7 %collective-permute-start.2 = (bf16[32,1152]{1,0:T(8,128)(2,1)S(1)}, bf16[32,1152]{1,0:T(8,128)(2,1)S(1)}, u32[]{:S(2)}, u32[]{:S(2)}) collective-permute-start(bf16[32,1152]{1,0:T(8,128)(2,1)S(1)} %get-tuple-element.32), channel_id=1, source_target_pairs={{0,4},{1,5},{2,6},{3,7},{4,0},{5,1},{6,2},{7,3},{8,12},{9,13},{10,... | collective-permute-start | bytes 221192 | tf_op jit(solution)/shard_map/ppermute | solution.py:189
  5.9 1.6 %collective-permute-start.4 = (bf16[64,1152]{1,0:T(8,128)(2,1)S(1)}, bf16[64,1152]{1,0:T(8,128)(2,1)S(1)}, u32[]{:S(2)}, u32[]{:S(2)}) collective-permute-start(bf16[64,1152]{1,0:T(8,128)(2,1)S(1)} %get-tuple-element.31.refs_0_), channel_id=1, source_target_pairs={{0,2},{1,3},{2,0},{3,1},{4,6},{5,7},{6,4},{7,5},{8,10},{9,11},{10,... | collective-permute-start | bytes 442376 | tf_op jit(solution)/shard_map/ppermute | solution.py:189
  7.5 0.0 collective-permute-start.6
  7.5 1.9 %collective-permute-start.3 = (bf16[32,1152]{1,0:T(8,128)(2,1)S(1)}, bf16[32,1152]{1,0:T(8,128)(2,1)S(1)}, u32[]{:S(2)}, u32[]{:S(2)}) collective-permute-start(bf16[32,1152]{1,0:T(8,128)(2,1)S(1)} %get-tuple-element.33), channel_id=1, source_target_pairs={{0,4},{1,5},{2,6},{3,7},{4,0},{5,1},{6,2},{7,3},{8,12},{9,13},{10,... | collective-permute-start | bytes 221192 | tf_op jit(solution)/shard_map/ppermute | solution.py:189
  9.4 1.2 %collective-permute-done.2.refs_1_ = bf16[32,1152]{1,0:T(8,128)(2,1)S(1)} collective-permute-done((bf16[32,1152]{1,0:T(8,128)(2,1)S(1)}, bf16[32,1152]{1,0:T(8,128)(2,1)S(1)}, u32[]{:S(2)}, u32[]{:S(2)}) %collective-permute-start.2) | collective-permute-done | bytes 73760 | tf_op jit(solution)/shard_map/ppermute | solution.py:189
  10.6 1.3 %collective-permute-start.5 = (bf16[32,1152]{1,0:T(8,128)(2,1)S(1)}, bf16[32,1152]{1,0:T(8,128)(2,1)S(1)}, u32[]{:S(2)}, u32[]{:S(2)}) collective-permute-start(bf16[32,1152]{1,0:T(8,128)(2,1)S(1)} %collective-permute-done.2.refs_1_), channel_id=1, source_target_pairs={{0,2},{1,3},{2,0},{3,1},{4,6},{5,7},{6,4},{7,5},{8,10},{9,11},{10,... | collective-permute-start | bytes 221192 | tf_op jit(solution)/shard_map/ppermute | solution.py:189
  11.9 0.0 collective-permute-done.other
  11.9 0.0 collective-permute-start.1
  13.2 1.5 %shard_map.69 = (bf16[256,1152]{1,0:T(8,128)(2,1)S(1)}, bf16[256,1152]{1,0:T(8,128)(2,1)S(1)}, bf16[1152,256]{1,0:T(8,128)(2,1)S(1)}, f32[64,1152]{1,0:T(8,128)S(1)}, f32[64,128]{1,0:T(8,128)S(1)}) custom-call(s32[1]{0:T(128)} %bitcast.place, f32[256,1152]{1,0:T(8,128)S(1)} %collective-permute-done.other, f32[256,1152]{1,0:T(8,128)} %source.3), custom_call_target="tpu_custom_call" | custom-call | flops 2359296 | bytes 4456452 | tf_op jit(solution)/shard_map/pallas_call | solution.py:25
  14.7 0.0 copy-start
  14.7 0.0 collective-permute-done.1.perm
  14.7 0.5 %collective-permute-done.6.refs_5_ = bf16[32,1152]{1,0:T(8,128)(2,1)S(1)} collective-permute-done((bf16[32,1152]{1,0:T(8,128)(2,1)S(1)}, bf16[32,1152]{1,0:T(8,128)(2,1)S(1)}, u32[]{:S(2)}, u32[]{:S(2)}) %collective-permute-start.6) | collective-permute-done | bytes 73760 | tf_op jit(solution)/shard_map/ppermute | solution.py:189
  15.2 1.7 %collective-permute-done.3.refs_2_ = bf16[32,1152]{1,0:T(8,128)(2,1)S(1)} collective-permute-done((bf16[32,1152]{1,0:T(8,128)(2,1)S(1)}, bf16[32,1152]{1,0:T(8,128)(2,1)S(1)}, u32[]{:S(2)}, u32[]{:S(2)}) %collective-permute-start.3) | collective-permute-done | bytes 73760 | tf_op jit(solution)/shard_map/ppermute | solution.py:189
  16.9 0.2 collective-permute-done.5.refs_4_
  17.0 0.0 collective-permute-done.4.refs_3_
  17.1 1.0 %shard_map.70 = (bf16[256,256]{1,0:T(8,128)(2,1)S(1)}, bf16[256,1152]{1,0:T(8,128)(2,1)S(1)}) custom-call(s32[1]{0:T(128)} %bitcast.place, s32[1]{0:T(128)} %bitcast.1.column, f32[1]{0:T(128)S(6)} %copy.9.scale, f32[1]{0:T(128)S(6)} %copy.10.shift, s32[1,256]{1,0:T(1,128)S(1)} %collective-permute-done.1.perm, ...), custom_call_target="tpu_custom_call" | custom-call | flops 301989888 | bytes 1901584 | tf_op jit(solution)/shard_map/pallas_call | solution.py:25
  18.1 0.1 collective-permute-start.7
  18.1 0.0 copy-done
  18.1 1.4 %shard_map.71 = (f32[256,1152]{1,0:T(8,128)S(1)}, f32[256,1152]{1,0:T(8,128)S(1)}) custom-call(s32[1]{0:T(128)} %bitcast.place, s32[1]{0:T(128)} %bitcast.1.column, f32[1]{0:T(128)S(6)} %copy.9.scale, f32[1]{0:T(128)S(6)} %copy.10.shift, s32[1,256]{1,0:T(1,128)S(1)} %bitcast.4, bf16[256,1152]{1,0:T(8,128)(2,1)S(1)} %get-tuple-element.28.img, ...), custom_call_target="tpu_custom_call" | custom-call | flops 603979776 | bytes 4260880 | tf_op jit(solution)/shard_map/pallas_call | solution.py:25
  19.5 0.6 %collective-permute-done.7.other = bf16[256,1152]{1,0:T(8,128)(2,1)S(1)} collective-permute-done((bf16[256,1152]{1,0:T(8,128)(2,1)S(1)}, bf16[256,1152]{1,0:T(8,128)(2,1)S(1)}, u32[]{:S(2)}, u32[]{:S(2)}) %collective-permute-start.7) | collective-permute-done | bytes 589856 | tf_op jit(solution)/shard_map/ppermute | solution.py:189
  20.1 0.2 shard_map.72
  20.3 1.6 %collective-permute-start.8 = (bf16[64,1152]{1,0:T(8,128)(2,1)S(1)}, bf16[64,1152]{1,0:T(8,128)(2,1)S(1)}, u32[]{:S(2)}, u32[]{:S(2)}) collective-permute-start(bf16[64,1152]{1,0:T(8,128)(2,1)S(1)} %get-tuple-element.42), channel_id=1, source_target_pairs={{0,8},{8,0},{16,24},{24,16},{1,9},{9,1},{17,25},{25,17},{2,10},{10... | collective-permute-start | bytes 442376 | tf_op jit(solution)/shard_map/ppermute | solution.py:189
  21.9 1.5 %collective-permute-start.9 = (bf16[64,1152]{1,0:T(8,128)(2,1)S(1)}, bf16[64,1152]{1,0:T(8,128)(2,1)S(1)}, u32[]{:S(2)}, u32[]{:S(2)}) collective-permute-start(bf16[64,1152]{1,0:T(8,128)(2,1)S(1)} %get-tuple-element.43), channel_id=1, source_target_pairs={{0,16},{8,24},{16,0},{24,8},{1,17},{9,25},{17,1},{25,9},{2,18},{10... | collective-permute-start | bytes 442376 | tf_op jit(solution)/shard_map/ppermute | solution.py:189
  23.4 0.4 %collective-permute-start.10 = (bf16[64,1152]{1,0:T(8,128)(2,1)S(1)}, bf16[64,1152]{1,0:T(8,128)(2,1)S(1)}, u32[]{:S(2)}, u32[]{:S(2)}) collective-permute-start(bf16[64,1152]{1,0:T(8,128)(2,1)S(1)} %get-tuple-element.44), channel_id=1, source_target_pairs={{0,24},{8,16},{16,8},{24,0},{1,25},{9,17},{17,9},{25,1},{2,26},{10... | collective-permute-start | bytes 442376 | tf_op jit(solution)/shard_map/ppermute | solution.py:189
  23.8 1.5 %collective-permute-start.12 = (bf16[64,1152]{1,0:T(8,128)(2,1)S(1)}, bf16[64,1152]{1,0:T(8,128)(2,1)S(1)}, u32[]{:S(2)}, u32[]{:S(2)}) collective-permute-start(bf16[64,1152]{1,0:T(8,128)(2,1)S(1)} %get-tuple-element.45), channel_id=1, source_target_pairs={{0,2},{1,3},{2,0},{3,1},{4,6},{5,7},{6,4},{7,5},{8,10},{9,11},{10,... | collective-permute-start | bytes 442376 | tf_op jit(solution)/shard_map/ppermute | solution.py:189
  25.3 2.4 %collective-permute-start.13 = (bf16[64,1152]{1,0:T(8,128)(2,1)S(1)}, bf16[64,1152]{1,0:T(8,128)(2,1)S(1)}, u32[]{:S(2)}, u32[]{:S(2)}) collective-permute-start(bf16[64,1152]{1,0:T(8,128)(2,1)S(1)} %get-tuple-element.46), channel_id=1, source_target_pairs={{0,4},{1,5},{2,6},{3,7},{4,0},{5,1},{6,2},{7,3},{8,12},{9,13},{10,... | collective-permute-start | bytes 442376 | tf_op jit(solution)/shard_map/ppermute | solution.py:189
  27.7 0.0 collective-permute-done.8.refs_0_
  27.7 2.5 %collective-permute-start.14 = (bf16[64,1152]{1,0:T(8,128)(2,1)S(1)}, bf16[64,1152]{1,0:T(8,128)(2,1)S(1)}, u32[]{:S(2)}, u32[]{:S(2)}) collective-permute-start(bf16[64,1152]{1,0:T(8,128)(2,1)S(1)} %get-tuple-element.47), channel_id=1, source_target_pairs={{0,6},{1,7},{2,4},{3,5},{4,2},{5,3},{6,0},{7,1},{8,14},{9,15},{10,... | collective-permute-start | bytes 442376 | tf_op jit(solution)/shard_map/ppermute | solution.py:189
  30.2 0.4 %collective-permute-done.9.refs_1_ = bf16[64,1152]{1,0:T(8,128)(2,1)S(1)} collective-permute-done((bf16[64,1152]{1,0:T(8,128)(2,1)S(1)}, bf16[64,1152]{1,0:T(8,128)(2,1)S(1)}, u32[]{:S(2)}, u32[]{:S(2)}) %collective-permute-start.9) | collective-permute-done | bytes 147488 | tf_op jit(solution)/shard_map/ppermute | solution.py:189
  30.7 0.0 collective-permute-done.10.refs_2_
  30.7 0.2 shard_map.73.refs_0_
  30.9 1.3 %collective-permute-start.11 = (bf16[64,1152]{1,0:T(8,128)(2,1)S(1)}, bf16[64,1152]{1,0:T(8,128)(2,1)S(1)}, u32[]{:S(2)}, u32[]{:S(2)}) collective-permute-start(bf16[64,1152]{1,0:T(8,128)(2,1)S(1)} %shard_map.73.refs_0_), channel_id=1, source_target_pairs={{0,8},{8,0},{16,24},{24,16},{1,9},{9,1},{17,25},{25,17},{2,10},{10... | collective-permute-start | bytes 442376 | tf_op jit(solution)/shard_map/ppermute | solution.py:189
  32.2 1.5 %collective-permute-start.16 = (bf16[64,1152]{1,0:T(8,128)(2,1)S(1)}, bf16[64,1152]{1,0:T(8,128)(2,1)S(1)}, u32[]{:S(2)}, u32[]{:S(2)}) collective-permute-start(bf16[64,1152]{1,0:T(8,128)(2,1)S(1)} %shard_map.73.refs_0_), channel_id=1, source_target_pairs={{0,16},{8,24},{16,0},{24,8},{1,17},{9,25},{17,1},{25,9},{2,18},{10... | collective-permute-start | bytes 442376 | tf_op jit(solution)/shard_map/ppermute | solution.py:189
  33.6 0.0 collective-permute-done.12.refs_2_
  33.6 0.8 %collective-permute-start.15 = (bf16[64,1152]{1,0:T(8,128)(2,1)S(1)}, bf16[64,1152]{1,0:T(8,128)(2,1)S(1)}, u32[]{:S(2)}, u32[]{:S(2)}) collective-permute-start(bf16[64,1152]{1,0:T(8,128)(2,1)S(1)} %shard_map.73.refs_0_), channel_id=1, source_target_pairs={{0,24},{8,16},{16,8},{24,0},{1,25},{9,17},{17,9},{25,1},{2,26},{10... | collective-permute-start | bytes 442376 | tf_op jit(solution)/shard_map/ppermute | solution.py:189
  34.4 4.5 %collective-permute-done.13.refs_3_ = bf16[64,1152]{1,0:T(8,128)(2,1)S(1)} collective-permute-done((bf16[64,1152]{1,0:T(8,128)(2,1)S(1)}, bf16[64,1152]{1,0:T(8,128)(2,1)S(1)}, u32[]{:S(2)}, u32[]{:S(2)}) %collective-permute-start.13) | collective-permute-done | bytes 147488 | tf_op jit(solution)/shard_map/ppermute | solution.py:189
  38.9 0.0 collective-permute-done.14.refs_4_
  38.9 0.0 collective-permute-done.11.refs_1_
  38.9 1.0 %shard_map.74 = (f32[256,1152]{1,0:T(8,128)}, f32[64,1152]{1,0:T(8,128)}) custom-call(s32[1]{0:T(128)} %bitcast.place, f32[1]{0:T(128)S(6)} %copy.9.scale, f32[64,1152]{1,0:T(8,128)S(1)} %get-tuple-element.26.unit, f32[64,128]{1,0:T(8,128)S(1)} %get-tuple-element.27.inverse, f32[64,1152]{1,0:T(8,128)S(1)} %get-tuple-element.38.own, ...), custom_call_target="tpu_custom_call" | custom-call | flops 737280 | bytes 2359296 | tf_op jit(solution)/shard_map/pallas_call | solution.py:279
  40.0 0.1 collective-permute-done.16.refs_1_
  40.1 0.0 collective-permute-done.15.refs_0_
  40.1 0.8 %shard_map.75 = f32[256,1152]{1,0:T(8,128)} custom-call(s32[1]{0:T(128)} %bitcast.place, f32[256,1152]{1,0:T(8,128)} %get-tuple-element.48.begun, bf16[64,1152]{1,0:T(8,128)(2,1)S(1)} %collective-permute-done.15.refs_0_, bf16[64,1152]{1,0:T(8,128)(2,1)S(1)} %collective-permute-done.16.refs_1_), custom_call_target="tpu_custom_call", output_to_operand_aliasing={{}: (1, {})} | custom-call | flops 294912 | bytes 2359296 | tf_op jit(solution)/shard_map/pallas_call | solution.py:294
Async XLA Ops:
  0.6 11.3 %collective-permute-start = (f32[256,1152]{1,0:T(8,128)}, f32[256,1152]{1,0:T(8,128)S(1)}, u32[]{:S(2)}, u32[]{:S(2)}) collective-permute-start(f32[256,1152]{1,0:T(8,128)} %source.3), channel_id=1, source_target_pairs={{0,1},{1,0},{2,3},{3,2},{4,5},{5,4},{6,7},{7,6},{8,9},{9,8},{10,11... | collective-permute-start | bytes 3538952 | tf_op jit(solution)/shard_map/ppermute | solution.py:189
  2.3 8.4 %collective-permute-start.2 = (bf16[32,1152]{1,0:T(8,128)(2,1)S(1)}, bf16[32,1152]{1,0:T(8,128)(2,1)S(1)}, u32[]{:S(2)}, u32[]{:S(2)}) collective-permute-start(bf16[32,1152]{1,0:T(8,128)(2,1)S(1)} %get-tuple-element.32), channel_id=1, source_target_pairs={{0,4},{1,5},{2,6},{3,7},{4,0},{5,1},{6,2},{7,3},{8,12},{9,13},{10,... | collective-permute-start | bytes 221192 | tf_op jit(solution)/shard_map/ppermute | solution.py:189
  5.9 11.1 %collective-permute-start.4 = (bf16[64,1152]{1,0:T(8,128)(2,1)S(1)}, bf16[64,1152]{1,0:T(8,128)(2,1)S(1)}, u32[]{:S(2)}, u32[]{:S(2)}) collective-permute-start(bf16[64,1152]{1,0:T(8,128)(2,1)S(1)} %get-tuple-element.31.refs_0_), channel_id=1, source_target_pairs={{0,2},{1,3},{2,0},{3,1},{4,6},{5,7},{6,4},{7,5},{8,10},{9,11},{10,... | collective-permute-start | bytes 442376 | tf_op jit(solution)/shard_map/ppermute | solution.py:189
  7.5 7.7 %collective-permute-start.6 = (bf16[32,1152]{1,0:T(8,128)(2,1)S(1)}, bf16[32,1152]{1,0:T(8,128)(2,1)S(1)}, u32[]{:S(2)}, u32[]{:S(2)}) collective-permute-start(bf16[32,1152]{1,0:T(8,128)(2,1)S(1)} %get-tuple-element.33), channel_id=1, source_target_pairs={{0,6},{1,7},{2,4},{3,5},{4,2},{5,3},{6,0},{7,1},{8,14},{9,15},{10,... | collective-permute-start | bytes 221192 | tf_op jit(solution)/shard_map/ppermute | solution.py:189
  7.5 9.4 %collective-permute-start.3 = (bf16[32,1152]{1,0:T(8,128)(2,1)S(1)}, bf16[32,1152]{1,0:T(8,128)(2,1)S(1)}, u32[]{:S(2)}, u32[]{:S(2)}) collective-permute-start(bf16[32,1152]{1,0:T(8,128)(2,1)S(1)} %get-tuple-element.33), channel_id=1, source_target_pairs={{0,4},{1,5},{2,6},{3,7},{4,0},{5,1},{6,2},{7,3},{8,12},{9,13},{10,... | collective-permute-start | bytes 221192 | tf_op jit(solution)/shard_map/ppermute | solution.py:189
  10.6 6.4 %collective-permute-start.5 = (bf16[32,1152]{1,0:T(8,128)(2,1)S(1)}, bf16[32,1152]{1,0:T(8,128)(2,1)S(1)}, u32[]{:S(2)}, u32[]{:S(2)}) collective-permute-start(bf16[32,1152]{1,0:T(8,128)(2,1)S(1)} %collective-permute-done.2.refs_1_), channel_id=1, source_target_pairs={{0,2},{1,3},{2,0},{3,1},{4,6},{5,7},{6,4},{7,5},{8,10},{9,11},{10,... | collective-permute-start | bytes 221192 | tf_op jit(solution)/shard_map/ppermute | solution.py:189
  11.9 2.8 %collective-permute-start.1 = (s32[1,256]{1,0:T(1,128)}, s32[1,256]{1,0:T(1,128)S(1)}, u32[]{:S(2)}, u32[]{:S(2)}) collective-permute-start(s32[1,256]{1,0:T(1,128)} %bitcast.3), channel_id=1, source_target_pairs={{0,1},{1,0},{2,3},{3,2},{4,5},{5,4},{6,7},{7,6},{8,9},{9,8},{10,11... | collective-permute-start | bytes 3080 | tf_op jit(solution)/shard_map/ppermute | solution.py:189
  14.7 3.4 %copy-start = (s32[256]{0:T(256)S(1)}, s32[256]{0:T(256)}, u32[]{:S(2)}) copy-start(s32[256]{0:T(256)} %param.7) | copy-start | bytes 3076
  18.1 2.1 %collective-permute-start.7 = (bf16[256,1152]{1,0:T(8,128)(2,1)S(1)}, bf16[256,1152]{1,0:T(8,128)(2,1)S(1)}, u32[]{:S(2)}, u32[]{:S(2)}) collective-permute-start(bf16[256,1152]{1,0:T(8,128)(2,1)S(1)} %get-tuple-element.36), channel_id=1, source_target_pairs={{0,1},{1,0},{2,3},{3,2},{4,5},{5,4},{6,7},{7,6},{8,9},{9,8},{10,11... | collective-permute-start | bytes 1769480 | tf_op jit(solution)/shard_map/ppermute | solution.py:189
  20.3 7.4 %collective-permute-start.8 = (bf16[64,1152]{1,0:T(8,128)(2,1)S(1)}, bf16[64,1152]{1,0:T(8,128)(2,1)S(1)}, u32[]{:S(2)}, u32[]{:S(2)}) collective-permute-start(bf16[64,1152]{1,0:T(8,128)(2,1)S(1)} %get-tuple-element.42), channel_id=1, source_target_pairs={{0,8},{8,0},{16,24},{24,16},{1,9},{9,1},{17,25},{25,17},{2,10},{10... | collective-permute-start | bytes 442376 | tf_op jit(solution)/shard_map/ppermute | solution.py:189
  21.9 8.8 %collective-permute-start.9 = (bf16[64,1152]{1,0:T(8,128)(2,1)S(1)}, bf16[64,1152]{1,0:T(8,128)(2,1)S(1)}, u32[]{:S(2)}, u32[]{:S(2)}) collective-permute-start(bf16[64,1152]{1,0:T(8,128)(2,1)S(1)} %get-tuple-element.43), channel_id=1, source_target_pairs={{0,16},{8,24},{16,0},{24,8},{1,17},{9,25},{17,1},{25,9},{2,18},{10... | collective-permute-start | bytes 442376 | tf_op jit(solution)/shard_map/ppermute | solution.py:189
  23.4 7.3 %collective-permute-start.10 = (bf16[64,1152]{1,0:T(8,128)(2,1)S(1)}, bf16[64,1152]{1,0:T(8,128)(2,1)S(1)}, u32[]{:S(2)}, u32[]{:S(2)}) collective-permute-start(bf16[64,1152]{1,0:T(8,128)(2,1)S(1)} %get-tuple-element.44), channel_id=1, source_target_pairs={{0,24},{8,16},{16,8},{24,0},{1,25},{9,17},{17,9},{25,1},{2,26},{10... | collective-permute-start | bytes 442376 | tf_op jit(solution)/shard_map/ppermute | solution.py:189
  23.8 9.8 %collective-permute-start.12 = (bf16[64,1152]{1,0:T(8,128)(2,1)S(1)}, bf16[64,1152]{1,0:T(8,128)(2,1)S(1)}, u32[]{:S(2)}, u32[]{:S(2)}) collective-permute-start(bf16[64,1152]{1,0:T(8,128)(2,1)S(1)} %get-tuple-element.45), channel_id=1, source_target_pairs={{0,2},{1,3},{2,0},{3,1},{4,6},{5,7},{6,4},{7,5},{8,10},{9,11},{10,... | collective-permute-start | bytes 442376 | tf_op jit(solution)/shard_map/ppermute | solution.py:189
  25.3 13.6 %collective-permute-start.13 = (bf16[64,1152]{1,0:T(8,128)(2,1)S(1)}, bf16[64,1152]{1,0:T(8,128)(2,1)S(1)}, u32[]{:S(2)}, u32[]{:S(2)}) collective-permute-start(bf16[64,1152]{1,0:T(8,128)(2,1)S(1)} %get-tuple-element.46), channel_id=1, source_target_pairs={{0,4},{1,5},{2,6},{3,7},{4,0},{5,1},{6,2},{7,3},{8,12},{9,13},{10,... | collective-permute-start | bytes 442376 | tf_op jit(solution)/shard_map/ppermute | solution.py:189
  27.7 11.2 %collective-permute-start.14 = (bf16[64,1152]{1,0:T(8,128)(2,1)S(1)}, bf16[64,1152]{1,0:T(8,128)(2,1)S(1)}, u32[]{:S(2)}, u32[]{:S(2)}) collective-permute-start(bf16[64,1152]{1,0:T(8,128)(2,1)S(1)} %get-tuple-element.47), channel_id=1, source_target_pairs={{0,6},{1,7},{2,4},{3,5},{4,2},{5,3},{6,0},{7,1},{8,14},{9,15},{10,... | collective-permute-start | bytes 442376 | tf_op jit(solution)/shard_map/ppermute | solution.py:189
  30.9 8.1 %collective-permute-start.11 = (bf16[64,1152]{1,0:T(8,128)(2,1)S(1)}, bf16[64,1152]{1,0:T(8,128)(2,1)S(1)}, u32[]{:S(2)}, u32[]{:S(2)}) collective-permute-start(bf16[64,1152]{1,0:T(8,128)(2,1)S(1)} %shard_map.73.refs_0_), channel_id=1, source_target_pairs={{0,8},{8,0},{16,24},{24,16},{1,9},{9,1},{17,25},{25,17},{2,10},{10... | collective-permute-start | bytes 442376 | tf_op jit(solution)/shard_map/ppermute | solution.py:189
  32.2 7.9 %collective-permute-start.16 = (bf16[64,1152]{1,0:T(8,128)(2,1)S(1)}, bf16[64,1152]{1,0:T(8,128)(2,1)S(1)}, u32[]{:S(2)}, u32[]{:S(2)}) collective-permute-start(bf16[64,1152]{1,0:T(8,128)(2,1)S(1)} %shard_map.73.refs_0_), channel_id=1, source_target_pairs={{0,16},{8,24},{16,0},{24,8},{1,17},{9,25},{17,1},{25,9},{2,18},{10... | collective-permute-start | bytes 442376 | tf_op jit(solution)/shard_map/ppermute | solution.py:189
  33.6 6.5 %collective-permute-start.15 = (bf16[64,1152]{1,0:T(8,128)(2,1)S(1)}, bf16[64,1152]{1,0:T(8,128)(2,1)S(1)}, u32[]{:S(2)}, u32[]{:S(2)}) collective-permute-start(bf16[64,1152]{1,0:T(8,128)(2,1)S(1)} %shard_map.73.refs_0_), channel_id=1, source_target_pairs={{0,24},{8,16},{16,8},{24,0},{1,25},{9,17},{17,9},{25,1},{2,26},{10... | collective-permute-start | bytes 442376 | tf_op jit(solution)/shard_map/ppermute | solution.py:189

commit v15 on v14

--- a/solution.py
+++ b/solution.py
@@ -98,17 +98,17 @@
     return jnp.concatenate([t[...] for t in tiles], axis=0)
 
 
-def other_body(order, line, place, column, scale, shift, perm, turned, *refs):
+def other_body(slots, order, line, place, column, scale, shift, perm, turned, *refs):
     *txt, kept, out = refs
-    tile = joined(txt)
+    tile = joined([txt[k] for k in slots])
     weights = weights_of(tile, order, line, place, column, scale, shift, perm[...], turned[...], 0)
     kept[...] = weights
     out[...] = to_images(weights, tile).astype(BF16)
 
 
-def own_body(order, line, place, column, scale, shift, perm, img, img_other, kept, *refs):
+def own_body(slots, order, line, place, column, scale, shift, perm, img, img_other, kept, *refs):
     *txt, own_sum, txt_sums = refs
-    tile = joined(txt)
+    tile = joined([txt[k] for k in slots])
     weights = weights_of(tile, order, line, place, column, scale, shift, perm[...], img[...])
     own_sum[...] = to_images(weights, tile)
     txt_sums[...] = to_texts(weights, img[...]) + to_texts(kept[...], img_other[...])
@@ -219,7 +219,10 @@
     near = [swapped(txt_bf, "txt", 2)]
     for k in range(1, half):
         near += [swapped(far[2 * k - 2], "txt", 2), swapped(tail, "txt", 4 * k + 2)]
-    tiles = [txt_bf] + far + near
+    ranks = [0, *(1, 5) * (half - 1), 2, *(3, 4) * (half - 1)]
+    stand = sorted(range(len(ranks)), key=lambda k: ranks[k])
+    tiles = [([txt_bf] + far + near)[k] for k in stand]
+    slots = [stand.index(k) for k in range(len(stand))]
     img_bf, img_other, turned_other, img_unit, img_inv = call(
         unit_img_body,
         [struct(rows, width, BF16)] * 2
@@ -233,7 +236,7 @@
     scalars = [place, column, scale, shift]
     pairs = 2 * rows * blocks * txt_rows * width
     kept, other_img = call(
-        functools.partial(other_body, order, line),
+        functools.partial(other_body, slots, order, line),
         [struct(blocks * txt_rows, rows, BF16), struct(rows, width, BF16)],
         [*scalars, perm_other, turned_other, *tiles],
         [SMEM] * 4 + [VMEM] * (2 + len(tiles)),
@@ -242,7 +245,7 @@
     )
     from_other = swapped(other_img, "txt", 1)
     own_img, txt_sums = call(
-        functools.partial(own_body, order, line),
+        functools.partial(own_body, slots, order, line),
         [struct(rows, width, F32), struct(blocks * txt_rows, width, F32)],
         [*scalars, perm_row, img_bf, img_other, kept, *tiles],
         [SMEM] * 4 + [VMEM] * (4 + len(tiles)),

time: 41.2 us -> 41.2 us (level)
  no operation moved by 1% of the time
where the time goes in v15:
time: 41.2 us; the launch traced here: 41 us
  starting transfers between devices  22.3 us (54%)
  waiting for transfers between devices  9.38 us (23%)
  Pallas kernels  7.21 us (18%)
  between operations  2.02 us (5%)
    ppermute x17, starting transfers between devices, swapped(): return lax.ppermute(value, axis, [(s, s ^ step) for s in range(count)])  22.3 us
    ppermute x17, waiting for transfers between devices, swapped(): return lax.ppermute(value, axis, [(s, s ^ step) for s in range(count)])  9.38 us
    pallas_call x6, Pallas kernels, call(): pl.pallas_call(body, out_shape=outs, in_specs=specs, out_specs=[VMEM] * l...  5.31 us
    pallas_call x1, Pallas kernels, local(): pl.pallas_call(functools.partial(first_body, partners[:early]), out_shape...  1.05 us
    pallas_call x1, Pallas kernels, local(): pl.pallas_call(functools.partial(last_body, partners[early:]), out_shape=...  0.85 us
  transfers between devices with their start and end apart: 17, of which 8 were waited for; matrix products, arithmetic and copies ran while one was open for 0% of the time, Pallas kernels for 13%

profile of v15, /device:TPU:0, one launch (start us, length us, event | category | flops | bytes accessed | tf_op | source)
XLA Modules:
  0.0 41.0 jit_solution(2532118056847117273)
XLA Ops:
  0.6 0.5 %collective-permute-start = (f32[256,1152]{1,0:T(8,128)}, f32[256,1152]{1,0:T(8,128)S(1)}, u32[]{:S(2)}, u32[]{:S(2)}) collective-permute-start(f32[256,1152]{1,0:T(8,128)} %source.3), channel_id=1, source_target_pairs={{0,1},{1,0},{2,3},{3,2},{4,5},{5,4},{6,7},{7,6},{8,9},{9,8},{10,11... | collective-permute-start | bytes 3538952 | tf_op jit(solution)/shard_map/ppermute | solution.py:189
  1.1 1.1 %shard_map.68 = (bf16[64,1152]{1,0:T(8,128)(2,1)S(1)}, bf16[32,1152]{1,0:T(8,128)(2,1)S(1)}, bf16[32,1152]{1,0:T(8,128)(2,1)S(1)}, f32[64,1152]{1,0:T(8,128)S(1)}, f32[64,128]{1,0:T(8,128)S(1)}) custom-call(f32[64,1152]{1,0:T(8,128)} %source.2), custom_call_target="tpu_custom_call" | custom-call | flops 294912 | bytes 917504 | tf_op jit(solution)/shard_map/pallas_call | solution.py:25
  2.3 3.7 %collective-permute-start.2 = (bf16[32,1152]{1,0:T(8,128)(2,1)S(1)}, bf16[32,1152]{1,0:T(8,128)(2,1)S(1)}, u32[]{:S(2)}, u32[]{:S(2)}) collective-permute-start(bf16[32,1152]{1,0:T(8,128)(2,1)S(1)} %get-tuple-element.32), channel_id=1, source_target_pairs={{0,4},{1,5},{2,6},{3,7},{4,0},{5,1},{6,2},{7,3},{8,12},{9,13},{10,... | collective-permute-start | bytes 221192 | tf_op jit(solution)/shard_map/ppermute | solution.py:189
  5.9 1.6 %collective-permute-start.3 = (bf16[64,1152]{1,0:T(8,128)(2,1)S(1)}, bf16[64,1152]{1,0:T(8,128)(2,1)S(1)}, u32[]{:S(2)}, u32[]{:S(2)}) collective-permute-start(bf16[64,1152]{1,0:T(8,128)(2,1)S(1)} %get-tuple-element.31.refs_0_), channel_id=1, source_target_pairs={{0,2},{1,3},{2,0},{3,1},{4,6},{5,7},{6,4},{7,5},{8,10},{9,11},{10,... | collective-permute-start | bytes 442376 | tf_op jit(solution)/shard_map/ppermute | solution.py:189
  7.5 0.3 collective-permute-start.6
  7.8 2.5 %collective-permute-start.5 = (bf16[32,1152]{1,0:T(8,128)(2,1)S(1)}, bf16[32,1152]{1,0:T(8,128)(2,1)S(1)}, u32[]{:S(2)}, u32[]{:S(2)}) collective-permute-start(bf16[32,1152]{1,0:T(8,128)(2,1)S(1)} %get-tuple-element.33), channel_id=1, source_target_pairs={{0,6},{1,7},{2,4},{3,5},{4,2},{5,3},{6,0},{7,1},{8,14},{9,15},{10,... | collective-permute-start | bytes 221192 | tf_op jit(solution)/shard_map/ppermute | solution.py:189
  10.3 0.2 collective-permute-done.2.refs_1_
  10.5 0.7 %collective-permute-start.4 = (bf16[32,1152]{1,0:T(8,128)(2,1)S(1)}, bf16[32,1152]{1,0:T(8,128)(2,1)S(1)}, u32[]{:S(2)}, u32[]{:S(2)}) collective-permute-start(bf16[32,1152]{1,0:T(8,128)(2,1)S(1)} %collective-permute-done.2.refs_1_), channel_id=1, source_target_pairs={{0,2},{1,3},{2,0},{3,1},{4,6},{5,7},{6,4},{7,5},{8,10},{9,11},{10,... | collective-permute-start | bytes 221192 | tf_op jit(solution)/shard_map/ppermute | solution.py:189
  11.2 0.0 collective-permute-done.other
  11.2 0.0 collective-permute-start.1
  12.5 1.5 %shard_map.69 = (bf16[256,1152]{1,0:T(8,128)(2,1)S(1)}, bf16[256,1152]{1,0:T(8,128)(2,1)S(1)}, bf16[1152,256]{1,0:T(8,128)(2,1)S(1)}, f32[64,1152]{1,0:T(8,128)S(1)}, f32[64,128]{1,0:T(8,128)S(1)}) custom-call(s32[1]{0:T(128)} %bitcast.place, f32[256,1152]{1,0:T(8,128)S(1)} %collective-permute-done.other, f32[256,1152]{1,0:T(8,128)} %source.3), custom_call_target="tpu_custom_call" | custom-call | flops 2359296 | bytes 4456452 | tf_op jit(solution)/shard_map/pallas_call | solution.py:25
  14.0 0.0 copy-start
  14.0 0.0 collective-permute-done.1.perm
  14.1 2.3 %collective-permute-done.6.refs_5_ = bf16[32,1152]{1,0:T(8,128)(2,1)S(1)} collective-permute-done((bf16[32,1152]{1,0:T(8,128)(2,1)S(1)}, bf16[32,1152]{1,0:T(8,128)(2,1)S(1)}, u32[]{:S(2)}, u32[]{:S(2)}) %collective-permute-start.6) | collective-permute-done | bytes 73760 | tf_op jit(solution)/shard_map/ppermute | solution.py:189
  16.3 0.4 collective-permute-done.5.refs_4_
  16.7 0.3 collective-permute-done.4.refs_3_
  17.0 0.0 collective-permute-done.3.refs_2_
  17.1 1.0 %shard_map.70 = (bf16[256,256]{1,0:T(8,128)(2,1)S(1)}, bf16[256,1152]{1,0:T(8,128)(2,1)S(1)}) custom-call(s32[1]{0:T(128)} %bitcast.place, s32[1]{0:T(128)} %bitcast.1.column, f32[1]{0:T(128)S(6)} %copy.9.scale, f32[1]{0:T(128)S(6)} %copy.10.shift, s32[1,256]{1,0:T(1,128)S(1)} %collective-permute-done.1.perm, ...), custom_call_target="tpu_custom_call" | custom-call | flops 301989888 | bytes 1901584 | tf_op jit(solution)/shard_map/pallas_call | solution.py:25
  18.1 0.1 collective-permute-start.7
  18.1 0.0 copy-done
  18.1 1.4 %shard_map.71 = (f32[256,1152]{1,0:T(8,128)S(1)}, f32[256,1152]{1,0:T(8,128)S(1)}) custom-call(s32[1]{0:T(128)} %bitcast.place, s32[1]{0:T(128)} %bitcast.1.column, f32[1]{0:T(128)S(6)} %copy.9.scale, f32[1]{0:T(128)S(6)} %copy.10.shift, s32[1,256]{1,0:T(1,128)S(1)} %bitcast.4, bf16[256,1152]{1,0:T(8,128)(2,1)S(1)} %get-tuple-element.28.img, ...), custom_call_target="tpu_custom_call" | custom-call | flops 603979776 | bytes 4260880 | tf_op jit(solution)/shard_map/pallas_call | solution.py:25
  19.5 0.6 %collective-permute-done.7.other = bf16[256,1152]{1,0:T(8,128)(2,1)S(1)} collective-permute-done((bf16[256,1152]{1,0:T(8,128)(2,1)S(1)}, bf16[256,1152]{1,0:T(8,128)(2,1)S(1)}, u32[]{:S(2)}, u32[]{:S(2)}) %collective-permute-start.7) | collective-permute-done | bytes 589856 | tf_op jit(solution)/shard_map/ppermute | solution.py:189
  20.1 0.2 shard_map.72
  20.3 1.6 %collective-permute-start.8 = (bf16[64,1152]{1,0:T(8,128)(2,1)S(1)}, bf16[64,1152]{1,0:T(8,128)(2,1)S(1)}, u32[]{:S(2)}, u32[]{:S(2)}) collective-permute-start(bf16[64,1152]{1,0:T(8,128)(2,1)S(1)} %get-tuple-element.42), channel_id=1, source_target_pairs={{0,8},{8,0},{16,24},{24,16},{1,9},{9,1},{17,25},{25,17},{2,10},{10... | collective-permute-start | bytes 442376 | tf_op jit(solution)/shard_map/ppermute | solution.py:189
  21.9 1.5 %collective-permute-start.9 = (bf16[64,1152]{1,0:T(8,128)(2,1)S(1)}, bf16[64,1152]{1,0:T(8,128)(2,1)S(1)}, u32[]{:S(2)}, u32[]{:S(2)}) collective-permute-start(bf16[64,1152]{1,0:T(8,128)(2,1)S(1)} %get-tuple-element.43), channel_id=1, source_target_pairs={{0,16},{8,24},{16,0},{24,8},{1,17},{9,25},{17,1},{25,9},{2,18},{10... | collective-permute-start | bytes 442376 | tf_op jit(solution)/shard_map/ppermute | solution.py:189
  23.4 0.4 %collective-permute-start.10 = (bf16[64,1152]{1,0:T(8,128)(2,1)S(1)}, bf16[64,1152]{1,0:T(8,128)(2,1)S(1)}, u32[]{:S(2)}, u32[]{:S(2)}) collective-permute-start(bf16[64,1152]{1,0:T(8,128)(2,1)S(1)} %get-tuple-element.44), channel_id=1, source_target_pairs={{0,24},{8,16},{16,8},{24,0},{1,25},{9,17},{17,9},{25,1},{2,26},{10... | collective-permute-start | bytes 442376 | tf_op jit(solution)/shard_map/ppermute | solution.py:189
  23.8 1.5 %collective-permute-start.12 = (bf16[64,1152]{1,0:T(8,128)(2,1)S(1)}, bf16[64,1152]{1,0:T(8,128)(2,1)S(1)}, u32[]{:S(2)}, u32[]{:S(2)}) collective-permute-start(bf16[64,1152]{1,0:T(8,128)(2,1)S(1)} %get-tuple-element.45), channel_id=1, source_target_pairs={{0,2},{1,3},{2,0},{3,1},{4,6},{5,7},{6,4},{7,5},{8,10},{9,11},{10,... | collective-permute-start | bytes 442376 | tf_op jit(solution)/shard_map/ppermute | solution.py:189
  25.3 1.9 %collective-permute-start.13 = (bf16[64,1152]{1,0:T(8,128)(2,1)S(1)}, bf16[64,1152]{1,0:T(8,128)(2,1)S(1)}, u32[]{:S(2)}, u32[]{:S(2)}) collective-permute-start(bf16[64,1152]{1,0:T(8,128)(2,1)S(1)} %get-tuple-element.46), channel_id=1, source_target_pairs={{0,4},{1,5},{2,6},{3,7},{4,0},{5,1},{6,2},{7,3},{8,12},{9,13},{10,... | collective-permute-start | bytes 442376 | tf_op jit(solution)/shard_map/ppermute | solution.py:189
  27.2 0.0 collective-permute-done.8.refs_0_
  27.2 2.5 %collective-permute-start.14 = (bf16[64,1152]{1,0:T(8,128)(2,1)S(1)}, bf16[64,1152]{1,0:T(8,128)(2,1)S(1)}, u32[]{:S(2)}, u32[]{:S(2)}) collective-permute-start(bf16[64,1152]{1,0:T(8,128)(2,1)S(1)} %get-tuple-element.47), channel_id=1, source_target_pairs={{0,6},{1,7},{2,4},{3,5},{4,2},{5,3},{6,0},{7,1},{8,14},{9,15},{10,... | collective-permute-start | bytes 442376 | tf_op jit(solution)/shard_map/ppermute | solution.py:189
  29.7 0.9 %collective-permute-done.9.refs_1_ = bf16[64,1152]{1,0:T(8,128)(2,1)S(1)} collective-permute-done((bf16[64,1152]{1,0:T(8,128)(2,1)S(1)}, bf16[64,1152]{1,0:T(8,128)(2,1)S(1)}, u32[]{:S(2)}, u32[]{:S(2)}) %collective-permute-start.9) | collective-permute-done | bytes 147488 | tf_op jit(solution)/shard_map/ppermute | solution.py:189
  30.7 0.0 collective-permute-done.10.refs_2_
  30.7 0.2 shard_map.73.refs_0_
  30.9 1.3 %collective-permute-start.11 = (bf16[64,1152]{1,0:T(8,128)(2,1)S(1)}, bf16[64,1152]{1,0:T(8,128)(2,1)S(1)}, u32[]{:S(2)}, u32[]{:S(2)}) collective-permute-start(bf16[64,1152]{1,0:T(8,128)(2,1)S(1)} %shard_map.73.refs_0_), channel_id=1, source_target_pairs={{0,8},{8,0},{16,24},{24,16},{1,9},{9,1},{17,25},{25,17},{2,10},{10... | collective-permute-start | bytes 442376 | tf_op jit(solution)/shard_map/ppermute | solution.py:189
  32.2 1.0 %collective-permute-start.16 = (bf16[64,1152]{1,0:T(8,128)(2,1)S(1)}, bf16[64,1152]{1,0:T(8,128)(2,1)S(1)}, u32[]{:S(2)}, u32[]{:S(2)}) collective-permute-start(bf16[64,1152]{1,0:T(8,128)(2,1)S(1)} %shard_map.73.refs_0_), channel_id=1, source_target_pairs={{0,16},{8,24},{16,0},{24,8},{1,17},{9,25},{17,1},{25,9},{2,18},{10... | collective-permute-start | bytes 442376 | tf_op jit(solution)/shard_map/ppermute | solution.py:189
  33.1 0.0 collective-permute-done.12.refs_2_
  33.1 1.3 %collective-permute-start.15 = (bf16[64,1152]{1,0:T(8,128)(2,1)S(1)}, bf16[64,1152]{1,0:T(8,128)(2,1)S(1)}, u32[]{:S(2)}, u32[]{:S(2)}) collective-permute-start(bf16[64,1152]{1,0:T(8,128)(2,1)S(1)} %shard_map.73.refs_0_), channel_id=1, source_target_pairs={{0,24},{8,16},{16,8},{24,0},{1,25},{9,17},{17,9},{25,1},{2,26},{10... | collective-permute-start | bytes 442376 | tf_op jit(solution)/shard_map/ppermute | solution.py:189
  34.4 4.5 %collective-permute-done.13.refs_3_ = bf16[64,1152]{1,0:T(8,128)(2,1)S(1)} collective-permute-done((bf16[64,1152]{1,0:T(8,128)(2,1)S(1)}, bf16[64,1152]{1,0:T(8,128)(2,1)S(1)}, u32[]{:S(2)}, u32[]{:S(2)}) %collective-permute-start.13) | collective-permute-done | bytes 147488 | tf_op jit(solution)/shard_map/ppermute | solution.py:189
  38.9 0.0 collective-permute-done.14.refs_4_
  38.9 0.0 collective-permute-done.11.refs_1_
  38.9 1.0 %shard_map.74 = (f32[256,1152]{1,0:T(8,128)}, f32[64,1152]{1,0:T(8,128)}) custom-call(s32[1]{0:T(128)} %bitcast.place, f32[1]{0:T(128)S(6)} %copy.9.scale, f32[64,1152]{1,0:T(8,128)S(1)} %get-tuple-element.26.unit, f32[64,128]{1,0:T(8,128)S(1)} %get-tuple-element.27.inverse, f32[64,1152]{1,0:T(8,128)S(1)} %get-tuple-element.38.own, ...), custom_call_target="tpu_custom_call" | custom-call | flops 737280 | bytes 2359296 | tf_op jit(solution)/shard_map/pallas_call | solution.py:282
  40.0 0.1 collective-permute-done.16.refs_1_
  40.1 0.0 collective-permute-done.15.refs_0_
  40.1 0.8 %shard_map.75 = f32[256,1152]{1,0:T(8,128)} custom-call(s32[1]{0:T(128)} %bitcast.place, f32[256,1152]{1,0:T(8,128)} %get-tuple-element.48.begun, bf16[64,1152]{1,0:T(8,128)(2,1)S(1)} %collective-permute-done.15.refs_0_, bf16[64,1152]{1,0:T(8,128)(2,1)S(1)} %collective-permute-done.16.refs_1_), custom_call_target="tpu_custom_call", output_to_operand_aliasing={{}: (1, {})} | custom-call | flops 294912 | bytes 2359296 | tf_op jit(solution)/shard_map/pallas_call | solution.py:297
Async XLA Ops:
  0.6 10.6 %collective-permute-start = (f32[256,1152]{1,0:T(8,128)}, f32[256,1152]{1,0:T(8,128)S(1)}, u32[]{:S(2)}, u32[]{:S(2)}) collective-permute-start(f32[256,1152]{1,0:T(8,128)} %source.3), channel_id=1, source_target_pairs={{0,1},{1,0},{2,3},{3,2},{4,5},{5,4},{6,7},{7,6},{8,9},{9,8},{10,11... | collective-permute-start | bytes 3538952 | tf_op jit(solution)/shard_map/ppermute | solution.py:189
  2.3 8.3 %collective-permute-start.2 = (bf16[32,1152]{1,0:T(8,128)(2,1)S(1)}, bf16[32,1152]{1,0:T(8,128)(2,1)S(1)}, u32[]{:S(2)}, u32[]{:S(2)}) collective-permute-start(bf16[32,1152]{1,0:T(8,128)(2,1)S(1)} %get-tuple-element.32), channel_id=1, source_target_pairs={{0,4},{1,5},{2,6},{3,7},{4,0},{5,1},{6,2},{7,3},{8,12},{9,13},{10,... | collective-permute-start | bytes 221192 | tf_op jit(solution)/shard_map/ppermute | solution.py:189
  5.9 11.1 %collective-permute-start.3 = (bf16[64,1152]{1,0:T(8,128)(2,1)S(1)}, bf16[64,1152]{1,0:T(8,128)(2,1)S(1)}, u32[]{:S(2)}, u32[]{:S(2)}) collective-permute-start(bf16[64,1152]{1,0:T(8,128)(2,1)S(1)} %get-tuple-element.31.refs_0_), channel_id=1, source_target_pairs={{0,2},{1,3},{2,0},{3,1},{4,6},{5,7},{6,4},{7,5},{8,10},{9,11},{10,... | collective-permute-start | bytes 442376 | tf_op jit(solution)/shard_map/ppermute | solution.py:189
  7.5 8.8 %collective-permute-start.6 = (bf16[32,1152]{1,0:T(8,128)(2,1)S(1)}, bf16[32,1152]{1,0:T(8,128)(2,1)S(1)}, u32[]{:S(2)}, u32[]{:S(2)}) collective-permute-start(bf16[32,1152]{1,0:T(8,128)(2,1)S(1)} %get-tuple-element.33), channel_id=1, source_target_pairs={{0,4},{1,5},{2,6},{3,7},{4,0},{5,1},{6,2},{7,3},{8,12},{9,13},{10,... | collective-permute-start | bytes 221192 | tf_op jit(solution)/shard_map/ppermute | solution.py:189
  7.8 8.9 %collective-permute-start.5 = (bf16[32,1152]{1,0:T(8,128)(2,1)S(1)}, bf16[32,1152]{1,0:T(8,128)(2,1)S(1)}, u32[]{:S(2)}, u32[]{:S(2)}) collective-permute-start(bf16[32,1152]{1,0:T(8,128)(2,1)S(1)} %get-tuple-element.33), channel_id=1, source_target_pairs={{0,6},{1,7},{2,4},{3,5},{4,2},{5,3},{6,0},{7,1},{8,14},{9,15},{10,... | collective-permute-start | bytes 221192 | tf_op jit(solution)/shard_map/ppermute | solution.py:189
  10.5 6.5 %collective-permute-start.4 = (bf16[32,1152]{1,0:T(8,128)(2,1)S(1)}, bf16[32,1152]{1,0:T(8,128)(2,1)S(1)}, u32[]{:S(2)}, u32[]{:S(2)}) collective-permute-start(bf16[32,1152]{1,0:T(8,128)(2,1)S(1)} %collective-permute-done.2.refs_1_), channel_id=1, source_target_pairs={{0,2},{1,3},{2,0},{3,1},{4,6},{5,7},{6,4},{7,5},{8,10},{9,11},{10,... | collective-permute-start | bytes 221192 | tf_op jit(solution)/shard_map/ppermute | solution.py:189
  11.2 2.8 %collective-permute-start.1 = (s32[1,256]{1,0:T(1,128)}, s32[1,256]{1,0:T(1,128)S(1)}, u32[]{:S(2)}, u32[]{:S(2)}) collective-permute-start(s32[1,256]{1,0:T(1,128)} %bitcast.3), channel_id=1, source_target_pairs={{0,1},{1,0},{2,3},{3,2},{4,5},{5,4},{6,7},{7,6},{8,9},{9,8},{10,11... | collective-permute-start | bytes 3080 | tf_op jit(solution)/shard_map/ppermute | solution.py:189
  14.0 4.1 %copy-start = (s32[256]{0:T(256)S(1)}, s32[256]{0:T(256)}, u32[]{:S(2)}) copy-start(s32[256]{0:T(256)} %param.7) | copy-start | bytes 3076
  18.1 2.1 %collective-permute-start.7 = (bf16[256,1152]{1,0:T(8,128)(2,1)S(1)}, bf16[256,1152]{1,0:T(8,128)(2,1)S(1)}, u32[]{:S(2)}, u32[]{:S(2)}) collective-permute-start(bf16[256,1152]{1,0:T(8,128)(2,1)S(1)} %get-tuple-element.36), channel_id=1, source_target_pairs={{0,1},{1,0},{2,3},{3,2},{4,5},{5,4},{6,7},{7,6},{8,9},{9,8},{10,11... | collective-permute-start | bytes 1769480 | tf_op jit(solution)/shard_map/ppermute | solution.py:189
  20.3 6.9 %collective-permute-start.8 = (bf16[64,1152]{1,0:T(8,128)(2,1)S(1)}, bf16[64,1152]{1,0:T(8,128)(2,1)S(1)}, u32[]{:S(2)}, u32[]{:S(2)}) collective-permute-start(bf16[64,1152]{1,0:T(8,128)(2,1)S(1)} %get-tuple-element.42), channel_id=1, source_target_pairs={{0,8},{8,0},{16,24},{24,16},{1,9},{9,1},{17,25},{25,17},{2,10},{10... | collective-permute-start | bytes 442376 | tf_op jit(solution)/shard_map/ppermute | solution.py:189
  21.9 8.8 %collective-permute-start.9 = (bf16[64,1152]{1,0:T(8,128)(2,1)S(1)}, bf16[64,1152]{1,0:T(8,128)(2,1)S(1)}, u32[]{:S(2)}, u32[]{:S(2)}) collective-permute-start(bf16[64,1152]{1,0:T(8,128)(2,1)S(1)} %get-tuple-element.43), channel_id=1, source_target_pairs={{0,16},{8,24},{16,0},{24,8},{1,17},{9,25},{17,1},{25,9},{2,18},{10... | collective-permute-start | bytes 442376 | tf_op jit(solution)/shard_map/ppermute | solution.py:189
  23.4 7.3 %collective-permute-start.10 = (bf16[64,1152]{1,0:T(8,128)(2,1)S(1)}, bf16[64,1152]{1,0:T(8,128)(2,1)S(1)}, u32[]{:S(2)}, u32[]{:S(2)}) collective-permute-start(bf16[64,1152]{1,0:T(8,128)(2,1)S(1)} %get-tuple-element.44), channel_id=1, source_target_pairs={{0,24},{8,16},{16,8},{24,0},{1,25},{9,17},{17,9},{25,1},{2,26},{10... | collective-permute-start | bytes 442376 | tf_op jit(solution)/shard_map/ppermute | solution.py:189
  23.8 9.3 %collective-permute-start.12 = (bf16[64,1152]{1,0:T(8,128)(2,1)S(1)}, bf16[64,1152]{1,0:T(8,128)(2,1)S(1)}, u32[]{:S(2)}, u32[]{:S(2)}) collective-permute-start(bf16[64,1152]{1,0:T(8,128)(2,1)S(1)} %get-tuple-element.45), channel_id=1, source_target_pairs={{0,2},{1,3},{2,0},{3,1},{4,6},{5,7},{6,4},{7,5},{8,10},{9,11},{10,... | collective-permute-start | bytes 442376 | tf_op jit(solution)/shard_map/ppermute | solution.py:189
  25.3 13.6 %collective-permute-start.13 = (bf16[64,1152]{1,0:T(8,128)(2,1)S(1)}, bf16[64,1152]{1,0:T(8,128)(2,1)S(1)}, u32[]{:S(2)}, u32[]{:S(2)}) collective-permute-start(bf16[64,1152]{1,0:T(8,128)(2,1)S(1)} %get-tuple-element.46), channel_id=1, source_target_pairs={{0,4},{1,5},{2,6},{3,7},{4,0},{5,1},{6,2},{7,3},{8,12},{9,13},{10,... | collective-permute-start | bytes 442376 | tf_op jit(solution)/shard_map/ppermute | solution.py:189
  27.2 11.7 %collective-permute-start.14 = (bf16[64,1152]{1,0:T(8,128)(2,1)S(1)}, bf16[64,1152]{1,0:T(8,128)(2,1)S(1)}, u32[]{:S(2)}, u32[]{:S(2)}) collective-permute-start(bf16[64,1152]{1,0:T(8,128)(2,1)S(1)} %get-tuple-element.47), channel_id=1, source_target_pairs={{0,6},{1,7},{2,4},{3,5},{4,2},{5,3},{6,0},{7,1},{8,14},{9,15},{10,... | collective-permute-start | bytes 442376 | tf_op jit(solution)/shard_map/ppermute | solution.py:189
  30.9 8.1 %collective-permute-start.11 = (bf16[64,1152]{1,0:T(8,128)(2,1)S(1)}, bf16[64,1152]{1,0:T(8,128)(2,1)S(1)}, u32[]{:S(2)}, u32[]{:S(2)}) collective-permute-start(bf16[64,1152]{1,0:T(8,128)(2,1)S(1)} %shard_map.73.refs_0_), channel_id=1, source_target_pairs={{0,8},{8,0},{16,24},{24,16},{1,9},{9,1},{17,25},{25,17},{2,10},{10... | collective-permute-start | bytes 442376 | tf_op jit(solution)/shard_map/ppermute | solution.py:189
  32.2 7.9 %collective-permute-start.16 = (bf16[64,1152]{1,0:T(8,128)(2,1)S(1)}, bf16[64,1152]{1,0:T(8,128)(2,1)S(1)}, u32[]{:S(2)}, u32[]{:S(2)}) collective-permute-start(bf16[64,1152]{1,0:T(8,128)(2,1)S(1)} %shard_map.73.refs_0_), channel_id=1, source_target_pairs={{0,16},{8,24},{16,0},{24,8},{1,17},{9,25},{17,1},{25,9},{2,18},{10... | collective-permute-start | bytes 442376 | tf_op jit(solution)/shard_map/ppermute | solution.py:189
  33.1 7.0 %collective-permute-start.15 = (bf16[64,1152]{1,0:T(8,128)(2,1)S(1)}, bf16[64,1152]{1,0:T(8,128)(2,1)S(1)}, u32[]{:S(2)}, u32[]{:S(2)}) collective-permute-start(bf16[64,1152]{1,0:T(8,128)(2,1)S(1)} %shard_map.73.refs_0_), channel_id=1, source_target_pairs={{0,24},{8,16},{16,8},{24,0},{1,25},{9,17},{17,9},{25,1},{2,26},{10... | collective-permute-start | bytes 442376 | tf_op jit(solution)/shard_map/ppermute | solution.py:189

commit v16 on v15

--- a/solution.py
+++ b/solution.py
@@ -264,7 +264,7 @@
         rows * width,
     )
     (own_txt, *send_txt), (keep, *send) = outs[:blocks], outs[blocks:]
-    got = [swapped(send[k - 1], "img", k) for k in range(1, count)]
+    got = [swapped(send[k - 1], "img", k) for k in (2, 1, *range(3, count))]
     homes = sorted(zip(order[1:], send_txt), key=lambda pair: pair[0])
     back = [swapped(block, "txt", 2 * k) for k, block in homes]
     (grad_part,) = call(

time: 41.2 us -> 41.6 us (level)
  waiting for transfers between devices: 9.38 us -> 10.6 us
  starting transfers between devices: 22.3 us -> 21.6 us
    ppermute x17, waiting for transfers between devices: 9.38 us -> 10.6 us  [swapped(): return lax.ppermute(value, axis, [(s, s ^ step) for s in range(count)])]
    ppermute x17, starting transfers between devices: 22.3 us -> 21.6 us  [swapped(): return lax.ppermute(value, axis, [(s, s ^ step) for s in range(count)])]
where the time goes in v16:
time: 41.6 us; the launch traced here: 41.4 us
  starting transfers between devices  21.6 us (52%)
  waiting for transfers between devices  10.6 us (25%)
  Pallas kernels  7.21 us (17%)
  between operations  2.02 us (5%)
    ppermute x17, starting transfers between devices, swapped(): return lax.ppermute(value, axis, [(s, s ^ step) for s in range(count)])  21.6 us
    ppermute x17, waiting for transfers between devices, swapped(): return lax.ppermute(value, axis, [(s, s ^ step) for s in range(count)])  10.6 us
    pallas_call x6, Pallas kernels, call(): pl.pallas_call(body, out_shape=outs, in_specs=specs, out_specs=[VMEM] * l...  5.31 us
    pallas_call x1, Pallas kernels, local(): pl.pallas_call(functools.partial(first_body, partners[:early]), out_shape...  1.05 us
    pallas_call x1, Pallas kernels, local(): pl.pallas_call(functools.partial(last_body, partners[early:]), out_shape=...  0.85 us
  transfers between devices with their start and end apart: 17, of which 8 were waited for; matrix products, arithmetic and copies ran while one was open for 0% of the time, Pallas kernels for 13%

profile of v16, /device:TPU:0, one launch (start us, length us, event | category | flops | bytes accessed | tf_op | source)
XLA Modules:
  0.0 41.4 jit_solution(9208544997003521449)
XLA Ops:
  0.6 0.5 %collective-permute-start = (f32[256,1152]{1,0:T(8,128)}, f32[256,1152]{1,0:T(8,128)S(1)}, u32[]{:S(2)}, u32[]{:S(2)}) collective-permute-start(f32[256,1152]{1,0:T(8,128)} %source.3), channel_id=1, source_target_pairs={{0,1},{1,0},{2,3},{3,2},{4,5},{5,4},{6,7},{7,6},{8,9},{9,8},{10,11... | collective-permute-start | bytes 3538952 | tf_op jit(solution)/shard_map/ppermute | solution.py:189
  1.1 1.1 %shard_map.68 = (bf16[64,1152]{1,0:T(8,128)(2,1)S(1)}, bf16[32,1152]{1,0:T(8,128)(2,1)S(1)}, bf16[32,1152]{1,0:T(8,128)(2,1)S(1)}, f32[64,1152]{1,0:T(8,128)S(1)}, f32[64,128]{1,0:T(8,128)S(1)}) custom-call(f32[64,1152]{1,0:T(8,128)} %source.2), custom_call_target="tpu_custom_call" | custom-call | flops 294912 | bytes 917504 | tf_op jit(solution)/shard_map/pallas_call | solution.py:25
  2.3 3.7 %collective-permute-start.2 = (bf16[32,1152]{1,0:T(8,128)(2,1)S(1)}, bf16[32,1152]{1,0:T(8,128)(2,1)S(1)}, u32[]{:S(2)}, u32[]{:S(2)}) collective-permute-start(bf16[32,1152]{1,0:T(8,128)(2,1)S(1)} %get-tuple-element.32), channel_id=1, source_target_pairs={{0,4},{1,5},{2,6},{3,7},{4,0},{5,1},{6,2},{7,3},{8,12},{9,13},{10,... | collective-permute-start | bytes 221192 | tf_op jit(solution)/shard_map/ppermute | solution.py:189
  5.9 1.6 %collective-permute-start.3 = (bf16[64,1152]{1,0:T(8,128)(2,1)S(1)}, bf16[64,1152]{1,0:T(8,128)(2,1)S(1)}, u32[]{:S(2)}, u32[]{:S(2)}) collective-permute-start(bf16[64,1152]{1,0:T(8,128)(2,1)S(1)} %get-tuple-element.31.refs_0_), channel_id=1, source_target_pairs={{0,2},{1,3},{2,0},{3,1},{4,6},{5,7},{6,4},{7,5},{8,10},{9,11},{10,... | collective-permute-start | bytes 442376 | tf_op jit(solution)/shard_map/ppermute | solution.py:189
  7.5 0.3 collective-permute-start.6
  7.8 2.5 %collective-permute-start.5 = (bf16[32,1152]{1,0:T(8,128)(2,1)S(1)}, bf16[32,1152]{1,0:T(8,128)(2,1)S(1)}, u32[]{:S(2)}, u32[]{:S(2)}) collective-permute-start(bf16[32,1152]{1,0:T(8,128)(2,1)S(1)} %get-tuple-element.33), channel_id=1, source_target_pairs={{0,6},{1,7},{2,4},{3,5},{4,2},{5,3},{6,0},{7,1},{8,14},{9,15},{10,... | collective-permute-start | bytes 221192 | tf_op jit(solution)/shard_map/ppermute | solution.py:189
  10.3 0.2 collective-permute-done.2.refs_1_
  10.5 0.7 %collective-permute-start.4 = (bf16[32,1152]{1,0:T(8,128)(2,1)S(1)}, bf16[32,1152]{1,0:T(8,128)(2,1)S(1)}, u32[]{:S(2)}, u32[]{:S(2)}) collective-permute-start(bf16[32,1152]{1,0:T(8,128)(2,1)S(1)} %collective-permute-done.2.refs_1_), channel_id=1, source_target_pairs={{0,2},{1,3},{2,0},{3,1},{4,6},{5,7},{6,4},{7,5},{8,10},{9,11},{10,... | collective-permute-start | bytes 221192 | tf_op jit(solution)/shard_map/ppermute | solution.py:189
  11.2 0.0 collective-permute-done.other
  11.2 0.0 collective-permute-start.1
  12.5 1.5 %shard_map.69 = (bf16[256,1152]{1,0:T(8,128)(2,1)S(1)}, bf16[256,1152]{1,0:T(8,128)(2,1)S(1)}, bf16[1152,256]{1,0:T(8,128)(2,1)S(1)}, f32[64,1152]{1,0:T(8,128)S(1)}, f32[64,128]{1,0:T(8,128)S(1)}) custom-call(s32[1]{0:T(128)} %bitcast.place, f32[256,1152]{1,0:T(8,128)S(1)} %collective-permute-done.other, f32[256,1152]{1,0:T(8,128)} %source.3), custom_call_target="tpu_custom_call" | custom-call | flops 2359296 | bytes 4456452 | tf_op jit(solution)/shard_map/pallas_call | solution.py:25
  14.0 0.0 copy-start
  14.0 0.0 collective-permute-done.1.perm
  14.1 2.3 %collective-permute-done.6.refs_5_ = bf16[32,1152]{1,0:T(8,128)(2,1)S(1)} collective-permute-done((bf16[32,1152]{1,0:T(8,128)(2,1)S(1)}, bf16[32,1152]{1,0:T(8,128)(2,1)S(1)}, u32[]{:S(2)}, u32[]{:S(2)}) %collective-permute-start.6) | collective-permute-done | bytes 73760 | tf_op jit(solution)/shard_map/ppermute | solution.py:189
  16.3 0.4 collective-permute-done.5.refs_4_
  16.7 0.3 collective-permute-done.4.refs_3_
  17.0 0.0 collective-permute-done.3.refs_2_
  17.1 1.0 %shard_map.70 = (bf16[256,256]{1,0:T(8,128)(2,1)S(1)}, bf16[256,1152]{1,0:T(8,128)(2,1)S(1)}) custom-call(s32[1]{0:T(128)} %bitcast.place, s32[1]{0:T(128)} %bitcast.1.column, f32[1]{0:T(128)S(6)} %copy.9.scale, f32[1]{0:T(128)S(6)} %copy.10.shift, s32[1,256]{1,0:T(1,128)S(1)} %collective-permute-done.1.perm, ...), custom_call_target="tpu_custom_call" | custom-call | flops 301989888 | bytes 1901584 | tf_op jit(solution)/shard_map/pallas_call | solution.py:25
  18.1 0.1 collective-permute-start.7
  18.1 0.0 copy-done
  18.1 1.4 %shard_map.71 = (f32[256,1152]{1,0:T(8,128)S(1)}, f32[256,1152]{1,0:T(8,128)S(1)}) custom-call(s32[1]{0:T(128)} %bitcast.place, s32[1]{0:T(128)} %bitcast.1.column, f32[1]{0:T(128)S(6)} %copy.9.scale, f32[1]{0:T(128)S(6)} %copy.10.shift, s32[1,256]{1,0:T(1,128)S(1)} %bitcast.4, bf16[256,1152]{1,0:T(8,128)(2,1)S(1)} %get-tuple-element.28.img, ...), custom_call_target="tpu_custom_call" | custom-call | flops 603979776 | bytes 4260880 | tf_op jit(solution)/shard_map/pallas_call | solution.py:25
  19.5 0.6 %collective-permute-done.7.other = bf16[256,1152]{1,0:T(8,128)(2,1)S(1)} collective-permute-done((bf16[256,1152]{1,0:T(8,128)(2,1)S(1)}, bf16[256,1152]{1,0:T(8,128)(2,1)S(1)}, u32[]{:S(2)}, u32[]{:S(2)}) %collective-permute-start.7) | collective-permute-done | bytes 589856 | tf_op jit(solution)/shard_map/ppermute | solution.py:189
  20.1 0.2 shard_map.72
  20.3 1.6 %collective-permute-start.8 = (bf16[64,1152]{1,0:T(8,128)(2,1)S(1)}, bf16[64,1152]{1,0:T(8,128)(2,1)S(1)}, u32[]{:S(2)}, u32[]{:S(2)}) collective-permute-start(bf16[64,1152]{1,0:T(8,128)(2,1)S(1)} %get-tuple-element.42), channel_id=1, source_target_pairs={{0,16},{8,24},{16,0},{24,8},{1,17},{9,25},{17,1},{25,9},{2,18},{10... | collective-permute-start | bytes 442376 | tf_op jit(solution)/shard_map/ppermute | solution.py:189
  21.9 1.5 %collective-permute-start.9 = (bf16[64,1152]{1,0:T(8,128)(2,1)S(1)}, bf16[64,1152]{1,0:T(8,128)(2,1)S(1)}, u32[]{:S(2)}, u32[]{:S(2)}) collective-permute-start(bf16[64,1152]{1,0:T(8,128)(2,1)S(1)} %get-tuple-element.43), channel_id=1, source_target_pairs={{0,8},{8,0},{16,24},{24,16},{1,9},{9,1},{17,25},{25,17},{2,10},{10... | collective-permute-start | bytes 442376 | tf_op jit(solution)/shard_map/ppermute | solution.py:189
  23.4 0.4 %collective-permute-start.10 = (bf16[64,1152]{1,0:T(8,128)(2,1)S(1)}, bf16[64,1152]{1,0:T(8,128)(2,1)S(1)}, u32[]{:S(2)}, u32[]{:S(2)}) collective-permute-start(bf16[64,1152]{1,0:T(8,128)(2,1)S(1)} %get-tuple-element.44), channel_id=1, source_target_pairs={{0,24},{8,16},{16,8},{24,0},{1,25},{9,17},{17,9},{25,1},{2,26},{10... | collective-permute-start | bytes 442376 | tf_op jit(solution)/shard_map/ppermute | solution.py:189
  23.8 1.5 %collective-permute-start.12 = (bf16[64,1152]{1,0:T(8,128)(2,1)S(1)}, bf16[64,1152]{1,0:T(8,128)(2,1)S(1)}, u32[]{:S(2)}, u32[]{:S(2)}) collective-permute-start(bf16[64,1152]{1,0:T(8,128)(2,1)S(1)} %get-tuple-element.45), channel_id=1, source_target_pairs={{0,2},{1,3},{2,0},{3,1},{4,6},{5,7},{6,4},{7,5},{8,10},{9,11},{10,... | collective-permute-start | bytes 442376 | tf_op jit(solution)/shard_map/ppermute | solution.py:189
  25.3 1.9 %collective-permute-start.13 = (bf16[64,1152]{1,0:T(8,128)(2,1)S(1)}, bf16[64,1152]{1,0:T(8,128)(2,1)S(1)}, u32[]{:S(2)}, u32[]{:S(2)}) collective-permute-start(bf16[64,1152]{1,0:T(8,128)(2,1)S(1)} %get-tuple-element.46), channel_id=1, source_target_pairs={{0,4},{1,5},{2,6},{3,7},{4,0},{5,1},{6,2},{7,3},{8,12},{9,13},{10,... | collective-permute-start | bytes 442376 | tf_op jit(solution)/shard_map/ppermute | solution.py:189
  27.2 0.0 collective-permute-done.8.refs_0_
  27.2 1.8 %collective-permute-start.14 = (bf16[64,1152]{1,0:T(8,128)(2,1)S(1)}, bf16[64,1152]{1,0:T(8,128)(2,1)S(1)}, u32[]{:S(2)}, u32[]{:S(2)}) collective-permute-start(bf16[64,1152]{1,0:T(8,128)(2,1)S(1)} %get-tuple-element.47), channel_id=1, source_target_pairs={{0,6},{1,7},{2,4},{3,5},{4,2},{5,3},{6,0},{7,1},{8,14},{9,15},{10,... | collective-permute-start | bytes 442376 | tf_op jit(solution)/shard_map/ppermute | solution.py:189
  29.0 0.0 collective-permute-done.9.refs_1_
  29.0 1.5 %collective-permute-done.10.refs_2_ = bf16[64,1152]{1,0:T(8,128)(2,1)S(1)} collective-permute-done((bf16[64,1152]{1,0:T(8,128)(2,1)S(1)}, bf16[64,1152]{1,0:T(8,128)(2,1)S(1)}, u32[]{:S(2)}, u32[]{:S(2)}) %collective-permute-start.10) | collective-permute-done | bytes 147488 | tf_op jit(solution)/shard_map/ppermute | solution.py:189
  30.6 0.2 shard_map.73.refs_0_
  30.8 1.6 %collective-permute-start.11 = (bf16[64,1152]{1,0:T(8,128)(2,1)S(1)}, bf16[64,1152]{1,0:T(8,128)(2,1)S(1)}, u32[]{:S(2)}, u32[]{:S(2)}) collective-permute-start(bf16[64,1152]{1,0:T(8,128)(2,1)S(1)} %shard_map.73.refs_0_), channel_id=1, source_target_pairs={{0,8},{8,0},{16,24},{24,16},{1,9},{9,1},{17,25},{25,17},{2,10},{10... | collective-permute-start | bytes 442376 | tf_op jit(solution)/shard_map/ppermute | solution.py:189
  32.4 1.5 %collective-permute-start.16 = (bf16[64,1152]{1,0:T(8,128)(2,1)S(1)}, bf16[64,1152]{1,0:T(8,128)(2,1)S(1)}, u32[]{:S(2)}, u32[]{:S(2)}) collective-permute-start(bf16[64,1152]{1,0:T(8,128)(2,1)S(1)} %shard_map.73.refs_0_), channel_id=1, source_target_pairs={{0,16},{8,24},{16,0},{24,8},{1,17},{9,25},{17,1},{25,9},{2,18},{10... | collective-permute-start | bytes 442376 | tf_op jit(solution)/shard_map/ppermute | solution.py:189
  33.9 0.0 collective-permute-done.12.refs_2_
  33.9 0.4 %collective-permute-start.15 = (bf16[64,1152]{1,0:T(8,128)(2,1)S(1)}, bf16[64,1152]{1,0:T(8,128)(2,1)S(1)}, u32[]{:S(2)}, u32[]{:S(2)}) collective-permute-start(bf16[64,1152]{1,0:T(8,128)(2,1)S(1)} %shard_map.73.refs_0_), channel_id=1, source_target_pairs={{0,24},{8,16},{16,8},{24,0},{1,25},{9,17},{17,9},{25,1},{2,26},{10... | collective-permute-start | bytes 442376 | tf_op jit(solution)/shard_map/ppermute | solution.py:189
  34.3 4.6 %collective-permute-done.13.refs_3_ = bf16[64,1152]{1,0:T(8,128)(2,1)S(1)} collective-permute-done((bf16[64,1152]{1,0:T(8,128)(2,1)S(1)}, bf16[64,1152]{1,0:T(8,128)(2,1)S(1)}, u32[]{:S(2)}, u32[]{:S(2)}) %collective-permute-start.13) | collective-permute-done | bytes 147488 | tf_op jit(solution)/shard_map/ppermute | solution.py:189
  38.9 0.0 collective-permute-done.14.refs_4_
  38.9 0.0 collective-permute-done.11.refs_1_
  38.9 1.0 %shard_map.74 = (f32[256,1152]{1,0:T(8,128)}, f32[64,1152]{1,0:T(8,128)}) custom-call(s32[1]{0:T(128)} %bitcast.place, f32[1]{0:T(128)S(6)} %copy.9.scale, f32[64,1152]{1,0:T(8,128)S(1)} %get-tuple-element.26.unit, f32[64,128]{1,0:T(8,128)S(1)} %get-tuple-element.27.inverse, f32[64,1152]{1,0:T(8,128)S(1)} %get-tuple-element.38.own, ...), custom_call_target="tpu_custom_call" | custom-call | flops 737280 | bytes 2359296 | tf_op jit(solution)/shard_map/pallas_call | solution.py:282
  40.0 0.6 %collective-permute-done.16.refs_1_ = bf16[64,1152]{1,0:T(8,128)(2,1)S(1)} collective-permute-done((bf16[64,1152]{1,0:T(8,128)(2,1)S(1)}, bf16[64,1152]{1,0:T(8,128)(2,1)S(1)}, u32[]{:S(2)}, u32[]{:S(2)}) %collective-permute-start.16) | collective-permute-done | bytes 147488 | tf_op jit(solution)/shard_map/ppermute | solution.py:189
  40.6 0.0 collective-permute-done.15.refs_0_
  40.6 0.8 %shard_map.75 = f32[256,1152]{1,0:T(8,128)} custom-call(s32[1]{0:T(128)} %bitcast.place, f32[256,1152]{1,0:T(8,128)} %get-tuple-element.48.begun, bf16[64,1152]{1,0:T(8,128)(2,1)S(1)} %collective-permute-done.15.refs_0_, bf16[64,1152]{1,0:T(8,128)(2,1)S(1)} %collective-permute-done.16.refs_1_), custom_call_target="tpu_custom_call", output_to_operand_aliasing={{}: (1, {})} | custom-call | flops 294912 | bytes 2359296 | tf_op jit(solution)/shard_map/pallas_call | solution.py:297
Async XLA Ops:
  0.6 10.6 %collective-permute-start = (f32[256,1152]{1,0:T(8,128)}, f32[256,1152]{1,0:T(8,128)S(1)}, u32[]{:S(2)}, u32[]{:S(2)}) collective-permute-start(f32[256,1152]{1,0:T(8,128)} %source.3), channel_id=1, source_target_pairs={{0,1},{1,0},{2,3},{3,2},{4,5},{5,4},{6,7},{7,6},{8,9},{9,8},{10,11... | collective-permute-start | bytes 3538952 | tf_op jit(solution)/shard_map/ppermute | solution.py:189
  2.3 8.3 %collective-permute-start.2 = (bf16[32,1152]{1,0:T(8,128)(2,1)S(1)}, bf16[32,1152]{1,0:T(8,128)(2,1)S(1)}, u32[]{:S(2)}, u32[]{:S(2)}) collective-permute-start(bf16[32,1152]{1,0:T(8,128)(2,1)S(1)} %get-tuple-element.32), channel_id=1, source_target_pairs={{0,4},{1,5},{2,6},{3,7},{4,0},{5,1},{6,2},{7,3},{8,12},{9,13},{10,... | collective-permute-start | bytes 221192 | tf_op jit(solution)/shard_map/ppermute | solution.py:189
  5.9 11.1 %collective-permute-start.3 = (bf16[64,1152]{1,0:T(8,128)(2,1)S(1)}, bf16[64,1152]{1,0:T(8,128)(2,1)S(1)}, u32[]{:S(2)}, u32[]{:S(2)}) collective-permute-start(bf16[64,1152]{1,0:T(8,128)(2,1)S(1)} %get-tuple-element.31.refs_0_), channel_id=1, source_target_pairs={{0,2},{1,3},{2,0},{3,1},{4,6},{5,7},{6,4},{7,5},{8,10},{9,11},{10,... | collective-permute-start | bytes 442376 | tf_op jit(solution)/shard_map/ppermute | solution.py:189
  7.5 8.8 %collective-permute-start.6 = (bf16[32,1152]{1,0:T(8,128)(2,1)S(1)}, bf16[32,1152]{1,0:T(8,128)(2,1)S(1)}, u32[]{:S(2)}, u32[]{:S(2)}) collective-permute-start(bf16[32,1152]{1,0:T(8,128)(2,1)S(1)} %get-tuple-element.33), channel_id=1, source_target_pairs={{0,4},{1,5},{2,6},{3,7},{4,0},{5,1},{6,2},{7,3},{8,12},{9,13},{10,... | collective-permute-start | bytes 221192 | tf_op jit(solution)/shard_map/ppermute | solution.py:189
  7.8 8.9 %collective-permute-start.5 = (bf16[32,1152]{1,0:T(8,128)(2,1)S(1)}, bf16[32,1152]{1,0:T(8,128)(2,1)S(1)}, u32[]{:S(2)}, u32[]{:S(2)}) collective-permute-start(bf16[32,1152]{1,0:T(8,128)(2,1)S(1)} %get-tuple-element.33), channel_id=1, source_target_pairs={{0,6},{1,7},{2,4},{3,5},{4,2},{5,3},{6,0},{7,1},{8,14},{9,15},{10,... | collective-permute-start | bytes 221192 | tf_op jit(solution)/shard_map/ppermute | solution.py:189
  10.5 6.5 %collective-permute-start.4 = (bf16[32,1152]{1,0:T(8,128)(2,1)S(1)}, bf16[32,1152]{1,0:T(8,128)(2,1)S(1)}, u32[]{:S(2)}, u32[]{:S(2)}) collective-permute-start(bf16[32,1152]{1,0:T(8,128)(2,1)S(1)} %collective-permute-done.2.refs_1_), channel_id=1, source_target_pairs={{0,2},{1,3},{2,0},{3,1},{4,6},{5,7},{6,4},{7,5},{8,10},{9,11},{10,... | collective-permute-start | bytes 221192 | tf_op jit(solution)/shard_map/ppermute | solution.py:189
  11.2 2.8 %collective-permute-start.1 = (s32[1,256]{1,0:T(1,128)}, s32[1,256]{1,0:T(1,128)S(1)}, u32[]{:S(2)}, u32[]{:S(2)}) collective-permute-start(s32[1,256]{1,0:T(1,128)} %bitcast.3), channel_id=1, source_target_pairs={{0,1},{1,0},{2,3},{3,2},{4,5},{5,4},{6,7},{7,6},{8,9},{9,8},{10,11... | collective-permute-start | bytes 3080 | tf_op jit(solution)/shard_map/ppermute | solution.py:189
  14.0 4.1 %copy-start = (s32[256]{0:T(256)S(1)}, s32[256]{0:T(256)}, u32[]{:S(2)}) copy-start(s32[256]{0:T(256)} %param.7) | copy-start | bytes 3076
  18.1 2.1 %collective-permute-start.7 = (bf16[256,1152]{1,0:T(8,128)(2,1)S(1)}, bf16[256,1152]{1,0:T(8,128)(2,1)S(1)}, u32[]{:S(2)}, u32[]{:S(2)}) collective-permute-start(bf16[256,1152]{1,0:T(8,128)(2,1)S(1)} %get-tuple-element.36), channel_id=1, source_target_pairs={{0,1},{1,0},{2,3},{3,2},{4,5},{5,4},{6,7},{7,6},{8,9},{9,8},{10,11... | collective-permute-start | bytes 1769480 | tf_op jit(solution)/shard_map/ppermute | solution.py:189
  20.3 6.9 %collective-permute-start.8 = (bf16[64,1152]{1,0:T(8,128)(2,1)S(1)}, bf16[64,1152]{1,0:T(8,128)(2,1)S(1)}, u32[]{:S(2)}, u32[]{:S(2)}) collective-permute-start(bf16[64,1152]{1,0:T(8,128)(2,1)S(1)} %get-tuple-element.42), channel_id=1, source_target_pairs={{0,16},{8,24},{16,0},{24,8},{1,17},{9,25},{17,1},{25,9},{2,18},{10... | collective-permute-start | bytes 442376 | tf_op jit(solution)/shard_map/ppermute | solution.py:189
  21.9 7.1 %collective-permute-start.9 = (bf16[64,1152]{1,0:T(8,128)(2,1)S(1)}, bf16[64,1152]{1,0:T(8,128)(2,1)S(1)}, u32[]{:S(2)}, u32[]{:S(2)}) collective-permute-start(bf16[64,1152]{1,0:T(8,128)(2,1)S(1)} %get-tuple-element.43), channel_id=1, source_target_pairs={{0,8},{8,0},{16,24},{24,16},{1,9},{9,1},{17,25},{25,17},{2,10},{10... | collective-permute-start | bytes 442376 | tf_op jit(solution)/shard_map/ppermute | solution.py:189
  23.4 7.2 %collective-permute-start.10 = (bf16[64,1152]{1,0:T(8,128)(2,1)S(1)}, bf16[64,1152]{1,0:T(8,128)(2,1)S(1)}, u32[]{:S(2)}, u32[]{:S(2)}) collective-permute-start(bf16[64,1152]{1,0:T(8,128)(2,1)S(1)} %get-tuple-element.44), channel_id=1, source_target_pairs={{0,24},{8,16},{16,8},{24,0},{1,25},{9,17},{17,9},{25,1},{2,26},{10... | collective-permute-start | bytes 442376 | tf_op jit(solution)/shard_map/ppermute | solution.py:189
  23.8 10.1 %collective-permute-start.12 = (bf16[64,1152]{1,0:T(8,128)(2,1)S(1)}, bf16[64,1152]{1,0:T(8,128)(2,1)S(1)}, u32[]{:S(2)}, u32[]{:S(2)}) collective-permute-start(bf16[64,1152]{1,0:T(8,128)(2,1)S(1)} %get-tuple-element.45), channel_id=1, source_target_pairs={{0,2},{1,3},{2,0},{3,1},{4,6},{5,7},{6,4},{7,5},{8,10},{9,11},{10,... | collective-permute-start | bytes 442376 | tf_op jit(solution)/shard_map/ppermute | solution.py:189
  25.3 13.6 %collective-permute-start.13 = (bf16[64,1152]{1,0:T(8,128)(2,1)S(1)}, bf16[64,1152]{1,0:T(8,128)(2,1)S(1)}, u32[]{:S(2)}, u32[]{:S(2)}) collective-permute-start(bf16[64,1152]{1,0:T(8,128)(2,1)S(1)} %get-tuple-element.46), channel_id=1, source_target_pairs={{0,4},{1,5},{2,6},{3,7},{4,0},{5,1},{6,2},{7,3},{8,12},{9,13},{10,... | collective-permute-start | bytes 442376 | tf_op jit(solution)/shard_map/ppermute | solution.py:189
  27.2 11.7 %collective-permute-start.14 = (bf16[64,1152]{1,0:T(8,128)(2,1)S(1)}, bf16[64,1152]{1,0:T(8,128)(2,1)S(1)}, u32[]{:S(2)}, u32[]{:S(2)}) collective-permute-start(bf16[64,1152]{1,0:T(8,128)(2,1)S(1)} %get-tuple-element.47), channel_id=1, source_target_pairs={{0,6},{1,7},{2,4},{3,5},{4,2},{5,3},{6,0},{7,1},{8,14},{9,15},{10,... | collective-permute-start | bytes 442376 | tf_op jit(solution)/shard_map/ppermute | solution.py:189
  30.8 8.2 %collective-permute-start.11 = (bf16[64,1152]{1,0:T(8,128)(2,1)S(1)}, bf16[64,1152]{1,0:T(8,128)(2,1)S(1)}, u32[]{:S(2)}, u32[]{:S(2)}) collective-permute-start(bf16[64,1152]{1,0:T(8,128)(2,1)S(1)} %shard_map.73.refs_0_), channel_id=1, source_target_pairs={{0,8},{8,0},{16,24},{24,16},{1,9},{9,1},{17,25},{25,17},{2,10},{10... | collective-permute-start | bytes 442376 | tf_op jit(solution)/shard_map/ppermute | solution.py:189
  32.4 8.2 %collective-permute-start.16 = (bf16[64,1152]{1,0:T(8,128)(2,1)S(1)}, bf16[64,1152]{1,0:T(8,128)(2,1)S(1)}, u32[]{:S(2)}, u32[]{:S(2)}) collective-permute-start(bf16[64,1152]{1,0:T(8,128)(2,1)S(1)} %shard_map.73.refs_0_), channel_id=1, source_target_pairs={{0,16},{8,24},{16,0},{24,8},{1,17},{9,25},{17,1},{25,9},{2,18},{10... | collective-permute-start | bytes 442376 | tf_op jit(solution)/shard_map/ppermute | solution.py:189
  33.9 6.7 %collective-permute-start.15 = (bf16[64,1152]{1,0:T(8,128)(2,1)S(1)}, bf16[64,1152]{1,0:T(8,128)(2,1)S(1)}, u32[]{:S(2)}, u32[]{:S(2)}) collective-permute-start(bf16[64,1152]{1,0:T(8,128)(2,1)S(1)} %shard_map.73.refs_0_), channel_id=1, source_target_pairs={{0,24},{8,16},{16,8},{24,0},{1,25},{9,17},{17,9},{25,1},{2,26},{10... | collective-permute-start | bytes 442376 | tf_op jit(solution)/shard_map/ppermute | solution.py:189

commit v17 on v16

--- a/solution.py
+++ b/solution.py
@@ -114,19 +114,17 @@
     txt_sums[...] = to_texts(weights, img[...]) + to_texts(kept[...], img_other[...])
 
 
-def split_body(count, blocks, place, own, other, txt_sums, *refs):
+def split_body(partners, blocks, place, column, own, other, txt_sums, *refs):
     txt_out, (keep, *send) = refs[:blocks], refs[blocks:]
     rows = txt_out[0].shape[0]
     for k, out in enumerate(txt_out):
         out[...] = txt_sums[k * rows : (k + 1) * rows, :].astype(out.dtype)
     rows = keep.shape[0]
-    for k in range(count):
-        start = pl.multiple_of((place[0] ^ k) * rows, rows)
+    core = column[0] & 1
+    for out, (even, odd) in zip([keep, *send], [(0, 0), *partners]):
+        start = pl.multiple_of((place[0] ^ (even + core * (odd - even))) * rows, rows)
         part = own[pl.ds(start, rows), :] + other[pl.ds(start, rows), :].astype(F32)
-        if k == 0:
-            keep[...] = part
-        else:
-            send[k - 1][...] = part.astype(BF16)
+        out[...] = part.astype(out.dtype)
 
 
 def total_of(own, parts):
@@ -187,6 +185,16 @@
 def swapped(value, axis, step):
     count = lax.axis_size(axis)
     return lax.ppermute(value, axis, [(s, s ^ step) for s in range(count)])
+
+
+def plane_swapped(value, even, odd):
+    count, line = lax.axis_size("img"), lax.axis_size("txt")
+    pairs = [
+        (i * line + t, (i ^ (odd if t % 2 else even)) * line + t)
+        for i in range(count)
+        for t in range(line)
+    ]
+    return lax.ppermute(value, ("img", "txt"), pairs)
 
 
 def local(images, texts, perm, scale, shift):
@@ -252,19 +260,20 @@
         40 << 20,
         4 * pairs,
     )
+    turns = [(1, 3), (2, 1), (3, 2)] + [(k, k) for k in range(4, count)]
     outs = call(
-        functools.partial(split_body, count, blocks),
+        functools.partial(split_body, turns, blocks),
         [struct(txt_rows, width, F32)]
         + [struct(txt_rows, width, BF16)] * (blocks - 1)
         + [struct(part, width, F32)]
         + [struct(part, width, BF16)] * (count - 1),
-        [place, own_img, from_other, txt_sums],
-        [SMEM] + [VMEM] * 3,
+        [place, column, own_img, from_other, txt_sums],
+        [SMEM] * 2 + [VMEM] * 3,
         24 << 20,
         rows * width,
     )
     (own_txt, *send_txt), (keep, *send) = outs[:blocks], outs[blocks:]
-    got = [swapped(send[k - 1], "img", k) for k in (2, 1, *range(3, count))]
+    got = [plane_swapped(block, *turn) for block, turn in zip(send, turns)]
     homes = sorted(zip(order[1:], send_txt), key=lambda pair: pair[0])
     back = [swapped(block, "txt", 2 * k) for k, block in homes]
     (grad_part,) = call(

time: 41.6 us -> 41.9 us (level)
  starting transfers between devices: 21.6 us -> 22.3 us
  waiting for transfers between devices: 10.6 us -> 10.1 us
    ppermute x0 -> x3, starting transfers between devices: none -> 3.55 us  [plane_swapped(): return lax.ppermute(value, ('img', 'txt'), pairs)]
    ppermute x17 -> x14, starting transfers between devices: 21.6 us -> 18.8 us  [swapped(): return lax.ppermute(value, axis, [(s, s ^ step) for s in range(count)])]
    ppermute x17 -> x14, waiting for transfers between devices: 10.6 us -> 9.34 us  [swapped(): return lax.ppermute(value, axis, [(s, s ^ step) for s in range(count)])]
    ppermute x0 -> x3, waiting for transfers between devices: none -> 0.79 us  [plane_swapped(): return lax.ppermute(value, ('img', 'txt'), pairs)]
  transfers between devices with their start and end apart: 17 -> 17, of which waited for: 8 -> 8; matrix products, arithmetic and copies ran while one was open for 0% -> 0% of each run, Pallas kernels for 13% -> 12%
where the time goes in v17:
time: 41.9 us; the launch traced here: 41.7 us
  starting transfers between devices  22.3 us (53%)
  waiting for transfers between devices  10.1 us (24%)
  Pallas kernels  7.21 us (17%)
  between operations  2.02 us (5%)
    ppermute x14, starting transfers between devices, swapped(): return lax.ppermute(value, axis, [(s, s ^ step) for s in range(count)])  18.8 us
    ppermute x14, waiting for transfers between devices, swapped(): return lax.ppermute(value, axis, [(s, s ^ step) for s in range(count)])  9.34 us
    pallas_call x6, Pallas kernels, call(): pl.pallas_call(body, out_shape=outs, in_specs=specs, out_specs=[VMEM] * l...  5.31 us
    ppermute x3, starting transfers between devices, plane_swapped(): return lax.ppermute(value, ('img', 'txt'), pairs)  3.55 us
    pallas_call x1, Pallas kernels, local(): pl.pallas_call(functools.partial(first_body, partners[:early]), out_shape...  1.05 us
    pallas_call x1, Pallas kernels, local(): pl.pallas_call(functools.partial(last_body, partners[early:]), out_shape=...  0.85 us
  transfers between devices with their start and end apart: 17, of which 8 were waited for; matrix products, arithmetic and copies ran while one was open for 0% of the time, Pallas kernels for 12%

profile of v17, /device:TPU:0, one launch (start us, length us, event | category | flops | bytes accessed | tf_op | source)
XLA Modules:
  0.0 41.7 jit_solution(4209000706477286525)
XLA Ops:
  0.6 0.5 %collective-permute-start = (f32[256,1152]{1,0:T(8,128)}, f32[256,1152]{1,0:T(8,128)S(1)}, u32[]{:S(2)}, u32[]{:S(2)}) collective-permute-start(f32[256,1152]{1,0:T(8,128)} %source.3), channel_id=1, source_target_pairs={{0,1},{1,0},{2,3},{3,2},{4,5},{5,4},{6,7},{7,6},{8,9},{9,8},{10,11... | collective-permute-start | bytes 3538952 | tf_op jit(solution)/shard_map/ppermute | solution.py:187
  1.1 1.1 %shard_map.68 = (bf16[64,1152]{1,0:T(8,128)(2,1)S(1)}, bf16[32,1152]{1,0:T(8,128)(2,1)S(1)}, bf16[32,1152]{1,0:T(8,128)(2,1)S(1)}, f32[64,1152]{1,0:T(8,128)S(1)}, f32[64,128]{1,0:T(8,128)S(1)}) custom-call(f32[64,1152]{1,0:T(8,128)} %source.2), custom_call_target="tpu_custom_call" | custom-call | flops 294912 | bytes 917504 | tf_op jit(solution)/shard_map/pallas_call | solution.py:25
  2.3 3.7 %collective-permute-start.2 = (bf16[32,1152]{1,0:T(8,128)(2,1)S(1)}, bf16[32,1152]{1,0:T(8,128)(2,1)S(1)}, u32[]{:S(2)}, u32[]{:S(2)}) collective-permute-start(bf16[32,1152]{1,0:T(8,128)(2,1)S(1)} %get-tuple-element.32), channel_id=1, source_target_pairs={{0,4},{1,5},{2,6},{3,7},{4,0},{5,1},{6,2},{7,3},{8,12},{9,13},{10,... | collective-permute-start | bytes 221192 | tf_op jit(solution)/shard_map/ppermute | solution.py:187
  5.9 1.6 %collective-permute-start.3 = (bf16[64,1152]{1,0:T(8,128)(2,1)S(1)}, bf16[64,1152]{1,0:T(8,128)(2,1)S(1)}, u32[]{:S(2)}, u32[]{:S(2)}) collective-permute-start(bf16[64,1152]{1,0:T(8,128)(2,1)S(1)} %get-tuple-element.31.refs_0_), channel_id=1, source_target_pairs={{0,2},{1,3},{2,0},{3,1},{4,6},{5,7},{6,4},{7,5},{8,10},{9,11},{10,... | collective-permute-start | bytes 442376 | tf_op jit(solution)/shard_map/ppermute | solution.py:187
  7.5 0.3 collective-permute-start.6
  7.8 2.5 %collective-permute-start.5 = (bf16[32,1152]{1,0:T(8,128)(2,1)S(1)}, bf16[32,1152]{1,0:T(8,128)(2,1)S(1)}, u32[]{:S(2)}, u32[]{:S(2)}) collective-permute-start(bf16[32,1152]{1,0:T(8,128)(2,1)S(1)} %get-tuple-element.33), channel_id=1, source_target_pairs={{0,6},{1,7},{2,4},{3,5},{4,2},{5,3},{6,0},{7,1},{8,14},{9,15},{10,... | collective-permute-start | bytes 221192 | tf_op jit(solution)/shard_map/ppermute | solution.py:187
  10.3 0.2 collective-permute-done.2.refs_1_
  10.5 0.7 %collective-permute-start.4 = (bf16[32,1152]{1,0:T(8,128)(2,1)S(1)}, bf16[32,1152]{1,0:T(8,128)(2,1)S(1)}, u32[]{:S(2)}, u32[]{:S(2)}) collective-permute-start(bf16[32,1152]{1,0:T(8,128)(2,1)S(1)} %collective-permute-done.2.refs_1_), channel_id=1, source_target_pairs={{0,2},{1,3},{2,0},{3,1},{4,6},{5,7},{6,4},{7,5},{8,10},{9,11},{10,... | collective-permute-start | bytes 221192 | tf_op jit(solution)/shard_map/ppermute | solution.py:187
  11.2 0.0 collective-permute-done.other
  11.2 0.0 collective-permute-start.1
  12.5 1.5 %shard_map.69 = (bf16[256,1152]{1,0:T(8,128)(2,1)S(1)}, bf16[256,1152]{1,0:T(8,128)(2,1)S(1)}, bf16[1152,256]{1,0:T(8,128)(2,1)S(1)}, f32[64,1152]{1,0:T(8,128)S(1)}, f32[64,128]{1,0:T(8,128)S(1)}) custom-call(s32[1]{0:T(128)} %bitcast.place, f32[256,1152]{1,0:T(8,128)S(1)} %collective-permute-done.other, f32[256,1152]{1,0:T(8,128)} %source.3), custom_call_target="tpu_custom_call" | custom-call | flops 2359296 | bytes 4456452 | tf_op jit(solution)/shard_map/pallas_call | solution.py:25
  14.0 0.0 copy-start
  14.0 0.0 collective-permute-done.1.perm
  14.1 2.3 %collective-permute-done.6.refs_5_ = bf16[32,1152]{1,0:T(8,128)(2,1)S(1)} collective-permute-done((bf16[32,1152]{1,0:T(8,128)(2,1)S(1)}, bf16[32,1152]{1,0:T(8,128)(2,1)S(1)}, u32[]{:S(2)}, u32[]{:S(2)}) %collective-permute-start.6) | collective-permute-done | bytes 73760 | tf_op jit(solution)/shard_map/ppermute | solution.py:187
  16.3 0.4 collective-permute-done.5.refs_4_
  16.7 0.3 collective-permute-done.4.refs_3_
  17.0 0.0 collective-permute-done.3.refs_2_
  17.1 1.0 %shard_map.70 = (bf16[256,256]{1,0:T(8,128)(2,1)S(1)}, bf16[256,1152]{1,0:T(8,128)(2,1)S(1)}) custom-call(s32[1]{0:T(128)} %bitcast.place, s32[1]{0:T(128)} %bitcast.1.column, f32[1]{0:T(128)S(6)} %copy.9.scale, f32[1]{0:T(128)S(6)} %copy.10.shift, s32[1,256]{1,0:T(1,128)S(1)} %collective-permute-done.1.perm, ...), custom_call_target="tpu_custom_call" | custom-call | flops 301989888 | bytes 1901584 | tf_op jit(solution)/shard_map/pallas_call | solution.py:25
  18.1 0.1 collective-permute-start.7
  18.1 0.0 copy-done
  18.1 1.4 %shard_map.71 = (f32[256,1152]{1,0:T(8,128)S(1)}, f32[256,1152]{1,0:T(8,128)S(1)}) custom-call(s32[1]{0:T(128)} %bitcast.place, s32[1]{0:T(128)} %bitcast.1.column, f32[1]{0:T(128)S(6)} %copy.9.scale, f32[1]{0:T(128)S(6)} %copy.10.shift, s32[1,256]{1,0:T(1,128)S(1)} %bitcast.4, bf16[256,1152]{1,0:T(8,128)(2,1)S(1)} %get-tuple-element.28.img, ...), custom_call_target="tpu_custom_call" | custom-call | flops 603979776 | bytes 4260880 | tf_op jit(solution)/shard_map/pallas_call | solution.py:25
  19.5 0.6 %collective-permute-done.7.other = bf16[256,1152]{1,0:T(8,128)(2,1)S(1)} collective-permute-done((bf16[256,1152]{1,0:T(8,128)(2,1)S(1)}, bf16[256,1152]{1,0:T(8,128)(2,1)S(1)}, u32[]{:S(2)}, u32[]{:S(2)}) %collective-permute-start.7) | collective-permute-done | bytes 589856 | tf_op jit(solution)/shard_map/ppermute | solution.py:187
  20.1 0.2 shard_map.72
  20.3 1.6 %collective-permute-start.8 = (bf16[64,1152]{1,0:T(8,128)(2,1)S(1)}, bf16[64,1152]{1,0:T(8,128)(2,1)S(1)}, u32[]{:S(2)}, u32[]{:S(2)}) collective-permute-start(bf16[64,1152]{1,0:T(8,128)(2,1)S(1)} %get-tuple-element.42), channel_id=1, source_target_pairs={{0,8},{1,25},{2,10},{3,27},{4,12},{5,29},{6,14},{7,31},{8,0},{9,17... | collective-permute-start | bytes 442376 | tf_op jit(solution)/shard_map/ppermute | solution.py:197
  21.9 1.5 %collective-permute-start.9 = (bf16[64,1152]{1,0:T(8,128)(2,1)S(1)}, bf16[64,1152]{1,0:T(8,128)(2,1)S(1)}, u32[]{:S(2)}, u32[]{:S(2)}) collective-permute-start(bf16[64,1152]{1,0:T(8,128)(2,1)S(1)} %get-tuple-element.43), channel_id=1, source_target_pairs={{0,16},{1,9},{2,18},{3,11},{4,20},{5,13},{6,22},{7,15},{8,24},{9,1... | collective-permute-start | bytes 442376 | tf_op jit(solution)/shard_map/ppermute | solution.py:197
  23.4 0.4 %collective-permute-start.10 = (bf16[64,1152]{1,0:T(8,128)(2,1)S(1)}, bf16[64,1152]{1,0:T(8,128)(2,1)S(1)}, u32[]{:S(2)}, u32[]{:S(2)}) collective-permute-start(bf16[64,1152]{1,0:T(8,128)(2,1)S(1)} %get-tuple-element.44), channel_id=1, source_target_pairs={{0,24},{1,17},{2,26},{3,19},{4,28},{5,21},{6,30},{7,23},{8,16},{9,... | collective-permute-start | bytes 442376 | tf_op jit(solution)/shard_map/ppermute | solution.py:197
  23.8 1.5 %collective-permute-start.12 = (bf16[64,1152]{1,0:T(8,128)(2,1)S(1)}, bf16[64,1152]{1,0:T(8,128)(2,1)S(1)}, u32[]{:S(2)}, u32[]{:S(2)}) collective-permute-start(bf16[64,1152]{1,0:T(8,128)(2,1)S(1)} %get-tuple-element.45), channel_id=1, source_target_pairs={{0,2},{1,3},{2,0},{3,1},{4,6},{5,7},{6,4},{7,5},{8,10},{9,11},{10,... | collective-permute-start | bytes 442376 | tf_op jit(solution)/shard_map/ppermute | solution.py:187
  25.3 1.9 %collective-permute-start.13 = (bf16[64,1152]{1,0:T(8,128)(2,1)S(1)}, bf16[64,1152]{1,0:T(8,128)(2,1)S(1)}, u32[]{:S(2)}, u32[]{:S(2)}) collective-permute-start(bf16[64,1152]{1,0:T(8,128)(2,1)S(1)} %get-tuple-element.46), channel_id=1, source_target_pairs={{0,4},{1,5},{2,6},{3,7},{4,0},{5,1},{6,2},{7,3},{8,12},{9,13},{10,... | collective-permute-start | bytes 442376 | tf_op jit(solution)/shard_map/ppermute | solution.py:187
  27.2 0.0 collective-permute-done.8.refs_0_
  27.2 2.5 %collective-permute-start.14 = (bf16[64,1152]{1,0:T(8,128)(2,1)S(1)}, bf16[64,1152]{1,0:T(8,128)(2,1)S(1)}, u32[]{:S(2)}, u32[]{:S(2)}) collective-permute-start(bf16[64,1152]{1,0:T(8,128)(2,1)S(1)} %get-tuple-element.47), channel_id=1, source_target_pairs={{0,6},{1,7},{2,4},{3,5},{4,2},{5,3},{6,0},{7,1},{8,14},{9,15},{10,... | collective-permute-start | bytes 442376 | tf_op jit(solution)/shard_map/ppermute | solution.py:187
  29.7 0.8 %collective-permute-done.9.refs_1_ = bf16[64,1152]{1,0:T(8,128)(2,1)S(1)} collective-permute-done((bf16[64,1152]{1,0:T(8,128)(2,1)S(1)}, bf16[64,1152]{1,0:T(8,128)(2,1)S(1)}, u32[]{:S(2)}, u32[]{:S(2)}) %collective-permute-start.9) | collective-permute-done | bytes 147488 | tf_op jit(solution)/shard_map/ppermute | solution.py:197
  30.5 0.0 collective-permute-done.10.refs_2_
  30.5 0.2 shard_map.73.refs_0_
  30.7 1.4 %collective-permute-start.11 = (bf16[64,1152]{1,0:T(8,128)(2,1)S(1)}, bf16[64,1152]{1,0:T(8,128)(2,1)S(1)}, u32[]{:S(2)}, u32[]{:S(2)}) collective-permute-start(bf16[64,1152]{1,0:T(8,128)(2,1)S(1)} %shard_map.73.refs_0_), channel_id=1, source_target_pairs={{0,8},{8,0},{16,24},{24,16},{1,9},{9,1},{17,25},{25,17},{2,10},{10... | collective-permute-start | bytes 442376 | tf_op jit(solution)/shard_map/ppermute | solution.py:187
  32.1 1.7 %collective-permute-start.16 = (bf16[64,1152]{1,0:T(8,128)(2,1)S(1)}, bf16[64,1152]{1,0:T(8,128)(2,1)S(1)}, u32[]{:S(2)}, u32[]{:S(2)}) collective-permute-start(bf16[64,1152]{1,0:T(8,128)(2,1)S(1)} %shard_map.73.refs_0_), channel_id=1, source_target_pairs={{0,16},{8,24},{16,0},{24,8},{1,17},{9,25},{17,1},{25,9},{2,18},{10... | collective-permute-start | bytes 442376 | tf_op jit(solution)/shard_map/ppermute | solution.py:187
  33.8 0.0 collective-permute-done.12.refs_2_
  33.8 0.4 %collective-permute-start.15 = (bf16[64,1152]{1,0:T(8,128)(2,1)S(1)}, bf16[64,1152]{1,0:T(8,128)(2,1)S(1)}, u32[]{:S(2)}, u32[]{:S(2)}) collective-permute-start(bf16[64,1152]{1,0:T(8,128)(2,1)S(1)} %shard_map.73.refs_0_), channel_id=1, source_target_pairs={{0,24},{8,16},{16,8},{24,0},{1,25},{9,17},{17,9},{25,1},{2,26},{10... | collective-permute-start | bytes 442376 | tf_op jit(solution)/shard_map/ppermute | solution.py:187
  34.3 4.6 %collective-permute-done.13.refs_3_ = bf16[64,1152]{1,0:T(8,128)(2,1)S(1)} collective-permute-done((bf16[64,1152]{1,0:T(8,128)(2,1)S(1)}, bf16[64,1152]{1,0:T(8,128)(2,1)S(1)}, u32[]{:S(2)}, u32[]{:S(2)}) %collective-permute-start.13) | collective-permute-done | bytes 147488 | tf_op jit(solution)/shard_map/ppermute | solution.py:187
  38.9 0.0 collective-permute-done.14.refs_4_
  38.9 0.0 collective-permute-done.11.refs_1_
  38.9 1.0 %shard_map.74 = (f32[256,1152]{1,0:T(8,128)}, f32[64,1152]{1,0:T(8,128)}) custom-call(s32[1]{0:T(128)} %bitcast.place, f32[1]{0:T(128)S(6)} %copy.9.scale, f32[64,1152]{1,0:T(8,128)S(1)} %get-tuple-element.26.unit, f32[64,128]{1,0:T(8,128)S(1)} %get-tuple-element.27.inverse, f32[64,1152]{1,0:T(8,128)S(1)} %get-tuple-element.38.own, ...), custom_call_target="tpu_custom_call" | custom-call | flops 737280 | bytes 2359296 | tf_op jit(solution)/shard_map/pallas_call | solution.py:291
  40.0 0.9 %collective-permute-done.16.refs_1_ = bf16[64,1152]{1,0:T(8,128)(2,1)S(1)} collective-permute-done((bf16[64,1152]{1,0:T(8,128)(2,1)S(1)}, bf16[64,1152]{1,0:T(8,128)(2,1)S(1)}, u32[]{:S(2)}, u32[]{:S(2)}) %collective-permute-start.16) | collective-permute-done | bytes 147488 | tf_op jit(solution)/shard_map/ppermute | solution.py:187
  40.9 0.0 collective-permute-done.15.refs_0_
  40.9 0.8 %shard_map.75 = f32[256,1152]{1,0:T(8,128)} custom-call(s32[1]{0:T(128)} %bitcast.place, f32[256,1152]{1,0:T(8,128)} %get-tuple-element.48.begun, bf16[64,1152]{1,0:T(8,128)(2,1)S(1)} %collective-permute-done.15.refs_0_, bf16[64,1152]{1,0:T(8,128)(2,1)S(1)} %collective-permute-done.16.refs_1_), custom_call_target="tpu_custom_call", output_to_operand_aliasing={{}: (1, {})} | custom-call | flops 294912 | bytes 2359296 | tf_op jit(solution)/shard_map/pallas_call | solution.py:306
Async XLA Ops:
  0.6 10.6 %collective-permute-start = (f32[256,1152]{1,0:T(8,128)}, f32[256,1152]{1,0:T(8,128)S(1)}, u32[]{:S(2)}, u32[]{:S(2)}) collective-permute-start(f32[256,1152]{1,0:T(8,128)} %source.3), channel_id=1, source_target_pairs={{0,1},{1,0},{2,3},{3,2},{4,5},{5,4},{6,7},{7,6},{8,9},{9,8},{10,11... | collective-permute-start | bytes 3538952 | tf_op jit(solution)/shard_map/ppermute | solution.py:187
  2.3 8.3 %collective-permute-start.2 = (bf16[32,1152]{1,0:T(8,128)(2,1)S(1)}, bf16[32,1152]{1,0:T(8,128)(2,1)S(1)}, u32[]{:S(2)}, u32[]{:S(2)}) collective-permute-start(bf16[32,1152]{1,0:T(8,128)(2,1)S(1)} %get-tuple-element.32), channel_id=1, source_target_pairs={{0,4},{1,5},{2,6},{3,7},{4,0},{5,1},{6,2},{7,3},{8,12},{9,13},{10,... | collective-permute-start | bytes 221192 | tf_op jit(solution)/shard_map/ppermute | solution.py:187
  5.9 11.1 %collective-permute-start.3 = (bf16[64,1152]{1,0:T(8,128)(2,1)S(1)}, bf16[64,1152]{1,0:T(8,128)(2,1)S(1)}, u32[]{:S(2)}, u32[]{:S(2)}) collective-permute-start(bf16[64,1152]{1,0:T(8,128)(2,1)S(1)} %get-tuple-element.31.refs_0_), channel_id=1, source_target_pairs={{0,2},{1,3},{2,0},{3,1},{4,6},{5,7},{6,4},{7,5},{8,10},{9,11},{10,... | collective-permute-start | bytes 442376 | tf_op jit(solution)/shard_map/ppermute | solution.py:187
  7.5 8.8 %collective-permute-start.6 = (bf16[32,1152]{1,0:T(8,128)(2,1)S(1)}, bf16[32,1152]{1,0:T(8,128)(2,1)S(1)}, u32[]{:S(2)}, u32[]{:S(2)}) collective-permute-start(bf16[32,1152]{1,0:T(8,128)(2,1)S(1)} %get-tuple-element.33), channel_id=1, source_target_pairs={{0,4},{1,5},{2,6},{3,7},{4,0},{5,1},{6,2},{7,3},{8,12},{9,13},{10,... | collective-permute-start | bytes 221192 | tf_op jit(solution)/shard_map/ppermute | solution.py:187
  7.8 8.9 %collective-permute-start.5 = (bf16[32,1152]{1,0:T(8,128)(2,1)S(1)}, bf16[32,1152]{1,0:T(8,128)(2,1)S(1)}, u32[]{:S(2)}, u32[]{:S(2)}) collective-permute-start(bf16[32,1152]{1,0:T(8,128)(2,1)S(1)} %get-tuple-element.33), channel_id=1, source_target_pairs={{0,6},{1,7},{2,4},{3,5},{4,2},{5,3},{6,0},{7,1},{8,14},{9,15},{10,... | collective-permute-start | bytes 221192 | tf_op jit(solution)/shard_map/ppermute | solution.py:187
  10.5 6.5 %collective-permute-start.4 = (bf16[32,1152]{1,0:T(8,128)(2,1)S(1)}, bf16[32,1152]{1,0:T(8,128)(2,1)S(1)}, u32[]{:S(2)}, u32[]{:S(2)}) collective-permute-start(bf16[32,1152]{1,0:T(8,128)(2,1)S(1)} %collective-permute-done.2.refs_1_), channel_id=1, source_target_pairs={{0,2},{1,3},{2,0},{3,1},{4,6},{5,7},{6,4},{7,5},{8,10},{9,11},{10,... | collective-permute-start | bytes 221192 | tf_op jit(solution)/shard_map/ppermute | solution.py:187
  11.2 2.8 %collective-permute-start.1 = (s32[1,256]{1,0:T(1,128)}, s32[1,256]{1,0:T(1,128)S(1)}, u32[]{:S(2)}, u32[]{:S(2)}) collective-permute-start(s32[1,256]{1,0:T(1,128)} %bitcast.3), channel_id=1, source_target_pairs={{0,1},{1,0},{2,3},{3,2},{4,5},{5,4},{6,7},{7,6},{8,9},{9,8},{10,11... | collective-permute-start | bytes 3080 | tf_op jit(solution)/shard_map/ppermute | solution.py:187
  14.0 4.1 %copy-start = (s32[256]{0:T(256)S(1)}, s32[256]{0:T(256)}, u32[]{:S(2)}) copy-start(s32[256]{0:T(256)} %param.7) | copy-start | bytes 3076
  18.1 2.1 %collective-permute-start.7 = (bf16[256,1152]{1,0:T(8,128)(2,1)S(1)}, bf16[256,1152]{1,0:T(8,128)(2,1)S(1)}, u32[]{:S(2)}, u32[]{:S(2)}) collective-permute-start(bf16[256,1152]{1,0:T(8,128)(2,1)S(1)} %get-tuple-element.36), channel_id=1, source_target_pairs={{0,1},{1,0},{2,3},{3,2},{4,5},{5,4},{6,7},{7,6},{8,9},{9,8},{10,11... | collective-permute-start | bytes 1769480 | tf_op jit(solution)/shard_map/ppermute | solution.py:187
  20.3 6.9 %collective-permute-start.8 = (bf16[64,1152]{1,0:T(8,128)(2,1)S(1)}, bf16[64,1152]{1,0:T(8,128)(2,1)S(1)}, u32[]{:S(2)}, u32[]{:S(2)}) collective-permute-start(bf16[64,1152]{1,0:T(8,128)(2,1)S(1)} %get-tuple-element.42), channel_id=1, source_target_pairs={{0,8},{1,25},{2,10},{3,27},{4,12},{5,29},{6,14},{7,31},{8,0},{9,17... | collective-permute-start | bytes 442376 | tf_op jit(solution)/shard_map/ppermute | solution.py:197
  21.9 8.6 %collective-permute-start.9 = (bf16[64,1152]{1,0:T(8,128)(2,1)S(1)}, bf16[64,1152]{1,0:T(8,128)(2,1)S(1)}, u32[]{:S(2)}, u32[]{:S(2)}) collective-permute-start(bf16[64,1152]{1,0:T(8,128)(2,1)S(1)} %get-tuple-element.43), channel_id=1, source_target_pairs={{0,16},{1,9},{2,18},{3,11},{4,20},{5,13},{6,22},{7,15},{8,24},{9,1... | collective-permute-start | bytes 442376 | tf_op jit(solution)/shard_map/ppermute | solution.py:197
  23.4 7.1 %collective-permute-start.10 = (bf16[64,1152]{1,0:T(8,128)(2,1)S(1)}, bf16[64,1152]{1,0:T(8,128)(2,1)S(1)}, u32[]{:S(2)}, u32[]{:S(2)}) collective-permute-start(bf16[64,1152]{1,0:T(8,128)(2,1)S(1)} %get-tuple-element.44), channel_id=1, source_target_pairs={{0,24},{1,17},{2,26},{3,19},{4,28},{5,21},{6,30},{7,23},{8,16},{9,... | collective-permute-start | bytes 442376 | tf_op jit(solution)/shard_map/ppermute | solution.py:197
  23.8 10.0 %collective-permute-start.12 = (bf16[64,1152]{1,0:T(8,128)(2,1)S(1)}, bf16[64,1152]{1,0:T(8,128)(2,1)S(1)}, u32[]{:S(2)}, u32[]{:S(2)}) collective-permute-start(bf16[64,1152]{1,0:T(8,128)(2,1)S(1)} %get-tuple-element.45), channel_id=1, source_target_pairs={{0,2},{1,3},{2,0},{3,1},{4,6},{5,7},{6,4},{7,5},{8,10},{9,11},{10,... | collective-permute-start | bytes 442376 | tf_op jit(solution)/shard_map/ppermute | solution.py:187
  25.3 13.6 %collective-permute-start.13 = (bf16[64,1152]{1,0:T(8,128)(2,1)S(1)}, bf16[64,1152]{1,0:T(8,128)(2,1)S(1)}, u32[]{:S(2)}, u32[]{:S(2)}) collective-permute-start(bf16[64,1152]{1,0:T(8,128)(2,1)S(1)} %get-tuple-element.46), channel_id=1, source_target_pairs={{0,4},{1,5},{2,6},{3,7},{4,0},{5,1},{6,2},{7,3},{8,12},{9,13},{10,... | collective-permute-start | bytes 442376 | tf_op jit(solution)/shard_map/ppermute | solution.py:187
  27.2 11.7 %collective-permute-start.14 = (bf16[64,1152]{1,0:T(8,128)(2,1)S(1)}, bf16[64,1152]{1,0:T(8,128)(2,1)S(1)}, u32[]{:S(2)}, u32[]{:S(2)}) collective-permute-start(bf16[64,1152]{1,0:T(8,128)(2,1)S(1)} %get-tuple-element.47), channel_id=1, source_target_pairs={{0,6},{1,7},{2,4},{3,5},{4,2},{5,3},{6,0},{7,1},{8,14},{9,15},{10,... | collective-permute-start | bytes 442376 | tf_op jit(solution)/shard_map/ppermute | solution.py:187
  30.7 8.2 %collective-permute-start.11 = (bf16[64,1152]{1,0:T(8,128)(2,1)S(1)}, bf16[64,1152]{1,0:T(8,128)(2,1)S(1)}, u32[]{:S(2)}, u32[]{:S(2)}) collective-permute-start(bf16[64,1152]{1,0:T(8,128)(2,1)S(1)} %shard_map.73.refs_0_), channel_id=1, source_target_pairs={{0,8},{8,0},{16,24},{24,16},{1,9},{9,1},{17,25},{25,17},{2,10},{10... | collective-permute-start | bytes 442376 | tf_op jit(solution)/shard_map/ppermute | solution.py:187
  32.1 8.8 %collective-permute-start.16 = (bf16[64,1152]{1,0:T(8,128)(2,1)S(1)}, bf16[64,1152]{1,0:T(8,128)(2,1)S(1)}, u32[]{:S(2)}, u32[]{:S(2)}) collective-permute-start(bf16[64,1152]{1,0:T(8,128)(2,1)S(1)} %shard_map.73.refs_0_), channel_id=1, source_target_pairs={{0,16},{8,24},{16,0},{24,8},{1,17},{9,25},{17,1},{25,9},{2,18},{10... | collective-permute-start | bytes 442376 | tf_op jit(solution)/shard_map/ppermute | solution.py:187
  33.8 7.0 %collective-permute-start.15 = (bf16[64,1152]{1,0:T(8,128)(2,1)S(1)}, bf16[64,1152]{1,0:T(8,128)(2,1)S(1)}, u32[]{:S(2)}, u32[]{:S(2)}) collective-permute-start(bf16[64,1152]{1,0:T(8,128)(2,1)S(1)} %shard_map.73.refs_0_), channel_id=1, source_target_pairs={{0,24},{8,16},{16,8},{24,0},{1,25},{9,17},{17,9},{25,1},{2,26},{10... | collective-permute-start | bytes 442376 | tf_op jit(solution)/shard_map/ppermute | solution.py:187

commit v18 on v15

--- a/solution.py
+++ b/solution.py
@@ -265,7 +265,7 @@
     )
     (own_txt, *send_txt), (keep, *send) = outs[:blocks], outs[blocks:]
     got = [swapped(send[k - 1], "img", k) for k in range(1, count)]
-    homes = sorted(zip(order[1:], send_txt), key=lambda pair: pair[0])
+    homes = sorted(zip(order[1:], send_txt), key=lambda pair: (pair[0] % 2, pair[0]))
     back = [swapped(block, "txt", 2 * k) for k, block in homes]
     (grad_part,) = call(
         finish_img_body,

time: 41.2 us -> 44.3 us (1.075)
  waiting for transfers between devices: 9.38 us -> 11.4 us
  starting transfers between devices: 22.3 us -> 23.5 us
    ppermute x17, waiting for transfers between devices: 9.38 us -> 11.4 us  [swapped(): return lax.ppermute(value, axis, [(s, s ^ step) for s in range(count)])]
    ppermute x17, starting transfers between devices: 22.3 us -> 23.5 us  [swapped(): return lax.ppermute(value, axis, [(s, s ^ step) for s in range(count)])]
  transfers between devices with their start and end apart: 17 -> 17, of which waited for: 8 -> 8; matrix products, arithmetic and copies ran while one was open for 0% -> 0% of each run, Pallas kernels for 13% -> 12%
where the time goes in v18:
time: 44.3 us; the launch traced here: 44.1 us
  starting transfers between devices  23.5 us (53%)
  waiting for transfers between devices  11.4 us (26%)
  Pallas kernels  7.21 us (16%)
  between operations  2.03 us (5%)
    ppermute x17, starting transfers between devices, swapped(): return lax.ppermute(value, axis, [(s, s ^ step) for s in range(count)])  23.5 us
    ppermute x17, waiting for transfers between devices, swapped(): return lax.ppermute(value, axis, [(s, s ^ step) for s in range(count)])  11.4 us
    pallas_call x6, Pallas kernels, call(): pl.pallas_call(body, out_shape=outs, in_specs=specs, out_specs=[VMEM] * l...  5.31 us
    pallas_call x1, Pallas kernels, local(): pl.pallas_call(functools.partial(first_body, partners[:early]), out_shape...  1.05 us
  transfers between devices with their start and end apart: 17, of which 8 were waited for; matrix products, arithmetic and copies ran while one was open for 0% of the time, Pallas kernels for 12%

profile of v18, /device:TPU:0, one launch (start us, length us, event | category | flops | bytes accessed | tf_op | source)
XLA Modules:
  0.0 44.1 jit_solution(7671369721814861971)
XLA Ops:
  0.6 0.5 %collective-permute-start = (f32[256,1152]{1,0:T(8,128)}, f32[256,1152]{1,0:T(8,128)S(1)}, u32[]{:S(2)}, u32[]{:S(2)}) collective-permute-start(f32[256,1152]{1,0:T(8,128)} %source.3), channel_id=1, source_target_pairs={{0,1},{1,0},{2,3},{3,2},{4,5},{5,4},{6,7},{7,6},{8,9},{9,8},{10,11... | collective-permute-start | bytes 3538952 | tf_op jit(solution)/shard_map/ppermute | solution.py:189
  1.1 1.1 %shard_map.68 = (bf16[64,1152]{1,0:T(8,128)(2,1)S(1)}, bf16[32,1152]{1,0:T(8,128)(2,1)S(1)}, bf16[32,1152]{1,0:T(8,128)(2,1)S(1)}, f32[64,1152]{1,0:T(8,128)S(1)}, f32[64,128]{1,0:T(8,128)S(1)}) custom-call(f32[64,1152]{1,0:T(8,128)} %source.2), custom_call_target="tpu_custom_call" | custom-call | flops 294912 | bytes 917504 | tf_op jit(solution)/shard_map/pallas_call | solution.py:25
  2.3 3.7 %collective-permute-start.2 = (bf16[32,1152]{1,0:T(8,128)(2,1)S(1)}, bf16[32,1152]{1,0:T(8,128)(2,1)S(1)}, u32[]{:S(2)}, u32[]{:S(2)}) collective-permute-start(bf16[32,1152]{1,0:T(8,128)(2,1)S(1)} %get-tuple-element.32), channel_id=1, source_target_pairs={{0,4},{1,5},{2,6},{3,7},{4,0},{5,1},{6,2},{7,3},{8,12},{9,13},{10,... | collective-permute-start | bytes 221192 | tf_op jit(solution)/shard_map/ppermute | solution.py:189
  5.9 1.6 %collective-permute-start.3 = (bf16[64,1152]{1,0:T(8,128)(2,1)S(1)}, bf16[64,1152]{1,0:T(8,128)(2,1)S(1)}, u32[]{:S(2)}, u32[]{:S(2)}) collective-permute-start(bf16[64,1152]{1,0:T(8,128)(2,1)S(1)} %get-tuple-element.31.refs_0_), channel_id=1, source_target_pairs={{0,2},{1,3},{2,0},{3,1},{4,6},{5,7},{6,4},{7,5},{8,10},{9,11},{10,... | collective-permute-start | bytes 442376 | tf_op jit(solution)/shard_map/ppermute | solution.py:189
  7.5 0.3 collective-permute-start.6
  7.8 2.5 %collective-permute-start.5 = (bf16[32,1152]{1,0:T(8,128)(2,1)S(1)}, bf16[32,1152]{1,0:T(8,128)(2,1)S(1)}, u32[]{:S(2)}, u32[]{:S(2)}) collective-permute-start(bf16[32,1152]{1,0:T(8,128)(2,1)S(1)} %get-tuple-element.33), channel_id=1, source_target_pairs={{0,6},{1,7},{2,4},{3,5},{4,2},{5,3},{6,0},{7,1},{8,14},{9,15},{10,... | collective-permute-start | bytes 221192 | tf_op jit(solution)/shard_map/ppermute | solution.py:189
  10.3 0.2 collective-permute-done.2.refs_1_
  10.5 0.7 %collective-permute-start.4 = (bf16[32,1152]{1,0:T(8,128)(2,1)S(1)}, bf16[32,1152]{1,0:T(8,128)(2,1)S(1)}, u32[]{:S(2)}, u32[]{:S(2)}) collective-permute-start(bf16[32,1152]{1,0:T(8,128)(2,1)S(1)} %collective-permute-done.2.refs_1_), channel_id=1, source_target_pairs={{0,2},{1,3},{2,0},{3,1},{4,6},{5,7},{6,4},{7,5},{8,10},{9,11},{10,... | collective-permute-start | bytes 221192 | tf_op jit(solution)/shard_map/ppermute | solution.py:189
  11.2 0.0 collective-permute-done.other
  11.2 0.0 collective-permute-start.1
  12.5 1.5 %shard_map.69 = (bf16[256,1152]{1,0:T(8,128)(2,1)S(1)}, bf16[256,1152]{1,0:T(8,128)(2,1)S(1)}, bf16[1152,256]{1,0:T(8,128)(2,1)S(1)}, f32[64,1152]{1,0:T(8,128)S(1)}, f32[64,128]{1,0:T(8,128)S(1)}) custom-call(s32[1]{0:T(128)} %bitcast.place, f32[256,1152]{1,0:T(8,128)S(1)} %collective-permute-done.other, f32[256,1152]{1,0:T(8,128)} %source.3), custom_call_target="tpu_custom_call" | custom-call | flops 2359296 | bytes 4456452 | tf_op jit(solution)/shard_map/pallas_call | solution.py:25
  14.0 0.0 copy-start
  14.0 0.0 collective-permute-done.1.perm
  14.1 2.3 %collective-permute-done.6.refs_5_ = bf16[32,1152]{1,0:T(8,128)(2,1)S(1)} collective-permute-done((bf16[32,1152]{1,0:T(8,128)(2,1)S(1)}, bf16[32,1152]{1,0:T(8,128)(2,1)S(1)}, u32[]{:S(2)}, u32[]{:S(2)}) %collective-permute-start.6) | collective-permute-done | bytes 73760 | tf_op jit(solution)/shard_map/ppermute | solution.py:189
  16.3 0.4 collective-permute-done.5.refs_4_
  16.7 0.3 collective-permute-done.4.refs_3_
  17.0 0.0 collective-permute-done.3.refs_2_
  17.1 1.0 %shard_map.70 = (bf16[256,256]{1,0:T(8,128)(2,1)S(1)}, bf16[256,1152]{1,0:T(8,128)(2,1)S(1)}) custom-call(s32[1]{0:T(128)} %bitcast.place, s32[1]{0:T(128)} %bitcast.1.column, f32[1]{0:T(128)S(6)} %copy.9.scale, f32[1]{0:T(128)S(6)} %copy.10.shift, s32[1,256]{1,0:T(1,128)S(1)} %collective-permute-done.1.perm, ...), custom_call_target="tpu_custom_call" | custom-call | flops 301989888 | bytes 1901584 | tf_op jit(solution)/shard_map/pallas_call | solution.py:25
  18.1 0.1 collective-permute-start.7
  18.1 0.0 copy-done
  18.1 1.4 %shard_map.71 = (f32[256,1152]{1,0:T(8,128)S(1)}, f32[256,1152]{1,0:T(8,128)S(1)}) custom-call(s32[1]{0:T(128)} %bitcast.place, s32[1]{0:T(128)} %bitcast.1.column, f32[1]{0:T(128)S(6)} %copy.9.scale, f32[1]{0:T(128)S(6)} %copy.10.shift, s32[1,256]{1,0:T(1,128)S(1)} %bitcast.4, bf16[256,1152]{1,0:T(8,128)(2,1)S(1)} %get-tuple-element.28.img, ...), custom_call_target="tpu_custom_call" | custom-call | flops 603979776 | bytes 4260880 | tf_op jit(solution)/shard_map/pallas_call | solution.py:25
  19.5 0.6 %collective-permute-done.7.other = bf16[256,1152]{1,0:T(8,128)(2,1)S(1)} collective-permute-done((bf16[256,1152]{1,0:T(8,128)(2,1)S(1)}, bf16[256,1152]{1,0:T(8,128)(2,1)S(1)}, u32[]{:S(2)}, u32[]{:S(2)}) %collective-permute-start.7) | collective-permute-done | bytes 589856 | tf_op jit(solution)/shard_map/ppermute | solution.py:189
  20.1 0.2 shard_map.72
  20.3 1.6 %collective-permute-start.8 = (bf16[64,1152]{1,0:T(8,128)(2,1)S(1)}, bf16[64,1152]{1,0:T(8,128)(2,1)S(1)}, u32[]{:S(2)}, u32[]{:S(2)}) collective-permute-start(bf16[64,1152]{1,0:T(8,128)(2,1)S(1)} %get-tuple-element.42), channel_id=1, source_target_pairs={{0,8},{8,0},{16,24},{24,16},{1,9},{9,1},{17,25},{25,17},{2,10},{10... | collective-permute-start | bytes 442376 | tf_op jit(solution)/shard_map/ppermute | solution.py:189
  21.9 1.5 %collective-permute-start.9 = (bf16[64,1152]{1,0:T(8,128)(2,1)S(1)}, bf16[64,1152]{1,0:T(8,128)(2,1)S(1)}, u32[]{:S(2)}, u32[]{:S(2)}) collective-permute-start(bf16[64,1152]{1,0:T(8,128)(2,1)S(1)} %get-tuple-element.43), channel_id=1, source_target_pairs={{0,16},{8,24},{16,0},{24,8},{1,17},{9,25},{17,1},{25,9},{2,18},{10... | collective-permute-start | bytes 442376 | tf_op jit(solution)/shard_map/ppermute | solution.py:189
  23.4 0.4 collective-permute-start.10
  23.8 2.4 %collective-permute-start.12 = (bf16[64,1152]{1,0:T(8,128)(2,1)S(1)}, bf16[64,1152]{1,0:T(8,128)(2,1)S(1)}, u32[]{:S(2)}, u32[]{:S(2)}) collective-permute-start(bf16[64,1152]{1,0:T(8,128)(2,1)S(1)} %get-tuple-element.45), channel_id=1, source_target_pairs={{0,4},{1,5},{2,6},{3,7},{4,0},{5,1},{6,2},{7,3},{8,12},{9,13},{10,... | collective-permute-start | bytes 442376 | tf_op jit(solution)/shard_map/ppermute | solution.py:189
  26.2 1.0 %collective-permute-start.13 = (bf16[64,1152]{1,0:T(8,128)(2,1)S(1)}, bf16[64,1152]{1,0:T(8,128)(2,1)S(1)}, u32[]{:S(2)}, u32[]{:S(2)}) collective-permute-start(bf16[64,1152]{1,0:T(8,128)(2,1)S(1)} %get-tuple-element.46), channel_id=1, source_target_pairs={{0,2},{1,3},{2,0},{3,1},{4,6},{5,7},{6,4},{7,5},{8,10},{9,11},{10,... | collective-permute-start | bytes 442376 | tf_op jit(solution)/shard_map/ppermute | solution.py:189
  27.2 0.0 collective-permute-done.8.refs_0_
  27.2 2.5 %collective-permute-start.14 = (bf16[64,1152]{1,0:T(8,128)(2,1)S(1)}, bf16[64,1152]{1,0:T(8,128)(2,1)S(1)}, u32[]{:S(2)}, u32[]{:S(2)}) collective-permute-start(bf16[64,1152]{1,0:T(8,128)(2,1)S(1)} %get-tuple-element.47), channel_id=1, source_target_pairs={{0,6},{1,7},{2,4},{3,5},{4,2},{5,3},{6,0},{7,1},{8,14},{9,15},{10,... | collective-permute-start | bytes 442376 | tf_op jit(solution)/shard_map/ppermute | solution.py:189
  29.7 0.9 %collective-permute-done.9.refs_1_ = bf16[64,1152]{1,0:T(8,128)(2,1)S(1)} collective-permute-done((bf16[64,1152]{1,0:T(8,128)(2,1)S(1)}, bf16[64,1152]{1,0:T(8,128)(2,1)S(1)}, u32[]{:S(2)}, u32[]{:S(2)}) %collective-permute-start.9) | collective-permute-done | bytes 147488 | tf_op jit(solution)/shard_map/ppermute | solution.py:189
  30.7 0.0 collective-permute-done.10.refs_2_
  30.7 0.2 shard_map.73.refs_0_
  30.9 1.3 %collective-permute-start.11 = (bf16[64,1152]{1,0:T(8,128)(2,1)S(1)}, bf16[64,1152]{1,0:T(8,128)(2,1)S(1)}, u32[]{:S(2)}, u32[]{:S(2)}) collective-permute-start(bf16[64,1152]{1,0:T(8,128)(2,1)S(1)} %shard_map.73.refs_0_), channel_id=1, source_target_pairs={{0,8},{8,0},{16,24},{24,16},{1,9},{9,1},{17,25},{25,17},{2,10},{10... | collective-permute-start | bytes 442376 | tf_op jit(solution)/shard_map/ppermute | solution.py:189
  32.2 1.0 %collective-permute-start.16 = (bf16[64,1152]{1,0:T(8,128)(2,1)S(1)}, bf16[64,1152]{1,0:T(8,128)(2,1)S(1)}, u32[]{:S(2)}, u32[]{:S(2)}) collective-permute-start(bf16[64,1152]{1,0:T(8,128)(2,1)S(1)} %shard_map.73.refs_0_), channel_id=1, source_target_pairs={{0,16},{8,24},{16,0},{24,8},{1,17},{9,25},{17,1},{25,9},{2,18},{10... | collective-permute-start | bytes 442376 | tf_op jit(solution)/shard_map/ppermute | solution.py:189
  33.1 4.1 %collective-permute-done.12.refs_2_ = bf16[64,1152]{1,0:T(8,128)(2,1)S(1)} collective-permute-done((bf16[64,1152]{1,0:T(8,128)(2,1)S(1)}, bf16[64,1152]{1,0:T(8,128)(2,1)S(1)}, u32[]{:S(2)}, u32[]{:S(2)}) %collective-permute-start.12) | collective-permute-done | bytes 147488 | tf_op jit(solution)/shard_map/ppermute | solution.py:189
  37.2 2.4 %collective-permute-start.15 = (bf16[64,1152]{1,0:T(8,128)(2,1)S(1)}, bf16[64,1152]{1,0:T(8,128)(2,1)S(1)}, u32[]{:S(2)}, u32[]{:S(2)}) collective-permute-start(bf16[64,1152]{1,0:T(8,128)(2,1)S(1)} %shard_map.73.refs_0_), channel_id=1, source_target_pairs={{0,24},{8,16},{16,8},{24,0},{1,25},{9,17},{17,9},{25,1},{2,26},{10... | collective-permute-start | bytes 442376 | tf_op jit(solution)/shard_map/ppermute | solution.py:189
  39.6 0.0 collective-permute-done.13.refs_3_
  39.6 0.0 collective-permute-done.14.refs_4_
  39.7 0.0 collective-permute-done.11.refs_1_
  39.7 1.1 %shard_map.74 = (f32[256,1152]{1,0:T(8,128)}, f32[64,1152]{1,0:T(8,128)}) custom-call(s32[1]{0:T(128)} %bitcast.place, f32[1]{0:T(128)S(6)} %copy.9.scale, f32[64,1152]{1,0:T(8,128)S(1)} %get-tuple-element.26.unit, f32[64,128]{1,0:T(8,128)S(1)} %get-tuple-element.27.inverse, f32[64,1152]{1,0:T(8,128)S(1)} %get-tuple-element.38.own, ...), custom_call_target="tpu_custom_call" | custom-call | flops 737280 | bytes 2359296 | tf_op jit(solution)/shard_map/pallas_call | solution.py:282
  40.7 0.0 collective-permute-done.16.refs_1_
  40.7 2.5 %collective-permute-done.15.refs_0_ = bf16[64,1152]{1,0:T(8,128)(2,1)S(1)} collective-permute-done((bf16[64,1152]{1,0:T(8,128)(2,1)S(1)}, bf16[64,1152]{1,0:T(8,128)(2,1)S(1)}, u32[]{:S(2)}, u32[]{:S(2)}) %collective-permute-start.15) | collective-permute-done | bytes 147488 | tf_op jit(solution)/shard_map/ppermute | solution.py:189
  43.2 0.8 %shard_map.75 = f32[256,1152]{1,0:T(8,128)} custom-call(s32[1]{0:T(128)} %bitcast.place, f32[256,1152]{1,0:T(8,128)} %get-tuple-element.48.begun, bf16[64,1152]{1,0:T(8,128)(2,1)S(1)} %collective-permute-done.15.refs_0_, bf16[64,1152]{1,0:T(8,128)(2,1)S(1)} %collective-permute-done.16.refs_1_), custom_call_target="tpu_custom_call", output_to_operand_aliasing={{}: (1, {})} | custom-call | flops 294912 | bytes 2359296 | tf_op jit(solution)/shard_map/pallas_call | solution.py:297
Async XLA Ops:
  0.6 10.6 %collective-permute-start = (f32[256,1152]{1,0:T(8,128)}, f32[256,1152]{1,0:T(8,128)S(1)}, u32[]{:S(2)}, u32[]{:S(2)}) collective-permute-start(f32[256,1152]{1,0:T(8,128)} %source.3), channel_id=1, source_target_pairs={{0,1},{1,0},{2,3},{3,2},{4,5},{5,4},{6,7},{7,6},{8,9},{9,8},{10,11... | collective-permute-start | bytes 3538952 | tf_op jit(solution)/shard_map/ppermute | solution.py:189
  2.3 8.3 %collective-permute-start.2 = (bf16[32,1152]{1,0:T(8,128)(2,1)S(1)}, bf16[32,1152]{1,0:T(8,128)(2,1)S(1)}, u32[]{:S(2)}, u32[]{:S(2)}) collective-permute-start(bf16[32,1152]{1,0:T(8,128)(2,1)S(1)} %get-tuple-element.32), channel_id=1, source_target_pairs={{0,4},{1,5},{2,6},{3,7},{4,0},{5,1},{6,2},{7,3},{8,12},{9,13},{10,... | collective-permute-start | bytes 221192 | tf_op jit(solution)/shard_map/ppermute | solution.py:189
  5.9 11.1 %collective-permute-start.3 = (bf16[64,1152]{1,0:T(8,128)(2,1)S(1)}, bf16[64,1152]{1,0:T(8,128)(2,1)S(1)}, u32[]{:S(2)}, u32[]{:S(2)}) collective-permute-start(bf16[64,1152]{1,0:T(8,128)(2,1)S(1)} %get-tuple-element.31.refs_0_), channel_id=1, source_target_pairs={{0,2},{1,3},{2,0},{3,1},{4,6},{5,7},{6,4},{7,5},{8,10},{9,11},{10,... | collective-permute-start | bytes 442376 | tf_op jit(solution)/shard_map/ppermute | solution.py:189
  7.5 8.8 %collective-permute-start.6 = (bf16[32,1152]{1,0:T(8,128)(2,1)S(1)}, bf16[32,1152]{1,0:T(8,128)(2,1)S(1)}, u32[]{:S(2)}, u32[]{:S(2)}) collective-permute-start(bf16[32,1152]{1,0:T(8,128)(2,1)S(1)} %get-tuple-element.33), channel_id=1, source_target_pairs={{0,4},{1,5},{2,6},{3,7},{4,0},{5,1},{6,2},{7,3},{8,12},{9,13},{10,... | collective-permute-start | bytes 221192 | tf_op jit(solution)/shard_map/ppermute | solution.py:189
  7.8 8.9 %collective-permute-start.5 = (bf16[32,1152]{1,0:T(8,128)(2,1)S(1)}, bf16[32,1152]{1,0:T(8,128)(2,1)S(1)}, u32[]{:S(2)}, u32[]{:S(2)}) collective-permute-start(bf16[32,1152]{1,0:T(8,128)(2,1)S(1)} %get-tuple-element.33), channel_id=1, source_target_pairs={{0,6},{1,7},{2,4},{3,5},{4,2},{5,3},{6,0},{7,1},{8,14},{9,15},{10,... | collective-permute-start | bytes 221192 | tf_op jit(solution)/shard_map/ppermute | solution.py:189
  10.5 6.5 %collective-permute-start.4 = (bf16[32,1152]{1,0:T(8,128)(2,1)S(1)}, bf16[32,1152]{1,0:T(8,128)(2,1)S(1)}, u32[]{:S(2)}, u32[]{:S(2)}) collective-permute-start(bf16[32,1152]{1,0:T(8,128)(2,1)S(1)} %collective-permute-done.2.refs_1_), channel_id=1, source_target_pairs={{0,2},{1,3},{2,0},{3,1},{4,6},{5,7},{6,4},{7,5},{8,10},{9,11},{10,... | collective-permute-start | bytes 221192 | tf_op jit(solution)/shard_map/ppermute | solution.py:189
  11.2 2.8 %collective-permute-start.1 = (s32[1,256]{1,0:T(1,128)}, s32[1,256]{1,0:T(1,128)S(1)}, u32[]{:S(2)}, u32[]{:S(2)}) collective-permute-start(s32[1,256]{1,0:T(1,128)} %bitcast.3), channel_id=1, source_target_pairs={{0,1},{1,0},{2,3},{3,2},{4,5},{5,4},{6,7},{7,6},{8,9},{9,8},{10,11... | collective-permute-start | bytes 3080 | tf_op jit(solution)/shard_map/ppermute | solution.py:189
  14.0 4.1 %copy-start = (s32[256]{0:T(256)S(1)}, s32[256]{0:T(256)}, u32[]{:S(2)}) copy-start(s32[256]{0:T(256)} %param.7) | copy-start | bytes 3076
  18.1 2.1 %collective-permute-start.7 = (bf16[256,1152]{1,0:T(8,128)(2,1)S(1)}, bf16[256,1152]{1,0:T(8,128)(2,1)S(1)}, u32[]{:S(2)}, u32[]{:S(2)}) collective-permute-start(bf16[256,1152]{1,0:T(8,128)(2,1)S(1)} %get-tuple-element.36), channel_id=1, source_target_pairs={{0,1},{1,0},{2,3},{3,2},{4,5},{5,4},{6,7},{7,6},{8,9},{9,8},{10,11... | collective-permute-start | bytes 1769480 | tf_op jit(solution)/shard_map/ppermute | solution.py:189
  20.3 6.9 %collective-permute-start.8 = (bf16[64,1152]{1,0:T(8,128)(2,1)S(1)}, bf16[64,1152]{1,0:T(8,128)(2,1)S(1)}, u32[]{:S(2)}, u32[]{:S(2)}) collective-permute-start(bf16[64,1152]{1,0:T(8,128)(2,1)S(1)} %get-tuple-element.42), channel_id=1, source_target_pairs={{0,8},{8,0},{16,24},{24,16},{1,9},{9,1},{17,25},{25,17},{2,10},{10... | collective-permute-start | bytes 442376 | tf_op jit(solution)/shard_map/ppermute | solution.py:189
  21.9 8.8 %collective-permute-start.9 = (bf16[64,1152]{1,0:T(8,128)(2,1)S(1)}, bf16[64,1152]{1,0:T(8,128)(2,1)S(1)}, u32[]{:S(2)}, u32[]{:S(2)}) collective-permute-start(bf16[64,1152]{1,0:T(8,128)(2,1)S(1)} %get-tuple-element.43), channel_id=1, source_target_pairs={{0,16},{8,24},{16,0},{24,8},{1,17},{9,25},{17,1},{25,9},{2,18},{10... | collective-permute-start | bytes 442376 | tf_op jit(solution)/shard_map/ppermute | solution.py:189
  23.4 7.3 %collective-permute-start.10 = (bf16[64,1152]{1,0:T(8,128)(2,1)S(1)}, bf16[64,1152]{1,0:T(8,128)(2,1)S(1)}, u32[]{:S(2)}, u32[]{:S(2)}) collective-permute-start(bf16[64,1152]{1,0:T(8,128)(2,1)S(1)} %get-tuple-element.44), channel_id=1, source_target_pairs={{0,24},{8,16},{16,8},{24,0},{1,25},{9,17},{17,9},{25,1},{2,26},{10... | collective-permute-start | bytes 442376 | tf_op jit(solution)/shard_map/ppermute | solution.py:189
  23.8 13.4 %collective-permute-start.12 = (bf16[64,1152]{1,0:T(8,128)(2,1)S(1)}, bf16[64,1152]{1,0:T(8,128)(2,1)S(1)}, u32[]{:S(2)}, u32[]{:S(2)}) collective-permute-start(bf16[64,1152]{1,0:T(8,128)(2,1)S(1)} %get-tuple-element.45), channel_id=1, source_target_pairs={{0,4},{1,5},{2,6},{3,7},{4,0},{5,1},{6,2},{7,3},{8,12},{9,13},{10,... | collective-permute-start | bytes 442376 | tf_op jit(solution)/shard_map/ppermute | solution.py:189
  26.2 13.4 %collective-permute-start.13 = (bf16[64,1152]{1,0:T(8,128)(2,1)S(1)}, bf16[64,1152]{1,0:T(8,128)(2,1)S(1)}, u32[]{:S(2)}, u32[]{:S(2)}) collective-permute-start(bf16[64,1152]{1,0:T(8,128)(2,1)S(1)} %get-tuple-element.46), channel_id=1, source_target_pairs={{0,2},{1,3},{2,0},{3,1},{4,6},{5,7},{6,4},{7,5},{8,10},{9,11},{10,... | collective-permute-start | bytes 442376 | tf_op jit(solution)/shard_map/ppermute | solution.py:189
  27.2 12.5 %collective-permute-start.14 = (bf16[64,1152]{1,0:T(8,128)(2,1)S(1)}, bf16[64,1152]{1,0:T(8,128)(2,1)S(1)}, u32[]{:S(2)}, u32[]{:S(2)}) collective-permute-start(bf16[64,1152]{1,0:T(8,128)(2,1)S(1)} %get-tuple-element.47), channel_id=1, source_target_pairs={{0,6},{1,7},{2,4},{3,5},{4,2},{5,3},{6,0},{7,1},{8,14},{9,15},{10,... | collective-permute-start | bytes 442376 | tf_op jit(solution)/shard_map/ppermute | solution.py:189
  30.9 8.8 %collective-permute-start.11 = (bf16[64,1152]{1,0:T(8,128)(2,1)S(1)}, bf16[64,1152]{1,0:T(8,128)(2,1)S(1)}, u32[]{:S(2)}, u32[]{:S(2)}) collective-permute-start(bf16[64,1152]{1,0:T(8,128)(2,1)S(1)} %shard_map.73.refs_0_), channel_id=1, source_target_pairs={{0,8},{8,0},{16,24},{24,16},{1,9},{9,1},{17,25},{25,17},{2,10},{10... | collective-permute-start | bytes 442376 | tf_op jit(solution)/shard_map/ppermute | solution.py:189
  32.2 8.6 %collective-permute-start.16 = (bf16[64,1152]{1,0:T(8,128)(2,1)S(1)}, bf16[64,1152]{1,0:T(8,128)(2,1)S(1)}, u32[]{:S(2)}, u32[]{:S(2)}) collective-permute-start(bf16[64,1152]{1,0:T(8,128)(2,1)S(1)} %shard_map.73.refs_0_), channel_id=1, source_target_pairs={{0,16},{8,24},{16,0},{24,8},{1,17},{9,25},{17,1},{25,9},{2,18},{10... | collective-permute-start | bytes 442376 | tf_op jit(solution)/shard_map/ppermute | solution.py:189
  37.2 6.0 %collective-permute-start.15 = (bf16[64,1152]{1,0:T(8,128)(2,1)S(1)}, bf16[64,1152]{1,0:T(8,128)(2,1)S(1)}, u32[]{:S(2)}, u32[]{:S(2)}) collective-permute-start(bf16[64,1152]{1,0:T(8,128)(2,1)S(1)} %shard_map.73.refs_0_), channel_id=1, source_target_pairs={{0,24},{8,16},{16,8},{24,0},{1,25},{9,17},{17,9},{25,1},{2,26},{10... | collective-permute-start | bytes 442376 | tf_op jit(solution)/shard_map/ppermute | solution.py:189

commit v19 on v15

--- a/solution.py
+++ b/solution.py
@@ -94,6 +94,15 @@
     return jnp.dot(weights, img, preferred_element_type=F32)
 
 
+def batch_body(*refs):
+    *pieces, out = refs
+    out[...] = joined(pieces)
+
+
+def half_body(source, out):
+    out[...] = source[out.shape[0] :, :]
+
+
 def joined(tiles):
     return jnp.concatenate([t[...] for t in tiles], axis=0)
 
@@ -107,11 +116,14 @@
 
 
 def own_body(slots, order, line, place, column, scale, shift, perm, img, img_other, kept, *refs):
-    *txt, own_sum, txt_sums = refs
+    *txt, own_sum, txt_sums, near_txt = refs
     tile = joined([txt[k] for k in slots])
     weights = weights_of(tile, order, line, place, column, scale, shift, perm[...], img[...])
     own_sum[...] = to_images(weights, tile)
-    txt_sums[...] = to_texts(weights, img[...]) + to_texts(kept[...], img_other[...])
+    sums = to_texts(weights, img[...]) + to_texts(kept[...], img_other[...])
+    txt_sums[...] = sums
+    near = order.index(1) * near_txt.shape[0]
+    near_txt[...] = sums[near : near + near_txt.shape[0]].astype(BF16)
 
 
 def split_body(count, blocks, place, own, other, txt_sums, *refs):
@@ -170,7 +182,8 @@
     parts = refs[:count]
     *back, img_out, txt_out, img_held, txt_held, sems = refs[count:]
     copies = quarter_copies(partners, place, parts, img_out, img_held, sems)
-    txt_held[...] = backward_unit(unit[...], inverse[...], scale[0] * total_of(own, back))
+    total = total_of(own, back[1:]) + back[0][: own.shape[0], :].astype(F32)
+    txt_held[...] = backward_unit(unit[...], inverse[...], scale[0] * total)
     copies.append(pltpu.make_async_copy(txt_held, txt_out, sems.at[count]))
     copies[-1].start()
     for copy in copies:
@@ -187,6 +200,11 @@
 def swapped(value, axis, step):
     count = lax.axis_size(axis)
     return lax.ppermute(value, axis, [(s, s ^ step) for s in range(count)])
+
+
+def sent(value, step, core):
+    line = lax.axis_size("txt")
+    return lax.ppermute(value, "txt", [(t, t ^ step) for t in range(core, line, 2)])
 
 
 def local(images, texts, perm, scale, shift):
@@ -244,9 +262,10 @@
         2 * pairs,
     )
     from_other = swapped(other_img, "txt", 1)
-    own_img, txt_sums = call(
+    own_img, txt_sums, near_txt = call(
         functools.partial(own_body, slots, order, line),
-        [struct(rows, width, F32), struct(blocks * txt_rows, width, F32)],
+        [struct(rows, width, F32), struct(blocks * txt_rows, width, F32)]
+        + [struct(txt_rows, width, BF16)],
         [*scalars, perm_row, img_bf, img_other, kept, *tiles],
         [SMEM] * 4 + [VMEM] * (4 + len(tiles)),
         40 << 20,
@@ -266,7 +285,20 @@
     (own_txt, *send_txt), (keep, *send) = outs[:blocks], outs[blocks:]
     got = [swapped(send[k - 1], "img", k) for k in range(1, count)]
     homes = sorted(zip(order[1:], send_txt), key=lambda pair: pair[0])
-    back = [swapped(block, "txt", 2 * k) for k, block in homes]
+    (both,) = call(
+        batch_body,
+        [struct(2 * txt_rows, width, BF16)],
+        [near_txt, sent(near_txt, 1, 0)],
+        [VMEM] * 2,
+        16 << 20,
+        txt_rows * width,
+    )
+    both = sent(both, 2, 1)
+    (other_half,) = call(
+        half_body, [struct(txt_rows, width, BF16)], [both], [VMEM], 16 << 20, txt_rows * width
+    )
+    back = [both, sent(other_half, 1, 1)]
+    back += [swapped(block, "txt", 2 * k) for k, block in homes[1:]]
     (grad_part,) = call(
         finish_img_body,
         [struct(part, width, BF16)],
@@ -282,7 +314,7 @@
     begun, grad_texts = pl.pallas_call(
         functools.partial(first_body, partners[:early]),
         out_shape=[struct(rows, width, F32), struct(txt_rows, width, F32)],
-        in_specs=[SMEM] * 2 + [VMEM] * (2 + early + blocks),
+        in_specs=[SMEM] * 2 + [VMEM] * (3 + early + blocks),
         out_specs=[ANY] * 2,
         scratch_shapes=[
             pltpu.VMEM((early * part, width), F32),

time: 41.2 us -> 46.6 us (1.13)
  starting transfers between devices: 22.3 us -> 24.7 us
  waiting for transfers between devices: 9.38 us -> 11.7 us
  Pallas kernels: 7.21 us -> 7.93 us
    ppermute x0 -> x3, starting transfers between devices: none -> 4.37 us  [sent(): lax.ppermute(value, 'txt', [(t, t ^ step) for t in range(core, line, 2)])]
    ppermute x17 -> x16, starting transfers between devices: 22.3 us -> 20.3 us  [swapped(): return lax.ppermute(value, axis, [(s, s ^ step) for s in range(count)])]
    ppermute x17 -> x16, waiting for transfers between devices: 9.38 us -> 10.7 us  [swapped(): return lax.ppermute(value, axis, [(s, s ^ step) for s in range(count)])]
    ppermute x0 -> x3, waiting for transfers between devices: none -> 0.99 us  [sent(): lax.ppermute(value, 'txt', [(t, t ^ step) for t in range(core, line, 2)])]
    pallas_call x6 -> x8, Pallas kernels: 5.31 us -> 6 us  [call(): pl.pallas_call(body, out_shape=outs, in_specs=specs, out_specs=[VMEM] * l...]
  transfers between devices with their start and end apart: 17 -> 19, of which waited for: 8 -> 8; matrix products, arithmetic and copies ran while one was open for 0% -> 0% of each run, Pallas kernels for 13% -> 13%
where the time goes in v19:
time: 46.6 us; the launch traced here: 46.3 us
  starting transfers between devices  24.7 us (53%)
  waiting for transfers between devices  11.7 us (25%)
  Pallas kernels  7.93 us (17%)
  between operations  2.06 us (4%)
    ppermute x16, starting transfers between devices, swapped(): return lax.ppermute(value, axis, [(s, s ^ step) for s in range(count)])  20.3 us
    ppermute x16, waiting for transfers between devices, swapped(): return lax.ppermute(value, axis, [(s, s ^ step) for s in range(count)])  10.7 us
    pallas_call x8, Pallas kernels, call(): pl.pallas_call(body, out_shape=outs, in_specs=specs, out_specs=[VMEM] * l...  6 us
    ppermute x3, starting transfers between devices, sent(): lax.ppermute(value, 'txt', [(t, t ^ step) for t in range(core, line, 2)])  4.37 us
    pallas_call x1, Pallas kernels, local(): pl.pallas_call(functools.partial(first_body, partners[:early]), out_shape...  1.08 us
    ppermute x3, waiting for transfers between devices, sent(): lax.ppermute(value, 'txt', [(t, t ^ step) for t in range(core, line, 2)])  0.99 us
  transfers between devices with their start and end apart: 19, of which 8 were waited for; matrix products, arithmetic and copies ran while one was open for 0% of the time, Pallas kernels for 13%

profile of v19, /device:TPU:0, one launch (start us, length us, event | category | flops | bytes accessed | tf_op | source)
XLA Modules:
  0.0 46.3 jit_solution(11339312593808590411)
XLA Ops:
  0.6 0.5 %collective-permute-start = (f32[256,1152]{1,0:T(8,128)}, f32[256,1152]{1,0:T(8,128)S(1)}, u32[]{:S(2)}, u32[]{:S(2)}) collective-permute-start(f32[256,1152]{1,0:T(8,128)} %source.3), channel_id=1, source_target_pairs={{0,1},{1,0},{2,3},{3,2},{4,5},{5,4},{6,7},{7,6},{8,9},{9,8},{10,11... | collective-permute-start | bytes 3538952 | tf_op jit(solution)/shard_map/ppermute | solution.py:202
  1.1 1.1 %shard_map.68 = (bf16[64,1152]{1,0:T(8,128)(2,1)S(1)}, bf16[32,1152]{1,0:T(8,128)(2,1)S(1)}, bf16[32,1152]{1,0:T(8,128)(2,1)S(1)}, f32[64,1152]{1,0:T(8,128)S(1)}, f32[64,128]{1,0:T(8,128)S(1)}) custom-call(f32[64,1152]{1,0:T(8,128)} %source.2), custom_call_target="tpu_custom_call" | custom-call | flops 294912 | bytes 917504 | tf_op jit(solution)/shard_map/pallas_call | solution.py:25
  2.3 3.7 %collective-permute-start.2 = (bf16[32,1152]{1,0:T(8,128)(2,1)S(1)}, bf16[32,1152]{1,0:T(8,128)(2,1)S(1)}, u32[]{:S(2)}, u32[]{:S(2)}) collective-permute-start(bf16[32,1152]{1,0:T(8,128)(2,1)S(1)} %get-tuple-element.32), channel_id=1, source_target_pairs={{0,4},{1,5},{2,6},{3,7},{4,0},{5,1},{6,2},{7,3},{8,12},{9,13},{10,... | collective-permute-start | bytes 221192 | tf_op jit(solution)/shard_map/ppermute | solution.py:202
  5.9 1.6 %collective-permute-start.3 = (bf16[64,1152]{1,0:T(8,128)(2,1)S(1)}, bf16[64,1152]{1,0:T(8,128)(2,1)S(1)}, u32[]{:S(2)}, u32[]{:S(2)}) collective-permute-start(bf16[64,1152]{1,0:T(8,128)(2,1)S(1)} %get-tuple-element.31.refs_0_), channel_id=1, source_target_pairs={{0,2},{1,3},{2,0},{3,1},{4,6},{5,7},{6,4},{7,5},{8,10},{9,11},{10,... | collective-permute-start | bytes 442376 | tf_op jit(solution)/shard_map/ppermute | solution.py:202
  7.5 0.3 collective-permute-start.6
  7.8 2.5 %collective-permute-start.5 = (bf16[32,1152]{1,0:T(8,128)(2,1)S(1)}, bf16[32,1152]{1,0:T(8,128)(2,1)S(1)}, u32[]{:S(2)}, u32[]{:S(2)}) collective-permute-start(bf16[32,1152]{1,0:T(8,128)(2,1)S(1)} %get-tuple-element.33), channel_id=1, source_target_pairs={{0,6},{1,7},{2,4},{3,5},{4,2},{5,3},{6,0},{7,1},{8,14},{9,15},{10,... | collective-permute-start | bytes 221192 | tf_op jit(solution)/shard_map/ppermute | solution.py:202
  10.3 0.2 collective-permute-done.2.refs_1_
  10.5 0.7 %collective-permute-start.4 = (bf16[32,1152]{1,0:T(8,128)(2,1)S(1)}, bf16[32,1152]{1,0:T(8,128)(2,1)S(1)}, u32[]{:S(2)}, u32[]{:S(2)}) collective-permute-start(bf16[32,1152]{1,0:T(8,128)(2,1)S(1)} %collective-permute-done.2.refs_1_), channel_id=1, source_target_pairs={{0,2},{1,3},{2,0},{3,1},{4,6},{5,7},{6,4},{7,5},{8,10},{9,11},{10,... | collective-permute-start | bytes 221192 | tf_op jit(solution)/shard_map/ppermute | solution.py:202
  11.2 0.0 collective-permute-done.other
  11.2 0.0 collective-permute-start.1
  12.5 1.5 %shard_map.69 = (bf16[256,1152]{1,0:T(8,128)(2,1)S(1)}, bf16[256,1152]{1,0:T(8,128)(2,1)S(1)}, bf16[1152,256]{1,0:T(8,128)(2,1)S(1)}, f32[64,1152]{1,0:T(8,128)S(1)}, f32[64,128]{1,0:T(8,128)S(1)}) custom-call(s32[1]{0:T(128)} %bitcast.place, f32[256,1152]{1,0:T(8,128)S(1)} %collective-permute-done.other, f32[256,1152]{1,0:T(8,128)} %source.3), custom_call_target="tpu_custom_call" | custom-call | flops 2359296 | bytes 4456452 | tf_op jit(solution)/shard_map/pallas_call | solution.py:25
  14.0 0.0 copy-start
  14.0 0.0 collective-permute-done.1.perm
  14.1 2.3 %collective-permute-done.6.refs_5_ = bf16[32,1152]{1,0:T(8,128)(2,1)S(1)} collective-permute-done((bf16[32,1152]{1,0:T(8,128)(2,1)S(1)}, bf16[32,1152]{1,0:T(8,128)(2,1)S(1)}, u32[]{:S(2)}, u32[]{:S(2)}) %collective-permute-start.6) | collective-permute-done | bytes 73760 | tf_op jit(solution)/shard_map/ppermute | solution.py:202
  16.3 0.4 collective-permute-done.5.refs_4_
  16.7 0.3 collective-permute-done.4.refs_3_
  17.0 0.0 collective-permute-done.3.refs_2_
  17.1 1.0 %shard_map.70 = (bf16[256,256]{1,0:T(8,128)(2,1)S(1)}, bf16[256,1152]{1,0:T(8,128)(2,1)S(1)}) custom-call(s32[1]{0:T(128)} %bitcast.place, s32[1]{0:T(128)} %bitcast.1.column, f32[1]{0:T(128)S(6)} %copy.9.scale, f32[1]{0:T(128)S(6)} %copy.10.shift, s32[1,256]{1,0:T(1,128)S(1)} %collective-permute-done.1.perm, ...), custom_call_target="tpu_custom_call" | custom-call | flops 301989888 | bytes 1901584 | tf_op jit(solution)/shard_map/pallas_call | solution.py:25
  18.1 0.1 collective-permute-start.7
  18.1 0.0 copy-done
  18.1 1.4 %shard_map.71 = (f32[256,1152]{1,0:T(8,128)S(1)}, f32[256,1152]{1,0:T(8,128)S(1)}, bf16[64,1152]{1,0:T(8,128)(2,1)S(1)}) custom-call(s32[1]{0:T(128)} %bitcast.place, s32[1]{0:T(128)} %bitcast.1.column, f32[1]{0:T(128)S(6)} %copy.9.scale, f32[1]{0:T(128)S(6)} %copy.10.shift, s32[1,256]{1,0:T(1,128)S(1)} %bitcast.4, ...), custom_call_target="tpu_custom_call" | custom-call | flops 603979776 | bytes 4408336 | tf_op jit(solution)/shard_map/pallas_call | solution.py:25
  19.5 2.4 %collective-permute-start.12 = (bf16[64,1152]{1,0:T(8,128)(2,1)S(1)}, bf16[64,1152]{1,0:T(8,128)(2,1)S(1)}, u32[]{:S(2)}, u32[]{:S(2)}) collective-permute-start(bf16[64,1152]{1,0:T(8,128)(2,1)S(1)} %get-tuple-element.45.refs_0_), channel_id=1, source_target_pairs={{0,1},{2,3},{4,5},{6,7},{8,9},{10,11},{12,13},{14,15},{16,17},{18,... | collective-permute-start | bytes 442376 | tf_op jit(solution)/shard_map/ppermute | solution.py:207
  21.9 1.0 %collective-permute-done.12.refs_1_ = bf16[64,1152]{1,0:T(8,128)(2,1)S(1)} collective-permute-done((bf16[64,1152]{1,0:T(8,128)(2,1)S(1)}, bf16[64,1152]{1,0:T(8,128)(2,1)S(1)}, u32[]{:S(2)}, u32[]{:S(2)}) %collective-permute-start.12) | collective-permute-done | bytes 147488 | tf_op jit(solution)/shard_map/ppermute | solution.py:207
  23.0 0.7 %collective-permute-start.13 = (bf16[128,1152]{1,0:T(8,128)(2,1)S(1)}, bf16[128,1152]{1,0:T(8,128)(2,1)S(1)}, u32[]{:S(2)}, u32[]{:S(2)}) collective-permute-start(bf16[128,1152]{1,0:T(8,128)(2,1)S(1)} %shard_map.74), channel_id=1, source_target_pairs={{1,3},{3,1},{5,7},{7,5},{9,11},{11,9},{13,15},{15,13},{17,19},{19,... | collective-permute-start | bytes 884744 | tf_op jit(solution)/shard_map/ppermute | solution.py:207
  23.6 0.0 collective-permute-done.7.other
  23.6 0.8 %shard_map.72 = (f32[64,1152]{1,0:T(8,128)S(1)}, bf16[64,1152]{1,0:T(8,128)(2,1)S(1)}, bf16[64,1152]{1,0:T(8,128)(2,1)}, bf16[64,1152]{1,0:T(8,128)(2,1)S(1)}, f...) custom-call(s32[1]{0:T(128)} %bitcast.place, ...), custom_call_target="tpu_custom_call" | custom-call | flops 294912 | bytes 4423684 | tf_op jit(solution)/shard_map/pallas_call | solution.py:25
  24.5 1.5 %collective-permute-start.8 = (bf16[64,1152]{1,0:T(8,128)(2,1)S(1)}, bf16[64,1152]{1,0:T(8,128)(2,1)S(1)}, u32[]{:S(2)}, u32[]{:S(2)}) collective-permute-start(bf16[64,1152]{1,0:T(8,128)(2,1)S(1)} %get-tuple-element.42), channel_id=1, source_target_pairs={{0,8},{8,0},{16,24},{24,16},{1,9},{9,1},{17,25},{25,17},{2,10},{10... | collective-permute-start | bytes 442376 | tf_op jit(solution)/shard_map/ppermute | solution.py:202
  26.0 1.5 %collective-permute-start.9 = (bf16[64,1152]{1,0:T(8,128)(2,1)S(1)}, bf16[64,1152]{1,0:T(8,128)(2,1)S(1)}, u32[]{:S(2)}, u32[]{:S(2)}) collective-permute-start(bf16[64,1152]{1,0:T(8,128)(2,1)S(1)} %get-tuple-element.43), channel_id=1, source_target_pairs={{0,16},{8,24},{16,0},{24,8},{1,17},{9,25},{17,1},{25,9},{2,18},{10... | collective-permute-start | bytes 442376 | tf_op jit(solution)/shard_map/ppermute | solution.py:202
  27.5 0.4 collective-permute-start.10
  28.0 0.0 collective-permute-done.13.source.refs_2_
  28.0 1.3 %collective-permute-start.14 = (bf16[64,1152]{1,0:T(8,128)(2,1)S(1)}, bf16[64,1152]{1,0:T(8,128)(2,1)S(1)}, u32[]{:S(2)}, u32[]{:S(2)}) collective-permute-start(bf16[64,1152]{1,0:T(8,128)(2,1)S(1)} %shard_map.75), channel_id=1, source_target_pairs={{1,0},{3,2},{5,4},{7,6},{9,8},{11,10},{13,12},{15,14},{17,16},{19,... | collective-permute-start | bytes 442376 | tf_op jit(solution)/shard_map/ppermute | solution.py:207
  29.3 2.5 %collective-permute-start.15 = (bf16[64,1152]{1,0:T(8,128)(2,1)S(1)}, bf16[64,1152]{1,0:T(8,128)(2,1)S(1)}, u32[]{:S(2)}, u32[]{:S(2)}) collective-permute-start(bf16[64,1152]{1,0:T(8,128)(2,1)S(1)} %get-tuple-element.46), channel_id=1, source_target_pairs={{0,4},{1,5},{2,6},{3,7},{4,0},{5,1},{6,2},{7,3},{8,12},{9,13},{10,... | collective-permute-start | bytes 442376 | tf_op jit(solution)/shard_map/ppermute | solution.py:202
  31.7 0.0 collective-permute-done.8.refs_0_
  31.7 1.5 %collective-permute-start.16 = (bf16[64,1152]{1,0:T(8,128)(2,1)S(1)}, bf16[64,1152]{1,0:T(8,128)(2,1)S(1)}, u32[]{:S(2)}, u32[]{:S(2)}) collective-permute-start(bf16[64,1152]{1,0:T(8,128)(2,1)S(1)} %get-tuple-element.47), channel_id=1, source_target_pairs={{0,6},{1,7},{2,4},{3,5},{4,2},{5,3},{6,0},{7,1},{8,14},{9,15},{10,... | collective-permute-start | bytes 442376 | tf_op jit(solution)/shard_map/ppermute | solution.py:202
  33.2 0.0 collective-permute-done.9.refs_1_
  33.2 1.6 %collective-permute-done.10.refs_2_ = bf16[64,1152]{1,0:T(8,128)(2,1)S(1)} collective-permute-done((bf16[64,1152]{1,0:T(8,128)(2,1)S(1)}, bf16[64,1152]{1,0:T(8,128)(2,1)S(1)}, u32[]{:S(2)}, u32[]{:S(2)}) %collective-permute-start.10) | collective-permute-done | bytes 147488 | tf_op jit(solution)/shard_map/ppermute | solution.py:202
  34.8 0.2 shard_map.73.refs_0_
  35.0 0.9 %collective-permute-start.11 = (bf16[64,1152]{1,0:T(8,128)(2,1)S(1)}, bf16[64,1152]{1,0:T(8,128)(2,1)S(1)}, u32[]{:S(2)}, u32[]{:S(2)}) collective-permute-start(bf16[64,1152]{1,0:T(8,128)(2,1)S(1)} %shard_map.73.refs_0_), channel_id=1, source_target_pairs={{0,8},{8,0},{16,24},{24,16},{1,9},{9,1},{17,25},{25,17},{2,10},{10... | collective-permute-start | bytes 442376 | tf_op jit(solution)/shard_map/ppermute | solution.py:202
  35.9 0.6 %collective-permute-start.18 = (bf16[64,1152]{1,0:T(8,128)(2,1)S(1)}, bf16[64,1152]{1,0:T(8,128)(2,1)S(1)}, u32[]{:S(2)}, u32[]{:S(2)}) collective-permute-start(bf16[64,1152]{1,0:T(8,128)(2,1)S(1)} %shard_map.73.refs_0_), channel_id=1, source_target_pairs={{0,16},{8,24},{16,0},{24,8},{1,17},{9,25},{17,1},{25,9},{2,18},{10... | collective-permute-start | bytes 442376 | tf_op jit(solution)/shard_map/ppermute | solution.py:202
  36.5 0.0 collective-permute-done.14.refs_3_
  36.5 2.1 %collective-permute-start.17 = (bf16[64,1152]{1,0:T(8,128)(2,1)S(1)}, bf16[64,1152]{1,0:T(8,128)(2,1)S(1)}, u32[]{:S(2)}, u32[]{:S(2)}) collective-permute-start(bf16[64,1152]{1,0:T(8,128)(2,1)S(1)} %shard_map.73.refs_0_), channel_id=1, source_target_pairs={{0,24},{8,16},{16,8},{24,0},{1,25},{9,17},{17,9},{25,1},{2,26},{10... | collective-permute-start | bytes 442376 | tf_op jit(solution)/shard_map/ppermute | solution.py:202
  38.6 3.6 %collective-permute-done.15.refs_4_ = bf16[64,1152]{1,0:T(8,128)(2,1)S(1)} collective-permute-done((bf16[64,1152]{1,0:T(8,128)(2,1)S(1)}, bf16[64,1152]{1,0:T(8,128)(2,1)S(1)}, u32[]{:S(2)}, u32[]{:S(2)}) %collective-permute-start.15) | collective-permute-done | bytes 147488 | tf_op jit(solution)/shard_map/ppermute | solution.py:202
  42.2 0.0 collective-permute-done.16.refs_5_
  42.2 0.0 collective-permute-done.11.refs_1_
  42.2 1.1 %shard_map.76 = (f32[256,1152]{1,0:T(8,128)}, f32[64,1152]{1,0:T(8,128)}) custom-call(s32[1]{0:T(128)} %bitcast.place, f32[1]{0:T(128)S(6)} %copy.9.scale, f32[64,1152]{1,0:T(8,128)S(1)} %get-tuple-element.26.unit, f32[64,128]{1,0:T(8,128)S(1)} %get-tuple-element.27.inverse, f32[64,1152]{1,0:T(8,128)S(1)} %get-tuple-element.38.own, ...), custom_call_target="tpu_custom_call" | custom-call | flops 737280 | bytes 2359296 | tf_op jit(solution)/shard_map/pallas_call | solution.py:314
  43.3 2.2 %collective-permute-done.18.refs_1_ = bf16[64,1152]{1,0:T(8,128)(2,1)S(1)} collective-permute-done((bf16[64,1152]{1,0:T(8,128)(2,1)S(1)}, bf16[64,1152]{1,0:T(8,128)(2,1)S(1)}, u32[]{:S(2)}, u32[]{:S(2)}) %collective-permute-start.18) | collective-permute-done | bytes 147488 | tf_op jit(solution)/shard_map/ppermute | solution.py:202
  45.5 0.0 collective-permute-done.17.refs_0_
  45.5 0.8 %shard_map.77 = f32[256,1152]{1,0:T(8,128)} custom-call(s32[1]{0:T(128)} %bitcast.place, f32[256,1152]{1,0:T(8,128)} %get-tuple-element.48.begun, bf16[64,1152]{1,0:T(8,128)(2,1)S(1)} %collective-permute-done.17.refs_0_, bf16[64,1152]{1,0:T(8,128)(2,1)S(1)} %collective-permute-done.18.refs_1_), custom_call_target="tpu_custom_call", output_to_operand_aliasing={{}: (1, {})} | custom-call | flops 294912 | bytes 2359296 | tf_op jit(solution)/shard_map/pallas_call | solution.py:329
  (2 shorter events, 0.0 us)
Async XLA Ops:
  0.6 10.6 %collective-permute-start = (f32[256,1152]{1,0:T(8,128)}, f32[256,1152]{1,0:T(8,128)S(1)}, u32[]{:S(2)}, u32[]{:S(2)}) collective-permute-start(f32[256,1152]{1,0:T(8,128)} %source.3), channel_id=1, source_target_pairs={{0,1},{1,0},{2,3},{3,2},{4,5},{5,4},{6,7},{7,6},{8,9},{9,8},{10,11... | collective-permute-start | bytes 3538952 | tf_op jit(solution)/shard_map/ppermute | solution.py:202
  2.3 8.3 %collective-permute-start.2 = (bf16[32,1152]{1,0:T(8,128)(2,1)S(1)}, bf16[32,1152]{1,0:T(8,128)(2,1)S(1)}, u32[]{:S(2)}, u32[]{:S(2)}) collective-permute-start(bf16[32,1152]{1,0:T(8,128)(2,1)S(1)} %get-tuple-element.32), channel_id=1, source_target_pairs={{0,4},{1,5},{2,6},{3,7},{4,0},{5,1},{6,2},{7,3},{8,12},{9,13},{10,... | collective-permute-start | bytes 221192 | tf_op jit(solution)/shard_map/ppermute | solution.py:202
  5.9 11.1 %collective-permute-start.3 = (bf16[64,1152]{1,0:T(8,128)(2,1)S(1)}, bf16[64,1152]{1,0:T(8,128)(2,1)S(1)}, u32[]{:S(2)}, u32[]{:S(2)}) collective-permute-start(bf16[64,1152]{1,0:T(8,128)(2,1)S(1)} %get-tuple-element.31.refs_0_), channel_id=1, source_target_pairs={{0,2},{1,3},{2,0},{3,1},{4,6},{5,7},{6,4},{7,5},{8,10},{9,11},{10,... | collective-permute-start | bytes 442376 | tf_op jit(solution)/shard_map/ppermute | solution.py:202
  7.5 8.8 %collective-permute-start.6 = (bf16[32,1152]{1,0:T(8,128)(2,1)S(1)}, bf16[32,1152]{1,0:T(8,128)(2,1)S(1)}, u32[]{:S(2)}, u32[]{:S(2)}) collective-permute-start(bf16[32,1152]{1,0:T(8,128)(2,1)S(1)} %get-tuple-element.33), channel_id=1, source_target_pairs={{0,4},{1,5},{2,6},{3,7},{4,0},{5,1},{6,2},{7,3},{8,12},{9,13},{10,... | collective-permute-start | bytes 221192 | tf_op jit(solution)/shard_map/ppermute | solution.py:202
  7.8 8.9 %collective-permute-start.5 = (bf16[32,1152]{1,0:T(8,128)(2,1)S(1)}, bf16[32,1152]{1,0:T(8,128)(2,1)S(1)}, u32[]{:S(2)}, u32[]{:S(2)}) collective-permute-start(bf16[32,1152]{1,0:T(8,128)(2,1)S(1)} %get-tuple-element.33), channel_id=1, source_target_pairs={{0,6},{1,7},{2,4},{3,5},{4,2},{5,3},{6,0},{7,1},{8,14},{9,15},{10,... | collective-permute-start | bytes 221192 | tf_op jit(solution)/shard_map/ppermute | solution.py:202
  10.5 6.5 %collective-permute-start.4 = (bf16[32,1152]{1,0:T(8,128)(2,1)S(1)}, bf16[32,1152]{1,0:T(8,128)(2,1)S(1)}, u32[]{:S(2)}, u32[]{:S(2)}) collective-permute-start(bf16[32,1152]{1,0:T(8,128)(2,1)S(1)} %collective-permute-done.2.refs_1_), channel_id=1, source_target_pairs={{0,2},{1,3},{2,0},{3,1},{4,6},{5,7},{6,4},{7,5},{8,10},{9,11},{10,... | collective-permute-start | bytes 221192 | tf_op jit(solution)/shard_map/ppermute | solution.py:202
  11.2 2.8 %collective-permute-start.1 = (s32[1,256]{1,0:T(1,128)}, s32[1,256]{1,0:T(1,128)S(1)}, u32[]{:S(2)}, u32[]{:S(2)}) collective-permute-start(s32[1,256]{1,0:T(1,128)} %bitcast.3), channel_id=1, source_target_pairs={{0,1},{1,0},{2,3},{3,2},{4,5},{5,4},{6,7},{7,6},{8,9},{9,8},{10,11... | collective-permute-start | bytes 3080 | tf_op jit(solution)/shard_map/ppermute | solution.py:202
  14.0 4.1 %copy-start = (s32[256]{0:T(256)S(1)}, s32[256]{0:T(256)}, u32[]{:S(2)}) copy-start(s32[256]{0:T(256)} %param.7) | copy-start | bytes 3076
  18.1 5.6 %collective-permute-start.7 = (bf16[256,1152]{1,0:T(8,128)(2,1)S(1)}, bf16[256,1152]{1,0:T(8,128)(2,1)S(1)}, u32[]{:S(2)}, u32[]{:S(2)}) collective-permute-start(bf16[256,1152]{1,0:T(8,128)(2,1)S(1)} %get-tuple-element.36), channel_id=1, source_target_pairs={{0,1},{1,0},{2,3},{3,2},{4,5},{5,4},{6,7},{7,6},{8,9},{9,8},{10,11... | collective-permute-start | bytes 1769480 | tf_op jit(solution)/shard_map/ppermute | solution.py:202
  19.5 3.4 %collective-permute-start.12 = (bf16[64,1152]{1,0:T(8,128)(2,1)S(1)}, bf16[64,1152]{1,0:T(8,128)(2,1)S(1)}, u32[]{:S(2)}, u32[]{:S(2)}) collective-permute-start(bf16[64,1152]{1,0:T(8,128)(2,1)S(1)} %get-tuple-element.45.refs_0_), channel_id=1, source_target_pairs={{0,1},{2,3},{4,5},{6,7},{8,9},{10,11},{12,13},{14,15},{16,17},{18,... | collective-permute-start | bytes 442376 | tf_op jit(solution)/shard_map/ppermute | solution.py:207
  23.0 5.0 %collective-permute-start.13 = (bf16[128,1152]{1,0:T(8,128)(2,1)S(1)}, bf16[128,1152]{1,0:T(8,128)(2,1)S(1)}, u32[]{:S(2)}, u32[]{:S(2)}) collective-permute-start(bf16[128,1152]{1,0:T(8,128)(2,1)S(1)} %shard_map.74), channel_id=1, source_target_pairs={{1,3},{3,1},{5,7},{7,5},{9,11},{11,9},{13,15},{15,13},{17,19},{19,... | collective-permute-start | bytes 884744 | tf_op jit(solution)/shard_map/ppermute | solution.py:207
  24.5 7.3 %collective-permute-start.8 = (bf16[64,1152]{1,0:T(8,128)(2,1)S(1)}, bf16[64,1152]{1,0:T(8,128)(2,1)S(1)}, u32[]{:S(2)}, u32[]{:S(2)}) collective-permute-start(bf16[64,1152]{1,0:T(8,128)(2,1)S(1)} %get-tuple-element.42), channel_id=1, source_target_pairs={{0,8},{8,0},{16,24},{24,16},{1,9},{9,1},{17,25},{25,17},{2,10},{10... | collective-permute-start | bytes 442376 | tf_op jit(solution)/shard_map/ppermute | solution.py:202
  26.0 7.2 %collective-permute-start.9 = (bf16[64,1152]{1,0:T(8,128)(2,1)S(1)}, bf16[64,1152]{1,0:T(8,128)(2,1)S(1)}, u32[]{:S(2)}, u32[]{:S(2)}) collective-permute-start(bf16[64,1152]{1,0:T(8,128)(2,1)S(1)} %get-tuple-element.43), channel_id=1, source_target_pairs={{0,16},{8,24},{16,0},{24,8},{1,17},{9,25},{17,1},{25,9},{2,18},{10... | collective-permute-start | bytes 442376 | tf_op jit(solution)/shard_map/ppermute | solution.py:202
  27.5 7.3 %collective-permute-start.10 = (bf16[64,1152]{1,0:T(8,128)(2,1)S(1)}, bf16[64,1152]{1,0:T(8,128)(2,1)S(1)}, u32[]{:S(2)}, u32[]{:S(2)}) collective-permute-start(bf16[64,1152]{1,0:T(8,128)(2,1)S(1)} %get-tuple-element.44), channel_id=1, source_target_pairs={{0,24},{8,16},{16,8},{24,0},{1,25},{9,17},{17,9},{25,1},{2,26},{10... | collective-permute-start | bytes 442376 | tf_op jit(solution)/shard_map/ppermute | solution.py:202
  28.0 8.5 %collective-permute-start.14 = (bf16[64,1152]{1,0:T(8,128)(2,1)S(1)}, bf16[64,1152]{1,0:T(8,128)(2,1)S(1)}, u32[]{:S(2)}, u32[]{:S(2)}) collective-permute-start(bf16[64,1152]{1,0:T(8,128)(2,1)S(1)} %shard_map.75), channel_id=1, source_target_pairs={{1,0},{3,2},{5,4},{7,6},{9,8},{11,10},{13,12},{15,14},{17,16},{19,... | collective-permute-start | bytes 442376 | tf_op jit(solution)/shard_map/ppermute | solution.py:207
  29.3 12.9 %collective-permute-start.15 = (bf16[64,1152]{1,0:T(8,128)(2,1)S(1)}, bf16[64,1152]{1,0:T(8,128)(2,1)S(1)}, u32[]{:S(2)}, u32[]{:S(2)}) collective-permute-start(bf16[64,1152]{1,0:T(8,128)(2,1)S(1)} %get-tuple-element.46), channel_id=1, source_target_pairs={{0,4},{1,5},{2,6},{3,7},{4,0},{5,1},{6,2},{7,3},{8,12},{9,13},{10,... | collective-permute-start | bytes 442376 | tf_op jit(solution)/shard_map/ppermute | solution.py:202
  31.7 10.5 %collective-permute-start.16 = (bf16[64,1152]{1,0:T(8,128)(2,1)S(1)}, bf16[64,1152]{1,0:T(8,128)(2,1)S(1)}, u32[]{:S(2)}, u32[]{:S(2)}) collective-permute-start(bf16[64,1152]{1,0:T(8,128)(2,1)S(1)} %get-tuple-element.47), channel_id=1, source_target_pairs={{0,6},{1,7},{2,4},{3,5},{4,2},{5,3},{6,0},{7,1},{8,14},{9,15},{10,... | collective-permute-start | bytes 442376 | tf_op jit(solution)/shard_map/ppermute | solution.py:202
  35.0 7.2 %collective-permute-start.11 = (bf16[64,1152]{1,0:T(8,128)(2,1)S(1)}, bf16[64,1152]{1,0:T(8,128)(2,1)S(1)}, u32[]{:S(2)}, u32[]{:S(2)}) collective-permute-start(bf16[64,1152]{1,0:T(8,128)(2,1)S(1)} %shard_map.73.refs_0_), channel_id=1, source_target_pairs={{0,8},{8,0},{16,24},{24,16},{1,9},{9,1},{17,25},{25,17},{2,10},{10... | collective-permute-start | bytes 442376 | tf_op jit(solution)/shard_map/ppermute | solution.py:202
  35.9 9.6 %collective-permute-start.18 = (bf16[64,1152]{1,0:T(8,128)(2,1)S(1)}, bf16[64,1152]{1,0:T(8,128)(2,1)S(1)}, u32[]{:S(2)}, u32[]{:S(2)}) collective-permute-start(bf16[64,1152]{1,0:T(8,128)(2,1)S(1)} %shard_map.73.refs_0_), channel_id=1, source_target_pairs={{0,16},{8,24},{16,0},{24,8},{1,17},{9,25},{17,1},{25,9},{2,18},{10... | collective-permute-start | bytes 442376 | tf_op jit(solution)/shard_map/ppermute | solution.py:202
  36.5 9.0 %collective-permute-start.17 = (bf16[64,1152]{1,0:T(8,128)(2,1)S(1)}, bf16[64,1152]{1,0:T(8,128)(2,1)S(1)}, u32[]{:S(2)}, u32[]{:S(2)}) collective-permute-start(bf16[64,1152]{1,0:T(8,128)(2,1)S(1)} %shard_map.73.refs_0_), channel_id=1, source_target_pairs={{0,24},{8,16},{16,8},{24,0},{1,25},{9,17},{17,9},{25,1},{2,26},{10... | collective-permute-start | bytes 442376 | tf_op jit(solution)/shard_map/ppermute | solution.py:202

commit v20 on v15

--- a/solution.py
+++ b/solution.py
@@ -56,13 +56,11 @@
     inv[...] = jnp.broadcast_to(inverse, inv.shape)
 
 
-def unit_img_body(place, other, source, bf, other_bf, other_turned, unit_out, inv, held, sem):
+def unit_img_body(place, other, source, bf, other_bf, unit_out, inv, held, sem):
     copy = pltpu.make_async_copy(source, held, sem)
     copy.start()
     values = other[...]
-    rounded = (values * inverse_norm(values)).astype(BF16)
-    other_bf[...] = rounded
-    other_turned[...] = rounded.T
+    other_bf[...] = (values * inverse_norm(values)).astype(BF16)
     copy.wait()
     values = held[...]
     bf[...] = (values * inverse_norm(values)).astype(BF16)
@@ -73,15 +71,13 @@
     inv[...] = jnp.broadcast_to(inverse, inv.shape)
 
 
-def weights_of(tile, order, line, place, column, scale, shift, perm, img, img_dim=1):
+def weights_of(tile, order, line, place, column, scale, shift, perm, img):
     rows = tile.shape[0] // len(order)
     row = lax.broadcasted_iota(jnp.int32, (rows, 1), 0)
     ids = jnp.concatenate(
         [row + (place[0] * line + (column[0] ^ (2 * k))) * rows for k in order], axis=0
     )
-    products = lax.dot_general(
-        tile, img, (((1,), (img_dim,)), ((), ())), preferred_element_type=F32
-    )
+    products = lax.dot_general(tile, img, (((1,), (1,)), ((), ())), preferred_element_type=F32)
     positive = (ids == perm).astype(F32)
     return (jax.nn.sigmoid(scale[0] * products + shift[0]) - positive).astype(BF16)
 
@@ -98,27 +94,42 @@
     return jnp.concatenate([t[...] for t in tiles], axis=0)
 
 
-def other_body(slots, order, line, place, column, scale, shift, perm, turned, *refs):
+def other_body(slots, order, line, place, column, scale, shift, perm, img, *refs):
     *txt, kept, out = refs
     tile = joined([txt[k] for k in slots])
-    weights = weights_of(tile, order, line, place, column, scale, shift, perm[...], turned[...], 0)
+    texts, images = tile.shape[0], img.shape[0]
+    rows = texts // len(order)
+    lane = lax.broadcasted_iota(jnp.int32, (1, texts), 1)
+    ids = lane
+    for j, k in enumerate(order):
+        shift_by = (place[0] * line + (column[0] ^ (2 * k))) * rows - j * rows
+        ids = jnp.where(lane // rows == j, lane + shift_by, ids)
+    paired = jnp.broadcast_to(perm[...], (128, images)).T[:, :1]
+    products = lax.dot_general(
+        img[...], tile, (((1,), (1,)), ((), ())), preferred_element_type=F32
+    )
+    positive = (paired == ids).astype(F32)
+    weights = (jax.nn.sigmoid(scale[0] * products + shift[0]) - positive).astype(BF16)
     kept[...] = weights
-    out[...] = to_images(weights, tile).astype(BF16)
+    out[...] = jnp.dot(weights, tile, preferred_element_type=F32).astype(BF16)
 
 
 def own_body(slots, order, line, place, column, scale, shift, perm, img, img_other, kept, *refs):
-    *txt, own_sum, txt_sums = refs
+    *txt, own_sum, own_txt, txt_sums = refs
     tile = joined([txt[k] for k in slots])
     weights = weights_of(tile, order, line, place, column, scale, shift, perm[...], img[...])
     own_sum[...] = to_images(weights, tile)
-    txt_sums[...] = to_texts(weights, img[...]) + to_texts(kept[...], img_other[...])
+    sums = to_texts(weights, img[...]) + to_images(kept[...], img_other[...])
+    rows = own_txt.shape[0]
+    own_txt[...] = sums[:rows]
+    txt_sums[...] = sums[rows:].astype(BF16)
 
 
 def split_body(count, blocks, place, own, other, txt_sums, *refs):
     txt_out, (keep, *send) = refs[:blocks], refs[blocks:]
     rows = txt_out[0].shape[0]
     for k, out in enumerate(txt_out):
-        out[...] = txt_sums[k * rows : (k + 1) * rows, :].astype(out.dtype)
+        out[...] = txt_sums[k * rows : (k + 1) * rows, :]
     rows = keep.shape[0]
     for k in range(count):
         start = pl.multiple_of((place[0] ^ k) * rows, rows)
@@ -223,10 +234,9 @@
     stand = sorted(range(len(ranks)), key=lambda k: ranks[k])
     tiles = [([txt_bf] + far + near)[k] for k in stand]
     slots = [stand.index(k) for k in range(len(stand))]
-    img_bf, img_other, turned_other, img_unit, img_inv = call(
+    img_bf, img_other, img_unit, img_inv = call(
         unit_img_body,
-        [struct(rows, width, BF16)] * 2
-        + [struct(width, rows, BF16), struct(part, width, F32), struct(part, 128, F32)],
+        [struct(rows, width, BF16)] * 2 + [struct(part, width, F32), struct(part, 128, F32)],
         [place, raw_other, in_hbm(images)],
         [SMEM, VMEM, ANY],
         24 << 20,
@@ -237,25 +247,28 @@
     pairs = 2 * rows * blocks * txt_rows * width
     kept, other_img = call(
         functools.partial(other_body, slots, order, line),
-        [struct(blocks * txt_rows, rows, BF16), struct(rows, width, BF16)],
-        [*scalars, perm_other, turned_other, *tiles],
+        [struct(rows, blocks * txt_rows, BF16), struct(rows, width, BF16)],
+        [*scalars, perm_other, img_other, *tiles],
         [SMEM] * 4 + [VMEM] * (2 + len(tiles)),
         40 << 20,
         2 * pairs,
     )
     from_other = swapped(other_img, "txt", 1)
-    own_img, txt_sums = call(
+    own_img, own_txt, txt_sums = call(
         functools.partial(own_body, slots, order, line),
-        [struct(rows, width, F32), struct(blocks * txt_rows, width, F32)],
+        [
+            struct(rows, width, F32),
+            struct(txt_rows, width, F32),
+            struct((blocks - 1) * txt_rows, width, BF16),
+        ],
         [*scalars, perm_row, img_bf, img_other, kept, *tiles],
         [SMEM] * 4 + [VMEM] * (4 + len(tiles)),
         40 << 20,
         4 * pairs,
     )
     outs = call(
-        functools.partial(split_body, count, blocks),
-        [struct(txt_rows, width, F32)]
-        + [struct(txt_rows, width, BF16)] * (blocks - 1)
+        functools.partial(split_body, count, blocks - 1),
+        [struct(txt_rows, width, BF16)] * (blocks - 1)
         + [struct(part, width, F32)]
         + [struct(part, width, BF16)] * (count - 1),
         [place, own_img, from_other, txt_sums],
@@ -263,7 +276,7 @@
         24 << 20,
         rows * width,
     )
-    (own_txt, *send_txt), (keep, *send) = outs[:blocks], outs[blocks:]
+    send_txt, (keep, *send) = outs[: blocks - 1], outs[blocks - 1 :]
     got = [swapped(send[k - 1], "img", k) for k in range(1, count)]
     homes = sorted(zip(order[1:], send_txt), key=lambda pair: pair[0])
     back = [swapped(block, "txt", 2 * k) for k, block in homes]

time: 41.2 us -> 41.1 us (level)
  no operation moved by 1% of the time
where the time goes in v20:
time: 41.1 us; the launch traced here: 40.9 us
  starting transfers between devices  22.3 us (54%)
  waiting for transfers between devices  9.35 us (23%)
  Pallas kernels  7.14 us (17%)
  between operations  2.03 us (5%)
    ppermute x17, starting transfers between devices, swapped(): return lax.ppermute(value, axis, [(s, s ^ step) for s in range(count)])  22.3 us
    ppermute x17, waiting for transfers between devices, swapped(): return lax.ppermute(value, axis, [(s, s ^ step) for s in range(count)])  9.35 us
    pallas_call x6, Pallas kernels, call(): pl.pallas_call(body, out_shape=outs, in_specs=specs, out_specs=[VMEM] * l...  5.24 us
    pallas_call x1, Pallas kernels, local(): pl.pallas_call(functools.partial(first_body, partners[:early]), out_shape...  1.05 us
    pallas_call x1, Pallas kernels, local(): pl.pallas_call(functools.partial(last_body, partners[early:]), out_shape=...  0.85 us
  transfers between devices with their start and end apart: 17, of which 8 were waited for; matrix products, arithmetic and copies ran while one was open for 0% of the time, Pallas kernels for 13%

profile of v20, /device:TPU:0, one launch (start us, length us, event | category | flops | bytes accessed | tf_op | source)
XLA Modules:
  0.0 40.9 jit_solution(3359416000871065946)
XLA Ops:
  0.6 0.5 %collective-permute-start = (f32[256,1152]{1,0:T(8,128)}, f32[256,1152]{1,0:T(8,128)S(1)}, u32[]{:S(2)}, u32[]{:S(2)}) collective-permute-start(f32[256,1152]{1,0:T(8,128)} %source.3), channel_id=1, source_target_pairs={{0,1},{1,0},{2,3},{3,2},{4,5},{5,4},{6,7},{7,6},{8,9},{9,8},{10,11... | collective-permute-start | bytes 3538952 | tf_op jit(solution)/shard_map/ppermute | solution.py:200
  1.1 1.1 %shard_map.68 = (bf16[64,1152]{1,0:T(8,128)(2,1)S(1)}, bf16[32,1152]{1,0:T(8,128)(2,1)S(1)}, bf16[32,1152]{1,0:T(8,128)(2,1)S(1)}, f32[64,1152]{1,0:T(8,128)S(1)}, f32[64,128]{1,0:T(8,128)S(1)}) custom-call(f32[64,1152]{1,0:T(8,128)} %source.2), custom_call_target="tpu_custom_call" | custom-call | flops 294912 | bytes 917504 | tf_op jit(solution)/shard_map/pallas_call | solution.py:25
  2.3 3.7 %collective-permute-start.2 = (bf16[32,1152]{1,0:T(8,128)(2,1)S(1)}, bf16[32,1152]{1,0:T(8,128)(2,1)S(1)}, u32[]{:S(2)}, u32[]{:S(2)}) collective-permute-start(bf16[32,1152]{1,0:T(8,128)(2,1)S(1)} %get-tuple-element.30), channel_id=1, source_target_pairs={{0,4},{1,5},{2,6},{3,7},{4,0},{5,1},{6,2},{7,3},{8,12},{9,13},{10,... | collective-permute-start | bytes 221192 | tf_op jit(solution)/shard_map/ppermute | solution.py:200
  5.9 1.6 %collective-permute-start.3 = (bf16[64,1152]{1,0:T(8,128)(2,1)S(1)}, bf16[64,1152]{1,0:T(8,128)(2,1)S(1)}, u32[]{:S(2)}, u32[]{:S(2)}) collective-permute-start(bf16[64,1152]{1,0:T(8,128)(2,1)S(1)} %get-tuple-element.29.refs_0_), channel_id=1, source_target_pairs={{0,2},{1,3},{2,0},{3,1},{4,6},{5,7},{6,4},{7,5},{8,10},{9,11},{10,... | collective-permute-start | bytes 442376 | tf_op jit(solution)/shard_map/ppermute | solution.py:200
  7.5 0.3 collective-permute-start.6
  7.8 2.5 %collective-permute-start.5 = (bf16[32,1152]{1,0:T(8,128)(2,1)S(1)}, bf16[32,1152]{1,0:T(8,128)(2,1)S(1)}, u32[]{:S(2)}, u32[]{:S(2)}) collective-permute-start(bf16[32,1152]{1,0:T(8,128)(2,1)S(1)} %get-tuple-element.31), channel_id=1, source_target_pairs={{0,6},{1,7},{2,4},{3,5},{4,2},{5,3},{6,0},{7,1},{8,14},{9,15},{10,... | collective-permute-start | bytes 221192 | tf_op jit(solution)/shard_map/ppermute | solution.py:200
  10.3 0.2 collective-permute-done.2.refs_1_
  10.5 0.7 %collective-permute-start.4 = (bf16[32,1152]{1,0:T(8,128)(2,1)S(1)}, bf16[32,1152]{1,0:T(8,128)(2,1)S(1)}, u32[]{:S(2)}, u32[]{:S(2)}) collective-permute-start(bf16[32,1152]{1,0:T(8,128)(2,1)S(1)} %collective-permute-done.2.refs_1_), channel_id=1, source_target_pairs={{0,2},{1,3},{2,0},{3,1},{4,6},{5,7},{6,4},{7,5},{8,10},{9,11},{10,... | collective-permute-start | bytes 221192 | tf_op jit(solution)/shard_map/ppermute | solution.py:200
  11.2 0.0 collective-permute-done.other
  11.2 0.0 collective-permute-start.1
  12.5 1.5 %shard_map.69 = (bf16[256,1152]{1,0:T(8,128)(2,1)S(1)}, bf16[256,1152]{1,0:T(8,128)(2,1)S(1)}, f32[64,1152]{1,0:T(8,128)S(1)}, f32[64,128]{1,0:T(8,128)S(1)}) custom-call(s32[1]{0:T(128)} %bitcast.place, f32[256,1152]{1,0:T(8,128)S(1)} %collective-permute-done.other, f32[256,1152]{1,0:T(8,128)} %source.3), custom_call_target="tpu_custom_call" | custom-call | flops 2359296 | bytes 3866628 | tf_op jit(solution)/shard_map/pallas_call | solution.py:25
  14.0 0.0 copy-start
  14.0 0.0 collective-permute-done.1.perm
  14.1 2.3 %collective-permute-done.6.refs_5_ = bf16[32,1152]{1,0:T(8,128)(2,1)S(1)} collective-permute-done((bf16[32,1152]{1,0:T(8,128)(2,1)S(1)}, bf16[32,1152]{1,0:T(8,128)(2,1)S(1)}, u32[]{:S(2)}, u32[]{:S(2)}) %collective-permute-start.6) | collective-permute-done | bytes 73760 | tf_op jit(solution)/shard_map/ppermute | solution.py:200
  16.3 0.4 collective-permute-done.5.refs_4_
  16.7 0.3 collective-permute-done.4.refs_3_
  17.0 0.0 collective-permute-done.3.refs_2_
  17.1 0.9 %shard_map.70 = (bf16[256,256]{1,0:T(8,128)(2,1)S(1)}, bf16[256,1152]{1,0:T(8,128)(2,1)S(1)}) custom-call(s32[1]{0:T(128)} %bitcast.place, s32[1]{0:T(128)} %bitcast.1.column, f32[1]{0:T(128)S(6)} %copy.9.scale, f32[1]{0:T(128)S(6)} %copy.10.shift, s32[1,256]{1,0:T(1,128)S(1)} %collective-permute-done.1.perm, ...), custom_call_target="tpu_custom_call" | custom-call | flops 301989888 | bytes 1901584 | tf_op jit(solution)/shard_map/pallas_call | solution.py:25
  18.0 0.1 collective-permute-start.7
  18.1 0.0 copy-done
  18.1 1.4 %shard_map.71 = (f32[256,1152]{1,0:T(8,128)S(1)}, f32[64,1152]{1,0:T(8,128)S(1)}, bf16[192,1152]{1,0:T(8,128)(2,1)S(1)}) custom-call(s32[1]{0:T(128)} %bitcast.place, s32[1]{0:T(128)} %bitcast.1.column, f32[1]{0:T(128)S(6)} %copy.9.scale, f32[1]{0:T(128)S(6)} %copy.10.shift, s32[1,256]{1,0:T(1,128)S(1)} %bitcast.4, ...), custom_call_target="tpu_custom_call" | custom-call | flops 603979776 | bytes 3818512 | tf_op jit(solution)/shard_map/pallas_call | solution.py:25
  19.5 0.6 %collective-permute-done.7.other = bf16[256,1152]{1,0:T(8,128)(2,1)S(1)} collective-permute-done((bf16[256,1152]{1,0:T(8,128)(2,1)S(1)}, bf16[256,1152]{1,0:T(8,128)(2,1)S(1)}, u32[]{:S(2)}, u32[]{:S(2)}) %collective-permute-start.7) | collective-permute-done | bytes 589856 | tf_op jit(solution)/shard_map/ppermute | solution.py:200
  20.1 0.1 shard_map.72
  20.2 1.6 %collective-permute-start.8 = (bf16[64,1152]{1,0:T(8,128)(2,1)S(1)}, bf16[64,1152]{1,0:T(8,128)(2,1)S(1)}, u32[]{:S(2)}, u32[]{:S(2)}) collective-permute-start(bf16[64,1152]{1,0:T(8,128)(2,1)S(1)} %get-tuple-element.40), channel_id=1, source_target_pairs={{0,8},{8,0},{16,24},{24,16},{1,9},{9,1},{17,25},{25,17},{2,10},{10... | collective-permute-start | bytes 442376 | tf_op jit(solution)/shard_map/ppermute | solution.py:200
  21.8 1.5 %collective-permute-start.9 = (bf16[64,1152]{1,0:T(8,128)(2,1)S(1)}, bf16[64,1152]{1,0:T(8,128)(2,1)S(1)}, u32[]{:S(2)}, u32[]{:S(2)}) collective-permute-start(bf16[64,1152]{1,0:T(8,128)(2,1)S(1)} %get-tuple-element.41), channel_id=1, source_target_pairs={{0,16},{8,24},{16,0},{24,8},{1,17},{9,25},{17,1},{25,9},{2,18},{10... | collective-permute-start | bytes 442376 | tf_op jit(solution)/shard_map/ppermute | solution.py:200
  23.3 0.4 %collective-permute-start.10 = (bf16[64,1152]{1,0:T(8,128)(2,1)S(1)}, bf16[64,1152]{1,0:T(8,128)(2,1)S(1)}, u32[]{:S(2)}, u32[]{:S(2)}) collective-permute-start(bf16[64,1152]{1,0:T(8,128)(2,1)S(1)} %get-tuple-element.42), channel_id=1, source_target_pairs={{0,24},{8,16},{16,8},{24,0},{1,25},{9,17},{17,9},{25,1},{2,26},{10... | collective-permute-start | bytes 442376 | tf_op jit(solution)/shard_map/ppermute | solution.py:200
  23.7 1.5 %collective-permute-start.12 = (bf16[64,1152]{1,0:T(8,128)(2,1)S(1)}, bf16[64,1152]{1,0:T(8,128)(2,1)S(1)}, u32[]{:S(2)}, u32[]{:S(2)}) collective-permute-start(bf16[64,1152]{1,0:T(8,128)(2,1)S(1)} %get-tuple-element.43), channel_id=1, source_target_pairs={{0,2},{1,3},{2,0},{3,1},{4,6},{5,7},{6,4},{7,5},{8,10},{9,11},{10,... | collective-permute-start | bytes 442376 | tf_op jit(solution)/shard_map/ppermute | solution.py:200
  25.2 1.9 %collective-permute-start.13 = (bf16[64,1152]{1,0:T(8,128)(2,1)S(1)}, bf16[64,1152]{1,0:T(8,128)(2,1)S(1)}, u32[]{:S(2)}, u32[]{:S(2)}) collective-permute-start(bf16[64,1152]{1,0:T(8,128)(2,1)S(1)} %get-tuple-element.44), channel_id=1, source_target_pairs={{0,4},{1,5},{2,6},{3,7},{4,0},{5,1},{6,2},{7,3},{8,12},{9,13},{10,... | collective-permute-start | bytes 442376 | tf_op jit(solution)/shard_map/ppermute | solution.py:200
  27.1 0.0 collective-permute-done.8.refs_0_
  27.1 2.5 %collective-permute-start.14 = (bf16[64,1152]{1,0:T(8,128)(2,1)S(1)}, bf16[64,1152]{1,0:T(8,128)(2,1)S(1)}, u32[]{:S(2)}, u32[]{:S(2)}) collective-permute-start(bf16[64,1152]{1,0:T(8,128)(2,1)S(1)} %get-tuple-element.45), channel_id=1, source_target_pairs={{0,6},{1,7},{2,4},{3,5},{4,2},{5,3},{6,0},{7,1},{8,14},{9,15},{10,... | collective-permute-start | bytes 442376 | tf_op jit(solution)/shard_map/ppermute | solution.py:200
  29.6 0.9 %collective-permute-done.9.refs_1_ = bf16[64,1152]{1,0:T(8,128)(2,1)S(1)} collective-permute-done((bf16[64,1152]{1,0:T(8,128)(2,1)S(1)}, bf16[64,1152]{1,0:T(8,128)(2,1)S(1)}, u32[]{:S(2)}, u32[]{:S(2)}) %collective-permute-start.9) | collective-permute-done | bytes 147488 | tf_op jit(solution)/shard_map/ppermute | solution.py:200
  30.6 0.0 collective-permute-done.10.refs_2_
  30.6 0.2 shard_map.73.refs_0_
  30.8 1.3 %collective-permute-start.11 = (bf16[64,1152]{1,0:T(8,128)(2,1)S(1)}, bf16[64,1152]{1,0:T(8,128)(2,1)S(1)}, u32[]{:S(2)}, u32[]{:S(2)}) collective-permute-start(bf16[64,1152]{1,0:T(8,128)(2,1)S(1)} %shard_map.73.refs_0_), channel_id=1, source_target_pairs={{0,8},{8,0},{16,24},{24,16},{1,9},{9,1},{17,25},{25,17},{2,10},{10... | collective-permute-start | bytes 442376 | tf_op jit(solution)/shard_map/ppermute | solution.py:200
  32.1 1.0 %collective-permute-start.16 = (bf16[64,1152]{1,0:T(8,128)(2,1)S(1)}, bf16[64,1152]{1,0:T(8,128)(2,1)S(1)}, u32[]{:S(2)}, u32[]{:S(2)}) collective-permute-start(bf16[64,1152]{1,0:T(8,128)(2,1)S(1)} %shard_map.73.refs_0_), channel_id=1, source_target_pairs={{0,16},{8,24},{16,0},{24,8},{1,17},{9,25},{17,1},{25,9},{2,18},{10... | collective-permute-start | bytes 442376 | tf_op jit(solution)/shard_map/ppermute | solution.py:200
  33.0 0.0 collective-permute-done.12.refs_2_
  33.0 1.3 %collective-permute-start.15 = (bf16[64,1152]{1,0:T(8,128)(2,1)S(1)}, bf16[64,1152]{1,0:T(8,128)(2,1)S(1)}, u32[]{:S(2)}, u32[]{:S(2)}) collective-permute-start(bf16[64,1152]{1,0:T(8,128)(2,1)S(1)} %shard_map.73.refs_0_), channel_id=1, source_target_pairs={{0,24},{8,16},{16,8},{24,0},{1,25},{9,17},{17,9},{25,1},{2,26},{10... | collective-permute-start | bytes 442376 | tf_op jit(solution)/shard_map/ppermute | solution.py:200
  34.3 4.5 %collective-permute-done.13.refs_3_ = bf16[64,1152]{1,0:T(8,128)(2,1)S(1)} collective-permute-done((bf16[64,1152]{1,0:T(8,128)(2,1)S(1)}, bf16[64,1152]{1,0:T(8,128)(2,1)S(1)}, u32[]{:S(2)}, u32[]{:S(2)}) %collective-permute-start.13) | collective-permute-done | bytes 147488 | tf_op jit(solution)/shard_map/ppermute | solution.py:200
  38.8 0.0 collective-permute-done.14.refs_4_
  38.8 0.0 collective-permute-done.11.refs_1_
  38.8 1.1 %shard_map.74 = (f32[256,1152]{1,0:T(8,128)}, f32[64,1152]{1,0:T(8,128)}) custom-call(s32[1]{0:T(128)} %bitcast.place, f32[1]{0:T(128)S(6)} %copy.9.scale, f32[64,1152]{1,0:T(8,128)S(1)} %get-tuple-element.25.unit, f32[64,128]{1,0:T(8,128)S(1)} %get-tuple-element.26.inverse, f32[64,1152]{1,0:T(8,128)S(1)} %get-tuple-element.33.own, ...), custom_call_target="tpu_custom_call" | custom-call | flops 737280 | bytes 2359296 | tf_op jit(solution)/shard_map/pallas_call | solution.py:295
  39.9 0.1 collective-permute-done.16.refs_1_
  40.0 0.0 collective-permute-done.15.refs_0_
  40.0 0.8 %shard_map.75 = f32[256,1152]{1,0:T(8,128)} custom-call(s32[1]{0:T(128)} %bitcast.place, f32[256,1152]{1,0:T(8,128)} %get-tuple-element.46.begun, bf16[64,1152]{1,0:T(8,128)(2,1)S(1)} %collective-permute-done.15.refs_0_, bf16[64,1152]{1,0:T(8,128)(2,1)S(1)} %collective-permute-done.16.refs_1_), custom_call_target="tpu_custom_call", output_to_operand_aliasing={{}: (1, {})} | custom-call | flops 294912 | bytes 2359296 | tf_op jit(solution)/shard_map/pallas_call | solution.py:310
Async XLA Ops:
  0.6 10.6 %collective-permute-start = (f32[256,1152]{1,0:T(8,128)}, f32[256,1152]{1,0:T(8,128)S(1)}, u32[]{:S(2)}, u32[]{:S(2)}) collective-permute-start(f32[256,1152]{1,0:T(8,128)} %source.3), channel_id=1, source_target_pairs={{0,1},{1,0},{2,3},{3,2},{4,5},{5,4},{6,7},{7,6},{8,9},{9,8},{10,11... | collective-permute-start | bytes 3538952 | tf_op jit(solution)/shard_map/ppermute | solution.py:200
  2.3 8.3 %collective-permute-start.2 = (bf16[32,1152]{1,0:T(8,128)(2,1)S(1)}, bf16[32,1152]{1,0:T(8,128)(2,1)S(1)}, u32[]{:S(2)}, u32[]{:S(2)}) collective-permute-start(bf16[32,1152]{1,0:T(8,128)(2,1)S(1)} %get-tuple-element.30), channel_id=1, source_target_pairs={{0,4},{1,5},{2,6},{3,7},{4,0},{5,1},{6,2},{7,3},{8,12},{9,13},{10,... | collective-permute-start | bytes 221192 | tf_op jit(solution)/shard_map/ppermute | solution.py:200
  5.9 11.1 %collective-permute-start.3 = (bf16[64,1152]{1,0:T(8,128)(2,1)S(1)}, bf16[64,1152]{1,0:T(8,128)(2,1)S(1)}, u32[]{:S(2)}, u32[]{:S(2)}) collective-permute-start(bf16[64,1152]{1,0:T(8,128)(2,1)S(1)} %get-tuple-element.29.refs_0_), channel_id=1, source_target_pairs={{0,2},{1,3},{2,0},{3,1},{4,6},{5,7},{6,4},{7,5},{8,10},{9,11},{10,... | collective-permute-start | bytes 442376 | tf_op jit(solution)/shard_map/ppermute | solution.py:200
  7.5 8.8 %collective-permute-start.6 = (bf16[32,1152]{1,0:T(8,128)(2,1)S(1)}, bf16[32,1152]{1,0:T(8,128)(2,1)S(1)}, u32[]{:S(2)}, u32[]{:S(2)}) collective-permute-start(bf16[32,1152]{1,0:T(8,128)(2,1)S(1)} %get-tuple-element.31), channel_id=1, source_target_pairs={{0,4},{1,5},{2,6},{3,7},{4,0},{5,1},{6,2},{7,3},{8,12},{9,13},{10,... | collective-permute-start | bytes 221192 | tf_op jit(solution)/shard_map/ppermute | solution.py:200
  7.8 8.9 %collective-permute-start.5 = (bf16[32,1152]{1,0:T(8,128)(2,1)S(1)}, bf16[32,1152]{1,0:T(8,128)(2,1)S(1)}, u32[]{:S(2)}, u32[]{:S(2)}) collective-permute-start(bf16[32,1152]{1,0:T(8,128)(2,1)S(1)} %get-tuple-element.31), channel_id=1, source_target_pairs={{0,6},{1,7},{2,4},{3,5},{4,2},{5,3},{6,0},{7,1},{8,14},{9,15},{10,... | collective-permute-start | bytes 221192 | tf_op jit(solution)/shard_map/ppermute | solution.py:200
  10.5 6.5 %collective-permute-start.4 = (bf16[32,1152]{1,0:T(8,128)(2,1)S(1)}, bf16[32,1152]{1,0:T(8,128)(2,1)S(1)}, u32[]{:S(2)}, u32[]{:S(2)}) collective-permute-start(bf16[32,1152]{1,0:T(8,128)(2,1)S(1)} %collective-permute-done.2.refs_1_), channel_id=1, source_target_pairs={{0,2},{1,3},{2,0},{3,1},{4,6},{5,7},{6,4},{7,5},{8,10},{9,11},{10,... | collective-permute-start | bytes 221192 | tf_op jit(solution)/shard_map/ppermute | solution.py:200
  11.2 2.8 %collective-permute-start.1 = (s32[1,256]{1,0:T(1,128)}, s32[1,256]{1,0:T(1,128)S(1)}, u32[]{:S(2)}, u32[]{:S(2)}) collective-permute-start(s32[1,256]{1,0:T(1,128)} %bitcast.3), channel_id=1, source_target_pairs={{0,1},{1,0},{2,3},{3,2},{4,5},{5,4},{6,7},{7,6},{8,9},{9,8},{10,11... | collective-permute-start | bytes 3080 | tf_op jit(solution)/shard_map/ppermute | solution.py:200
  14.0 4.0 %copy-start = (s32[256]{0:T(256)S(1)}, s32[256]{0:T(256)}, u32[]{:S(2)}) copy-start(s32[256]{0:T(256)} %param.7) | copy-start | bytes 3076
  18.0 2.1 %collective-permute-start.7 = (bf16[256,1152]{1,0:T(8,128)(2,1)S(1)}, bf16[256,1152]{1,0:T(8,128)(2,1)S(1)}, u32[]{:S(2)}, u32[]{:S(2)}) collective-permute-start(bf16[256,1152]{1,0:T(8,128)(2,1)S(1)} %get-tuple-element.37), channel_id=1, source_target_pairs={{0,1},{1,0},{2,3},{3,2},{4,5},{5,4},{6,7},{7,6},{8,9},{9,8},{10,11... | collective-permute-start | bytes 1769480 | tf_op jit(solution)/shard_map/ppermute | solution.py:200
  20.2 6.9 %collective-permute-start.8 = (bf16[64,1152]{1,0:T(8,128)(2,1)S(1)}, bf16[64,1152]{1,0:T(8,128)(2,1)S(1)}, u32[]{:S(2)}, u32[]{:S(2)}) collective-permute-start(bf16[64,1152]{1,0:T(8,128)(2,1)S(1)} %get-tuple-element.40), channel_id=1, source_target_pairs={{0,8},{8,0},{16,24},{24,16},{1,9},{9,1},{17,25},{25,17},{2,10},{10... | collective-permute-start | bytes 442376 | tf_op jit(solution)/shard_map/ppermute | solution.py:200
  21.8 8.8 %collective-permute-start.9 = (bf16[64,1152]{1,0:T(8,128)(2,1)S(1)}, bf16[64,1152]{1,0:T(8,128)(2,1)S(1)}, u32[]{:S(2)}, u32[]{:S(2)}) collective-permute-start(bf16[64,1152]{1,0:T(8,128)(2,1)S(1)} %get-tuple-element.41), channel_id=1, source_target_pairs={{0,16},{8,24},{16,0},{24,8},{1,17},{9,25},{17,1},{25,9},{2,18},{10... | collective-permute-start | bytes 442376 | tf_op jit(solution)/shard_map/ppermute | solution.py:200
  23.3 7.3 %collective-permute-start.10 = (bf16[64,1152]{1,0:T(8,128)(2,1)S(1)}, bf16[64,1152]{1,0:T(8,128)(2,1)S(1)}, u32[]{:S(2)}, u32[]{:S(2)}) collective-permute-start(bf16[64,1152]{1,0:T(8,128)(2,1)S(1)} %get-tuple-element.42), channel_id=1, source_target_pairs={{0,24},{8,16},{16,8},{24,0},{1,25},{9,17},{17,9},{25,1},{2,26},{10... | collective-permute-start | bytes 442376 | tf_op jit(solution)/shard_map/ppermute | solution.py:200
  23.7 9.3 %collective-permute-start.12 = (bf16[64,1152]{1,0:T(8,128)(2,1)S(1)}, bf16[64,1152]{1,0:T(8,128)(2,1)S(1)}, u32[]{:S(2)}, u32[]{:S(2)}) collective-permute-start(bf16[64,1152]{1,0:T(8,128)(2,1)S(1)} %get-tuple-element.43), channel_id=1, source_target_pairs={{0,2},{1,3},{2,0},{3,1},{4,6},{5,7},{6,4},{7,5},{8,10},{9,11},{10,... | collective-permute-start | bytes 442376 | tf_op jit(solution)/shard_map/ppermute | solution.py:200
  25.2 13.6 %collective-permute-start.13 = (bf16[64,1152]{1,0:T(8,128)(2,1)S(1)}, bf16[64,1152]{1,0:T(8,128)(2,1)S(1)}, u32[]{:S(2)}, u32[]{:S(2)}) collective-permute-start(bf16[64,1152]{1,0:T(8,128)(2,1)S(1)} %get-tuple-element.44), channel_id=1, source_target_pairs={{0,4},{1,5},{2,6},{3,7},{4,0},{5,1},{6,2},{7,3},{8,12},{9,13},{10,... | collective-permute-start | bytes 442376 | tf_op jit(solution)/shard_map/ppermute | solution.py:200
  27.1 11.7 %collective-permute-start.14 = (bf16[64,1152]{1,0:T(8,128)(2,1)S(1)}, bf16[64,1152]{1,0:T(8,128)(2,1)S(1)}, u32[]{:S(2)}, u32[]{:S(2)}) collective-permute-start(bf16[64,1152]{1,0:T(8,128)(2,1)S(1)} %get-tuple-element.45), channel_id=1, source_target_pairs={{0,6},{1,7},{2,4},{3,5},{4,2},{5,3},{6,0},{7,1},{8,14},{9,15},{10,... | collective-permute-start | bytes 442376 | tf_op jit(solution)/shard_map/ppermute | solution.py:200
  30.8 8.1 %collective-permute-start.11 = (bf16[64,1152]{1,0:T(8,128)(2,1)S(1)}, bf16[64,1152]{1,0:T(8,128)(2,1)S(1)}, u32[]{:S(2)}, u32[]{:S(2)}) collective-permute-start(bf16[64,1152]{1,0:T(8,128)(2,1)S(1)} %shard_map.73.refs_0_), channel_id=1, source_target_pairs={{0,8},{8,0},{16,24},{24,16},{1,9},{9,1},{17,25},{25,17},{2,10},{10... | collective-permute-start | bytes 442376 | tf_op jit(solution)/shard_map/ppermute | solution.py:200
  32.1 7.9 %collective-permute-start.16 = (bf16[64,1152]{1,0:T(8,128)(2,1)S(1)}, bf16[64,1152]{1,0:T(8,128)(2,1)S(1)}, u32[]{:S(2)}, u32[]{:S(2)}) collective-permute-start(bf16[64,1152]{1,0:T(8,128)(2,1)S(1)} %shard_map.73.refs_0_), channel_id=1, source_target_pairs={{0,16},{8,24},{16,0},{24,8},{1,17},{9,25},{17,1},{25,9},{2,18},{10... | collective-permute-start | bytes 442376 | tf_op jit(solution)/shard_map/ppermute | solution.py:200
  33.0 7.0 %collective-permute-start.15 = (bf16[64,1152]{1,0:T(8,128)(2,1)S(1)}, bf16[64,1152]{1,0:T(8,128)(2,1)S(1)}, u32[]{:S(2)}, u32[]{:S(2)}) collective-permute-start(bf16[64,1152]{1,0:T(8,128)(2,1)S(1)} %shard_map.73.refs_0_), channel_id=1, source_target_pairs={{0,24},{8,16},{16,8},{24,0},{1,25},{9,17},{17,9},{25,1},{2,26},{10... | collective-permute-start | bytes 442376 | tf_op jit(solution)/shard_map/ppermute | solution.py:200

commit v21 on v20

--- a/solution.py
+++ b/solution.py
@@ -288,7 +288,7 @@
         24 << 20,
         10 * part * width,
     )
-    partners = [1, *range(count - 1, 1, -1)]
+    partners = [2, *range(count - 1, 2, -1), 1]
     grads = [grad_part] + [swapped(grad_part, "img", k) for k in partners]
     partners = [0, *partners]
     early = 2

time: 41.1 us -> 41.2 us (level)
  no operation moved by 1% of the time
where the time goes in v21:
time: 41.2 us; the launch traced here: 41 us
  starting transfers between devices  22.3 us (54%)
  waiting for transfers between devices  9.46 us (23%)
  Pallas kernels  7.14 us (17%)
  between operations  2.03 us (5%)
    ppermute x17, starting transfers between devices, swapped(): return lax.ppermute(value, axis, [(s, s ^ step) for s in range(count)])  22.3 us
    ppermute x17, waiting for transfers between devices, swapped(): return lax.ppermute(value, axis, [(s, s ^ step) for s in range(count)])  9.46 us
    pallas_call x6, Pallas kernels, call(): pl.pallas_call(body, out_shape=outs, in_specs=specs, out_specs=[VMEM] * l...  5.24 us
    pallas_call x1, Pallas kernels, local(): pl.pallas_call(functools.partial(first_body, partners[:early]), out_shape...  1.05 us
    pallas_call x1, Pallas kernels, local(): pl.pallas_call(functools.partial(last_body, partners[early:]), out_shape=...  0.85 us
  transfers between devices with their start and end apart: 17, of which 8 were waited for; matrix products, arithmetic and copies ran while one was open for 0% of the time, Pallas kernels for 13%

profile of v21, /device:TPU:0, one launch (start us, length us, event | category | flops | bytes accessed | tf_op | source)
XLA Modules:
  0.0 41.0 jit_solution(15685655736285013301)
XLA Ops:
  0.6 0.5 %collective-permute-start = (f32[256,1152]{1,0:T(8,128)}, f32[256,1152]{1,0:T(8,128)S(1)}, u32[]{:S(2)}, u32[]{:S(2)}) collective-permute-start(f32[256,1152]{1,0:T(8,128)} %source.3), channel_id=1, source_target_pairs={{0,1},{1,0},{2,3},{3,2},{4,5},{5,4},{6,7},{7,6},{8,9},{9,8},{10,11... | collective-permute-start | bytes 3538952 | tf_op jit(solution)/shard_map/ppermute | solution.py:200
  1.1 1.1 %shard_map.68 = (bf16[64,1152]{1,0:T(8,128)(2,1)S(1)}, bf16[32,1152]{1,0:T(8,128)(2,1)S(1)}, bf16[32,1152]{1,0:T(8,128)(2,1)S(1)}, f32[64,1152]{1,0:T(8,128)S(1)}, f32[64,128]{1,0:T(8,128)S(1)}) custom-call(f32[64,1152]{1,0:T(8,128)} %source.2), custom_call_target="tpu_custom_call" | custom-call | flops 294912 | bytes 917504 | tf_op jit(solution)/shard_map/pallas_call | solution.py:25
  2.3 3.7 %collective-permute-start.2 = (bf16[32,1152]{1,0:T(8,128)(2,1)S(1)}, bf16[32,1152]{1,0:T(8,128)(2,1)S(1)}, u32[]{:S(2)}, u32[]{:S(2)}) collective-permute-start(bf16[32,1152]{1,0:T(8,128)(2,1)S(1)} %get-tuple-element.30), channel_id=1, source_target_pairs={{0,4},{1,5},{2,6},{3,7},{4,0},{5,1},{6,2},{7,3},{8,12},{9,13},{10,... | collective-permute-start | bytes 221192 | tf_op jit(solution)/shard_map/ppermute | solution.py:200
  5.9 1.6 %collective-permute-start.3 = (bf16[64,1152]{1,0:T(8,128)(2,1)S(1)}, bf16[64,1152]{1,0:T(8,128)(2,1)S(1)}, u32[]{:S(2)}, u32[]{:S(2)}) collective-permute-start(bf16[64,1152]{1,0:T(8,128)(2,1)S(1)} %get-tuple-element.29.refs_0_), channel_id=1, source_target_pairs={{0,2},{1,3},{2,0},{3,1},{4,6},{5,7},{6,4},{7,5},{8,10},{9,11},{10,... | collective-permute-start | bytes 442376 | tf_op jit(solution)/shard_map/ppermute | solution.py:200
  7.5 0.3 collective-permute-start.6
  7.8 2.5 %collective-permute-start.5 = (bf16[32,1152]{1,0:T(8,128)(2,1)S(1)}, bf16[32,1152]{1,0:T(8,128)(2,1)S(1)}, u32[]{:S(2)}, u32[]{:S(2)}) collective-permute-start(bf16[32,1152]{1,0:T(8,128)(2,1)S(1)} %get-tuple-element.31), channel_id=1, source_target_pairs={{0,6},{1,7},{2,4},{3,5},{4,2},{5,3},{6,0},{7,1},{8,14},{9,15},{10,... | collective-permute-start | bytes 221192 | tf_op jit(solution)/shard_map/ppermute | solution.py:200
  10.3 0.2 collective-permute-done.2.refs_1_
  10.5 0.7 %collective-permute-start.4 = (bf16[32,1152]{1,0:T(8,128)(2,1)S(1)}, bf16[32,1152]{1,0:T(8,128)(2,1)S(1)}, u32[]{:S(2)}, u32[]{:S(2)}) collective-permute-start(bf16[32,1152]{1,0:T(8,128)(2,1)S(1)} %collective-permute-done.2.refs_1_), channel_id=1, source_target_pairs={{0,2},{1,3},{2,0},{3,1},{4,6},{5,7},{6,4},{7,5},{8,10},{9,11},{10,... | collective-permute-start | bytes 221192 | tf_op jit(solution)/shard_map/ppermute | solution.py:200
  11.2 0.0 collective-permute-done.other
  11.2 0.0 collective-permute-start.1
  12.5 1.5 %shard_map.69 = (bf16[256,1152]{1,0:T(8,128)(2,1)S(1)}, bf16[256,1152]{1,0:T(8,128)(2,1)S(1)}, f32[64,1152]{1,0:T(8,128)S(1)}, f32[64,128]{1,0:T(8,128)S(1)}) custom-call(s32[1]{0:T(128)} %bitcast.place, f32[256,1152]{1,0:T(8,128)S(1)} %collective-permute-done.other, f32[256,1152]{1,0:T(8,128)} %source.3), custom_call_target="tpu_custom_call" | custom-call | flops 2359296 | bytes 3866628 | tf_op jit(solution)/shard_map/pallas_call | solution.py:25
  14.0 0.0 copy-start
  14.0 0.0 collective-permute-done.1.perm
  14.1 2.3 %collective-permute-done.6.refs_5_ = bf16[32,1152]{1,0:T(8,128)(2,1)S(1)} collective-permute-done((bf16[32,1152]{1,0:T(8,128)(2,1)S(1)}, bf16[32,1152]{1,0:T(8,128)(2,1)S(1)}, u32[]{:S(2)}, u32[]{:S(2)}) %collective-permute-start.6) | collective-permute-done | bytes 73760 | tf_op jit(solution)/shard_map/ppermute | solution.py:200
  16.3 0.4 collective-permute-done.5.refs_4_
  16.7 0.3 collective-permute-done.4.refs_3_
  17.0 0.0 collective-permute-done.3.refs_2_
  17.1 0.9 %shard_map.70 = (bf16[256,256]{1,0:T(8,128)(2,1)S(1)}, bf16[256,1152]{1,0:T(8,128)(2,1)S(1)}) custom-call(s32[1]{0:T(128)} %bitcast.place, s32[1]{0:T(128)} %bitcast.1.column, f32[1]{0:T(128)S(6)} %copy.9.scale, f32[1]{0:T(128)S(6)} %copy.10.shift, s32[1,256]{1,0:T(1,128)S(1)} %collective-permute-done.1.perm, ...), custom_call_target="tpu_custom_call" | custom-call | flops 301989888 | bytes 1901584 | tf_op jit(solution)/shard_map/pallas_call | solution.py:25
  18.0 0.1 collective-permute-start.7
  18.1 0.0 copy-done
  18.1 1.4 %shard_map.71 = (f32[256,1152]{1,0:T(8,128)S(1)}, f32[64,1152]{1,0:T(8,128)S(1)}, bf16[192,1152]{1,0:T(8,128)(2,1)S(1)}) custom-call(s32[1]{0:T(128)} %bitcast.place, s32[1]{0:T(128)} %bitcast.1.column, f32[1]{0:T(128)S(6)} %copy.9.scale, f32[1]{0:T(128)S(6)} %copy.10.shift, s32[1,256]{1,0:T(1,128)S(1)} %bitcast.4, ...), custom_call_target="tpu_custom_call" | custom-call | flops 603979776 | bytes 3818512 | tf_op jit(solution)/shard_map/pallas_call | solution.py:25
  19.5 0.6 %collective-permute-done.7.other = bf16[256,1152]{1,0:T(8,128)(2,1)S(1)} collective-permute-done((bf16[256,1152]{1,0:T(8,128)(2,1)S(1)}, bf16[256,1152]{1,0:T(8,128)(2,1)S(1)}, u32[]{:S(2)}, u32[]{:S(2)}) %collective-permute-start.7) | collective-permute-done | bytes 589856 | tf_op jit(solution)/shard_map/ppermute | solution.py:200
  20.1 0.1 shard_map.72
  20.2 1.6 %collective-permute-start.8 = (bf16[64,1152]{1,0:T(8,128)(2,1)S(1)}, bf16[64,1152]{1,0:T(8,128)(2,1)S(1)}, u32[]{:S(2)}, u32[]{:S(2)}) collective-permute-start(bf16[64,1152]{1,0:T(8,128)(2,1)S(1)} %get-tuple-element.40), channel_id=1, source_target_pairs={{0,8},{8,0},{16,24},{24,16},{1,9},{9,1},{17,25},{25,17},{2,10},{10... | collective-permute-start | bytes 442376 | tf_op jit(solution)/shard_map/ppermute | solution.py:200
  21.8 1.5 %collective-permute-start.9 = (bf16[64,1152]{1,0:T(8,128)(2,1)S(1)}, bf16[64,1152]{1,0:T(8,128)(2,1)S(1)}, u32[]{:S(2)}, u32[]{:S(2)}) collective-permute-start(bf16[64,1152]{1,0:T(8,128)(2,1)S(1)} %get-tuple-element.41), channel_id=1, source_target_pairs={{0,16},{8,24},{16,0},{24,8},{1,17},{9,25},{17,1},{25,9},{2,18},{10... | collective-permute-start | bytes 442376 | tf_op jit(solution)/shard_map/ppermute | solution.py:200
  23.3 0.4 %collective-permute-start.10 = (bf16[64,1152]{1,0:T(8,128)(2,1)S(1)}, bf16[64,1152]{1,0:T(8,128)(2,1)S(1)}, u32[]{:S(2)}, u32[]{:S(2)}) collective-permute-start(bf16[64,1152]{1,0:T(8,128)(2,1)S(1)} %get-tuple-element.42), channel_id=1, source_target_pairs={{0,24},{8,16},{16,8},{24,0},{1,25},{9,17},{17,9},{25,1},{2,26},{10... | collective-permute-start | bytes 442376 | tf_op jit(solution)/shard_map/ppermute | solution.py:200
  23.7 1.5 %collective-permute-start.12 = (bf16[64,1152]{1,0:T(8,128)(2,1)S(1)}, bf16[64,1152]{1,0:T(8,128)(2,1)S(1)}, u32[]{:S(2)}, u32[]{:S(2)}) collective-permute-start(bf16[64,1152]{1,0:T(8,128)(2,1)S(1)} %get-tuple-element.43), channel_id=1, source_target_pairs={{0,2},{1,3},{2,0},{3,1},{4,6},{5,7},{6,4},{7,5},{8,10},{9,11},{10,... | collective-permute-start | bytes 442376 | tf_op jit(solution)/shard_map/ppermute | solution.py:200
  25.2 1.9 %collective-permute-start.13 = (bf16[64,1152]{1,0:T(8,128)(2,1)S(1)}, bf16[64,1152]{1,0:T(8,128)(2,1)S(1)}, u32[]{:S(2)}, u32[]{:S(2)}) collective-permute-start(bf16[64,1152]{1,0:T(8,128)(2,1)S(1)} %get-tuple-element.44), channel_id=1, source_target_pairs={{0,4},{1,5},{2,6},{3,7},{4,0},{5,1},{6,2},{7,3},{8,12},{9,13},{10,... | collective-permute-start | bytes 442376 | tf_op jit(solution)/shard_map/ppermute | solution.py:200
  27.1 0.0 collective-permute-done.8.refs_0_
  27.1 2.5 %collective-permute-start.14 = (bf16[64,1152]{1,0:T(8,128)(2,1)S(1)}, bf16[64,1152]{1,0:T(8,128)(2,1)S(1)}, u32[]{:S(2)}, u32[]{:S(2)}) collective-permute-start(bf16[64,1152]{1,0:T(8,128)(2,1)S(1)} %get-tuple-element.45), channel_id=1, source_target_pairs={{0,6},{1,7},{2,4},{3,5},{4,2},{5,3},{6,0},{7,1},{8,14},{9,15},{10,... | collective-permute-start | bytes 442376 | tf_op jit(solution)/shard_map/ppermute | solution.py:200
  29.6 0.9 %collective-permute-done.9.refs_1_ = bf16[64,1152]{1,0:T(8,128)(2,1)S(1)} collective-permute-done((bf16[64,1152]{1,0:T(8,128)(2,1)S(1)}, bf16[64,1152]{1,0:T(8,128)(2,1)S(1)}, u32[]{:S(2)}, u32[]{:S(2)}) %collective-permute-start.9) | collective-permute-done | bytes 147488 | tf_op jit(solution)/shard_map/ppermute | solution.py:200
  30.6 0.0 collective-permute-done.10.refs_2_
  30.6 0.2 shard_map.73.refs_0_
  30.8 1.6 %collective-permute-start.11 = (bf16[64,1152]{1,0:T(8,128)(2,1)S(1)}, bf16[64,1152]{1,0:T(8,128)(2,1)S(1)}, u32[]{:S(2)}, u32[]{:S(2)}) collective-permute-start(bf16[64,1152]{1,0:T(8,128)(2,1)S(1)} %shard_map.73.refs_0_), channel_id=1, source_target_pairs={{0,16},{8,24},{16,0},{24,8},{1,17},{9,25},{17,1},{25,9},{2,18},{10... | collective-permute-start | bytes 442376 | tf_op jit(solution)/shard_map/ppermute | solution.py:200
  32.4 0.7 %collective-permute-start.16 = (bf16[64,1152]{1,0:T(8,128)(2,1)S(1)}, bf16[64,1152]{1,0:T(8,128)(2,1)S(1)}, u32[]{:S(2)}, u32[]{:S(2)}) collective-permute-start(bf16[64,1152]{1,0:T(8,128)(2,1)S(1)} %shard_map.73.refs_0_), channel_id=1, source_target_pairs={{0,8},{8,0},{16,24},{24,16},{1,9},{9,1},{17,25},{25,17},{2,10},{10... | collective-permute-start | bytes 442376 | tf_op jit(solution)/shard_map/ppermute | solution.py:200
  33.0 0.0 collective-permute-done.12.refs_2_
  33.0 1.3 %collective-permute-start.15 = (bf16[64,1152]{1,0:T(8,128)(2,1)S(1)}, bf16[64,1152]{1,0:T(8,128)(2,1)S(1)}, u32[]{:S(2)}, u32[]{:S(2)}) collective-permute-start(bf16[64,1152]{1,0:T(8,128)(2,1)S(1)} %shard_map.73.refs_0_), channel_id=1, source_target_pairs={{0,24},{8,16},{16,8},{24,0},{1,25},{9,17},{17,9},{25,1},{2,26},{10... | collective-permute-start | bytes 442376 | tf_op jit(solution)/shard_map/ppermute | solution.py:200
  34.3 4.5 %collective-permute-done.13.refs_3_ = bf16[64,1152]{1,0:T(8,128)(2,1)S(1)} collective-permute-done((bf16[64,1152]{1,0:T(8,128)(2,1)S(1)}, bf16[64,1152]{1,0:T(8,128)(2,1)S(1)}, u32[]{:S(2)}, u32[]{:S(2)}) %collective-permute-start.13) | collective-permute-done | bytes 147488 | tf_op jit(solution)/shard_map/ppermute | solution.py:200
  38.8 0.0 collective-permute-done.14.refs_4_
  38.8 0.0 collective-permute-done.11.refs_1_
  38.8 1.1 %shard_map.74 = (f32[256,1152]{1,0:T(8,128)}, f32[64,1152]{1,0:T(8,128)}) custom-call(s32[1]{0:T(128)} %bitcast.place, f32[1]{0:T(128)S(6)} %copy.9.scale, f32[64,1152]{1,0:T(8,128)S(1)} %get-tuple-element.25.unit, f32[64,128]{1,0:T(8,128)S(1)} %get-tuple-element.26.inverse, f32[64,1152]{1,0:T(8,128)S(1)} %get-tuple-element.33.own, ...), custom_call_target="tpu_custom_call" | custom-call | flops 737280 | bytes 2359296 | tf_op jit(solution)/shard_map/pallas_call | solution.py:295
  39.9 0.0 collective-permute-done.16.refs_1_
  39.9 0.2 collective-permute-done.15.refs_0_
  40.1 0.8 %shard_map.75 = f32[256,1152]{1,0:T(8,128)} custom-call(s32[1]{0:T(128)} %bitcast.place, f32[256,1152]{1,0:T(8,128)} %get-tuple-element.46.begun, bf16[64,1152]{1,0:T(8,128)(2,1)S(1)} %collective-permute-done.15.refs_0_, bf16[64,1152]{1,0:T(8,128)(2,1)S(1)} %collective-permute-done.16.refs_1_), custom_call_target="tpu_custom_call", output_to_operand_aliasing={{}: (1, {})} | custom-call | flops 294912 | bytes 2359296 | tf_op jit(solution)/shard_map/pallas_call | solution.py:310
Async XLA Ops:
  0.6 10.6 %collective-permute-start = (f32[256,1152]{1,0:T(8,128)}, f32[256,1152]{1,0:T(8,128)S(1)}, u32[]{:S(2)}, u32[]{:S(2)}) collective-permute-start(f32[256,1152]{1,0:T(8,128)} %source.3), channel_id=1, source_target_pairs={{0,1},{1,0},{2,3},{3,2},{4,5},{5,4},{6,7},{7,6},{8,9},{9,8},{10,11... | collective-permute-start | bytes 3538952 | tf_op jit(solution)/shard_map/ppermute | solution.py:200
  2.3 8.3 %collective-permute-start.2 = (bf16[32,1152]{1,0:T(8,128)(2,1)S(1)}, bf16[32,1152]{1,0:T(8,128)(2,1)S(1)}, u32[]{:S(2)}, u32[]{:S(2)}) collective-permute-start(bf16[32,1152]{1,0:T(8,128)(2,1)S(1)} %get-tuple-element.30), channel_id=1, source_target_pairs={{0,4},{1,5},{2,6},{3,7},{4,0},{5,1},{6,2},{7,3},{8,12},{9,13},{10,... | collective-permute-start | bytes 221192 | tf_op jit(solution)/shard_map/ppermute | solution.py:200
  5.9 11.1 %collective-permute-start.3 = (bf16[64,1152]{1,0:T(8,128)(2,1)S(1)}, bf16[64,1152]{1,0:T(8,128)(2,1)S(1)}, u32[]{:S(2)}, u32[]{:S(2)}) collective-permute-start(bf16[64,1152]{1,0:T(8,128)(2,1)S(1)} %get-tuple-element.29.refs_0_), channel_id=1, source_target_pairs={{0,2},{1,3},{2,0},{3,1},{4,6},{5,7},{6,4},{7,5},{8,10},{9,11},{10,... | collective-permute-start | bytes 442376 | tf_op jit(solution)/shard_map/ppermute | solution.py:200
  7.5 8.8 %collective-permute-start.6 = (bf16[32,1152]{1,0:T(8,128)(2,1)S(1)}, bf16[32,1152]{1,0:T(8,128)(2,1)S(1)}, u32[]{:S(2)}, u32[]{:S(2)}) collective-permute-start(bf16[32,1152]{1,0:T(8,128)(2,1)S(1)} %get-tuple-element.31), channel_id=1, source_target_pairs={{0,4},{1,5},{2,6},{3,7},{4,0},{5,1},{6,2},{7,3},{8,12},{9,13},{10,... | collective-permute-start | bytes 221192 | tf_op jit(solution)/shard_map/ppermute | solution.py:200
  7.8 8.9 %collective-permute-start.5 = (bf16[32,1152]{1,0:T(8,128)(2,1)S(1)}, bf16[32,1152]{1,0:T(8,128)(2,1)S(1)}, u32[]{:S(2)}, u32[]{:S(2)}) collective-permute-start(bf16[32,1152]{1,0:T(8,128)(2,1)S(1)} %get-tuple-element.31), channel_id=1, source_target_pairs={{0,6},{1,7},{2,4},{3,5},{4,2},{5,3},{6,0},{7,1},{8,14},{9,15},{10,... | collective-permute-start | bytes 221192 | tf_op jit(solution)/shard_map/ppermute | solution.py:200
  10.5 6.5 %collective-permute-start.4 = (bf16[32,1152]{1,0:T(8,128)(2,1)S(1)}, bf16[32,1152]{1,0:T(8,128)(2,1)S(1)}, u32[]{:S(2)}, u32[]{:S(2)}) collective-permute-start(bf16[32,1152]{1,0:T(8,128)(2,1)S(1)} %collective-permute-done.2.refs_1_), channel_id=1, source_target_pairs={{0,2},{1,3},{2,0},{3,1},{4,6},{5,7},{6,4},{7,5},{8,10},{9,11},{10,... | collective-permute-start | bytes 221192 | tf_op jit(solution)/shard_map/ppermute | solution.py:200
  11.2 2.8 %collective-permute-start.1 = (s32[1,256]{1,0:T(1,128)}, s32[1,256]{1,0:T(1,128)S(1)}, u32[]{:S(2)}, u32[]{:S(2)}) collective-permute-start(s32[1,256]{1,0:T(1,128)} %bitcast.3), channel_id=1, source_target_pairs={{0,1},{1,0},{2,3},{3,2},{4,5},{5,4},{6,7},{7,6},{8,9},{9,8},{10,11... | collective-permute-start | bytes 3080 | tf_op jit(solution)/shard_map/ppermute | solution.py:200
  14.0 4.0 %copy-start = (s32[256]{0:T(256)S(1)}, s32[256]{0:T(256)}, u32[]{:S(2)}) copy-start(s32[256]{0:T(256)} %param.7) | copy-start | bytes 3076
  18.0 2.1 %collective-permute-start.7 = (bf16[256,1152]{1,0:T(8,128)(2,1)S(1)}, bf16[256,1152]{1,0:T(8,128)(2,1)S(1)}, u32[]{:S(2)}, u32[]{:S(2)}) collective-permute-start(bf16[256,1152]{1,0:T(8,128)(2,1)S(1)} %get-tuple-element.37), channel_id=1, source_target_pairs={{0,1},{1,0},{2,3},{3,2},{4,5},{5,4},{6,7},{7,6},{8,9},{9,8},{10,11... | collective-permute-start | bytes 1769480 | tf_op jit(solution)/shard_map/ppermute | solution.py:200
  20.2 6.9 %collective-permute-start.8 = (bf16[64,1152]{1,0:T(8,128)(2,1)S(1)}, bf16[64,1152]{1,0:T(8,128)(2,1)S(1)}, u32[]{:S(2)}, u32[]{:S(2)}) collective-permute-start(bf16[64,1152]{1,0:T(8,128)(2,1)S(1)} %get-tuple-element.40), channel_id=1, source_target_pairs={{0,8},{8,0},{16,24},{24,16},{1,9},{9,1},{17,25},{25,17},{2,10},{10... | collective-permute-start | bytes 442376 | tf_op jit(solution)/shard_map/ppermute | solution.py:200
  21.8 8.8 %collective-permute-start.9 = (bf16[64,1152]{1,0:T(8,128)(2,1)S(1)}, bf16[64,1152]{1,0:T(8,128)(2,1)S(1)}, u32[]{:S(2)}, u32[]{:S(2)}) collective-permute-start(bf16[64,1152]{1,0:T(8,128)(2,1)S(1)} %get-tuple-element.41), channel_id=1, source_target_pairs={{0,16},{8,24},{16,0},{24,8},{1,17},{9,25},{17,1},{25,9},{2,18},{10... | collective-permute-start | bytes 442376 | tf_op jit(solution)/shard_map/ppermute | solution.py:200
  23.3 7.3 %collective-permute-start.10 = (bf16[64,1152]{1,0:T(8,128)(2,1)S(1)}, bf16[64,1152]{1,0:T(8,128)(2,1)S(1)}, u32[]{:S(2)}, u32[]{:S(2)}) collective-permute-start(bf16[64,1152]{1,0:T(8,128)(2,1)S(1)} %get-tuple-element.42), channel_id=1, source_target_pairs={{0,24},{8,16},{16,8},{24,0},{1,25},{9,17},{17,9},{25,1},{2,26},{10... | collective-permute-start | bytes 442376 | tf_op jit(solution)/shard_map/ppermute | solution.py:200
  23.7 9.3 %collective-permute-start.12 = (bf16[64,1152]{1,0:T(8,128)(2,1)S(1)}, bf16[64,1152]{1,0:T(8,128)(2,1)S(1)}, u32[]{:S(2)}, u32[]{:S(2)}) collective-permute-start(bf16[64,1152]{1,0:T(8,128)(2,1)S(1)} %get-tuple-element.43), channel_id=1, source_target_pairs={{0,2},{1,3},{2,0},{3,1},{4,6},{5,7},{6,4},{7,5},{8,10},{9,11},{10,... | collective-permute-start | bytes 442376 | tf_op jit(solution)/shard_map/ppermute | solution.py:200
  25.2 13.6 %collective-permute-start.13 = (bf16[64,1152]{1,0:T(8,128)(2,1)S(1)}, bf16[64,1152]{1,0:T(8,128)(2,1)S(1)}, u32[]{:S(2)}, u32[]{:S(2)}) collective-permute-start(bf16[64,1152]{1,0:T(8,128)(2,1)S(1)} %get-tuple-element.44), channel_id=1, source_target_pairs={{0,4},{1,5},{2,6},{3,7},{4,0},{5,1},{6,2},{7,3},{8,12},{9,13},{10,... | collective-permute-start | bytes 442376 | tf_op jit(solution)/shard_map/ppermute | solution.py:200
  27.1 11.7 %collective-permute-start.14 = (bf16[64,1152]{1,0:T(8,128)(2,1)S(1)}, bf16[64,1152]{1,0:T(8,128)(2,1)S(1)}, u32[]{:S(2)}, u32[]{:S(2)}) collective-permute-start(bf16[64,1152]{1,0:T(8,128)(2,1)S(1)} %get-tuple-element.45), channel_id=1, source_target_pairs={{0,6},{1,7},{2,4},{3,5},{4,2},{5,3},{6,0},{7,1},{8,14},{9,15},{10,... | collective-permute-start | bytes 442376 | tf_op jit(solution)/shard_map/ppermute | solution.py:200
  30.8 8.1 %collective-permute-start.11 = (bf16[64,1152]{1,0:T(8,128)(2,1)S(1)}, bf16[64,1152]{1,0:T(8,128)(2,1)S(1)}, u32[]{:S(2)}, u32[]{:S(2)}) collective-permute-start(bf16[64,1152]{1,0:T(8,128)(2,1)S(1)} %shard_map.73.refs_0_), channel_id=1, source_target_pairs={{0,16},{8,24},{16,0},{24,8},{1,17},{9,25},{17,1},{25,9},{2,18},{10... | collective-permute-start | bytes 442376 | tf_op jit(solution)/shard_map/ppermute | solution.py:200
  32.4 7.6 %collective-permute-start.16 = (bf16[64,1152]{1,0:T(8,128)(2,1)S(1)}, bf16[64,1152]{1,0:T(8,128)(2,1)S(1)}, u32[]{:S(2)}, u32[]{:S(2)}) collective-permute-start(bf16[64,1152]{1,0:T(8,128)(2,1)S(1)} %shard_map.73.refs_0_), channel_id=1, source_target_pairs={{0,8},{8,0},{16,24},{24,16},{1,9},{9,1},{17,25},{25,17},{2,10},{10... | collective-permute-start | bytes 442376 | tf_op jit(solution)/shard_map/ppermute | solution.py:200
  33.0 7.1 %collective-permute-start.15 = (bf16[64,1152]{1,0:T(8,128)(2,1)S(1)}, bf16[64,1152]{1,0:T(8,128)(2,1)S(1)}, u32[]{:S(2)}, u32[]{:S(2)}) collective-permute-start(bf16[64,1152]{1,0:T(8,128)(2,1)S(1)} %shard_map.73.refs_0_), channel_id=1, source_target_pairs={{0,24},{8,16},{16,8},{24,0},{1,25},{9,17},{17,9},{25,1},{2,26},{10... | collective-permute-start | bytes 442376 | tf_op jit(solution)/shard_map/ppermute | solution.py:200

commit v22 on v20

--- a/solution.py
+++ b/solution.py
@@ -278,7 +278,7 @@
     )
     send_txt, (keep, *send) = outs[: blocks - 1], outs[blocks - 1 :]
     got = [swapped(send[k - 1], "img", k) for k in range(1, count)]
-    homes = sorted(zip(order[1:], send_txt), key=lambda pair: pair[0])
+    homes = sorted(zip(order[1:], send_txt), key=lambda pair: (pair[0] % 2 == 0, pair[0]))
     back = [swapped(block, "txt", 2 * k) for k, block in homes]
     (grad_part,) = call(
         finish_img_body,

time: 41.1 us -> 42 us (1.022)
  waiting for transfers between devices: 9.35 us -> 10.6 us
    ppermute x17, waiting for transfers between devices: 9.35 us -> 10.6 us  [swapped(): return lax.ppermute(value, axis, [(s, s ^ step) for s in range(count)])]
where the time goes in v22:
time: 42 us; the launch traced here: 41.8 us
  starting transfers between devices  21.9 us (52%)
  waiting for transfers between devices  10.6 us (25%)
  Pallas kernels  7.14 us (17%)
  between operations  2.04 us (5%)
    ppermute x17, starting transfers between devices, swapped(): return lax.ppermute(value, axis, [(s, s ^ step) for s in range(count)])  21.9 us
    ppermute x17, waiting for transfers between devices, swapped(): return lax.ppermute(value, axis, [(s, s ^ step) for s in range(count)])  10.6 us
    pallas_call x6, Pallas kernels, call(): pl.pallas_call(body, out_shape=outs, in_specs=specs, out_specs=[VMEM] * l...  5.24 us
    pallas_call x1, Pallas kernels, local(): pl.pallas_call(functools.partial(first_body, partners[:early]), out_shape...  1.05 us
    pallas_call x1, Pallas kernels, local(): pl.pallas_call(functools.partial(last_body, partners[early:]), out_shape=...  0.85 us
  transfers between devices with their start and end apart: 17, of which 8 were waited for; matrix products, arithmetic and copies ran while one was open for 0% of the time, Pallas kernels for 13%

profile of v22, /device:TPU:0, one launch (start us, length us, event | category | flops | bytes accessed | tf_op | source)
XLA Modules:
  0.0 41.8 jit_solution(17468385994554459807)
XLA Ops:
  0.6 0.5 %collective-permute-start = (f32[256,1152]{1,0:T(8,128)}, f32[256,1152]{1,0:T(8,128)S(1)}, u32[]{:S(2)}, u32[]{:S(2)}) collective-permute-start(f32[256,1152]{1,0:T(8,128)} %source.3), channel_id=1, source_target_pairs={{0,1},{1,0},{2,3},{3,2},{4,5},{5,4},{6,7},{7,6},{8,9},{9,8},{10,11... | collective-permute-start | bytes 3538952 | tf_op jit(solution)/shard_map/ppermute | solution.py:200
  1.1 1.1 %shard_map.68 = (bf16[64,1152]{1,0:T(8,128)(2,1)S(1)}, bf16[32,1152]{1,0:T(8,128)(2,1)S(1)}, bf16[32,1152]{1,0:T(8,128)(2,1)S(1)}, f32[64,1152]{1,0:T(8,128)S(1)}, f32[64,128]{1,0:T(8,128)S(1)}) custom-call(f32[64,1152]{1,0:T(8,128)} %source.2), custom_call_target="tpu_custom_call" | custom-call | flops 294912 | bytes 917504 | tf_op jit(solution)/shard_map/pallas_call | solution.py:25
  2.3 3.7 %collective-permute-start.2 = (bf16[32,1152]{1,0:T(8,128)(2,1)S(1)}, bf16[32,1152]{1,0:T(8,128)(2,1)S(1)}, u32[]{:S(2)}, u32[]{:S(2)}) collective-permute-start(bf16[32,1152]{1,0:T(8,128)(2,1)S(1)} %get-tuple-element.30), channel_id=1, source_target_pairs={{0,4},{1,5},{2,6},{3,7},{4,0},{5,1},{6,2},{7,3},{8,12},{9,13},{10,... | collective-permute-start | bytes 221192 | tf_op jit(solution)/shard_map/ppermute | solution.py:200
  5.9 1.6 %collective-permute-start.3 = (bf16[64,1152]{1,0:T(8,128)(2,1)S(1)}, bf16[64,1152]{1,0:T(8,128)(2,1)S(1)}, u32[]{:S(2)}, u32[]{:S(2)}) collective-permute-start(bf16[64,1152]{1,0:T(8,128)(2,1)S(1)} %get-tuple-element.29.refs_0_), channel_id=1, source_target_pairs={{0,2},{1,3},{2,0},{3,1},{4,6},{5,7},{6,4},{7,5},{8,10},{9,11},{10,... | collective-permute-start | bytes 442376 | tf_op jit(solution)/shard_map/ppermute | solution.py:200
  7.5 0.3 collective-permute-start.6
  7.8 2.5 %collective-permute-start.5 = (bf16[32,1152]{1,0:T(8,128)(2,1)S(1)}, bf16[32,1152]{1,0:T(8,128)(2,1)S(1)}, u32[]{:S(2)}, u32[]{:S(2)}) collective-permute-start(bf16[32,1152]{1,0:T(8,128)(2,1)S(1)} %get-tuple-element.31), channel_id=1, source_target_pairs={{0,6},{1,7},{2,4},{3,5},{4,2},{5,3},{6,0},{7,1},{8,14},{9,15},{10,... | collective-permute-start | bytes 221192 | tf_op jit(solution)/shard_map/ppermute | solution.py:200
  10.3 0.2 collective-permute-done.2.refs_1_
  10.5 0.7 %collective-permute-start.4 = (bf16[32,1152]{1,0:T(8,128)(2,1)S(1)}, bf16[32,1152]{1,0:T(8,128)(2,1)S(1)}, u32[]{:S(2)}, u32[]{:S(2)}) collective-permute-start(bf16[32,1152]{1,0:T(8,128)(2,1)S(1)} %collective-permute-done.2.refs_1_), channel_id=1, source_target_pairs={{0,2},{1,3},{2,0},{3,1},{4,6},{5,7},{6,4},{7,5},{8,10},{9,11},{10,... | collective-permute-start | bytes 221192 | tf_op jit(solution)/shard_map/ppermute | solution.py:200
  11.2 0.0 collective-permute-done.other
  11.2 0.0 collective-permute-start.1
  12.5 1.5 %shard_map.69 = (bf16[256,1152]{1,0:T(8,128)(2,1)S(1)}, bf16[256,1152]{1,0:T(8,128)(2,1)S(1)}, f32[64,1152]{1,0:T(8,128)S(1)}, f32[64,128]{1,0:T(8,128)S(1)}) custom-call(s32[1]{0:T(128)} %bitcast.place, f32[256,1152]{1,0:T(8,128)S(1)} %collective-permute-done.other, f32[256,1152]{1,0:T(8,128)} %source.3), custom_call_target="tpu_custom_call" | custom-call | flops 2359296 | bytes 3866628 | tf_op jit(solution)/shard_map/pallas_call | solution.py:25
  14.0 0.0 copy-start
  14.0 0.0 collective-permute-done.1.perm
  14.1 2.3 %collective-permute-done.6.refs_5_ = bf16[32,1152]{1,0:T(8,128)(2,1)S(1)} collective-permute-done((bf16[32,1152]{1,0:T(8,128)(2,1)S(1)}, bf16[32,1152]{1,0:T(8,128)(2,1)S(1)}, u32[]{:S(2)}, u32[]{:S(2)}) %collective-permute-start.6) | collective-permute-done | bytes 73760 | tf_op jit(solution)/shard_map/ppermute | solution.py:200
  16.3 0.4 collective-permute-done.5.refs_4_
  16.7 0.3 collective-permute-done.4.refs_3_
  17.0 0.0 collective-permute-done.3.refs_2_
  17.1 0.9 %shard_map.70 = (bf16[256,256]{1,0:T(8,128)(2,1)S(1)}, bf16[256,1152]{1,0:T(8,128)(2,1)S(1)}) custom-call(s32[1]{0:T(128)} %bitcast.place, s32[1]{0:T(128)} %bitcast.1.column, f32[1]{0:T(128)S(6)} %copy.9.scale, f32[1]{0:T(128)S(6)} %copy.10.shift, s32[1,256]{1,0:T(1,128)S(1)} %collective-permute-done.1.perm, ...), custom_call_target="tpu_custom_call" | custom-call | flops 301989888 | bytes 1901584 | tf_op jit(solution)/shard_map/pallas_call | solution.py:25
  18.0 0.1 collective-permute-start.7
  18.1 0.0 copy-done
  18.1 1.4 %shard_map.71 = (f32[256,1152]{1,0:T(8,128)S(1)}, f32[64,1152]{1,0:T(8,128)S(1)}, bf16[192,1152]{1,0:T(8,128)(2,1)S(1)}) custom-call(s32[1]{0:T(128)} %bitcast.place, s32[1]{0:T(128)} %bitcast.1.column, f32[1]{0:T(128)S(6)} %copy.9.scale, f32[1]{0:T(128)S(6)} %copy.10.shift, s32[1,256]{1,0:T(1,128)S(1)} %bitcast.4, ...), custom_call_target="tpu_custom_call" | custom-call | flops 603979776 | bytes 3818512 | tf_op jit(solution)/shard_map/pallas_call | solution.py:25
  19.5 0.6 %collective-permute-done.7.other = bf16[256,1152]{1,0:T(8,128)(2,1)S(1)} collective-permute-done((bf16[256,1152]{1,0:T(8,128)(2,1)S(1)}, bf16[256,1152]{1,0:T(8,128)(2,1)S(1)}, u32[]{:S(2)}, u32[]{:S(2)}) %collective-permute-start.7) | collective-permute-done | bytes 589856 | tf_op jit(solution)/shard_map/ppermute | solution.py:200
  20.1 0.1 shard_map.72
  20.2 1.6 %collective-permute-start.8 = (bf16[64,1152]{1,0:T(8,128)(2,1)S(1)}, bf16[64,1152]{1,0:T(8,128)(2,1)S(1)}, u32[]{:S(2)}, u32[]{:S(2)}) collective-permute-start(bf16[64,1152]{1,0:T(8,128)(2,1)S(1)} %get-tuple-element.40), channel_id=1, source_target_pairs={{0,8},{8,0},{16,24},{24,16},{1,9},{9,1},{17,25},{25,17},{2,10},{10... | collective-permute-start | bytes 442376 | tf_op jit(solution)/shard_map/ppermute | solution.py:200
  21.8 1.5 %collective-permute-start.9 = (bf16[64,1152]{1,0:T(8,128)(2,1)S(1)}, bf16[64,1152]{1,0:T(8,128)(2,1)S(1)}, u32[]{:S(2)}, u32[]{:S(2)}) collective-permute-start(bf16[64,1152]{1,0:T(8,128)(2,1)S(1)} %get-tuple-element.41), channel_id=1, source_target_pairs={{0,16},{8,24},{16,0},{24,8},{1,17},{9,25},{17,1},{25,9},{2,18},{10... | collective-permute-start | bytes 442376 | tf_op jit(solution)/shard_map/ppermute | solution.py:200
  23.3 0.4 %collective-permute-start.10 = (bf16[64,1152]{1,0:T(8,128)(2,1)S(1)}, bf16[64,1152]{1,0:T(8,128)(2,1)S(1)}, u32[]{:S(2)}, u32[]{:S(2)}) collective-permute-start(bf16[64,1152]{1,0:T(8,128)(2,1)S(1)} %get-tuple-element.42), channel_id=1, source_target_pairs={{0,24},{8,16},{16,8},{24,0},{1,25},{9,17},{17,9},{25,1},{2,26},{10... | collective-permute-start | bytes 442376 | tf_op jit(solution)/shard_map/ppermute | solution.py:200
  23.7 1.5 %collective-permute-start.12 = (bf16[64,1152]{1,0:T(8,128)(2,1)S(1)}, bf16[64,1152]{1,0:T(8,128)(2,1)S(1)}, u32[]{:S(2)}, u32[]{:S(2)}) collective-permute-start(bf16[64,1152]{1,0:T(8,128)(2,1)S(1)} %get-tuple-element.43), channel_id=1, source_target_pairs={{0,2},{1,3},{2,0},{3,1},{4,6},{5,7},{6,4},{7,5},{8,10},{9,11},{10,... | collective-permute-start | bytes 442376 | tf_op jit(solution)/shard_map/ppermute | solution.py:200
  25.2 2.4 %collective-permute-start.13 = (bf16[64,1152]{1,0:T(8,128)(2,1)S(1)}, bf16[64,1152]{1,0:T(8,128)(2,1)S(1)}, u32[]{:S(2)}, u32[]{:S(2)}) collective-permute-start(bf16[64,1152]{1,0:T(8,128)(2,1)S(1)} %get-tuple-element.44), channel_id=1, source_target_pairs={{0,6},{1,7},{2,4},{3,5},{4,2},{5,3},{6,0},{7,1},{8,14},{9,15},{10,... | collective-permute-start | bytes 442376 | tf_op jit(solution)/shard_map/ppermute | solution.py:200
  27.6 0.0 collective-permute-done.8.refs_0_
  27.6 1.6 %collective-permute-start.14 = (bf16[64,1152]{1,0:T(8,128)(2,1)S(1)}, bf16[64,1152]{1,0:T(8,128)(2,1)S(1)}, u32[]{:S(2)}, u32[]{:S(2)}) collective-permute-start(bf16[64,1152]{1,0:T(8,128)(2,1)S(1)} %get-tuple-element.45), channel_id=1, source_target_pairs={{0,4},{1,5},{2,6},{3,7},{4,0},{5,1},{6,2},{7,3},{8,12},{9,13},{10,... | collective-permute-start | bytes 442376 | tf_op jit(solution)/shard_map/ppermute | solution.py:200
  29.2 1.3 %collective-permute-done.9.refs_1_ = bf16[64,1152]{1,0:T(8,128)(2,1)S(1)} collective-permute-done((bf16[64,1152]{1,0:T(8,128)(2,1)S(1)}, bf16[64,1152]{1,0:T(8,128)(2,1)S(1)}, u32[]{:S(2)}, u32[]{:S(2)}) %collective-permute-start.9) | collective-permute-done | bytes 147488 | tf_op jit(solution)/shard_map/ppermute | solution.py:200
  30.6 0.0 collective-permute-done.10.refs_2_
  30.6 0.2 shard_map.73.refs_0_
  30.8 1.3 %collective-permute-start.11 = (bf16[64,1152]{1,0:T(8,128)(2,1)S(1)}, bf16[64,1152]{1,0:T(8,128)(2,1)S(1)}, u32[]{:S(2)}, u32[]{:S(2)}) collective-permute-start(bf16[64,1152]{1,0:T(8,128)(2,1)S(1)} %shard_map.73.refs_0_), channel_id=1, source_target_pairs={{0,8},{8,0},{16,24},{24,16},{1,9},{9,1},{17,25},{25,17},{2,10},{10... | collective-permute-start | bytes 442376 | tf_op jit(solution)/shard_map/ppermute | solution.py:200
  32.1 0.8 %collective-permute-start.16 = (bf16[64,1152]{1,0:T(8,128)(2,1)S(1)}, bf16[64,1152]{1,0:T(8,128)(2,1)S(1)}, u32[]{:S(2)}, u32[]{:S(2)}) collective-permute-start(bf16[64,1152]{1,0:T(8,128)(2,1)S(1)} %shard_map.73.refs_0_), channel_id=1, source_target_pairs={{0,16},{8,24},{16,0},{24,8},{1,17},{9,25},{17,1},{25,9},{2,18},{10... | collective-permute-start | bytes 442376 | tf_op jit(solution)/shard_map/ppermute | solution.py:200
  32.9 0.0 collective-permute-done.12.refs_2_
  32.9 1.4 %collective-permute-start.15 = (bf16[64,1152]{1,0:T(8,128)(2,1)S(1)}, bf16[64,1152]{1,0:T(8,128)(2,1)S(1)}, u32[]{:S(2)}, u32[]{:S(2)}) collective-permute-start(bf16[64,1152]{1,0:T(8,128)(2,1)S(1)} %shard_map.73.refs_0_), channel_id=1, source_target_pairs={{0,24},{8,16},{16,8},{24,0},{1,25},{9,17},{17,9},{25,1},{2,26},{10... | collective-permute-start | bytes 442376 | tf_op jit(solution)/shard_map/ppermute | solution.py:200
  34.3 1.0 %collective-permute-done.13.refs_3_ = bf16[64,1152]{1,0:T(8,128)(2,1)S(1)} collective-permute-done((bf16[64,1152]{1,0:T(8,128)(2,1)S(1)}, bf16[64,1152]{1,0:T(8,128)(2,1)S(1)}, u32[]{:S(2)}, u32[]{:S(2)}) %collective-permute-start.13) | collective-permute-done | bytes 147488 | tf_op jit(solution)/shard_map/ppermute | solution.py:200
  35.4 4.5 %collective-permute-done.14.refs_4_ = bf16[64,1152]{1,0:T(8,128)(2,1)S(1)} collective-permute-done((bf16[64,1152]{1,0:T(8,128)(2,1)S(1)}, bf16[64,1152]{1,0:T(8,128)(2,1)S(1)}, u32[]{:S(2)}, u32[]{:S(2)}) %collective-permute-start.14) | collective-permute-done | bytes 147488 | tf_op jit(solution)/shard_map/ppermute | solution.py:200
  39.8 0.0 collective-permute-done.11.refs_1_
  39.8 1.0 %shard_map.74 = (f32[256,1152]{1,0:T(8,128)}, f32[64,1152]{1,0:T(8,128)}) custom-call(s32[1]{0:T(128)} %bitcast.place, f32[1]{0:T(128)S(6)} %copy.9.scale, f32[64,1152]{1,0:T(8,128)S(1)} %get-tuple-element.25.unit, f32[64,128]{1,0:T(8,128)S(1)} %get-tuple-element.26.inverse, f32[64,1152]{1,0:T(8,128)S(1)} %get-tuple-element.33.own, ...), custom_call_target="tpu_custom_call" | custom-call | flops 737280 | bytes 2359296 | tf_op jit(solution)/shard_map/pallas_call | solution.py:295
  40.9 0.0 collective-permute-done.16.refs_1_
  40.9 0.0 collective-permute-done.15.refs_0_
  40.9 0.9 %shard_map.75 = f32[256,1152]{1,0:T(8,128)} custom-call(s32[1]{0:T(128)} %bitcast.place, f32[256,1152]{1,0:T(8,128)} %get-tuple-element.46.begun, bf16[64,1152]{1,0:T(8,128)(2,1)S(1)} %collective-permute-done.15.refs_0_, bf16[64,1152]{1,0:T(8,128)(2,1)S(1)} %collective-permute-done.16.refs_1_), custom_call_target="tpu_custom_call", output_to_operand_aliasing={{}: (1, {})} | custom-call | flops 294912 | bytes 2359296 | tf_op jit(solution)/shard_map/pallas_call | solution.py:310
Async XLA Ops:
  0.6 10.6 %collective-permute-start = (f32[256,1152]{1,0:T(8,128)}, f32[256,1152]{1,0:T(8,128)S(1)}, u32[]{:S(2)}, u32[]{:S(2)}) collective-permute-start(f32[256,1152]{1,0:T(8,128)} %source.3), channel_id=1, source_target_pairs={{0,1},{1,0},{2,3},{3,2},{4,5},{5,4},{6,7},{7,6},{8,9},{9,8},{10,11... | collective-permute-start | bytes 3538952 | tf_op jit(solution)/shard_map/ppermute | solution.py:200
  2.3 8.3 %collective-permute-start.2 = (bf16[32,1152]{1,0:T(8,128)(2,1)S(1)}, bf16[32,1152]{1,0:T(8,128)(2,1)S(1)}, u32[]{:S(2)}, u32[]{:S(2)}) collective-permute-start(bf16[32,1152]{1,0:T(8,128)(2,1)S(1)} %get-tuple-element.30), channel_id=1, source_target_pairs={{0,4},{1,5},{2,6},{3,7},{4,0},{5,1},{6,2},{7,3},{8,12},{9,13},{10,... | collective-permute-start | bytes 221192 | tf_op jit(solution)/shard_map/ppermute | solution.py:200
  5.9 11.1 %collective-permute-start.3 = (bf16[64,1152]{1,0:T(8,128)(2,1)S(1)}, bf16[64,1152]{1,0:T(8,128)(2,1)S(1)}, u32[]{:S(2)}, u32[]{:S(2)}) collective-permute-start(bf16[64,1152]{1,0:T(8,128)(2,1)S(1)} %get-tuple-element.29.refs_0_), channel_id=1, source_target_pairs={{0,2},{1,3},{2,0},{3,1},{4,6},{5,7},{6,4},{7,5},{8,10},{9,11},{10,... | collective-permute-start | bytes 442376 | tf_op jit(solution)/shard_map/ppermute | solution.py:200
  7.5 8.8 %collective-permute-start.6 = (bf16[32,1152]{1,0:T(8,128)(2,1)S(1)}, bf16[32,1152]{1,0:T(8,128)(2,1)S(1)}, u32[]{:S(2)}, u32[]{:S(2)}) collective-permute-start(bf16[32,1152]{1,0:T(8,128)(2,1)S(1)} %get-tuple-element.31), channel_id=1, source_target_pairs={{0,4},{1,5},{2,6},{3,7},{4,0},{5,1},{6,2},{7,3},{8,12},{9,13},{10,... | collective-permute-start | bytes 221192 | tf_op jit(solution)/shard_map/ppermute | solution.py:200
  7.8 8.9 %collective-permute-start.5 = (bf16[32,1152]{1,0:T(8,128)(2,1)S(1)}, bf16[32,1152]{1,0:T(8,128)(2,1)S(1)}, u32[]{:S(2)}, u32[]{:S(2)}) collective-permute-start(bf16[32,1152]{1,0:T(8,128)(2,1)S(1)} %get-tuple-element.31), channel_id=1, source_target_pairs={{0,6},{1,7},{2,4},{3,5},{4,2},{5,3},{6,0},{7,1},{8,14},{9,15},{10,... | collective-permute-start | bytes 221192 | tf_op jit(solution)/shard_map/ppermute | solution.py:200
  10.5 6.5 %collective-permute-start.4 = (bf16[32,1152]{1,0:T(8,128)(2,1)S(1)}, bf16[32,1152]{1,0:T(8,128)(2,1)S(1)}, u32[]{:S(2)}, u32[]{:S(2)}) collective-permute-start(bf16[32,1152]{1,0:T(8,128)(2,1)S(1)} %collective-permute-done.2.refs_1_), channel_id=1, source_target_pairs={{0,2},{1,3},{2,0},{3,1},{4,6},{5,7},{6,4},{7,5},{8,10},{9,11},{10,... | collective-permute-start | bytes 221192 | tf_op jit(solution)/shard_map/ppermute | solution.py:200
  11.2 2.8 %collective-permute-start.1 = (s32[1,256]{1,0:T(1,128)}, s32[1,256]{1,0:T(1,128)S(1)}, u32[]{:S(2)}, u32[]{:S(2)}) collective-permute-start(s32[1,256]{1,0:T(1,128)} %bitcast.3), channel_id=1, source_target_pairs={{0,1},{1,0},{2,3},{3,2},{4,5},{5,4},{6,7},{7,6},{8,9},{9,8},{10,11... | collective-permute-start | bytes 3080 | tf_op jit(solution)/shard_map/ppermute | solution.py:200
  14.0 4.0 %copy-start = (s32[256]{0:T(256)S(1)}, s32[256]{0:T(256)}, u32[]{:S(2)}) copy-start(s32[256]{0:T(256)} %param.7) | copy-start | bytes 3076
  18.0 2.1 %collective-permute-start.7 = (bf16[256,1152]{1,0:T(8,128)(2,1)S(1)}, bf16[256,1152]{1,0:T(8,128)(2,1)S(1)}, u32[]{:S(2)}, u32[]{:S(2)}) collective-permute-start(bf16[256,1152]{1,0:T(8,128)(2,1)S(1)} %get-tuple-element.37), channel_id=1, source_target_pairs={{0,1},{1,0},{2,3},{3,2},{4,5},{5,4},{6,7},{7,6},{8,9},{9,8},{10,11... | collective-permute-start | bytes 1769480 | tf_op jit(solution)/shard_map/ppermute | solution.py:200
  20.2 7.4 %collective-permute-start.8 = (bf16[64,1152]{1,0:T(8,128)(2,1)S(1)}, bf16[64,1152]{1,0:T(8,128)(2,1)S(1)}, u32[]{:S(2)}, u32[]{:S(2)}) collective-permute-start(bf16[64,1152]{1,0:T(8,128)(2,1)S(1)} %get-tuple-element.40), channel_id=1, source_target_pairs={{0,8},{8,0},{16,24},{24,16},{1,9},{9,1},{17,25},{25,17},{2,10},{10... | collective-permute-start | bytes 442376 | tf_op jit(solution)/shard_map/ppermute | solution.py:200
  21.8 8.8 %collective-permute-start.9 = (bf16[64,1152]{1,0:T(8,128)(2,1)S(1)}, bf16[64,1152]{1,0:T(8,128)(2,1)S(1)}, u32[]{:S(2)}, u32[]{:S(2)}) collective-permute-start(bf16[64,1152]{1,0:T(8,128)(2,1)S(1)} %get-tuple-element.41), channel_id=1, source_target_pairs={{0,16},{8,24},{16,0},{24,8},{1,17},{9,25},{17,1},{25,9},{2,18},{10... | collective-permute-start | bytes 442376 | tf_op jit(solution)/shard_map/ppermute | solution.py:200
  23.3 7.3 %collective-permute-start.10 = (bf16[64,1152]{1,0:T(8,128)(2,1)S(1)}, bf16[64,1152]{1,0:T(8,128)(2,1)S(1)}, u32[]{:S(2)}, u32[]{:S(2)}) collective-permute-start(bf16[64,1152]{1,0:T(8,128)(2,1)S(1)} %get-tuple-element.42), channel_id=1, source_target_pairs={{0,24},{8,16},{16,8},{24,0},{1,25},{9,17},{17,9},{25,1},{2,26},{10... | collective-permute-start | bytes 442376 | tf_op jit(solution)/shard_map/ppermute | solution.py:200
  23.7 9.1 %collective-permute-start.12 = (bf16[64,1152]{1,0:T(8,128)(2,1)S(1)}, bf16[64,1152]{1,0:T(8,128)(2,1)S(1)}, u32[]{:S(2)}, u32[]{:S(2)}) collective-permute-start(bf16[64,1152]{1,0:T(8,128)(2,1)S(1)} %get-tuple-element.43), channel_id=1, source_target_pairs={{0,2},{1,3},{2,0},{3,1},{4,6},{5,7},{6,4},{7,5},{8,10},{9,11},{10,... | collective-permute-start | bytes 442376 | tf_op jit(solution)/shard_map/ppermute | solution.py:200
  25.2 10.1 %collective-permute-start.13 = (bf16[64,1152]{1,0:T(8,128)(2,1)S(1)}, bf16[64,1152]{1,0:T(8,128)(2,1)S(1)}, u32[]{:S(2)}, u32[]{:S(2)}) collective-permute-start(bf16[64,1152]{1,0:T(8,128)(2,1)S(1)} %get-tuple-element.44), channel_id=1, source_target_pairs={{0,6},{1,7},{2,4},{3,5},{4,2},{5,3},{6,0},{7,1},{8,14},{9,15},{10,... | collective-permute-start | bytes 442376 | tf_op jit(solution)/shard_map/ppermute | solution.py:200
  27.6 12.2 %collective-permute-start.14 = (bf16[64,1152]{1,0:T(8,128)(2,1)S(1)}, bf16[64,1152]{1,0:T(8,128)(2,1)S(1)}, u32[]{:S(2)}, u32[]{:S(2)}) collective-permute-start(bf16[64,1152]{1,0:T(8,128)(2,1)S(1)} %get-tuple-element.45), channel_id=1, source_target_pairs={{0,4},{1,5},{2,6},{3,7},{4,0},{5,1},{6,2},{7,3},{8,12},{9,13},{10,... | collective-permute-start | bytes 442376 | tf_op jit(solution)/shard_map/ppermute | solution.py:200
  30.8 9.1 %collective-permute-start.11 = (bf16[64,1152]{1,0:T(8,128)(2,1)S(1)}, bf16[64,1152]{1,0:T(8,128)(2,1)S(1)}, u32[]{:S(2)}, u32[]{:S(2)}) collective-permute-start(bf16[64,1152]{1,0:T(8,128)(2,1)S(1)} %shard_map.73.refs_0_), channel_id=1, source_target_pairs={{0,8},{8,0},{16,24},{24,16},{1,9},{9,1},{17,25},{25,17},{2,10},{10... | collective-permute-start | bytes 442376 | tf_op jit(solution)/shard_map/ppermute | solution.py:200
  32.1 8.8 %collective-permute-start.16 = (bf16[64,1152]{1,0:T(8,128)(2,1)S(1)}, bf16[64,1152]{1,0:T(8,128)(2,1)S(1)}, u32[]{:S(2)}, u32[]{:S(2)}) collective-permute-start(bf16[64,1152]{1,0:T(8,128)(2,1)S(1)} %shard_map.73.refs_0_), channel_id=1, source_target_pairs={{0,16},{8,24},{16,0},{24,8},{1,17},{9,25},{17,1},{25,9},{2,18},{10... | collective-permute-start | bytes 442376 | tf_op jit(solution)/shard_map/ppermute | solution.py:200
  32.9 8.0 %collective-permute-start.15 = (bf16[64,1152]{1,0:T(8,128)(2,1)S(1)}, bf16[64,1152]{1,0:T(8,128)(2,1)S(1)}, u32[]{:S(2)}, u32[]{:S(2)}) collective-permute-start(bf16[64,1152]{1,0:T(8,128)(2,1)S(1)} %shard_map.73.refs_0_), channel_id=1, source_target_pairs={{0,24},{8,16},{16,8},{24,0},{1,25},{9,17},{17,9},{25,1},{2,26},{10... | collective-permute-start | bytes 442376 | tf_op jit(solution)/shard_map/ppermute | solution.py:200

commit v23 on v21

--- a/solution.py
+++ b/solution.py
@@ -159,12 +159,13 @@
     ).astype(BF16)
 
 
-def quarter_copies(partners, place, parts, img_out, img_held, sems):
+def quarter_copies(partners, place, column, parts, img_out, img_held, sems):
     rows = parts[0].shape[0]
+    core = column[0] & 1
     copies = []
-    for k, (partner, part) in enumerate(zip(partners, parts)):
+    for k, ((even, odd), part) in enumerate(zip(partners, parts)):
         img_held[k * rows : (k + 1) * rows, :] = part[...].astype(F32)
-        start = pl.multiple_of((place[0] ^ partner) * rows, rows)
+        start = pl.multiple_of((place[0] ^ (even + core * (odd - even))) * rows, rows)
         copies.append(
             pltpu.make_async_copy(
                 img_held.at[pl.ds(k * rows, rows), :],
@@ -176,11 +177,11 @@
     return copies
 
 
-def first_body(partners, place, scale, unit, inverse, own, *refs):
+def first_body(partners, place, column, scale, unit, inverse, own, *refs):
     count = len(partners)
     parts = refs[:count]
     *back, img_out, txt_out, img_held, txt_held, sems = refs[count:]
-    copies = quarter_copies(partners, place, parts, img_out, img_held, sems)
+    copies = quarter_copies(partners, place, column, parts, img_out, img_held, sems)
     txt_held[...] = backward_unit(unit[...], inverse[...], scale[0] * total_of(own, back))
     copies.append(pltpu.make_async_copy(txt_held, txt_out, sems.at[count]))
     copies[-1].start()
@@ -188,16 +189,26 @@
         copy.wait()
 
 
-def last_body(partners, place, begun, *refs):
+def last_body(partners, place, column, begun, *refs):
     del begun
     *parts, img_out, img_held, sems = refs
-    for copy in quarter_copies(partners, place, parts, img_out, img_held, sems):
+    for copy in quarter_copies(partners, place, column, parts, img_out, img_held, sems):
         copy.wait()
 
 
 def swapped(value, axis, step):
     count = lax.axis_size(axis)
     return lax.ppermute(value, axis, [(s, s ^ step) for s in range(count)])
+
+
+def plane_swapped(value, even, odd):
+    count, line = lax.axis_size("img"), lax.axis_size("txt")
+    pairs = [
+        (i * line + t, (i ^ (odd if t % 2 else even)) * line + t)
+        for i in range(count)
+        for t in range(line)
+    ]
+    return lax.ppermute(value, ("img", "txt"), pairs)
 
 
 def local(images, texts, perm, scale, shift):
@@ -288,14 +299,14 @@
         24 << 20,
         10 * part * width,
     )
-    partners = [2, *range(count - 1, 2, -1), 1]
-    grads = [grad_part] + [swapped(grad_part, "img", k) for k in partners]
-    partners = [0, *partners]
+    partners = [(1, 2), *[(k, k) for k in range(count - 1, 2, -1)], (2, 1)]
+    grads = [grad_part] + [plane_swapped(grad_part, *pair) for pair in partners]
+    partners = [(0, 0), *partners]
     early = 2
     begun, grad_texts = pl.pallas_call(
         functools.partial(first_body, partners[:early]),
         out_shape=[struct(rows, width, F32), struct(txt_rows, width, F32)],
-        in_specs=[SMEM] * 2 + [VMEM] * (2 + early + blocks),
+        in_specs=[SMEM] * 3 + [VMEM] * (2 + early + blocks),
         out_specs=[ANY] * 2,
         scratch_shapes=[
             pltpu.VMEM((early * part, width), F32),
@@ -306,22 +317,22 @@
         cost_estimate=pl.CostEstimate(
             flops=10 * txt_rows * width, bytes_accessed=8 * rows * width, transcendentals=0
         ),
-    )(place, scale, txt_unit, txt_inv, own_txt, *grads[:early], *back)
+    )(place, column, scale, txt_unit, txt_inv, own_txt, *grads[:early], *back)
     grad_images = pl.pallas_call(
         functools.partial(last_body, partners[early:]),
         out_shape=struct(rows, width, F32),
-        in_specs=[SMEM, ANY] + [VMEM] * (count - early),
+        in_specs=[SMEM] * 2 + [ANY] + [VMEM] * (count - early),
         out_specs=ANY,
         scratch_shapes=[
             pltpu.VMEM(((count - early) * part, width), F32),
             pltpu.SemaphoreType.DMA((count - early,)),
         ],
-        input_output_aliases={1: 0},
+        input_output_aliases={2: 0},
         compiler_params=pltpu.CompilerParams(vmem_limit_bytes=24 << 20),
         cost_estimate=pl.CostEstimate(
             flops=rows * width, bytes_accessed=8 * rows * width, transcendentals=0
         ),
-    )(place, begun, *grads[early:])
+    )(place, column, begun, *grads[early:])
     return (grad_images, grad_texts)
 
 

time: 41.2 us -> 41.3 us (level)
    ppermute x17 -> x14, starting transfers between devices: 22.3 us -> 18.8 us  [swapped(): return lax.ppermute(value, axis, [(s, s ^ step) for s in range(count)])]
    ppermute x0 -> x3, starting transfers between devices: none -> 3.55 us  [plane_swapped(): return lax.ppermute(value, ('img', 'txt'), pairs)]
    ppermute x17 -> x14, waiting for transfers between devices: 9.46 us -> 9.24 us  [swapped(): return lax.ppermute(value, axis, [(s, s ^ step) for s in range(count)])]
where the time goes in v23:
time: 41.3 us; the launch traced here: 41.1 us
  starting transfers between devices  22.3 us (54%)
  waiting for transfers between devices  9.57 us (23%)
  Pallas kernels  7.14 us (17%)
  between operations  2.03 us (5%)
    ppermute x14, starting transfers between devices, swapped(): return lax.ppermute(value, axis, [(s, s ^ step) for s in range(count)])  18.8 us
    ppermute x14, waiting for transfers between devices, swapped(): return lax.ppermute(value, axis, [(s, s ^ step) for s in range(count)])  9.24 us
    pallas_call x6, Pallas kernels, call(): pl.pallas_call(body, out_shape=outs, in_specs=specs, out_specs=[VMEM] * l...  5.24 us
    ppermute x3, starting transfers between devices, plane_swapped(): return lax.ppermute(value, ('img', 'txt'), pairs)  3.55 us
    pallas_call x1, Pallas kernels, local(): pl.pallas_call(functools.partial(first_body, partners[:early]), out_shape...  1.05 us
    pallas_call x1, Pallas kernels, local(): pl.pallas_call(functools.partial(last_body, partners[early:]), out_shape=...  0.85 us
  transfers between devices with their start and end apart: 17, of which 8 were waited for; matrix products, arithmetic and copies ran while one was open for 0% of the time, Pallas kernels for 13%

profile of v23, /device:TPU:0, one launch (start us, length us, event | category | flops | bytes accessed | tf_op | source)
XLA Modules:
  0.0 41.1 jit_solution(13051969499160597531)
XLA Ops:
  0.6 0.5 %collective-permute-start = (f32[256,1152]{1,0:T(8,128)}, f32[256,1152]{1,0:T(8,128)S(1)}, u32[]{:S(2)}, u32[]{:S(2)}) collective-permute-start(f32[256,1152]{1,0:T(8,128)} %source.3), channel_id=1, source_target_pairs={{0,1},{1,0},{2,3},{3,2},{4,5},{5,4},{6,7},{7,6},{8,9},{9,8},{10,11... | collective-permute-start | bytes 3538952 | tf_op jit(solution)/shard_map/ppermute | solution.py:201
  1.1 1.1 %shard_map.68 = (bf16[64,1152]{1,0:T(8,128)(2,1)S(1)}, bf16[32,1152]{1,0:T(8,128)(2,1)S(1)}, bf16[32,1152]{1,0:T(8,128)(2,1)S(1)}, f32[64,1152]{1,0:T(8,128)S(1)}, f32[64,128]{1,0:T(8,128)S(1)}) custom-call(f32[64,1152]{1,0:T(8,128)} %source.2), custom_call_target="tpu_custom_call" | custom-call | flops 294912 | bytes 917504 | tf_op jit(solution)/shard_map/pallas_call | solution.py:25
  2.3 3.7 %collective-permute-start.2 = (bf16[32,1152]{1,0:T(8,128)(2,1)S(1)}, bf16[32,1152]{1,0:T(8,128)(2,1)S(1)}, u32[]{:S(2)}, u32[]{:S(2)}) collective-permute-start(bf16[32,1152]{1,0:T(8,128)(2,1)S(1)} %get-tuple-element.30), channel_id=1, source_target_pairs={{0,4},{1,5},{2,6},{3,7},{4,0},{5,1},{6,2},{7,3},{8,12},{9,13},{10,... | collective-permute-start | bytes 221192 | tf_op jit(solution)/shard_map/ppermute | solution.py:201
  5.9 1.6 %collective-permute-start.3 = (bf16[64,1152]{1,0:T(8,128)(2,1)S(1)}, bf16[64,1152]{1,0:T(8,128)(2,1)S(1)}, u32[]{:S(2)}, u32[]{:S(2)}) collective-permute-start(bf16[64,1152]{1,0:T(8,128)(2,1)S(1)} %get-tuple-element.29.refs_0_), channel_id=1, source_target_pairs={{0,2},{1,3},{2,0},{3,1},{4,6},{5,7},{6,4},{7,5},{8,10},{9,11},{10,... | collective-permute-start | bytes 442376 | tf_op jit(solution)/shard_map/ppermute | solution.py:201
  7.5 0.3 collective-permute-start.6
  7.8 2.5 %collective-permute-start.5 = (bf16[32,1152]{1,0:T(8,128)(2,1)S(1)}, bf16[32,1152]{1,0:T(8,128)(2,1)S(1)}, u32[]{:S(2)}, u32[]{:S(2)}) collective-permute-start(bf16[32,1152]{1,0:T(8,128)(2,1)S(1)} %get-tuple-element.31), channel_id=1, source_target_pairs={{0,6},{1,7},{2,4},{3,5},{4,2},{5,3},{6,0},{7,1},{8,14},{9,15},{10,... | collective-permute-start | bytes 221192 | tf_op jit(solution)/shard_map/ppermute | solution.py:201
  10.3 0.2 collective-permute-done.2.refs_1_
  10.5 0.7 %collective-permute-start.4 = (bf16[32,1152]{1,0:T(8,128)(2,1)S(1)}, bf16[32,1152]{1,0:T(8,128)(2,1)S(1)}, u32[]{:S(2)}, u32[]{:S(2)}) collective-permute-start(bf16[32,1152]{1,0:T(8,128)(2,1)S(1)} %collective-permute-done.2.refs_1_), channel_id=1, source_target_pairs={{0,2},{1,3},{2,0},{3,1},{4,6},{5,7},{6,4},{7,5},{8,10},{9,11},{10,... | collective-permute-start | bytes 221192 | tf_op jit(solution)/shard_map/ppermute | solution.py:201
  11.2 0.0 collective-permute-done.other
  11.2 0.0 collective-permute-start.1
  12.5 1.5 %shard_map.69 = (bf16[256,1152]{1,0:T(8,128)(2,1)S(1)}, bf16[256,1152]{1,0:T(8,128)(2,1)S(1)}, f32[64,1152]{1,0:T(8,128)S(1)}, f32[64,128]{1,0:T(8,128)S(1)}) custom-call(s32[1]{0:T(128)} %bitcast.place, f32[256,1152]{1,0:T(8,128)S(1)} %collective-permute-done.other, f32[256,1152]{1,0:T(8,128)} %source.3), custom_call_target="tpu_custom_call" | custom-call | flops 2359296 | bytes 3866628 | tf_op jit(solution)/shard_map/pallas_call | solution.py:25
  14.0 0.0 copy-start
  14.0 0.0 collective-permute-done.1.perm
  14.1 2.3 %collective-permute-done.6.refs_5_ = bf16[32,1152]{1,0:T(8,128)(2,1)S(1)} collective-permute-done((bf16[32,1152]{1,0:T(8,128)(2,1)S(1)}, bf16[32,1152]{1,0:T(8,128)(2,1)S(1)}, u32[]{:S(2)}, u32[]{:S(2)}) %collective-permute-start.6) | collective-permute-done | bytes 73760 | tf_op jit(solution)/shard_map/ppermute | solution.py:201
  16.3 0.4 collective-permute-done.5.refs_4_
  16.7 0.3 collective-permute-done.4.refs_3_
  17.0 0.0 collective-permute-done.3.refs_2_
  17.1 0.9 %shard_map.70 = (bf16[256,256]{1,0:T(8,128)(2,1)S(1)}, bf16[256,1152]{1,0:T(8,128)(2,1)S(1)}) custom-call(s32[1]{0:T(128)} %bitcast.place, s32[1]{0:T(128)} %bitcast.1.column, f32[1]{0:T(128)S(6)} %copy.9.scale, f32[1]{0:T(128)S(6)} %copy.10.shift, s32[1,256]{1,0:T(1,128)S(1)} %collective-permute-done.1.perm, ...), custom_call_target="tpu_custom_call" | custom-call | flops 301989888 | bytes 1901584 | tf_op jit(solution)/shard_map/pallas_call | solution.py:25
  18.0 0.1 collective-permute-start.7
  18.1 0.0 copy-done
  18.1 1.4 %shard_map.71 = (f32[256,1152]{1,0:T(8,128)S(1)}, f32[64,1152]{1,0:T(8,128)S(1)}, bf16[192,1152]{1,0:T(8,128)(2,1)S(1)}) custom-call(s32[1]{0:T(128)} %bitcast.place, s32[1]{0:T(128)} %bitcast.1.column, f32[1]{0:T(128)S(6)} %copy.9.scale, f32[1]{0:T(128)S(6)} %copy.10.shift, s32[1,256]{1,0:T(1,128)S(1)} %bitcast.4, ...), custom_call_target="tpu_custom_call" | custom-call | flops 603979776 | bytes 3818512 | tf_op jit(solution)/shard_map/pallas_call | solution.py:25
  19.5 0.6 %collective-permute-done.7.other = bf16[256,1152]{1,0:T(8,128)(2,1)S(1)} collective-permute-done((bf16[256,1152]{1,0:T(8,128)(2,1)S(1)}, bf16[256,1152]{1,0:T(8,128)(2,1)S(1)}, u32[]{:S(2)}, u32[]{:S(2)}) %collective-permute-start.7) | collective-permute-done | bytes 589856 | tf_op jit(solution)/shard_map/ppermute | solution.py:201
  20.1 0.1 shard_map.72
  20.2 1.6 %collective-permute-start.8 = (bf16[64,1152]{1,0:T(8,128)(2,1)S(1)}, bf16[64,1152]{1,0:T(8,128)(2,1)S(1)}, u32[]{:S(2)}, u32[]{:S(2)}) collective-permute-start(bf16[64,1152]{1,0:T(8,128)(2,1)S(1)} %get-tuple-element.40), channel_id=1, source_target_pairs={{0,8},{8,0},{16,24},{24,16},{1,9},{9,1},{17,25},{25,17},{2,10},{10... | collective-permute-start | bytes 442376 | tf_op jit(solution)/shard_map/ppermute | solution.py:201
  21.8 1.5 %collective-permute-start.9 = (bf16[64,1152]{1,0:T(8,128)(2,1)S(1)}, bf16[64,1152]{1,0:T(8,128)(2,1)S(1)}, u32[]{:S(2)}, u32[]{:S(2)}) collective-permute-start(bf16[64,1152]{1,0:T(8,128)(2,1)S(1)} %get-tuple-element.41), channel_id=1, source_target_pairs={{0,16},{8,24},{16,0},{24,8},{1,17},{9,25},{17,1},{25,9},{2,18},{10... | collective-permute-start | bytes 442376 | tf_op jit(solution)/shard_map/ppermute | solution.py:201
  23.3 0.4 %collective-permute-start.10 = (bf16[64,1152]{1,0:T(8,128)(2,1)S(1)}, bf16[64,1152]{1,0:T(8,128)(2,1)S(1)}, u32[]{:S(2)}, u32[]{:S(2)}) collective-permute-start(bf16[64,1152]{1,0:T(8,128)(2,1)S(1)} %get-tuple-element.42), channel_id=1, source_target_pairs={{0,24},{8,16},{16,8},{24,0},{1,25},{9,17},{17,9},{25,1},{2,26},{10... | collective-permute-start | bytes 442376 | tf_op jit(solution)/shard_map/ppermute | solution.py:201
  23.7 1.5 %collective-permute-start.12 = (bf16[64,1152]{1,0:T(8,128)(2,1)S(1)}, bf16[64,1152]{1,0:T(8,128)(2,1)S(1)}, u32[]{:S(2)}, u32[]{:S(2)}) collective-permute-start(bf16[64,1152]{1,0:T(8,128)(2,1)S(1)} %get-tuple-element.43), channel_id=1, source_target_pairs={{0,2},{1,3},{2,0},{3,1},{4,6},{5,7},{6,4},{7,5},{8,10},{9,11},{10,... | collective-permute-start | bytes 442376 | tf_op jit(solution)/shard_map/ppermute | solution.py:201
  25.2 1.9 %collective-permute-start.13 = (bf16[64,1152]{1,0:T(8,128)(2,1)S(1)}, bf16[64,1152]{1,0:T(8,128)(2,1)S(1)}, u32[]{:S(2)}, u32[]{:S(2)}) collective-permute-start(bf16[64,1152]{1,0:T(8,128)(2,1)S(1)} %get-tuple-element.44), channel_id=1, source_target_pairs={{0,4},{1,5},{2,6},{3,7},{4,0},{5,1},{6,2},{7,3},{8,12},{9,13},{10,... | collective-permute-start | bytes 442376 | tf_op jit(solution)/shard_map/ppermute | solution.py:201
  27.1 0.0 collective-permute-done.8.refs_0_
  27.1 2.5 %collective-permute-start.14 = (bf16[64,1152]{1,0:T(8,128)(2,1)S(1)}, bf16[64,1152]{1,0:T(8,128)(2,1)S(1)}, u32[]{:S(2)}, u32[]{:S(2)}) collective-permute-start(bf16[64,1152]{1,0:T(8,128)(2,1)S(1)} %get-tuple-element.45), channel_id=1, source_target_pairs={{0,6},{1,7},{2,4},{3,5},{4,2},{5,3},{6,0},{7,1},{8,14},{9,15},{10,... | collective-permute-start | bytes 442376 | tf_op jit(solution)/shard_map/ppermute | solution.py:201
  29.6 0.9 %collective-permute-done.9.refs_1_ = bf16[64,1152]{1,0:T(8,128)(2,1)S(1)} collective-permute-done((bf16[64,1152]{1,0:T(8,128)(2,1)S(1)}, bf16[64,1152]{1,0:T(8,128)(2,1)S(1)}, u32[]{:S(2)}, u32[]{:S(2)}) %collective-permute-start.9) | collective-permute-done | bytes 147488 | tf_op jit(solution)/shard_map/ppermute | solution.py:201
  30.6 0.0 collective-permute-done.10.refs_2_
  30.6 0.2 shard_map.73.refs_0_
  30.8 1.3 %collective-permute-start.11 = (bf16[64,1152]{1,0:T(8,128)(2,1)S(1)}, bf16[64,1152]{1,0:T(8,128)(2,1)S(1)}, u32[]{:S(2)}, u32[]{:S(2)}) collective-permute-start(bf16[64,1152]{1,0:T(8,128)(2,1)S(1)} %shard_map.73.refs_0_), channel_id=1, source_target_pairs={{0,8},{1,17},{2,10},{3,19},{4,12},{5,21},{6,14},{7,23},{8,0},{9,25... | collective-permute-start | bytes 442376 | tf_op jit(solution)/shard_map/ppermute | solution.py:211
  32.1 1.0 %collective-permute-start.16 = (bf16[64,1152]{1,0:T(8,128)(2,1)S(1)}, bf16[64,1152]{1,0:T(8,128)(2,1)S(1)}, u32[]{:S(2)}, u32[]{:S(2)}) collective-permute-start(bf16[64,1152]{1,0:T(8,128)(2,1)S(1)} %shard_map.73.refs_0_), channel_id=1, source_target_pairs={{0,16},{1,9},{2,18},{3,11},{4,20},{5,13},{6,22},{7,15},{8,24},{9,1... | collective-permute-start | bytes 442376 | tf_op jit(solution)/shard_map/ppermute | solution.py:211
  33.0 0.0 collective-permute-done.12.refs_2_
  33.0 1.3 %collective-permute-start.15 = (bf16[64,1152]{1,0:T(8,128)(2,1)S(1)}, bf16[64,1152]{1,0:T(8,128)(2,1)S(1)}, u32[]{:S(2)}, u32[]{:S(2)}) collective-permute-start(bf16[64,1152]{1,0:T(8,128)(2,1)S(1)} %shard_map.73.refs_0_), channel_id=1, source_target_pairs={{0,24},{1,25},{2,26},{3,27},{4,28},{5,29},{6,30},{7,31},{8,16},{9,... | collective-permute-start | bytes 442376 | tf_op jit(solution)/shard_map/ppermute | solution.py:211
  34.3 4.5 %collective-permute-done.13.refs_3_ = bf16[64,1152]{1,0:T(8,128)(2,1)S(1)} collective-permute-done((bf16[64,1152]{1,0:T(8,128)(2,1)S(1)}, bf16[64,1152]{1,0:T(8,128)(2,1)S(1)}, u32[]{:S(2)}, u32[]{:S(2)}) %collective-permute-start.13) | collective-permute-done | bytes 147488 | tf_op jit(solution)/shard_map/ppermute | solution.py:201
  38.8 0.0 collective-permute-done.14.refs_4_
  38.8 0.0 collective-permute-done.11.refs_1_
  38.8 1.1 %shard_map.74 = (f32[256,1152]{1,0:T(8,128)}, f32[64,1152]{1,0:T(8,128)}) custom-call(s32[1]{0:T(128)} %bitcast.place, s32[1]{0:T(128)} %bitcast.1.column, f32[1]{0:T(128)S(6)} %copy.9.scale, f32[64,1152]{1,0:T(8,128)S(1)} %get-tuple-element.25.unit, f32[64,128]{1,0:T(8,128)S(1)} %get-tuple-element.26.inverse, f32[64,1152]{1,0:T(8,128)S(1)} %get-tuple-element.33.own, ...), custom_call_target="tpu_custom_call" | custom-call | flops 737280 | bytes 2359296 | tf_op jit(solution)/shard_map/pallas_call | solution.py:306
  39.9 0.3 collective-permute-done.16.refs_1_
  40.2 0.0 collective-permute-done.15.refs_0_
  40.2 0.8 %shard_map.75 = f32[256,1152]{1,0:T(8,128)} custom-call(s32[1]{0:T(128)} %bitcast.place, s32[1]{0:T(128)} %bitcast.1.column, f32[256,1152]{1,0:T(8,128)} %get-tuple-element.46.begun, bf16[64,1152]{1,0:T(8,128)(2,1)S(1)} %collective-permute-done.15.refs_0_, bf16[64,1152]{1,0:T(8,128)(2,1)S(1)} %collective-permute-done.16.refs_1_), custom_call_target="tpu_custom_call", output_to_operand_aliasing={{}: (2, {})} | custom-call | flops 294912 | bytes 2359296 | tf_op jit(solution)/shard_map/pallas_call | solution.py:321
Async XLA Ops:
  0.6 10.6 %collective-permute-start = (f32[256,1152]{1,0:T(8,128)}, f32[256,1152]{1,0:T(8,128)S(1)}, u32[]{:S(2)}, u32[]{:S(2)}) collective-permute-start(f32[256,1152]{1,0:T(8,128)} %source.3), channel_id=1, source_target_pairs={{0,1},{1,0},{2,3},{3,2},{4,5},{5,4},{6,7},{7,6},{8,9},{9,8},{10,11... | collective-permute-start | bytes 3538952 | tf_op jit(solution)/shard_map/ppermute | solution.py:201
  2.3 8.3 %collective-permute-start.2 = (bf16[32,1152]{1,0:T(8,128)(2,1)S(1)}, bf16[32,1152]{1,0:T(8,128)(2,1)S(1)}, u32[]{:S(2)}, u32[]{:S(2)}) collective-permute-start(bf16[32,1152]{1,0:T(8,128)(2,1)S(1)} %get-tuple-element.30), channel_id=1, source_target_pairs={{0,4},{1,5},{2,6},{3,7},{4,0},{5,1},{6,2},{7,3},{8,12},{9,13},{10,... | collective-permute-start | bytes 221192 | tf_op jit(solution)/shard_map/ppermute | solution.py:201
  5.9 11.1 %collective-permute-start.3 = (bf16[64,1152]{1,0:T(8,128)(2,1)S(1)}, bf16[64,1152]{1,0:T(8,128)(2,1)S(1)}, u32[]{:S(2)}, u32[]{:S(2)}) collective-permute-start(bf16[64,1152]{1,0:T(8,128)(2,1)S(1)} %get-tuple-element.29.refs_0_), channel_id=1, source_target_pairs={{0,2},{1,3},{2,0},{3,1},{4,6},{5,7},{6,4},{7,5},{8,10},{9,11},{10,... | collective-permute-start | bytes 442376 | tf_op jit(solution)/shard_map/ppermute | solution.py:201
  7.5 8.8 %collective-permute-start.6 = (bf16[32,1152]{1,0:T(8,128)(2,1)S(1)}, bf16[32,1152]{1,0:T(8,128)(2,1)S(1)}, u32[]{:S(2)}, u32[]{:S(2)}) collective-permute-start(bf16[32,1152]{1,0:T(8,128)(2,1)S(1)} %get-tuple-element.31), channel_id=1, source_target_pairs={{0,4},{1,5},{2,6},{3,7},{4,0},{5,1},{6,2},{7,3},{8,12},{9,13},{10,... | collective-permute-start | bytes 221192 | tf_op jit(solution)/shard_map/ppermute | solution.py:201
  7.8 8.9 %collective-permute-start.5 = (bf16[32,1152]{1,0:T(8,128)(2,1)S(1)}, bf16[32,1152]{1,0:T(8,128)(2,1)S(1)}, u32[]{:S(2)}, u32[]{:S(2)}) collective-permute-start(bf16[32,1152]{1,0:T(8,128)(2,1)S(1)} %get-tuple-element.31), channel_id=1, source_target_pairs={{0,6},{1,7},{2,4},{3,5},{4,2},{5,3},{6,0},{7,1},{8,14},{9,15},{10,... | collective-permute-start | bytes 221192 | tf_op jit(solution)/shard_map/ppermute | solution.py:201
  10.5 6.5 %collective-permute-start.4 = (bf16[32,1152]{1,0:T(8,128)(2,1)S(1)}, bf16[32,1152]{1,0:T(8,128)(2,1)S(1)}, u32[]{:S(2)}, u32[]{:S(2)}) collective-permute-start(bf16[32,1152]{1,0:T(8,128)(2,1)S(1)} %collective-permute-done.2.refs_1_), channel_id=1, source_target_pairs={{0,2},{1,3},{2,0},{3,1},{4,6},{5,7},{6,4},{7,5},{8,10},{9,11},{10,... | collective-permute-start | bytes 221192 | tf_op jit(solution)/shard_map/ppermute | solution.py:201
  11.2 2.8 %collective-permute-start.1 = (s32[1,256]{1,0:T(1,128)}, s32[1,256]{1,0:T(1,128)S(1)}, u32[]{:S(2)}, u32[]{:S(2)}) collective-permute-start(s32[1,256]{1,0:T(1,128)} %bitcast.3), channel_id=1, source_target_pairs={{0,1},{1,0},{2,3},{3,2},{4,5},{5,4},{6,7},{7,6},{8,9},{9,8},{10,11... | collective-permute-start | bytes 3080 | tf_op jit(solution)/shard_map/ppermute | solution.py:201
  14.0 4.0 %copy-start = (s32[256]{0:T(256)S(1)}, s32[256]{0:T(256)}, u32[]{:S(2)}) copy-start(s32[256]{0:T(256)} %param.7) | copy-start | bytes 3076
  18.0 2.1 %collective-permute-start.7 = (bf16[256,1152]{1,0:T(8,128)(2,1)S(1)}, bf16[256,1152]{1,0:T(8,128)(2,1)S(1)}, u32[]{:S(2)}, u32[]{:S(2)}) collective-permute-start(bf16[256,1152]{1,0:T(8,128)(2,1)S(1)} %get-tuple-element.37), channel_id=1, source_target_pairs={{0,1},{1,0},{2,3},{3,2},{4,5},{5,4},{6,7},{7,6},{8,9},{9,8},{10,11... | collective-permute-start | bytes 1769480 | tf_op jit(solution)/shard_map/ppermute | solution.py:201
  20.2 6.9 %collective-permute-start.8 = (bf16[64,1152]{1,0:T(8,128)(2,1)S(1)}, bf16[64,1152]{1,0:T(8,128)(2,1)S(1)}, u32[]{:S(2)}, u32[]{:S(2)}) collective-permute-start(bf16[64,1152]{1,0:T(8,128)(2,1)S(1)} %get-tuple-element.40), channel_id=1, source_target_pairs={{0,8},{8,0},{16,24},{24,16},{1,9},{9,1},{17,25},{25,17},{2,10},{10... | collective-permute-start | bytes 442376 | tf_op jit(solution)/shard_map/ppermute | solution.py:201
  21.8 8.8 %collective-permute-start.9 = (bf16[64,1152]{1,0:T(8,128)(2,1)S(1)}, bf16[64,1152]{1,0:T(8,128)(2,1)S(1)}, u32[]{:S(2)}, u32[]{:S(2)}) collective-permute-start(bf16[64,1152]{1,0:T(8,128)(2,1)S(1)} %get-tuple-element.41), channel_id=1, source_target_pairs={{0,16},{8,24},{16,0},{24,8},{1,17},{9,25},{17,1},{25,9},{2,18},{10... | collective-permute-start | bytes 442376 | tf_op jit(solution)/shard_map/ppermute | solution.py:201
  23.3 7.3 %collective-permute-start.10 = (bf16[64,1152]{1,0:T(8,128)(2,1)S(1)}, bf16[64,1152]{1,0:T(8,128)(2,1)S(1)}, u32[]{:S(2)}, u32[]{:S(2)}) collective-permute-start(bf16[64,1152]{1,0:T(8,128)(2,1)S(1)} %get-tuple-element.42), channel_id=1, source_target_pairs={{0,24},{8,16},{16,8},{24,0},{1,25},{9,17},{17,9},{25,1},{2,26},{10... | collective-permute-start | bytes 442376 | tf_op jit(solution)/shard_map/ppermute | solution.py:201
  23.7 9.3 %collective-permute-start.12 = (bf16[64,1152]{1,0:T(8,128)(2,1)S(1)}, bf16[64,1152]{1,0:T(8,128)(2,1)S(1)}, u32[]{:S(2)}, u32[]{:S(2)}) collective-permute-start(bf16[64,1152]{1,0:T(8,128)(2,1)S(1)} %get-tuple-element.43), channel_id=1, source_target_pairs={{0,2},{1,3},{2,0},{3,1},{4,6},{5,7},{6,4},{7,5},{8,10},{9,11},{10,... | collective-permute-start | bytes 442376 | tf_op jit(solution)/shard_map/ppermute | solution.py:201
  25.2 13.6 %collective-permute-start.13 = (bf16[64,1152]{1,0:T(8,128)(2,1)S(1)}, bf16[64,1152]{1,0:T(8,128)(2,1)S(1)}, u32[]{:S(2)}, u32[]{:S(2)}) collective-permute-start(bf16[64,1152]{1,0:T(8,128)(2,1)S(1)} %get-tuple-element.44), channel_id=1, source_target_pairs={{0,4},{1,5},{2,6},{3,7},{4,0},{5,1},{6,2},{7,3},{8,12},{9,13},{10,... | collective-permute-start | bytes 442376 | tf_op jit(solution)/shard_map/ppermute | solution.py:201
  27.1 11.7 %collective-permute-start.14 = (bf16[64,1152]{1,0:T(8,128)(2,1)S(1)}, bf16[64,1152]{1,0:T(8,128)(2,1)S(1)}, u32[]{:S(2)}, u32[]{:S(2)}) collective-permute-start(bf16[64,1152]{1,0:T(8,128)(2,1)S(1)} %get-tuple-element.45), channel_id=1, source_target_pairs={{0,6},{1,7},{2,4},{3,5},{4,2},{5,3},{6,0},{7,1},{8,14},{9,15},{10,... | collective-permute-start | bytes 442376 | tf_op jit(solution)/shard_map/ppermute | solution.py:201
  30.8 8.1 %collective-permute-start.11 = (bf16[64,1152]{1,0:T(8,128)(2,1)S(1)}, bf16[64,1152]{1,0:T(8,128)(2,1)S(1)}, u32[]{:S(2)}, u32[]{:S(2)}) collective-permute-start(bf16[64,1152]{1,0:T(8,128)(2,1)S(1)} %shard_map.73.refs_0_), channel_id=1, source_target_pairs={{0,8},{1,17},{2,10},{3,19},{4,12},{5,21},{6,14},{7,23},{8,0},{9,25... | collective-permute-start | bytes 442376 | tf_op jit(solution)/shard_map/ppermute | solution.py:211
  32.1 8.2 %collective-permute-start.16 = (bf16[64,1152]{1,0:T(8,128)(2,1)S(1)}, bf16[64,1152]{1,0:T(8,128)(2,1)S(1)}, u32[]{:S(2)}, u32[]{:S(2)}) collective-permute-start(bf16[64,1152]{1,0:T(8,128)(2,1)S(1)} %shard_map.73.refs_0_), channel_id=1, source_target_pairs={{0,16},{1,9},{2,18},{3,11},{4,20},{5,13},{6,22},{7,15},{8,24},{9,1... | collective-permute-start | bytes 442376 | tf_op jit(solution)/shard_map/ppermute | solution.py:211
  33.0 7.2 %collective-permute-start.15 = (bf16[64,1152]{1,0:T(8,128)(2,1)S(1)}, bf16[64,1152]{1,0:T(8,128)(2,1)S(1)}, u32[]{:S(2)}, u32[]{:S(2)}) collective-permute-start(bf16[64,1152]{1,0:T(8,128)(2,1)S(1)} %shard_map.73.refs_0_), channel_id=1, source_target_pairs={{0,24},{1,25},{2,26},{3,27},{4,28},{5,29},{6,30},{7,31},{8,16},{9,... | collective-permute-start | bytes 442376 | tf_op jit(solution)/shard_map/ppermute | solution.py:211

commit v24 on v20

--- a/solution.py
+++ b/solution.py
@@ -176,22 +176,32 @@
     return copies
 
 
-def first_body(partners, place, scale, unit, inverse, own, *refs):
-    count = len(partners)
+def first_body(count, scale, unit, inverse, own, *refs):
     parts = refs[:count]
-    *back, img_out, txt_out, img_held, txt_held, sems = refs[count:]
-    copies = quarter_copies(partners, place, parts, img_out, img_held, sems)
-    txt_held[...] = backward_unit(unit[...], inverse[...], scale[0] * total_of(own, back))
-    copies.append(pltpu.make_async_copy(txt_held, txt_out, sems.at[count]))
-    copies[-1].start()
+    *back, img_out, txt_out = refs[count:]
+    rows = parts[0].shape[0]
+    for k, part in enumerate(parts):
+        img_out[k * rows : (k + 1) * rows, :] = part[...].astype(F32)
+    txt_out[...] = backward_unit(unit[...], inverse[...], scale[0] * total_of(own, back))
+
+
+def last_body(early, partners, place, ready, grad_txt, *refs):
+    *parts, img_out, txt_out, img_held, sems = refs
+    rows = parts[0].shape[0]
+    copies = [pltpu.make_async_copy(grad_txt, txt_out, sems.at[len(parts)])]
+    for k, partner in enumerate(early):
+        start = pl.multiple_of((place[0] ^ partner) * rows, rows)
+        copies.append(
+            pltpu.make_async_copy(
+                ready.at[pl.ds(k * rows, rows), :],
+                img_out.at[pl.ds(start, rows), :],
+                sems.at[len(parts) + 1 + k],
+            )
+        )
     for copy in copies:
-        copy.wait()
-
-
-def last_body(partners, place, begun, *refs):
-    del begun
-    *parts, img_out, img_held, sems = refs
-    for copy in quarter_copies(partners, place, parts, img_out, img_held, sems):
+        copy.start()
+    copies += quarter_copies(partners, place, parts, img_out, img_held, sems)
+    for copy in copies:
         copy.wait()
 
 
@@ -292,37 +302,28 @@
     grads = [grad_part] + [swapped(grad_part, "img", k) for k in partners]
     partners = [0, *partners]
     early = 2
-    begun, grad_texts = pl.pallas_call(
-        functools.partial(first_body, partners[:early]),
+    ready, grad_txt = call(
+        functools.partial(first_body, early),
+        [struct(early * part, width, F32), struct(txt_rows, width, F32)],
+        [scale, txt_unit, txt_inv, own_txt, *grads[:early], *back],
+        [SMEM] + [VMEM] * (2 + early + blocks),
+        24 << 20,
+        10 * txt_rows * width,
+    )
+    return pl.pallas_call(
+        functools.partial(last_body, partners[:early], partners[early:]),
         out_shape=[struct(rows, width, F32), struct(txt_rows, width, F32)],
-        in_specs=[SMEM] * 2 + [VMEM] * (2 + early + blocks),
+        in_specs=[SMEM] + [VMEM] * (2 + count - early),
         out_specs=[ANY] * 2,
         scratch_shapes=[
-            pltpu.VMEM((early * part, width), F32),
-            pltpu.VMEM((txt_rows, width), F32),
-            pltpu.SemaphoreType.DMA((early + 1,)),
+            pltpu.VMEM(((count - early) * part, width), F32),
+            pltpu.SemaphoreType.DMA((count + 1,)),
         ],
-        compiler_params=pltpu.CompilerParams(vmem_limit_bytes=24 << 20),
-        cost_estimate=pl.CostEstimate(
-            flops=10 * txt_rows * width, bytes_accessed=8 * rows * width, transcendentals=0
-        ),
-    )(place, scale, txt_unit, txt_inv, own_txt, *grads[:early], *back)
-    grad_images = pl.pallas_call(
-        functools.partial(last_body, partners[early:]),
-        out_shape=struct(rows, width, F32),
-        in_specs=[SMEM, ANY] + [VMEM] * (count - early),
-        out_specs=ANY,
-        scratch_shapes=[
-            pltpu.VMEM(((count - early) * part, width), F32),
-            pltpu.SemaphoreType.DMA((count - early,)),
-        ],
-        input_output_aliases={1: 0},
         compiler_params=pltpu.CompilerParams(vmem_limit_bytes=24 << 20),
         cost_estimate=pl.CostEstimate(
             flops=rows * width, bytes_accessed=8 * rows * width, transcendentals=0
         ),
-    )(place, begun, *grads[early:])
-    return (grad_images, grad_texts)
+    )(place, ready, grad_txt, *grads[early:])
 
 
 def solution(mesh):

time: 41.1 us -> 41.4 us (level)
  waiting for transfers between devices: 9.35 us -> 10.2 us
  Pallas kernels: 7.14 us -> 6.57 us
    ppermute x17, waiting for transfers between devices: 9.35 us -> 10.2 us  [swapped(): return lax.ppermute(value, axis, [(s, s ^ step) for s in range(count)])]
    pallas_call x2 -> x1, Pallas kernels: 1.9 us -> 1.15 us  [local(): pl.pallas_call(functools.partial(last_body, partners[:early], partners[ea...]
    pallas_call x6 -> x7, Pallas kernels: 5.24 us -> 5.42 us  [call(): pl.pallas_call(body, out_shape=outs, in_specs=specs, out_specs=[VMEM] * l...]
  transfers between devices with their start and end apart: 17 -> 17, of which waited for: 8 -> 8; matrix products, arithmetic and copies ran while one was open for 0% -> 0% of each run, Pallas kernels for 13% -> 11%
where the time goes in v24:
time: 41.4 us; the launch traced here: 41.2 us
  starting transfers between devices  22.3 us (54%)
  waiting for transfers between devices  10.2 us (25%)
  Pallas kernels  6.57 us (16%)
  between operations  2.03 us (5%)
    ppermute x17, starting transfers between devices, swapped(): return lax.ppermute(value, axis, [(s, s ^ step) for s in range(count)])  22.3 us
    ppermute x17, waiting for transfers between devices, swapped(): return lax.ppermute(value, axis, [(s, s ^ step) for s in range(count)])  10.2 us
    pallas_call x7, Pallas kernels, call(): pl.pallas_call(body, out_shape=outs, in_specs=specs, out_specs=[VMEM] * l...  5.42 us
    pallas_call x1, Pallas kernels, local(): pl.pallas_call(functools.partial(last_body, partners[:early], partners[ea...  1.15 us
  transfers between devices with their start and end apart: 17, of which 8 were waited for; matrix products, arithmetic and copies ran while one was open for 0% of the time, Pallas kernels for 11%

profile of v24, /device:TPU:0, one launch (start us, length us, event | category | flops | bytes accessed | tf_op | source)
XLA Modules:
  0.0 41.2 jit_solution(13447694270199441786)
XLA Ops:
  0.6 0.5 %collective-permute-start = (f32[256,1152]{1,0:T(8,128)}, f32[256,1152]{1,0:T(8,128)S(1)}, u32[]{:S(2)}, u32[]{:S(2)}) collective-permute-start(f32[256,1152]{1,0:T(8,128)} %source.3), channel_id=1, source_target_pairs={{0,1},{1,0},{2,3},{3,2},{4,5},{5,4},{6,7},{7,6},{8,9},{9,8},{10,11... | collective-permute-start | bytes 3538952 | tf_op jit(solution)/shard_map/ppermute | solution.py:210
  1.1 1.1 %shard_map.68 = (bf16[64,1152]{1,0:T(8,128)(2,1)S(1)}, bf16[32,1152]{1,0:T(8,128)(2,1)S(1)}, bf16[32,1152]{1,0:T(8,128)(2,1)S(1)}, f32[64,1152]{1,0:T(8,128)S(1)}, f32[64,128]{1,0:T(8,128)S(1)}) custom-call(f32[64,1152]{1,0:T(8,128)} %source.2), custom_call_target="tpu_custom_call" | custom-call | flops 294912 | bytes 917504 | tf_op jit(solution)/shard_map/pallas_call | solution.py:25
  2.3 3.7 %collective-permute-start.2 = (bf16[32,1152]{1,0:T(8,128)(2,1)S(1)}, bf16[32,1152]{1,0:T(8,128)(2,1)S(1)}, u32[]{:S(2)}, u32[]{:S(2)}) collective-permute-start(bf16[32,1152]{1,0:T(8,128)(2,1)S(1)} %get-tuple-element.30), channel_id=1, source_target_pairs={{0,4},{1,5},{2,6},{3,7},{4,0},{5,1},{6,2},{7,3},{8,12},{9,13},{10,... | collective-permute-start | bytes 221192 | tf_op jit(solution)/shard_map/ppermute | solution.py:210
  5.9 1.6 %collective-permute-start.3 = (bf16[64,1152]{1,0:T(8,128)(2,1)S(1)}, bf16[64,1152]{1,0:T(8,128)(2,1)S(1)}, u32[]{:S(2)}, u32[]{:S(2)}) collective-permute-start(bf16[64,1152]{1,0:T(8,128)(2,1)S(1)} %get-tuple-element.29.refs_0_), channel_id=1, source_target_pairs={{0,2},{1,3},{2,0},{3,1},{4,6},{5,7},{6,4},{7,5},{8,10},{9,11},{10,... | collective-permute-start | bytes 442376 | tf_op jit(solution)/shard_map/ppermute | solution.py:210
  7.5 0.3 collective-permute-start.6
  7.8 2.5 %collective-permute-start.5 = (bf16[32,1152]{1,0:T(8,128)(2,1)S(1)}, bf16[32,1152]{1,0:T(8,128)(2,1)S(1)}, u32[]{:S(2)}, u32[]{:S(2)}) collective-permute-start(bf16[32,1152]{1,0:T(8,128)(2,1)S(1)} %get-tuple-element.31), channel_id=1, source_target_pairs={{0,6},{1,7},{2,4},{3,5},{4,2},{5,3},{6,0},{7,1},{8,14},{9,15},{10,... | collective-permute-start | bytes 221192 | tf_op jit(solution)/shard_map/ppermute | solution.py:210
  10.3 0.2 collective-permute-done.2.refs_1_
  10.5 0.7 %collective-permute-start.4 = (bf16[32,1152]{1,0:T(8,128)(2,1)S(1)}, bf16[32,1152]{1,0:T(8,128)(2,1)S(1)}, u32[]{:S(2)}, u32[]{:S(2)}) collective-permute-start(bf16[32,1152]{1,0:T(8,128)(2,1)S(1)} %collective-permute-done.2.refs_1_), channel_id=1, source_target_pairs={{0,2},{1,3},{2,0},{3,1},{4,6},{5,7},{6,4},{7,5},{8,10},{9,11},{10,... | collective-permute-start | bytes 221192 | tf_op jit(solution)/shard_map/ppermute | solution.py:210
  11.2 0.0 collective-permute-done.other
  11.2 0.0 collective-permute-start.1
  12.5 1.5 %shard_map.69 = (bf16[256,1152]{1,0:T(8,128)(2,1)S(1)}, bf16[256,1152]{1,0:T(8,128)(2,1)S(1)}, f32[64,1152]{1,0:T(8,128)S(1)}, f32[64,128]{1,0:T(8,128)S(1)}) custom-call(s32[1]{0:T(128)} %bitcast.place, f32[256,1152]{1,0:T(8,128)S(1)} %collective-permute-done.other, f32[256,1152]{1,0:T(8,128)} %source.3), custom_call_target="tpu_custom_call" | custom-call | flops 2359296 | bytes 3866628 | tf_op jit(solution)/shard_map/pallas_call | solution.py:25
  14.0 0.0 copy-start
  14.0 0.0 collective-permute-done.1.perm
  14.1 2.3 %collective-permute-done.6.refs_5_ = bf16[32,1152]{1,0:T(8,128)(2,1)S(1)} collective-permute-done((bf16[32,1152]{1,0:T(8,128)(2,1)S(1)}, bf16[32,1152]{1,0:T(8,128)(2,1)S(1)}, u32[]{:S(2)}, u32[]{:S(2)}) %collective-permute-start.6) | collective-permute-done | bytes 73760 | tf_op jit(solution)/shard_map/ppermute | solution.py:210
  16.3 0.4 collective-permute-done.5.refs_4_
  16.7 0.3 collective-permute-done.4.refs_3_
  17.0 0.0 collective-permute-done.3.refs_2_
  17.1 0.9 %shard_map.70 = (bf16[256,256]{1,0:T(8,128)(2,1)S(1)}, bf16[256,1152]{1,0:T(8,128)(2,1)S(1)}) custom-call(s32[1]{0:T(128)} %bitcast.place, s32[1]{0:T(128)} %bitcast.1.column, f32[1]{0:T(128)S(6)} %copy.7.scale, f32[1]{0:T(128)S(6)} %copy.8.shift, s32[1,256]{1,0:T(1,128)S(1)} %collective-permute-done.1.perm, ...), custom_call_target="tpu_custom_call" | custom-call | flops 301989888 | bytes 1901584 | tf_op jit(solution)/shard_map/pallas_call | solution.py:25
  18.0 0.1 collective-permute-start.7
  18.1 0.0 copy-done
  18.1 1.4 %shard_map.71 = (f32[256,1152]{1,0:T(8,128)S(1)}, f32[64,1152]{1,0:T(8,128)S(1)}, bf16[192,1152]{1,0:T(8,128)(2,1)S(1)}) custom-call(s32[1]{0:T(128)} %bitcast.place, s32[1]{0:T(128)} %bitcast.1.column, f32[1]{0:T(128)S(6)} %copy.7.scale, f32[1]{0:T(128)S(6)} %copy.8.shift, s32[1,256]{1,0:T(1,128)S(1)} %bitcast.4, ...), custom_call_target="tpu_custom_call" | custom-call | flops 603979776 | bytes 3818512 | tf_op jit(solution)/shard_map/pallas_call | solution.py:25
  19.5 0.6 %collective-permute-done.7.other = bf16[256,1152]{1,0:T(8,128)(2,1)S(1)} collective-permute-done((bf16[256,1152]{1,0:T(8,128)(2,1)S(1)}, bf16[256,1152]{1,0:T(8,128)(2,1)S(1)}, u32[]{:S(2)}, u32[]{:S(2)}) %collective-permute-start.7) | collective-permute-done | bytes 589856 | tf_op jit(solution)/shard_map/ppermute | solution.py:210
  20.1 0.1 shard_map.72
  20.2 1.6 %collective-permute-start.8 = (bf16[64,1152]{1,0:T(8,128)(2,1)S(1)}, bf16[64,1152]{1,0:T(8,128)(2,1)S(1)}, u32[]{:S(2)}, u32[]{:S(2)}) collective-permute-start(bf16[64,1152]{1,0:T(8,128)(2,1)S(1)} %get-tuple-element.40), channel_id=1, source_target_pairs={{0,8},{8,0},{16,24},{24,16},{1,9},{9,1},{17,25},{25,17},{2,10},{10... | collective-permute-start | bytes 442376 | tf_op jit(solution)/shard_map/ppermute | solution.py:210
  21.8 1.5 %collective-permute-start.9 = (bf16[64,1152]{1,0:T(8,128)(2,1)S(1)}, bf16[64,1152]{1,0:T(8,128)(2,1)S(1)}, u32[]{:S(2)}, u32[]{:S(2)}) collective-permute-start(bf16[64,1152]{1,0:T(8,128)(2,1)S(1)} %get-tuple-element.41), channel_id=1, source_target_pairs={{0,16},{8,24},{16,0},{24,8},{1,17},{9,25},{17,1},{25,9},{2,18},{10... | collective-permute-start | bytes 442376 | tf_op jit(solution)/shard_map/ppermute | solution.py:210
  23.3 0.4 %collective-permute-start.10 = (bf16[64,1152]{1,0:T(8,128)(2,1)S(1)}, bf16[64,1152]{1,0:T(8,128)(2,1)S(1)}, u32[]{:S(2)}, u32[]{:S(2)}) collective-permute-start(bf16[64,1152]{1,0:T(8,128)(2,1)S(1)} %get-tuple-element.42), channel_id=1, source_target_pairs={{0,24},{8,16},{16,8},{24,0},{1,25},{9,17},{17,9},{25,1},{2,26},{10... | collective-permute-start | bytes 442376 | tf_op jit(solution)/shard_map/ppermute | solution.py:210
  23.7 1.5 %collective-permute-start.12 = (bf16[64,1152]{1,0:T(8,128)(2,1)S(1)}, bf16[64,1152]{1,0:T(8,128)(2,1)S(1)}, u32[]{:S(2)}, u32[]{:S(2)}) collective-permute-start(bf16[64,1152]{1,0:T(8,128)(2,1)S(1)} %get-tuple-element.43), channel_id=1, source_target_pairs={{0,2},{1,3},{2,0},{3,1},{4,6},{5,7},{6,4},{7,5},{8,10},{9,11},{10,... | collective-permute-start | bytes 442376 | tf_op jit(solution)/shard_map/ppermute | solution.py:210
  25.2 1.9 %collective-permute-start.13 = (bf16[64,1152]{1,0:T(8,128)(2,1)S(1)}, bf16[64,1152]{1,0:T(8,128)(2,1)S(1)}, u32[]{:S(2)}, u32[]{:S(2)}) collective-permute-start(bf16[64,1152]{1,0:T(8,128)(2,1)S(1)} %get-tuple-element.44), channel_id=1, source_target_pairs={{0,4},{1,5},{2,6},{3,7},{4,0},{5,1},{6,2},{7,3},{8,12},{9,13},{10,... | collective-permute-start | bytes 442376 | tf_op jit(solution)/shard_map/ppermute | solution.py:210
  27.1 0.0 collective-permute-done.8.refs_0_
  27.1 2.5 %collective-permute-start.14 = (bf16[64,1152]{1,0:T(8,128)(2,1)S(1)}, bf16[64,1152]{1,0:T(8,128)(2,1)S(1)}, u32[]{:S(2)}, u32[]{:S(2)}) collective-permute-start(bf16[64,1152]{1,0:T(8,128)(2,1)S(1)} %get-tuple-element.45), channel_id=1, source_target_pairs={{0,6},{1,7},{2,4},{3,5},{4,2},{5,3},{6,0},{7,1},{8,14},{9,15},{10,... | collective-permute-start | bytes 442376 | tf_op jit(solution)/shard_map/ppermute | solution.py:210
  29.6 0.9 %collective-permute-done.9.refs_1_ = bf16[64,1152]{1,0:T(8,128)(2,1)S(1)} collective-permute-done((bf16[64,1152]{1,0:T(8,128)(2,1)S(1)}, bf16[64,1152]{1,0:T(8,128)(2,1)S(1)}, u32[]{:S(2)}, u32[]{:S(2)}) %collective-permute-start.9) | collective-permute-done | bytes 147488 | tf_op jit(solution)/shard_map/ppermute | solution.py:210
  30.6 0.0 collective-permute-done.10.refs_2_
  30.6 0.2 shard_map.73.refs_0_
  30.8 1.3 %collective-permute-start.11 = (bf16[64,1152]{1,0:T(8,128)(2,1)S(1)}, bf16[64,1152]{1,0:T(8,128)(2,1)S(1)}, u32[]{:S(2)}, u32[]{:S(2)}) collective-permute-start(bf16[64,1152]{1,0:T(8,128)(2,1)S(1)} %shard_map.73.refs_0_), channel_id=1, source_target_pairs={{0,8},{8,0},{16,24},{24,16},{1,9},{9,1},{17,25},{25,17},{2,10},{10... | collective-permute-start | bytes 442376 | tf_op jit(solution)/shard_map/ppermute | solution.py:210
  32.1 1.0 %collective-permute-start.16 = (bf16[64,1152]{1,0:T(8,128)(2,1)S(1)}, bf16[64,1152]{1,0:T(8,128)(2,1)S(1)}, u32[]{:S(2)}, u32[]{:S(2)}) collective-permute-start(bf16[64,1152]{1,0:T(8,128)(2,1)S(1)} %shard_map.73.refs_0_), channel_id=1, source_target_pairs={{0,16},{8,24},{16,0},{24,8},{1,17},{9,25},{17,1},{25,9},{2,18},{10... | collective-permute-start | bytes 442376 | tf_op jit(solution)/shard_map/ppermute | solution.py:210
  33.0 0.0 collective-permute-done.12.refs_2_
  33.0 1.3 %collective-permute-start.15 = (bf16[64,1152]{1,0:T(8,128)(2,1)S(1)}, bf16[64,1152]{1,0:T(8,128)(2,1)S(1)}, u32[]{:S(2)}, u32[]{:S(2)}) collective-permute-start(bf16[64,1152]{1,0:T(8,128)(2,1)S(1)} %shard_map.73.refs_0_), channel_id=1, source_target_pairs={{0,24},{8,16},{16,8},{24,0},{1,25},{9,17},{17,9},{25,1},{2,26},{10... | collective-permute-start | bytes 442376 | tf_op jit(solution)/shard_map/ppermute | solution.py:210
  34.3 4.5 %collective-permute-done.13.refs_3_ = bf16[64,1152]{1,0:T(8,128)(2,1)S(1)} collective-permute-done((bf16[64,1152]{1,0:T(8,128)(2,1)S(1)}, bf16[64,1152]{1,0:T(8,128)(2,1)S(1)}, u32[]{:S(2)}, u32[]{:S(2)}) %collective-permute-start.13) | collective-permute-done | bytes 147488 | tf_op jit(solution)/shard_map/ppermute | solution.py:210
  38.8 0.0 collective-permute-done.14.refs_4_
  38.8 0.0 collective-permute-done.11.refs_1_
  38.8 0.2 shard_map.74
  39.0 1.0 %collective-permute-done.16.refs_1_ = bf16[64,1152]{1,0:T(8,128)(2,1)S(1)} collective-permute-done((bf16[64,1152]{1,0:T(8,128)(2,1)S(1)}, bf16[64,1152]{1,0:T(8,128)(2,1)S(1)}, u32[]{:S(2)}, u32[]{:S(2)}) %collective-permute-start.16) | collective-permute-done | bytes 147488 | tf_op jit(solution)/shard_map/ppermute | solution.py:210
  40.0 0.0 collective-permute-done.15.refs_0_
  40.0 1.1 %shard_map.75 = (f32[256,1152]{1,0:T(8,128)}, f32[64,1152]{1,0:T(8,128)}) custom-call(s32[1]{0:T(128)} %bitcast.place, f32[128,1152]{1,0:T(8,128)S(1)} %get-tuple-element.46.ready, f32[64,1152]{1,0:T(8,128)S(1)} %get-tuple-element.47.grad_txt, bf16[64,1152]{1,0:T(8,128)(2,1)S(1)} %collective-permute-done.15.refs_0_, ...), custom_call_target="tpu_custom_call" | custom-call | flops 294912 | bytes 2359296 | tf_op jit(solution)/shard_map/pallas_call | solution.py:313
Async XLA Ops:
  0.6 10.6 %collective-permute-start = (f32[256,1152]{1,0:T(8,128)}, f32[256,1152]{1,0:T(8,128)S(1)}, u32[]{:S(2)}, u32[]{:S(2)}) collective-permute-start(f32[256,1152]{1,0:T(8,128)} %source.3), channel_id=1, source_target_pairs={{0,1},{1,0},{2,3},{3,2},{4,5},{5,4},{6,7},{7,6},{8,9},{9,8},{10,11... | collective-permute-start | bytes 3538952 | tf_op jit(solution)/shard_map/ppermute | solution.py:210
  2.3 8.3 %collective-permute-start.2 = (bf16[32,1152]{1,0:T(8,128)(2,1)S(1)}, bf16[32,1152]{1,0:T(8,128)(2,1)S(1)}, u32[]{:S(2)}, u32[]{:S(2)}) collective-permute-start(bf16[32,1152]{1,0:T(8,128)(2,1)S(1)} %get-tuple-element.30), channel_id=1, source_target_pairs={{0,4},{1,5},{2,6},{3,7},{4,0},{5,1},{6,2},{7,3},{8,12},{9,13},{10,... | collective-permute-start | bytes 221192 | tf_op jit(solution)/shard_map/ppermute | solution.py:210
  5.9 11.1 %collective-permute-start.3 = (bf16[64,1152]{1,0:T(8,128)(2,1)S(1)}, bf16[64,1152]{1,0:T(8,128)(2,1)S(1)}, u32[]{:S(2)}, u32[]{:S(2)}) collective-permute-start(bf16[64,1152]{1,0:T(8,128)(2,1)S(1)} %get-tuple-element.29.refs_0_), channel_id=1, source_target_pairs={{0,2},{1,3},{2,0},{3,1},{4,6},{5,7},{6,4},{7,5},{8,10},{9,11},{10,... | collective-permute-start | bytes 442376 | tf_op jit(solution)/shard_map/ppermute | solution.py:210
  7.5 8.8 %collective-permute-start.6 = (bf16[32,1152]{1,0:T(8,128)(2,1)S(1)}, bf16[32,1152]{1,0:T(8,128)(2,1)S(1)}, u32[]{:S(2)}, u32[]{:S(2)}) collective-permute-start(bf16[32,1152]{1,0:T(8,128)(2,1)S(1)} %get-tuple-element.31), channel_id=1, source_target_pairs={{0,4},{1,5},{2,6},{3,7},{4,0},{5,1},{6,2},{7,3},{8,12},{9,13},{10,... | collective-permute-start | bytes 221192 | tf_op jit(solution)/shard_map/ppermute | solution.py:210
  7.8 8.9 %collective-permute-start.5 = (bf16[32,1152]{1,0:T(8,128)(2,1)S(1)}, bf16[32,1152]{1,0:T(8,128)(2,1)S(1)}, u32[]{:S(2)}, u32[]{:S(2)}) collective-permute-start(bf16[32,1152]{1,0:T(8,128)(2,1)S(1)} %get-tuple-element.31), channel_id=1, source_target_pairs={{0,6},{1,7},{2,4},{3,5},{4,2},{5,3},{6,0},{7,1},{8,14},{9,15},{10,... | collective-permute-start | bytes 221192 | tf_op jit(solution)/shard_map/ppermute | solution.py:210
  10.5 6.5 %collective-permute-start.4 = (bf16[32,1152]{1,0:T(8,128)(2,1)S(1)}, bf16[32,1152]{1,0:T(8,128)(2,1)S(1)}, u32[]{:S(2)}, u32[]{:S(2)}) collective-permute-start(bf16[32,1152]{1,0:T(8,128)(2,1)S(1)} %collective-permute-done.2.refs_1_), channel_id=1, source_target_pairs={{0,2},{1,3},{2,0},{3,1},{4,6},{5,7},{6,4},{7,5},{8,10},{9,11},{10,... | collective-permute-start | bytes 221192 | tf_op jit(solution)/shard_map/ppermute | solution.py:210
  11.2 2.8 %collective-permute-start.1 = (s32[1,256]{1,0:T(1,128)}, s32[1,256]{1,0:T(1,128)S(1)}, u32[]{:S(2)}, u32[]{:S(2)}) collective-permute-start(s32[1,256]{1,0:T(1,128)} %bitcast.3), channel_id=1, source_target_pairs={{0,1},{1,0},{2,3},{3,2},{4,5},{5,4},{6,7},{7,6},{8,9},{9,8},{10,11... | collective-permute-start | bytes 3080 | tf_op jit(solution)/shard_map/ppermute | solution.py:210
  14.0 4.0 %copy-start = (s32[256]{0:T(256)S(1)}, s32[256]{0:T(256)}, u32[]{:S(2)}) copy-start(s32[256]{0:T(256)} %param.7) | copy-start | bytes 3076
  18.0 2.1 %collective-permute-start.7 = (bf16[256,1152]{1,0:T(8,128)(2,1)S(1)}, bf16[256,1152]{1,0:T(8,128)(2,1)S(1)}, u32[]{:S(2)}, u32[]{:S(2)}) collective-permute-start(bf16[256,1152]{1,0:T(8,128)(2,1)S(1)} %get-tuple-element.37), channel_id=1, source_target_pairs={{0,1},{1,0},{2,3},{3,2},{4,5},{5,4},{6,7},{7,6},{8,9},{9,8},{10,11... | collective-permute-start | bytes 1769480 | tf_op jit(solution)/shard_map/ppermute | solution.py:210
  20.2 6.9 %collective-permute-start.8 = (bf16[64,1152]{1,0:T(8,128)(2,1)S(1)}, bf16[64,1152]{1,0:T(8,128)(2,1)S(1)}, u32[]{:S(2)}, u32[]{:S(2)}) collective-permute-start(bf16[64,1152]{1,0:T(8,128)(2,1)S(1)} %get-tuple-element.40), channel_id=1, source_target_pairs={{0,8},{8,0},{16,24},{24,16},{1,9},{9,1},{17,25},{25,17},{2,10},{10... | collective-permute-start | bytes 442376 | tf_op jit(solution)/shard_map/ppermute | solution.py:210
  21.8 8.8 %collective-permute-start.9 = (bf16[64,1152]{1,0:T(8,128)(2,1)S(1)}, bf16[64,1152]{1,0:T(8,128)(2,1)S(1)}, u32[]{:S(2)}, u32[]{:S(2)}) collective-permute-start(bf16[64,1152]{1,0:T(8,128)(2,1)S(1)} %get-tuple-element.41), channel_id=1, source_target_pairs={{0,16},{8,24},{16,0},{24,8},{1,17},{9,25},{17,1},{25,9},{2,18},{10... | collective-permute-start | bytes 442376 | tf_op jit(solution)/shard_map/ppermute | solution.py:210
  23.3 7.3 %collective-permute-start.10 = (bf16[64,1152]{1,0:T(8,128)(2,1)S(1)}, bf16[64,1152]{1,0:T(8,128)(2,1)S(1)}, u32[]{:S(2)}, u32[]{:S(2)}) collective-permute-start(bf16[64,1152]{1,0:T(8,128)(2,1)S(1)} %get-tuple-element.42), channel_id=1, source_target_pairs={{0,24},{8,16},{16,8},{24,0},{1,25},{9,17},{17,9},{25,1},{2,26},{10... | collective-permute-start | bytes 442376 | tf_op jit(solution)/shard_map/ppermute | solution.py:210
  23.7 9.3 %collective-permute-start.12 = (bf16[64,1152]{1,0:T(8,128)(2,1)S(1)}, bf16[64,1152]{1,0:T(8,128)(2,1)S(1)}, u32[]{:S(2)}, u32[]{:S(2)}) collective-permute-start(bf16[64,1152]{1,0:T(8,128)(2,1)S(1)} %get-tuple-element.43), channel_id=1, source_target_pairs={{0,2},{1,3},{2,0},{3,1},{4,6},{5,7},{6,4},{7,5},{8,10},{9,11},{10,... | collective-permute-start | bytes 442376 | tf_op jit(solution)/shard_map/ppermute | solution.py:210
  25.2 13.6 %collective-permute-start.13 = (bf16[64,1152]{1,0:T(8,128)(2,1)S(1)}, bf16[64,1152]{1,0:T(8,128)(2,1)S(1)}, u32[]{:S(2)}, u32[]{:S(2)}) collective-permute-start(bf16[64,1152]{1,0:T(8,128)(2,1)S(1)} %get-tuple-element.44), channel_id=1, source_target_pairs={{0,4},{1,5},{2,6},{3,7},{4,0},{5,1},{6,2},{7,3},{8,12},{9,13},{10,... | collective-permute-start | bytes 442376 | tf_op jit(solution)/shard_map/ppermute | solution.py:210
  27.1 11.7 %collective-permute-start.14 = (bf16[64,1152]{1,0:T(8,128)(2,1)S(1)}, bf16[64,1152]{1,0:T(8,128)(2,1)S(1)}, u32[]{:S(2)}, u32[]{:S(2)}) collective-permute-start(bf16[64,1152]{1,0:T(8,128)(2,1)S(1)} %get-tuple-element.45), channel_id=1, source_target_pairs={{0,6},{1,7},{2,4},{3,5},{4,2},{5,3},{6,0},{7,1},{8,14},{9,15},{10,... | collective-permute-start | bytes 442376 | tf_op jit(solution)/shard_map/ppermute | solution.py:210
  30.8 8.1 %collective-permute-start.11 = (bf16[64,1152]{1,0:T(8,128)(2,1)S(1)}, bf16[64,1152]{1,0:T(8,128)(2,1)S(1)}, u32[]{:S(2)}, u32[]{:S(2)}) collective-permute-start(bf16[64,1152]{1,0:T(8,128)(2,1)S(1)} %shard_map.73.refs_0_), channel_id=1, source_target_pairs={{0,8},{8,0},{16,24},{24,16},{1,9},{9,1},{17,25},{25,17},{2,10},{10... | collective-permute-start | bytes 442376 | tf_op jit(solution)/shard_map/ppermute | solution.py:210
  32.1 7.9 %collective-permute-start.16 = (bf16[64,1152]{1,0:T(8,128)(2,1)S(1)}, bf16[64,1152]{1,0:T(8,128)(2,1)S(1)}, u32[]{:S(2)}, u32[]{:S(2)}) collective-permute-start(bf16[64,1152]{1,0:T(8,128)(2,1)S(1)} %shard_map.73.refs_0_), channel_id=1, source_target_pairs={{0,16},{8,24},{16,0},{24,8},{1,17},{9,25},{17,1},{25,9},{2,18},{10... | collective-permute-start | bytes 442376 | tf_op jit(solution)/shard_map/ppermute | solution.py:210
  33.0 7.0 %collective-permute-start.15 = (bf16[64,1152]{1,0:T(8,128)(2,1)S(1)}, bf16[64,1152]{1,0:T(8,128)(2,1)S(1)}, u32[]{:S(2)}, u32[]{:S(2)}) collective-permute-start(bf16[64,1152]{1,0:T(8,128)(2,1)S(1)} %shard_map.73.refs_0_), channel_id=1, source_target_pairs={{0,24},{8,16},{16,8},{24,0},{1,25},{9,17},{17,9},{25,1},{2,26},{10... | collective-permute-start | bytes 442376 | tf_op jit(solution)/shard_map/ppermute | solution.py:210

commit v25 on v24

--- a/solution.py
+++ b/solution.py
@@ -298,7 +298,7 @@
         24 << 20,
         10 * part * width,
     )
-    partners = [1, *range(count - 1, 1, -1)]
+    partners = list(range(count - 1, 0, -1))
     grads = [grad_part] + [swapped(grad_part, "img", k) for k in partners]
     partners = [0, *partners]
     early = 2

time: 41.4 us -> 41.2 us (level)
  transfers between devices with their start and end apart: 17 -> 17, of which waited for: 8 -> 9; matrix products, arithmetic and copies ran while one was open for 0% -> 0% of each run, Pallas kernels for 11% -> 11%
where the time goes in v25:
time: 41.2 us; the launch traced here: 41 us
  starting transfers between devices  22.3 us (54%)
  waiting for transfers between devices  10.1 us (25%)
  Pallas kernels  6.57 us (16%)
  between operations  2.03 us (5%)
    ppermute x17, starting transfers between devices, swapped(): return lax.ppermute(value, axis, [(s, s ^ step) for s in range(count)])  22.3 us
    ppermute x17, waiting for transfers between devices, swapped(): return lax.ppermute(value, axis, [(s, s ^ step) for s in range(count)])  10.1 us
    pallas_call x7, Pallas kernels, call(): pl.pallas_call(body, out_shape=outs, in_specs=specs, out_specs=[VMEM] * l...  5.42 us
    pallas_call x1, Pallas kernels, local(): pl.pallas_call(functools.partial(last_body, partners[:early], partners[ea...  1.15 us
  transfers between devices with their start and end apart: 17, of which 9 were waited for; matrix products, arithmetic and copies ran while one was open for 0% of the time, Pallas kernels for 11%

profile of v25, /device:TPU:0, one launch (start us, length us, event | category | flops | bytes accessed | tf_op | source)
XLA Modules:
  0.0 41.0 jit_solution(15618647075886526635)
XLA Ops:
  0.6 0.5 %collective-permute-start = (f32[256,1152]{1,0:T(8,128)}, f32[256,1152]{1,0:T(8,128)S(1)}, u32[]{:S(2)}, u32[]{:S(2)}) collective-permute-start(f32[256,1152]{1,0:T(8,128)} %source.3), channel_id=1, source_target_pairs={{0,1},{1,0},{2,3},{3,2},{4,5},{5,4},{6,7},{7,6},{8,9},{9,8},{10,11... | collective-permute-start | bytes 3538952 | tf_op jit(solution)/shard_map/ppermute | solution.py:210
  1.1 1.1 %shard_map.68 = (bf16[64,1152]{1,0:T(8,128)(2,1)S(1)}, bf16[32,1152]{1,0:T(8,128)(2,1)S(1)}, bf16[32,1152]{1,0:T(8,128)(2,1)S(1)}, f32[64,1152]{1,0:T(8,128)S(1)}, f32[64,128]{1,0:T(8,128)S(1)}) custom-call(f32[64,1152]{1,0:T(8,128)} %source.2), custom_call_target="tpu_custom_call" | custom-call | flops 294912 | bytes 917504 | tf_op jit(solution)/shard_map/pallas_call | solution.py:25
  2.3 3.7 %collective-permute-start.2 = (bf16[32,1152]{1,0:T(8,128)(2,1)S(1)}, bf16[32,1152]{1,0:T(8,128)(2,1)S(1)}, u32[]{:S(2)}, u32[]{:S(2)}) collective-permute-start(bf16[32,1152]{1,0:T(8,128)(2,1)S(1)} %get-tuple-element.30), channel_id=1, source_target_pairs={{0,4},{1,5},{2,6},{3,7},{4,0},{5,1},{6,2},{7,3},{8,12},{9,13},{10,... | collective-permute-start | bytes 221192 | tf_op jit(solution)/shard_map/ppermute | solution.py:210
  5.9 1.6 %collective-permute-start.3 = (bf16[64,1152]{1,0:T(8,128)(2,1)S(1)}, bf16[64,1152]{1,0:T(8,128)(2,1)S(1)}, u32[]{:S(2)}, u32[]{:S(2)}) collective-permute-start(bf16[64,1152]{1,0:T(8,128)(2,1)S(1)} %get-tuple-element.29.refs_0_), channel_id=1, source_target_pairs={{0,2},{1,3},{2,0},{3,1},{4,6},{5,7},{6,4},{7,5},{8,10},{9,11},{10,... | collective-permute-start | bytes 442376 | tf_op jit(solution)/shard_map/ppermute | solution.py:210
  7.5 0.3 collective-permute-start.6
  7.8 2.5 %collective-permute-start.5 = (bf16[32,1152]{1,0:T(8,128)(2,1)S(1)}, bf16[32,1152]{1,0:T(8,128)(2,1)S(1)}, u32[]{:S(2)}, u32[]{:S(2)}) collective-permute-start(bf16[32,1152]{1,0:T(8,128)(2,1)S(1)} %get-tuple-element.31), channel_id=1, source_target_pairs={{0,6},{1,7},{2,4},{3,5},{4,2},{5,3},{6,0},{7,1},{8,14},{9,15},{10,... | collective-permute-start | bytes 221192 | tf_op jit(solution)/shard_map/ppermute | solution.py:210
  10.3 0.2 collective-permute-done.2.refs_1_
  10.5 0.7 %collective-permute-start.4 = (bf16[32,1152]{1,0:T(8,128)(2,1)S(1)}, bf16[32,1152]{1,0:T(8,128)(2,1)S(1)}, u32[]{:S(2)}, u32[]{:S(2)}) collective-permute-start(bf16[32,1152]{1,0:T(8,128)(2,1)S(1)} %collective-permute-done.2.refs_1_), channel_id=1, source_target_pairs={{0,2},{1,3},{2,0},{3,1},{4,6},{5,7},{6,4},{7,5},{8,10},{9,11},{10,... | collective-permute-start | bytes 221192 | tf_op jit(solution)/shard_map/ppermute | solution.py:210
  11.2 0.0 collective-permute-done.other
  11.2 0.0 collective-permute-start.1
  12.5 1.5 %shard_map.69 = (bf16[256,1152]{1,0:T(8,128)(2,1)S(1)}, bf16[256,1152]{1,0:T(8,128)(2,1)S(1)}, f32[64,1152]{1,0:T(8,128)S(1)}, f32[64,128]{1,0:T(8,128)S(1)}) custom-call(s32[1]{0:T(128)} %bitcast.place, f32[256,1152]{1,0:T(8,128)S(1)} %collective-permute-done.other, f32[256,1152]{1,0:T(8,128)} %source.3), custom_call_target="tpu_custom_call" | custom-call | flops 2359296 | bytes 3866628 | tf_op jit(solution)/shard_map/pallas_call | solution.py:25
  14.0 0.0 copy-start
  14.0 0.0 collective-permute-done.1.perm
  14.1 2.3 %collective-permute-done.6.refs_5_ = bf16[32,1152]{1,0:T(8,128)(2,1)S(1)} collective-permute-done((bf16[32,1152]{1,0:T(8,128)(2,1)S(1)}, bf16[32,1152]{1,0:T(8,128)(2,1)S(1)}, u32[]{:S(2)}, u32[]{:S(2)}) %collective-permute-start.6) | collective-permute-done | bytes 73760 | tf_op jit(solution)/shard_map/ppermute | solution.py:210
  16.3 0.4 collective-permute-done.5.refs_4_
  16.7 0.3 collective-permute-done.4.refs_3_
  17.0 0.0 collective-permute-done.3.refs_2_
  17.1 0.9 %shard_map.70 = (bf16[256,256]{1,0:T(8,128)(2,1)S(1)}, bf16[256,1152]{1,0:T(8,128)(2,1)S(1)}) custom-call(s32[1]{0:T(128)} %bitcast.place, s32[1]{0:T(128)} %bitcast.1.column, f32[1]{0:T(128)S(6)} %copy.7.scale, f32[1]{0:T(128)S(6)} %copy.8.shift, s32[1,256]{1,0:T(1,128)S(1)} %collective-permute-done.1.perm, ...), custom_call_target="tpu_custom_call" | custom-call | flops 301989888 | bytes 1901584 | tf_op jit(solution)/shard_map/pallas_call | solution.py:25
  18.0 0.1 collective-permute-start.7
  18.1 0.0 copy-done
  18.1 1.4 %shard_map.71 = (f32[256,1152]{1,0:T(8,128)S(1)}, f32[64,1152]{1,0:T(8,128)S(1)}, bf16[192,1152]{1,0:T(8,128)(2,1)S(1)}) custom-call(s32[1]{0:T(128)} %bitcast.place, s32[1]{0:T(128)} %bitcast.1.column, f32[1]{0:T(128)S(6)} %copy.7.scale, f32[1]{0:T(128)S(6)} %copy.8.shift, s32[1,256]{1,0:T(1,128)S(1)} %bitcast.4, ...), custom_call_target="tpu_custom_call" | custom-call | flops 603979776 | bytes 3818512 | tf_op jit(solution)/shard_map/pallas_call | solution.py:25
  19.5 0.6 %collective-permute-done.7.other = bf16[256,1152]{1,0:T(8,128)(2,1)S(1)} collective-permute-done((bf16[256,1152]{1,0:T(8,128)(2,1)S(1)}, bf16[256,1152]{1,0:T(8,128)(2,1)S(1)}, u32[]{:S(2)}, u32[]{:S(2)}) %collective-permute-start.7) | collective-permute-done | bytes 589856 | tf_op jit(solution)/shard_map/ppermute | solution.py:210
  20.1 0.1 shard_map.72
  20.2 1.6 %collective-permute-start.8 = (bf16[64,1152]{1,0:T(8,128)(2,1)S(1)}, bf16[64,1152]{1,0:T(8,128)(2,1)S(1)}, u32[]{:S(2)}, u32[]{:S(2)}) collective-permute-start(bf16[64,1152]{1,0:T(8,128)(2,1)S(1)} %get-tuple-element.40), channel_id=1, source_target_pairs={{0,8},{8,0},{16,24},{24,16},{1,9},{9,1},{17,25},{25,17},{2,10},{10... | collective-permute-start | bytes 442376 | tf_op jit(solution)/shard_map/ppermute | solution.py:210
  21.8 1.5 %collective-permute-start.9 = (bf16[64,1152]{1,0:T(8,128)(2,1)S(1)}, bf16[64,1152]{1,0:T(8,128)(2,1)S(1)}, u32[]{:S(2)}, u32[]{:S(2)}) collective-permute-start(bf16[64,1152]{1,0:T(8,128)(2,1)S(1)} %get-tuple-element.41), channel_id=1, source_target_pairs={{0,16},{8,24},{16,0},{24,8},{1,17},{9,25},{17,1},{25,9},{2,18},{10... | collective-permute-start | bytes 442376 | tf_op jit(solution)/shard_map/ppermute | solution.py:210
  23.3 0.4 %collective-permute-start.10 = (bf16[64,1152]{1,0:T(8,128)(2,1)S(1)}, bf16[64,1152]{1,0:T(8,128)(2,1)S(1)}, u32[]{:S(2)}, u32[]{:S(2)}) collective-permute-start(bf16[64,1152]{1,0:T(8,128)(2,1)S(1)} %get-tuple-element.42), channel_id=1, source_target_pairs={{0,24},{8,16},{16,8},{24,0},{1,25},{9,17},{17,9},{25,1},{2,26},{10... | collective-permute-start | bytes 442376 | tf_op jit(solution)/shard_map/ppermute | solution.py:210
  23.7 1.5 %collective-permute-start.12 = (bf16[64,1152]{1,0:T(8,128)(2,1)S(1)}, bf16[64,1152]{1,0:T(8,128)(2,1)S(1)}, u32[]{:S(2)}, u32[]{:S(2)}) collective-permute-start(bf16[64,1152]{1,0:T(8,128)(2,1)S(1)} %get-tuple-element.43), channel_id=1, source_target_pairs={{0,2},{1,3},{2,0},{3,1},{4,6},{5,7},{6,4},{7,5},{8,10},{9,11},{10,... | collective-permute-start | bytes 442376 | tf_op jit(solution)/shard_map/ppermute | solution.py:210
  25.2 1.9 %collective-permute-start.13 = (bf16[64,1152]{1,0:T(8,128)(2,1)S(1)}, bf16[64,1152]{1,0:T(8,128)(2,1)S(1)}, u32[]{:S(2)}, u32[]{:S(2)}) collective-permute-start(bf16[64,1152]{1,0:T(8,128)(2,1)S(1)} %get-tuple-element.44), channel_id=1, source_target_pairs={{0,4},{1,5},{2,6},{3,7},{4,0},{5,1},{6,2},{7,3},{8,12},{9,13},{10,... | collective-permute-start | bytes 442376 | tf_op jit(solution)/shard_map/ppermute | solution.py:210
  27.1 0.0 collective-permute-done.8.refs_0_
  27.1 2.5 %collective-permute-start.14 = (bf16[64,1152]{1,0:T(8,128)(2,1)S(1)}, bf16[64,1152]{1,0:T(8,128)(2,1)S(1)}, u32[]{:S(2)}, u32[]{:S(2)}) collective-permute-start(bf16[64,1152]{1,0:T(8,128)(2,1)S(1)} %get-tuple-element.45), channel_id=1, source_target_pairs={{0,6},{1,7},{2,4},{3,5},{4,2},{5,3},{6,0},{7,1},{8,14},{9,15},{10,... | collective-permute-start | bytes 442376 | tf_op jit(solution)/shard_map/ppermute | solution.py:210
  29.6 0.9 %collective-permute-done.9.refs_1_ = bf16[64,1152]{1,0:T(8,128)(2,1)S(1)} collective-permute-done((bf16[64,1152]{1,0:T(8,128)(2,1)S(1)}, bf16[64,1152]{1,0:T(8,128)(2,1)S(1)}, u32[]{:S(2)}, u32[]{:S(2)}) %collective-permute-start.9) | collective-permute-done | bytes 147488 | tf_op jit(solution)/shard_map/ppermute | solution.py:210
  30.6 0.0 collective-permute-done.10.refs_2_
  30.6 0.2 shard_map.73.refs_0_
  30.8 1.7 %collective-permute-start.11 = (bf16[64,1152]{1,0:T(8,128)(2,1)S(1)}, bf16[64,1152]{1,0:T(8,128)(2,1)S(1)}, u32[]{:S(2)}, u32[]{:S(2)}) collective-permute-start(bf16[64,1152]{1,0:T(8,128)(2,1)S(1)} %shard_map.73.refs_0_), channel_id=1, source_target_pairs={{0,24},{8,16},{16,8},{24,0},{1,25},{9,17},{17,9},{25,1},{2,26},{10... | collective-permute-start | bytes 442376 | tf_op jit(solution)/shard_map/ppermute | solution.py:210
  32.5 1.4 %collective-permute-start.16 = (bf16[64,1152]{1,0:T(8,128)(2,1)S(1)}, bf16[64,1152]{1,0:T(8,128)(2,1)S(1)}, u32[]{:S(2)}, u32[]{:S(2)}) collective-permute-start(bf16[64,1152]{1,0:T(8,128)(2,1)S(1)} %shard_map.73.refs_0_), channel_id=1, source_target_pairs={{0,8},{8,0},{16,24},{24,16},{1,9},{9,1},{17,25},{25,17},{2,10},{10... | collective-permute-start | bytes 442376 | tf_op jit(solution)/shard_map/ppermute | solution.py:210
  33.8 0.0 collective-permute-done.12.refs_2_
  33.8 0.5 %collective-permute-start.15 = (bf16[64,1152]{1,0:T(8,128)(2,1)S(1)}, bf16[64,1152]{1,0:T(8,128)(2,1)S(1)}, u32[]{:S(2)}, u32[]{:S(2)}) collective-permute-start(bf16[64,1152]{1,0:T(8,128)(2,1)S(1)} %shard_map.73.refs_0_), channel_id=1, source_target_pairs={{0,16},{8,24},{16,0},{24,8},{1,17},{9,25},{17,1},{25,9},{2,18},{10... | collective-permute-start | bytes 442376 | tf_op jit(solution)/shard_map/ppermute | solution.py:210
  34.3 4.5 %collective-permute-done.13.refs_3_ = bf16[64,1152]{1,0:T(8,128)(2,1)S(1)} collective-permute-done((bf16[64,1152]{1,0:T(8,128)(2,1)S(1)}, bf16[64,1152]{1,0:T(8,128)(2,1)S(1)}, u32[]{:S(2)}, u32[]{:S(2)}) %collective-permute-start.13) | collective-permute-done | bytes 147488 | tf_op jit(solution)/shard_map/ppermute | solution.py:210
  38.8 0.0 collective-permute-done.14.refs_4_
  38.8 0.0 collective-permute-done.11.refs_1_
  38.8 0.2 shard_map.74
  39.0 0.7 %collective-permute-done.16.refs_1_ = bf16[64,1152]{1,0:T(8,128)(2,1)S(1)} collective-permute-done((bf16[64,1152]{1,0:T(8,128)(2,1)S(1)}, bf16[64,1152]{1,0:T(8,128)(2,1)S(1)}, u32[]{:S(2)}, u32[]{:S(2)}) %collective-permute-start.16) | collective-permute-done | bytes 147488 | tf_op jit(solution)/shard_map/ppermute | solution.py:210
  39.7 0.2 collective-permute-done.15.refs_0_
  39.8 1.1 %shard_map.75 = (f32[256,1152]{1,0:T(8,128)}, f32[64,1152]{1,0:T(8,128)}) custom-call(s32[1]{0:T(128)} %bitcast.place, f32[128,1152]{1,0:T(8,128)S(1)} %get-tuple-element.46.ready, f32[64,1152]{1,0:T(8,128)S(1)} %get-tuple-element.47.grad_txt, bf16[64,1152]{1,0:T(8,128)(2,1)S(1)} %collective-permute-done.15.refs_0_, ...), custom_call_target="tpu_custom_call" | custom-call | flops 294912 | bytes 2359296 | tf_op jit(solution)/shard_map/pallas_call | solution.py:313
Async XLA Ops:
  0.6 10.6 %collective-permute-start = (f32[256,1152]{1,0:T(8,128)}, f32[256,1152]{1,0:T(8,128)S(1)}, u32[]{:S(2)}, u32[]{:S(2)}) collective-permute-start(f32[256,1152]{1,0:T(8,128)} %source.3), channel_id=1, source_target_pairs={{0,1},{1,0},{2,3},{3,2},{4,5},{5,4},{6,7},{7,6},{8,9},{9,8},{10,11... | collective-permute-start | bytes 3538952 | tf_op jit(solution)/shard_map/ppermute | solution.py:210
  2.3 8.3 %collective-permute-start.2 = (bf16[32,1152]{1,0:T(8,128)(2,1)S(1)}, bf16[32,1152]{1,0:T(8,128)(2,1)S(1)}, u32[]{:S(2)}, u32[]{:S(2)}) collective-permute-start(bf16[32,1152]{1,0:T(8,128)(2,1)S(1)} %get-tuple-element.30), channel_id=1, source_target_pairs={{0,4},{1,5},{2,6},{3,7},{4,0},{5,1},{6,2},{7,3},{8,12},{9,13},{10,... | collective-permute-start | bytes 221192 | tf_op jit(solution)/shard_map/ppermute | solution.py:210
  5.9 11.1 %collective-permute-start.3 = (bf16[64,1152]{1,0:T(8,128)(2,1)S(1)}, bf16[64,1152]{1,0:T(8,128)(2,1)S(1)}, u32[]{:S(2)}, u32[]{:S(2)}) collective-permute-start(bf16[64,1152]{1,0:T(8,128)(2,1)S(1)} %get-tuple-element.29.refs_0_), channel_id=1, source_target_pairs={{0,2},{1,3},{2,0},{3,1},{4,6},{5,7},{6,4},{7,5},{8,10},{9,11},{10,... | collective-permute-start | bytes 442376 | tf_op jit(solution)/shard_map/ppermute | solution.py:210
  7.5 8.8 %collective-permute-start.6 = (bf16[32,1152]{1,0:T(8,128)(2,1)S(1)}, bf16[32,1152]{1,0:T(8,128)(2,1)S(1)}, u32[]{:S(2)}, u32[]{:S(2)}) collective-permute-start(bf16[32,1152]{1,0:T(8,128)(2,1)S(1)} %get-tuple-element.31), channel_id=1, source_target_pairs={{0,4},{1,5},{2,6},{3,7},{4,0},{5,1},{6,2},{7,3},{8,12},{9,13},{10,... | collective-permute-start | bytes 221192 | tf_op jit(solution)/shard_map/ppermute | solution.py:210
  7.8 8.9 %collective-permute-start.5 = (bf16[32,1152]{1,0:T(8,128)(2,1)S(1)}, bf16[32,1152]{1,0:T(8,128)(2,1)S(1)}, u32[]{:S(2)}, u32[]{:S(2)}) collective-permute-start(bf16[32,1152]{1,0:T(8,128)(2,1)S(1)} %get-tuple-element.31), channel_id=1, source_target_pairs={{0,6},{1,7},{2,4},{3,5},{4,2},{5,3},{6,0},{7,1},{8,14},{9,15},{10,... | collective-permute-start | bytes 221192 | tf_op jit(solution)/shard_map/ppermute | solution.py:210
  10.5 6.5 %collective-permute-start.4 = (bf16[32,1152]{1,0:T(8,128)(2,1)S(1)}, bf16[32,1152]{1,0:T(8,128)(2,1)S(1)}, u32[]{:S(2)}, u32[]{:S(2)}) collective-permute-start(bf16[32,1152]{1,0:T(8,128)(2,1)S(1)} %collective-permute-done.2.refs_1_), channel_id=1, source_target_pairs={{0,2},{1,3},{2,0},{3,1},{4,6},{5,7},{6,4},{7,5},{8,10},{9,11},{10,... | collective-permute-start | bytes 221192 | tf_op jit(solution)/shard_map/ppermute | solution.py:210
  11.2 2.8 %collective-permute-start.1 = (s32[1,256]{1,0:T(1,128)}, s32[1,256]{1,0:T(1,128)S(1)}, u32[]{:S(2)}, u32[]{:S(2)}) collective-permute-start(s32[1,256]{1,0:T(1,128)} %bitcast.3), channel_id=1, source_target_pairs={{0,1},{1,0},{2,3},{3,2},{4,5},{5,4},{6,7},{7,6},{8,9},{9,8},{10,11... | collective-permute-start | bytes 3080 | tf_op jit(solution)/shard_map/ppermute | solution.py:210
  14.0 4.0 %copy-start = (s32[256]{0:T(256)S(1)}, s32[256]{0:T(256)}, u32[]{:S(2)}) copy-start(s32[256]{0:T(256)} %param.7) | copy-start | bytes 3076
  18.0 2.1 %collective-permute-start.7 = (bf16[256,1152]{1,0:T(8,128)(2,1)S(1)}, bf16[256,1152]{1,0:T(8,128)(2,1)S(1)}, u32[]{:S(2)}, u32[]{:S(2)}) collective-permute-start(bf16[256,1152]{1,0:T(8,128)(2,1)S(1)} %get-tuple-element.37), channel_id=1, source_target_pairs={{0,1},{1,0},{2,3},{3,2},{4,5},{5,4},{6,7},{7,6},{8,9},{9,8},{10,11... | collective-permute-start | bytes 1769480 | tf_op jit(solution)/shard_map/ppermute | solution.py:210
  20.2 6.9 %collective-permute-start.8 = (bf16[64,1152]{1,0:T(8,128)(2,1)S(1)}, bf16[64,1152]{1,0:T(8,128)(2,1)S(1)}, u32[]{:S(2)}, u32[]{:S(2)}) collective-permute-start(bf16[64,1152]{1,0:T(8,128)(2,1)S(1)} %get-tuple-element.40), channel_id=1, source_target_pairs={{0,8},{8,0},{16,24},{24,16},{1,9},{9,1},{17,25},{25,17},{2,10},{10... | collective-permute-start | bytes 442376 | tf_op jit(solution)/shard_map/ppermute | solution.py:210
  21.8 8.8 %collective-permute-start.9 = (bf16[64,1152]{1,0:T(8,128)(2,1)S(1)}, bf16[64,1152]{1,0:T(8,128)(2,1)S(1)}, u32[]{:S(2)}, u32[]{:S(2)}) collective-permute-start(bf16[64,1152]{1,0:T(8,128)(2,1)S(1)} %get-tuple-element.41), channel_id=1, source_target_pairs={{0,16},{8,24},{16,0},{24,8},{1,17},{9,25},{17,1},{25,9},{2,18},{10... | collective-permute-start | bytes 442376 | tf_op jit(solution)/shard_map/ppermute | solution.py:210
  23.3 7.3 %collective-permute-start.10 = (bf16[64,1152]{1,0:T(8,128)(2,1)S(1)}, bf16[64,1152]{1,0:T(8,128)(2,1)S(1)}, u32[]{:S(2)}, u32[]{:S(2)}) collective-permute-start(bf16[64,1152]{1,0:T(8,128)(2,1)S(1)} %get-tuple-element.42), channel_id=1, source_target_pairs={{0,24},{8,16},{16,8},{24,0},{1,25},{9,17},{17,9},{25,1},{2,26},{10... | collective-permute-start | bytes 442376 | tf_op jit(solution)/shard_map/ppermute | solution.py:210
  23.7 10.1 %collective-permute-start.12 = (bf16[64,1152]{1,0:T(8,128)(2,1)S(1)}, bf16[64,1152]{1,0:T(8,128)(2,1)S(1)}, u32[]{:S(2)}, u32[]{:S(2)}) collective-permute-start(bf16[64,1152]{1,0:T(8,128)(2,1)S(1)} %get-tuple-element.43), channel_id=1, source_target_pairs={{0,2},{1,3},{2,0},{3,1},{4,6},{5,7},{6,4},{7,5},{8,10},{9,11},{10,... | collective-permute-start | bytes 442376 | tf_op jit(solution)/shard_map/ppermute | solution.py:210
  25.2 13.6 %collective-permute-start.13 = (bf16[64,1152]{1,0:T(8,128)(2,1)S(1)}, bf16[64,1152]{1,0:T(8,128)(2,1)S(1)}, u32[]{:S(2)}, u32[]{:S(2)}) collective-permute-start(bf16[64,1152]{1,0:T(8,128)(2,1)S(1)} %get-tuple-element.44), channel_id=1, source_target_pairs={{0,4},{1,5},{2,6},{3,7},{4,0},{5,1},{6,2},{7,3},{8,12},{9,13},{10,... | collective-permute-start | bytes 442376 | tf_op jit(solution)/shard_map/ppermute | solution.py:210
  27.1 11.7 %collective-permute-start.14 = (bf16[64,1152]{1,0:T(8,128)(2,1)S(1)}, bf16[64,1152]{1,0:T(8,128)(2,1)S(1)}, u32[]{:S(2)}, u32[]{:S(2)}) collective-permute-start(bf16[64,1152]{1,0:T(8,128)(2,1)S(1)} %get-tuple-element.45), channel_id=1, source_target_pairs={{0,6},{1,7},{2,4},{3,5},{4,2},{5,3},{6,0},{7,1},{8,14},{9,15},{10,... | collective-permute-start | bytes 442376 | tf_op jit(solution)/shard_map/ppermute | solution.py:210
  30.8 8.1 %collective-permute-start.11 = (bf16[64,1152]{1,0:T(8,128)(2,1)S(1)}, bf16[64,1152]{1,0:T(8,128)(2,1)S(1)}, u32[]{:S(2)}, u32[]{:S(2)}) collective-permute-start(bf16[64,1152]{1,0:T(8,128)(2,1)S(1)} %shard_map.73.refs_0_), channel_id=1, source_target_pairs={{0,24},{8,16},{16,8},{24,0},{1,25},{9,17},{17,9},{25,1},{2,26},{10... | collective-permute-start | bytes 442376 | tf_op jit(solution)/shard_map/ppermute | solution.py:210
  32.5 7.2 %collective-permute-start.16 = (bf16[64,1152]{1,0:T(8,128)(2,1)S(1)}, bf16[64,1152]{1,0:T(8,128)(2,1)S(1)}, u32[]{:S(2)}, u32[]{:S(2)}) collective-permute-start(bf16[64,1152]{1,0:T(8,128)(2,1)S(1)} %shard_map.73.refs_0_), channel_id=1, source_target_pairs={{0,8},{8,0},{16,24},{24,16},{1,9},{9,1},{17,25},{25,17},{2,10},{10... | collective-permute-start | bytes 442376 | tf_op jit(solution)/shard_map/ppermute | solution.py:210
  33.8 6.0 %collective-permute-start.15 = (bf16[64,1152]{1,0:T(8,128)(2,1)S(1)}, bf16[64,1152]{1,0:T(8,128)(2,1)S(1)}, u32[]{:S(2)}, u32[]{:S(2)}) collective-permute-start(bf16[64,1152]{1,0:T(8,128)(2,1)S(1)} %shard_map.73.refs_0_), channel_id=1, source_target_pairs={{0,16},{8,24},{16,0},{24,8},{1,17},{9,25},{17,1},{25,9},{2,18},{10... | collective-permute-start | bytes 442376 | tf_op jit(solution)/shard_map/ppermute | solution.py:210
